TPU v7x, 32 devices: a whole 2x2x4 slice. The times are simulated.
32 devices in a mesh: outer: 4 (over z), inner: 8 (over y, x, core).
Axes of the slice: x: 2, y: 2, z: 4, core: 2. Of those that a mesh axis runs over, the one named last changes fastest.
Arguments:
- queries: bfloat16 [4096, 2048], P(('outer', 'inner')), may hold values from -6 to 6
- keys: bfloat16 [4096, 2048], P(('outer', 'inner')), may hold values from -6 to 6
- values: bfloat16 [4096, 2048], P(('outer', 'inner')), may hold values from -6 to 6
- cotangent: bfloat16 [4096, 2048], P(('outer', 'inner')), may hold values from -6 to 6
Outputs:
- attended: bfloat16 [4096, 2048], P(('outer', 'inner'))
- grad_queries: bfloat16 [4096, 2048], P(('outer', 'inner'))
- grad_keys: bfloat16 [4096, 2048], P(('outer', 'inner'))
- grad_values: bfloat16 [4096, 2048], P(('outer', 'inner'))
All inputs are finite; a program needn't handle non-finite values.
Results may differ from a plain program's by a relative error of at most 0.013.
Values may be sent and summed in bfloat16 or wider, within the bound.
No kernel may reach another device: no remote copies, remote signals or barrier semaphores. Data moves between devices by JAX's collectives and lax.ppermute only.
A program may use at most 64 MiB of HBM per device.

v0:
```python
import jax
import jax.numpy as jnp
from jax import lax
from jax.sharding import PartitionSpec as P

HEADS = 16
HEAD = 128
BLOCK = 512


def carried_in(x, axis, combine, identity, reverse):
    count, place = (lax.axis_size(axis), lax.axis_index(axis))
    everything = lax.all_gather(x, axis)
    start = jnp.broadcast_to(jnp.asarray(identity, x.dtype), x.shape)

    def turn(k, before):
        at = count - 1 - k if reverse else k
        reached = at > place if reverse else at < place
        new = combine(before, everything[at])
        return jnp.where(reached, new, before)

    return lax.fori_loop(0, count, turn, start)


def add_states(earlier, later):
    return earlier + later


def body(queries, keys, values, cotangent):
    rows = queries.shape[0]
    inner_count = lax.axis_size("inner")
    outer_count = lax.axis_size("outer")
    units = 2 * HEADS
    half = HEAD // 2
    width = HEADS * HEAD
    scale = float(HEAD * rows * inner_count * outer_count) ** (-0.5)
    lower = jnp.arange(BLOCK)[:, None] >= jnp.arange(BLOCK)[None, :]
    local_units = units // inner_count

    def doubled(x):
        return jnp.broadcast_to(x.reshape(rows, HEADS, 1, HEAD), (rows, HEADS, 2, HEAD)).reshape(
            rows, units, HEAD
        )

    packed = jnp.concatenate(
        [
            doubled(queries),
            doubled(keys),
            values.reshape(rows, units, half),
            cotangent.reshape(rows, units, half),
        ],
        axis=2,
    )
    arrived = lax.all_to_all(packed, "inner", split_axis=1, concat_axis=0, tiled=True)
    group = arrived.shape[0]
    nblocks = group // BLOCK
    blocks = arrived.reshape(nblocks, BLOCK, local_units, 3 * HEAD)
    q_all = blocks[..., :HEAD]
    k_all = blocks[..., HEAD : 2 * HEAD]
    v_all = blocks[..., 2 * HEAD : 2 * HEAD + half]
    d_all = blocks[..., 2 * HEAD + half :]
    kv_blocks = jnp.einsum("nsuk,nsuv->nukv", k_all, v_all, preferred_element_type=jnp.float32)
    qd_blocks = jnp.einsum("ntuk,ntuv->nukv", q_all, d_all, preferred_element_type=jnp.float32)
    own_qd = jnp.sum(qd_blocks, 0)
    kv_total = jnp.sum(kv_blocks, 0)
    before_kv = jnp.zeros_like(kv_total)
    after_qd = jnp.zeros_like(own_qd)
    state_shape = kv_total.shape
    zeros = jnp.zeros(state_shape, jnp.float32)
    carried_kv = carried_in(kv_total, "outer", add_states, zeros, False)
    carried_qd = carried_in(own_qd, "outer", add_states, zeros, True)
    s_before = (carried_kv + before_kv)[None] + jnp.cumsum(kv_blocks, 0) - kv_blocks
    g_after = (carried_qd + after_qd + own_qd)[None] - jnp.cumsum(qd_blocks, 0)

    def one_block(parts):
        qq, kk, vv, dd, state, adjoint = parts
        s_round = state.astype(jnp.bfloat16)
        g_round = adjoint.astype(jnp.bfloat16)
        scores = jnp.einsum("tuk,suk->uts", qq, kk, preferred_element_type=jnp.float32)
        a_round = jnp.where(lower[None], scores, 0.0).astype(jnp.bfloat16)
        back = jnp.einsum("tuv,suv->uts", dd, vv, preferred_element_type=jnp.float32)
        b_round = jnp.where(lower[None], back, 0.0).astype(jnp.bfloat16)
        attended = scale * (
            jnp.einsum("tuk,ukv->tuv", qq, s_round, preferred_element_type=jnp.float32)
            + jnp.einsum("uts,suv->tuv", a_round, vv, preferred_element_type=jnp.float32)
        )
        part_q = scale * (
            jnp.einsum("tuv,ukv->tuk", dd, s_round, preferred_element_type=jnp.float32)
            + jnp.einsum("uts,suk->tuk", b_round, kk, preferred_element_type=jnp.float32)
        )
        part_k = scale * (
            jnp.einsum("suv,ukv->suk", vv, g_round, preferred_element_type=jnp.float32)
            + jnp.einsum("uts,tuk->suk", b_round, qq, preferred_element_type=jnp.float32)
        )
        grad_v = scale * (
            jnp.einsum("suk,ukv->suv", kk, g_round, preferred_element_type=jnp.float32)
            + jnp.einsum("uts,tuv->suv", a_round, dd, preferred_element_type=jnp.float32)
        )
        return (attended.astype(jnp.bfloat16), grad_v.astype(jnp.bfloat16), part_q, part_k)

    attended, grad_v, part_q, part_k = lax.map(
        one_block, (q_all, k_all, v_all, d_all, s_before, g_after)
    )
    attended = attended.reshape(group, local_units, half)
    grad_v = grad_v.reshape(group, local_units, half)
    part_q = part_q.reshape(group, local_units, HEAD)
    part_k = part_k.reshape(group, local_units, HEAD)
    light = jnp.concatenate([attended, grad_v], axis=2)
    heavy = jnp.concatenate([part_q, part_k], axis=2)
    light_back, heavy_back = (
        lax.all_to_all(
            light.astype(jnp.float32), "inner", split_axis=0, concat_axis=1, tiled=True
        ).astype(light.dtype),
        lax.all_to_all(heavy, "inner", split_axis=0, concat_axis=1, tiled=True),
    )
    light_four = light_back.reshape(rows, HEADS, 2, HEAD)
    heavy_four = heavy_back.reshape(rows, HEADS, 2, 2 * HEAD)
    summed = heavy_four[:, :, 0] + heavy_four[:, :, 1]
    out_main = light_four[..., :half].reshape(rows, width)
    out_values = light_four[..., half:].reshape(rows, width)
    out_queries = summed[..., :HEAD].reshape(rows, width).astype(jnp.bfloat16)
    out_keys = summed[..., HEAD:].reshape(rows, width).astype(jnp.bfloat16)
    return (out_main, out_queries, out_keys, out_values)


def solution(mesh):
    in_specs = (
        P(("outer", "inner"), None),
        P(("outer", "inner"), None),
        P(("outer", "inner"), None),
        P(("outer", "inner"), None),
    )
    out_specs = (
        P(("outer", "inner"), None),
        P(("outer", "inner"), None),
        P(("outer", "inner"), None),
        P(("outer", "inner"), None),
    )
    return jax.shard_map(body, mesh=mesh, in_specs=in_specs, out_specs=out_specs, check_vma=False)
```

profile of v0, /device:TPU:0, one launch (start us, length us, event | category | flops | bytes accessed | tf_op | source)
XLA Modules:
  0.0 229.0 jit_solution(8367733335784398497)
XLA Ops:
  6.9 2.6 %pad_maximum_fusion.1 = bf16[128,32,384]{2,0,1:T(8,128)(2,1)} fusion(bf16[128,32,64]{2,0,1:T(8,128)(2,1)S(1)} %copy.106, bf16[128,32,64]{2,0,1:T(8,128)(2,1)S(1)} %copy.105, bf16[128,32,128]{2,0,1:T(8,128)(2,1)S(1)} %bitcast.167, bf16[128,32,128]{2,0,1:T(8,128)(2,1)S(1)} %bitcast.166), kind=kLoop, calls=%fused_computation.69 | loop fusion | flops 12582912 | bytes 6291456 | tf_op jit(solution)/shard_map/concatenate | solution.py:45
  9.5 5.2 %all-to-all-start = ((bf16[128,32,384]{2,0,1:T(8,128)(2,1)}), bf16[128,32,384]{2,0,1:T(8,128)(2,1)S(1)}, u32[]{:S(2)}, u32[]{:S(2)}) async-start(bf16[128,32,384]{2,0,1:T(8,128)(2,1)} %pad_maximum_fusion.1), calls=%async_computation | async-start | bytes 6291456 | tf_op jit(solution)/shard_map/all_to_all | solution.py:54
  14.7 37.8 %all-to-all-done = bf16[128,32,384]{2,0,1:T(8,128)(2,1)S(1)} async-done(((bf16[128,32,384]{2,0,1:T(8,128)(2,1)}), bf16[128,32,384]{2,0,1:T(8,128)(2,1)S(1)}, u32[]{:S(2)}, u32[]{:S(2)}) %all-to-all-start) | async-done | bytes 3145760 | tf_op jit(solution)/shard_map/all_to_all | solution.py:54
  55.3 2.3 %copy.144 = bf16[2,512,4,64]{1,3,2,0:T(8,128)(2,1)} copy(bf16[2,512,4,64]{3,1,0,2:T(8,128)(2,1)} %get-tuple-element.432) | data formatting | bytes 1048576
  60.0 2.3 %copy.142 = bf16[2,512,4,64]{1,3,2,0:T(8,128)(2,1)} copy(bf16[2,512,4,64]{3,1,0,2:T(8,128)(2,1)} %get-tuple-element.433) | data formatting | bytes 1048576
  64.8 16.2 %all-gather = f32[16,128,64]{1,2,0:T(8,128)S(1)} all-gather(f32[4,128,64]{1,2,0:T(8,128)S(1)} %get-tuple-element.440), channel_id=2, replica_groups=mesh['outer'=4,'inner'=8] {'outer'}, dimensions={0}, use_global_device_ids=true | all-gather | bytes 655360 | tf_op jit(solution)/shard_map/all_gather | solution.py:13
  82.2 16.0 %all-gather.1 = f32[16,128,64]{1,2,0:T(8,128)S(1)} all-gather(f32[4,128,64]{1,2,0:T(8,128)S(1)} %get-tuple-element.442), channel_id=3, replica_groups=mesh['outer'=4,'inner'=8] {'outer'}, dimensions={0}, use_global_device_ids=true | all-gather | bytes 655360 | tf_op jit(solution)/shard_map/all_gather | solution.py:13
  100.1 45.9 %while.48 = (s32[]{:T(128)}, bf16[2,512,4,64]{1,3,2,0:T(8,128)(2,1)}, bf16[2,512,4,64]{1,3,2,0:T(8,128)(2,1)}, f32[2,512,4,128]{3,1,0,2:T(8,128)}, f32[2,512,4,1...) while((s32[]{:T(128)}, ...), condition=%wide.region_9.10_spmd.clone.clone, body=%wide.region_8.9_spmd.clone.clone.sunk | while | flops 1348468736 | bytes 81797536 | solution.py:101
  100.2 2.2 fusion.131
  102.5 2.2 fusion.129
  106.5 2.9 %fusion.135 = f32[4,128,512]{2,1,0:T(8,128)} fusion(bf16[4,512,512]{2,1,0:T(8,128)(2,1)S(1)} %select_convert_fusion.5, bf16[2,512,4,128]{3,1,2,0:T(8,128)(2,1)} %get-tuple-element.639, s32[]{:T(128)S(6)} %copy.195), kind=kOutput, calls=%fused_computation.20.clone.1 | convolution fusion | flops 268435456 | bytes 3670020 | tf_op jit(solution)/shard_map/while/body/eval_jaxpr/uts,suk->tuk/dot_general | solution.py:89
  114.6 2.1 select_convert_fusion.4
  118.3 1.9 fusion.130
  123.2 2.2 fusion.131
  125.4 2.2 fusion.129
  129.4 2.9 %fusion.135 = f32[4,128,512]{2,1,0:T(8,128)} fusion(bf16[4,512,512]{2,1,0:T(8,128)(2,1)S(1)} %select_convert_fusion.5, bf16[2,512,4,128]{3,1,2,0:T(8,128)(2,1)} %get-tuple-element.639, s32[]{:T(128)S(6)} %copy.195), kind=kOutput, calls=%fused_computation.20.clone.1 | convolution fusion | flops 268435456 | bytes 3670020 | tf_op jit(solution)/shard_map/while/body/eval_jaxpr/uts,suk->tuk/dot_general | solution.py:89
  137.5 2.1 select_convert_fusion.4
  141.3 1.9 fusion.130
  149.8 3.7 %all-to-all-start.1 = ((bf16[1024,4,128]{2,1,0:T(4,128)(2,1)}), bf16[1024,4,128]{2,1,0:T(4,128)(2,1)S(1)}, u32[]{:S(2)}, u32[]{:S(2)}) async-start(bf16[1024,4,128]{2,1,0:T(4,128)(2,1)} %copy.118), calls=%async_computation.1 | async-start | bytes 2097152 | tf_op jit(solution)/shard_map/all_to_all | solution.py:111
  155.4 4.6 %copy.124 = f32[1024,4,256]{2,1,0:T(4,128)} copy(f32[1024,4,256]{2,0,1:T(8,128)S(1)} %pad_maximum_fusion) | data formatting | bytes 8388608 | tf_op jit(solution)/shard_map/concatenate | solution.py:109
  160.1 8.6 %all-to-all-done.1 = bf16[1024,4,128]{2,1,0:T(4,128)(2,1)S(1)} async-done(((bf16[1024,4,128]{2,1,0:T(4,128)(2,1)}), bf16[1024,4,128]{2,1,0:T(4,128)(2,1)S(1)}, u32[]{:S(2)}, u32[]{:S(2)}) %all-to-all-start.1) | async-done | bytes 1048608 | tf_op jit(solution)/shard_map/all_to_all | solution.py:111
  168.7 4.6 %all-to-all-start.2 = ((f32[1024,4,256]{2,1,0:T(4,128)}), f32[1024,4,256]{2,1,0:T(4,128)}, u32[]{:S(2)}, u32[]{:S(2)}) async-start(f32[1024,4,256]{2,1,0:T(4,128)} %copy.124), calls=%async_computation.2 | async-start | bytes 8388608 | tf_op jit(solution)/shard_map/all_to_all | solution.py:114
  176.8 45.6 %all-to-all-done.2 = f32[1024,4,256]{2,1,0:T(4,128)} async-done(((f32[1024,4,256]{2,1,0:T(4,128)}), f32[1024,4,256]{2,1,0:T(4,128)}, u32[]{:S(2)}, u32[]{:S(2)}) %all-to-all-start.2) | async-done | bytes 4194336 | tf_op jit(solution)/shard_map/all_to_all | solution.py:114
  222.4 3.0 %copy.125 = f32[1024,4,256]{2,0,1:T(8,128)S(1)} copy(f32[1024,4,256]{2,1,0:T(4,128)} %all-to-all-done.2) | data formatting | bytes 8388608 | tf_op jit(solution)/shard_map/all_to_all | solution.py:114
  (141 shorter events, 54.4 us)
Async XLA Ops:
  0.6 2.4 %copy-start.10 = (bf16[128,2048]{1,0:T(8,128)(2,1)S(1)}, bf16[128,2048]{1,0:T(8,128)(2,1)}, u32[]{:S(2)}) copy-start(bf16[128,2048]{1,0:T(8,128)(2,1)} %param.12) | copy-start | bytes 1572868
  1.8 2.0 copy-start.11
  9.5 43.1 %all-to-all-start = ((bf16[128,32,384]{2,0,1:T(8,128)(2,1)}), bf16[128,32,384]{2,0,1:T(8,128)(2,1)S(1)}, u32[]{:S(2)}, u32[]{:S(2)}) async-start(bf16[128,32,384]{2,0,1:T(8,128)(2,1)} %pad_maximum_fusion.1), calls=%async_computation | async-start | bytes 6291456 | tf_op jit(solution)/shard_map/all_to_all | solution.py:54
  62.4 18.6 %copy-start.4 = (f32[4,128,64]{2,1,0:T(8,128)S(1)}, f32[4,128,64]{2,1,0:T(8,128)}, u32[]{:S(2)}) copy-start(f32[4,128,64]{2,1,0:T(8,128)} %custom-call) | copy-start | bytes 393220
  114.6 2.1 copy-start.3
  114.6 2.1 copy-start.12
  116.7 1.6 copy-start.2
  116.7 1.6 copy-start.14
  116.7 3.6 %copy-start.8 = (f32[2,512,4,128]{3,1,0,2:T(8,128)S(1)}, f32[2,512,4,128]{3,1,0,2:T(8,128)}, u32[]{:S(2)}) copy-start(f32[2,512,4,128]{3,1,0,2:T(8,128)} %get-tuple-element.622) | copy-start | bytes 6291460 | tf_op jit(solution)/shard_map/while
  118.3 2.2 copy-start.13
  118.3 2.0 copy-start.5
  121.1 2.0 copy-start.9
  137.5 2.1 copy-start.3
  137.5 2.1 copy-start.12
  139.6 1.6 copy-start.2
  139.6 1.6 copy-start.14
  139.7 3.6 %copy-start.8 = (f32[2,512,4,128]{3,1,0,2:T(8,128)S(1)}, f32[2,512,4,128]{3,1,0,2:T(8,128)}, u32[]{:S(2)}) copy-start(f32[2,512,4,128]{3,1,0,2:T(8,128)} %get-tuple-element.622) | copy-start | bytes 6291460 | tf_op jit(solution)/shard_map/while
  141.3 2.2 copy-start.13
  141.3 2.0 copy-start.5
  144.0 2.0 copy-start.9
  148.3 5.2 %copy-start.7 = (f32[2,512,4,128]{3,1,0,2:T(8,128)S(1)}, f32[2,512,4,128]{3,1,0,2:T(8,128)}, u32[]{:S(2)}) copy-start(f32[2,512,4,128]{3,1,0,2:T(8,128)} %get-tuple-element.266) | copy-start | bytes 6291460
  149.8 18.9 %all-to-all-start.1 = ((bf16[1024,4,128]{2,1,0:T(4,128)(2,1)}), bf16[1024,4,128]{2,1,0:T(4,128)(2,1)S(1)}, u32[]{:S(2)}, u32[]{:S(2)}) async-start(bf16[1024,4,128]{2,1,0:T(4,128)(2,1)} %copy.118), calls=%async_computation.1 | async-start | bytes 2097152 | tf_op jit(solution)/shard_map/all_to_all | solution.py:111
  168.7 53.7 %all-to-all-start.2 = ((f32[1024,4,256]{2,1,0:T(4,128)}), f32[1024,4,256]{2,1,0:T(4,128)}, u32[]{:S(2)}, u32[]{:S(2)}) async-start(f32[1024,4,256]{2,1,0:T(4,128)} %copy.124), calls=%async_computation.2 | async-start | bytes 8388608 | tf_op jit(solution)/shard_map/all_to_all | solution.py:114
  226.4 2.6 %copy-start.1 = (bf16[128,2048]{1,0:T(8,128)(2,1)S(1)}, bf16[128,2048]{1,0:T(8,128)(2,1)}, u32[]{:S(2)}) copy-start(bf16[128,2048]{1,0:T(8,128)(2,1)} %param.10) | copy-start | bytes 1572868
  (5 other events, 5.3 us)
where the time goes:
time: 230 us; the launch traced here: 229 us
  waiting for transfers between devices  92.1 us (40%)
  local copies, waits for them, and re-layouts  42.1 us (18%)
  matrix products  41.1 us (18%)
  blocking collectives  32.2 us (14%)
  starting transfers between devices  13.5 us (6%)
  other arithmetic  6.43 us (3%)
    all_to_all x1, waiting for transfers between devices, body(): lax.all_to_all(heavy, 'inner', split_axis=0, concat_axis=1, tiled=True)  45.6 us
    all_to_all x1, waiting for transfers between devices, body(): lax.all_to_all(packed, 'inner', split_axis=1, concat_axis=0, tiled=True)  37.8 us
    all_gather x2, blocking collectives, carried_in(): everything = lax.all_gather(x, axis)  32.2 us
    unnamed x22, local copies, waits for them, and re-layouts  13.2 us
    all_to_all x1, waiting for transfers between devices, body(): lax.all_to_all(light.astype(jnp.float32), 'inner', split_axis=0, concat_a...  8.64 us
    dot_general x2, matrix products, one_block(): jnp.einsum('uts,suk->tuk', b_round, kk, preferred_element_type=jnp.float32)  5.74 us
    while x40, local copies, waits for them, and re-layouts  5.3 us
    all_to_all x1, starting transfers between devices, body(): lax.all_to_all(packed, 'inner', split_axis=1, concat_axis=0, tiled=True)  5.17 us
  transfers between devices with their start and end apart: 3, of which 3 were waited for; matrix products, arithmetic and copies ran while one was open for 4% of the time, Pallas kernels for 0%

commit v1 on v0

v1 whole, which is shorter than its diff:
```python
import functools

import jax
import jax.numpy as jnp
from jax import lax
from jax.experimental import pallas as pl
from jax.experimental.pallas import tpu as pltpu
from jax.sharding import PartitionSpec as P

HEAD = 128
GROUP = 4
MIB = 1024 * 1024


def dot(a, b, over_a, over_b):
    return lax.dot_general(
        a, b, (((over_a,), (over_b,)), ((), ())), preferred_element_type=jnp.float32
    )


def own_states_kernel(q_ref, k_ref, v_ref, d_ref, states_ref):
    slices, _, depth, _ = states_ref.shape
    kv, qd = [], []
    for h in range(q_ref.shape[1] // HEAD):
        cols = slice(h * HEAD, (h + 1) * HEAD)
        kv.append(dot(k_ref[:, cols], v_ref[:, cols], 0, 0).astype(jnp.bfloat16))
        qd.append(dot(q_ref[:, cols], d_ref[:, cols], 0, 0).astype(jnp.bfloat16))
    kv = jnp.concatenate(kv, axis=0)
    qd = jnp.concatenate(qd, axis=0)
    for j in range(slices):
        states_ref[j, 0] = kv[j * depth : (j + 1) * depth]
        states_ref[j, 1] = qd[j * depth : (j + 1) * depth]


def own_states(queries, keys, values, cotangent, count):
    rows, width = queries.shape
    depth = width // count
    steps = width // (HEAD * GROUP)
    tokens = pl.BlockSpec((rows, GROUP * HEAD), lambda g: (0, g))
    return pl.pallas_call(
        own_states_kernel,
        grid=(steps,),
        in_specs=[tokens] * 4,
        out_specs=pl.BlockSpec((count // steps, 2, depth, HEAD), lambda g: (g, 0, 0, 0)),
        out_shape=jax.ShapeDtypeStruct((count, 2, depth, HEAD), jnp.bfloat16),
        cost_estimate=pl.CostEstimate(
            flops=4 * rows * width * HEAD, bytes_accessed=12 * rows * width, transcendentals=0
        ),
        compiler_params=pltpu.CompilerParams(vmem_limit_bytes=32 * MIB),
    )(queries, keys, values, cotangent)


def scan_kernel(place_ref, arrived_ref, groups_ref, out_ref):
    count = arrived_ref.shape[0]
    outer_count = groups_ref.shape[0]
    place = place_ref[0]
    before = jnp.zeros(arrived_ref.shape[2:], jnp.float32)
    after = before
    for z in range(outer_count):
        before += jnp.where(z < place, groups_ref[z, 0], 0.0)
        after += jnp.where(z > place, groups_ref[z, 1], 0.0)
    for i in range(count):
        out_ref[i, 0] = before.astype(jnp.bfloat16)
        before += arrived_ref[i, 0].astype(jnp.float32)
    for i in reversed(range(count)):
        out_ref[i, 1] = after.astype(jnp.bfloat16)
        after += arrived_ref[i, 1].astype(jnp.float32)


def scan_states(arrived, groups, place):
    return pl.pallas_call(
        scan_kernel,
        in_specs=[
            pl.BlockSpec(memory_space=pltpu.SMEM),
            pl.BlockSpec(memory_space=pltpu.VMEM),
            pl.BlockSpec(memory_space=pltpu.VMEM),
        ],
        out_specs=pl.BlockSpec(memory_space=pltpu.VMEM),
        out_shape=jax.ShapeDtypeStruct(arrived.shape, jnp.bfloat16),
        compiler_params=pltpu.CompilerParams(vmem_limit_bytes=32 * MIB),
    )(place, arrived, groups)


def finish_kernel(scale, q_ref, k_ref, v_ref, d_ref, states_ref, att_ref, gq_ref, gk_ref, gv_ref):
    rows = q_ref.shape[0]
    at = lax.broadcasted_iota(jnp.int32, (rows, rows), 0)
    to = lax.broadcasted_iota(jnp.int32, (rows, rows), 1)
    lower, upper = at >= to, at <= to
    slices, _, depth, _ = states_ref.shape
    s_all = jnp.concatenate([states_ref[j, 0] for j in range(slices)], axis=0)
    g_all = jnp.concatenate([states_ref[j, 1] for j in range(slices)], axis=0)

    def masked(mask, a, b):
        return jnp.where(mask, dot(a, b, 1, 1), 0.0).astype(jnp.bfloat16)

    for h in range(q_ref.shape[1] // HEAD):
        cols = slice(h * HEAD, (h + 1) * HEAD)
        q, k, v, d = (ref[:, cols] for ref in (q_ref, k_ref, v_ref, d_ref))
        s, g = s_all[cols], g_all[cols]
        a, a_t = masked(lower, q, k), masked(upper, k, q)
        b, b_t = masked(lower, d, v), masked(upper, v, d)
        att = dot(q, s, 1, 0) + dot(a, v, 1, 0)
        gq = dot(d, s, 1, 1) + dot(b, k, 1, 0)
        gk = dot(v, g, 1, 1) + dot(b_t, q, 1, 0)
        gv = dot(k, g, 1, 0) + dot(a_t, d, 1, 0)
        att_ref[:, cols] = (scale * att).astype(jnp.bfloat16)
        gq_ref[:, cols] = (scale * gq).astype(jnp.bfloat16)
        gk_ref[:, cols] = (scale * gk).astype(jnp.bfloat16)
        gv_ref[:, cols] = (scale * gv).astype(jnp.bfloat16)


def finish(queries, keys, values, cotangent, states, scale):
    rows, width = queries.shape
    count, _, depth, _ = states.shape
    steps = width // (HEAD * GROUP)
    tokens = pl.BlockSpec((rows, GROUP * HEAD), lambda g: (0, g))
    out = jax.ShapeDtypeStruct((rows, width), jnp.bfloat16)
    return pl.pallas_call(
        functools.partial(finish_kernel, scale),
        grid=(steps,),
        in_specs=[tokens] * 4
        + [pl.BlockSpec((count // steps, 2, depth, HEAD), lambda g: (g, 0, 0, 0))],
        out_specs=[tokens] * 4,
        out_shape=[out] * 4,
        cost_estimate=pl.CostEstimate(
            flops=24 * rows * width * HEAD, bytes_accessed=20 * rows * width, transcendentals=0
        ),
        compiler_params=pltpu.CompilerParams(vmem_limit_bytes=32 * MIB),
    )(queries, keys, values, cotangent, states)


def body(queries, keys, values, cotangent):
    rows = queries.shape[0]
    count = lax.axis_size("inner")
    outer_count = lax.axis_size("outer")
    scale = float(HEAD * rows * count * outer_count) ** (-0.5)
    own = own_states(queries, keys, values, cotangent, count)
    arrived = lax.all_to_all(own, "inner", split_axis=0, concat_axis=0, tiled=True)
    total = jnp.sum(arrived.astype(jnp.float32), 0)
    groups = lax.all_gather(total, "outer")
    place = lax.axis_index("outer").astype(jnp.int32).reshape(1)
    scanned = scan_states(arrived, groups, place)
    states = lax.all_to_all(scanned, "inner", split_axis=0, concat_axis=0, tiled=True)
    return tuple(finish(queries, keys, values, cotangent, states, scale))


def solution(mesh):
    spec = P(("outer", "inner"), None)
    return jax.shard_map(
        body, mesh=mesh, in_specs=(spec,) * 4, out_specs=(spec,) * 4, check_vma=False
    )
```

time: 230 us -> 94.8 us (0.41)
  waiting for transfers between devices: 92.1 us -> 27.5 us
  matrix products: 41.1 us -> 0 us
  local copies, waits for them, and re-layouts: 42.1 us -> 5.41 us
  starting transfers between devices: 13.5 us -> 0.04 us
  between operations: 0.98 us -> 14.1 us
  Pallas kernels: 0 us -> 7.22 us
  blocking collectives: 32.2 us -> 39.3 us
  other arithmetic: 6.43 us -> 0.84 us
    all_to_all x3 -> x0, waiting for transfers between devices: 92.1 us -> none  [the longest x1 45.6 us: body(): lax.all_to_all(heavy, 'inner', split_axis=0, concat_axis=1, tiled=True)]
    dot_general x22 -> x0, matrix products: 41.1 us -> none  [the longest x2 5.74 us: one_block(): jnp.einsum('uts,suk->tuk', b_round, kk, preferred_element_type=jnp.float32)]
    all_to_all x0 -> x2, blocking collectives: none -> 39.3 us  [the longest x1 20.3 us: body(): lax.all_to_all(own, 'inner', split_axis=0, concat_axis=0, tiled=True)]
    all_gather x2 -> x0, blocking collectives: 32.2 us -> none  [carried_in(): everything = lax.all_gather(x, axis)]
    all_gather x0 -> x1, waiting for transfers between devices: none -> 27.5 us  [body(): groups = lax.all_gather(total, 'outer')]
    all_to_all x3 -> x0, starting transfers between devices: 13.5 us -> none  [the longest x1 5.17 us: body(): lax.all_to_all(packed, 'inner', split_axis=1, concat_axis=0, tiled=True)]
    unnamed x22 -> x18, local copies, waits for them, and re-layouts: 13.2 us -> 5.41 us
    pallas_call x0 -> x3, Pallas kernels: none -> 7.22 us  [the longest x1 5.74 us: finish(): pl.pallas_call(functools.partial(finish_kernel, scale), grid=(steps,), in...]
  transfers between devices with their start and end apart: 3 -> 1, of which waited for: 3 -> 1; matrix products, arithmetic and copies ran while one was open for 4% -> 0% of each run, Pallas kernels for 0% -> 0%
where the time goes in v1:
time: 94.8 us; the launch traced here: 94.3 us
  blocking collectives  39.3 us (41%)
  waiting for transfers between devices  27.5 us (29%)
  between operations  14.1 us (15%)
  Pallas kernels  7.22 us (8%)
  local copies, waits for them, and re-layouts  5.41 us (6%)
    all_gather x1, waiting for transfers between devices, body(): groups = lax.all_gather(total, 'outer')  27.5 us
    all_to_all x1, blocking collectives, body(): lax.all_to_all(own, 'inner', split_axis=0, concat_axis=0, tiled=True)  20.3 us
    all_to_all x1, blocking collectives, body(): lax.all_to_all(scanned, 'inner', split_axis=0, concat_axis=0, tiled=True)  18.9 us
    pallas_call x1, Pallas kernels, finish(): pl.pallas_call(functools.partial(finish_kernel, scale), grid=(steps,), in...  5.74 us
    unnamed x18, local copies, waits for them, and re-layouts  5.41 us
  transfers between devices with their start and end apart: 1, of which 1 were waited for; matrix products, arithmetic and copies ran while one was open for 0% of the time, Pallas kernels for 0%

profile of v1, /device:TPU:0, one launch (start us, length us, event | category | flops | bytes accessed | tf_op | source)
XLA Modules:
  0.0 94.3 jit_solution(3229842783930386026)
XLA Ops:
  7.2 0.0 all-gather.3.cloned.1.call-start
  7.2 0.0 copy-start
  7.2 1.0 %copy-done = bf16[128,2048]{1,0:T(8,128)(2,1)S(1)} copy-done((bf16[128,2048]{1,0:T(8,128)(2,1)S(1)}, bf16[128,2048]{1,0:T(8,128)(2,1)}, u32[]{:S(2)}) %copy-start) | copy-done | bytes 524312
  8.3 0.0 copy-start.2
  8.3 1.0 %copy-done.2 = bf16[128,2048]{1,0:T(8,128)(2,1)S(1)} copy-done((bf16[128,2048]{1,0:T(8,128)(2,1)S(1)}, bf16[128,2048]{1,0:T(8,128)(2,1)}, u32[]{:S(2)}) %copy-start.2) | copy-done | bytes 524312
  9.3 1.0 %copy-done.4 = bf16[128,2048]{1,0:T(8,128)(2,1)S(1)} copy-done((bf16[128,2048]{1,0:T(8,128)(2,1)S(1)}, bf16[128,2048]{1,0:T(8,128)(2,1)}, u32[]{:S(2)}) %copy-start.4) | copy-done | bytes 524312
  10.3 1.0 %copy-done.6 = bf16[128,2048]{1,0:T(8,128)(2,1)S(1)} copy-done((bf16[128,2048]{1,0:T(8,128)(2,1)S(1)}, bf16[128,2048]{1,0:T(8,128)(2,1)}, u32[]{:S(2)}) %copy-start.6) | copy-done | bytes 524312
  11.4 1.3 %shard_map.75 = bf16[8,2,256,128]{3,2,1,0:T(8,128)(2,1)S(1)} custom-call(bf16[128,2048]{1,0:T(8,128)(2,1)S(1)} %copy-done, bf16[128,2048]{1,0:T(8,128)(2,1)S(1)} %copy-done.2, bf16[128,2048]{1,0:T(8,128)(2,1)S(1)} %copy-done.4, bf16[128,2048]{1,0:T(8,128)(2,1)S(1)} %copy-done.6), custom_call_target="tpu_custom_call" | custom-call | flops 134217728 | bytes 3145728 | tf_op jit(solution)/shard_map/pallas_call | solution.py:40
  12.7 20.3 %all_to_all.10.arrived_ref = bf16[8,2,256,128]{3,2,1,0:T(8,128)(2,1)S(1)} all-to-all(bf16[8,2,256,128]{3,2,1,0:T(8,128)(2,1)S(1)} %shard_map.75), channel_id=1, replica_groups=mesh['outer'=4,'inner'=8] {'inner'}, dimensions={0} | all-to-all | bytes 2097152 | tf_op jit(solution)/shard_map/all_to_all | solution.py:138
  33.0 0.8 convert_reduce_fusion
  33.8 0.0 all-gather.3.cloned.1.call-update
  33.9 27.5 %all-gather.3.cloned.1.call-done = f32[8,256,128]{2,1,0:T(8,128)} async-done(((f32[2,256,128]{2,1,0:T(8,128)}), f32[8,256,128]{2,1,0:T(8,128)}) %all-gather.3.cloned.1.call-update) | async-done | bytes 1048592 | tf_op jit(solution)/shard_map/all_gather | solution.py:140
  61.3 1.2 %copy-done.8 = f32[8,256,128]{2,1,0:T(8,128)S(1)} copy-done((f32[8,256,128]{2,1,0:T(8,128)S(1)}, f32[8,256,128]{2,1,0:T(8,128)}, u32[]{:S(2)}) %copy-start.8) | copy-done | bytes 1048600
  62.5 0.2 shard_map.76
  62.7 0.0 copy-start.1
  62.8 0.0 copy-start.3
  62.8 0.0 copy-start.5
  62.8 0.0 copy-start.7
  62.8 18.9 %all_to_all.11.states_ref = bf16[8,2,256,128]{3,2,1,0:T(8,128)(2,1)S(1)} all-to-all(bf16[8,2,256,128]{3,2,1,0:T(8,128)(2,1)S(1)} %shard_map.76), channel_id=1, replica_groups=mesh['outer'=4,'inner'=8] {'inner'}, dimensions={0} | all-to-all | bytes 2097152 | tf_op jit(solution)/shard_map/all_to_all | solution.py:143
  81.7 0.0 copy-done.1
  81.7 0.0 copy-done.3
  81.7 0.0 copy-done.5
  81.7 0.0 copy-done.7
  81.8 5.7 %shard_map.77 = (bf16[128,2048]{1,0:T(8,128)(2,1)}, bf16[128,2048]{1,0:T(8,128)(2,1)}, bf16[128,2048]{1,0:T(8,128)(2,1)}, bf16[128,2048]{1,0:T(8,128)(2,1)}) custom-call(bf16[128,2048]{1,0:T(8,128)(2,1)S(1)} %copy-done.1, bf16[128,2048]{1,0:T(8,128)(2,1)S(1)} %copy-done.3, bf16[128,2048]{1,0:T(8,128)(2,1)S(1)} %copy-done.5, bf16[128,2048]{1,0:T(8,128)(2,1)S(1)} %copy-done.7, ...), custom_call_target="tpu_custom_call" | custom-call | flops 805306368 | bytes 5242880 | tf_op jit(solution)/shard_map/pallas_call | solution.py:118
  (3 shorter events, 0.0 us)
Async XLA Ops:
  7.2 54.1 %all-gather.3.cloned.1.call-start = ((), (), s32[]{:S(2)}) async-start(), calls=%async_computation.2 | async-start | bytes 1310720 | tf_op jit(solution)/shard_map/all_gather | solution.py:140
  7.2 1.0 %copy-start = (bf16[128,2048]{1,0:T(8,128)(2,1)S(1)}, bf16[128,2048]{1,0:T(8,128)(2,1)}, u32[]{:S(2)}) copy-start(bf16[128,2048]{1,0:T(8,128)(2,1)} %q_ref.3) | copy-start | bytes 1572868
  8.3 1.0 %copy-start.2 = (bf16[128,2048]{1,0:T(8,128)(2,1)S(1)}, bf16[128,2048]{1,0:T(8,128)(2,1)}, u32[]{:S(2)}) copy-start(bf16[128,2048]{1,0:T(8,128)(2,1)} %k_ref.3) | copy-start | bytes 1572868
  9.3 1.0 %copy-start.4 = (bf16[128,2048]{1,0:T(8,128)(2,1)S(1)}, bf16[128,2048]{1,0:T(8,128)(2,1)}, u32[]{:S(2)}) copy-start(bf16[128,2048]{1,0:T(8,128)(2,1)} %v_ref.3) | copy-start | bytes 1572868
  10.3 1.0 %copy-start.6 = (bf16[128,2048]{1,0:T(8,128)(2,1)S(1)}, bf16[128,2048]{1,0:T(8,128)(2,1)}, u32[]{:S(2)}) copy-start(bf16[128,2048]{1,0:T(8,128)(2,1)} %d_ref.3) | copy-start | bytes 1572868
  61.3 1.2 %copy-start.8 = (f32[8,256,128]{2,1,0:T(8,128)S(1)}, f32[8,256,128]{2,1,0:T(8,128)}, u32[]{:S(2)}) copy-start(f32[8,256,128]{2,1,0:T(8,128)} %all-gather.3.cloned.1.call-done) | copy-start | bytes 3145732
  62.7 19.0 %copy-start.1 = (bf16[128,2048]{1,0:T(8,128)(2,1)S(1)}, bf16[128,2048]{1,0:T(8,128)(2,1)}, u32[]{:S(2)}) copy-start(bf16[128,2048]{1,0:T(8,128)(2,1)} %q_ref.3) | copy-start | bytes 1572868
  62.8 19.0 %copy-start.3 = (bf16[128,2048]{1,0:T(8,128)(2,1)S(1)}, bf16[128,2048]{1,0:T(8,128)(2,1)}, u32[]{:S(2)}) copy-start(bf16[128,2048]{1,0:T(8,128)(2,1)} %k_ref.3) | copy-start | bytes 1572868
  62.8 19.0 %copy-start.5 = (bf16[128,2048]{1,0:T(8,128)(2,1)S(1)}, bf16[128,2048]{1,0:T(8,128)(2,1)}, u32[]{:S(2)}) copy-start(bf16[128,2048]{1,0:T(8,128)(2,1)} %v_ref.3) | copy-start | bytes 1572868
  62.8 19.0 %copy-start.7 = (bf16[128,2048]{1,0:T(8,128)(2,1)S(1)}, bf16[128,2048]{1,0:T(8,128)(2,1)}, u32[]{:S(2)}) copy-start(bf16[128,2048]{1,0:T(8,128)(2,1)} %d_ref.3) | copy-start | bytes 1572868
Sparse Core Ops, SparseCore 0:
  34.0 27.2 all-gather.2

commit v2 on v1

v2 whole, which is shorter than its diff:
```python
import functools

import jax
import jax.numpy as jnp
from jax import lax
from jax.experimental import pallas as pl
from jax.experimental.pallas import tpu as pltpu
from jax.sharding import PartitionSpec as P

HEAD = 128
GROUP = 4
MIB = 1024 * 1024
ANY = pl.BlockSpec(memory_space=pl.ANY)
SMEM = pl.BlockSpec(memory_space=pltpu.SMEM)
VMEM = pl.BlockSpec(memory_space=pltpu.VMEM)


def dot(a, b, over_a, over_b):
    return lax.dot_general(
        a, b, (((over_a,), (over_b,)), ((), ())), preferred_element_type=jnp.float32
    )


def own_states_kernel(place_ref, q_ref, k_ref, v_ref, d_ref, *refs):
    count = len(refs) - 1
    slots, whole = refs[:count], refs[count]
    depth = slots[0].shape[1]
    wide = max(depth, HEAD)
    inner = place_ref[1]
    for s, slot in enumerate(slots):
        row = (inner ^ s) * depth
        first = pl.multiple_of(row // HEAD * HEAD, HEAD)
        for h in range(wide // HEAD):
            cols = pl.ds(pl.multiple_of(first + h * HEAD, HEAD), HEAD)
            into = slice(h * HEAD, (h + 1) * HEAD)
            kv = dot(k_ref[:, cols], v_ref[:, cols], 0, 0)
            qd = dot(q_ref[:, cols], d_ref[:, cols], 0, 0)
            if depth >= HEAD:
                slot[0, into] = kv.astype(jnp.bfloat16)
                slot[1, into] = qd.astype(jnp.bfloat16)
            else:
                whole[0], whole[1] = kv, qd
                part = pl.ds(pl.multiple_of(row - first, depth), depth)
                slot[0] = whole[0, part].astype(jnp.bfloat16)
                slot[1] = whole[1, part].astype(jnp.bfloat16)


def own_states(place, queries, keys, values, cotangent, count):
    rows, width = queries.shape
    depth = width // count
    slot = jax.ShapeDtypeStruct((2, depth, HEAD), jnp.bfloat16)
    return pl.pallas_call(
        own_states_kernel,
        in_specs=[SMEM] + [VMEM] * 4,
        out_specs=[VMEM] * count,
        out_shape=[slot] * count,
        scratch_shapes=[pltpu.VMEM((2, HEAD, HEAD), jnp.float32)],
        cost_estimate=pl.CostEstimate(
            flops=4 * rows * width * HEAD, bytes_accessed=12 * rows * width, transcendentals=0
        ),
        compiler_params=pltpu.CompilerParams(vmem_limit_bytes=60 * MIB),
    )(place, queries, keys, values, cotangent)


def fetch(slots, held, sems, inner):
    copies = [
        pltpu.make_async_copy(slot, held.at[inner ^ s], sems.at[s]) for s, slot in enumerate(slots)
    ]
    for copy in copies:
        copy.start()
    for copy in copies:
        copy.wait()


def totals_kernel(count, outer_count, place_ref, *refs):
    slots, sends = refs[:count], refs[count : count + outer_count - 1]
    held, sems = refs[-2:]
    outer = place_ref[0]
    fetch(slots, held, sems, place_ref[1])
    totals = []
    for which in range(2):
        total = held[0, which].astype(jnp.float32)
        for i in range(1, count):
            total += held[i, which].astype(jnp.float32)
        totals.append(total.astype(jnp.bfloat16))
    for s, send in enumerate(sends):
        upward = outer + s + 1 < outer_count

        @pl.when(upward)
        def _():
            send[...] = totals[0]

        @pl.when(jnp.logical_not(upward))
        def _():
            send[...] = totals[1]


def totals(place, slots, outer_count):
    count, shape = len(slots), slots[0].shape
    return pl.pallas_call(
        functools.partial(totals_kernel, count, outer_count),
        in_specs=[SMEM] + [ANY] * count,
        out_specs=[VMEM] * (outer_count - 1),
        out_shape=[jax.ShapeDtypeStruct(shape[1:], jnp.bfloat16)] * (outer_count - 1),
        scratch_shapes=[
            pltpu.VMEM((count, *shape), jnp.bfloat16),
            pltpu.SemaphoreType.DMA((count,)),
        ],
        compiler_params=pltpu.CompilerParams(vmem_limit_bytes=32 * MIB),
    )(place, *slots)


def scan_kernel(count, place_ref, *refs):
    slots, refs = refs[:count], refs[count:]
    outs, held, scanned, sems = refs[-count - 3 : -3], *refs[-3:]
    others = refs[: -count - 3]
    outer_count = len(others) + 1
    outer, inner = place_ref[0], place_ref[1]
    fetch(slots, held, sems, inner)
    before = jnp.zeros(held.shape[2:], jnp.float32)
    after = before
    for s, other in enumerate(others):
        term = other[...].astype(jnp.float32)
        lower = outer >= s + 1
        before += jnp.where(lower, term, 0.0)
        after += jnp.where(lower, 0.0, term)
    for i in range(count):
        scanned[i, 0] = before.astype(jnp.bfloat16)
        before += held[i, 0].astype(jnp.float32)
    for i in reversed(range(count)):
        scanned[i, 1] = after.astype(jnp.bfloat16)
        after += held[i, 1].astype(jnp.float32)
    for s, out in enumerate(outs):
        out[...] = scanned[inner ^ s]


def scan_states(place, slots, others):
    count, slot = len(slots), jax.ShapeDtypeStruct(slots[0].shape, jnp.bfloat16)
    held = pltpu.VMEM((count, *slot.shape), jnp.bfloat16)
    return pl.pallas_call(
        functools.partial(scan_kernel, count),
        in_specs=[SMEM] + [ANY] * count + [VMEM] * len(others),
        out_specs=[VMEM] * count,
        out_shape=[slot] * count,
        scratch_shapes=[held, held, pltpu.SemaphoreType.DMA((count,))],
        compiler_params=pltpu.CompilerParams(vmem_limit_bytes=32 * MIB),
    )(place, *slots, *others)


def finish_kernel(scale, count, place_ref, q_ref, k_ref, v_ref, d_ref, *refs):
    slots, (att_ref, gq_ref, gk_ref, gv_ref, held, sems) = refs[:count], refs[count:]
    rows, width = q_ref.shape
    depth = held.shape[2]
    step = pl.program_id(0)

    @pl.when(step == 0)
    def _():
        fetch(slots, held, sems, place_ref[1])

    at = lax.broadcasted_iota(jnp.int32, (rows, rows), 0)
    to = lax.broadcasted_iota(jnp.int32, (rows, rows), 1)
    lower, upper = at >= to, at <= to

    def state(which, h):
        row = (step * (width // HEAD) + h) * HEAD
        if depth >= HEAD:
            return held[row // depth, which, pl.ds(pl.multiple_of(row % depth, HEAD), HEAD)]
        parts = range(HEAD // depth)
        return jnp.concatenate([held[row // depth + p, which] for p in parts], axis=0)

    def masked(mask, a, b):
        return jnp.where(mask, dot(a, b, 1, 1), 0.0).astype(jnp.bfloat16)

    for h in range(width // HEAD):
        cols = slice(h * HEAD, (h + 1) * HEAD)
        q, k, v, d = (ref[:, cols] for ref in (q_ref, k_ref, v_ref, d_ref))
        s, g = state(0, h), state(1, h)
        a, a_t = masked(lower, q, k), masked(upper, k, q)
        b, b_t = masked(lower, d, v), masked(upper, v, d)
        att = dot(q, s, 1, 0) + dot(a, v, 1, 0)
        gq = dot(d, s, 1, 1) + dot(b, k, 1, 0)
        gk = dot(v, g, 1, 1) + dot(b_t, q, 1, 0)
        gv = dot(k, g, 1, 0) + dot(a_t, d, 1, 0)
        att_ref[:, cols] = (scale * att).astype(jnp.bfloat16)
        gq_ref[:, cols] = (scale * gq).astype(jnp.bfloat16)
        gk_ref[:, cols] = (scale * gk).astype(jnp.bfloat16)
        gv_ref[:, cols] = (scale * gv).astype(jnp.bfloat16)


def finish(place, queries, keys, values, cotangent, slots, scale):
    rows, width = queries.shape
    count = len(slots)
    tokens = pl.BlockSpec((rows, GROUP * HEAD), lambda g: (0, g))
    out = jax.ShapeDtypeStruct((rows, width), jnp.bfloat16)
    return pl.pallas_call(
        functools.partial(finish_kernel, scale, count),
        grid=(width // (HEAD * GROUP),),
        in_specs=[SMEM] + [tokens] * 4 + [ANY] * count,
        out_specs=[tokens] * 4,
        out_shape=[out] * 4,
        scratch_shapes=[
            pltpu.VMEM((count, *slots[0].shape), jnp.bfloat16),
            pltpu.SemaphoreType.DMA((count,)),
        ],
        cost_estimate=pl.CostEstimate(
            flops=24 * rows * width * HEAD, bytes_accessed=20 * rows * width, transcendentals=0
        ),
        compiler_params=pltpu.CompilerParams(vmem_limit_bytes=32 * MIB),
    )(place, queries, keys, values, cotangent, *slots)


def swap(slots):
    count = len(slots)
    return [slots[0]] + [
        lax.ppermute(slots[s], "inner", [(i, i ^ s) for i in range(count)])
        for s in range(1, count)
    ]


def body(queries, keys, values, cotangent):
    rows = queries.shape[0]
    count = lax.axis_size("inner")
    outer_count = lax.axis_size("outer")
    scale = float(HEAD * rows * count * outer_count) ** (-0.5)
    place = jnp.stack([lax.axis_index("outer"), lax.axis_index("inner")]).astype(jnp.int32)
    slots = swap(own_states(place, queries, keys, values, cotangent, count))
    sends = totals(place, slots, outer_count)
    others = [
        lax.ppermute(send, "outer", [(z, (z + s + 1) % outer_count) for z in range(outer_count)])
        for s, send in enumerate(sends)
    ]
    slots = swap(scan_states(place, slots, others))
    return tuple(finish(place, queries, keys, values, cotangent, slots, scale))


def solution(mesh):
    spec = P(("outer", "inner"), None)
    return jax.shard_map(
        body, mesh=mesh, in_specs=(spec,) * 4, out_specs=(spec,) * 4, check_vma=False
    )
```

time: 94.8 us -> 60 us (0.63)
  blocking collectives: 39.3 us -> 0 us
  starting transfers between devices: 0.04 us -> 22.4 us
  between operations: 14.1 us -> 0.72 us
  Pallas kernels: 7.22 us -> 15.5 us
  waiting for transfers between devices: 27.5 us -> 19.7 us
  local copies, waits for them, and re-layouts: 5.41 us -> 0.92 us
    all_to_all x2 -> x0, blocking collectives: 39.3 us -> none  [the longest x1 20.3 us: body(): lax.all_to_all(own, 'inner', split_axis=0, concat_axis=0, tiled=True)]
    all_gather x1 -> x0, waiting for transfers between devices: 27.5 us -> none  [body(): groups = lax.all_gather(total, 'outer')]
    ppermute x0 -> x17, starting transfers between devices: none -> 22.4 us  [the longest x14 16.5 us: swap(): lax.ppermute(slots[s], 'inner', [(i, i ^ s) for i in range(count)])]
    ppermute x0 -> x17, waiting for transfers between devices: none -> 19.7 us  [the longest x14 15.8 us: swap(): lax.ppermute(slots[s], 'inner', [(i, i ^ s) for i in range(count)])]
    pallas_call x3 -> x4, Pallas kernels: 7.22 us -> 15.5 us  [the longest x1 7.78 us: finish(): pl.pallas_call(functools.partial(finish_kernel, scale, count), grid=(widt...]
    unnamed x18 -> x12, local copies, waits for them, and re-layouts: 5.41 us -> 0.92 us
  transfers between devices with their start and end apart: 1 -> 17, of which waited for: 1 -> 9; matrix products, arithmetic and copies ran while one was open for 0% -> 0% of each run, Pallas kernels for 0% -> 0%
where the time goes in v2:
time: 60 us; the launch traced here: 59.8 us
  starting transfers between devices  22.4 us (37%)
  waiting for transfers between devices  19.7 us (33%)
  Pallas kernels  15.5 us (26%)
  local copies, waits for them, and re-layouts  0.92 us (2%)
  between operations  0.72 us (1%)
  other arithmetic  0.65 us (1%)
    ppermute x14, starting transfers between devices, swap(): lax.ppermute(slots[s], 'inner', [(i, i ^ s) for i in range(count)])  16.5 us
    ppermute x14, waiting for transfers between devices, swap(): lax.ppermute(slots[s], 'inner', [(i, i ^ s) for i in range(count)])  15.8 us
    pallas_call x1, Pallas kernels, finish(): pl.pallas_call(functools.partial(finish_kernel, scale, count), grid=(widt...  7.78 us
    ppermute x3, starting transfers between devices, body(): lax.ppermute(send, 'outer', [(z, (z + s + 1) % outer_count) for z in rang...  5.83 us
    ppermute x3, waiting for transfers between devices, body(): lax.ppermute(send, 'outer', [(z, (z + s + 1) % outer_count) for z in rang...  3.89 us
    pallas_call x1, Pallas kernels, own_states(): pl.pallas_call(own_states_kernel, in_specs=[SMEM] + [VMEM] * 4, out_specs...  3.14 us
    pallas_call x1, Pallas kernels, scan_states(): pl.pallas_call(functools.partial(scan_kernel, count), in_specs=[SMEM] + [...  2.39 us
    pallas_call x1, Pallas kernels, totals(): pl.pallas_call(functools.partial(totals_kernel, count, outer_count), in_s...  2.16 us
  transfers between devices with their start and end apart: 17, of which 9 were waited for; matrix products, arithmetic and copies ran while one was open for 0% of the time, Pallas kernels for 0%

profile of v2, /device:TPU:0, one launch (start us, length us, event | category | flops | bytes accessed | tf_op | source)
XLA Modules:
  0.0 59.8 jit_solution(12425517386423379194)
XLA Ops:
  0.6 0.6 %pad_add_fusion.place_ref = s32[2]{0:T(128)} fusion(s32[1]{0:T(128)} %bitcast.1, s32[1]{0:T(128)} %bitcast), kind=kLoop, calls=%fused_computation | loop fusion | flops 2 | bytes 16 | tf_op jit(solution)/shard_map/stack | solution.py:225
  1.3 3.1 %shard_map.75 = (bf16[2,256,128]{2,1,0:T(8,128)(2,1)}, bf16[2,256,128]{2,1,0:T(8,128)(2,1)}, bf16[2,256,128]{2,1,0:T(8,128)(2,1)}, bf16[2,256,128]{2,1,0:T(8,128...) custom-call(s32[2]{0:T(128)} %pad_add_fusion.place_ref, ...), custom_call_target="tpu_custom_call" | custom-call | flops 134217728 | bytes 3145728 | tf_op jit(solution)/shard_map/pallas_call | solution.py:52
  4.4 0.5 collective-permute-start
  4.9 2.5 %collective-permute-start.1 = (bf16[2,256,128]{2,1,0:T(8,128)(2,1)}, bf16[2,256,128]{2,1,0:T(8,128)(2,1)S(1)}, u32[]{:S(2)}, u32[]{:S(2)}) collective-permute-start(bf16[2,256,128]{2,1,0:T(8,128)(2,1)} %get-tuple-element.25), channel_id=1, source_target_pairs={{0,2},{1,3},{2,0},{3,1},{4,6},{5,7},{6,4},{7,5},{8,10},{9,11},{10,... | collective-permute-start | bytes 393224 | tf_op jit(solution)/shard_map/ppermute | solution.py:215
  7.5 1.7 %collective-permute-start.3 = (bf16[2,256,128]{2,1,0:T(8,128)(2,1)}, bf16[2,256,128]{2,1,0:T(8,128)(2,1)S(1)}, u32[]{:S(2)}, u32[]{:S(2)}) collective-permute-start(bf16[2,256,128]{2,1,0:T(8,128)(2,1)} %get-tuple-element.27), channel_id=1, source_target_pairs={{0,4},{1,5},{2,6},{3,7},{4,0},{5,1},{6,2},{7,3},{8,12},{9,13},{10,... | collective-permute-start | bytes 393224 | tf_op jit(solution)/shard_map/ppermute | solution.py:215
  9.3 2.6 %collective-permute-start.5 = (bf16[2,256,128]{2,1,0:T(8,128)(2,1)}, bf16[2,256,128]{2,1,0:T(8,128)(2,1)S(1)}, u32[]{:S(2)}, u32[]{:S(2)}) collective-permute-start(bf16[2,256,128]{2,1,0:T(8,128)(2,1)} %get-tuple-element.29), channel_id=1, source_target_pairs={{0,6},{1,7},{2,4},{3,5},{4,2},{5,3},{6,0},{7,1},{8,14},{9,15},{10,... | collective-permute-start | bytes 393224 | tf_op jit(solution)/shard_map/ppermute | solution.py:215
  12.0 1.7 %collective-permute-start.6 = (bf16[2,256,128]{2,1,0:T(8,128)(2,1)}, bf16[2,256,128]{2,1,0:T(8,128)(2,1)S(1)}, u32[]{:S(2)}, u32[]{:S(2)}) collective-permute-start(bf16[2,256,128]{2,1,0:T(8,128)(2,1)} %get-tuple-element.30), channel_id=1, source_target_pairs={{0,7},{1,6},{2,5},{3,4},{4,3},{5,2},{6,1},{7,0},{8,15},{9,14},{10,... | collective-permute-start | bytes 393224 | tf_op jit(solution)/shard_map/ppermute | solution.py:215
  13.7 0.6 %collective-permute-done.2.refs_3_ = bf16[2,256,128]{2,1,0:T(8,128)(2,1)S(1)} collective-permute-done((bf16[2,256,128]{2,1,0:T(8,128)(2,1)}, bf16[2,256,128]{2,1,0:T(8,128)(2,1)S(1)}, u32[]{:S(2)}, u32[]{:S(2)}) %collective-permute-start.2) | collective-permute-done | bytes 131104 | tf_op jit(solution)/shard_map/ppermute | solution.py:215
  14.4 6.9 %collective-permute-done.4.refs_5_ = bf16[2,256,128]{2,1,0:T(8,128)(2,1)S(1)} collective-permute-done((bf16[2,256,128]{2,1,0:T(8,128)(2,1)}, bf16[2,256,128]{2,1,0:T(8,128)(2,1)S(1)}, u32[]{:S(2)}, u32[]{:S(2)}) %collective-permute-start.4) | collective-permute-done | bytes 131104 | tf_op jit(solution)/shard_map/ppermute | solution.py:215
  21.3 0.9 %copy-done.4 = bf16[2,256,128]{2,1,0:T(8,128)(2,1)S(1)} copy-done((bf16[2,256,128]{2,1,0:T(8,128)(2,1)S(1)}, bf16[2,256,128]{2,1,0:T(8,128)(2,1)}, u32[]{:S(2)}) %copy-start.4) | copy-done | bytes 131096
  22.2 2.2 %shard_map.76 = (bf16[256,128]{1,0:T(8,128)(2,1)S(1)}, bf16[256,128]{1,0:T(8,128)(2,1)S(1)}, bf16[256,128]{1,0:T(8,128)(2,1)S(1)}) custom-call(s32[2]{0:T(128)S(1)} %copy-done.5, bf16[2,256,128]{2,1,0:T(8,128)(2,1)S(1)} %copy-done.4, bf16[2,256,128]{2,1,0:T(8,128)(2,1)S(1)} %collective-permute-done.refs_1_, ...), custom_call_target="tpu_custom_call" | custom-call | tf_op jit(solution)/shard_map/pallas_call | solution.py:100
  24.3 1.9 %collective-permute-start.7 = (bf16[256,128]{1,0:T(8,128)(2,1)S(1)}, bf16[256,128]{1,0:T(8,128)(2,1)S(1)}, u32[]{:S(2)}, u32[]{:S(2)}) collective-permute-start(bf16[256,128]{1,0:T(8,128)(2,1)S(1)} %get-tuple-element.31), channel_id=1, source_target_pairs={{0,8},{8,16},{16,24},{24,0},{1,9},{9,17},{17,25},{25,1},{2,10},{10... | collective-permute-start | bytes 196616 | tf_op jit(solution)/shard_map/ppermute | solution.py:229
  26.2 2.6 %collective-permute-start.8 = (bf16[256,128]{1,0:T(8,128)(2,1)S(1)}, bf16[256,128]{1,0:T(8,128)(2,1)S(1)}, u32[]{:S(2)}, u32[]{:S(2)}) collective-permute-start(bf16[256,128]{1,0:T(8,128)(2,1)S(1)} %get-tuple-element.32), channel_id=1, source_target_pairs={{0,16},{8,24},{16,0},{24,8},{1,17},{9,25},{17,1},{25,9},{2,18},{10... | collective-permute-start | bytes 196616 | tf_op jit(solution)/shard_map/ppermute | solution.py:229
  28.8 1.4 %collective-permute-start.9 = (bf16[256,128]{1,0:T(8,128)(2,1)S(1)}, bf16[256,128]{1,0:T(8,128)(2,1)S(1)}, u32[]{:S(2)}, u32[]{:S(2)}) collective-permute-start(bf16[256,128]{1,0:T(8,128)(2,1)S(1)} %get-tuple-element.33), channel_id=1, source_target_pairs={{0,24},{8,0},{16,8},{24,16},{1,25},{9,1},{17,9},{25,17},{2,26},{10... | collective-permute-start | bytes 196616 | tf_op jit(solution)/shard_map/ppermute | solution.py:229
  30.2 0.8 %collective-permute-done.7.refs_8_ = bf16[256,128]{1,0:T(8,128)(2,1)S(1)} collective-permute-done((bf16[256,128]{1,0:T(8,128)(2,1)S(1)}, bf16[256,128]{1,0:T(8,128)(2,1)S(1)}, u32[]{:S(2)}, u32[]{:S(2)}) %collective-permute-start.7) | collective-permute-done | bytes 65568 | tf_op jit(solution)/shard_map/ppermute | solution.py:229
  31.0 2.8 %collective-permute-done.8.refs_9_ = bf16[256,128]{1,0:T(8,128)(2,1)S(1)} collective-permute-done((bf16[256,128]{1,0:T(8,128)(2,1)S(1)}, bf16[256,128]{1,0:T(8,128)(2,1)S(1)}, u32[]{:S(2)}, u32[]{:S(2)}) %collective-permute-start.8) | collective-permute-done | bytes 65568 | tf_op jit(solution)/shard_map/ppermute | solution.py:229
  34.1 2.4 %shard_map.77 = (bf16[2,256,128]{2,1,0:T(8,128)(2,1)S(1)}, bf16[2,256,128]{2,1,0:T(8,128)(2,1)S(1)}, bf16[2,256,128]{2,1,0:T(8,128)(2,1)S(1)}, bf16[2,256,128]{2...) custom-call(s32[2]{0:T(128)S(1)} %copy-done.5, ...), custom_call_target="tpu_custom_call" | custom-call | tf_op jit(solution)/shard_map/pallas_call | solution.py:140
  36.5 1.6 %collective-permute-start.11 = (bf16[2,256,128]{2,1,0:T(8,128)(2,1)S(1)}, bf16[2,256,128]{2,1,0:T(8,128)(2,1)S(1)}, u32[]{:S(2)}, u32[]{:S(2)}) collective-permute-start(bf16[2,256,128]{2,1,0:T(8,128)(2,1)S(1)} %get-tuple-element.36), channel_id=1, source_target_pairs={{0,2},{1,3},{2,0},{3,1},{4,6},{5,7},{6,4},{7,5},{8,10},{9,11},{10,... | collective-permute-start | bytes 393224 | tf_op jit(solution)/shard_map/ppermute | solution.py:215
  38.4 1.5 %collective-permute-start.13 = (bf16[2,256,128]{2,1,0:T(8,128)(2,1)S(1)}, bf16[2,256,128]{2,1,0:T(8,128)(2,1)S(1)}, u32[]{:S(2)}, u32[]{:S(2)}) collective-permute-start(bf16[2,256,128]{2,1,0:T(8,128)(2,1)S(1)} %get-tuple-element.38), channel_id=1, source_target_pairs={{0,4},{1,5},{2,6},{3,7},{4,0},{5,1},{6,2},{7,3},{8,12},{9,13},{10,... | collective-permute-start | bytes 393224 | tf_op jit(solution)/shard_map/ppermute | solution.py:215
  40.1 2.5 %collective-permute-start.15 = (bf16[2,256,128]{2,1,0:T(8,128)(2,1)S(1)}, bf16[2,256,128]{2,1,0:T(8,128)(2,1)S(1)}, u32[]{:S(2)}, u32[]{:S(2)}) collective-permute-start(bf16[2,256,128]{2,1,0:T(8,128)(2,1)S(1)} %get-tuple-element.40), channel_id=1, source_target_pairs={{0,6},{1,7},{2,4},{3,5},{4,2},{5,3},{6,0},{7,1},{8,14},{9,15},{10,... | collective-permute-start | bytes 393224 | tf_op jit(solution)/shard_map/ppermute | solution.py:215
  42.9 1.3 %collective-permute-start.16 = (bf16[2,256,128]{2,1,0:T(8,128)(2,1)S(1)}, bf16[2,256,128]{2,1,0:T(8,128)(2,1)S(1)}, u32[]{:S(2)}, u32[]{:S(2)}) collective-permute-start(bf16[2,256,128]{2,1,0:T(8,128)(2,1)S(1)} %get-tuple-element.41), channel_id=1, source_target_pairs={{0,7},{1,6},{2,5},{3,4},{4,3},{5,2},{6,1},{7,0},{8,15},{9,14},{10,... | collective-permute-start | bytes 393224 | tf_op jit(solution)/shard_map/ppermute | solution.py:215
  44.2 0.6 %collective-permute-done.12.refs_3_ = bf16[2,256,128]{2,1,0:T(8,128)(2,1)S(1)} collective-permute-done((bf16[2,256,128]{2,1,0:T(8,128)(2,1)S(1)}, bf16[2,256,128]{2,1,0:T(8,128)(2,1)S(1)}, u32[]{:S(2)}, u32[]{:S(2)}) %collective-permute-start.12) | collective-permute-done | bytes 131104 | tf_op jit(solution)/shard_map/ppermute | solution.py:215
  44.8 7.2 %collective-permute-done.14.refs_5_ = bf16[2,256,128]{2,1,0:T(8,128)(2,1)S(1)} collective-permute-done((bf16[2,256,128]{2,1,0:T(8,128)(2,1)S(1)}, bf16[2,256,128]{2,1,0:T(8,128)(2,1)S(1)}, u32[]{:S(2)}, u32[]{:S(2)}) %collective-permute-start.14) | collective-permute-done | bytes 131104 | tf_op jit(solution)/shard_map/ppermute | solution.py:215
  52.0 7.8 %shard_map.78 = (bf16[128,2048]{1,0:T(8,128)(2,1)}, bf16[128,2048]{1,0:T(8,128)(2,1)}, bf16[128,2048]{1,0:T(8,128)(2,1)}, bf16[128,2048]{1,0:T(8,128)(2,1)}) custom-call(s32[2]{0:T(128)S(1)} %copy-done.5, bf16[128,2048]{1,0:T(8,128)(2,1)S(1)} %copy-done, bf16[128,2048]{1,0:T(8,128)(2,1)S(1)} %copy-done.1, bf16[128,2048]{1,0:T(8,128)(2,1)S(1)} %copy-done.2, ...), custom_call_target="tpu_custom_call" | custom-call | flops 805306368 | bytes 5242880 | tf_op jit(solution)/shard_map/pallas_call | solution.py:195
  (27 shorter events, 1.4 us)
Async XLA Ops:
  4.4 4.8 %collective-permute-start = (bf16[2,256,128]{2,1,0:T(8,128)(2,1)}, bf16[2,256,128]{2,1,0:T(8,128)(2,1)S(1)}, u32[]{:S(2)}, u32[]{:S(2)}) collective-permute-start(bf16[2,256,128]{2,1,0:T(8,128)(2,1)} %get-tuple-element.24), channel_id=1, source_target_pairs={{0,1},{1,0},{2,3},{3,2},{4,5},{5,4},{6,7},{7,6},{8,9},{9,8},{10,11... | collective-permute-start | bytes 393224 | tf_op jit(solution)/shard_map/ppermute | solution.py:215
  4.9 7.1 %collective-permute-start.1 = (bf16[2,256,128]{2,1,0:T(8,128)(2,1)}, bf16[2,256,128]{2,1,0:T(8,128)(2,1)S(1)}, u32[]{:S(2)}, u32[]{:S(2)}) collective-permute-start(bf16[2,256,128]{2,1,0:T(8,128)(2,1)} %get-tuple-element.25), channel_id=1, source_target_pairs={{0,2},{1,3},{2,0},{3,1},{4,6},{5,7},{6,4},{7,5},{8,10},{9,11},{10,... | collective-permute-start | bytes 393224 | tf_op jit(solution)/shard_map/ppermute | solution.py:215
  7.4 6.9 %collective-permute-start.2 = (bf16[2,256,128]{2,1,0:T(8,128)(2,1)}, bf16[2,256,128]{2,1,0:T(8,128)(2,1)S(1)}, u32[]{:S(2)}, u32[]{:S(2)}) collective-permute-start(bf16[2,256,128]{2,1,0:T(8,128)(2,1)} %get-tuple-element.26), channel_id=1, source_target_pairs={{0,3},{1,2},{2,1},{3,0},{4,7},{5,6},{6,5},{7,4},{8,11},{9,10},{10,... | collective-permute-start | bytes 393224 | tf_op jit(solution)/shard_map/ppermute | solution.py:215
  7.5 6.8 %collective-permute-start.3 = (bf16[2,256,128]{2,1,0:T(8,128)(2,1)}, bf16[2,256,128]{2,1,0:T(8,128)(2,1)S(1)}, u32[]{:S(2)}, u32[]{:S(2)}) collective-permute-start(bf16[2,256,128]{2,1,0:T(8,128)(2,1)} %get-tuple-element.27), channel_id=1, source_target_pairs={{0,4},{1,5},{2,6},{3,7},{4,0},{5,1},{6,2},{7,3},{8,12},{9,13},{10,... | collective-permute-start | bytes 393224 | tf_op jit(solution)/shard_map/ppermute | solution.py:215
  9.3 12.0 %collective-permute-start.4 = (bf16[2,256,128]{2,1,0:T(8,128)(2,1)}, bf16[2,256,128]{2,1,0:T(8,128)(2,1)S(1)}, u32[]{:S(2)}, u32[]{:S(2)}) collective-permute-start(bf16[2,256,128]{2,1,0:T(8,128)(2,1)} %get-tuple-element.28), channel_id=1, source_target_pairs={{0,5},{1,4},{2,7},{3,6},{4,1},{5,0},{6,3},{7,2},{8,13},{9,12},{10,... | collective-permute-start | bytes 393224 | tf_op jit(solution)/shard_map/ppermute | solution.py:215
  9.3 12.0 %collective-permute-start.5 = (bf16[2,256,128]{2,1,0:T(8,128)(2,1)}, bf16[2,256,128]{2,1,0:T(8,128)(2,1)S(1)}, u32[]{:S(2)}, u32[]{:S(2)}) collective-permute-start(bf16[2,256,128]{2,1,0:T(8,128)(2,1)} %get-tuple-element.29), channel_id=1, source_target_pairs={{0,6},{1,7},{2,4},{3,5},{4,2},{5,3},{6,0},{7,1},{8,14},{9,15},{10,... | collective-permute-start | bytes 393224 | tf_op jit(solution)/shard_map/ppermute | solution.py:215
  12.0 9.3 %copy-start.5 = (s32[2]{0:T(128)S(1)}, s32[2]{0:T(128)}, u32[]{:S(2)}) copy-start(s32[2]{0:T(128)} %pad_add_fusion.place_ref) | copy-start | bytes 28
  12.0 9.3 %collective-permute-start.6 = (bf16[2,256,128]{2,1,0:T(8,128)(2,1)}, bf16[2,256,128]{2,1,0:T(8,128)(2,1)S(1)}, u32[]{:S(2)}, u32[]{:S(2)}) collective-permute-start(bf16[2,256,128]{2,1,0:T(8,128)(2,1)} %get-tuple-element.30), channel_id=1, source_target_pairs={{0,7},{1,6},{2,5},{3,4},{4,3},{5,2},{6,1},{7,0},{8,15},{9,14},{10,... | collective-permute-start | bytes 393224 | tf_op jit(solution)/shard_map/ppermute | solution.py:215
  21.3 0.9 %copy-start.4 = (bf16[2,256,128]{2,1,0:T(8,128)(2,1)S(1)}, bf16[2,256,128]{2,1,0:T(8,128)(2,1)}, u32[]{:S(2)}) copy-start(bf16[2,256,128]{2,1,0:T(8,128)(2,1)} %get-tuple-element.23.refs_0_) | copy-start | bytes 393220
  22.2 29.8 %copy-start.2 = (bf16[128,2048]{1,0:T(8,128)(2,1)S(1)}, bf16[128,2048]{1,0:T(8,128)(2,1)}, u32[]{:S(2)}) copy-start(bf16[128,2048]{1,0:T(8,128)(2,1)} %v_ref.3) | copy-start | bytes 1572868
  22.2 29.9 %copy-start.3 = (bf16[128,2048]{1,0:T(8,128)(2,1)S(1)}, bf16[128,2048]{1,0:T(8,128)(2,1)}, u32[]{:S(2)}) copy-start(bf16[128,2048]{1,0:T(8,128)(2,1)} %d_ref.3) | copy-start | bytes 1572868
  24.3 6.7 %collective-permute-start.7 = (bf16[256,128]{1,0:T(8,128)(2,1)S(1)}, bf16[256,128]{1,0:T(8,128)(2,1)S(1)}, u32[]{:S(2)}, u32[]{:S(2)}) collective-permute-start(bf16[256,128]{1,0:T(8,128)(2,1)S(1)} %get-tuple-element.31), channel_id=1, source_target_pairs={{0,8},{8,16},{16,24},{24,0},{1,9},{9,17},{17,25},{25,1},{2,10},{10... | collective-permute-start | bytes 196616 | tf_op jit(solution)/shard_map/ppermute | solution.py:229
  26.2 7.6 %collective-permute-start.8 = (bf16[256,128]{1,0:T(8,128)(2,1)S(1)}, bf16[256,128]{1,0:T(8,128)(2,1)S(1)}, u32[]{:S(2)}, u32[]{:S(2)}) collective-permute-start(bf16[256,128]{1,0:T(8,128)(2,1)S(1)} %get-tuple-element.32), channel_id=1, source_target_pairs={{0,16},{8,24},{16,0},{24,8},{1,17},{9,25},{17,1},{25,9},{2,18},{10... | collective-permute-start | bytes 196616 | tf_op jit(solution)/shard_map/ppermute | solution.py:229
  28.8 23.2 %copy-start = (bf16[128,2048]{1,0:T(8,128)(2,1)S(1)}, bf16[128,2048]{1,0:T(8,128)(2,1)}, u32[]{:S(2)}) copy-start(bf16[128,2048]{1,0:T(8,128)(2,1)} %q_ref.3) | copy-start | bytes 1572868
  28.8 23.2 %copy-start.1 = (bf16[128,2048]{1,0:T(8,128)(2,1)S(1)}, bf16[128,2048]{1,0:T(8,128)(2,1)}, u32[]{:S(2)}) copy-start(bf16[128,2048]{1,0:T(8,128)(2,1)} %k_ref.3) | copy-start | bytes 1572868
  28.8 5.3 %collective-permute-start.9 = (bf16[256,128]{1,0:T(8,128)(2,1)S(1)}, bf16[256,128]{1,0:T(8,128)(2,1)S(1)}, u32[]{:S(2)}, u32[]{:S(2)}) collective-permute-start(bf16[256,128]{1,0:T(8,128)(2,1)S(1)} %get-tuple-element.33), channel_id=1, source_target_pairs={{0,24},{8,0},{16,8},{24,16},{1,25},{9,1},{17,9},{25,17},{2,26},{10... | collective-permute-start | bytes 196616 | tf_op jit(solution)/shard_map/ppermute | solution.py:229
  36.5 3.6 %collective-permute-start.10 = (bf16[2,256,128]{2,1,0:T(8,128)(2,1)S(1)}, bf16[2,256,128]{2,1,0:T(8,128)(2,1)S(1)}, u32[]{:S(2)}, u32[]{:S(2)}) collective-permute-start(bf16[2,256,128]{2,1,0:T(8,128)(2,1)S(1)} %get-tuple-element.35), channel_id=1, source_target_pairs={{0,1},{1,0},{2,3},{3,2},{4,5},{5,4},{6,7},{7,6},{8,9},{9,8},{10,11... | collective-permute-start | bytes 393224 | tf_op jit(solution)/shard_map/ppermute | solution.py:215
  36.5 6.4 %collective-permute-start.11 = (bf16[2,256,128]{2,1,0:T(8,128)(2,1)S(1)}, bf16[2,256,128]{2,1,0:T(8,128)(2,1)S(1)}, u32[]{:S(2)}, u32[]{:S(2)}) collective-permute-start(bf16[2,256,128]{2,1,0:T(8,128)(2,1)S(1)} %get-tuple-element.36), channel_id=1, source_target_pairs={{0,2},{1,3},{2,0},{3,1},{4,6},{5,7},{6,4},{7,5},{8,10},{9,11},{10,... | collective-permute-start | bytes 393224 | tf_op jit(solution)/shard_map/ppermute | solution.py:215
  38.1 6.7 %collective-permute-start.12 = (bf16[2,256,128]{2,1,0:T(8,128)(2,1)S(1)}, bf16[2,256,128]{2,1,0:T(8,128)(2,1)S(1)}, u32[]{:S(2)}, u32[]{:S(2)}) collective-permute-start(bf16[2,256,128]{2,1,0:T(8,128)(2,1)S(1)} %get-tuple-element.37), channel_id=1, source_target_pairs={{0,3},{1,2},{2,1},{3,0},{4,7},{5,6},{6,5},{7,4},{8,11},{9,10},{10,... | collective-permute-start | bytes 393224 | tf_op jit(solution)/shard_map/ppermute | solution.py:215
  38.4 6.4 %collective-permute-start.13 = (bf16[2,256,128]{2,1,0:T(8,128)(2,1)S(1)}, bf16[2,256,128]{2,1,0:T(8,128)(2,1)S(1)}, u32[]{:S(2)}, u32[]{:S(2)}) collective-permute-start(bf16[2,256,128]{2,1,0:T(8,128)(2,1)S(1)} %get-tuple-element.38), channel_id=1, source_target_pairs={{0,4},{1,5},{2,6},{3,7},{4,0},{5,1},{6,2},{7,3},{8,12},{9,13},{10,... | collective-permute-start | bytes 393224 | tf_op jit(solution)/shard_map/ppermute | solution.py:215
  39.9 12.1 %collective-permute-start.14 = (bf16[2,256,128]{2,1,0:T(8,128)(2,1)S(1)}, bf16[2,256,128]{2,1,0:T(8,128)(2,1)S(1)}, u32[]{:S(2)}, u32[]{:S(2)}) collective-permute-start(bf16[2,256,128]{2,1,0:T(8,128)(2,1)S(1)} %get-tuple-element.39), channel_id=1, source_target_pairs={{0,5},{1,4},{2,7},{3,6},{4,1},{5,0},{6,3},{7,2},{8,13},{9,12},{10,... | collective-permute-start | bytes 393224 | tf_op jit(solution)/shard_map/ppermute | solution.py:215
  40.1 11.9 %collective-permute-start.15 = (bf16[2,256,128]{2,1,0:T(8,128)(2,1)S(1)}, bf16[2,256,128]{2,1,0:T(8,128)(2,1)S(1)}, u32[]{:S(2)}, u32[]{:S(2)}) collective-permute-start(bf16[2,256,128]{2,1,0:T(8,128)(2,1)S(1)} %get-tuple-element.40), channel_id=1, source_target_pairs={{0,6},{1,7},{2,4},{3,5},{4,2},{5,3},{6,0},{7,1},{8,14},{9,15},{10,... | collective-permute-start | bytes 393224 | tf_op jit(solution)/shard_map/ppermute | solution.py:215
  42.9 9.1 %collective-permute-start.16 = (bf16[2,256,128]{2,1,0:T(8,128)(2,1)S(1)}, bf16[2,256,128]{2,1,0:T(8,128)(2,1)S(1)}, u32[]{:S(2)}, u32[]{:S(2)}) collective-permute-start(bf16[2,256,128]{2,1,0:T(8,128)(2,1)S(1)} %get-tuple-element.41), channel_id=1, source_target_pairs={{0,7},{1,6},{2,5},{3,4},{4,3},{5,2},{6,1},{7,0},{8,15},{9,14},{10,... | collective-permute-start | bytes 393224 | tf_op jit(solution)/shard_map/ppermute | solution.py:215

commit v3 on v1

v3 whole, which is shorter than its diff:
```python
import functools

import jax
import jax.numpy as jnp
from jax import lax
from jax.experimental import pallas as pl
from jax.experimental.pallas import tpu as pltpu
from jax.sharding import PartitionSpec as P

HEAD = 128
GROUP = 4
PIECES = 2
MIB = 1024 * 1024
ANY = pl.BlockSpec(memory_space=pl.ANY)
HBM = pl.BlockSpec(memory_space=pltpu.HBM)
VMEM = pl.BlockSpec(memory_space=pltpu.VMEM)
BF16 = jnp.bfloat16
F32 = jnp.float32


def dot(a, b, over_a, over_b):
    return lax.dot_general(
        a, b, (((over_a,), (over_b,)), ((), ())), preferred_element_type=F32
    )


def near_far():
    inner = lax.axis_index("inner")
    return lax.rem(inner, 2), lax.div(inner, 2)


def states_kernel(other, *refs):
    tokens, (out, held, sems) = refs[:4], refs[4:]
    half = out.shape[1]
    piece = half // PIECES
    near, _ = near_far()
    side = 1 - near if other else near
    copies = [
        [
            pltpu.make_async_copy(
                ref.at[:, pl.ds(pl.multiple_of(side * half + p * piece, piece), piece)],
                held.at[i, :, pl.ds(p * piece, piece)],
                sems.at[i, p],
            )
            for i, ref in enumerate(tokens)
        ]
        for p in range(PIECES)
    ]
    for group in copies:
        for copy in group:
            copy.start()
    for p, group in enumerate(copies):
        for copy in group:
            copy.wait()
        for h in range(p * piece // HEAD, (p + 1) * piece // HEAD):
            cols = slice(h * HEAD, (h + 1) * HEAD)
            out[0, cols] = dot(held[1, :, cols], held[2, :, cols], 0, 0).astype(BF16)
            out[1, cols] = dot(held[0, :, cols], held[3, :, cols], 0, 0).astype(BF16)


def half_states(tokens, other):
    rows, width = tokens[0].shape
    half = width // 2
    return pl.pallas_call(
        functools.partial(states_kernel, other),
        in_specs=[HBM] * 4,
        out_specs=VMEM,
        out_shape=jax.ShapeDtypeStruct((2, half, HEAD), BF16),
        scratch_shapes=[
            pltpu.VMEM((4, rows, half), BF16),
            pltpu.SemaphoreType.DMA((4, PIECES)),
        ],
        cost_estimate=pl.CostEstimate(
            flops=4 * rows * half * HEAD, bytes_accessed=12 * rows * half, transcendentals=0
        ),
        compiler_params=pltpu.CompilerParams(vmem_limit_bytes=(60 if other else 16) * MIB),
    )(*tokens)


def pair_kernel(keep_ref, got_ref, *slots):
    depth = slots[0].shape[1]
    _, far = near_far()
    for s, slot in enumerate(slots):
        part = pl.ds(pl.multiple_of((far ^ s) * depth, depth), depth)
        for which in range(2):
            both = keep_ref[which, part].astype(F32) + got_ref[which, part].astype(F32)
            slot[which] = both.astype(BF16)


def pair_slots(keep, got, far_count):
    slot = jax.ShapeDtypeStruct((2, keep.shape[1] // far_count, HEAD), BF16)
    return pl.pallas_call(
        pair_kernel,
        in_specs=[VMEM] * 2,
        out_specs=[VMEM] * far_count,
        out_shape=[slot] * far_count,
        compiler_params=pltpu.CompilerParams(vmem_limit_bytes=32 * MIB),
    )(keep, got)


def totals_kernel(far_count, *refs):
    slots, sends = refs[:far_count], refs[far_count:]
    outer = lax.axis_index("outer")
    totals = []
    for which in range(2):
        total = slots[0][which].astype(F32)
        for slot in slots[1:]:
            total += slot[which].astype(F32)
        totals.append(total.astype(BF16))
    for s, send in enumerate(sends):
        upward = (outer ^ (s + 1)) > outer
        send[...] = jnp.where(upward, totals[0], totals[1])


def group_sends(slots, outer_count):
    send = jax.ShapeDtypeStruct(slots[0].shape[1:], BF16)
    return pl.pallas_call(
        functools.partial(totals_kernel, len(slots)),
        in_specs=[VMEM] * len(slots),
        out_specs=[VMEM] * (outer_count - 1),
        out_shape=[send] * (outer_count - 1),
        compiler_params=pltpu.CompilerParams(vmem_limit_bytes=32 * MIB),
    )(*slots)


def scan_kernel(far_count, *refs):
    slots, others, outs = refs[:far_count], refs[far_count:-far_count], refs[-far_count:]
    outer = lax.axis_index("outer")
    _, far = near_far()
    for which in range(2):
        base = jnp.zeros(slots[0].shape[1:], F32)
        for s, other in enumerate(others):
            below = (outer ^ (s + 1)) < outer
            wanted = below if which == 0 else jnp.logical_not(below)
            base += jnp.where(wanted, other[...].astype(F32), 0.0)
        terms = [slot[which].astype(F32) for slot in slots]
        for s, out in enumerate(outs):
            total = base
            for t, term in enumerate(terms):
                if s != t:
                    below = (far ^ t) < (far ^ s)
                    wanted = below if which == 0 else jnp.logical_not(below)
                    total += jnp.where(wanted, term, 0.0)
            out[which] = total.astype(BF16)


def scan_slots(slots, others):
    far_count, slot = len(slots), jax.ShapeDtypeStruct(slots[0].shape, BF16)
    return pl.pallas_call(
        functools.partial(scan_kernel, far_count),
        in_specs=[VMEM] * (far_count + len(others)),
        out_specs=[VMEM] * far_count,
        out_shape=[slot] * far_count,
        compiler_params=pltpu.CompilerParams(vmem_limit_bytes=32 * MIB),
    )(*slots, *others)


def expand_kernel(far_count, *refs):
    slots, (keep, got, mine, theirs) = refs[:far_count], refs[far_count:]
    depth = slots[0].shape[1]
    near, far = near_far()
    for s, slot in enumerate(slots):
        part = pl.ds(pl.multiple_of((far ^ s) * depth, depth), depth)
        for which in range(2):
            base = slot[which].astype(F32)
            for_me = near == 1 - which
            own, others = keep[which, part].astype(F32), got[which, part].astype(F32)
            mine[which, part] = (base + jnp.where(for_me, others, 0.0)).astype(BF16)
            theirs[which, part] = (base + jnp.where(for_me, 0.0, own)).astype(BF16)


def expand(slots, keep, got):
    state = jax.ShapeDtypeStruct(keep.shape, BF16)
    return pl.pallas_call(
        functools.partial(expand_kernel, len(slots)),
        in_specs=[VMEM] * (len(slots) + 2),
        out_specs=[VMEM] * 2,
        out_shape=[state] * 2,
        compiler_params=pltpu.CompilerParams(vmem_limit_bytes=32 * MIB),
    )(*slots, keep, got)


def local_kernel(q_ref, k_ref, v_ref, d_ref, att_ref, gq_ref, gk_ref, gv_ref):
    rows = q_ref.shape[0]
    at = lax.broadcasted_iota(jnp.int32, (rows, rows), 0)
    to = lax.broadcasted_iota(jnp.int32, (rows, rows), 1)
    lower, upper = at >= to, at <= to

    def masked(mask, a, b):
        return jnp.where(mask, dot(a, b, 1, 1), 0.0).astype(BF16)

    for h in range(q_ref.shape[1] // HEAD):
        cols = slice(h * HEAD, (h + 1) * HEAD)
        q, k, v, d = (ref[:, cols] for ref in (q_ref, k_ref, v_ref, d_ref))
        att_ref[:, cols] = dot(masked(lower, q, k), v, 1, 0)
        gq_ref[:, cols] = dot(masked(lower, d, v), k, 1, 0)
        gk_ref[:, cols] = dot(masked(upper, v, d), q, 1, 0)
        gv_ref[:, cols] = dot(masked(upper, k, q), d, 1, 0)


def local_part(tokens):
    rows, width = tokens[0].shape
    block = pl.BlockSpec((rows, GROUP * HEAD), lambda g: (0, g))
    return pl.pallas_call(
        local_kernel,
        grid=(width // (HEAD * GROUP),),
        in_specs=[block] * 4,
        out_specs=[block] * 4,
        out_shape=[jax.ShapeDtypeStruct((rows, width), F32)] * 4,
        cost_estimate=pl.CostEstimate(
            flops=16 * rows * width * HEAD, bytes_accessed=24 * rows * width, transcendentals=0
        ),
        compiler_params=pltpu.CompilerParams(vmem_limit_bytes=32 * MIB),
    )(*tokens)


def finish_kernel(scale, side_ref, *refs):
    tokens, local, states, outs = refs[:4], refs[4:8], refs[8], refs[-4:]
    for h in range(tokens[0].shape[1] // HEAD):
        cols = slice(h * HEAD, (h + 1) * HEAD)
        q, k, v, d = (ref[:, cols] for ref in tokens)
        s, g = states[0, cols], states[1, cols]
        parts = (dot(q, s, 1, 0), dot(d, s, 1, 1), dot(v, g, 1, 1), dot(k, g, 1, 0))
        for part, near, out in zip(parts, local, outs):
            out[:, cols] = (scale * (part + near[:, cols])).astype(BF16)


def finish(side, tokens, local, states, scale, before=()):
    rows, width = tokens[0].shape
    steps = width // 2 // (HEAD * GROUP)
    block = pl.BlockSpec((rows, GROUP * HEAD), lambda g, side: (0, side[0] * steps + g))
    out = jax.ShapeDtypeStruct((rows, width), BF16)
    return pl.pallas_call(
        functools.partial(finish_kernel, scale),
        grid_spec=pltpu.PrefetchScalarGridSpec(
            num_scalar_prefetch=1,
            grid=(steps,),
            in_specs=[block] * 8
            + [pl.BlockSpec((2, GROUP * HEAD, HEAD), lambda g, side: (0, g, 0))]
            + [ANY] * len(before),
            out_specs=[block] * 4,
        ),
        out_shape=[out] * 4,
        input_output_aliases={10 + i: i for i in range(len(before))},
        cost_estimate=pl.CostEstimate(
            flops=4 * rows * width * HEAD, bytes_accessed=17 * rows * width, transcendentals=0
        ),
        compiler_params=pltpu.CompilerParams(vmem_limit_bytes=32 * MIB),
    )(side, *tokens, *local, states, *before)


def swap(x, axis, bits):
    return lax.ppermute(x, axis, [(i, i ^ bits) for i in range(lax.axis_size(axis))])


def swap_far(slots):
    sent = {s: swap(slots[s], "inner", 2 * s) for s in reversed(range(1, len(slots)))}
    return [slots[0]] + [sent[s] for s in range(1, len(slots))]


def body(queries, keys, values, cotangent):
    tokens = (queries, keys, values, cotangent)
    count = lax.axis_size("inner")
    outer_count = lax.axis_size("outer")
    scale = float(HEAD * queries.shape[0] * count * outer_count) ** (-0.5)
    got = swap(half_states(tokens, True), "inner", 1)
    keep = half_states(tokens, False)
    slots = swap_far(pair_slots(keep, got, count // 2))
    slots, local = lax.optimization_barrier((slots, local_part(tokens)))
    sends = group_sends(slots, outer_count)
    others = [swap(send, "outer", s + 1) for s, send in enumerate(sends)]
    slots = swap_far(scan_slots(slots, others))
    mine, theirs = expand(slots, keep, got)
    arrived = swap(theirs, "inner", 1)
    side = lax.rem(lax.axis_index("inner"), 2).astype(jnp.int32).reshape(1)
    outs = finish(side, tokens, local, mine, scale)
    return tuple(finish(1 - side, tokens, local, arrived, scale, outs))


def solution(mesh):
    spec = P(("outer", "inner"), None)
    return jax.shard_map(
        body, mesh=mesh, in_specs=(spec,) * 4, out_specs=(spec,) * 4, check_vma=False
    )
```

time: 94.8 us -> 55.6 us (0.59)
  blocking collectives: 39.3 us -> 0 us
  waiting for transfers between devices: 27.5 us -> 12.4 us
  between operations: 14.1 us -> 0.74 us
  Pallas kernels: 7.22 us -> 20.5 us
  starting transfers between devices: 0.04 us -> 13.2 us
  local copies, waits for them, and re-layouts: 5.41 us -> 8.47 us
    all_to_all x2 -> x0, blocking collectives: 39.3 us -> none  [the longest x1 20.3 us: body(): lax.all_to_all(own, 'inner', split_axis=0, concat_axis=0, tiled=True)]
    all_gather x1 -> x0, waiting for transfers between devices: 27.5 us -> none  [body(): groups = lax.all_gather(total, 'outer')]
    pallas_call x3 -> x9, Pallas kernels: 7.22 us -> 20.5 us  [the longest x1 10.7 us: local_part(): pl.pallas_call(local_kernel, grid=(width // (HEAD * GROUP),), in_specs=[b...]
    ppermute x0 -> x11, starting transfers between devices: none -> 13.2 us  [swap(): lax.ppermute(x, axis, [(i, i ^ bits) for i in range(lax.axis_size(axis))])]
    ppermute x0 -> x11, waiting for transfers between devices: none -> 12.4 us  [swap(): lax.ppermute(x, axis, [(i, i ^ bits) for i in range(lax.axis_size(axis))])]
    unnamed x18 -> x24, local copies, waits for them, and re-layouts: 5.41 us -> 8.47 us
  transfers between devices with their start and end apart: 1 -> 11, of which waited for: 1 -> 6; matrix products, arithmetic and copies ran while one was open for 0% -> 0% of each run, Pallas kernels for 0% -> 24%
where the time goes in v3:
time: 55.6 us; the launch traced here: 55.3 us
  Pallas kernels  20.5 us (37%)
  starting transfers between devices  13.2 us (24%)
  waiting for transfers between devices  12.4 us (22%)
  local copies, waits for them, and re-layouts  8.47 us (15%)
  between operations  0.74 us (1%)
    ppermute x11, starting transfers between devices, swap(): lax.ppermute(x, axis, [(i, i ^ bits) for i in range(lax.axis_size(axis))])  13.2 us
    ppermute x11, waiting for transfers between devices, swap(): lax.ppermute(x, axis, [(i, i ^ bits) for i in range(lax.axis_size(axis))])  12.4 us
    pallas_call x1, Pallas kernels, local_part(): pl.pallas_call(local_kernel, grid=(width // (HEAD * GROUP),), in_specs=[b...  10.7 us
    unnamed x24, local copies, waits for them, and re-layouts  8.47 us
    pallas_call x2, Pallas kernels, finish(): pl.pallas_call(functools.partial(finish_kernel, scale), grid_spec=pltpu.P...  4.72 us
    pallas_call x2, Pallas kernels, half_states(): pl.pallas_call(functools.partial(states_kernel, other), in_specs=[HBM] *...  3.44 us
  transfers between devices with their start and end apart: 11, of which 6 were waited for; matrix products, arithmetic and copies ran while one was open for 0% of the time, Pallas kernels for 24%

profile of v3, /device:TPU:0, one launch (start us, length us, event | category | flops | bytes accessed | tf_op | source)
XLA Modules:
  0.0 55.3 jit_solution(15242615037726475625)
XLA Ops:
  0.7 2.6 %shard_map.76 = bf16[2,1024,128]{2,1,0:T(8,128)(2,1)} custom-call(bf16[128,2048]{1,0:T(8,128)(2,1)} %refs_0_.7, bf16[128,2048]{1,0:T(8,128)(2,1)} %refs_1_.7, bf16[128,2048]{1,0:T(8,128)(2,1)} %refs_2_.7, bf16[128,2048]{1,0:T(8,128)(2,1)} %refs_3_.7), custom_call_target="tpu_custom_call" | custom-call | flops 67108864 | bytes 1572864 | tf_op jit(solution)/shard_map/pallas_call | solution.py:64
  4.7 0.9 %collective-permute-done.got_ref.refs_5_ = bf16[2,1024,128]{2,1,0:T(8,128)(2,1)S(1)} collective-permute-done((bf16[2,1024,128]{2,1,0:T(8,128)(2,1)}, bf16[2,1024,128]{2,1,0:T(8,128)(2,1)S(1)}, u32[]{:S(2)}, u32[]{:S(2)}) %collective-permute-start) | collective-permute-done | bytes 524320 | tf_op jit(solution)/shard_map/ppermute | solution.py:253
  5.7 2.9 %collective-permute-start.1 = (bf16[2,256,128]{2,1,0:T(8,128)(2,1)S(1)}, bf16[2,256,128]{2,1,0:T(8,128)(2,1)S(1)}, u32[]{:S(2)}, u32[]{:S(2)}) collective-permute-start(bf16[2,256,128]{2,1,0:T(8,128)(2,1)S(1)} %get-tuple-element.34), channel_id=1, source_target_pairs={{0,2},{1,3},{2,0},{3,1},{4,6},{5,7},{6,4},{7,5},{8,10},{9,11},{10,... | collective-permute-start | bytes 393224 | tf_op jit(solution)/shard_map/ppermute | solution.py:253
  8.6 1.5 %collective-permute-start.2 = (bf16[2,256,128]{2,1,0:T(8,128)(2,1)S(1)}, bf16[2,256,128]{2,1,0:T(8,128)(2,1)S(1)}, u32[]{:S(2)}, u32[]{:S(2)}) collective-permute-start(bf16[2,256,128]{2,1,0:T(8,128)(2,1)S(1)} %get-tuple-element.35), channel_id=1, source_target_pairs={{0,4},{1,5},{2,6},{3,7},{4,0},{5,1},{6,2},{7,3},{8,12},{9,13},{10,... | collective-permute-start | bytes 393224 | tf_op jit(solution)/shard_map/ppermute | solution.py:253
  10.2 10.7 %shard_map.78 = (f32[128,2048]{1,0:T(8,128)S(1)}, f32[128,2048]{1,0:T(8,128)S(1)}, f32[128,2048]{1,0:T(8,128)S(1)}, f32[128,2048]{1,0:T(8,128)S(1)}) custom-call(bf16[128,2048]{1,0:T(8,128)(2,1)S(1)} %copy-done, bf16[128,2048]{1,0:T(8,128)(2,1)S(1)} %copy-done.1, bf16[128,2048]{1,0:T(8,128)(2,1)S(1)} %copy-done.2, bf16[128,2048]{1,0:T(8,128)(2,1)S(1)} %copy-done.3), custom_call_target="tpu_custom_call" | custom-call | flops 536870912 | bytes 6291456 | tf_op jit(solution)/shard_map/pallas_call | solution.py:204
  20.9 1.0 %copy-done.4 = f32[128,2048]{1,0:T(8,128)} copy-done((f32[128,2048]{1,0:T(8,128)}, f32[128,2048]{1,0:T(8,128)S(1)}, u32[]{:S(2)}) %copy-start.4) | copy-done | bytes 1048600
  21.9 1.0 %copy-done.6 = f32[128,2048]{1,0:T(8,128)} copy-done((f32[128,2048]{1,0:T(8,128)}, f32[128,2048]{1,0:T(8,128)S(1)}, u32[]{:S(2)}) %copy-start.6) | copy-done | bytes 1048600
  22.8 1.0 %copy-done.8 = f32[128,2048]{1,0:T(8,128)} copy-done((f32[128,2048]{1,0:T(8,128)}, f32[128,2048]{1,0:T(8,128)S(1)}, u32[]{:S(2)}) %copy-start.8) | copy-done | bytes 1048600
  23.9 2.1 %collective-permute-start.4 = (bf16[256,128]{1,0:T(8,128)(2,1)S(1)}, bf16[256,128]{1,0:T(8,128)(2,1)S(1)}, u32[]{:S(2)}, u32[]{:S(2)}) collective-permute-start(bf16[256,128]{1,0:T(8,128)(2,1)S(1)} %get-tuple-element.49), channel_id=1, source_target_pairs={{0,8},{8,0},{16,24},{24,16},{1,9},{9,1},{17,25},{25,17},{2,10},{10... | collective-permute-start | bytes 196616 | tf_op jit(solution)/shard_map/ppermute | solution.py:253
  26.0 2.6 %collective-permute-start.5 = (bf16[256,128]{1,0:T(8,128)(2,1)S(1)}, bf16[256,128]{1,0:T(8,128)(2,1)S(1)}, u32[]{:S(2)}, u32[]{:S(2)}) collective-permute-start(bf16[256,128]{1,0:T(8,128)(2,1)S(1)} %get-tuple-element.50), channel_id=1, source_target_pairs={{0,16},{8,24},{16,0},{24,8},{1,17},{9,25},{17,1},{25,9},{2,18},{10... | collective-permute-start | bytes 196616 | tf_op jit(solution)/shard_map/ppermute | solution.py:253
  28.6 4.1 %collective-permute-done.5.refs_5_ = bf16[256,128]{1,0:T(8,128)(2,1)S(1)} collective-permute-done((bf16[256,128]{1,0:T(8,128)(2,1)S(1)}, bf16[256,128]{1,0:T(8,128)(2,1)S(1)}, u32[]{:S(2)}, u32[]{:S(2)}) %collective-permute-start.5) | collective-permute-done | bytes 65568 | tf_op jit(solution)/shard_map/ppermute | solution.py:253
  32.7 1.9 %collective-permute-done.6.refs_6_ = bf16[256,128]{1,0:T(8,128)(2,1)S(1)} collective-permute-done((bf16[256,128]{1,0:T(8,128)(2,1)S(1)}, bf16[256,128]{1,0:T(8,128)(2,1)S(1)}, u32[]{:S(2)}, u32[]{:S(2)}) %collective-permute-start.6) | collective-permute-done | bytes 65568 | tf_op jit(solution)/shard_map/ppermute | solution.py:253
  35.0 1.6 %collective-permute-start.7 = (bf16[2,256,128]{2,1,0:T(8,128)(2,1)S(1)}, bf16[2,256,128]{2,1,0:T(8,128)(2,1)S(1)}, u32[]{:S(2)}, u32[]{:S(2)}) collective-permute-start(bf16[2,256,128]{2,1,0:T(8,128)(2,1)S(1)} %get-tuple-element.53), channel_id=1, source_target_pairs={{0,2},{1,3},{2,0},{3,1},{4,6},{5,7},{6,4},{7,5},{8,10},{9,11},{10,... | collective-permute-start | bytes 393224 | tf_op jit(solution)/shard_map/ppermute | solution.py:253
  36.6 1.5 %collective-permute-start.8 = (bf16[2,256,128]{2,1,0:T(8,128)(2,1)S(1)}, bf16[2,256,128]{2,1,0:T(8,128)(2,1)S(1)}, u32[]{:S(2)}, u32[]{:S(2)}) collective-permute-start(bf16[2,256,128]{2,1,0:T(8,128)(2,1)S(1)} %get-tuple-element.54), channel_id=1, source_target_pairs={{0,4},{1,5},{2,6},{3,7},{4,0},{5,1},{6,2},{7,3},{8,12},{9,13},{10,... | collective-permute-start | bytes 393224 | tf_op jit(solution)/shard_map/ppermute | solution.py:253
  38.6 1.9 %collective-permute-done.7.refs_1_ = bf16[2,256,128]{2,1,0:T(8,128)(2,1)S(1)} collective-permute-done((bf16[2,256,128]{2,1,0:T(8,128)(2,1)S(1)}, bf16[2,256,128]{2,1,0:T(8,128)(2,1)S(1)}, u32[]{:S(2)}, u32[]{:S(2)}) %collective-permute-start.7) | collective-permute-done | bytes 131104 | tf_op jit(solution)/shard_map/ppermute | solution.py:253
  40.5 1.2 %collective-permute-done.8.refs_2_ = bf16[2,256,128]{2,1,0:T(8,128)(2,1)S(1)} collective-permute-done((bf16[2,256,128]{2,1,0:T(8,128)(2,1)S(1)}, bf16[2,256,128]{2,1,0:T(8,128)(2,1)S(1)}, u32[]{:S(2)}, u32[]{:S(2)}) %collective-permute-start.8) | collective-permute-done | bytes 131104 | tf_op jit(solution)/shard_map/ppermute | solution.py:253
  41.7 2.3 %collective-permute-done.9.refs_3_ = bf16[2,256,128]{2,1,0:T(8,128)(2,1)S(1)} collective-permute-done((bf16[2,256,128]{2,1,0:T(8,128)(2,1)S(1)}, bf16[2,256,128]{2,1,0:T(8,128)(2,1)S(1)}, u32[]{:S(2)}, u32[]{:S(2)}) %collective-permute-start.9) | collective-permute-done | bytes 131104 | tf_op jit(solution)/shard_map/ppermute | solution.py:253
  44.0 1.1 %shard_map.81 = (bf16[2,1024,128]{2,1,0:T(8,128)(2,1)S(1)}, bf16[2,1024,128]{2,1,0:T(8,128)(2,1)}) custom-call(bf16[2,256,128]{2,1,0:T(8,128)(2,1)S(1)} %get-tuple-element.52.refs_0_, bf16[2,256,128]{2,1,0:T(8,128)(2,1)S(1)} %collective-permute-done.7.refs_1_, bf16[2,256,128]{2,1,0:T(8,128)(2,1)S(1)} %collective-permute-done.8.refs_2_, ...), custom_call_target="tpu_custom_call" | custom-call | tf_op jit(solution)/shard_map/pallas_call | solution.py:174
  45.8 1.2 %copy-done.5 = f32[128,2048]{1,0:T(8,128)S(1)} copy-done((f32[128,2048]{1,0:T(8,128)S(1)}, f32[128,2048]{1,0:T(8,128)}, u32[]{:S(2)}) %copy-start.5) | copy-done | bytes 1048600
  47.1 1.2 %copy-done.7 = f32[128,2048]{1,0:T(8,128)S(1)} copy-done((f32[128,2048]{1,0:T(8,128)S(1)}, f32[128,2048]{1,0:T(8,128)}, u32[]{:S(2)}) %copy-start.7) | copy-done | bytes 1048600
  48.3 1.2 %copy-done.9 = f32[128,2048]{1,0:T(8,128)S(1)} copy-done((f32[128,2048]{1,0:T(8,128)S(1)}, f32[128,2048]{1,0:T(8,128)}, u32[]{:S(2)}) %copy-start.9) | copy-done | bytes 1048600
  49.5 1.0 %copy-done.11 = bf16[2,1024,128]{2,1,0:T(8,128)(2,1)S(1)} copy-done((bf16[2,1024,128]{2,1,0:T(8,128)(2,1)S(1)}, bf16[2,1024,128]{2,1,0:T(8,128)(2,1)}, u32[]{:S(2)}) %copy-start.11) | copy-done | bytes 524312
  50.6 2.0 %shard_map.82 = (bf16[128,2048]{1,0:T(8,128)(2,1)}, bf16[128,2048]{1,0:T(8,128)(2,1)}, bf16[128,2048]{1,0:T(8,128)(2,1)}, bf16[128,2048]{1,0:T(8,128)(2,1)}) custom-call(s32[1]{0:T(128)} %bitcast.side_ref, bf16[128,2048]{1,0:T(8,128)(2,1)S(1)} %copy-done, bf16[128,2048]{1,0:T(8,128)(2,1)S(1)} %copy-done.1, bf16[128,2048]{1,0:T(8,128)(2,1)S(1)} %copy-done.2, ...), custom_call_target="tpu_custom_call" | custom-call | flops 134217728 | bytes 4456448 | tf_op jit(solution)/shard_map/pallas_call | solution.py:233
  52.6 2.7 %shard_map.83 = (bf16[128,2048]{1,0:T(8,128)(2,1)}, bf16[128,2048]{1,0:T(8,128)(2,1)}, bf16[128,2048]{1,0:T(8,128)(2,1)}, bf16[128,2048]{1,0:T(8,128)(2,1)}) custom-call(s32[1]{0:T(128)S(6)} %sub.3.side_ref, bf16[128,2048]{1,0:T(8,128)(2,1)S(1)} %copy-done, ...), custom_call_target="tpu_custom_call", output_to_operand_aliasing={{0}: (10, {}), {1}: (11, {}), {2}: (12, {}), {3}: (13, {})} | custom-call | flops 134217728 | bytes 4456448 | tf_op jit(solution)/shard_map/pallas_call | solution.py:233
  (31 shorter events, 3.2 us)
Async XLA Ops:
  0.6 3.2 %copy-start.3 = (bf16[128,2048]{1,0:T(8,128)(2,1)S(1)}, bf16[128,2048]{1,0:T(8,128)(2,1)}, u32[]{:S(2)}) copy-start(bf16[128,2048]{1,0:T(8,128)(2,1)} %refs_3_.7) | copy-start | bytes 1572868
  0.6 3.2 %copy-start.2 = (bf16[128,2048]{1,0:T(8,128)(2,1)S(1)}, bf16[128,2048]{1,0:T(8,128)(2,1)}, u32[]{:S(2)}) copy-start(bf16[128,2048]{1,0:T(8,128)(2,1)} %refs_2_.7) | copy-start | bytes 1572868
  0.7 3.2 %copy-start.1 = (bf16[128,2048]{1,0:T(8,128)(2,1)S(1)}, bf16[128,2048]{1,0:T(8,128)(2,1)}, u32[]{:S(2)}) copy-start(bf16[128,2048]{1,0:T(8,128)(2,1)} %refs_1_.7) | copy-start | bytes 1572868
  0.7 3.2 %copy-start = (bf16[128,2048]{1,0:T(8,128)(2,1)S(1)}, bf16[128,2048]{1,0:T(8,128)(2,1)}, u32[]{:S(2)}) copy-start(bf16[128,2048]{1,0:T(8,128)(2,1)} %refs_0_.7) | copy-start | bytes 1572868
  3.3 2.3 %collective-permute-start = (bf16[2,1024,128]{2,1,0:T(8,128)(2,1)}, bf16[2,1024,128]{2,1,0:T(8,128)(2,1)S(1)}, u32[]{:S(2)}, u32[]{:S(2)}) collective-permute-start(bf16[2,1024,128]{2,1,0:T(8,128)(2,1)} %shard_map.76), channel_id=1, source_target_pairs={{0,1},{1,0},{2,3},{3,2},{4,5},{5,4},{6,7},{7,6},{8,9},{9,8},{10,11... | collective-permute-start | bytes 1572872 | tf_op jit(solution)/shard_map/ppermute | solution.py:253
  5.7 18.1 %collective-permute-start.1 = (bf16[2,256,128]{2,1,0:T(8,128)(2,1)S(1)}, bf16[2,256,128]{2,1,0:T(8,128)(2,1)S(1)}, u32[]{:S(2)}, u32[]{:S(2)}) collective-permute-start(bf16[2,256,128]{2,1,0:T(8,128)(2,1)S(1)} %get-tuple-element.34), channel_id=1, source_target_pairs={{0,2},{1,3},{2,0},{3,1},{4,6},{5,7},{6,4},{7,5},{8,10},{9,11},{10,... | collective-permute-start | bytes 393224 | tf_op jit(solution)/shard_map/ppermute | solution.py:253
  8.6 15.2 %collective-permute-start.2 = (bf16[2,256,128]{2,1,0:T(8,128)(2,1)S(1)}, bf16[2,256,128]{2,1,0:T(8,128)(2,1)S(1)}, u32[]{:S(2)}, u32[]{:S(2)}) collective-permute-start(bf16[2,256,128]{2,1,0:T(8,128)(2,1)S(1)} %get-tuple-element.35), channel_id=1, source_target_pairs={{0,4},{1,5},{2,6},{3,7},{4,0},{5,1},{6,2},{7,3},{8,12},{9,13},{10,... | collective-permute-start | bytes 393224 | tf_op jit(solution)/shard_map/ppermute | solution.py:253
  10.2 13.7 %collective-permute-start.3 = (bf16[2,256,128]{2,1,0:T(8,128)(2,1)S(1)}, bf16[2,256,128]{2,1,0:T(8,128)(2,1)S(1)}, u32[]{:S(2)}, u32[]{:S(2)}) collective-permute-start(bf16[2,256,128]{2,1,0:T(8,128)(2,1)S(1)} %get-tuple-element.36), channel_id=1, source_target_pairs={{0,6},{1,7},{2,4},{3,5},{4,2},{5,3},{6,0},{7,1},{8,14},{9,15},{10,... | collective-permute-start | bytes 393224 | tf_op jit(solution)/shard_map/ppermute | solution.py:253
  20.9 1.0 %copy-start.4 = (f32[128,2048]{1,0:T(8,128)}, f32[128,2048]{1,0:T(8,128)S(1)}, u32[]{:S(2)}) copy-start(f32[128,2048]{1,0:T(8,128)S(1)} %get-tuple-element.42.refs_5_) | copy-start | bytes 3145732
  21.9 1.0 %copy-start.6 = (f32[128,2048]{1,0:T(8,128)}, f32[128,2048]{1,0:T(8,128)S(1)}, u32[]{:S(2)}) copy-start(f32[128,2048]{1,0:T(8,128)S(1)} %get-tuple-element.43.refs_6_) | copy-start | bytes 3145732
  22.8 1.0 %copy-start.8 = (f32[128,2048]{1,0:T(8,128)}, f32[128,2048]{1,0:T(8,128)S(1)}, u32[]{:S(2)}) copy-start(f32[128,2048]{1,0:T(8,128)S(1)} %get-tuple-element.44.refs_7_) | copy-start | bytes 3145732
  23.9 4.7 %collective-permute-start.4 = (bf16[256,128]{1,0:T(8,128)(2,1)S(1)}, bf16[256,128]{1,0:T(8,128)(2,1)S(1)}, u32[]{:S(2)}, u32[]{:S(2)}) collective-permute-start(bf16[256,128]{1,0:T(8,128)(2,1)S(1)} %get-tuple-element.49), channel_id=1, source_target_pairs={{0,8},{8,0},{16,24},{24,16},{1,9},{9,1},{17,25},{25,17},{2,10},{10... | collective-permute-start | bytes 196616 | tf_op jit(solution)/shard_map/ppermute | solution.py:253
  26.0 6.7 %collective-permute-start.5 = (bf16[256,128]{1,0:T(8,128)(2,1)S(1)}, bf16[256,128]{1,0:T(8,128)(2,1)S(1)}, u32[]{:S(2)}, u32[]{:S(2)}) collective-permute-start(bf16[256,128]{1,0:T(8,128)(2,1)S(1)} %get-tuple-element.50), channel_id=1, source_target_pairs={{0,16},{8,24},{16,0},{24,8},{1,17},{9,25},{17,1},{25,9},{2,18},{10... | collective-permute-start | bytes 196616 | tf_op jit(solution)/shard_map/ppermute | solution.py:253
  28.6 6.1 %collective-permute-start.6 = (bf16[256,128]{1,0:T(8,128)(2,1)S(1)}, bf16[256,128]{1,0:T(8,128)(2,1)S(1)}, u32[]{:S(2)}, u32[]{:S(2)}) collective-permute-start(bf16[256,128]{1,0:T(8,128)(2,1)S(1)} %get-tuple-element.51), channel_id=1, source_target_pairs={{0,24},{8,16},{16,8},{24,0},{1,25},{9,17},{17,9},{25,1},{2,26},{10... | collective-permute-start | bytes 196616 | tf_op jit(solution)/shard_map/ppermute | solution.py:253
  35.0 5.5 %collective-permute-start.7 = (bf16[2,256,128]{2,1,0:T(8,128)(2,1)S(1)}, bf16[2,256,128]{2,1,0:T(8,128)(2,1)S(1)}, u32[]{:S(2)}, u32[]{:S(2)}) collective-permute-start(bf16[2,256,128]{2,1,0:T(8,128)(2,1)S(1)} %get-tuple-element.53), channel_id=1, source_target_pairs={{0,2},{1,3},{2,0},{3,1},{4,6},{5,7},{6,4},{7,5},{8,10},{9,11},{10,... | collective-permute-start | bytes 393224 | tf_op jit(solution)/shard_map/ppermute | solution.py:253
  36.6 5.1 %collective-permute-start.8 = (bf16[2,256,128]{2,1,0:T(8,128)(2,1)S(1)}, bf16[2,256,128]{2,1,0:T(8,128)(2,1)S(1)}, u32[]{:S(2)}, u32[]{:S(2)}) collective-permute-start(bf16[2,256,128]{2,1,0:T(8,128)(2,1)S(1)} %get-tuple-element.54), channel_id=1, source_target_pairs={{0,4},{1,5},{2,6},{3,7},{4,0},{5,1},{6,2},{7,3},{8,12},{9,13},{10,... | collective-permute-start | bytes 393224 | tf_op jit(solution)/shard_map/ppermute | solution.py:253
  38.1 5.9 %collective-permute-start.9 = (bf16[2,256,128]{2,1,0:T(8,128)(2,1)S(1)}, bf16[2,256,128]{2,1,0:T(8,128)(2,1)S(1)}, u32[]{:S(2)}, u32[]{:S(2)}) collective-permute-start(bf16[2,256,128]{2,1,0:T(8,128)(2,1)S(1)} %get-tuple-element.55), channel_id=1, source_target_pairs={{0,6},{1,7},{2,4},{3,5},{4,2},{5,3},{6,0},{7,1},{8,14},{9,15},{10,... | collective-permute-start | bytes 393224 | tf_op jit(solution)/shard_map/ppermute | solution.py:253
  45.0 0.8 %copy-start.10 = (bf16[2,1024,128]{2,1,0:T(8,128)(2,1)}, bf16[2,1024,128]{2,1,0:T(8,128)(2,1)S(1)}, u32[]{:S(2)}) copy-start(bf16[2,1024,128]{2,1,0:T(8,128)(2,1)S(1)} %get-tuple-element.57.refs_8_) | copy-start | bytes 1572868
  45.8 6.7 %collective-permute-start.10 = (bf16[2,1024,128]{2,1,0:T(8,128)(2,1)}, bf16[2,1024,128]{2,1,0:T(8,128)(2,1)}, u32[]{:S(2)}, u32[]{:S(2)}) collective-permute-start(bf16[2,1024,128]{2,1,0:T(8,128)(2,1)} %get-tuple-element.56), channel_id=1, source_target_pairs={{0,1},{1,0},{2,3},{3,2},{4,5},{5,4},{6,7},{7,6},{8,9},{9,8},{10,11... | collective-permute-start | bytes 1572872 | tf_op jit(solution)/shard_map/ppermute | solution.py:253
  45.8 1.2 %copy-start.5 = (f32[128,2048]{1,0:T(8,128)S(1)}, f32[128,2048]{1,0:T(8,128)}, u32[]{:S(2)}) copy-start(f32[128,2048]{1,0:T(8,128)} %copy-done.4) | copy-start | bytes 3145732
  47.1 1.2 %copy-start.7 = (f32[128,2048]{1,0:T(8,128)S(1)}, f32[128,2048]{1,0:T(8,128)}, u32[]{:S(2)}) copy-start(f32[128,2048]{1,0:T(8,128)} %copy-done.6) | copy-start | bytes 3145732
  48.3 1.2 %copy-start.9 = (f32[128,2048]{1,0:T(8,128)S(1)}, f32[128,2048]{1,0:T(8,128)}, u32[]{:S(2)}) copy-start(f32[128,2048]{1,0:T(8,128)} %copy-done.8) | copy-start | bytes 3145732
  49.5 1.0 %copy-start.11 = (bf16[2,1024,128]{2,1,0:T(8,128)(2,1)S(1)}, bf16[2,1024,128]{2,1,0:T(8,128)(2,1)}, u32[]{:S(2)}) copy-start(bf16[2,1024,128]{2,1,0:T(8,128)(2,1)} %copy-done.10) | copy-start | bytes 1572868

commit v4 on v3

--- a/solution.py
+++ b/solution.py
@@ -8,11 +8,9 @@
 from jax.sharding import PartitionSpec as P
 
 HEAD = 128
-GROUP = 4
-PIECES = 2
+PIECES = 4
 MIB = 1024 * 1024
 ANY = pl.BlockSpec(memory_space=pl.ANY)
-HBM = pl.BlockSpec(memory_space=pltpu.HBM)
 VMEM = pl.BlockSpec(memory_space=pltpu.VMEM)
 BF16 = jnp.bfloat16
 F32 = jnp.float32
@@ -30,8 +28,8 @@
 
 
 def states_kernel(other, *refs):
-    tokens, (out, held, sems) = refs[:4], refs[4:]
-    half = out.shape[1]
+    tokens, (out_ref, held, out, in_sems, out_sems) = refs[:4], refs[4:]
+    half = held.shape[2]
     piece = half // PIECES
     near, _ = near_far()
     side = 1 - near if other else near
@@ -40,11 +38,16 @@
             pltpu.make_async_copy(
                 ref.at[:, pl.ds(pl.multiple_of(side * half + p * piece, piece), piece)],
                 held.at[i, :, pl.ds(p * piece, piece)],
-                sems.at[i, p],
+                in_sems.at[i, p],
             )
             for i, ref in enumerate(tokens)
         ]
         for p in range(PIECES)
+    ]
+    backs = [
+        pltpu.make_async_copy(out.at[:, part], out_ref.at[:, part], out_sems.at[p])
+        for p in range(PIECES)
+        for part in [pl.ds(p * piece, piece)]
     ]
     for group in copies:
         for copy in group:
@@ -56,24 +59,50 @@
             cols = slice(h * HEAD, (h + 1) * HEAD)
             out[0, cols] = dot(held[1, :, cols], held[2, :, cols], 0, 0).astype(BF16)
             out[1, cols] = dot(held[0, :, cols], held[3, :, cols], 0, 0).astype(BF16)
+        backs[p].start()
+    for back in backs:
+        back.wait()
+
+
+def resident_states_kernel(q_ref, k_ref, v_ref, d_ref, out):
+    half = out.shape[1]
+    near, _ = near_far()
+    for h in range(half // HEAD):
+        cols = pl.ds(pl.multiple_of(near * half + h * HEAD, HEAD), HEAD)
+        into = slice(h * HEAD, (h + 1) * HEAD)
+        out[0, into] = dot(k_ref[:, cols], v_ref[:, cols], 0, 0).astype(BF16)
+        out[1, into] = dot(q_ref[:, cols], d_ref[:, cols], 0, 0).astype(BF16)
 
 
 def half_states(tokens, other):
     rows, width = tokens[0].shape
     half = width // 2
+    cost = pl.CostEstimate(
+        flops=4 * rows * half * HEAD, bytes_accessed=12 * rows * half, transcendentals=0
+    )
+    out = jax.ShapeDtypeStruct((2, half, HEAD), BF16)
+    if not other:
+        return pl.pallas_call(
+            resident_states_kernel,
+            in_specs=[VMEM] * 4,
+            out_specs=VMEM,
+            out_shape=out,
+            cost_estimate=cost,
+            compiler_params=pltpu.CompilerParams(vmem_limit_bytes=4 * MIB),
+        )(*tokens)
     return pl.pallas_call(
         functools.partial(states_kernel, other),
-        in_specs=[HBM] * 4,
-        out_specs=VMEM,
-        out_shape=jax.ShapeDtypeStruct((2, half, HEAD), BF16),
+        in_specs=[ANY] * 4,
+        out_specs=ANY,
+        out_shape=out,
         scratch_shapes=[
             pltpu.VMEM((4, rows, half), BF16),
+            pltpu.VMEM(out.shape, BF16),
             pltpu.SemaphoreType.DMA((4, PIECES)),
+            pltpu.SemaphoreType.DMA((PIECES,)),
         ],
-        cost_estimate=pl.CostEstimate(
-            flops=4 * rows * half * HEAD, bytes_accessed=12 * rows * half, transcendentals=0
-        ),
-        compiler_params=pltpu.CompilerParams(vmem_limit_bytes=(60 if other else 16) * MIB),
+        cost_estimate=cost,
+        compiler_params=pltpu.CompilerParams(vmem_limit_bytes=60 * MIB),
     )(*tokens)
 
 
@@ -94,7 +123,7 @@
         in_specs=[VMEM] * 2,
         out_specs=[VMEM] * far_count,
         out_shape=[slot] * far_count,
-        compiler_params=pltpu.CompilerParams(vmem_limit_bytes=32 * MIB),
+        compiler_params=pltpu.CompilerParams(vmem_limit_bytes=4 * MIB),
     )(keep, got)
 
 
@@ -119,7 +148,7 @@
         in_specs=[VMEM] * len(slots),
         out_specs=[VMEM] * (outer_count - 1),
         out_shape=[send] * (outer_count - 1),
-        compiler_params=pltpu.CompilerParams(vmem_limit_bytes=32 * MIB),
+        compiler_params=pltpu.CompilerParams(vmem_limit_bytes=4 * MIB),
     )(*slots)
 
 
@@ -151,33 +180,39 @@
         in_specs=[VMEM] * (far_count + len(others)),
         out_specs=[VMEM] * far_count,
         out_shape=[slot] * far_count,
-        compiler_params=pltpu.CompilerParams(vmem_limit_bytes=32 * MIB),
+        compiler_params=pltpu.CompilerParams(vmem_limit_bytes=4 * MIB),
     )(*slots, *others)
 
 
-def expand_kernel(far_count, *refs):
-    slots, (keep, got, mine, theirs) = refs[:far_count], refs[far_count:]
+def expand(slots, out, extras, extra_which):
     depth = slots[0].shape[1]
-    near, far = near_far()
+    _, far = near_far()
     for s, slot in enumerate(slots):
         part = pl.ds(pl.multiple_of((far ^ s) * depth, depth), depth)
         for which in range(2):
-            base = slot[which].astype(F32)
-            for_me = near == 1 - which
-            own, others = keep[which, part].astype(F32), got[which, part].astype(F32)
-            mine[which, part] = (base + jnp.where(for_me, others, 0.0)).astype(BF16)
-            theirs[which, part] = (base + jnp.where(for_me, 0.0, own)).astype(BF16)
-
-
-def expand(slots, keep, got):
-    state = jax.ShapeDtypeStruct(keep.shape, BF16)
-    return pl.pallas_call(
-        functools.partial(expand_kernel, len(slots)),
-        in_specs=[VMEM] * (len(slots) + 2),
-        out_specs=[VMEM] * 2,
-        out_shape=[state] * 2,
-        compiler_params=pltpu.CompilerParams(vmem_limit_bytes=32 * MIB),
-    )(*slots, keep, got)
+            @pl.when(extra_which == which)
+            def _():
+                out[which, part] = (slot[which].astype(F32) + extras[which, part].astype(F32)).astype(BF16)
+
+            @pl.when(extra_which != which)
+            def _():
+                out[which, part] = slot[which]
+
+
+def theirs_kernel(*refs):
+    slots, (keep, out) = refs[:-2], refs[-2:]
+    near, _ = near_far()
+    expand(slots, out, keep, near)
+
+
+def state_for_neighbour(slots, keep):
+    return pl.pallas_call(
+        theirs_kernel,
+        in_specs=[VMEM] * (len(slots) + 1),
+        out_specs=VMEM,
+        out_shape=jax.ShapeDtypeStruct(keep.shape, BF16),
+        compiler_params=pltpu.CompilerParams(vmem_limit_bytes=4 * MIB),
+    )(*slots, keep)
 
 
 def local_kernel(q_ref, k_ref, v_ref, d_ref, att_ref, gq_ref, gk_ref, gv_ref):
@@ -200,53 +235,70 @@
 
 def local_part(tokens):
     rows, width = tokens[0].shape
-    block = pl.BlockSpec((rows, GROUP * HEAD), lambda g: (0, g))
     return pl.pallas_call(
         local_kernel,
-        grid=(width // (HEAD * GROUP),),
-        in_specs=[block] * 4,
-        out_specs=[block] * 4,
+        in_specs=[VMEM] * 4,
+        out_specs=[VMEM] * 4,
         out_shape=[jax.ShapeDtypeStruct((rows, width), F32)] * 4,
         cost_estimate=pl.CostEstimate(
             flops=16 * rows * width * HEAD, bytes_accessed=24 * rows * width, transcendentals=0
         ),
-        compiler_params=pltpu.CompilerParams(vmem_limit_bytes=32 * MIB),
+        compiler_params=pltpu.CompilerParams(vmem_limit_bytes=4 * MIB),
     )(*tokens)
 
 
-def finish_kernel(scale, side_ref, *refs):
-    tokens, local, states, outs = refs[:4], refs[4:8], refs[8], refs[-4:]
-    for h in range(tokens[0].shape[1] // HEAD):
-        cols = slice(h * HEAD, (h + 1) * HEAD)
-        q, k, v, d = (ref[:, cols] for ref in tokens)
-        s, g = states[0, cols], states[1, cols]
-        parts = (dot(q, s, 1, 0), dot(d, s, 1, 1), dot(v, g, 1, 1), dot(k, g, 1, 0))
-        for part, near, out in zip(parts, local, outs):
-            out[:, cols] = (scale * (part + near[:, cols])).astype(BF16)
-
-
-def finish(side, tokens, local, states, scale, before=()):
+def finish_kernel(scale, slot_count, *refs):
+    tokens, local, refs = refs[:4], refs[4:8], refs[8:]
+    held, sems = refs[-2:]
+    near, _ = near_far()
+    if slot_count:
+        outs, states = refs[-7:-3], refs[-3]
+        expand(refs[:slot_count], states, refs[slot_count], 1 - near)
+        side = near
+    else:
+        outs, states, side = refs[-6:-2], refs[0], 1 - near
+    half = held.shape[2]
+    piece = half // PIECES
+    copies = []
+    for p in range(PIECES):
+        for h in range(p * piece // HEAD, (p + 1) * piece // HEAD):
+            into = slice(h * HEAD, (h + 1) * HEAD)
+            cols = pl.ds(pl.multiple_of(side * half + h * HEAD, HEAD), HEAD)
+            q, k, v, d = (ref[:, cols] for ref in tokens)
+            s, g = states[0, into], states[1, into]
+            parts = (dot(q, s, 1, 0), dot(d, s, 1, 1), dot(v, g, 1, 1), dot(k, g, 1, 0))
+            for i, part in enumerate(parts):
+                held[i, :, into] = (scale * (part + local[i][:, cols])).astype(BF16)
+        for i, out in enumerate(outs):
+            there = pl.ds(pl.multiple_of(side * half + p * piece, piece), piece)
+            copy = pltpu.make_async_copy(
+                held.at[i, :, pl.ds(p * piece, piece)], out.at[:, there], sems.at[i, p]
+            )
+            copy.start()
+            copies.append(copy)
+    for copy in copies:
+        copy.wait()
+
+
+def finish(tokens, local, states, scale, before=()):
     rows, width = tokens[0].shape
-    steps = width // 2 // (HEAD * GROUP)
-    block = pl.BlockSpec((rows, GROUP * HEAD), lambda g, side: (0, side[0] * steps + g))
+    half = width // 2
+    slot_count = 0 if before else len(states) - 1
     out = jax.ShapeDtypeStruct((rows, width), BF16)
-    return pl.pallas_call(
-        functools.partial(finish_kernel, scale),
-        grid_spec=pltpu.PrefetchScalarGridSpec(
-            num_scalar_prefetch=1,
-            grid=(steps,),
-            in_specs=[block] * 8
-            + [pl.BlockSpec((2, GROUP * HEAD, HEAD), lambda g, side: (0, g, 0))]
-            + [ANY] * len(before),
-            out_specs=[block] * 4,
-        ),
+    scratch = [pltpu.VMEM((2, half, HEAD), BF16)] if slot_count else []
+    return pl.pallas_call(
+        functools.partial(finish_kernel, scale, slot_count),
+        in_specs=[VMEM] * (8 + len(states)) + [ANY] * len(before),
+        out_specs=[ANY] * 4,
         out_shape=[out] * 4,
-        input_output_aliases={10 + i: i for i in range(len(before))},
+        scratch_shapes=scratch
+        + [pltpu.VMEM((4, rows, half), BF16), pltpu.SemaphoreType.DMA((4, PIECES))],
+        input_output_aliases={8 + len(states) + i: i for i in range(len(before))},
         cost_estimate=pl.CostEstimate(
             flops=4 * rows * width * HEAD, bytes_accessed=17 * rows * width, transcendentals=0
         ),
-        compiler_params=pltpu.CompilerParams(vmem_limit_bytes=32 * MIB),
-    )(side, *tokens, *local, states, *before)
+        compiler_params=pltpu.CompilerParams(vmem_limit_bytes=8 * MIB),
+    )(*tokens, *local, *states, *before)
 
 
 def swap(x, axis, bits):
@@ -270,11 +322,9 @@
     sends = group_sends(slots, outer_count)
     others = [swap(send, "outer", s + 1) for s, send in enumerate(sends)]
     slots = swap_far(scan_slots(slots, others))
-    mine, theirs = expand(slots, keep, got)
-    arrived = swap(theirs, "inner", 1)
-    side = lax.rem(lax.axis_index("inner"), 2).astype(jnp.int32).reshape(1)
-    outs = finish(side, tokens, local, mine, scale)
-    return tuple(finish(1 - side, tokens, local, arrived, scale, outs))
+    arrived = swap(state_for_neighbour(slots, keep), "inner", 1)
+    outs = finish(tokens, local, (*slots, got), scale)
+    return tuple(finish(tokens, local, (arrived,), scale, outs))
 
 
 def solution(mesh):

time: 55.6 us -> 44.1 us (0.79)
  local copies, waits for them, and re-layouts: 8.47 us -> 0.02 us
  Pallas kernels: 20.5 us -> 16.9 us
  waiting for transfers between devices: 12.4 us -> 13 us
    unnamed x24 -> x8, local copies, waits for them, and re-layouts: 8.47 us -> 0.02 us
    pallas_call x6, Pallas kernels: 19.9 us -> 16.4 us  [the longest x1 9.82 us: local_part(): pl.pallas_call(local_kernel, in_specs=[VMEM] * 4, out_specs=[VMEM] * 4, o...]
    ppermute x11, waiting for transfers between devices: 12.4 us -> 13 us  [swap(): lax.ppermute(x, axis, [(i, i ^ bits) for i in range(lax.axis_size(axis))])]
  transfers between devices with their start and end apart: 11 -> 11, of which waited for: 6 -> 7; matrix products, arithmetic and copies ran while one was open for 0% -> 0% of each run, Pallas kernels for 24% -> 27%
where the time goes in v4:
time: 44.1 us; the launch traced here: 44 us
  Pallas kernels  16.9 us (38%)
  starting transfers between devices  13.3 us (30%)
  waiting for transfers between devices  13 us (29%)
  between operations  0.76 us (2%)
    ppermute x11, starting transfers between devices, swap(): lax.ppermute(x, axis, [(i, i ^ bits) for i in range(lax.axis_size(axis))])  13.3 us
    ppermute x11, waiting for transfers between devices, swap(): lax.ppermute(x, axis, [(i, i ^ bits) for i in range(lax.axis_size(axis))])  13 us
    pallas_call x1, Pallas kernels, local_part(): pl.pallas_call(local_kernel, in_specs=[VMEM] * 4, out_specs=[VMEM] * 4, o...  9.82 us
    pallas_call x2, Pallas kernels, finish(): pl.pallas_call(functools.partial(finish_kernel, scale, slot_count), in_sp...  3.14 us
    pallas_call x1, Pallas kernels, half_states(): pl.pallas_call(functools.partial(states_kernel, other), in_specs=[ANY] *...  2.83 us
  transfers between devices with their start and end apart: 11, of which 7 were waited for; matrix products, arithmetic and copies ran while one was open for 0% of the time, Pallas kernels for 27%

profile of v4, /device:TPU:0, one launch (start us, length us, event | category | flops | bytes accessed | tf_op | source)
XLA Modules:
  0.0 44.0 jit_solution(16137773864750574577)
XLA Ops:
  0.7 2.8 %shard_map.76 = bf16[2,1024,128]{2,1,0:T(8,128)(2,1)} custom-call(bf16[128,2048]{1,0:T(8,128)(2,1)} %refs_0_.5, bf16[128,2048]{1,0:T(8,128)(2,1)} %refs_1_.5, bf16[128,2048]{1,0:T(8,128)(2,1)} %refs_2_.5, bf16[128,2048]{1,0:T(8,128)(2,1)} %refs_3_.5), custom_call_target="tpu_custom_call" | custom-call | flops 67108864 | bytes 1572864 | tf_op jit(solution)/shard_map/pallas_call | solution.py:93
  3.5 0.5 %collective-permute-start = (bf16[2,1024,128]{2,1,0:T(8,128)(2,1)}, bf16[2,1024,128]{2,1,0:T(8,128)(2,1)S(1)}, u32[]{:S(2)}, u32[]{:S(2)}) collective-permute-start(bf16[2,1024,128]{2,1,0:T(8,128)(2,1)} %shard_map.76), channel_id=1, source_target_pairs={{0,1},{1,0},{2,3},{3,2},{4,5},{5,4},{6,7},{7,6},{8,9},{9,8},{10,11... | collective-permute-start | bytes 1572872 | tf_op jit(solution)/shard_map/ppermute | solution.py:305
  4.0 0.5 %shard_map.75.keep_ref.refs_4_ = bf16[2,1024,128]{2,1,0:T(8,128)(2,1)S(1)} custom-call(bf16[128,2048]{1,0:T(8,128)(2,1)S(1)} %copy-done, bf16[128,2048]{1,0:T(8,128)(2,1)S(1)} %copy-done.1, bf16[128,2048]{1,0:T(8,128)(2,1)S(1)} %copy-done.2, bf16[128,2048]{1,0:T(8,128)(2,1)S(1)} %copy-done.3), custom_call_target="tpu_custom_call" | custom-call | flops 67108864 | bytes 1572864 | tf_op jit(solution)/shard_map/pallas_call | solution.py:85
  4.5 1.2 %collective-permute-done.got_ref.refs_12_ = bf16[2,1024,128]{2,1,0:T(8,128)(2,1)S(1)} collective-permute-done((bf16[2,1024,128]{2,1,0:T(8,128)(2,1)}, bf16[2,1024,128]{2,1,0:T(8,128)(2,1)S(1)}, u32[]{:S(2)}, u32[]{:S(2)}) %collective-permute-start) | collective-permute-done | bytes 524320 | tf_op jit(solution)/shard_map/ppermute | solution.py:305
  5.8 0.1 shard_map.77
  5.9 2.9 %collective-permute-start.1 = (bf16[2,256,128]{2,1,0:T(8,128)(2,1)S(1)}, bf16[2,256,128]{2,1,0:T(8,128)(2,1)S(1)}, u32[]{:S(2)}, u32[]{:S(2)}) collective-permute-start(bf16[2,256,128]{2,1,0:T(8,128)(2,1)S(1)} %get-tuple-element.32), channel_id=1, source_target_pairs={{0,2},{1,3},{2,0},{3,1},{4,6},{5,7},{6,4},{7,5},{8,10},{9,11},{10,... | collective-permute-start | bytes 393224 | tf_op jit(solution)/shard_map/ppermute | solution.py:305
  8.8 1.5 %collective-permute-start.2 = (bf16[2,256,128]{2,1,0:T(8,128)(2,1)S(1)}, bf16[2,256,128]{2,1,0:T(8,128)(2,1)S(1)}, u32[]{:S(2)}, u32[]{:S(2)}) collective-permute-start(bf16[2,256,128]{2,1,0:T(8,128)(2,1)S(1)} %get-tuple-element.33), channel_id=1, source_target_pairs={{0,4},{1,5},{2,6},{3,7},{4,0},{5,1},{6,2},{7,3},{8,12},{9,13},{10,... | collective-permute-start | bytes 393224 | tf_op jit(solution)/shard_map/ppermute | solution.py:305
  10.4 9.8 %shard_map.78 = (f32[128,2048]{1,0:T(8,128)S(1)}, f32[128,2048]{1,0:T(8,128)S(1)}, f32[128,2048]{1,0:T(8,128)S(1)}, f32[128,2048]{1,0:T(8,128)S(1)}) custom-call(bf16[128,2048]{1,0:T(8,128)(2,1)S(1)} %copy-done, bf16[128,2048]{1,0:T(8,128)(2,1)S(1)} %copy-done.1, bf16[128,2048]{1,0:T(8,128)(2,1)S(1)} %copy-done.2, bf16[128,2048]{1,0:T(8,128)(2,1)S(1)} %copy-done.3), custom_call_target="tpu_custom_call" | custom-call | flops 536870912 | bytes 6291456 | tf_op jit(solution)/shard_map/pallas_call | solution.py:238
  20.2 0.1 shard_map.79
  20.3 2.1 %collective-permute-start.4 = (bf16[256,128]{1,0:T(8,128)(2,1)S(1)}, bf16[256,128]{1,0:T(8,128)(2,1)S(1)}, u32[]{:S(2)}, u32[]{:S(2)}) collective-permute-start(bf16[256,128]{1,0:T(8,128)(2,1)S(1)} %get-tuple-element.47), channel_id=1, source_target_pairs={{0,8},{8,0},{16,24},{24,16},{1,9},{9,1},{17,25},{25,17},{2,10},{10... | collective-permute-start | bytes 196616 | tf_op jit(solution)/shard_map/ppermute | solution.py:305
  22.4 2.6 %collective-permute-start.5 = (bf16[256,128]{1,0:T(8,128)(2,1)S(1)}, bf16[256,128]{1,0:T(8,128)(2,1)S(1)}, u32[]{:S(2)}, u32[]{:S(2)}) collective-permute-start(bf16[256,128]{1,0:T(8,128)(2,1)S(1)} %get-tuple-element.48), channel_id=1, source_target_pairs={{0,16},{8,24},{16,0},{24,8},{1,17},{9,25},{17,1},{25,9},{2,18},{10... | collective-permute-start | bytes 196616 | tf_op jit(solution)/shard_map/ppermute | solution.py:305
  25.0 4.1 %collective-permute-done.5.refs_5_ = bf16[256,128]{1,0:T(8,128)(2,1)S(1)} collective-permute-done((bf16[256,128]{1,0:T(8,128)(2,1)S(1)}, bf16[256,128]{1,0:T(8,128)(2,1)S(1)}, u32[]{:S(2)}, u32[]{:S(2)}) %collective-permute-start.5) | collective-permute-done | bytes 65568 | tf_op jit(solution)/shard_map/ppermute | solution.py:305
  29.1 1.9 %collective-permute-done.6.refs_6_ = bf16[256,128]{1,0:T(8,128)(2,1)S(1)} collective-permute-done((bf16[256,128]{1,0:T(8,128)(2,1)S(1)}, bf16[256,128]{1,0:T(8,128)(2,1)S(1)}, u32[]{:S(2)}, u32[]{:S(2)}) %collective-permute-start.6) | collective-permute-done | bytes 65568 | tf_op jit(solution)/shard_map/ppermute | solution.py:305
  31.1 0.3 shard_map.80
  31.4 1.6 %collective-permute-start.7 = (bf16[2,256,128]{2,1,0:T(8,128)(2,1)S(1)}, bf16[2,256,128]{2,1,0:T(8,128)(2,1)S(1)}, u32[]{:S(2)}, u32[]{:S(2)}) collective-permute-start(bf16[2,256,128]{2,1,0:T(8,128)(2,1)S(1)} %get-tuple-element.51), channel_id=1, source_target_pairs={{0,2},{1,3},{2,0},{3,1},{4,6},{5,7},{6,4},{7,5},{8,10},{9,11},{10,... | collective-permute-start | bytes 393224 | tf_op jit(solution)/shard_map/ppermute | solution.py:305
  33.0 1.5 %collective-permute-start.8 = (bf16[2,256,128]{2,1,0:T(8,128)(2,1)S(1)}, bf16[2,256,128]{2,1,0:T(8,128)(2,1)S(1)}, u32[]{:S(2)}, u32[]{:S(2)}) collective-permute-start(bf16[2,256,128]{2,1,0:T(8,128)(2,1)S(1)} %get-tuple-element.52), channel_id=1, source_target_pairs={{0,4},{1,5},{2,6},{3,7},{4,0},{5,1},{6,2},{7,3},{8,12},{9,13},{10,... | collective-permute-start | bytes 393224 | tf_op jit(solution)/shard_map/ppermute | solution.py:305
  34.5 0.5 %collective-permute-start.9 = (bf16[2,256,128]{2,1,0:T(8,128)(2,1)S(1)}, bf16[2,256,128]{2,1,0:T(8,128)(2,1)S(1)}, u32[]{:S(2)}, u32[]{:S(2)}) collective-permute-start(bf16[2,256,128]{2,1,0:T(8,128)(2,1)S(1)} %get-tuple-element.53), channel_id=1, source_target_pairs={{0,6},{1,7},{2,4},{3,5},{4,2},{5,3},{6,0},{7,1},{8,14},{9,15},{10,... | collective-permute-start | bytes 393224 | tf_op jit(solution)/shard_map/ppermute | solution.py:305
  35.0 1.9 %collective-permute-done.7.refs_1_.refs_9_ = bf16[2,256,128]{2,1,0:T(8,128)(2,1)S(1)} collective-permute-done((bf16[2,256,128]{2,1,0:T(8,128)(2,1)S(1)}, bf16[2,256,128]{2,1,0:T(8,128)(2,1)S(1)}, u32[]{:S(2)}, u32[]{:S(2)}) %collective-permute-start.7) | collective-permute-done | bytes 131104 | tf_op jit(solution)/shard_map/ppermute | solution.py:305
  36.9 1.2 %collective-permute-done.8.refs_2_.refs_10_ = bf16[2,256,128]{2,1,0:T(8,128)(2,1)S(1)} collective-permute-done((bf16[2,256,128]{2,1,0:T(8,128)(2,1)S(1)}, bf16[2,256,128]{2,1,0:T(8,128)(2,1)S(1)}, u32[]{:S(2)}, u32[]{:S(2)}) %collective-permute-start.8) | collective-permute-done | bytes 131104 | tf_op jit(solution)/shard_map/ppermute | solution.py:305
  38.1 2.3 %collective-permute-done.9.refs_3_.refs_11_ = bf16[2,256,128]{2,1,0:T(8,128)(2,1)S(1)} collective-permute-done((bf16[2,256,128]{2,1,0:T(8,128)(2,1)S(1)}, bf16[2,256,128]{2,1,0:T(8,128)(2,1)S(1)}, u32[]{:S(2)}, u32[]{:S(2)}) %collective-permute-start.9) | collective-permute-done | bytes 131104 | tf_op jit(solution)/shard_map/ppermute | solution.py:305
  40.4 0.1 shard_map.81
  40.6 1.6 %shard_map.82 = (bf16[128,2048]{1,0:T(8,128)(2,1)}, bf16[128,2048]{1,0:T(8,128)(2,1)}, bf16[128,2048]{1,0:T(8,128)(2,1)}, bf16[128,2048]{1,0:T(8,128)(2,1)}) custom-call(bf16[128,2048]{1,0:T(8,128)(2,1)S(1)} %copy-done, bf16[128,2048]{1,0:T(8,128)(2,1)S(1)} %copy-done.1, bf16[128,2048]{1,0:T(8,128)(2,1)S(1)} %copy-done.2, bf16[128,2048]{1,0:T(8,128)(2,1)S(1)} %copy-done.3, ...), custom_call_target="tpu_custom_call" | custom-call | flops 134217728 | bytes 4456448 | tf_op jit(solution)/shard_map/pallas_call | solution.py:289
  42.2 0.2 collective-permute-done.10.refs_8_
  42.5 1.5 %shard_map.83 = (bf16[128,2048]{1,0:T(8,128)(2,1)}, bf16[128,2048]{1,0:T(8,128)(2,1)}, bf16[128,2048]{1,0:T(8,128)(2,1)}, bf16[128,2048]{1,0:T(8,128)(2,1)}) custom-call(bf16[128,2048]{1,0:T(8,128)(2,1)S(1)} %copy-done, bf16[128,2048]{1,0:T(8,128)(2,1)S(1)} %copy-done.1, ...), custom_call_target="tpu_custom_call", output_to_operand_aliasing={{0}: (9, {}), {1}: (10, {}), {2}: (11, {}), {3}: (12, {})} | custom-call | flops 134217728 | bytes 4456448 | tf_op jit(solution)/shard_map/pallas_call | solution.py:289
  (15 shorter events, 0.1 us)
Async XLA Ops:
  0.6 3.4 %copy-start.3 = (bf16[128,2048]{1,0:T(8,128)(2,1)S(1)}, bf16[128,2048]{1,0:T(8,128)(2,1)}, u32[]{:S(2)}) copy-start(bf16[128,2048]{1,0:T(8,128)(2,1)} %refs_3_.5) | copy-start | bytes 1572868
  0.6 3.4 %copy-start.2 = (bf16[128,2048]{1,0:T(8,128)(2,1)S(1)}, bf16[128,2048]{1,0:T(8,128)(2,1)}, u32[]{:S(2)}) copy-start(bf16[128,2048]{1,0:T(8,128)(2,1)} %refs_2_.5) | copy-start | bytes 1572868
  0.7 3.4 %copy-start.1 = (bf16[128,2048]{1,0:T(8,128)(2,1)S(1)}, bf16[128,2048]{1,0:T(8,128)(2,1)}, u32[]{:S(2)}) copy-start(bf16[128,2048]{1,0:T(8,128)(2,1)} %refs_1_.5) | copy-start | bytes 1572868
  0.7 3.4 %copy-start = (bf16[128,2048]{1,0:T(8,128)(2,1)S(1)}, bf16[128,2048]{1,0:T(8,128)(2,1)}, u32[]{:S(2)}) copy-start(bf16[128,2048]{1,0:T(8,128)(2,1)} %refs_0_.5) | copy-start | bytes 1572868
  3.5 2.3 %collective-permute-start = (bf16[2,1024,128]{2,1,0:T(8,128)(2,1)}, bf16[2,1024,128]{2,1,0:T(8,128)(2,1)S(1)}, u32[]{:S(2)}, u32[]{:S(2)}) collective-permute-start(bf16[2,1024,128]{2,1,0:T(8,128)(2,1)} %shard_map.76), channel_id=1, source_target_pairs={{0,1},{1,0},{2,3},{3,2},{4,5},{5,4},{6,7},{7,6},{8,9},{9,8},{10,11... | collective-permute-start | bytes 1572872 | tf_op jit(solution)/shard_map/ppermute | solution.py:305
  5.9 14.3 %collective-permute-start.1 = (bf16[2,256,128]{2,1,0:T(8,128)(2,1)S(1)}, bf16[2,256,128]{2,1,0:T(8,128)(2,1)S(1)}, u32[]{:S(2)}, u32[]{:S(2)}) collective-permute-start(bf16[2,256,128]{2,1,0:T(8,128)(2,1)S(1)} %get-tuple-element.32), channel_id=1, source_target_pairs={{0,2},{1,3},{2,0},{3,1},{4,6},{5,7},{6,4},{7,5},{8,10},{9,11},{10,... | collective-permute-start | bytes 393224 | tf_op jit(solution)/shard_map/ppermute | solution.py:305
  8.8 11.4 %collective-permute-start.2 = (bf16[2,256,128]{2,1,0:T(8,128)(2,1)S(1)}, bf16[2,256,128]{2,1,0:T(8,128)(2,1)S(1)}, u32[]{:S(2)}, u32[]{:S(2)}) collective-permute-start(bf16[2,256,128]{2,1,0:T(8,128)(2,1)S(1)} %get-tuple-element.33), channel_id=1, source_target_pairs={{0,4},{1,5},{2,6},{3,7},{4,0},{5,1},{6,2},{7,3},{8,12},{9,13},{10,... | collective-permute-start | bytes 393224 | tf_op jit(solution)/shard_map/ppermute | solution.py:305
  10.3 9.9 %collective-permute-start.3 = (bf16[2,256,128]{2,1,0:T(8,128)(2,1)S(1)}, bf16[2,256,128]{2,1,0:T(8,128)(2,1)S(1)}, u32[]{:S(2)}, u32[]{:S(2)}) collective-permute-start(bf16[2,256,128]{2,1,0:T(8,128)(2,1)S(1)} %get-tuple-element.34), channel_id=1, source_target_pairs={{0,6},{1,7},{2,4},{3,5},{4,2},{5,3},{6,0},{7,1},{8,14},{9,15},{10,... | collective-permute-start | bytes 393224 | tf_op jit(solution)/shard_map/ppermute | solution.py:305
  20.3 4.7 %collective-permute-start.4 = (bf16[256,128]{1,0:T(8,128)(2,1)S(1)}, bf16[256,128]{1,0:T(8,128)(2,1)S(1)}, u32[]{:S(2)}, u32[]{:S(2)}) collective-permute-start(bf16[256,128]{1,0:T(8,128)(2,1)S(1)} %get-tuple-element.47), channel_id=1, source_target_pairs={{0,8},{8,0},{16,24},{24,16},{1,9},{9,1},{17,25},{25,17},{2,10},{10... | collective-permute-start | bytes 196616 | tf_op jit(solution)/shard_map/ppermute | solution.py:305
  22.4 6.7 %collective-permute-start.5 = (bf16[256,128]{1,0:T(8,128)(2,1)S(1)}, bf16[256,128]{1,0:T(8,128)(2,1)S(1)}, u32[]{:S(2)}, u32[]{:S(2)}) collective-permute-start(bf16[256,128]{1,0:T(8,128)(2,1)S(1)} %get-tuple-element.48), channel_id=1, source_target_pairs={{0,16},{8,24},{16,0},{24,8},{1,17},{9,25},{17,1},{25,9},{2,18},{10... | collective-permute-start | bytes 196616 | tf_op jit(solution)/shard_map/ppermute | solution.py:305
  25.0 6.1 %collective-permute-start.6 = (bf16[256,128]{1,0:T(8,128)(2,1)S(1)}, bf16[256,128]{1,0:T(8,128)(2,1)S(1)}, u32[]{:S(2)}, u32[]{:S(2)}) collective-permute-start(bf16[256,128]{1,0:T(8,128)(2,1)S(1)} %get-tuple-element.49), channel_id=1, source_target_pairs={{0,24},{8,16},{16,8},{24,0},{1,25},{9,17},{17,9},{25,1},{2,26},{10... | collective-permute-start | bytes 196616 | tf_op jit(solution)/shard_map/ppermute | solution.py:305
  31.4 5.5 %collective-permute-start.7 = (bf16[2,256,128]{2,1,0:T(8,128)(2,1)S(1)}, bf16[2,256,128]{2,1,0:T(8,128)(2,1)S(1)}, u32[]{:S(2)}, u32[]{:S(2)}) collective-permute-start(bf16[2,256,128]{2,1,0:T(8,128)(2,1)S(1)} %get-tuple-element.51), channel_id=1, source_target_pairs={{0,2},{1,3},{2,0},{3,1},{4,6},{5,7},{6,4},{7,5},{8,10},{9,11},{10,... | collective-permute-start | bytes 393224 | tf_op jit(solution)/shard_map/ppermute | solution.py:305
  33.0 5.1 %collective-permute-start.8 = (bf16[2,256,128]{2,1,0:T(8,128)(2,1)S(1)}, bf16[2,256,128]{2,1,0:T(8,128)(2,1)S(1)}, u32[]{:S(2)}, u32[]{:S(2)}) collective-permute-start(bf16[2,256,128]{2,1,0:T(8,128)(2,1)S(1)} %get-tuple-element.52), channel_id=1, source_target_pairs={{0,4},{1,5},{2,6},{3,7},{4,0},{5,1},{6,2},{7,3},{8,12},{9,13},{10,... | collective-permute-start | bytes 393224 | tf_op jit(solution)/shard_map/ppermute | solution.py:305
  34.5 5.9 %collective-permute-start.9 = (bf16[2,256,128]{2,1,0:T(8,128)(2,1)S(1)}, bf16[2,256,128]{2,1,0:T(8,128)(2,1)S(1)}, u32[]{:S(2)}, u32[]{:S(2)}) collective-permute-start(bf16[2,256,128]{2,1,0:T(8,128)(2,1)S(1)} %get-tuple-element.53), channel_id=1, source_target_pairs={{0,6},{1,7},{2,4},{3,5},{4,2},{5,3},{6,0},{7,1},{8,14},{9,15},{10,... | collective-permute-start | bytes 393224 | tf_op jit(solution)/shard_map/ppermute | solution.py:305
  40.5 2.0 %collective-permute-start.10 = (bf16[2,1024,128]{2,1,0:T(8,128)(2,1)S(1)}, bf16[2,1024,128]{2,1,0:T(8,128)(2,1)S(1)}, u32[]{:S(2)}, u32[]{:S(2)}) collective-permute-start(bf16[2,1024,128]{2,1,0:T(8,128)(2,1)S(1)} %shard_map.81), channel_id=1, source_target_pairs={{0,1},{1,0},{2,3},{3,2},{4,5},{5,4},{6,7},{7,6},{8,9},{9,8},{10,11... | collective-permute-start | bytes 1572872 | tf_op jit(solution)/shard_map/ppermute | solution.py:305

commit v5 on v4

--- a/solution.py
+++ b/solution.py
@@ -27,27 +27,30 @@
     return lax.rem(inner, 2), lax.div(inner, 2)
 
 
-def states_kernel(other, *refs):
-    tokens, (out_ref, held, out, in_sems, out_sems) = refs[:4], refs[4:]
-    half = held.shape[2]
+def states_of(tokens, out, into, cols):
+    q, k, v, d = (ref[:, cols] for ref in tokens)
+    out[0, into] = dot(k, v, 0, 0).astype(BF16)
+    out[1, into] = dot(q, d, 0, 0).astype(BF16)
+
+
+def load_kernel(*refs):
+    tokens, held, (out, sems) = refs[:4], refs[4:8], refs[8:]
+    half = out.shape[1]
     piece = half // PIECES
     near, _ = near_far()
-    side = 1 - near if other else near
+
+    def columns(side, p):
+        return pl.ds(pl.multiple_of(side * half + p * piece, piece), piece)
+
     copies = [
         [
             pltpu.make_async_copy(
-                ref.at[:, pl.ds(pl.multiple_of(side * half + p * piece, piece), piece)],
-                held.at[i, :, pl.ds(p * piece, piece)],
-                in_sems.at[i, p],
+                ref.at[:, columns(side, p)], to.at[:, columns(side, p)], sems.at[turn, p, i]
             )
-            for i, ref in enumerate(tokens)
+            for i, (ref, to) in enumerate(zip(tokens, held))
         ]
+        for turn, side in enumerate((1 - near, near))
         for p in range(PIECES)
-    ]
-    backs = [
-        pltpu.make_async_copy(out.at[:, part], out_ref.at[:, part], out_sems.at[p])
-        for p in range(PIECES)
-        for part in [pl.ds(p * piece, piece)]
     ]
     for group in copies:
         for copy in group:
@@ -55,54 +58,50 @@
     for p, group in enumerate(copies):
         for copy in group:
             copy.wait()
-        for h in range(p * piece // HEAD, (p + 1) * piece // HEAD):
-            cols = slice(h * HEAD, (h + 1) * HEAD)
-            out[0, cols] = dot(held[1, :, cols], held[2, :, cols], 0, 0).astype(BF16)
-            out[1, cols] = dot(held[0, :, cols], held[3, :, cols], 0, 0).astype(BF16)
-        backs[p].start()
-    for back in backs:
-        back.wait()
-
-
-def resident_states_kernel(q_ref, k_ref, v_ref, d_ref, out):
+        if p < PIECES:
+            for h in range(p * piece // HEAD, (p + 1) * piece // HEAD):
+                cols = pl.ds(pl.multiple_of((1 - near) * half + h * HEAD, HEAD), HEAD)
+                states_of(held, out, slice(h * HEAD, (h + 1) * HEAD), cols)
+
+
+def load(tokens):
+    rows, width = tokens[0].shape
+    half = width // 2
+    *held, give = pl.pallas_call(
+        load_kernel,
+        in_specs=[ANY] * 4,
+        out_specs=[VMEM] * 5,
+        out_shape=[pltpu.VMEM((rows, width), BF16)] * 4 + [pltpu.VMEM((2, half, HEAD), BF16)],
+        scratch_shapes=[pltpu.SemaphoreType.DMA((2, PIECES, 4))],
+        cost_estimate=pl.CostEstimate(
+            flops=4 * rows * half * HEAD, bytes_accessed=20 * rows * half, transcendentals=0
+        ),
+        compiler_params=pltpu.CompilerParams(vmem_limit_bytes=4 * MIB),
+    )(*(pltpu.with_memory_space_constraint(x, pltpu.HBM) for x in tokens))
+    return tuple(held), give
+
+
+def keep_kernel(*refs):
+    tokens, out = refs[:4], refs[4]
     half = out.shape[1]
     near, _ = near_far()
     for h in range(half // HEAD):
         cols = pl.ds(pl.multiple_of(near * half + h * HEAD, HEAD), HEAD)
-        into = slice(h * HEAD, (h + 1) * HEAD)
-        out[0, into] = dot(k_ref[:, cols], v_ref[:, cols], 0, 0).astype(BF16)
-        out[1, into] = dot(q_ref[:, cols], d_ref[:, cols], 0, 0).astype(BF16)
-
-
-def half_states(tokens, other):
+        states_of(tokens, out, slice(h * HEAD, (h + 1) * HEAD), cols)
+
+
+def keep_states(tokens):
     rows, width = tokens[0].shape
     half = width // 2
-    cost = pl.CostEstimate(
-        flops=4 * rows * half * HEAD, bytes_accessed=12 * rows * half, transcendentals=0
-    )
-    out = jax.ShapeDtypeStruct((2, half, HEAD), BF16)
-    if not other:
-        return pl.pallas_call(
-            resident_states_kernel,
-            in_specs=[VMEM] * 4,
-            out_specs=VMEM,
-            out_shape=out,
-            cost_estimate=cost,
-            compiler_params=pltpu.CompilerParams(vmem_limit_bytes=4 * MIB),
-        )(*tokens)
-    return pl.pallas_call(
-        functools.partial(states_kernel, other),
-        in_specs=[ANY] * 4,
-        out_specs=ANY,
-        out_shape=out,
-        scratch_shapes=[
-            pltpu.VMEM((4, rows, half), BF16),
-            pltpu.VMEM(out.shape, BF16),
-            pltpu.SemaphoreType.DMA((4, PIECES)),
-            pltpu.SemaphoreType.DMA((PIECES,)),
-        ],
-        cost_estimate=cost,
-        compiler_params=pltpu.CompilerParams(vmem_limit_bytes=60 * MIB),
+    return pl.pallas_call(
+        keep_kernel,
+        in_specs=[VMEM] * 4,
+        out_specs=VMEM,
+        out_shape=jax.ShapeDtypeStruct((2, half, HEAD), BF16),
+        cost_estimate=pl.CostEstimate(
+            flops=4 * rows * half * HEAD, bytes_accessed=12 * rows * half, transcendentals=0
+        ),
+        compiler_params=pltpu.CompilerParams(vmem_limit_bytes=4 * MIB),
     )(*tokens)
 
 
@@ -216,21 +215,28 @@
 
 
 def local_kernel(q_ref, k_ref, v_ref, d_ref, att_ref, gq_ref, gk_ref, gv_ref):
-    rows = q_ref.shape[0]
+    rows, width = q_ref.shape
     at = lax.broadcasted_iota(jnp.int32, (rows, rows), 0)
     to = lax.broadcasted_iota(jnp.int32, (rows, rows), 1)
-    lower, upper = at >= to, at <= to
-
-    def masked(mask, a, b):
-        return jnp.where(mask, dot(a, b, 1, 1), 0.0).astype(BF16)
-
-    for h in range(q_ref.shape[1] // HEAD):
+    lower = at >= to
+
+    def masked(a, b):
+        return jnp.where(lower, dot(a, b, 1, 1), 0.0).astype(BF16)
+
+    def second(cols, a, b):
+        att_ref[:, cols] = dot(a, v_ref[:, cols], 1, 0)
+        gq_ref[:, cols] = dot(b, k_ref[:, cols], 1, 0)
+        gk_ref[:, cols] = dot(b, q_ref[:, cols], 0, 0)
+        gv_ref[:, cols] = dot(a, d_ref[:, cols], 0, 0)
+
+    last = None
+    for h in range(width // HEAD):
         cols = slice(h * HEAD, (h + 1) * HEAD)
-        q, k, v, d = (ref[:, cols] for ref in (q_ref, k_ref, v_ref, d_ref))
-        att_ref[:, cols] = dot(masked(lower, q, k), v, 1, 0)
-        gq_ref[:, cols] = dot(masked(lower, d, v), k, 1, 0)
-        gk_ref[:, cols] = dot(masked(upper, v, d), q, 1, 0)
-        gv_ref[:, cols] = dot(masked(upper, k, q), d, 1, 0)
+        a, b = masked(q_ref[:, cols], k_ref[:, cols]), masked(d_ref[:, cols], v_ref[:, cols])
+        if last:
+            second(*last)
+        last = (cols, a, b)
+    second(*last)
 
 
 def local_part(tokens):
@@ -315,12 +321,13 @@
     count = lax.axis_size("inner")
     outer_count = lax.axis_size("outer")
     scale = float(HEAD * queries.shape[0] * count * outer_count) ** (-0.5)
-    got = swap(half_states(tokens, True), "inner", 1)
-    keep = half_states(tokens, False)
+    tokens, give = load(tokens)
+    got = swap(give, "inner", 1)
+    keep = keep_states(tokens)
     slots = swap_far(pair_slots(keep, got, count // 2))
     slots, local = lax.optimization_barrier((slots, local_part(tokens)))
     sends = group_sends(slots, outer_count)
-    others = [swap(send, "outer", s + 1) for s, send in enumerate(sends)]
+    others = [swap(sends[s], "outer", s + 1) for s in reversed(range(outer_count - 1))][::-1]
     slots = swap_far(scan_slots(slots, others))
     arrived = swap(state_for_neighbour(slots, keep), "inner", 1)
     outs = finish(tokens, local, (*slots, got), scale)

time: 44.1 us -> 38.5 us (0.87)
  Pallas kernels: 16.9 us -> 8.61 us
  waiting for transfers between devices: 13 us -> 16 us
    pallas_call x1, Pallas kernels: 9.82 us -> 2.16 us  [local_part(): pl.pallas_call(local_kernel, in_specs=[VMEM] * 4, out_specs=[VMEM] * 4, o...]
    ppermute x11, waiting for transfers between devices: 13 us -> 16 us  [swap(): lax.ppermute(x, axis, [(i, i ^ bits) for i in range(lax.axis_size(axis))])]
    pallas_call x2, Pallas kernels: 3.31 us -> 2.65 us  [the longest x1 2.18 us: load(): pl.pallas_call(load_kernel, in_specs=[ANY] * 4, out_specs=[VMEM] * 5, out...]
  transfers between devices with their start and end apart: 11 -> 11, of which waited for: 7 -> 10; matrix products, arithmetic and copies ran while one was open for 0% -> 0% of each run, Pallas kernels for 27% -> 11%
where the time goes in v5:
time: 38.5 us; the launch traced here: 38.3 us
  waiting for transfers between devices  16 us (42%)
  starting transfers between devices  13.1 us (34%)
  Pallas kernels  8.61 us (22%)
  between operations  0.7 us (2%)
    ppermute x11, waiting for transfers between devices, swap(): lax.ppermute(x, axis, [(i, i ^ bits) for i in range(lax.axis_size(axis))])  16 us
    ppermute x11, starting transfers between devices, swap(): lax.ppermute(x, axis, [(i, i ^ bits) for i in range(lax.axis_size(axis))])  13.1 us
    pallas_call x2, Pallas kernels, finish(): pl.pallas_call(functools.partial(finish_kernel, scale, slot_count), in_sp...  3.14 us
    pallas_call x1, Pallas kernels, load(): pl.pallas_call(load_kernel, in_specs=[ANY] * 4, out_specs=[VMEM] * 5, out...  2.18 us
    pallas_call x1, Pallas kernels, local_part(): pl.pallas_call(local_kernel, in_specs=[VMEM] * 4, out_specs=[VMEM] * 4, o...  2.16 us
  transfers between devices with their start and end apart: 11, of which 10 were waited for; matrix products, arithmetic and copies ran while one was open for 0% of the time, Pallas kernels for 11%

profile of v5, /device:TPU:0, one launch (start us, length us, event | category | flops | bytes accessed | tf_op | source)
XLA Modules:
  0.0 38.3 jit_solution(6181266353549444493)
XLA Ops:
  0.6 2.2 %shard_map.75 = (bf16[128,2048]{1,0:T(8,128)(2,1)S(1)}, bf16[128,2048]{1,0:T(8,128)(2,1)S(1)}, bf16[128,2048]{1,0:T(8,128)(2,1)S(1)}, bf16[128,2048]{1,0:T(8,128)(2,1)S(1)}, bf16[2,1024,128]{2,1,0:T(8,128)(2,1)S(1)}) custom-call(bf16[128,2048]{1,0:T(8,128)(2,1)} %refs_0_.1, bf16[128,2048]{1,0:T(8,128)(2,1)} %refs_1_.1, bf16[128,2048]{1,0:T(8,128)(2,1)} %refs_2_.1, ...), custom_call_target="tpu_custom_call" | custom-call | flops 67108864 | bytes 2621440 | tf_op jit(solution)/shard_map/pallas_call | solution.py:70
  2.8 0.5 %collective-permute-start = (bf16[2,1024,128]{2,1,0:T(8,128)(2,1)S(1)}, bf16[2,1024,128]{2,1,0:T(8,128)(2,1)S(1)}, u32[]{:S(2)}, u32[]{:S(2)}) collective-permute-start(bf16[2,1024,128]{2,1,0:T(8,128)(2,1)S(1)} %get-tuple-element.40), channel_id=1, source_target_pairs={{0,1},{1,0},{2,3},{3,2},{4,5},{5,4},{6,7},{7,6},{8,9},{9,8},{10,11... | collective-permute-start | bytes 1572872 | tf_op jit(solution)/shard_map/ppermute | solution.py:311
  3.3 0.5 %shard_map.76.keep_ref.refs_4_ = bf16[2,1024,128]{2,1,0:T(8,128)(2,1)S(1)} custom-call(bf16[128,2048]{1,0:T(8,128)(2,1)S(1)} %get-tuple-element.36.refs_0_.q_ref, bf16[128,2048]{1,0:T(8,128)(2,1)S(1)} %get-tuple-element.37.refs_1_.k_ref, bf16[128,2048]{1,0:T(8,128)(2,1)S(1)} %get-tuple-element.38.refs_2_.v_ref, ...), custom_call_target="tpu_custom_call" | custom-call | flops 67108864 | bytes 1572864 | tf_op jit(solution)/shard_map/pallas_call | solution.py:96
  3.8 1.1 %collective-permute-done.got_ref.refs_12_ = bf16[2,1024,128]{2,1,0:T(8,128)(2,1)S(1)} collective-permute-done((bf16[2,1024,128]{2,1,0:T(8,128)(2,1)S(1)}, bf16[2,1024,128]{2,1,0:T(8,128)(2,1)S(1)}, u32[]{:S(2)}, u32[]{:S(2)}) %collective-permute-start) | collective-permute-done | bytes 524320 | tf_op jit(solution)/shard_map/ppermute | solution.py:311
  5.0 2.9 %collective-permute-start.1 = (bf16[2,256,128]{2,1,0:T(8,128)(2,1)S(1)}, bf16[2,256,128]{2,1,0:T(8,128)(2,1)S(1)}, u32[]{:S(2)}, u32[]{:S(2)}) collective-permute-start(bf16[2,256,128]{2,1,0:T(8,128)(2,1)S(1)} %get-tuple-element.42), channel_id=1, source_target_pairs={{0,2},{1,3},{2,0},{3,1},{4,6},{5,7},{6,4},{7,5},{8,10},{9,11},{10,... | collective-permute-start | bytes 393224 | tf_op jit(solution)/shard_map/ppermute | solution.py:311
  7.9 1.5 %collective-permute-start.2 = (bf16[2,256,128]{2,1,0:T(8,128)(2,1)S(1)}, bf16[2,256,128]{2,1,0:T(8,128)(2,1)S(1)}, u32[]{:S(2)}, u32[]{:S(2)}) collective-permute-start(bf16[2,256,128]{2,1,0:T(8,128)(2,1)S(1)} %get-tuple-element.43), channel_id=1, source_target_pairs={{0,4},{1,5},{2,6},{3,7},{4,0},{5,1},{6,2},{7,3},{8,12},{9,13},{10,... | collective-permute-start | bytes 393224 | tf_op jit(solution)/shard_map/ppermute | solution.py:311
  9.5 2.2 %shard_map.78 = (f32[128,2048]{1,0:T(8,128)S(1)}, f32[128,2048]{1,0:T(8,128)S(1)}, f32[128,2048]{1,0:T(8,128)S(1)}, f32[128,2048]{1,0:T(8,128)S(1)}) custom-call(bf16[128,2048]{1,0:T(8,128)(2,1)S(1)} %get-tuple-element.36.refs_0_.q_ref, bf16[128,2048]{1,0:T(8,128)(2,1)S(1)} %get-tuple-element.37.refs_1_.k_ref, ...), custom_call_target="tpu_custom_call" | custom-call | flops 536870912 | bytes 6291456 | tf_op jit(solution)/shard_map/pallas_call | solution.py:244
  11.8 4.2 %collective-permute-done.2.refs_2_ = bf16[2,256,128]{2,1,0:T(8,128)(2,1)S(1)} collective-permute-done((bf16[2,256,128]{2,1,0:T(8,128)(2,1)S(1)}, bf16[2,256,128]{2,1,0:T(8,128)(2,1)S(1)}, u32[]{:S(2)}, u32[]{:S(2)}) %collective-permute-start.2) | collective-permute-done | bytes 131104 | tf_op jit(solution)/shard_map/ppermute | solution.py:311
  16.1 1.6 %collective-permute-start.4 = (bf16[256,128]{1,0:T(8,128)(2,1)S(1)}, bf16[256,128]{1,0:T(8,128)(2,1)S(1)}, u32[]{:S(2)}, u32[]{:S(2)}) collective-permute-start(bf16[256,128]{1,0:T(8,128)(2,1)S(1)} %get-tuple-element.57), channel_id=1, source_target_pairs={{0,8},{8,0},{16,24},{24,16},{1,9},{9,1},{17,25},{25,17},{2,10},{10... | collective-permute-start | bytes 196616 | tf_op jit(solution)/shard_map/ppermute | solution.py:311
  17.7 2.6 %collective-permute-start.5 = (bf16[256,128]{1,0:T(8,128)(2,1)S(1)}, bf16[256,128]{1,0:T(8,128)(2,1)S(1)}, u32[]{:S(2)}, u32[]{:S(2)}) collective-permute-start(bf16[256,128]{1,0:T(8,128)(2,1)S(1)} %get-tuple-element.58), channel_id=1, source_target_pairs={{0,16},{8,24},{16,0},{24,8},{1,17},{9,25},{17,1},{25,9},{2,18},{10... | collective-permute-start | bytes 196616 | tf_op jit(solution)/shard_map/ppermute | solution.py:311
  20.3 0.2 collective-permute-start.6
  20.5 0.5 %collective-permute-done.4.refs_4_ = bf16[256,128]{1,0:T(8,128)(2,1)S(1)} collective-permute-done((bf16[256,128]{1,0:T(8,128)(2,1)S(1)}, bf16[256,128]{1,0:T(8,128)(2,1)S(1)}, u32[]{:S(2)}, u32[]{:S(2)}) %collective-permute-start.4) | collective-permute-done | bytes 65568 | tf_op jit(solution)/shard_map/ppermute | solution.py:311
  21.1 3.2 %collective-permute-done.5.refs_5_ = bf16[256,128]{1,0:T(8,128)(2,1)S(1)} collective-permute-done((bf16[256,128]{1,0:T(8,128)(2,1)S(1)}, bf16[256,128]{1,0:T(8,128)(2,1)S(1)}, u32[]{:S(2)}, u32[]{:S(2)}) %collective-permute-start.5) | collective-permute-done | bytes 65568 | tf_op jit(solution)/shard_map/ppermute | solution.py:311
  24.3 2.1 %collective-permute-done.6.refs_6_ = bf16[256,128]{1,0:T(8,128)(2,1)S(1)} collective-permute-done((bf16[256,128]{1,0:T(8,128)(2,1)S(1)}, bf16[256,128]{1,0:T(8,128)(2,1)S(1)}, u32[]{:S(2)}, u32[]{:S(2)}) %collective-permute-start.6) | collective-permute-done | bytes 65568 | tf_op jit(solution)/shard_map/ppermute | solution.py:311
  26.4 0.3 shard_map.80
  26.7 1.3 %collective-permute-start.7 = (bf16[2,256,128]{2,1,0:T(8,128)(2,1)S(1)}, bf16[2,256,128]{2,1,0:T(8,128)(2,1)S(1)}, u32[]{:S(2)}, u32[]{:S(2)}) collective-permute-start(bf16[2,256,128]{2,1,0:T(8,128)(2,1)S(1)} %get-tuple-element.61), channel_id=1, source_target_pairs={{0,2},{1,3},{2,0},{3,1},{4,6},{5,7},{6,4},{7,5},{8,10},{9,11},{10,... | collective-permute-start | bytes 393224 | tf_op jit(solution)/shard_map/ppermute | solution.py:311
  28.0 0.8 %collective-permute-start.8 = (bf16[2,256,128]{2,1,0:T(8,128)(2,1)S(1)}, bf16[2,256,128]{2,1,0:T(8,128)(2,1)S(1)}, u32[]{:S(2)}, u32[]{:S(2)}) collective-permute-start(bf16[2,256,128]{2,1,0:T(8,128)(2,1)S(1)} %get-tuple-element.62), channel_id=1, source_target_pairs={{0,4},{1,5},{2,6},{3,7},{4,0},{5,1},{6,2},{7,3},{8,12},{9,13},{10,... | collective-permute-start | bytes 393224 | tf_op jit(solution)/shard_map/ppermute | solution.py:311
  28.8 1.4 %collective-permute-start.9 = (bf16[2,256,128]{2,1,0:T(8,128)(2,1)S(1)}, bf16[2,256,128]{2,1,0:T(8,128)(2,1)S(1)}, u32[]{:S(2)}, u32[]{:S(2)}) collective-permute-start(bf16[2,256,128]{2,1,0:T(8,128)(2,1)S(1)} %get-tuple-element.63), channel_id=1, source_target_pairs={{0,6},{1,7},{2,4},{3,5},{4,2},{5,3},{6,0},{7,1},{8,14},{9,15},{10,... | collective-permute-start | bytes 393224 | tf_op jit(solution)/shard_map/ppermute | solution.py:311
  30.3 1.6 %collective-permute-done.7.refs_1_.refs_9_ = bf16[2,256,128]{2,1,0:T(8,128)(2,1)S(1)} collective-permute-done((bf16[2,256,128]{2,1,0:T(8,128)(2,1)S(1)}, bf16[2,256,128]{2,1,0:T(8,128)(2,1)S(1)}, u32[]{:S(2)}, u32[]{:S(2)}) %collective-permute-start.7) | collective-permute-done | bytes 131104 | tf_op jit(solution)/shard_map/ppermute | solution.py:311
  31.9 1.1 %collective-permute-done.8.refs_2_.refs_10_ = bf16[2,256,128]{2,1,0:T(8,128)(2,1)S(1)} collective-permute-done((bf16[2,256,128]{2,1,0:T(8,128)(2,1)S(1)}, bf16[2,256,128]{2,1,0:T(8,128)(2,1)S(1)}, u32[]{:S(2)}, u32[]{:S(2)}) %collective-permute-start.8) | collective-permute-done | bytes 131104 | tf_op jit(solution)/shard_map/ppermute | solution.py:311
  33.0 1.7 %collective-permute-done.9.refs_3_.refs_11_ = bf16[2,256,128]{2,1,0:T(8,128)(2,1)S(1)} collective-permute-done((bf16[2,256,128]{2,1,0:T(8,128)(2,1)S(1)}, bf16[2,256,128]{2,1,0:T(8,128)(2,1)S(1)}, u32[]{:S(2)}, u32[]{:S(2)}) %collective-permute-start.9) | collective-permute-done | bytes 131104 | tf_op jit(solution)/shard_map/ppermute | solution.py:311
  34.9 1.6 %shard_map.82 = (bf16[128,2048]{1,0:T(8,128)(2,1)}, bf16[128,2048]{1,0:T(8,128)(2,1)}, bf16[128,2048]{1,0:T(8,128)(2,1)}, bf16[128,2048]{1,0:T(8,128)(2,1)}) custom-call(bf16[128,2048]{1,0:T(8,128)(2,1)S(1)} %get-tuple-element.36.refs_0_.q_ref, bf16[128,2048]{1,0:T(8,128)(2,1)S(1)} %get-tuple-element.37.refs_1_.k_ref, ...), custom_call_target="tpu_custom_call" | custom-call | flops 134217728 | bytes 4456448 | tf_op jit(solution)/shard_map/pallas_call | solution.py:295
  36.6 0.2 collective-permute-done.10.refs_8_
  36.8 1.5 %shard_map.83 = (bf16[128,2048]{1,0:T(8,128)(2,1)}, bf16[128,2048]{1,0:T(8,128)(2,1)}, bf16[128,2048]{1,0:T(8,128)(2,1)}, bf16[128,2048]{1,0:T(8,128)(2,1)}) custom-call(bf16[128,2048]{1,0:T(8,128)(2,1)S(1)} %get-tuple-element.36.refs_0_.q_ref, ...), custom_call_target="tpu_custom_call", output_to_operand_aliasing={{0}: (9, {}), {1}: (10, {}), {2}: (11, {}), {3}: (12, {})} | custom-call | flops 134217728 | bytes 4456448 | tf_op jit(solution)/shard_map/pallas_call | solution.py:295
  (7 shorter events, 0.6 us)
Async XLA Ops:
  2.8 2.1 %collective-permute-start = (bf16[2,1024,128]{2,1,0:T(8,128)(2,1)S(1)}, bf16[2,1024,128]{2,1,0:T(8,128)(2,1)S(1)}, u32[]{:S(2)}, u32[]{:S(2)}) collective-permute-start(bf16[2,1024,128]{2,1,0:T(8,128)(2,1)S(1)} %get-tuple-element.40), channel_id=1, source_target_pairs={{0,1},{1,0},{2,3},{3,2},{4,5},{5,4},{6,7},{7,6},{8,9},{9,8},{10,11... | collective-permute-start | bytes 1572872 | tf_op jit(solution)/shard_map/ppermute | solution.py:311
  5.0 6.8 %collective-permute-start.1 = (bf16[2,256,128]{2,1,0:T(8,128)(2,1)S(1)}, bf16[2,256,128]{2,1,0:T(8,128)(2,1)S(1)}, u32[]{:S(2)}, u32[]{:S(2)}) collective-permute-start(bf16[2,256,128]{2,1,0:T(8,128)(2,1)S(1)} %get-tuple-element.42), channel_id=1, source_target_pairs={{0,2},{1,3},{2,0},{3,1},{4,6},{5,7},{6,4},{7,5},{8,10},{9,11},{10,... | collective-permute-start | bytes 393224 | tf_op jit(solution)/shard_map/ppermute | solution.py:311
  7.9 8.1 %collective-permute-start.2 = (bf16[2,256,128]{2,1,0:T(8,128)(2,1)S(1)}, bf16[2,256,128]{2,1,0:T(8,128)(2,1)S(1)}, u32[]{:S(2)}, u32[]{:S(2)}) collective-permute-start(bf16[2,256,128]{2,1,0:T(8,128)(2,1)S(1)} %get-tuple-element.43), channel_id=1, source_target_pairs={{0,4},{1,5},{2,6},{3,7},{4,0},{5,1},{6,2},{7,3},{8,12},{9,13},{10,... | collective-permute-start | bytes 393224 | tf_op jit(solution)/shard_map/ppermute | solution.py:311
  9.4 6.6 %collective-permute-start.3 = (bf16[2,256,128]{2,1,0:T(8,128)(2,1)S(1)}, bf16[2,256,128]{2,1,0:T(8,128)(2,1)S(1)}, u32[]{:S(2)}, u32[]{:S(2)}) collective-permute-start(bf16[2,256,128]{2,1,0:T(8,128)(2,1)S(1)} %get-tuple-element.44), channel_id=1, source_target_pairs={{0,6},{1,7},{2,4},{3,5},{4,2},{5,3},{6,0},{7,1},{8,14},{9,15},{10,... | collective-permute-start | bytes 393224 | tf_op jit(solution)/shard_map/ppermute | solution.py:311
  16.1 5.0 %collective-permute-start.4 = (bf16[256,128]{1,0:T(8,128)(2,1)S(1)}, bf16[256,128]{1,0:T(8,128)(2,1)S(1)}, u32[]{:S(2)}, u32[]{:S(2)}) collective-permute-start(bf16[256,128]{1,0:T(8,128)(2,1)S(1)} %get-tuple-element.57), channel_id=1, source_target_pairs={{0,8},{8,0},{16,24},{24,16},{1,9},{9,1},{17,25},{25,17},{2,10},{10... | collective-permute-start | bytes 196616 | tf_op jit(solution)/shard_map/ppermute | solution.py:311
  17.7 6.6 %collective-permute-start.5 = (bf16[256,128]{1,0:T(8,128)(2,1)S(1)}, bf16[256,128]{1,0:T(8,128)(2,1)S(1)}, u32[]{:S(2)}, u32[]{:S(2)}) collective-permute-start(bf16[256,128]{1,0:T(8,128)(2,1)S(1)} %get-tuple-element.58), channel_id=1, source_target_pairs={{0,16},{8,24},{16,0},{24,8},{1,17},{9,25},{17,1},{25,9},{2,18},{10... | collective-permute-start | bytes 196616 | tf_op jit(solution)/shard_map/ppermute | solution.py:311
  20.3 6.1 %collective-permute-start.6 = (bf16[256,128]{1,0:T(8,128)(2,1)S(1)}, bf16[256,128]{1,0:T(8,128)(2,1)S(1)}, u32[]{:S(2)}, u32[]{:S(2)}) collective-permute-start(bf16[256,128]{1,0:T(8,128)(2,1)S(1)} %get-tuple-element.59), channel_id=1, source_target_pairs={{0,24},{8,16},{16,8},{24,0},{1,25},{9,17},{17,9},{25,1},{2,26},{10... | collective-permute-start | bytes 196616 | tf_op jit(solution)/shard_map/ppermute | solution.py:311
  26.7 5.2 %collective-permute-start.7 = (bf16[2,256,128]{2,1,0:T(8,128)(2,1)S(1)}, bf16[2,256,128]{2,1,0:T(8,128)(2,1)S(1)}, u32[]{:S(2)}, u32[]{:S(2)}) collective-permute-start(bf16[2,256,128]{2,1,0:T(8,128)(2,1)S(1)} %get-tuple-element.61), channel_id=1, source_target_pairs={{0,2},{1,3},{2,0},{3,1},{4,6},{5,7},{6,4},{7,5},{8,10},{9,11},{10,... | collective-permute-start | bytes 393224 | tf_op jit(solution)/shard_map/ppermute | solution.py:311
  28.0 5.0 %collective-permute-start.8 = (bf16[2,256,128]{2,1,0:T(8,128)(2,1)S(1)}, bf16[2,256,128]{2,1,0:T(8,128)(2,1)S(1)}, u32[]{:S(2)}, u32[]{:S(2)}) collective-permute-start(bf16[2,256,128]{2,1,0:T(8,128)(2,1)S(1)} %get-tuple-element.62), channel_id=1, source_target_pairs={{0,4},{1,5},{2,6},{3,7},{4,0},{5,1},{6,2},{7,3},{8,12},{9,13},{10,... | collective-permute-start | bytes 393224 | tf_op jit(solution)/shard_map/ppermute | solution.py:311
  28.8 5.9 %collective-permute-start.9 = (bf16[2,256,128]{2,1,0:T(8,128)(2,1)S(1)}, bf16[2,256,128]{2,1,0:T(8,128)(2,1)S(1)}, u32[]{:S(2)}, u32[]{:S(2)}) collective-permute-start(bf16[2,256,128]{2,1,0:T(8,128)(2,1)S(1)} %get-tuple-element.63), channel_id=1, source_target_pairs={{0,6},{1,7},{2,4},{3,5},{4,2},{5,3},{6,0},{7,1},{8,14},{9,15},{10,... | collective-permute-start | bytes 393224 | tf_op jit(solution)/shard_map/ppermute | solution.py:311
  34.8 2.0 %collective-permute-start.10 = (bf16[2,1024,128]{2,1,0:T(8,128)(2,1)S(1)}, bf16[2,1024,128]{2,1,0:T(8,128)(2,1)S(1)}, u32[]{:S(2)}, u32[]{:S(2)}) collective-permute-start(bf16[2,1024,128]{2,1,0:T(8,128)(2,1)S(1)} %shard_map.81), channel_id=1, source_target_pairs={{0,1},{1,0},{2,3},{3,2},{4,5},{5,4},{6,7},{7,6},{8,9},{9,8},{10,11... | collective-permute-start | bytes 1572872 | tf_op jit(solution)/shard_map/ppermute | solution.py:311

commit v6 on v5

v6 whole, which is shorter than its diff:
```python
import functools

import jax
import jax.numpy as jnp
from jax import lax
from jax.experimental import pallas as pl
from jax.experimental.pallas import tpu as pltpu
from jax.sharding import PartitionSpec as P

HEAD = 128
PIECES = 4
MIB = 1024 * 1024
ANY = pl.BlockSpec(memory_space=pl.ANY)
VMEM = pl.BlockSpec(memory_space=pltpu.VMEM)
BF16 = jnp.bfloat16
F32 = jnp.float32
SMALL = pltpu.CompilerParams(vmem_limit_bytes=4 * MIB)


def dot(a, b, over_a, over_b):
    return lax.dot_general(
        a, b, (((over_a,), (over_b,)), ((), ())), preferred_element_type=F32
    )


def near_far():
    inner = lax.axis_index("inner")
    return lax.rem(inner, 2), lax.div(inner, 2)


def outer_product(a, b, cols):
    return dot(a[:, cols], b[:, cols], 0, 0).astype(BF16)


def head_columns(side, half, h):
    return pl.ds(pl.multiple_of(side * half + h * HEAD, HEAD), HEAD)


def load_kernel(*refs):
    tokens, held, (out, sems) = refs[:4], refs[4:8], refs[8:]
    half = out.shape[0]
    piece = half // PIECES
    near, _ = near_far()
    other = 1 - near

    def copy(i, side, p):
        cols = pl.ds(pl.multiple_of(side * half + p * piece, piece), piece)
        return pltpu.make_async_copy(
            tokens[i].at[:, cols], held[i].at[:, cols], sems.at[i, int(side is near), p]
        )

    first = [[copy(i, other, p) for i in (1, 2)] for p in range(PIECES)]
    rest = [copy(i, other, p) for i in (0, 3) for p in range(PIECES)]
    rest += [copy(i, near, p) for i in range(4) for p in range(PIECES)]
    for c in sum(first, []) + rest:
        c.start()
    for p, group in enumerate(first):
        for c in group:
            c.wait()
        for h in range(p * piece // HEAD, (p + 1) * piece // HEAD):
            out[h * HEAD : (h + 1) * HEAD] = outer_product(
                held[1], held[2], head_columns(other, half, h)
            )
    for c in rest:
        c.wait()


def load(tokens):
    rows, width = tokens[0].shape
    half = width // 2
    *held, give = pl.pallas_call(
        load_kernel,
        name="load",
        in_specs=[ANY] * 4,
        out_specs=[VMEM] * 5,
        out_shape=[pltpu.VMEM((rows, width), BF16)] * 4 + [pltpu.VMEM((half, HEAD), BF16)],
        scratch_shapes=[pltpu.SemaphoreType.DMA((4, 2, PIECES))],
        cost_estimate=pl.CostEstimate(
            flops=2 * rows * half * HEAD, bytes_accessed=20 * rows * half, transcendentals=0
        ),
        compiler_params=SMALL,
    )(*(pltpu.with_memory_space_constraint(x, pltpu.HBM) for x in tokens))
    return tuple(held), give


def states_kernel(own, *refs):
    half = refs[-1].shape[0]
    near, _ = near_far()
    side = near if own else 1 - near
    outs = refs[len(refs) * 2 // 3 :]
    for n, out in enumerate(outs):
        for h in range(half // HEAD):
            out[h * HEAD : (h + 1) * HEAD] = outer_product(
                refs[2 * n], refs[2 * n + 1], head_columns(side, half, h)
            )


def states(own, *pairs):
    rows, width = pairs[0][0].shape
    half = width // 2
    return pl.pallas_call(
        functools.partial(states_kernel, own),
        name="states",
        in_specs=[VMEM] * (2 * len(pairs)),
        out_specs=[VMEM] * len(pairs),
        out_shape=[jax.ShapeDtypeStruct((half, HEAD), BF16)] * len(pairs),
        cost_estimate=pl.CostEstimate(
            flops=2 * rows * half * HEAD * len(pairs),
            bytes_accessed=6 * rows * half * len(pairs),
            transcendentals=0,
        ),
        compiler_params=SMALL,
    )(*(x for pair in pairs for x in pair))


def pair_kernel(keep_ref, got_ref, *slots):
    depth = slots[0].shape[0]
    _, far = near_far()
    for s, slot in enumerate(slots):
        part = pl.ds(pl.multiple_of((far ^ s) * depth, depth), depth)
        slot[...] = (keep_ref[part].astype(F32) + got_ref[part].astype(F32)).astype(BF16)


def pair_slots(keep, got, far_count):
    slot = jax.ShapeDtypeStruct((keep.shape[0] // far_count, HEAD), BF16)
    return pl.pallas_call(
        pair_kernel,
        name="pair",
        in_specs=[VMEM] * 2,
        out_specs=[VMEM] * far_count,
        out_shape=[slot] * far_count,
        compiler_params=SMALL,
    )(keep, got)


def total_kernel(*refs):
    total = refs[0][...].astype(F32)
    for slot in refs[1:-1]:
        total += slot[...].astype(F32)
    refs[-1][...] = total.astype(BF16)


def total_of(slots):
    return pl.pallas_call(
        total_kernel,
        name="total",
        in_specs=[VMEM] * len(slots),
        out_specs=VMEM,
        out_shape=jax.ShapeDtypeStruct(slots[0].shape, BF16),
        compiler_params=SMALL,
    )(*slots)


def scan_kernel(later, far_count, *refs):
    slots, others, outs = refs[:far_count], refs[far_count:-far_count], refs[-far_count:]
    _, far = near_far()
    base = jnp.zeros(slots[0].shape, F32)
    for other in others:
        base += other[...].astype(F32)
    terms = [slot[...].astype(F32) for slot in slots]
    for s, out in enumerate(outs):
        total = base
        for t, term in enumerate(terms):
            if s != t:
                wanted = (far ^ t) > (far ^ s) if later else (far ^ t) < (far ^ s)
                total += jnp.where(wanted, term, 0.0)
        out[...] = total.astype(BF16)


def scan_slots(later, slots, others):
    far_count, slot = len(slots), jax.ShapeDtypeStruct(slots[0].shape, BF16)
    return pl.pallas_call(
        functools.partial(scan_kernel, later, far_count),
        name="scan",
        in_specs=[VMEM] * (far_count + len(others)),
        out_specs=[VMEM] * far_count,
        out_shape=[slot] * far_count,
        compiler_params=SMALL,
    )(*slots, *others)


def expand(slots, out, extra, wanted):
    depth = slots[0].shape[0]
    _, far = near_far()
    for s, slot in enumerate(slots):
        part = pl.ds(pl.multiple_of((far ^ s) * depth, depth), depth)

        @pl.when(wanted)
        def _():
            out[part] = (slot[...].astype(F32) + extra[part].astype(F32)).astype(BF16)

        @pl.when(jnp.logical_not(wanted))
        def _():
            out[part] = slot[...]


def theirs_kernel(later, *refs):
    slots, (keep, out) = refs[:-2], refs[-2:]
    near, _ = near_far()
    expand(slots, out, keep, near == int(later))


def state_for_neighbour(later, slots, keep):
    return pl.pallas_call(
        functools.partial(theirs_kernel, later),
        name="theirs",
        in_specs=[VMEM] * (len(slots) + 1),
        out_specs=VMEM,
        out_shape=jax.ShapeDtypeStruct(keep.shape, BF16),
        compiler_params=SMALL,
    )(*slots, keep)


def local_kernel(q_ref, k_ref, v_ref, d_ref, att_ref, gq_ref, gv_ref, gk_ref):
    rows, width = q_ref.shape
    at = lax.broadcasted_iota(jnp.int32, (rows, rows), 0)
    to = lax.broadcasted_iota(jnp.int32, (rows, rows), 1)
    lower = at >= to

    def masked(a, b):
        return jnp.where(lower, dot(a, b, 1, 1), 0.0).astype(BF16)

    def second(cols, a, b):
        att_ref[:, cols] = dot(a, v_ref[:, cols], 1, 0)
        gq_ref[:, cols] = dot(b, k_ref[:, cols], 1, 0)
        gv_ref[:, cols] = dot(a, d_ref[:, cols], 0, 0)
        gk_ref[:, cols] = dot(b, q_ref[:, cols], 0, 0)

    last = None
    for h in range(width // HEAD):
        cols = slice(h * HEAD, (h + 1) * HEAD)
        a, b = masked(q_ref[:, cols], k_ref[:, cols]), masked(d_ref[:, cols], v_ref[:, cols])
        if last:
            second(*last)
        last = (cols, a, b)
    second(*last)


def local_part(tokens):
    rows, width = tokens[0].shape
    return pl.pallas_call(
        local_kernel,
        name="local",
        in_specs=[VMEM] * 4,
        out_specs=[VMEM] * 4,
        out_shape=[jax.ShapeDtypeStruct((rows, width), F32)] * 4,
        cost_estimate=pl.CostEstimate(
            flops=16 * rows * width * HEAD, bytes_accessed=24 * rows * width, transcendentals=0
        ),
        compiler_params=SMALL,
    )(*tokens)


def finish_kernel(scale, later, slot_count, *refs):
    a_ref, b_ref, *local = refs[:4]
    refs = refs[4:]
    held, sems = refs[-2:]
    near, _ = near_far()
    if slot_count:
        outs, state, side = refs[-5:-3], refs[-3], near
        expand(refs[:slot_count], state, refs[slot_count], near == 1 - int(later))
    else:
        outs, state, side = refs[-4:-2], refs[0], 1 - near
    half = held.shape[2]
    piece = half // PIECES
    copies = []
    for p in range(PIECES):
        for h in range(p * piece // HEAD, (p + 1) * piece // HEAD):
            into, cols = slice(h * HEAD, (h + 1) * HEAD), head_columns(side, half, h)
            x = state[into]
            parts = dot(a_ref[:, cols], x, 1, 0), dot(b_ref[:, cols], x, 1, 1)
            for i, part in enumerate(parts):
                held[i, :, into] = (scale * (part + local[i][:, cols])).astype(BF16)
        for i, out in enumerate(outs):
            there = pl.ds(pl.multiple_of(side * half + p * piece, piece), piece)
            copy = pltpu.make_async_copy(
                held.at[i, :, pl.ds(p * piece, piece)], out.at[:, there], sems.at[i, p]
            )
            copy.start()
            copies.append(copy)
    for copy in copies:
        copy.wait()


def finish(later, tokens, local, states, scale, before=()):
    rows, width = tokens[0].shape
    half = width // 2
    slot_count = 0 if before else len(states) - 1
    out = jax.ShapeDtypeStruct((rows, width), BF16)
    scratch = [pltpu.VMEM((half, HEAD), BF16)] if slot_count else []
    return pl.pallas_call(
        functools.partial(finish_kernel, scale, later, slot_count),
        name="finish",
        in_specs=[VMEM] * (4 + len(states)) + [ANY] * len(before),
        out_specs=[ANY] * 2,
        out_shape=[out] * 2,
        scratch_shapes=scratch
        + [pltpu.VMEM((2, rows, half), BF16), pltpu.SemaphoreType.DMA((2, PIECES))],
        input_output_aliases={4 + len(states) + i: i for i in range(len(before))},
        cost_estimate=pl.CostEstimate(
            flops=2 * rows * width * HEAD, bytes_accessed=9 * rows * width, transcendentals=0
        ),
        compiler_params=SMALL,
    )(*tokens, *local, *states, *before)


def swap(x, axis, bits):
    return lax.ppermute(x, axis, [(i, i ^ bits) for i in range(lax.axis_size(axis))])


def swap_far(slots):
    return [slots[0]] + [swap(slots[s], "inner", 2 * s) for s in range(1, len(slots))]


def from_groups(later, total):
    count = lax.axis_size("outer")
    pairs = [[(z, z ^ s) for z in range(count) if (z ^ s < z) == later] for s in range(1, count)]
    return [lax.ppermute(total, "outer", p) for p in pairs]


def body(queries, keys, values, cotangent):
    count = lax.axis_size("inner")
    outer_count = lax.axis_size("outer")
    scale = float(HEAD * queries.shape[0] * count * outer_count) ** (-0.5)
    tokens, give_s = load((queries, keys, values, cotangent))
    q, k, v, d = tokens
    got_s = swap(give_s, "inner", 1)
    got_g = swap(*states(False, (q, d)), "inner", 1)
    keep_s, keep_g = states(True, (k, v), (q, d))
    slots_s = swap_far(pair_slots(keep_s, got_s, count // 2))
    slots_g = swap_far(pair_slots(keep_g, got_g, count // 2))
    others_s = from_groups(False, total_of(slots_s))
    others_g = from_groups(True, total_of(slots_g))
    others_s, local = lax.optimization_barrier((others_s, local_part(tokens)))
    slots_s = swap_far(scan_slots(False, slots_s, others_s))
    slots_g = swap_far(scan_slots(True, slots_g, others_g))
    arrived_s = swap(state_for_neighbour(False, slots_s, keep_s), "inner", 1)
    outs_s = finish(False, (q, d), local[:2], (*slots_s, got_s), scale)
    outs_s = finish(False, (q, d), local[:2], (arrived_s,), scale, outs_s)
    slots_g, (att, gq) = lax.optimization_barrier((slots_g, tuple(outs_s)))
    arrived_g = swap(state_for_neighbour(True, slots_g, keep_g), "inner", 1)
    outs_g = finish(True, (k, v), local[2:], (*slots_g, got_g), scale)
    gv, gk = finish(True, (k, v), local[2:], (arrived_g,), scale, outs_g)
    return att, gq, gk, gv


def solution(mesh):
    spec = P(("outer", "inner"), None)
    return jax.shard_map(
        body, mesh=mesh, in_specs=(spec,) * 4, out_specs=(spec,) * 4, check_vma=False
    )
```

time: 38.5 us -> 61.9 us (1.61)
  starting transfers between devices: 13.1 us -> 29 us
  waiting for transfers between devices: 16 us -> 21.4 us
  Pallas kernels: 8.61 us -> 10.3 us
    ppermute x0 -> x6, starting transfers between devices: none -> 13.2 us  [from_groups(): return [lax.ppermute(total, 'outer', p) for p in pairs]]
    ppermute x0 -> x6, waiting for transfers between devices: none -> 7.95 us  [from_groups(): return [lax.ppermute(total, 'outer', p) for p in pairs]]
    ppermute x11 -> x16, starting transfers between devices: 13.1 us -> 15.9 us  [swap(): lax.ppermute(x, axis, [(i, i ^ bits) for i in range(lax.axis_size(axis))])]
    ppermute x11 -> x16, waiting for transfers between devices: 16 us -> 13.5 us  [swap(): lax.ppermute(x, axis, [(i, i ^ bits) for i in range(lax.axis_size(axis))])]
    pallas_call x9 -> x16, Pallas kernels: 8.61 us -> 10.3 us  [the longest x4 4.71 us: finish(): pl.pallas_call(functools.partial(finish_kernel, scale, later, slot_count)...]
  transfers between devices with their start and end apart: 11 -> 22, of which waited for: 10 -> 15; matrix products, arithmetic and copies ran while one was open for 0% -> 0% of each run, Pallas kernels for 11% -> 11%
where the time goes in v6:
time: 61.9 us; the launch traced here: 61.6 us
  starting transfers between devices  29 us (47%)
  waiting for transfers between devices  21.4 us (35%)
  Pallas kernels  10.3 us (17%)
  between operations  0.86 us (1%)
    ppermute x16, starting transfers between devices, swap(): lax.ppermute(x, axis, [(i, i ^ bits) for i in range(lax.axis_size(axis))])  15.9 us
    ppermute x16, waiting for transfers between devices, swap(): lax.ppermute(x, axis, [(i, i ^ bits) for i in range(lax.axis_size(axis))])  13.5 us
    ppermute x6, starting transfers between devices, from_groups(): return [lax.ppermute(total, 'outer', p) for p in pairs]  13.2 us
    ppermute x6, waiting for transfers between devices, from_groups(): return [lax.ppermute(total, 'outer', p) for p in pairs]  7.95 us
    pallas_call x4, Pallas kernels, finish(): pl.pallas_call(functools.partial(finish_kernel, scale, later, slot_count)...  4.71 us
    pallas_call x1, Pallas kernels, local_part(): pl.pallas_call(local_kernel, name='local', in_specs=[VMEM] * 4, out_specs...  2.15 us
    pallas_call x1, Pallas kernels, load(): pl.pallas_call(load_kernel, name='load', in_specs=[ANY] * 4, out_specs=[V...  2.06 us
  transfers between devices with their start and end apart: 22, of which 15 were waited for; matrix products, arithmetic and copies ran while one was open for 0% of the time, Pallas kernels for 11%

profile of v6, /device:TPU:0, one launch (start us, length us, event | category | flops | bytes accessed | tf_op | source)
XLA Modules:
  0.0 61.6 jit_solution(10130020276012816509)
XLA Ops:
  0.6 2.1 %load.1 = (bf16[128,2048]{1,0:T(8,128)(2,1)S(1)}, bf16[128,2048]{1,0:T(8,128)(2,1)S(1)}, bf16[128,2048]{1,0:T(8,128)(2,1)S(1)}, bf16[128,2048]{1,0:T(8,128)(2,1)S(1)}, bf16[1024,128]{1,0:T(8,128)(2,1)S(1)}) custom-call(bf16[128,2048]{1,0:T(8,128)(2,1)} %refs_0_.1, bf16[128,2048]{1,0:T(8,128)(2,1)} %refs_1_.1, bf16[128,2048]{1,0:T(8,128)(2,1)} %refs_2_.1, ...), custom_call_target="tpu_custom_call" | custom-call | flops 33554432 | bytes 2621440 | tf_op jit(solution)/shard_map/load/pallas_call | solution.py:71
  4.4 2.9 %collective-permute-start.11 = (bf16[256,128]{1,0:T(8,128)(2,1)S(1)}, bf16[256,128]{1,0:T(8,128)(2,1)S(1)}, u32[]{:S(2)}, u32[]{:S(2)}) collective-permute-start(bf16[256,128]{1,0:T(8,128)(2,1)S(1)} %get-tuple-element.68), channel_id=1, source_target_pairs={{0,2},{1,3},{2,0},{3,1},{4,6},{5,7},{6,4},{7,5},{8,10},{9,11},{10,... | collective-permute-start | bytes 196616 | tf_op jit(solution)/shard_map/ppermute | solution.py:308
  7.4 1.5 %collective-permute-start.12 = (bf16[256,128]{1,0:T(8,128)(2,1)S(1)}, bf16[256,128]{1,0:T(8,128)(2,1)S(1)}, u32[]{:S(2)}, u32[]{:S(2)}) collective-permute-start(bf16[256,128]{1,0:T(8,128)(2,1)S(1)} %get-tuple-element.69), channel_id=1, source_target_pairs={{0,4},{1,5},{2,6},{3,7},{4,0},{5,1},{6,2},{7,3},{8,12},{9,13},{10,... | collective-permute-start | bytes 196616 | tf_op jit(solution)/shard_map/ppermute | solution.py:308
  9.8 1.9 %collective-permute-done.12.refs_2_ = bf16[256,128]{1,0:T(8,128)(2,1)S(1)} collective-permute-done((bf16[256,128]{1,0:T(8,128)(2,1)S(1)}, bf16[256,128]{1,0:T(8,128)(2,1)S(1)}, u32[]{:S(2)}, u32[]{:S(2)}) %collective-permute-start.12) | collective-permute-done | bytes 65568 | tf_op jit(solution)/shard_map/ppermute | solution.py:308
  11.6 2.4 %collective-permute-done.13.refs_3_ = bf16[256,128]{1,0:T(8,128)(2,1)S(1)} collective-permute-done((bf16[256,128]{1,0:T(8,128)(2,1)S(1)}, bf16[256,128]{1,0:T(8,128)(2,1)S(1)}, u32[]{:S(2)}, u32[]{:S(2)}) %collective-permute-start.13) | collective-permute-done | bytes 65568 | tf_op jit(solution)/shard_map/ppermute | solution.py:308
  14.1 3.5 %collective-permute-start.14 = (bf16[256,128]{1,0:T(8,128)(2,1)S(1)}, bf16[256,128]{1,0:T(8,128)(2,1)S(1)}, u32[]{:S(2)}, u32[]{:S(2)}) collective-permute-start(bf16[256,128]{1,0:T(8,128)(2,1)S(1)} %total.3), channel_id=1, source_target_pairs={{0,8},{16,24},{1,9},{17,25},{2,10},{18,26},{3,11},{19,27},{4,12},{... | collective-permute-start | bytes 196616 | tf_op jit(solution)/shard_map/ppermute | solution.py:318
  17.6 4.5 %collective-permute-start.15 = (bf16[256,128]{1,0:T(8,128)(2,1)S(1)}, bf16[256,128]{1,0:T(8,128)(2,1)S(1)}, u32[]{:S(2)}, u32[]{:S(2)}) collective-permute-start(bf16[256,128]{1,0:T(8,128)(2,1)S(1)} %total.3), channel_id=1, source_target_pairs={{0,16},{8,24},{1,17},{9,25},{2,18},{10,26},{3,19},{11,27},{4,20},{... | collective-permute-start | bytes 196616 | tf_op jit(solution)/shard_map/ppermute | solution.py:318
  22.1 1.3 %collective-permute-start.16 = (bf16[256,128]{1,0:T(8,128)(2,1)S(1)}, bf16[256,128]{1,0:T(8,128)(2,1)S(1)}, u32[]{:S(2)}, u32[]{:S(2)}) collective-permute-start(bf16[256,128]{1,0:T(8,128)(2,1)S(1)} %total.3), channel_id=1, source_target_pairs={{0,24},{8,16},{1,25},{9,17},{2,26},{10,18},{3,27},{11,19},{4,28},{... | collective-permute-start | bytes 196616 | tf_op jit(solution)/shard_map/ppermute | solution.py:318
  23.4 2.2 %local.1 = (f32[128,2048]{1,0:T(8,128)S(1)}, f32[128,2048]{1,0:T(8,128)S(1)}, f32[128,2048]{1,0:T(8,128)S(1)}, f32[128,2048]{1,0:T(8,128)S(1)}) custom-call(bf16[128,2048]{1,0:T(8,128)(2,1)S(1)} %get-tuple-element.54.refs_2_.refs_0_.q_ref, bf16[128,2048]{1,0:T(8,128)(2,1)S(1)} %get-tuple-element.52.refs_0_.k_ref, ...), custom_call_target="tpu_custom_call" | custom-call | flops 536870912 | bytes 6291456 | tf_op jit(solution)/shard_map/local/pallas_call | solution.py:241
  26.9 2.4 %collective-permute-start.19 = (bf16[256,128]{1,0:T(8,128)(2,1)S(1)}, bf16[256,128]{1,0:T(8,128)(2,1)S(1)}, u32[]{:S(2)}, u32[]{:S(2)}) collective-permute-start(bf16[256,128]{1,0:T(8,128)(2,1)S(1)} %get-tuple-element.83), channel_id=1, source_target_pairs={{0,6},{1,7},{2,4},{3,5},{4,2},{5,3},{6,0},{7,1},{8,14},{9,15},{10,... | collective-permute-start | bytes 196616 | tf_op jit(solution)/shard_map/ppermute | solution.py:308
  30.6 1.4 %collective-permute-done.19.refs_3_.refs_7_ = bf16[256,128]{1,0:T(8,128)(2,1)S(1)} collective-permute-done((bf16[256,128]{1,0:T(8,128)(2,1)S(1)}, bf16[256,128]{1,0:T(8,128)(2,1)S(1)}, u32[]{:S(2)}, u32[]{:S(2)}) %collective-permute-start.19) | collective-permute-done | bytes 65568 | tf_op jit(solution)/shard_map/ppermute | solution.py:308
  32.3 1.6 %collective-permute-start.1 = (bf16[256,128]{1,0:T(8,128)(2,1)S(1)}, bf16[256,128]{1,0:T(8,128)(2,1)S(1)}, u32[]{:S(2)}, u32[]{:S(2)}) collective-permute-start(bf16[256,128]{1,0:T(8,128)(2,1)S(1)} %get-tuple-element.58), channel_id=1, source_target_pairs={{0,2},{1,3},{2,0},{3,1},{4,6},{5,7},{6,4},{7,5},{8,10},{9,11},{10,... | collective-permute-start | bytes 196616 | tf_op jit(solution)/shard_map/ppermute | solution.py:308
  33.8 1.5 %collective-permute-start.2 = (bf16[256,128]{1,0:T(8,128)(2,1)S(1)}, bf16[256,128]{1,0:T(8,128)(2,1)S(1)}, u32[]{:S(2)}, u32[]{:S(2)}) collective-permute-start(bf16[256,128]{1,0:T(8,128)(2,1)S(1)} %get-tuple-element.59), channel_id=1, source_target_pairs={{0,4},{1,5},{2,6},{3,7},{4,0},{5,1},{6,2},{7,3},{8,12},{9,13},{10,... | collective-permute-start | bytes 196616 | tf_op jit(solution)/shard_map/ppermute | solution.py:308
  36.8 1.3 %collective-permute-done.2.refs_2_ = bf16[256,128]{1,0:T(8,128)(2,1)S(1)} collective-permute-done((bf16[256,128]{1,0:T(8,128)(2,1)S(1)}, bf16[256,128]{1,0:T(8,128)(2,1)S(1)}, u32[]{:S(2)}, u32[]{:S(2)}) %collective-permute-start.2) | collective-permute-done | bytes 65568 | tf_op jit(solution)/shard_map/ppermute | solution.py:308
  38.1 2.4 %collective-permute-done.3.refs_3_ = bf16[256,128]{1,0:T(8,128)(2,1)S(1)} collective-permute-done((bf16[256,128]{1,0:T(8,128)(2,1)S(1)}, bf16[256,128]{1,0:T(8,128)(2,1)S(1)}, u32[]{:S(2)}, u32[]{:S(2)}) %collective-permute-start.3) | collective-permute-done | bytes 65568 | tf_op jit(solution)/shard_map/ppermute | solution.py:308
  40.6 1.3 %collective-permute-start.4 = (bf16[256,128]{1,0:T(8,128)(2,1)S(1)}, bf16[256,128]{1,0:T(8,128)(2,1)S(1)}, u32[]{:S(2)}, u32[]{:S(2)}) collective-permute-start(bf16[256,128]{1,0:T(8,128)(2,1)S(1)} %total.2), channel_id=1, source_target_pairs={{8,0},{24,16},{9,1},{25,17},{10,2},{26,18},{11,3},{27,19},{12,4},{... | collective-permute-start | bytes 196616 | tf_op jit(solution)/shard_map/ppermute | solution.py:318
  41.9 1.3 %collective-permute-start.5 = (bf16[256,128]{1,0:T(8,128)(2,1)S(1)}, bf16[256,128]{1,0:T(8,128)(2,1)S(1)}, u32[]{:S(2)}, u32[]{:S(2)}) collective-permute-start(bf16[256,128]{1,0:T(8,128)(2,1)S(1)} %total.2), channel_id=1, source_target_pairs={{16,0},{24,8},{17,1},{25,9},{18,2},{26,10},{19,3},{27,11},{20,4},{... | collective-permute-start | bytes 196616 | tf_op jit(solution)/shard_map/ppermute | solution.py:318
  43.2 1.3 %collective-permute-start.6 = (bf16[256,128]{1,0:T(8,128)(2,1)S(1)}, bf16[256,128]{1,0:T(8,128)(2,1)S(1)}, u32[]{:S(2)}, u32[]{:S(2)}) collective-permute-start(bf16[256,128]{1,0:T(8,128)(2,1)S(1)} %total.2), channel_id=1, source_target_pairs={{16,8},{24,0},{17,9},{25,1},{18,10},{26,2},{19,11},{27,3},{20,12},... | collective-permute-start | bytes 196616 | tf_op jit(solution)/shard_map/ppermute | solution.py:318
  44.5 3.0 %collective-permute-done.4.refs_4_ = bf16[256,128]{1,0:T(8,128)(2,1)S(1)} collective-permute-done((bf16[256,128]{1,0:T(8,128)(2,1)S(1)}, bf16[256,128]{1,0:T(8,128)(2,1)S(1)}, u32[]{:S(2)}, u32[]{:S(2)}) %collective-permute-start.4) | collective-permute-done | bytes 65568 | tf_op jit(solution)/shard_map/ppermute | solution.py:318
  47.4 4.1 %collective-permute-done.5.refs_5_ = bf16[256,128]{1,0:T(8,128)(2,1)S(1)} collective-permute-done((bf16[256,128]{1,0:T(8,128)(2,1)S(1)}, bf16[256,128]{1,0:T(8,128)(2,1)S(1)}, u32[]{:S(2)}, u32[]{:S(2)}) %collective-permute-start.5) | collective-permute-done | bytes 65568 | tf_op jit(solution)/shard_map/ppermute | solution.py:318
  53.7 2.4 %collective-permute-start.9 = (bf16[256,128]{1,0:T(8,128)(2,1)S(1)}, bf16[256,128]{1,0:T(8,128)(2,1)S(1)}, u32[]{:S(2)}, u32[]{:S(2)}) collective-permute-start(bf16[256,128]{1,0:T(8,128)(2,1)S(1)} %get-tuple-element.64), channel_id=1, source_target_pairs={{0,6},{1,7},{2,4},{3,5},{4,2},{5,3},{6,0},{7,1},{8,14},{9,15},{10,... | collective-permute-start | bytes 196616 | tf_op jit(solution)/shard_map/ppermute | solution.py:308
  56.1 1.2 %finish.4 = (bf16[128,2048]{1,0:T(8,128)(2,1)}, bf16[128,2048]{1,0:T(8,128)(2,1)}) custom-call(bf16[128,2048]{1,0:T(8,128)(2,1)S(1)} %get-tuple-element.54.refs_2_.refs_0_.q_ref, bf16[128,2048]{1,0:T(8,128)(2,1)S(1)} %get-tuple-element.55.refs_3_.refs_1_.d_ref, f32[128,2048]{1,0:T(8,128)S(1)} %get-tuple-element.75.refs_2_, ...), custom_call_target="tpu_custom_call" | custom-call | flops 67108864 | bytes 2359296 | tf_op jit(solution)/shard_map/finish/pallas_call | solution.py:291
  59.0 1.2 %finish.6 = (bf16[128,2048]{1,0:T(8,128)(2,1)}, bf16[128,2048]{1,0:T(8,128)(2,1)}) custom-call(bf16[128,2048]{1,0:T(8,128)(2,1)S(1)} %get-tuple-element.52.refs_0_.k_ref, bf16[128,2048]{1,0:T(8,128)(2,1)S(1)} %get-tuple-element.53.refs_1_.v_ref, f32[128,2048]{1,0:T(8,128)S(1)} %get-tuple-element.90.refs_2_, f32[128,2048]{1,0:T(8,128)S(1)} %get-tuple-element.91.refs_3_, ...), custom_call_target="tpu_custom_call" | custom-call | flops 67108864 | bytes 2359296 | tf_op jit(solution)/shard_map/finish/pallas_call | solution.py:291
  60.5 1.1 %finish.7 = (bf16[128,2048]{1,0:T(8,128)(2,1)}, bf16[128,2048]{1,0:T(8,128)(2,1)}) custom-call(bf16[128,2048]{1,0:T(8,128)(2,1)S(1)} %get-tuple-element.52.refs_0_.k_ref, bf16[128,2048]{1,0:T(8,128)(2,1)S(1)} %get-tuple-element.53.refs_1_.v_ref, f32[128,2048]{1,0:T(8,128)S(1)} %get-tuple-element.90.refs_2_, ...), custom_call_target="tpu_custom_call", output_to_operand_aliasing={{0}: (5, {}), {1}: (6, {})} | custom-call | flops 67108864 | bytes 2359296 | tf_op jit(solution)/shard_map/finish/pallas_call | solution.py:291
  (36 shorter events, 11.0 us)
Async XLA Ops:
  2.7 1.7 %collective-permute-start.10 = (bf16[1024,128]{1,0:T(8,128)(2,1)S(1)}, bf16[1024,128]{1,0:T(8,128)(2,1)S(1)}, u32[]{:S(2)}, u32[]{:S(2)}) collective-permute-start(bf16[1024,128]{1,0:T(8,128)(2,1)S(1)} %get-tuple-element.66), channel_id=1, source_target_pairs={{0,1},{1,0},{2,3},{3,2},{4,5},{5,4},{6,7},{7,6},{8,9},{9,8},{10,11... | collective-permute-start | bytes 786440 | tf_op jit(solution)/shard_map/ppermute | solution.py:308
  4.4 5.3 %collective-permute-start.11 = (bf16[256,128]{1,0:T(8,128)(2,1)S(1)}, bf16[256,128]{1,0:T(8,128)(2,1)S(1)}, u32[]{:S(2)}, u32[]{:S(2)}) collective-permute-start(bf16[256,128]{1,0:T(8,128)(2,1)S(1)} %get-tuple-element.68), channel_id=1, source_target_pairs={{0,2},{1,3},{2,0},{3,1},{4,6},{5,7},{6,4},{7,5},{8,10},{9,11},{10,... | collective-permute-start | bytes 196616 | tf_op jit(solution)/shard_map/ppermute | solution.py:308
  7.4 4.3 %collective-permute-start.12 = (bf16[256,128]{1,0:T(8,128)(2,1)S(1)}, bf16[256,128]{1,0:T(8,128)(2,1)S(1)}, u32[]{:S(2)}, u32[]{:S(2)}) collective-permute-start(bf16[256,128]{1,0:T(8,128)(2,1)S(1)} %get-tuple-element.69), channel_id=1, source_target_pairs={{0,4},{1,5},{2,6},{3,7},{4,0},{5,1},{6,2},{7,3},{8,12},{9,13},{10,... | collective-permute-start | bytes 196616 | tf_op jit(solution)/shard_map/ppermute | solution.py:308
  8.9 5.2 %collective-permute-start.13 = (bf16[256,128]{1,0:T(8,128)(2,1)S(1)}, bf16[256,128]{1,0:T(8,128)(2,1)S(1)}, u32[]{:S(2)}, u32[]{:S(2)}) collective-permute-start(bf16[256,128]{1,0:T(8,128)(2,1)S(1)} %get-tuple-element.70), channel_id=1, source_target_pairs={{0,6},{1,7},{2,4},{3,5},{4,2},{5,3},{6,0},{7,1},{8,14},{9,15},{10,... | collective-permute-start | bytes 196616 | tf_op jit(solution)/shard_map/ppermute | solution.py:308
  9.2 23.0 %collective-permute-start = (bf16[1024,128]{1,0:T(8,128)(2,1)S(1)}, bf16[1024,128]{1,0:T(8,128)(2,1)S(1)}, u32[]{:S(2)}, u32[]{:S(2)}) collective-permute-start(bf16[1024,128]{1,0:T(8,128)(2,1)S(1)} %states.3), channel_id=1, source_target_pairs={{0,1},{1,0},{2,3},{3,2},{4,5},{5,4},{6,7},{7,6},{8,9},{9,8},{10,11... | collective-permute-start | bytes 786440 | tf_op jit(solution)/shard_map/ppermute | solution.py:308
  14.1 11.5 %collective-permute-start.14 = (bf16[256,128]{1,0:T(8,128)(2,1)S(1)}, bf16[256,128]{1,0:T(8,128)(2,1)S(1)}, u32[]{:S(2)}, u32[]{:S(2)}) collective-permute-start(bf16[256,128]{1,0:T(8,128)(2,1)S(1)} %total.3), channel_id=1, source_target_pairs={{0,8},{16,24},{1,9},{17,25},{2,10},{18,26},{3,11},{19,27},{4,12},{... | collective-permute-start | bytes 196616 | tf_op jit(solution)/shard_map/ppermute | solution.py:318
  17.6 8.0 %collective-permute-start.15 = (bf16[256,128]{1,0:T(8,128)(2,1)S(1)}, bf16[256,128]{1,0:T(8,128)(2,1)S(1)}, u32[]{:S(2)}, u32[]{:S(2)}) collective-permute-start(bf16[256,128]{1,0:T(8,128)(2,1)S(1)} %total.3), channel_id=1, source_target_pairs={{0,16},{8,24},{1,17},{9,25},{2,18},{10,26},{3,19},{11,27},{4,20},{... | collective-permute-start | bytes 196616 | tf_op jit(solution)/shard_map/ppermute | solution.py:318
  22.1 3.5 %collective-permute-start.16 = (bf16[256,128]{1,0:T(8,128)(2,1)S(1)}, bf16[256,128]{1,0:T(8,128)(2,1)S(1)}, u32[]{:S(2)}, u32[]{:S(2)}) collective-permute-start(bf16[256,128]{1,0:T(8,128)(2,1)S(1)} %total.3), channel_id=1, source_target_pairs={{0,24},{8,16},{1,25},{9,17},{2,26},{10,18},{3,27},{11,19},{4,28},{... | collective-permute-start | bytes 196616 | tf_op jit(solution)/shard_map/ppermute | solution.py:318
  25.7 4.3 %collective-permute-start.17 = (bf16[256,128]{1,0:T(8,128)(2,1)S(1)}, bf16[256,128]{1,0:T(8,128)(2,1)S(1)}, u32[]{:S(2)}, u32[]{:S(2)}) collective-permute-start(bf16[256,128]{1,0:T(8,128)(2,1)S(1)} %get-tuple-element.81), channel_id=1, source_target_pairs={{0,2},{1,3},{2,0},{3,1},{4,6},{5,7},{6,4},{7,5},{8,10},{9,11},{10,... | collective-permute-start | bytes 196616 | tf_op jit(solution)/shard_map/ppermute | solution.py:308
  26.4 4.3 %collective-permute-start.18 = (bf16[256,128]{1,0:T(8,128)(2,1)S(1)}, bf16[256,128]{1,0:T(8,128)(2,1)S(1)}, u32[]{:S(2)}, u32[]{:S(2)}) collective-permute-start(bf16[256,128]{1,0:T(8,128)(2,1)S(1)} %get-tuple-element.82), channel_id=1, source_target_pairs={{0,4},{1,5},{2,6},{3,7},{4,0},{5,1},{6,2},{7,3},{8,12},{9,13},{10,... | collective-permute-start | bytes 196616 | tf_op jit(solution)/shard_map/ppermute | solution.py:308
  26.9 5.2 %collective-permute-start.19 = (bf16[256,128]{1,0:T(8,128)(2,1)S(1)}, bf16[256,128]{1,0:T(8,128)(2,1)S(1)}, u32[]{:S(2)}, u32[]{:S(2)}) collective-permute-start(bf16[256,128]{1,0:T(8,128)(2,1)S(1)} %get-tuple-element.83), channel_id=1, source_target_pairs={{0,6},{1,7},{2,4},{3,5},{4,2},{5,3},{6,0},{7,1},{8,14},{9,15},{10,... | collective-permute-start | bytes 196616 | tf_op jit(solution)/shard_map/ppermute | solution.py:308
  32.1 25.2 %collective-permute-start.20 = (bf16[1024,128]{1,0:T(8,128)(2,1)S(1)}, bf16[1024,128]{1,0:T(8,128)(2,1)S(1)}, u32[]{:S(2)}, u32[]{:S(2)}) collective-permute-start(bf16[1024,128]{1,0:T(8,128)(2,1)S(1)} %theirs.2), channel_id=1, source_target_pairs={{0,1},{1,0},{2,3},{3,2},{4,5},{5,4},{6,7},{7,6},{8,9},{9,8},{10,11... | collective-permute-start | bytes 786440 | tf_op jit(solution)/shard_map/ppermute | solution.py:308
  32.3 4.5 %collective-permute-start.1 = (bf16[256,128]{1,0:T(8,128)(2,1)S(1)}, bf16[256,128]{1,0:T(8,128)(2,1)S(1)}, u32[]{:S(2)}, u32[]{:S(2)}) collective-permute-start(bf16[256,128]{1,0:T(8,128)(2,1)S(1)} %get-tuple-element.58), channel_id=1, source_target_pairs={{0,2},{1,3},{2,0},{3,1},{4,6},{5,7},{6,4},{7,5},{8,10},{9,11},{10,... | collective-permute-start | bytes 196616 | tf_op jit(solution)/shard_map/ppermute | solution.py:308
  33.8 4.3 %collective-permute-start.2 = (bf16[256,128]{1,0:T(8,128)(2,1)S(1)}, bf16[256,128]{1,0:T(8,128)(2,1)S(1)}, u32[]{:S(2)}, u32[]{:S(2)}) collective-permute-start(bf16[256,128]{1,0:T(8,128)(2,1)S(1)} %get-tuple-element.59), channel_id=1, source_target_pairs={{0,4},{1,5},{2,6},{3,7},{4,0},{5,1},{6,2},{7,3},{8,12},{9,13},{10,... | collective-permute-start | bytes 196616 | tf_op jit(solution)/shard_map/ppermute | solution.py:308
  35.4 5.2 %collective-permute-start.3 = (bf16[256,128]{1,0:T(8,128)(2,1)S(1)}, bf16[256,128]{1,0:T(8,128)(2,1)S(1)}, u32[]{:S(2)}, u32[]{:S(2)}) collective-permute-start(bf16[256,128]{1,0:T(8,128)(2,1)S(1)} %get-tuple-element.60), channel_id=1, source_target_pairs={{0,6},{1,7},{2,4},{3,5},{4,2},{5,3},{6,0},{7,1},{8,14},{9,15},{10,... | collective-permute-start | bytes 196616 | tf_op jit(solution)/shard_map/ppermute | solution.py:308
  40.6 6.9 %collective-permute-start.4 = (bf16[256,128]{1,0:T(8,128)(2,1)S(1)}, bf16[256,128]{1,0:T(8,128)(2,1)S(1)}, u32[]{:S(2)}, u32[]{:S(2)}) collective-permute-start(bf16[256,128]{1,0:T(8,128)(2,1)S(1)} %total.2), channel_id=1, source_target_pairs={{8,0},{24,16},{9,1},{25,17},{10,2},{26,18},{11,3},{27,19},{12,4},{... | collective-permute-start | bytes 196616 | tf_op jit(solution)/shard_map/ppermute | solution.py:318
  41.9 9.7 %collective-permute-start.5 = (bf16[256,128]{1,0:T(8,128)(2,1)S(1)}, bf16[256,128]{1,0:T(8,128)(2,1)S(1)}, u32[]{:S(2)}, u32[]{:S(2)}) collective-permute-start(bf16[256,128]{1,0:T(8,128)(2,1)S(1)} %total.2), channel_id=1, source_target_pairs={{16,0},{24,8},{17,1},{25,9},{18,2},{26,10},{19,3},{27,11},{20,4},{... | collective-permute-start | bytes 196616 | tf_op jit(solution)/shard_map/ppermute | solution.py:318
  43.2 9.2 %collective-permute-start.6 = (bf16[256,128]{1,0:T(8,128)(2,1)S(1)}, bf16[256,128]{1,0:T(8,128)(2,1)S(1)}, u32[]{:S(2)}, u32[]{:S(2)}) collective-permute-start(bf16[256,128]{1,0:T(8,128)(2,1)S(1)} %total.2), channel_id=1, source_target_pairs={{16,8},{24,0},{17,9},{25,1},{18,10},{26,2},{19,11},{27,3},{20,12},... | collective-permute-start | bytes 196616 | tf_op jit(solution)/shard_map/ppermute | solution.py:318
  52.6 5.9 %collective-permute-start.7 = (bf16[256,128]{1,0:T(8,128)(2,1)S(1)}, bf16[256,128]{1,0:T(8,128)(2,1)S(1)}, u32[]{:S(2)}, u32[]{:S(2)}) collective-permute-start(bf16[256,128]{1,0:T(8,128)(2,1)S(1)} %get-tuple-element.62), channel_id=1, source_target_pairs={{0,2},{1,3},{2,0},{3,1},{4,6},{5,7},{6,4},{7,5},{8,10},{9,11},{10,... | collective-permute-start | bytes 196616 | tf_op jit(solution)/shard_map/ppermute | solution.py:308
  53.2 5.3 %collective-permute-start.8 = (bf16[256,128]{1,0:T(8,128)(2,1)S(1)}, bf16[256,128]{1,0:T(8,128)(2,1)S(1)}, u32[]{:S(2)}, u32[]{:S(2)}) collective-permute-start(bf16[256,128]{1,0:T(8,128)(2,1)S(1)} %get-tuple-element.63), channel_id=1, source_target_pairs={{0,4},{1,5},{2,6},{3,7},{4,0},{5,1},{6,2},{7,3},{8,12},{9,13},{10,... | collective-permute-start | bytes 196616 | tf_op jit(solution)/shard_map/ppermute | solution.py:308
  53.7 5.2 %collective-permute-start.9 = (bf16[256,128]{1,0:T(8,128)(2,1)S(1)}, bf16[256,128]{1,0:T(8,128)(2,1)S(1)}, u32[]{:S(2)}, u32[]{:S(2)}) collective-permute-start(bf16[256,128]{1,0:T(8,128)(2,1)S(1)} %get-tuple-element.64), channel_id=1, source_target_pairs={{0,6},{1,7},{2,4},{3,5},{4,2},{5,3},{6,0},{7,1},{8,14},{9,15},{10,... | collective-permute-start | bytes 196616 | tf_op jit(solution)/shard_map/ppermute | solution.py:308
  58.9 1.6 %collective-permute-start.21 = (bf16[1024,128]{1,0:T(8,128)(2,1)S(1)}, bf16[1024,128]{1,0:T(8,128)(2,1)S(1)}, u32[]{:S(2)}, u32[]{:S(2)}) collective-permute-start(bf16[1024,128]{1,0:T(8,128)(2,1)S(1)} %theirs.3), channel_id=1, source_target_pairs={{0,1},{1,0},{2,3},{3,2},{4,5},{5,4},{6,7},{7,6},{8,9},{9,8},{10,11... | collective-permute-start | bytes 786440 | tf_op jit(solution)/shard_map/ppermute | solution.py:308

commit v7 on v5

v7 whole, which is shorter than its diff:
```python
import functools

import jax
import jax.numpy as jnp
from jax import lax
from jax.experimental import pallas as pl
from jax.experimental.pallas import tpu as pltpu
from jax.sharding import PartitionSpec as P

HEAD = 128
PIECES = 4
MIB = 1024 * 1024
ANY = pl.BlockSpec(memory_space=pl.ANY)
VMEM = pl.BlockSpec(memory_space=pltpu.VMEM)
BF16 = jnp.bfloat16
F32 = jnp.float32
SMALL = pltpu.CompilerParams(vmem_limit_bytes=4 * MIB)


def dot(a, b, over_a, over_b):
    return lax.dot_general(
        a, b, (((over_a,), (over_b,)), ((), ())), preferred_element_type=F32
    )


def near_far():
    inner = lax.axis_index("inner")
    return lax.rem(inner, 2), lax.div(inner, 2)


def partner(s, far_count):
    return (s & ~3) | (0, 3, 1, 2)[s & 3] if far_count >= 4 else s


def slot_rows(s, far, far_count, depth):
    low, high = far & 1, (far >> 1) & 1
    place = (far - low - 2 * high) + 2 * (low ^ high) + high if far_count >= 4 else far
    return pl.ds(pl.multiple_of((place ^ s) * depth, depth), depth)


def distances(outer_count):
    return range(outer_count - 1, 0, -1)


def load_kernel(own, *refs):
    tokens, held, (out, sems) = refs[:4], refs[4:8], refs[8:]
    half = out.shape[1]
    piece = half // PIECES
    near, _ = near_far()
    side = near if own else 1 - near
    copies = [
        [
            pltpu.make_async_copy(
                ref.at[:, pl.ds(pl.multiple_of(side * half + p * piece, piece), piece)],
                to.at[:, pl.ds(p * piece, piece)],
                sems.at[p, i],
            )
            for i, (ref, to) in enumerate(zip(tokens, held))
        ]
        for p in range(PIECES)
    ]
    for group in copies:
        for copy in group:
            copy.start()
    for p, group in enumerate(copies):
        for copy in group:
            copy.wait()
        for h in range(p * piece // HEAD, (p + 1) * piece // HEAD):
            cols = slice(h * HEAD, (h + 1) * HEAD)
            q, k, v, d = (ref[:, cols] for ref in held)
            out[0, cols] = dot(k, v, 0, 0).astype(BF16)
            out[1, cols] = dot(q, d, 0, 0).astype(BF16)


def load(tokens, own):
    rows, width = tokens[0].shape
    half = width // 2
    *held, sums = pl.pallas_call(
        functools.partial(load_kernel, own),
        name="load",
        in_specs=[ANY] * 4,
        out_specs=[VMEM] * 5,
        out_shape=[pltpu.VMEM((rows, half), BF16)] * 4 + [pltpu.VMEM((2, half, HEAD), BF16)],
        scratch_shapes=[pltpu.SemaphoreType.DMA((PIECES, 4))],
        cost_estimate=pl.CostEstimate(
            flops=4 * rows * half * HEAD, bytes_accessed=20 * rows * half, transcendentals=0
        ),
        compiler_params=SMALL,
    )(*(pltpu.with_memory_space_constraint(x, pltpu.HBM) for x in tokens))
    return tuple(held), sums


def pair_kernel(keep_ref, got_ref, *slots):
    depth = slots[0].shape[1]
    _, far = near_far()
    for s, slot in enumerate(slots):
        part = slot_rows(s, far, len(slots), depth)
        for which in range(2):
            both = keep_ref[which, part].astype(F32) + got_ref[which, part].astype(F32)
            slot[which] = both.astype(BF16)


def pair_slots(keep, got, far_count):
    slot = jax.ShapeDtypeStruct((2, keep.shape[1] // far_count, HEAD), BF16)
    return pl.pallas_call(
        pair_kernel,
        name="pair",
        in_specs=[VMEM] * 2,
        out_specs=[VMEM] * far_count,
        out_shape=[slot] * far_count,
        compiler_params=SMALL,
    )(keep, got)


def totals_kernel(far_count, *refs):
    slots, sends = refs[:far_count], refs[far_count:]
    outer = lax.axis_index("outer")
    totals = []
    for which in range(2):
        total = slots[0][which].astype(F32)
        for slot in slots[1:]:
            total += slot[which].astype(F32)
        totals.append(total.astype(BF16))
    for s, send in zip(distances(len(sends) + 1), sends):
        upward = (outer ^ s) > outer
        send[...] = jnp.where(upward, totals[0], totals[1])


def group_sends(slots, outer_count):
    send = jax.ShapeDtypeStruct(slots[0].shape[1:], BF16)
    return pl.pallas_call(
        functools.partial(totals_kernel, len(slots)),
        name="totals",
        in_specs=[VMEM] * len(slots),
        out_specs=[VMEM] * (outer_count - 1),
        out_shape=[send] * (outer_count - 1),
        compiler_params=SMALL,
    )(*slots)


def scan_kernel(far_count, *refs):
    slots, others, outs = refs[:far_count], refs[far_count:-far_count], refs[-far_count:]
    outer = lax.axis_index("outer")
    _, far = near_far()
    for which in range(2):
        base = jnp.zeros(slots[0].shape[1:], F32)
        for s, other in zip(distances(len(others) + 1), others):
            below = (outer ^ s) < outer
            wanted = below if which == 0 else jnp.logical_not(below)
            base += jnp.where(wanted, other[...].astype(F32), 0.0)
        terms = [slot[which].astype(F32) for slot in slots]
        for s, out in enumerate(outs):
            total = base
            for t, term in enumerate(terms):
                if s != t:
                    below = (far ^ partner(t, far_count)) < (far ^ partner(s, far_count))
                    wanted = below if which == 0 else jnp.logical_not(below)
                    total += jnp.where(wanted, term, 0.0)
            out[which] = total.astype(BF16)


def scan_slots(slots, others):
    far_count, slot = len(slots), jax.ShapeDtypeStruct(slots[0].shape, BF16)
    return pl.pallas_call(
        functools.partial(scan_kernel, far_count),
        name="scan",
        in_specs=[VMEM] * (far_count + len(others)),
        out_specs=[VMEM] * far_count,
        out_shape=[slot] * far_count,
        compiler_params=SMALL,
    )(*slots, *others)


def expand(slots, out, extras, extra_which):
    depth = slots[0].shape[1]
    _, far = near_far()
    for s, slot in enumerate(slots):
        part = slot_rows(s, far, len(slots), depth)
        for which in range(2):
            @pl.when(extra_which == which)
            def _():
                out[which, part] = (slot[which].astype(F32) + extras[which, part].astype(F32)).astype(BF16)

            @pl.when(extra_which != which)
            def _():
                out[which, part] = slot[which]


def theirs_kernel(*refs):
    slots, (keep, out) = refs[:-2], refs[-2:]
    near, _ = near_far()
    expand(slots, out, keep, near)


def state_for_neighbour(slots, keep):
    return pl.pallas_call(
        theirs_kernel,
        name="theirs",
        in_specs=[VMEM] * (len(slots) + 1),
        out_specs=VMEM,
        out_shape=jax.ShapeDtypeStruct(keep.shape, BF16),
        compiler_params=SMALL,
    )(*slots, keep)


def local_kernel(*refs):
    rows, half = refs[0].shape
    at = lax.broadcasted_iota(jnp.int32, (rows, rows), 0)
    to = lax.broadcasted_iota(jnp.int32, (rows, rows), 1)
    lower = at >= to

    def masked(a, b):
        return jnp.where(lower, dot(a, b, 1, 1), 0.0).astype(BF16)

    def second(at, cols, a, b):
        q, k, v, d = (ref[:, cols] for ref in refs[at : at + 4])
        att, gq, gk, gv = refs[8 + at : 12 + at]
        att[:, cols] = dot(a, v, 1, 0)
        gq[:, cols] = dot(b, k, 1, 0)
        gk[:, cols] = dot(b, q, 0, 0)
        gv[:, cols] = dot(a, d, 0, 0)

    last = None
    for at in (0, 4):
        for h in range(half // HEAD):
            cols = slice(h * HEAD, (h + 1) * HEAD)
            q, k, v, d = (ref[:, cols] for ref in refs[at : at + 4])
            a, b = masked(q, k), masked(d, v)
            if last:
                second(*last)
            last = (at, cols, a, b)
    second(*last)


def local_part(own, other):
    rows, half = own[0].shape
    outs = pl.pallas_call(
        local_kernel,
        name="local",
        in_specs=[VMEM] * 8,
        out_specs=[VMEM] * 8,
        out_shape=[jax.ShapeDtypeStruct((rows, half), F32)] * 8,
        cost_estimate=pl.CostEstimate(
            flops=24 * rows * half * HEAD, bytes_accessed=48 * rows * half, transcendentals=0
        ),
        compiler_params=SMALL,
    )(*own, *other)
    return outs[:4], outs[4:]


def finish_kernel(scale, slot_count, *refs):
    tokens, local, refs = refs[:4], refs[4:8], refs[8:]
    held, sems = refs[-2:]
    near, _ = near_far()
    if slot_count:
        outs, states = refs[-7:-3], refs[-3]
        expand(refs[:slot_count], states, refs[slot_count], 1 - near)
        side = near
    else:
        outs, states, side = refs[-6:-2], refs[0], 1 - near
    half = held.shape[2]
    piece = half // PIECES
    copies = []
    for p in range(PIECES):
        for h in range(p * piece // HEAD, (p + 1) * piece // HEAD):
            into = slice(h * HEAD, (h + 1) * HEAD)
            q, k, v, d = (ref[:, into] for ref in tokens)
            s, g = states[0, into], states[1, into]
            parts = (dot(q, s, 1, 0), dot(d, s, 1, 1), dot(v, g, 1, 1), dot(k, g, 1, 0))
            for i, part in enumerate(parts):
                held[i, :, into] = (scale * (part + local[i][:, into])).astype(BF16)
        for i, out in enumerate(outs):
            there = pl.ds(pl.multiple_of(side * half + p * piece, piece), piece)
            copy = pltpu.make_async_copy(
                held.at[i, :, pl.ds(p * piece, piece)], out.at[:, there], sems.at[i, p]
            )
            copy.start()
            copies.append(copy)
    for copy in copies:
        copy.wait()


def finish(tokens, local, states, scale, before=()):
    rows, half = tokens[0].shape
    width = 2 * half
    slot_count = 0 if before else len(states) - 1
    out = jax.ShapeDtypeStruct((rows, width), BF16)
    scratch = [pltpu.VMEM((2, half, HEAD), BF16)] if slot_count else []
    return pl.pallas_call(
        functools.partial(finish_kernel, scale, slot_count),
        name="finish",
        in_specs=[VMEM] * (8 + len(states)) + [ANY] * len(before),
        out_specs=[ANY] * 4,
        out_shape=[out] * 4,
        scratch_shapes=scratch
        + [pltpu.VMEM((4, rows, half), BF16), pltpu.SemaphoreType.DMA((4, PIECES))],
        input_output_aliases={8 + len(states) + i: i for i in range(len(before))},
        cost_estimate=pl.CostEstimate(
            flops=4 * rows * width * HEAD, bytes_accessed=17 * rows * width, transcendentals=0
        ),
        compiler_params=SMALL,
    )(*tokens, *local, *states, *before)


def swap(x, axis, bits):
    return lax.ppermute(x, axis, [(i, i ^ bits) for i in range(lax.axis_size(axis))])


def swap_far(slots):
    count = len(slots)
    return [slots[0]] + [swap(slots[s], "inner", 2 * partner(s, count)) for s in range(1, count)]


def body(queries, keys, values, cotangent):
    tokens = (queries, keys, values, cotangent)
    count = lax.axis_size("inner")
    outer_count = lax.axis_size("outer")
    scale = float(HEAD * queries.shape[0] * count * outer_count) ** (-0.5)
    other, give = load(tokens, False)
    got = swap(give, "inner", 1)
    own, keep = load(tokens, True)
    slots = swap_far(pair_slots(keep, got, count // 2))
    slots, local = lax.optimization_barrier((slots, local_part(own, other)))
    sends = group_sends(slots, outer_count)
    others = [swap(send, "outer", s) for s, send in zip(distances(outer_count), sends)]
    slots = swap_far(scan_slots(slots, others))
    arrived = swap(state_for_neighbour(slots, keep), "inner", 1)
    outs = finish(own, local[0], (*slots, got), scale)
    return tuple(finish(other, local[1], (arrived,), scale, outs))


def solution(mesh):
    spec = P(("outer", "inner"), None)
    return jax.shard_map(
        body, mesh=mesh, in_specs=(spec,) * 4, out_specs=(spec,) * 4, check_vma=False
    )
```

time: 38.5 us -> 38.6 us (level)
  Pallas kernels: 8.61 us -> 9.85 us
  waiting for transfers between devices: 16 us -> 15.1 us
    pallas_call x9, Pallas kernels: 8.61 us -> 9.85 us  [the longest x2 3.98 us: load(): pl.pallas_call(functools.partial(load_kernel, own), name='load', in_specs...]
    ppermute x11, waiting for transfers between devices: 16 us -> 15.1 us  [swap(): lax.ppermute(x, axis, [(i, i ^ bits) for i in range(lax.axis_size(axis))])]
  transfers between devices with their start and end apart: 11 -> 11, of which waited for: 10 -> 8; matrix products, arithmetic and copies ran while one was open for 0% -> 0% of each run, Pallas kernels for 11% -> 15%
where the time goes in v7:
time: 38.6 us; the launch traced here: 38.4 us
  waiting for transfers between devices  15.1 us (39%)
  starting transfers between devices  12.8 us (33%)
  Pallas kernels  9.85 us (26%)
  between operations  0.71 us (2%)
    ppermute x11, waiting for transfers between devices, swap(): lax.ppermute(x, axis, [(i, i ^ bits) for i in range(lax.axis_size(axis))])  15.1 us
    ppermute x11, starting transfers between devices, swap(): lax.ppermute(x, axis, [(i, i ^ bits) for i in range(lax.axis_size(axis))])  12.8 us
    pallas_call x2, Pallas kernels, load(): pl.pallas_call(functools.partial(load_kernel, own), name='load', in_specs...  3.98 us
    pallas_call x2, Pallas kernels, finish(): pl.pallas_call(functools.partial(finish_kernel, scale, slot_count), name=...  3.02 us
    pallas_call x1, Pallas kernels, local_part(): pl.pallas_call(local_kernel, name='local', in_specs=[VMEM] * 8, out_specs...  2.15 us
  transfers between devices with their start and end apart: 11, of which 8 were waited for; matrix products, arithmetic and copies ran while one was open for 0% of the time, Pallas kernels for 15%

profile of v7, /device:TPU:0, one launch (start us, length us, event | category | flops | bytes accessed | tf_op | source)
XLA Modules:
  0.0 38.4 jit_solution(9428892839430309975)
XLA Ops:
  0.6 2.0 %load.2 = (bf16[128,1024]{1,0:T(8,128)(2,1)S(1)}, bf16[128,1024]{1,0:T(8,128)(2,1)S(1)}, bf16[128,1024]{1,0:T(8,128)(2,1)S(1)}, bf16[128,1024]{1,0:T(8,128)(2,1)S(1)}, bf16[2,1024,128]{2,1,0:T(8,128)(2,1)S(1)}) custom-call(bf16[128,2048]{1,0:T(8,128)(2,1)} %refs_0_.3, bf16[128,2048]{1,0:T(8,128)(2,1)} %refs_1_.3, bf16[128,2048]{1,0:T(8,128)(2,1)} %refs_2_.3, ...), custom_call_target="tpu_custom_call" | custom-call | flops 67108864 | bytes 2621440 | tf_op jit(solution)/shard_map/load/pallas_call | solution.py:78
  2.6 0.5 %collective-permute-start = (bf16[2,1024,128]{2,1,0:T(8,128)(2,1)S(1)}, bf16[2,1024,128]{2,1,0:T(8,128)(2,1)S(1)}, u32[]{:S(2)}, u32[]{:S(2)}) collective-permute-start(bf16[2,1024,128]{2,1,0:T(8,128)(2,1)S(1)} %get-tuple-element.54), channel_id=1, source_target_pairs={{0,1},{1,0},{2,3},{3,2},{4,5},{5,4},{6,7},{7,6},{8,9},{9,8},{10,11... | collective-permute-start | bytes 1572872 | tf_op jit(solution)/shard_map/ppermute | solution.py:306
  3.2 2.0 %load.3 = (bf16[128,1024]{1,0:T(8,128)(2,1)S(1)}, bf16[128,1024]{1,0:T(8,128)(2,1)S(1)}, bf16[128,1024]{1,0:T(8,128)(2,1)S(1)}, bf16[128,1024]{1,0:T(8,128)(2,1)S(1)}, bf16[2,1024,128]{2,1,0:T(8,128)(2,1)S(1)}) custom-call(bf16[128,2048]{1,0:T(8,128)(2,1)} %refs_0_.3, bf16[128,2048]{1,0:T(8,128)(2,1)} %refs_1_.3, bf16[128,2048]{1,0:T(8,128)(2,1)} %refs_2_.3, ...), custom_call_target="tpu_custom_call" | custom-call | flops 67108864 | bytes 2621440 | tf_op jit(solution)/shard_map/load/pallas_call | solution.py:78
  5.2 0.1 pair.1
  5.3 3.5 %collective-permute-start.1 = (bf16[2,256,128]{2,1,0:T(8,128)(2,1)S(1)}, bf16[2,256,128]{2,1,0:T(8,128)(2,1)S(1)}, u32[]{:S(2)}, u32[]{:S(2)}) collective-permute-start(bf16[2,256,128]{2,1,0:T(8,128)(2,1)S(1)} %get-tuple-element.56), channel_id=1, source_target_pairs={{0,6},{1,7},{2,4},{3,5},{4,2},{5,3},{6,0},{7,1},{8,14},{9,15},{10,... | collective-permute-start | bytes 393224 | tf_op jit(solution)/shard_map/ppermute | solution.py:306
  8.8 0.5 %collective-permute-start.2 = (bf16[2,256,128]{2,1,0:T(8,128)(2,1)S(1)}, bf16[2,256,128]{2,1,0:T(8,128)(2,1)S(1)}, u32[]{:S(2)}, u32[]{:S(2)}) collective-permute-start(bf16[2,256,128]{2,1,0:T(8,128)(2,1)S(1)} %get-tuple-element.57), channel_id=1, source_target_pairs={{0,2},{1,3},{2,0},{3,1},{4,6},{5,7},{6,4},{7,5},{8,10},{9,11},{10,... | collective-permute-start | bytes 393224 | tf_op jit(solution)/shard_map/ppermute | solution.py:306
  9.4 0.1 collective-permute-start.3
  9.5 2.2 %local.1 = (f32[128,1024]{1,0:T(8,128)S(1)}, f32[128,1024]{1,0:T(8,128)S(1)}, f32[128,1024]{1,0:T(8,128)S(1)}, f32[128,1024]{1,0:T(8,128)S(1)}, f32[128,1024]{1,...) custom-call(bf16[128,1024]{1,0:T(8,128)(2,1)S(1)} %get-tuple-element.59.refs_0_, ...), custom_call_target="tpu_custom_call" | custom-call | flops 402653184 | bytes 6291456 | tf_op jit(solution)/shard_map/local/pallas_call | solution.py:237
  11.6 1.6 %collective-permute-done.1.refs_1_ = bf16[2,256,128]{2,1,0:T(8,128)(2,1)S(1)} collective-permute-done((bf16[2,256,128]{2,1,0:T(8,128)(2,1)S(1)}, bf16[2,256,128]{2,1,0:T(8,128)(2,1)S(1)}, u32[]{:S(2)}, u32[]{:S(2)}) %collective-permute-start.1) | collective-permute-done | bytes 131104 | tf_op jit(solution)/shard_map/ppermute | solution.py:306
  13.2 2.9 %collective-permute-done.2.refs_2_ = bf16[2,256,128]{2,1,0:T(8,128)(2,1)S(1)} collective-permute-done((bf16[2,256,128]{2,1,0:T(8,128)(2,1)S(1)}, bf16[2,256,128]{2,1,0:T(8,128)(2,1)S(1)}, u32[]{:S(2)}, u32[]{:S(2)}) %collective-permute-start.2) | collective-permute-done | bytes 131104 | tf_op jit(solution)/shard_map/ppermute | solution.py:306
  16.2 3.7 %collective-permute-start.4 = (bf16[256,128]{1,0:T(8,128)(2,1)S(1)}, bf16[256,128]{1,0:T(8,128)(2,1)S(1)}, u32[]{:S(2)}, u32[]{:S(2)}) collective-permute-start(bf16[256,128]{1,0:T(8,128)(2,1)S(1)} %get-tuple-element.79), channel_id=1, source_target_pairs={{0,24},{8,16},{16,8},{24,0},{1,25},{9,17},{17,9},{25,1},{2,26},{10... | collective-permute-start | bytes 196616 | tf_op jit(solution)/shard_map/ppermute | solution.py:306
  19.9 0.8 %collective-permute-start.6 = (bf16[256,128]{1,0:T(8,128)(2,1)S(1)}, bf16[256,128]{1,0:T(8,128)(2,1)S(1)}, u32[]{:S(2)}, u32[]{:S(2)}) collective-permute-start(bf16[256,128]{1,0:T(8,128)(2,1)S(1)} %get-tuple-element.81), channel_id=1, source_target_pairs={{0,8},{8,0},{16,24},{24,16},{1,9},{9,1},{17,25},{25,17},{2,10},{10... | collective-permute-start | bytes 196616 | tf_op jit(solution)/shard_map/ppermute | solution.py:306
  20.6 2.1 %collective-permute-done.4.refs_4_ = bf16[256,128]{1,0:T(8,128)(2,1)S(1)} collective-permute-done((bf16[256,128]{1,0:T(8,128)(2,1)S(1)}, bf16[256,128]{1,0:T(8,128)(2,1)S(1)}, u32[]{:S(2)}, u32[]{:S(2)}) %collective-permute-start.4) | collective-permute-done | bytes 65568 | tf_op jit(solution)/shard_map/ppermute | solution.py:306
  22.7 2.8 %collective-permute-done.5.refs_5_ = bf16[256,128]{1,0:T(8,128)(2,1)S(1)} collective-permute-done((bf16[256,128]{1,0:T(8,128)(2,1)S(1)}, bf16[256,128]{1,0:T(8,128)(2,1)S(1)}, u32[]{:S(2)}, u32[]{:S(2)}) %collective-permute-start.5) | collective-permute-done | bytes 65568 | tf_op jit(solution)/shard_map/ppermute | solution.py:306
  25.5 0.3 scan.1
  25.9 2.5 %collective-permute-start.7 = (bf16[2,256,128]{2,1,0:T(8,128)(2,1)S(1)}, bf16[2,256,128]{2,1,0:T(8,128)(2,1)S(1)}, u32[]{:S(2)}, u32[]{:S(2)}) collective-permute-start(bf16[2,256,128]{2,1,0:T(8,128)(2,1)S(1)} %get-tuple-element.83), channel_id=1, source_target_pairs={{0,6},{1,7},{2,4},{3,5},{4,2},{5,3},{6,0},{7,1},{8,14},{9,15},{10,... | collective-permute-start | bytes 393224 | tf_op jit(solution)/shard_map/ppermute | solution.py:306
  28.4 0.5 %collective-permute-start.8 = (bf16[2,256,128]{2,1,0:T(8,128)(2,1)S(1)}, bf16[2,256,128]{2,1,0:T(8,128)(2,1)S(1)}, u32[]{:S(2)}, u32[]{:S(2)}) collective-permute-start(bf16[2,256,128]{2,1,0:T(8,128)(2,1)S(1)} %get-tuple-element.84), channel_id=1, source_target_pairs={{0,2},{1,3},{2,0},{3,1},{4,6},{5,7},{6,4},{7,5},{8,10},{9,11},{10,... | collective-permute-start | bytes 393224 | tf_op jit(solution)/shard_map/ppermute | solution.py:306
  28.9 0.5 %collective-permute-start.9 = (bf16[2,256,128]{2,1,0:T(8,128)(2,1)S(1)}, bf16[2,256,128]{2,1,0:T(8,128)(2,1)S(1)}, u32[]{:S(2)}, u32[]{:S(2)}) collective-permute-start(bf16[2,256,128]{2,1,0:T(8,128)(2,1)S(1)} %get-tuple-element.85), channel_id=1, source_target_pairs={{0,4},{1,5},{2,6},{3,7},{4,0},{5,1},{6,2},{7,3},{8,12},{9,13},{10,... | collective-permute-start | bytes 393224 | tf_op jit(solution)/shard_map/ppermute | solution.py:306
  29.4 3.8 %collective-permute-done.7.refs_1_.refs_9_ = bf16[2,256,128]{2,1,0:T(8,128)(2,1)S(1)} collective-permute-done((bf16[2,256,128]{2,1,0:T(8,128)(2,1)S(1)}, bf16[2,256,128]{2,1,0:T(8,128)(2,1)S(1)}, u32[]{:S(2)}, u32[]{:S(2)}) %collective-permute-start.7) | collective-permute-done | bytes 131104 | tf_op jit(solution)/shard_map/ppermute | solution.py:306
  33.2 1.6 %collective-permute-done.8.refs_2_.refs_10_ = bf16[2,256,128]{2,1,0:T(8,128)(2,1)S(1)} collective-permute-done((bf16[2,256,128]{2,1,0:T(8,128)(2,1)S(1)}, bf16[2,256,128]{2,1,0:T(8,128)(2,1)S(1)}, u32[]{:S(2)}, u32[]{:S(2)}) %collective-permute-start.8) | collective-permute-done | bytes 131104 | tf_op jit(solution)/shard_map/ppermute | solution.py:306
  34.9 0.1 theirs.1
  35.1 1.6 %finish.2 = (bf16[128,2048]{1,0:T(8,128)(2,1)}, bf16[128,2048]{1,0:T(8,128)(2,1)}, bf16[128,2048]{1,0:T(8,128)(2,1)}, bf16[128,2048]{1,0:T(8,128)(2,1)}) custom-call(bf16[128,1024]{1,0:T(8,128)(2,1)S(1)} %get-tuple-element.59.refs_0_, bf16[128,1024]{1,0:T(8,128)(2,1)S(1)} %get-tuple-element.60.refs_1_, bf16[128,1024]{1,0:T(8,128)(2,1)S(1)} %get-tuple-element.61.refs_2_, ...), custom_call_target="tpu_custom_call" | custom-call | flops 134217728 | bytes 4456448 | tf_op jit(solution)/shard_map/finish/pallas_call | solution.py:289
  36.7 0.3 collective-permute-done.10.refs_8_
  37.0 1.4 %finish.3 = (bf16[128,2048]{1,0:T(8,128)(2,1)}, bf16[128,2048]{1,0:T(8,128)(2,1)}, bf16[128,2048]{1,0:T(8,128)(2,1)}, bf16[128,2048]{1,0:T(8,128)(2,1)}) custom-call(bf16[128,1024]{1,0:T(8,128)(2,1)S(1)} %get-tuple-element.49.refs_4_.refs_0_, ...), custom_call_target="tpu_custom_call", output_to_operand_aliasing={{0}: (9, {}), {1}: (10, {}), {2}: (11, {}), {3}: (12, {})} | custom-call | flops 134217728 | bytes 4456448 | tf_op jit(solution)/shard_map/finish/pallas_call | solution.py:289
  (7 shorter events, 0.3 us)
Async XLA Ops:
  2.6 2.5 %collective-permute-start = (bf16[2,1024,128]{2,1,0:T(8,128)(2,1)S(1)}, bf16[2,1024,128]{2,1,0:T(8,128)(2,1)S(1)}, u32[]{:S(2)}, u32[]{:S(2)}) collective-permute-start(bf16[2,1024,128]{2,1,0:T(8,128)(2,1)S(1)} %get-tuple-element.54), channel_id=1, source_target_pairs={{0,1},{1,0},{2,3},{3,2},{4,5},{5,4},{6,7},{7,6},{8,9},{9,8},{10,11... | collective-permute-start | bytes 1572872 | tf_op jit(solution)/shard_map/ppermute | solution.py:306
  5.3 7.9 %collective-permute-start.1 = (bf16[2,256,128]{2,1,0:T(8,128)(2,1)S(1)}, bf16[2,256,128]{2,1,0:T(8,128)(2,1)S(1)}, u32[]{:S(2)}, u32[]{:S(2)}) collective-permute-start(bf16[2,256,128]{2,1,0:T(8,128)(2,1)S(1)} %get-tuple-element.56), channel_id=1, source_target_pairs={{0,6},{1,7},{2,4},{3,5},{4,2},{5,3},{6,0},{7,1},{8,14},{9,15},{10,... | collective-permute-start | bytes 393224 | tf_op jit(solution)/shard_map/ppermute | solution.py:306
  8.8 7.2 %collective-permute-start.2 = (bf16[2,256,128]{2,1,0:T(8,128)(2,1)S(1)}, bf16[2,256,128]{2,1,0:T(8,128)(2,1)S(1)}, u32[]{:S(2)}, u32[]{:S(2)}) collective-permute-start(bf16[2,256,128]{2,1,0:T(8,128)(2,1)S(1)} %get-tuple-element.57), channel_id=1, source_target_pairs={{0,2},{1,3},{2,0},{3,1},{4,6},{5,7},{6,4},{7,5},{8,10},{9,11},{10,... | collective-permute-start | bytes 393224 | tf_op jit(solution)/shard_map/ppermute | solution.py:306
  9.4 6.7 %collective-permute-start.3 = (bf16[2,256,128]{2,1,0:T(8,128)(2,1)S(1)}, bf16[2,256,128]{2,1,0:T(8,128)(2,1)S(1)}, u32[]{:S(2)}, u32[]{:S(2)}) collective-permute-start(bf16[2,256,128]{2,1,0:T(8,128)(2,1)S(1)} %get-tuple-element.58), channel_id=1, source_target_pairs={{0,4},{1,5},{2,6},{3,7},{4,0},{5,1},{6,2},{7,3},{8,12},{9,13},{10,... | collective-permute-start | bytes 393224 | tf_op jit(solution)/shard_map/ppermute | solution.py:306
  16.2 6.5 %collective-permute-start.4 = (bf16[256,128]{1,0:T(8,128)(2,1)S(1)}, bf16[256,128]{1,0:T(8,128)(2,1)S(1)}, u32[]{:S(2)}, u32[]{:S(2)}) collective-permute-start(bf16[256,128]{1,0:T(8,128)(2,1)S(1)} %get-tuple-element.79), channel_id=1, source_target_pairs={{0,24},{8,16},{16,8},{24,0},{1,25},{9,17},{17,9},{25,1},{2,26},{10... | collective-permute-start | bytes 196616 | tf_op jit(solution)/shard_map/ppermute | solution.py:306
  19.8 5.7 %collective-permute-start.5 = (bf16[256,128]{1,0:T(8,128)(2,1)S(1)}, bf16[256,128]{1,0:T(8,128)(2,1)S(1)}, u32[]{:S(2)}, u32[]{:S(2)}) collective-permute-start(bf16[256,128]{1,0:T(8,128)(2,1)S(1)} %get-tuple-element.80), channel_id=1, source_target_pairs={{0,16},{8,24},{16,0},{24,8},{1,17},{9,25},{17,1},{25,9},{2,18},{10... | collective-permute-start | bytes 196616 | tf_op jit(solution)/shard_map/ppermute | solution.py:306
  19.9 5.7 %collective-permute-start.6 = (bf16[256,128]{1,0:T(8,128)(2,1)S(1)}, bf16[256,128]{1,0:T(8,128)(2,1)S(1)}, u32[]{:S(2)}, u32[]{:S(2)}) collective-permute-start(bf16[256,128]{1,0:T(8,128)(2,1)S(1)} %get-tuple-element.81), channel_id=1, source_target_pairs={{0,8},{8,0},{16,24},{24,16},{1,9},{9,1},{17,25},{25,17},{2,10},{10... | collective-permute-start | bytes 196616 | tf_op jit(solution)/shard_map/ppermute | solution.py:306
  25.9 7.3 %collective-permute-start.7 = (bf16[2,256,128]{2,1,0:T(8,128)(2,1)S(1)}, bf16[2,256,128]{2,1,0:T(8,128)(2,1)S(1)}, u32[]{:S(2)}, u32[]{:S(2)}) collective-permute-start(bf16[2,256,128]{2,1,0:T(8,128)(2,1)S(1)} %get-tuple-element.83), channel_id=1, source_target_pairs={{0,6},{1,7},{2,4},{3,5},{4,2},{5,3},{6,0},{7,1},{8,14},{9,15},{10,... | collective-permute-start | bytes 393224 | tf_op jit(solution)/shard_map/ppermute | solution.py:306
  28.4 6.4 %collective-permute-start.8 = (bf16[2,256,128]{2,1,0:T(8,128)(2,1)S(1)}, bf16[2,256,128]{2,1,0:T(8,128)(2,1)S(1)}, u32[]{:S(2)}, u32[]{:S(2)}) collective-permute-start(bf16[2,256,128]{2,1,0:T(8,128)(2,1)S(1)} %get-tuple-element.84), channel_id=1, source_target_pairs={{0,2},{1,3},{2,0},{3,1},{4,6},{5,7},{6,4},{7,5},{8,10},{9,11},{10,... | collective-permute-start | bytes 393224 | tf_op jit(solution)/shard_map/ppermute | solution.py:306
  28.9 5.9 %collective-permute-start.9 = (bf16[2,256,128]{2,1,0:T(8,128)(2,1)S(1)}, bf16[2,256,128]{2,1,0:T(8,128)(2,1)S(1)}, u32[]{:S(2)}, u32[]{:S(2)}) collective-permute-start(bf16[2,256,128]{2,1,0:T(8,128)(2,1)S(1)} %get-tuple-element.85), channel_id=1, source_target_pairs={{0,4},{1,5},{2,6},{3,7},{4,0},{5,1},{6,2},{7,3},{8,12},{9,13},{10,... | collective-permute-start | bytes 393224 | tf_op jit(solution)/shard_map/ppermute | solution.py:306
  35.0 2.0 %collective-permute-start.10 = (bf16[2,1024,128]{2,1,0:T(8,128)(2,1)S(1)}, bf16[2,1024,128]{2,1,0:T(8,128)(2,1)S(1)}, u32[]{:S(2)}, u32[]{:S(2)}) collective-permute-start(bf16[2,1024,128]{2,1,0:T(8,128)(2,1)S(1)} %theirs.1), channel_id=1, source_target_pairs={{0,1},{1,0},{2,3},{3,2},{4,5},{5,4},{6,7},{7,6},{8,9},{9,8},{10,11... | collective-permute-start | bytes 1572872 | tf_op jit(solution)/shard_map/ppermute | solution.py:306

commit v8 on v7

v8 whole, which is shorter than its diff:
```python
import functools

import jax
import jax.numpy as jnp
from jax import lax
from jax.experimental import pallas as pl
from jax.experimental.pallas import tpu as pltpu
from jax.sharding import PartitionSpec as P

HEAD = 128
LOADS = 2
MIB = 1024 * 1024
ANY = pl.BlockSpec(memory_space=pl.ANY)
VMEM = pl.BlockSpec(memory_space=pltpu.VMEM)
BF16 = jnp.bfloat16
F32 = jnp.float32
SMALL = pltpu.CompilerParams(vmem_limit_bytes=4 * MIB)


def dot(a, b, over_a, over_b):
    return lax.dot_general(
        a, b, (((over_a,), (over_b,)), ((), ())), preferred_element_type=F32
    )


def near_far():
    inner = lax.axis_index("inner")
    return lax.rem(inner, 2), lax.div(inner, 2)


def slot_rows(s, far, depth):
    return pl.ds(pl.multiple_of((far ^ s) * depth, depth), depth)


def distances(outer_count):
    return range(outer_count - 1, 0, -1)


def sums_of(tokens, out, heads):
    for h in heads:
        cols = slice(h * HEAD, (h + 1) * HEAD)
        q, k, v, d = (ref[:, cols] for ref in tokens)
        out[0, cols] = dot(k, v, 0, 0).astype(BF16)
        out[1, cols] = dot(q, d, 0, 0).astype(BF16)


def load_kernel(*refs):
    tokens, other, own, (out, sems) = refs[:4], refs[4:8], refs[8:12], refs[12:]
    half = out.shape[1]
    piece = half // LOADS
    near, _ = near_far()

    def copy(i, to, side, p):
        there = pl.ds(pl.multiple_of(side * half + p * piece, piece), piece)
        here = pl.ds(p * piece, piece)
        sem = sems.at[0 if to is other else 1, p, i]
        return pltpu.make_async_copy(tokens[i].at[:, there], to[i].at[:, here], sem)

    first = [[copy(i, other, 1 - near, p) for i in range(4)] for p in range(LOADS)]
    rest = [copy(i, own, near, p) for p in range(LOADS) for i in range(4)]
    for c in sum(first, []) + rest:
        c.start()
    for p, group in enumerate(first):
        for c in group:
            c.wait()
        sums_of(other, out, range(p * piece // HEAD, (p + 1) * piece // HEAD))
    for c in rest:
        c.wait()


def load(tokens):
    rows, width = tokens[0].shape
    half = width // 2
    *held, sums = pl.pallas_call(
        load_kernel,
        name="load",
        in_specs=[ANY] * 4,
        out_specs=[VMEM] * 9,
        out_shape=[pltpu.VMEM((rows, half), BF16)] * 8 + [pltpu.VMEM((2, half, HEAD), BF16)],
        scratch_shapes=[pltpu.SemaphoreType.DMA((2, LOADS, 4))],
        cost_estimate=pl.CostEstimate(
            flops=4 * rows * half * HEAD, bytes_accessed=40 * rows * half, transcendentals=0
        ),
        compiler_params=SMALL,
    )(*(pltpu.with_memory_space_constraint(x, pltpu.HBM) for x in tokens))
    return tuple(held[:4]), tuple(held[4:]), sums


def keep_kernel(*refs):
    sums_of(refs[:4], refs[4], range(refs[0].shape[1] // HEAD))


def keep_sums(own):
    rows, half = own[0].shape
    return pl.pallas_call(
        keep_kernel,
        name="keep",
        in_specs=[VMEM] * 4,
        out_specs=VMEM,
        out_shape=jax.ShapeDtypeStruct((2, half, HEAD), BF16),
        cost_estimate=pl.CostEstimate(
            flops=4 * rows * half * HEAD, bytes_accessed=12 * rows * half, transcendentals=0
        ),
        compiler_params=SMALL,
    )(*own)


def pair_kernel(keep_ref, got_ref, *slots):
    depth = slots[0].shape[1]
    _, far = near_far()
    for s, slot in enumerate(slots):
        part = slot_rows(s, far, depth)
        for which in range(2):
            both = keep_ref[which, part].astype(F32) + got_ref[which, part].astype(F32)
            slot[which] = both.astype(BF16)


def pair_slots(keep, got, far_count):
    slot = jax.ShapeDtypeStruct((2, keep.shape[1] // far_count, HEAD), BF16)
    return pl.pallas_call(
        pair_kernel,
        name="pair",
        in_specs=[VMEM] * 2,
        out_specs=[VMEM] * far_count,
        out_shape=[slot] * far_count,
        compiler_params=SMALL,
    )(keep, got)


def totals_kernel(far_count, *refs):
    slots, sends = refs[:far_count], refs[far_count:]
    outer = lax.axis_index("outer")
    totals = []
    for which in range(2):
        total = slots[0][which].astype(F32)
        for slot in slots[1:]:
            total += slot[which].astype(F32)
        totals.append(total.astype(BF16))
    for s, send in zip(distances(len(sends) + 1), sends):
        upward = (outer ^ s) > outer
        send[...] = jnp.where(upward, totals[0], totals[1])


def group_sends(slots, outer_count):
    send = jax.ShapeDtypeStruct(slots[0].shape[1:], BF16)
    return pl.pallas_call(
        functools.partial(totals_kernel, len(slots)),
        name="totals",
        in_specs=[VMEM] * len(slots),
        out_specs=[VMEM] * (outer_count - 1),
        out_shape=[send] * (outer_count - 1),
        compiler_params=SMALL,
    )(*slots)


def scan_kernel(far_count, *refs):
    slots, others, outs = refs[:far_count], refs[far_count:-far_count], refs[-far_count:]
    outer = lax.axis_index("outer")
    _, far = near_far()
    for which in range(2):
        base = jnp.zeros(slots[0].shape[1:], F32)
        for s, other in zip(distances(len(others) + 1), others):
            below = (outer ^ s) < outer
            wanted = below if which == 0 else jnp.logical_not(below)
            base += jnp.where(wanted, other[...].astype(F32), 0.0)
        terms = [slot[which].astype(F32) for slot in slots]
        for s, out in enumerate(outs):
            total = base
            for t, term in enumerate(terms):
                if s != t:
                    below = (far ^ t) < (far ^ s)
                    wanted = below if which == 0 else jnp.logical_not(below)
                    total += jnp.where(wanted, term, 0.0)
            out[which] = total.astype(BF16)


def scan_slots(slots, others):
    far_count, slot = len(slots), jax.ShapeDtypeStruct(slots[0].shape, BF16)
    return pl.pallas_call(
        functools.partial(scan_kernel, far_count),
        name="scan",
        in_specs=[VMEM] * (far_count + len(others)),
        out_specs=[VMEM] * far_count,
        out_shape=[slot] * far_count,
        compiler_params=SMALL,
    )(*slots, *others)


def expand(blocks, slots, out, extras, extra_which):
    depth = slots[0].shape[1]
    size = len(slots) // len(blocks)
    _, far = near_far()
    rows = []
    for n, block in enumerate(blocks):
        row = lax.div(far, size) ^ block
        rows.append(pl.multiple_of(row * size * depth, size * depth))
        for s in range(size):
            at = lax.rem(far ^ s, size) * depth
            into = pl.ds(pl.multiple_of(n * size * depth + at, depth), depth)
            there = pl.ds(pl.multiple_of(rows[n] + at, depth), depth)
            slot = slots[n * size + s]
            for which in range(2):

                @pl.when(extra_which == which)
                def _():
                    total = slot[which].astype(F32) + extras[which, there].astype(F32)
                    out[which, into] = total.astype(BF16)

                @pl.when(extra_which != which)
                def _():
                    out[which, into] = slot[which]

    return rows


def theirs_kernel(blocks, *refs):
    slots, (keep, out) = refs[:-2], refs[-2:]
    near, _ = near_far()
    expand(blocks, slots, out, keep, near)


def state_for_neighbour(blocks, slots, keep):
    rows = len(slots) * slots[0].shape[1]
    return pl.pallas_call(
        functools.partial(theirs_kernel, blocks),
        name="theirs",
        in_specs=[VMEM] * (len(slots) + 1),
        out_specs=VMEM,
        out_shape=jax.ShapeDtypeStruct((2, rows, HEAD), BF16),
        compiler_params=SMALL,
    )(*slots, keep)


def local_kernel(*refs):
    rows, half = refs[0].shape
    at = lax.broadcasted_iota(jnp.int32, (rows, rows), 0)
    to = lax.broadcasted_iota(jnp.int32, (rows, rows), 1)
    lower = at >= to

    def masked(a, b):
        return jnp.where(lower, dot(a, b, 1, 1), 0.0).astype(BF16)

    def second(at, cols, a, b):
        q, k, v, d = (ref[:, cols] for ref in refs[at : at + 4])
        att, gq, gk, gv = refs[8 + at : 12 + at]
        att[:, cols] = dot(a, v, 1, 0)
        gq[:, cols] = dot(b, k, 1, 0)
        gk[:, cols] = dot(b, q, 0, 0)
        gv[:, cols] = dot(a, d, 0, 0)

    last = None
    for at in (0, 4):
        for h in range(half // HEAD):
            cols = slice(h * HEAD, (h + 1) * HEAD)
            q, k, v, d = (ref[:, cols] for ref in refs[at : at + 4])
            a, b = masked(q, k), masked(d, v)
            if last:
                second(*last)
            last = (at, cols, a, b)
    second(*last)


def local_part(own, other):
    rows, half = own[0].shape
    outs = pl.pallas_call(
        local_kernel,
        name="local",
        in_specs=[VMEM] * 8,
        out_specs=[VMEM] * 8,
        out_shape=[jax.ShapeDtypeStruct((rows, half), F32)] * 8,
        cost_estimate=pl.CostEstimate(
            flops=24 * rows * half * HEAD, bytes_accessed=48 * rows * half, transcendentals=0
        ),
        compiler_params=SMALL,
    )(*own, *other)
    return outs[:4], outs[4:]


def finish_kernel(scale, blocks, size, before_count, *refs):
    tokens, local, refs = refs[:4], refs[4:8], refs[8:]
    held, sems = refs[-2:]
    half = tokens[0].shape[1]
    width = held.shape[2] // len(blocks)
    near, far = near_far()
    if size:
        slot_count = len(blocks) * size
        states, side = refs[-3], near
        rows = expand(blocks, refs[:slot_count], states, refs[slot_count], 1 - near)
        outs = refs[slot_count + 1 + before_count : -3]
    else:
        states, side = refs[0], 1 - near
        count = half // width
        share = lax.axis_size("inner") // 2 // count
        rows = [pl.multiple_of((lax.div(far, share) ^ b) * width, width) for b in blocks]
        outs = refs[1 + before_count : -2]
    copies = []
    for n, row in enumerate(rows):
        for h in range(width // HEAD):
            into = slice(n * width + h * HEAD, n * width + (h + 1) * HEAD)
            cols = pl.ds(pl.multiple_of(row + h * HEAD, HEAD), HEAD)
            q, k, v, d = (ref[:, cols] for ref in tokens)
            s, g = states[0, into], states[1, into]
            parts = (dot(q, s, 1, 0), dot(d, s, 1, 1), dot(v, g, 1, 1), dot(k, g, 1, 0))
            for i, part in enumerate(parts):
                held[i, :, into] = (scale * (part + local[i][:, cols])).astype(BF16)
        for i, out in enumerate(outs):
            there = pl.ds(pl.multiple_of(side * half + row, width), width)
            copy = pltpu.make_async_copy(
                held.at[i, :, pl.ds(n * width, width)], out.at[:, there], sems.at[i, n]
            )
            copy.start()
            copies.append(copy)
    for copy in copies:
        copy.wait()


def finish(blocks, tokens, local, states, scale, before=()):
    rows, half = tokens[0].shape
    slots = states[:-1]
    held = len(slots) * slots[0].shape[1] if slots else states[0].shape[1]
    out = jax.ShapeDtypeStruct((rows, 2 * half), BF16)
    scratch = [pltpu.VMEM((2, held, HEAD), BF16)] if slots else []
    return pl.pallas_call(
        functools.partial(finish_kernel, scale, blocks, len(slots) // len(blocks), len(before)),
        name="finish",
        in_specs=[VMEM] * (8 + len(states)) + [ANY] * len(before),
        out_specs=[ANY] * 4,
        out_shape=[out] * 4,
        scratch_shapes=scratch
        + [pltpu.VMEM((4, rows, held), BF16), pltpu.SemaphoreType.DMA((4, len(blocks)))],
        input_output_aliases={8 + len(states) + i: i for i in range(len(before))},
        cost_estimate=pl.CostEstimate(
            flops=8 * rows * held * HEAD, bytes_accessed=34 * rows * held, transcendentals=0
        ),
        compiler_params=SMALL,
    )(*tokens, *local, *states, *before)


def swap(x, axis, bits):
    return lax.ppermute(x, axis, [(i, i ^ bits) for i in range(lax.axis_size(axis))])


def swap_far(slots):
    return [slots[0]] + [swap(slots[s], "inner", 2 * s) for s in range(1, len(slots))]


def body(queries, keys, values, cotangent):
    tokens = (queries, keys, values, cotangent)
    count = lax.axis_size("inner")
    outer_count = lax.axis_size("outer")
    scale = float(HEAD * queries.shape[0] * count * outer_count) ** (-0.5)
    other, own, give = load(tokens)
    got = swap(give, "inner", 1)
    keep = keep_sums(own)
    slots = swap_far(pair_slots(keep, got, count // 2))
    slots, local = lax.optimization_barrier((slots, local_part(own, other)))
    sends = group_sends(slots, outer_count)
    others = [swap(send, "outer", s) for s, send in zip(distances(outer_count), sends)]
    slots = swap_far(scan_slots(slots, others))
    size = max(1, HEAD // slots[0].shape[1])
    blocks = len(slots) // size
    outs = ()
    for chosen in (range(1), range(1, blocks)):
        part = slots[chosen[0] * size : (chosen[-1] + 1) * size]
        if outs:
            part, outs = lax.optimization_barrier((part, outs))
        arrived = swap(state_for_neighbour(chosen, part, keep), "inner", 1)
        outs = finish(chosen, own, local[0], (*part, got), scale, outs)
        outs = finish(chosen, other, local[1], (arrived,), scale, outs)
    return tuple(outs)


def solution(mesh):
    spec = P(("outer", "inner"), None)
    return jax.shard_map(
        body, mesh=mesh, in_specs=(spec,) * 4, out_specs=(spec,) * 4, check_vma=False
    )
```

time: 38.6 us -> 38.2 us (0.990)
  waiting for transfers between devices: 15.1 us -> 14.5 us
    ppermute x11 -> x12, waiting for transfers between devices: 15.1 us -> 14.5 us  [swap(): lax.ppermute(x, axis, [(i, i ^ bits) for i in range(lax.axis_size(axis))])]
    ppermute x11 -> x12, starting transfers between devices: 12.8 us -> 13.1 us  [swap(): lax.ppermute(x, axis, [(i, i ^ bits) for i in range(lax.axis_size(axis))])]
    pallas_call x5 -> x8, Pallas kernels: 7.13 us -> 6.98 us  [the longest x4 4.72 us: finish(): pl.pallas_call(functools.partial(finish_kernel, scale, blocks, len(slots)...]
  transfers between devices with their start and end apart: 11 -> 12, of which waited for: 8 -> 9; matrix products, arithmetic and copies ran while one was open for 0% -> 0% of each run, Pallas kernels for 15% -> 15%
where the time goes in v8:
time: 38.2 us; the launch traced here: 38.1 us
  waiting for transfers between devices  14.5 us (38%)
  starting transfers between devices  13.1 us (34%)
  Pallas kernels  9.68 us (25%)
  between operations  0.74 us (2%)
    ppermute x12, waiting for transfers between devices, swap(): lax.ppermute(x, axis, [(i, i ^ bits) for i in range(lax.axis_size(axis))])  14.5 us
    ppermute x12, starting transfers between devices, swap(): lax.ppermute(x, axis, [(i, i ^ bits) for i in range(lax.axis_size(axis))])  13.1 us
    pallas_call x4, Pallas kernels, finish(): pl.pallas_call(functools.partial(finish_kernel, scale, blocks, len(slots)...  4.72 us
    pallas_call x1, Pallas kernels, local_part(): pl.pallas_call(local_kernel, name='local', in_specs=[VMEM] * 8, out_specs...  2.15 us
    pallas_call x1, Pallas kernels, load(): pl.pallas_call(load_kernel, name='load', in_specs=[ANY] * 4, out_specs=[V...  1.8 us
  transfers between devices with their start and end apart: 12, of which 9 were waited for; matrix products, arithmetic and copies ran while one was open for 0% of the time, Pallas kernels for 15%

profile of v8, /device:TPU:0, one launch (start us, length us, event | category | flops | bytes accessed | tf_op | source)
XLA Modules:
  0.0 38.1 jit_solution(3683351060943641524)
XLA Ops:
  0.6 1.8 %load.1 = (bf16[128,1024]{1,0:T(8,128)(2,1)S(1)}, bf16[128,1024]{1,0:T(8,128)(2,1)S(1)}, bf16[128,1024]{1,0:T(8,128)(2,1)S(1)}, bf16[128,1024]{1,0:T(8,128)(2,1)...) custom-call(bf16[128,2048]{1,0:T(8,128)(2,1)} %refs_0_.1, ...), custom_call_target="tpu_custom_call" | custom-call | flops 67108864 | bytes 5242880 | tf_op jit(solution)/shard_map/load/pallas_call | solution.py:74
  2.4 0.5 %collective-permute-start = (bf16[2,1024,128]{2,1,0:T(8,128)(2,1)S(1)}, bf16[2,1024,128]{2,1,0:T(8,128)(2,1)S(1)}, u32[]{:S(2)}, u32[]{:S(2)}) collective-permute-start(bf16[2,1024,128]{2,1,0:T(8,128)(2,1)S(1)} %get-tuple-element.71), channel_id=1, source_target_pairs={{0,1},{1,0},{2,3},{3,2},{4,5},{5,4},{6,7},{7,6},{8,9},{9,8},{10,11... | collective-permute-start | bytes 1572872 | tf_op jit(solution)/shard_map/ppermute | solution.py:340
  3.0 0.3 keep.1.keep_ref.refs_1_.refs_3_
  3.3 1.2 %collective-permute-done.got_ref.refs_9_.refs_11_ = bf16[2,1024,128]{2,1,0:T(8,128)(2,1)S(1)} collective-permute-done((bf16[2,1024,128]{2,1,0:T(8,128)(2,1)S(1)}, bf16[2,1024,128]{2,1,0:T(8,128)(2,1)S(1)}, u32[]{:S(2)}, u32[]{:S(2)}) %collective-permute-start) | collective-permute-done | bytes 524320 | tf_op jit(solution)/shard_map/ppermute | solution.py:340
  4.6 2.9 %collective-permute-start.1 = (bf16[2,256,128]{2,1,0:T(8,128)(2,1)S(1)}, bf16[2,256,128]{2,1,0:T(8,128)(2,1)S(1)}, u32[]{:S(2)}, u32[]{:S(2)}) collective-permute-start(bf16[2,256,128]{2,1,0:T(8,128)(2,1)S(1)} %get-tuple-element.73), channel_id=1, source_target_pairs={{0,2},{1,3},{2,0},{3,1},{4,6},{5,7},{6,4},{7,5},{8,10},{9,11},{10,... | collective-permute-start | bytes 393224 | tf_op jit(solution)/shard_map/ppermute | solution.py:340
  7.5 1.5 %collective-permute-start.2 = (bf16[2,256,128]{2,1,0:T(8,128)(2,1)S(1)}, bf16[2,256,128]{2,1,0:T(8,128)(2,1)S(1)}, u32[]{:S(2)}, u32[]{:S(2)}) collective-permute-start(bf16[2,256,128]{2,1,0:T(8,128)(2,1)S(1)} %get-tuple-element.74), channel_id=1, source_target_pairs={{0,4},{1,5},{2,6},{3,7},{4,0},{5,1},{6,2},{7,3},{8,12},{9,13},{10,... | collective-permute-start | bytes 393224 | tf_op jit(solution)/shard_map/ppermute | solution.py:340
  9.1 2.1 %local.1 = (f32[128,1024]{1,0:T(8,128)S(1)}, f32[128,1024]{1,0:T(8,128)S(1)}, f32[128,1024]{1,0:T(8,128)S(1)}, f32[128,1024]{1,0:T(8,128)S(1)}, f32[128,1024]{1,...) custom-call(bf16[128,1024]{1,0:T(8,128)(2,1)S(1)} %get-tuple-element.67.refs_0_, ...), custom_call_target="tpu_custom_call" | custom-call | flops 402653184 | bytes 6291456 | tf_op jit(solution)/shard_map/local/pallas_call | solution.py:265
  11.4 4.2 %collective-permute-done.2.refs_2_ = bf16[2,256,128]{2,1,0:T(8,128)(2,1)S(1)} collective-permute-done((bf16[2,256,128]{2,1,0:T(8,128)(2,1)S(1)}, bf16[2,256,128]{2,1,0:T(8,128)(2,1)S(1)}, u32[]{:S(2)}, u32[]{:S(2)}) %collective-permute-start.2) | collective-permute-done | bytes 131104 | tf_op jit(solution)/shard_map/ppermute | solution.py:340
  15.7 3.7 %collective-permute-start.4 = (bf16[256,128]{1,0:T(8,128)(2,1)S(1)}, bf16[256,128]{1,0:T(8,128)(2,1)S(1)}, u32[]{:S(2)}, u32[]{:S(2)}) collective-permute-start(bf16[256,128]{1,0:T(8,128)(2,1)S(1)} %get-tuple-element.92), channel_id=1, source_target_pairs={{0,24},{8,16},{16,8},{24,0},{1,25},{9,17},{17,9},{25,1},{2,26},{10... | collective-permute-start | bytes 196616 | tf_op jit(solution)/shard_map/ppermute | solution.py:340
  19.4 0.8 %collective-permute-start.6 = (bf16[256,128]{1,0:T(8,128)(2,1)S(1)}, bf16[256,128]{1,0:T(8,128)(2,1)S(1)}, u32[]{:S(2)}, u32[]{:S(2)}) collective-permute-start(bf16[256,128]{1,0:T(8,128)(2,1)S(1)} %get-tuple-element.94), channel_id=1, source_target_pairs={{0,8},{8,0},{16,24},{24,16},{1,9},{9,1},{17,25},{25,17},{2,10},{10... | collective-permute-start | bytes 196616 | tf_op jit(solution)/shard_map/ppermute | solution.py:340
  20.2 1.8 %collective-permute-done.4.refs_4_ = bf16[256,128]{1,0:T(8,128)(2,1)S(1)} collective-permute-done((bf16[256,128]{1,0:T(8,128)(2,1)S(1)}, bf16[256,128]{1,0:T(8,128)(2,1)S(1)}, u32[]{:S(2)}, u32[]{:S(2)}) %collective-permute-start.4) | collective-permute-done | bytes 65568 | tf_op jit(solution)/shard_map/ppermute | solution.py:340
  22.0 2.8 %collective-permute-done.5.refs_5_ = bf16[256,128]{1,0:T(8,128)(2,1)S(1)} collective-permute-done((bf16[256,128]{1,0:T(8,128)(2,1)S(1)}, bf16[256,128]{1,0:T(8,128)(2,1)S(1)}, u32[]{:S(2)}, u32[]{:S(2)}) %collective-permute-start.5) | collective-permute-done | bytes 65568 | tf_op jit(solution)/shard_map/ppermute | solution.py:340
  24.7 0.3 scan.1
  25.2 1.2 %collective-permute-start.7 = (bf16[2,256,128]{2,1,0:T(8,128)(2,1)S(1)}, bf16[2,256,128]{2,1,0:T(8,128)(2,1)S(1)}, u32[]{:S(2)}, u32[]{:S(2)}) collective-permute-start(bf16[2,256,128]{2,1,0:T(8,128)(2,1)S(1)} %get-tuple-element.95), channel_id=1, source_target_pairs={{0,2},{1,3},{2,0},{3,1},{4,6},{5,7},{6,4},{7,5},{8,10},{9,11},{10,... | collective-permute-start | bytes 393224 | tf_op jit(solution)/shard_map/ppermute | solution.py:340
  26.4 0.9 %collective-permute-start.8 = (bf16[2,256,128]{2,1,0:T(8,128)(2,1)S(1)}, bf16[2,256,128]{2,1,0:T(8,128)(2,1)S(1)}, u32[]{:S(2)}, u32[]{:S(2)}) collective-permute-start(bf16[2,256,128]{2,1,0:T(8,128)(2,1)S(1)} %get-tuple-element.96), channel_id=1, source_target_pairs={{0,4},{1,5},{2,6},{3,7},{4,0},{5,1},{6,2},{7,3},{8,12},{9,13},{10,... | collective-permute-start | bytes 393224 | tf_op jit(solution)/shard_map/ppermute | solution.py:340
  27.3 1.4 %collective-permute-start.9 = (bf16[2,256,128]{2,1,0:T(8,128)(2,1)S(1)}, bf16[2,256,128]{2,1,0:T(8,128)(2,1)S(1)}, u32[]{:S(2)}, u32[]{:S(2)}) collective-permute-start(bf16[2,256,128]{2,1,0:T(8,128)(2,1)S(1)} %get-tuple-element.97), channel_id=1, source_target_pairs={{0,6},{1,7},{2,4},{3,5},{4,2},{5,3},{6,0},{7,1},{8,14},{9,15},{10,... | collective-permute-start | bytes 393224 | tf_op jit(solution)/shard_map/ppermute | solution.py:340
  28.8 1.0 %finish.4 = (bf16[128,2048]{1,0:T(8,128)(2,1)}, bf16[128,2048]{1,0:T(8,128)(2,1)}, bf16[128,2048]{1,0:T(8,128)(2,1)}, bf16[128,2048]{1,0:T(8,128)(2,1)}) custom-call(bf16[128,1024]{1,0:T(8,128)(2,1)S(1)} %get-tuple-element.67.refs_0_, bf16[128,1024]{1,0:T(8,128)(2,1)S(1)} %get-tuple-element.68.refs_1_, bf16[128,1024]{1,0:T(8,128)(2,1)S(1)} %get-tuple-element.69.refs_2_, ...), custom_call_target="tpu_custom_call" | custom-call | flops 33554432 | bytes 1114112 | tf_op jit(solution)/shard_map/finish/pallas_call | solution.py:323
  29.8 1.0 %finish.5 = (bf16[128,2048]{1,0:T(8,128)(2,1)}, bf16[128,2048]{1,0:T(8,128)(2,1)}, bf16[128,2048]{1,0:T(8,128)(2,1)}, bf16[128,2048]{1,0:T(8,128)(2,1)}) custom-call(bf16[128,1024]{1,0:T(8,128)(2,1)S(1)} %get-tuple-element.63.refs_4_.refs_0_, ...), custom_call_target="tpu_custom_call", output_to_operand_aliasing={{0}: (9, {}), {1}: (10, {}), {2}: (11, {}), {3}: (12, {})} | custom-call | flops 33554432 | bytes 1114112 | tf_op jit(solution)/shard_map/finish/pallas_call | solution.py:323
  30.8 0.8 %collective-permute-done.7.refs_0_.refs_8_ = bf16[2,256,128]{2,1,0:T(8,128)(2,1)S(1)} collective-permute-done((bf16[2,256,128]{2,1,0:T(8,128)(2,1)S(1)}, bf16[2,256,128]{2,1,0:T(8,128)(2,1)S(1)}, u32[]{:S(2)}, u32[]{:S(2)}) %collective-permute-start.7) | collective-permute-done | bytes 131104 | tf_op jit(solution)/shard_map/ppermute | solution.py:340
  31.6 1.7 %collective-permute-done.8.refs_1_.refs_9_ = bf16[2,256,128]{2,1,0:T(8,128)(2,1)S(1)} collective-permute-done((bf16[2,256,128]{2,1,0:T(8,128)(2,1)S(1)}, bf16[2,256,128]{2,1,0:T(8,128)(2,1)S(1)}, u32[]{:S(2)}, u32[]{:S(2)}) %collective-permute-start.8) | collective-permute-done | bytes 131104 | tf_op jit(solution)/shard_map/ppermute | solution.py:340
  33.3 1.6 %collective-permute-done.9.refs_2_.refs_10_ = bf16[2,256,128]{2,1,0:T(8,128)(2,1)S(1)} collective-permute-done((bf16[2,256,128]{2,1,0:T(8,128)(2,1)S(1)}, bf16[2,256,128]{2,1,0:T(8,128)(2,1)S(1)}, u32[]{:S(2)}, u32[]{:S(2)}) %collective-permute-start.9) | collective-permute-done | bytes 131104 | tf_op jit(solution)/shard_map/ppermute | solution.py:340
  35.1 1.4 %finish.6 = (bf16[128,2048]{1,0:T(8,128)(2,1)}, bf16[128,2048]{1,0:T(8,128)(2,1)}, bf16[128,2048]{1,0:T(8,128)(2,1)}, bf16[128,2048]{1,0:T(8,128)(2,1)}) custom-call(bf16[128,1024]{1,0:T(8,128)(2,1)S(1)} %get-tuple-element.67.refs_0_, ...), custom_call_target="tpu_custom_call", output_to_operand_aliasing={{0}: (12, {}), {1}: (13, {}), {2}: (14, {}), {3}: (15, {})} | custom-call | flops 100663296 | bytes 3342336 | tf_op jit(solution)/shard_map/finish/pallas_call | solution.py:323
  36.5 0.3 collective-permute-done.11.refs_8_
  36.8 1.3 %finish.7 = (bf16[128,2048]{1,0:T(8,128)(2,1)}, bf16[128,2048]{1,0:T(8,128)(2,1)}, bf16[128,2048]{1,0:T(8,128)(2,1)}, bf16[128,2048]{1,0:T(8,128)(2,1)}) custom-call(bf16[128,1024]{1,0:T(8,128)(2,1)S(1)} %get-tuple-element.63.refs_4_.refs_0_, ...), custom_call_target="tpu_custom_call", output_to_operand_aliasing={{0}: (9, {}), {1}: (10, {}), {2}: (11, {}), {3}: (12, {})} | custom-call | flops 100663296 | bytes 3342336 | tf_op jit(solution)/shard_map/finish/pallas_call | solution.py:323
  (12 shorter events, 0.7 us)
Async XLA Ops:
  2.4 2.1 %collective-permute-start = (bf16[2,1024,128]{2,1,0:T(8,128)(2,1)S(1)}, bf16[2,1024,128]{2,1,0:T(8,128)(2,1)S(1)}, u32[]{:S(2)}, u32[]{:S(2)}) collective-permute-start(bf16[2,1024,128]{2,1,0:T(8,128)(2,1)S(1)} %get-tuple-element.71), channel_id=1, source_target_pairs={{0,1},{1,0},{2,3},{3,2},{4,5},{5,4},{6,7},{7,6},{8,9},{9,8},{10,11... | collective-permute-start | bytes 1572872 | tf_op jit(solution)/shard_map/ppermute | solution.py:340
  4.6 6.8 %collective-permute-start.1 = (bf16[2,256,128]{2,1,0:T(8,128)(2,1)S(1)}, bf16[2,256,128]{2,1,0:T(8,128)(2,1)S(1)}, u32[]{:S(2)}, u32[]{:S(2)}) collective-permute-start(bf16[2,256,128]{2,1,0:T(8,128)(2,1)S(1)} %get-tuple-element.73), channel_id=1, source_target_pairs={{0,2},{1,3},{2,0},{3,1},{4,6},{5,7},{6,4},{7,5},{8,10},{9,11},{10,... | collective-permute-start | bytes 393224 | tf_op jit(solution)/shard_map/ppermute | solution.py:340
  7.5 8.1 %collective-permute-start.2 = (bf16[2,256,128]{2,1,0:T(8,128)(2,1)S(1)}, bf16[2,256,128]{2,1,0:T(8,128)(2,1)S(1)}, u32[]{:S(2)}, u32[]{:S(2)}) collective-permute-start(bf16[2,256,128]{2,1,0:T(8,128)(2,1)S(1)} %get-tuple-element.74), channel_id=1, source_target_pairs={{0,4},{1,5},{2,6},{3,7},{4,0},{5,1},{6,2},{7,3},{8,12},{9,13},{10,... | collective-permute-start | bytes 393224 | tf_op jit(solution)/shard_map/ppermute | solution.py:340
  9.1 6.5 %collective-permute-start.3 = (bf16[2,256,128]{2,1,0:T(8,128)(2,1)S(1)}, bf16[2,256,128]{2,1,0:T(8,128)(2,1)S(1)}, u32[]{:S(2)}, u32[]{:S(2)}) collective-permute-start(bf16[2,256,128]{2,1,0:T(8,128)(2,1)S(1)} %get-tuple-element.75), channel_id=1, source_target_pairs={{0,6},{1,7},{2,4},{3,5},{4,2},{5,3},{6,0},{7,1},{8,14},{9,15},{10,... | collective-permute-start | bytes 393224 | tf_op jit(solution)/shard_map/ppermute | solution.py:340
  15.7 6.3 %collective-permute-start.4 = (bf16[256,128]{1,0:T(8,128)(2,1)S(1)}, bf16[256,128]{1,0:T(8,128)(2,1)S(1)}, u32[]{:S(2)}, u32[]{:S(2)}) collective-permute-start(bf16[256,128]{1,0:T(8,128)(2,1)S(1)} %get-tuple-element.92), channel_id=1, source_target_pairs={{0,24},{8,16},{16,8},{24,0},{1,25},{9,17},{17,9},{25,1},{2,26},{10... | collective-permute-start | bytes 196616 | tf_op jit(solution)/shard_map/ppermute | solution.py:340
  19.4 5.4 %collective-permute-start.5 = (bf16[256,128]{1,0:T(8,128)(2,1)S(1)}, bf16[256,128]{1,0:T(8,128)(2,1)S(1)}, u32[]{:S(2)}, u32[]{:S(2)}) collective-permute-start(bf16[256,128]{1,0:T(8,128)(2,1)S(1)} %get-tuple-element.93), channel_id=1, source_target_pairs={{0,16},{8,24},{16,0},{24,8},{1,17},{9,25},{17,1},{25,9},{2,18},{10... | collective-permute-start | bytes 196616 | tf_op jit(solution)/shard_map/ppermute | solution.py:340
  19.4 5.4 %collective-permute-start.6 = (bf16[256,128]{1,0:T(8,128)(2,1)S(1)}, bf16[256,128]{1,0:T(8,128)(2,1)S(1)}, u32[]{:S(2)}, u32[]{:S(2)}) collective-permute-start(bf16[256,128]{1,0:T(8,128)(2,1)S(1)} %get-tuple-element.94), channel_id=1, source_target_pairs={{0,8},{8,0},{16,24},{24,16},{1,9},{9,1},{17,25},{25,17},{2,10},{10... | collective-permute-start | bytes 196616 | tf_op jit(solution)/shard_map/ppermute | solution.py:340
  25.1 4.6 %collective-permute-start.10 = (bf16[2,256,128]{2,1,0:T(8,128)(2,1)S(1)}, bf16[2,256,128]{2,1,0:T(8,128)(2,1)S(1)}, u32[]{:S(2)}, u32[]{:S(2)}) collective-permute-start(bf16[2,256,128]{2,1,0:T(8,128)(2,1)S(1)} %theirs.2), channel_id=1, source_target_pairs={{0,1},{1,0},{2,3},{3,2},{4,5},{5,4},{6,7},{7,6},{8,9},{9,8},{10,11... | collective-permute-start | bytes 393224 | tf_op jit(solution)/shard_map/ppermute | solution.py:340
  25.2 6.4 %collective-permute-start.7 = (bf16[2,256,128]{2,1,0:T(8,128)(2,1)S(1)}, bf16[2,256,128]{2,1,0:T(8,128)(2,1)S(1)}, u32[]{:S(2)}, u32[]{:S(2)}) collective-permute-start(bf16[2,256,128]{2,1,0:T(8,128)(2,1)S(1)} %get-tuple-element.95), channel_id=1, source_target_pairs={{0,2},{1,3},{2,0},{3,1},{4,6},{5,7},{6,4},{7,5},{8,10},{9,11},{10,... | collective-permute-start | bytes 393224 | tf_op jit(solution)/shard_map/ppermute | solution.py:340
  26.4 6.8 %collective-permute-start.8 = (bf16[2,256,128]{2,1,0:T(8,128)(2,1)S(1)}, bf16[2,256,128]{2,1,0:T(8,128)(2,1)S(1)}, u32[]{:S(2)}, u32[]{:S(2)}) collective-permute-start(bf16[2,256,128]{2,1,0:T(8,128)(2,1)S(1)} %get-tuple-element.96), channel_id=1, source_target_pairs={{0,4},{1,5},{2,6},{3,7},{4,0},{5,1},{6,2},{7,3},{8,12},{9,13},{10,... | collective-permute-start | bytes 393224 | tf_op jit(solution)/shard_map/ppermute | solution.py:340
  27.3 7.6 %collective-permute-start.9 = (bf16[2,256,128]{2,1,0:T(8,128)(2,1)S(1)}, bf16[2,256,128]{2,1,0:T(8,128)(2,1)S(1)}, u32[]{:S(2)}, u32[]{:S(2)}) collective-permute-start(bf16[2,256,128]{2,1,0:T(8,128)(2,1)S(1)} %get-tuple-element.97), channel_id=1, source_target_pairs={{0,6},{1,7},{2,4},{3,5},{4,2},{5,3},{6,0},{7,1},{8,14},{9,15},{10,... | collective-permute-start | bytes 393224 | tf_op jit(solution)/shard_map/ppermute | solution.py:340
  35.0 1.8 %collective-permute-start.11 = (bf16[2,768,128]{2,1,0:T(8,128)(2,1)S(1)}, bf16[2,768,128]{2,1,0:T(8,128)(2,1)S(1)}, u32[]{:S(2)}, u32[]{:S(2)}) collective-permute-start(bf16[2,768,128]{2,1,0:T(8,128)(2,1)S(1)} %theirs.3), channel_id=1, source_target_pairs={{0,1},{1,0},{2,3},{3,2},{4,5},{5,4},{6,7},{7,6},{8,9},{9,8},{10,11... | collective-permute-start | bytes 1179656 | tf_op jit(solution)/shard_map/ppermute | solution.py:340

commit v9 on v7

v9 whole, which is shorter than its diff:
```python
import functools

import jax
import jax.numpy as jnp
from jax import lax
from jax.experimental import pallas as pl
from jax.experimental.pallas import tpu as pltpu
from jax.sharding import PartitionSpec as P

HEAD = 128
PIECES = 2
MIB = 1024 * 1024
ANY = pl.BlockSpec(memory_space=pl.ANY)
VMEM = pl.BlockSpec(memory_space=pltpu.VMEM)
BF16 = jnp.bfloat16
F32 = jnp.float32
SMALL = pltpu.CompilerParams(vmem_limit_bytes=4 * MIB)


def dot(a, b, over_a, over_b):
    return lax.dot_general(
        a, b, (((over_a,), (over_b,)), ((), ())), preferred_element_type=F32
    )


def near_far():
    inner = lax.axis_index("inner")
    return lax.rem(inner, 2), lax.div(inner, 2)


def slot_rows(s, far, depth):
    return pl.ds(pl.multiple_of((far ^ s) * depth, depth), depth)


def distances(outer_count):
    return range(outer_count - 1, 0, -1)


def sums_of(tokens, out):
    q, k, v, d = tokens
    for h in range(out.shape[1] // HEAD):
        cols = slice(h * HEAD, (h + 1) * HEAD)
        out[0, cols] = dot(k[:, cols], v[:, cols], 0, 0).astype(BF16)
        out[1, cols] = dot(q[:, cols], d[:, cols], 0, 0).astype(BF16)


def load_kernel(*refs):
    tokens, held, (out, sems) = refs[:4], refs[4:20], refs[20:]
    part = out.shape[1]
    near, _ = near_far()
    copies = []
    for n in range(16):
        side = 1 - near if n < 8 else near
        there = pl.ds(pl.multiple_of((side * 2 + n // 4 % 2) * part, part), part)
        copies.append(pltpu.make_async_copy(tokens[n % 4].at[:, there], held[n], sems.at[n]))
    for copy in copies:
        copy.start()
    for copy in copies[:4]:
        copy.wait()
    sums_of(held[:4], out)
    for copy in copies[4:]:
        copy.wait()


def load(tokens):
    rows, width = tokens[0].shape
    part = width // 4
    *held, sums = pl.pallas_call(
        load_kernel,
        name="load",
        in_specs=[ANY] * 4,
        out_specs=[VMEM] * 17,
        out_shape=[pltpu.VMEM((rows, part), BF16)] * 16 + [pltpu.VMEM((2, part, HEAD), BF16)],
        scratch_shapes=[pltpu.SemaphoreType.DMA((16,))],
        cost_estimate=pl.CostEstimate(
            flops=4 * rows * part * HEAD, bytes_accessed=40 * rows * part, transcendentals=0
        ),
        compiler_params=SMALL,
    )(*(pltpu.with_memory_space_constraint(x, pltpu.HBM) for x in tokens))
    return (held[:4], held[4:8]), (held[8:12], held[12:]), sums


def sums_kernel(*refs):
    outs = refs[len(refs) * 4 // 5 :]
    for n, out in enumerate(outs):
        sums_of(refs[4 * n : 4 * n + 4], out)


def sums(*parts):
    rows, part = parts[0][0].shape
    return pl.pallas_call(
        sums_kernel,
        name="sums",
        in_specs=[VMEM] * (4 * len(parts)),
        out_specs=[VMEM] * len(parts),
        out_shape=[jax.ShapeDtypeStruct((2, part, HEAD), BF16)] * len(parts),
        cost_estimate=pl.CostEstimate(
            flops=4 * rows * part * HEAD, bytes_accessed=12 * rows * part, transcendentals=0
        ),
        compiler_params=SMALL,
    )(*(x for tokens in parts for x in tokens))


def pair_kernel(after, keep_ref, got_ref, *refs):
    slots = refs[after:]
    depth = slots[0].shape[1]
    _, far = near_far()
    for s, slot in enumerate(slots):
        part = slot_rows(s, far, depth)
        for which in range(2):
            both = keep_ref[which, part].astype(F32) + got_ref[which, part].astype(F32)
            slot[which] = both.astype(BF16)


def pair_slots(keep, got, far_count, after):
    slot = jax.ShapeDtypeStruct((2, keep.shape[1] // far_count, HEAD), BF16)
    return pl.pallas_call(
        functools.partial(pair_kernel, len(after)),
        name="pair",
        in_specs=[VMEM] * 2 + [ANY] * len(after),
        out_specs=[VMEM] * far_count,
        out_shape=[slot] * far_count,
        compiler_params=SMALL,
    )(keep, got, *after)


def totals_kernel(far_count, after, *refs):
    slots, sends = refs[:far_count], refs[far_count + after :]
    outer = lax.axis_index("outer")
    totals = []
    for which in range(2):
        total = slots[0][which].astype(F32)
        for slot in slots[1:]:
            total += slot[which].astype(F32)
        totals.append(total.astype(BF16))
    for s, send in zip(distances(len(sends) + 1), sends):
        upward = (outer ^ s) > outer
        send[...] = jnp.where(upward, totals[0], totals[1])


def group_sends(slots, outer_count, after):
    send = jax.ShapeDtypeStruct(slots[0].shape[1:], BF16)
    return pl.pallas_call(
        functools.partial(totals_kernel, len(slots), len(after)),
        name="totals",
        in_specs=[VMEM] * len(slots) + [ANY] * len(after),
        out_specs=[VMEM] * (outer_count - 1),
        out_shape=[send] * (outer_count - 1),
        compiler_params=SMALL,
    )(*slots, *after)


def scan_kernel(far_count, others_count, *refs):
    slots, outs = refs[:far_count], refs[-far_count:]
    others = refs[far_count : far_count + others_count]
    outer = lax.axis_index("outer")
    _, far = near_far()
    for which in range(2):
        base = jnp.zeros(slots[0].shape[1:], F32)
        for s, other in zip(distances(len(others) + 1), others):
            below = (outer ^ s) < outer
            wanted = below if which == 0 else jnp.logical_not(below)
            base += jnp.where(wanted, other[...].astype(F32), 0.0)
        terms = [slot[which].astype(F32) for slot in slots]
        for s, out in enumerate(outs):
            total = base
            for t, term in enumerate(terms):
                if s != t:
                    below = (far ^ t) < (far ^ s)
                    wanted = below if which == 0 else jnp.logical_not(below)
                    total += jnp.where(wanted, term, 0.0)
            out[which] = total.astype(BF16)


def scan_slots(slots, others, after):
    far_count, slot = len(slots), jax.ShapeDtypeStruct(slots[0].shape, BF16)
    return pl.pallas_call(
        functools.partial(scan_kernel, far_count, len(others)),
        name="scan",
        in_specs=[VMEM] * (far_count + len(others)) + [ANY] * len(after),
        out_specs=[VMEM] * far_count,
        out_shape=[slot] * far_count,
        compiler_params=SMALL,
    )(*slots, *others, *after)


def expand(slots, out, extras, extra_which):
    depth = slots[0].shape[1]
    _, far = near_far()
    for s, slot in enumerate(slots):
        part = slot_rows(s, far, depth)
        for which in range(2):

            @pl.when(extra_which == which)
            def _():
                total = slot[which].astype(F32) + extras[which, part].astype(F32)
                out[which, part] = total.astype(BF16)

            @pl.when(extra_which != which)
            def _():
                out[which, part] = slot[which]


def theirs_kernel(far_count, *refs):
    near, _ = near_far()
    expand(refs[:far_count], refs[-1], refs[far_count], near)


def state_for_neighbour(slots, keep, after):
    return pl.pallas_call(
        functools.partial(theirs_kernel, len(slots)),
        name="theirs",
        in_specs=[VMEM] * (len(slots) + 1) + [ANY] * len(after),
        out_specs=VMEM,
        out_shape=jax.ShapeDtypeStruct(keep.shape, BF16),
        compiler_params=SMALL,
    )(*slots, keep, *after)


def local_kernel(*refs):
    count = len(refs) // 2
    rows, part = refs[0].shape
    at = lax.broadcasted_iota(jnp.int32, (rows, rows), 0)
    to = lax.broadcasted_iota(jnp.int32, (rows, rows), 1)
    lower = at >= to

    def masked(a, b):
        return jnp.where(lower, dot(a, b, 1, 1), 0.0).astype(BF16)

    def second(at, cols, a, b):
        q, k, v, d = (ref[:, cols] for ref in refs[at : at + 4])
        att, gq, gk, gv = refs[count + at : count + at + 4]
        att[:, cols] = dot(a, v, 1, 0)
        gq[:, cols] = dot(b, k, 1, 0)
        gk[:, cols] = dot(b, q, 0, 0)
        gv[:, cols] = dot(a, d, 0, 0)

    last = None
    for at in range(0, count, 4):
        for h in range(part // HEAD):
            cols = slice(h * HEAD, (h + 1) * HEAD)
            q, k, v, d = (ref[:, cols] for ref in refs[at : at + 4])
            a, b = masked(q, k), masked(d, v)
            if last:
                second(*last)
            last = (at, cols, a, b)
    second(*last)


def local_part(*parts):
    rows, part = parts[0][0].shape
    count = 4 * len(parts)
    outs = pl.pallas_call(
        local_kernel,
        name="local",
        in_specs=[VMEM] * count,
        out_specs=[VMEM] * count,
        out_shape=[jax.ShapeDtypeStruct((rows, part), F32)] * count,
        cost_estimate=pl.CostEstimate(
            flops=3 * count * rows * part * HEAD,
            bytes_accessed=6 * count * rows * part,
            transcendentals=0,
        ),
        compiler_params=SMALL,
    )(*(x for tokens in parts for x in tokens))
    return [outs[n : n + 4] for n in range(0, count, 4)]


def finish_kernel(scale, at, slot_count, *refs):
    tokens, local, refs = refs[:4], refs[4:8], refs[8:]
    held, sems = refs[-2:]
    near, _ = near_far()
    if slot_count:
        outs, done, states, side = refs[-8:-4], refs[-4], refs[-3], near
        expand(refs[:slot_count], states, refs[slot_count], 1 - near)
    else:
        outs, done, states, side = refs[-7:-3], refs[-3], refs[0], 1 - near
    done[...] = jnp.zeros_like(done)
    part = held.shape[2]
    piece = part // PIECES
    copies = []
    for p in range(PIECES):
        for h in range(p * piece // HEAD, (p + 1) * piece // HEAD):
            cols = slice(h * HEAD, (h + 1) * HEAD)
            q, k, v, d = (ref[:, cols] for ref in tokens)
            s, g = states[0, cols], states[1, cols]
            parts = (dot(q, s, 1, 0), dot(d, s, 1, 1), dot(v, g, 1, 1), dot(k, g, 1, 0))
            for i, x in enumerate(parts):
                held[i, :, cols] = (scale * (x + local[i][:, cols])).astype(BF16)
        for i, out in enumerate(outs):
            first = (side * 2 + at) * part + p * piece
            copy = pltpu.make_async_copy(
                held.at[i, :, pl.ds(p * piece, piece)],
                out.at[:, pl.ds(pl.multiple_of(first, piece), piece)],
                sems.at[i, p],
            )
            copy.start()
            copies.append(copy)
    for copy in copies:
        copy.wait()


def finish(at, tokens, local, states, scale, before):
    rows, part = tokens[0].shape
    slot_count = len(states) - 1
    out = jax.ShapeDtypeStruct((rows, 4 * part), BF16)
    scratch = [pltpu.VMEM((2, part, HEAD), BF16)] if slot_count else []
    return pl.pallas_call(
        functools.partial(finish_kernel, scale, at, slot_count),
        name="finish",
        in_specs=[VMEM] * (8 + len(states)) + [ANY] * len(before),
        out_specs=[ANY] * 4 + [VMEM],
        out_shape=[out] * 4 + [pltpu.VMEM((8, HEAD), F32)],
        scratch_shapes=scratch
        + [pltpu.VMEM((4, rows, part), BF16), pltpu.SemaphoreType.DMA((4, PIECES))],
        input_output_aliases={8 + len(states) + i: i for i in range(len(before))},
        cost_estimate=pl.CostEstimate(
            flops=8 * rows * part * HEAD, bytes_accessed=34 * rows * part, transcendentals=0
        ),
        compiler_params=SMALL,
    )(*tokens, *local, *states, *before)


def swap(x, axis, bits):
    return lax.ppermute(x, axis, [(i, i ^ bits) for i in range(lax.axis_size(axis))])


def swap_far(slots):
    return [slots[0]] + [swap(slots[s], "inner", 2 * s) for s in range(1, len(slots))]


def body(queries, keys, values, cotangent):
    tokens = (queries, keys, values, cotangent)
    far_count = lax.axis_size("inner") // 2
    outer_count = lax.axis_size("outer")
    scale = float(HEAD * queries.shape[0] * 2 * far_count * outer_count) ** (-0.5)
    other, own, give = load(tokens)
    got = [swap(give, "inner", 1), swap(*sums(other[1]), "inner", 1)]
    keep = sums(*own)
    after, slots, sends = [], [], []
    for at in range(2):
        slots.append(pair_slots(keep[at], got[at], far_count, after))
        after = slots[at][:1]
    slots = [swap_far(x) for x in slots]
    for at in range(2):
        sends.append(group_sends(slots[at], outer_count, after))
        after = sends[at][:1]
    for at in range(2):
        others = [swap(x, "outer", s) for s, x in zip(distances(outer_count), sends[at])]
        slots[at] = scan_slots(slots[at], others, after)
        after = slots[at][:1]
    slots = [swap_far(x) for x in slots]
    local = local_part(*own, *other)
    outs = ()
    for at in range(2):
        arrived = swap(state_for_neighbour(slots[at], keep[at], after), "inner", 1)
        *outs, _ = finish(at, own[at], local[at], (*slots[at], got[at]), scale, outs)
        *outs, done = finish(at, other[at], local[2 + at], (arrived,), scale, outs)
        after = [done]
    return tuple(outs)


def solution(mesh):
    spec = P(("outer", "inner"), None)
    return jax.shard_map(
        body, mesh=mesh, in_specs=(spec,) * 4, out_specs=(spec,) * 4, check_vma=False
    )
```

time: 38.6 us -> 46.3 us (1.20)
  starting transfers between devices: 12.8 us -> 22.7 us
  waiting for transfers between devices: 15.1 us -> 10.8 us
  Pallas kernels: 9.85 us -> 11.8 us
    ppermute x11 -> x22, starting transfers between devices: 12.8 us -> 22.7 us  [swap(): lax.ppermute(x, axis, [(i, i ^ bits) for i in range(lax.axis_size(axis))])]
    ppermute x11 -> x22, waiting for transfers between devices: 15.1 us -> 10.8 us  [swap(): lax.ppermute(x, axis, [(i, i ^ bits) for i in range(lax.axis_size(axis))])]
    pallas_call x9 -> x16, Pallas kernels: 9.85 us -> 11.8 us  [the longest x4 6.49 us: finish(): pl.pallas_call(functools.partial(finish_kernel, scale, at, slot_count), n...]
  transfers between devices with their start and end apart: 11 -> 22, of which waited for: 8 -> 6; matrix products, arithmetic and copies ran while one was open for 0% -> 0% of each run, Pallas kernels for 15% -> 18%
where the time goes in v9:
time: 46.3 us; the launch traced here: 46.1 us
  starting transfers between devices  22.7 us (49%)
  Pallas kernels  11.8 us (25%)
  waiting for transfers between devices  10.8 us (23%)
  between operations  0.82 us (2%)
    ppermute x22, starting transfers between devices, swap(): lax.ppermute(x, axis, [(i, i ^ bits) for i in range(lax.axis_size(axis))])  22.7 us
    ppermute x22, waiting for transfers between devices, swap(): lax.ppermute(x, axis, [(i, i ^ bits) for i in range(lax.axis_size(axis))])  10.8 us
    pallas_call x4, Pallas kernels, finish(): pl.pallas_call(functools.partial(finish_kernel, scale, at, slot_count), n...  6.49 us
    pallas_call x1, Pallas kernels, local_part(): pl.pallas_call(local_kernel, name='local', in_specs=[VMEM] * count, out_s...  2.14 us
    pallas_call x1, Pallas kernels, load(): pl.pallas_call(load_kernel, name='load', in_specs=[ANY] * 4, out_specs=[V...  1.77 us
  transfers between devices with their start and end apart: 22, of which 6 were waited for; matrix products, arithmetic and copies ran while one was open for 0% of the time, Pallas kernels for 18%

profile of v9, /device:TPU:0, one launch (start us, length us, event | category | flops | bytes accessed | tf_op | source)
XLA Modules:
  0.0 46.1 jit_solution(10892989918487758192)
XLA Ops:
  0.6 1.8 %load.1 = (bf16[128,512]{1,0:T(8,128)(2,1)S(1)}, bf16[128,512]{1,0:T(8,128)(2,1)S(1)}, bf16[128,512]{1,0:T(8,128)(2,1)S(1)}, bf16[128,512]{1,0:T(8,128)(2,1)S(1)...) custom-call(bf16[128,2048]{1,0:T(8,128)(2,1)} %refs_0_.1, ...), custom_call_target="tpu_custom_call" | custom-call | flops 33554432 | bytes 2621440 | tf_op jit(solution)/shard_map/load/pallas_call | solution.py:68
  4.2 2.9 %collective-permute-start.5 = (bf16[2,128,128]{2,1,0:T(8,128)(2,1)S(1)}, bf16[2,128,128]{2,1,0:T(8,128)(2,1)S(1)}, u32[]{:S(2)}, u32[]{:S(2)}) collective-permute-start(bf16[2,128,128]{2,1,0:T(8,128)(2,1)S(1)} %get-tuple-element.106), channel_id=1, source_target_pairs={{0,2},{1,3},{2,0},{3,1},{4,6},{5,7},{6,4},{7,5},{8,10},{9,11},{10,... | collective-permute-start | bytes 196616 | tf_op jit(solution)/shard_map/ppermute | solution.py:325
  7.1 1.5 %collective-permute-start.6 = (bf16[2,128,128]{2,1,0:T(8,128)(2,1)S(1)}, bf16[2,128,128]{2,1,0:T(8,128)(2,1)S(1)}, u32[]{:S(2)}, u32[]{:S(2)}) collective-permute-start(bf16[2,128,128]{2,1,0:T(8,128)(2,1)S(1)} %get-tuple-element.107), channel_id=1, source_target_pairs={{0,4},{1,5},{2,6},{3,7},{4,0},{5,1},{6,2},{7,3},{8,12},{9,13},{10,... | collective-permute-start | bytes 196616 | tf_op jit(solution)/shard_map/ppermute | solution.py:325
  8.7 2.0 %collective-permute-start.2 = (bf16[2,128,128]{2,1,0:T(8,128)(2,1)S(1)}, bf16[2,128,128]{2,1,0:T(8,128)(2,1)S(1)}, u32[]{:S(2)}, u32[]{:S(2)}) collective-permute-start(bf16[2,128,128]{2,1,0:T(8,128)(2,1)S(1)} %get-tuple-element.103), channel_id=1, source_target_pairs={{0,2},{1,3},{2,0},{3,1},{4,6},{5,7},{6,4},{7,5},{8,10},{9,11},{10,... | collective-permute-start | bytes 196616 | tf_op jit(solution)/shard_map/ppermute | solution.py:325
  10.7 1.5 %collective-permute-start.3 = (bf16[2,128,128]{2,1,0:T(8,128)(2,1)S(1)}, bf16[2,128,128]{2,1,0:T(8,128)(2,1)S(1)}, u32[]{:S(2)}, u32[]{:S(2)}) collective-permute-start(bf16[2,128,128]{2,1,0:T(8,128)(2,1)S(1)} %get-tuple-element.104), channel_id=1, source_target_pairs={{0,4},{1,5},{2,6},{3,7},{4,0},{5,1},{6,2},{7,3},{8,12},{9,13},{10,... | collective-permute-start | bytes 196616 | tf_op jit(solution)/shard_map/ppermute | solution.py:325
  12.5 1.3 %collective-permute-done.7.refs_3_ = bf16[2,128,128]{2,1,0:T(8,128)(2,1)S(1)} collective-permute-done((bf16[2,128,128]{2,1,0:T(8,128)(2,1)S(1)}, bf16[2,128,128]{2,1,0:T(8,128)(2,1)S(1)}, u32[]{:S(2)}, u32[]{:S(2)}) %collective-permute-start.7) | collective-permute-done | bytes 65568 | tf_op jit(solution)/shard_map/ppermute | solution.py:325
  13.8 2.7 %collective-permute-start.12 = (bf16[128,128]{1,0:T(8,128)(2,1)S(1)}, bf16[128,128]{1,0:T(8,128)(2,1)S(1)}, u32[]{:S(2)}, u32[]{:S(2)}) collective-permute-start(bf16[128,128]{1,0:T(8,128)(2,1)S(1)} %get-tuple-element.113), channel_id=1, source_target_pairs={{0,16},{8,24},{16,0},{24,8},{1,17},{9,25},{17,1},{25,9},{2,18},{10... | collective-permute-start | bytes 98312 | tf_op jit(solution)/shard_map/ppermute | solution.py:325
  16.5 1.6 %collective-permute-start.13 = (bf16[128,128]{1,0:T(8,128)(2,1)S(1)}, bf16[128,128]{1,0:T(8,128)(2,1)S(1)}, u32[]{:S(2)}, u32[]{:S(2)}) collective-permute-start(bf16[128,128]{1,0:T(8,128)(2,1)S(1)} %get-tuple-element.114), channel_id=1, source_target_pairs={{0,8},{8,0},{16,24},{24,16},{1,9},{9,1},{17,25},{25,17},{2,10},{10... | collective-permute-start | bytes 98312 | tf_op jit(solution)/shard_map/ppermute | solution.py:325
  18.3 1.8 %collective-permute-start.9 = (bf16[128,128]{1,0:T(8,128)(2,1)S(1)}, bf16[128,128]{1,0:T(8,128)(2,1)S(1)}, u32[]{:S(2)}, u32[]{:S(2)}) collective-permute-start(bf16[128,128]{1,0:T(8,128)(2,1)S(1)} %get-tuple-element.111), channel_id=1, source_target_pairs={{0,16},{8,24},{16,0},{24,8},{1,17},{9,25},{17,1},{25,9},{2,18},{10... | collective-permute-start | bytes 98312 | tf_op jit(solution)/shard_map/ppermute | solution.py:325
  20.1 0.7 %collective-permute-done.13.refs_6_ = bf16[128,128]{1,0:T(8,128)(2,1)S(1)} collective-permute-done((bf16[128,128]{1,0:T(8,128)(2,1)S(1)}, bf16[128,128]{1,0:T(8,128)(2,1)S(1)}, u32[]{:S(2)}, u32[]{:S(2)}) %collective-permute-start.13) | collective-permute-done | bytes 32800 | tf_op jit(solution)/shard_map/ppermute | solution.py:325
  20.8 3.0 %collective-permute-done.11.refs_4_ = bf16[128,128]{1,0:T(8,128)(2,1)S(1)} collective-permute-done((bf16[128,128]{1,0:T(8,128)(2,1)S(1)}, bf16[128,128]{1,0:T(8,128)(2,1)S(1)}, u32[]{:S(2)}, u32[]{:S(2)}) %collective-permute-start.11) | collective-permute-done | bytes 32800 | tf_op jit(solution)/shard_map/ppermute | solution.py:325
  24.0 1.3 %collective-permute-start.17 = (bf16[2,128,128]{2,1,0:T(8,128)(2,1)S(1)}, bf16[2,128,128]{2,1,0:T(8,128)(2,1)S(1)}, u32[]{:S(2)}, u32[]{:S(2)}) collective-permute-start(bf16[2,128,128]{2,1,0:T(8,128)(2,1)S(1)} %get-tuple-element.124), channel_id=1, source_target_pairs={{0,2},{1,3},{2,0},{3,1},{4,6},{5,7},{6,4},{7,5},{8,10},{9,11},{10,... | collective-permute-start | bytes 196616 | tf_op jit(solution)/shard_map/ppermute | solution.py:325
  25.3 0.8 %collective-permute-start.18 = (bf16[2,128,128]{2,1,0:T(8,128)(2,1)S(1)}, bf16[2,128,128]{2,1,0:T(8,128)(2,1)S(1)}, u32[]{:S(2)}, u32[]{:S(2)}) collective-permute-start(bf16[2,128,128]{2,1,0:T(8,128)(2,1)S(1)} %get-tuple-element.125), channel_id=1, source_target_pairs={{0,4},{1,5},{2,6},{3,7},{4,0},{5,1},{6,2},{7,3},{8,12},{9,13},{10,... | collective-permute-start | bytes 196616 | tf_op jit(solution)/shard_map/ppermute | solution.py:325
  26.1 1.4 %collective-permute-start.19 = (bf16[2,128,128]{2,1,0:T(8,128)(2,1)S(1)}, bf16[2,128,128]{2,1,0:T(8,128)(2,1)S(1)}, u32[]{:S(2)}, u32[]{:S(2)}) collective-permute-start(bf16[2,128,128]{2,1,0:T(8,128)(2,1)S(1)} %get-tuple-element.126), channel_id=1, source_target_pairs={{0,6},{1,7},{2,4},{3,5},{4,2},{5,3},{6,0},{7,1},{8,14},{9,15},{10,... | collective-permute-start | bytes 196616 | tf_op jit(solution)/shard_map/ppermute | solution.py:325
  27.9 3.6 %collective-permute-done.10.refs_6_ = bf16[128,128]{1,0:T(8,128)(2,1)S(1)} collective-permute-done((bf16[128,128]{1,0:T(8,128)(2,1)S(1)}, bf16[128,128]{1,0:T(8,128)(2,1)S(1)}, u32[]{:S(2)}, u32[]{:S(2)}) %collective-permute-start.10) | collective-permute-done | bytes 32800 | tf_op jit(solution)/shard_map/ppermute | solution.py:325
  31.4 1.8 %collective-permute-done.8.refs_4_ = bf16[128,128]{1,0:T(8,128)(2,1)S(1)} collective-permute-done((bf16[128,128]{1,0:T(8,128)(2,1)S(1)}, bf16[128,128]{1,0:T(8,128)(2,1)S(1)}, u32[]{:S(2)}, u32[]{:S(2)}) %collective-permute-start.8) | collective-permute-done | bytes 32800 | tf_op jit(solution)/shard_map/ppermute | solution.py:325
  33.6 1.3 %collective-permute-start.14 = (bf16[2,128,128]{2,1,0:T(8,128)(2,1)S(1)}, bf16[2,128,128]{2,1,0:T(8,128)(2,1)S(1)}, u32[]{:S(2)}, u32[]{:S(2)}) collective-permute-start(bf16[2,128,128]{2,1,0:T(8,128)(2,1)S(1)} %get-tuple-element.117), channel_id=1, source_target_pairs={{0,2},{1,3},{2,0},{3,1},{4,6},{5,7},{6,4},{7,5},{8,10},{9,11},{10,... | collective-permute-start | bytes 196616 | tf_op jit(solution)/shard_map/ppermute | solution.py:325
  35.0 0.8 %collective-permute-start.15 = (bf16[2,128,128]{2,1,0:T(8,128)(2,1)S(1)}, bf16[2,128,128]{2,1,0:T(8,128)(2,1)S(1)}, u32[]{:S(2)}, u32[]{:S(2)}) collective-permute-start(bf16[2,128,128]{2,1,0:T(8,128)(2,1)S(1)} %get-tuple-element.118), channel_id=1, source_target_pairs={{0,4},{1,5},{2,6},{3,7},{4,0},{5,1},{6,2},{7,3},{8,12},{9,13},{10,... | collective-permute-start | bytes 196616 | tf_op jit(solution)/shard_map/ppermute | solution.py:325
  35.8 1.4 %collective-permute-start.16 = (bf16[2,128,128]{2,1,0:T(8,128)(2,1)S(1)}, bf16[2,128,128]{2,1,0:T(8,128)(2,1)S(1)}, u32[]{:S(2)}, u32[]{:S(2)}) collective-permute-start(bf16[2,128,128]{2,1,0:T(8,128)(2,1)S(1)} %get-tuple-element.119), channel_id=1, source_target_pairs={{0,6},{1,7},{2,4},{3,5},{4,2},{5,3},{6,0},{7,1},{8,14},{9,15},{10,... | collective-permute-start | bytes 196616 | tf_op jit(solution)/shard_map/ppermute | solution.py:325
  37.2 2.1 %local.1 = (f32[128,512]{1,0:T(8,128)S(1)}, f32[128,512]{1,0:T(8,128)S(1)}, f32[128,512]{1,0:T(8,128)S(1)}, f32[128,512]{1,0:T(8,128)S(1)}, f32[128,512]{1,0:T(8...) custom-call(bf16[128,512]{1,0:T(8,128)(2,1)S(1)} %get-tuple-element., ...), custom_call_target="tpu_custom_call" | custom-call | flops 402653184 | bytes 6291456 | tf_op jit(solution)/shard_map/local/pallas_call | solution.py:253
  39.4 1.8 %finish.4 = (bf16[128,2048]{1,0:T(8,128)(2,1)}, bf16[128,2048]{1,0:T(8,128)(2,1)}, bf16[128,2048]{1,0:T(8,128)(2,1)}, bf16[128,2048]{1,0:T(8,128)(2,1)}, f32[8,128]{1,0:T(8,128)}) custom-call(bf16[128,512]{1,0:T(8,128)(2,1)S(1)} %get-tuple-element.82.refs_0_, bf16[128,512]{1,0:T(8,128)(2,1)S(1)} %get-tuple-element.83.refs_1_, ...), custom_call_target="tpu_custom_call" | custom-call | flops 67108864 | bytes 2228224 | tf_op jit(solution)/shard_map/finish/pallas_call | solution.py:308
  41.2 1.1 %finish.5 = (bf16[128,2048]{1,0:T(8,128)(2,1)}, bf16[128,2048]{1,0:T(8,128)(2,1)}, bf16[128,2048]{1,0:T(8,128)(2,1)}, bf16[128,2048]{1,0:T(8,128)(2,1)}, f32[8,128]{1,0:T(8,128)S(1)}) custom-call(bf16[128,512]{1,0:T(8,128)(2,1)S(1)} %get-tuple-element.90.refs_8_.refs_0_, ...), custom_call_target="tpu_custom_call", output_to_operand_aliasing={{0}: (9, {}), {1}: (10, {}), {2}: (11, {}), {3}: (12, {})} | custom-call | flops 67108864 | bytes 2228224 | tf_op jit(solution)/shard_map/finish/pallas_call | solution.py:308
  42.6 1.8 %finish.6 = (bf16[128,2048]{1,0:T(8,128)(2,1)}, bf16[128,2048]{1,0:T(8,128)(2,1)}, bf16[128,2048]{1,0:T(8,128)(2,1)}, bf16[128,2048]{1,0:T(8,128)(2,1)}, f32[8,128]{1,0:T(8,128)}) custom-call(bf16[128,512]{1,0:T(8,128)(2,1)S(1)} %get-tuple-element.86.refs_4_.refs_0_, ...), custom_call_target="tpu_custom_call", output_to_operand_aliasing={{0}: (13, {}), {1}: (14, {}), {2}: (15, {}), {3}: (16, {})} | custom-call | flops 67108864 | bytes 2228224 | tf_op jit(solution)/shard_map/finish/pallas_call | solution.py:308
  44.4 1.7 %finish.7 = (bf16[128,2048]{1,0:T(8,128)(2,1)}, bf16[128,2048]{1,0:T(8,128)(2,1)}, bf16[128,2048]{1,0:T(8,128)(2,1)}, bf16[128,2048]{1,0:T(8,128)(2,1)}, f32[8,128]{1,0:T(8,128)}) custom-call(bf16[128,512]{1,0:T(8,128)(2,1)S(1)} %get-tuple-element.78.refs_12_.refs_0_, ...), custom_call_target="tpu_custom_call", output_to_operand_aliasing={{0}: (9, {}), {1}: (10, {}), {2}: (11, {}), {3}: (12, {})} | custom-call | flops 67108864 | bytes 2228224 | tf_op jit(solution)/shard_map/finish/pallas_call | solution.py:308
  (36 shorter events, 3.5 us)
Async XLA Ops:
  2.4 1.7 %collective-permute-start.1 = (bf16[2,512,128]{2,1,0:T(8,128)(2,1)S(1)}, bf16[2,512,128]{2,1,0:T(8,128)(2,1)S(1)}, u32[]{:S(2)}, u32[]{:S(2)}) collective-permute-start(bf16[2,512,128]{2,1,0:T(8,128)(2,1)S(1)} %get-tuple-element.100), channel_id=1, source_target_pairs={{0,1},{1,0},{2,3},{3,2},{4,5},{5,4},{6,7},{7,6},{8,9},{9,8},{10,11... | collective-permute-start | bytes 786440 | tf_op jit(solution)/shard_map/ppermute | solution.py:325
  3.2 5.4 %collective-permute-start = (bf16[2,512,128]{2,1,0:T(8,128)(2,1)S(1)}, bf16[2,512,128]{2,1,0:T(8,128)(2,1)S(1)}, u32[]{:S(2)}, u32[]{:S(2)}) collective-permute-start(bf16[2,512,128]{2,1,0:T(8,128)(2,1)S(1)} %sums.3), channel_id=1, source_target_pairs={{0,1},{1,0},{2,3},{3,2},{4,5},{5,4},{6,7},{7,6},{8,9},{9,8},{10,11... | collective-permute-start | bytes 786440 | tf_op jit(solution)/shard_map/ppermute | solution.py:325
  4.2 8.1 %collective-permute-start.5 = (bf16[2,128,128]{2,1,0:T(8,128)(2,1)S(1)}, bf16[2,128,128]{2,1,0:T(8,128)(2,1)S(1)}, u32[]{:S(2)}, u32[]{:S(2)}) collective-permute-start(bf16[2,128,128]{2,1,0:T(8,128)(2,1)S(1)} %get-tuple-element.106), channel_id=1, source_target_pairs={{0,2},{1,3},{2,0},{3,1},{4,6},{5,7},{6,4},{7,5},{8,10},{9,11},{10,... | collective-permute-start | bytes 196616 | tf_op jit(solution)/shard_map/ppermute | solution.py:325
  7.1 5.4 %collective-permute-start.6 = (bf16[2,128,128]{2,1,0:T(8,128)(2,1)S(1)}, bf16[2,128,128]{2,1,0:T(8,128)(2,1)S(1)}, u32[]{:S(2)}, u32[]{:S(2)}) collective-permute-start(bf16[2,128,128]{2,1,0:T(8,128)(2,1)S(1)} %get-tuple-element.107), channel_id=1, source_target_pairs={{0,4},{1,5},{2,6},{3,7},{4,0},{5,1},{6,2},{7,3},{8,12},{9,13},{10,... | collective-permute-start | bytes 196616 | tf_op jit(solution)/shard_map/ppermute | solution.py:325
  8.6 5.2 %collective-permute-start.7 = (bf16[2,128,128]{2,1,0:T(8,128)(2,1)S(1)}, bf16[2,128,128]{2,1,0:T(8,128)(2,1)S(1)}, u32[]{:S(2)}, u32[]{:S(2)}) collective-permute-start(bf16[2,128,128]{2,1,0:T(8,128)(2,1)S(1)} %get-tuple-element.108), channel_id=1, source_target_pairs={{0,6},{1,7},{2,4},{3,5},{4,2},{5,3},{6,0},{7,1},{8,14},{9,15},{10,... | collective-permute-start | bytes 196616 | tf_op jit(solution)/shard_map/ppermute | solution.py:325
  8.7 9.4 %collective-permute-start.2 = (bf16[2,128,128]{2,1,0:T(8,128)(2,1)S(1)}, bf16[2,128,128]{2,1,0:T(8,128)(2,1)S(1)}, u32[]{:S(2)}, u32[]{:S(2)}) collective-permute-start(bf16[2,128,128]{2,1,0:T(8,128)(2,1)S(1)} %get-tuple-element.103), channel_id=1, source_target_pairs={{0,2},{1,3},{2,0},{3,1},{4,6},{5,7},{6,4},{7,5},{8,10},{9,11},{10,... | collective-permute-start | bytes 196616 | tf_op jit(solution)/shard_map/ppermute | solution.py:325
  10.7 7.6 %collective-permute-start.3 = (bf16[2,128,128]{2,1,0:T(8,128)(2,1)S(1)}, bf16[2,128,128]{2,1,0:T(8,128)(2,1)S(1)}, u32[]{:S(2)}, u32[]{:S(2)}) collective-permute-start(bf16[2,128,128]{2,1,0:T(8,128)(2,1)S(1)} %get-tuple-element.104), channel_id=1, source_target_pairs={{0,4},{1,5},{2,6},{3,7},{4,0},{5,1},{6,2},{7,3},{8,12},{9,13},{10,... | collective-permute-start | bytes 196616 | tf_op jit(solution)/shard_map/ppermute | solution.py:325
  12.2 6.1 %collective-permute-start.4 = (bf16[2,128,128]{2,1,0:T(8,128)(2,1)S(1)}, bf16[2,128,128]{2,1,0:T(8,128)(2,1)S(1)}, u32[]{:S(2)}, u32[]{:S(2)}) collective-permute-start(bf16[2,128,128]{2,1,0:T(8,128)(2,1)S(1)} %get-tuple-element.105), channel_id=1, source_target_pairs={{0,6},{1,7},{2,4},{3,5},{4,2},{5,3},{6,0},{7,1},{8,14},{9,15},{10,... | collective-permute-start | bytes 196616 | tf_op jit(solution)/shard_map/ppermute | solution.py:325
  13.8 6.3 %collective-permute-start.12 = (bf16[128,128]{1,0:T(8,128)(2,1)S(1)}, bf16[128,128]{1,0:T(8,128)(2,1)S(1)}, u32[]{:S(2)}, u32[]{:S(2)}) collective-permute-start(bf16[128,128]{1,0:T(8,128)(2,1)S(1)} %get-tuple-element.113), channel_id=1, source_target_pairs={{0,16},{8,24},{16,0},{24,8},{1,17},{9,25},{17,1},{25,9},{2,18},{10... | collective-permute-start | bytes 98312 | tf_op jit(solution)/shard_map/ppermute | solution.py:325
  16.5 4.3 %collective-permute-start.13 = (bf16[128,128]{1,0:T(8,128)(2,1)S(1)}, bf16[128,128]{1,0:T(8,128)(2,1)S(1)}, u32[]{:S(2)}, u32[]{:S(2)}) collective-permute-start(bf16[128,128]{1,0:T(8,128)(2,1)S(1)} %get-tuple-element.114), channel_id=1, source_target_pairs={{0,8},{8,0},{16,24},{24,16},{1,9},{9,1},{17,25},{25,17},{2,10},{10... | collective-permute-start | bytes 98312 | tf_op jit(solution)/shard_map/ppermute | solution.py:325
  18.1 5.7 %collective-permute-start.11 = (bf16[128,128]{1,0:T(8,128)(2,1)S(1)}, bf16[128,128]{1,0:T(8,128)(2,1)S(1)}, u32[]{:S(2)}, u32[]{:S(2)}) collective-permute-start(bf16[128,128]{1,0:T(8,128)(2,1)S(1)} %get-tuple-element.109.refs_4_), channel_id=1, source_target_pairs={{0,24},{8,16},{16,8},{24,0},{1,25},{9,17},{17,9},{25,1},{2,26},{10... | collective-permute-start | bytes 98312 | tf_op jit(solution)/shard_map/ppermute | solution.py:325
  18.3 9.2 %collective-permute-start.9 = (bf16[128,128]{1,0:T(8,128)(2,1)S(1)}, bf16[128,128]{1,0:T(8,128)(2,1)S(1)}, u32[]{:S(2)}, u32[]{:S(2)}) collective-permute-start(bf16[128,128]{1,0:T(8,128)(2,1)S(1)} %get-tuple-element.111), channel_id=1, source_target_pairs={{0,16},{8,24},{16,0},{24,8},{1,17},{9,25},{17,1},{25,9},{2,18},{10... | collective-permute-start | bytes 98312 | tf_op jit(solution)/shard_map/ppermute | solution.py:325
  24.0 9.5 %collective-permute-start.17 = (bf16[2,128,128]{2,1,0:T(8,128)(2,1)S(1)}, bf16[2,128,128]{2,1,0:T(8,128)(2,1)S(1)}, u32[]{:S(2)}, u32[]{:S(2)}) collective-permute-start(bf16[2,128,128]{2,1,0:T(8,128)(2,1)S(1)} %get-tuple-element.124), channel_id=1, source_target_pairs={{0,2},{1,3},{2,0},{3,1},{4,6},{5,7},{6,4},{7,5},{8,10},{9,11},{10,... | collective-permute-start | bytes 196616 | tf_op jit(solution)/shard_map/ppermute | solution.py:325
  25.3 8.1 %collective-permute-start.18 = (bf16[2,128,128]{2,1,0:T(8,128)(2,1)S(1)}, bf16[2,128,128]{2,1,0:T(8,128)(2,1)S(1)}, u32[]{:S(2)}, u32[]{:S(2)}) collective-permute-start(bf16[2,128,128]{2,1,0:T(8,128)(2,1)S(1)} %get-tuple-element.125), channel_id=1, source_target_pairs={{0,4},{1,5},{2,6},{3,7},{4,0},{5,1},{6,2},{7,3},{8,12},{9,13},{10,... | collective-permute-start | bytes 196616 | tf_op jit(solution)/shard_map/ppermute | solution.py:325
  26.1 7.4 %collective-permute-start.19 = (bf16[2,128,128]{2,1,0:T(8,128)(2,1)S(1)}, bf16[2,128,128]{2,1,0:T(8,128)(2,1)S(1)}, u32[]{:S(2)}, u32[]{:S(2)}) collective-permute-start(bf16[2,128,128]{2,1,0:T(8,128)(2,1)S(1)} %get-tuple-element.126), channel_id=1, source_target_pairs={{0,6},{1,7},{2,4},{3,5},{4,2},{5,3},{6,0},{7,1},{8,14},{9,15},{10,... | collective-permute-start | bytes 196616 | tf_op jit(solution)/shard_map/ppermute | solution.py:325
  27.5 3.9 %collective-permute-start.10 = (bf16[128,128]{1,0:T(8,128)(2,1)S(1)}, bf16[128,128]{1,0:T(8,128)(2,1)S(1)}, u32[]{:S(2)}, u32[]{:S(2)}) collective-permute-start(bf16[128,128]{1,0:T(8,128)(2,1)S(1)} %get-tuple-element.112), channel_id=1, source_target_pairs={{0,8},{8,0},{16,24},{24,16},{1,9},{9,1},{17,25},{25,17},{2,10},{10... | collective-permute-start | bytes 98312 | tf_op jit(solution)/shard_map/ppermute | solution.py:325
  27.5 5.7 %collective-permute-start.8 = (bf16[128,128]{1,0:T(8,128)(2,1)S(1)}, bf16[128,128]{1,0:T(8,128)(2,1)S(1)}, u32[]{:S(2)}, u32[]{:S(2)}) collective-permute-start(bf16[128,128]{1,0:T(8,128)(2,1)S(1)} %get-tuple-element.110.refs_7_), channel_id=1, source_target_pairs={{0,24},{8,16},{16,8},{24,0},{1,25},{9,17},{17,9},{25,1},{2,26},{10... | collective-permute-start | bytes 98312 | tf_op jit(solution)/shard_map/ppermute | solution.py:325
  33.6 7.6 %collective-permute-start.20 = (bf16[2,512,128]{2,1,0:T(8,128)(2,1)S(1)}, bf16[2,512,128]{2,1,0:T(8,128)(2,1)S(1)}, u32[]{:S(2)}, u32[]{:S(2)}) collective-permute-start(bf16[2,512,128]{2,1,0:T(8,128)(2,1)S(1)} %theirs.2), channel_id=1, source_target_pairs={{0,1},{1,0},{2,3},{3,2},{4,5},{5,4},{6,7},{7,6},{8,9},{9,8},{10,11... | collective-permute-start | bytes 786440 | tf_op jit(solution)/shard_map/ppermute | solution.py:325
  33.6 8.7 %collective-permute-start.14 = (bf16[2,128,128]{2,1,0:T(8,128)(2,1)S(1)}, bf16[2,128,128]{2,1,0:T(8,128)(2,1)S(1)}, u32[]{:S(2)}, u32[]{:S(2)}) collective-permute-start(bf16[2,128,128]{2,1,0:T(8,128)(2,1)S(1)} %get-tuple-element.117), channel_id=1, source_target_pairs={{0,2},{1,3},{2,0},{3,1},{4,6},{5,7},{6,4},{7,5},{8,10},{9,11},{10,... | collective-permute-start | bytes 196616 | tf_op jit(solution)/shard_map/ppermute | solution.py:325
  35.0 7.4 %collective-permute-start.15 = (bf16[2,128,128]{2,1,0:T(8,128)(2,1)S(1)}, bf16[2,128,128]{2,1,0:T(8,128)(2,1)S(1)}, u32[]{:S(2)}, u32[]{:S(2)}) collective-permute-start(bf16[2,128,128]{2,1,0:T(8,128)(2,1)S(1)} %get-tuple-element.118), channel_id=1, source_target_pairs={{0,4},{1,5},{2,6},{3,7},{4,0},{5,1},{6,2},{7,3},{8,12},{9,13},{10,... | collective-permute-start | bytes 196616 | tf_op jit(solution)/shard_map/ppermute | solution.py:325
  35.8 6.6 %collective-permute-start.16 = (bf16[2,128,128]{2,1,0:T(8,128)(2,1)S(1)}, bf16[2,128,128]{2,1,0:T(8,128)(2,1)S(1)}, u32[]{:S(2)}, u32[]{:S(2)}) collective-permute-start(bf16[2,128,128]{2,1,0:T(8,128)(2,1)S(1)} %get-tuple-element.119), channel_id=1, source_target_pairs={{0,6},{1,7},{2,4},{3,5},{4,2},{5,3},{6,0},{7,1},{8,14},{9,15},{10,... | collective-permute-start | bytes 196616 | tf_op jit(solution)/shard_map/ppermute | solution.py:325
  42.5 1.9 %collective-permute-start.21 = (bf16[2,512,128]{2,1,0:T(8,128)(2,1)S(1)}, bf16[2,512,128]{2,1,0:T(8,128)(2,1)S(1)}, u32[]{:S(2)}, u32[]{:S(2)}) collective-permute-start(bf16[2,512,128]{2,1,0:T(8,128)(2,1)S(1)} %theirs.3), channel_id=1, source_target_pairs={{0,1},{1,0},{2,3},{3,2},{4,5},{5,4},{6,7},{7,6},{8,9},{9,8},{10,11... | collective-permute-start | bytes 786440 | tf_op jit(solution)/shard_map/ppermute | solution.py:325

commit v10 on v7

v10 whole, which is shorter than its diff:
```python
import functools

import jax
import jax.numpy as jnp
from jax import lax
from jax.experimental import pallas as pl
from jax.experimental.pallas import tpu as pltpu
from jax.sharding import PartitionSpec as P

HEAD = 128
PIECES = 4
MIB = 1024 * 1024
ANY = pl.BlockSpec(memory_space=pl.ANY)
VMEM = pl.BlockSpec(memory_space=pltpu.VMEM)
BF16 = jnp.bfloat16
F32 = jnp.float32
SMALL = pltpu.CompilerParams(vmem_limit_bytes=4 * MIB)


def dot(a, b, over_a, over_b):
    return lax.dot_general(
        a, b, (((over_a,), (over_b,)), ((), ())), preferred_element_type=F32
    )


def near_far():
    inner = lax.axis_index("inner")
    return lax.rem(inner, 2), lax.div(inner, 2)


def distances(outer_count):
    return range(outer_count - 1, 0, -1)


def block_start(own, block, half):
    near, far = near_far()
    side = near if own else 1 - near
    top = lax.div(far, lax.axis_size("inner") // 4)
    return side * half + (1 - top if block else top) * (half // 2)


def columns(start, n):
    return pl.ds(pl.multiple_of(start + n * HEAD, HEAD), HEAD)


def slot_rows(s, count, depth):
    _, far = near_far()
    return pl.ds(pl.multiple_of(lax.rem(far ^ s, count) * depth, depth), depth)


def sums_of(tokens, start, out):
    for n in range(out.shape[1] // HEAD):
        q, k, v, d = (ref[:, columns(start, n)] for ref in tokens)
        out[0, n * HEAD : (n + 1) * HEAD] = dot(k, v, 0, 0).astype(BF16)
        out[1, n * HEAD : (n + 1) * HEAD] = dot(q, d, 0, 0).astype(BF16)


def load_kernel(*refs):
    tokens, held, (out, sems) = refs[:4], refs[4:8], refs[8:]
    copies = [
        pltpu.make_async_copy(ref, to, sems.at[i]) for i, (ref, to) in enumerate(zip(tokens, held))
    ]
    for copy in copies:
        copy.start()
    for copy in copies:
        copy.wait()
    sums_of(held, block_start(False, 0, held[0].shape[1] // 2), out)


def load(tokens):
    rows, width = tokens[0].shape
    *held, sums = pl.pallas_call(
        load_kernel,
        name="load",
        in_specs=[ANY] * 4,
        out_specs=[VMEM] * 5,
        out_shape=[pltpu.VMEM((rows, width), BF16)] * 4 + [pltpu.VMEM((2, width // 4, HEAD), BF16)],
        scratch_shapes=[pltpu.SemaphoreType.DMA((4,))],
        cost_estimate=pl.CostEstimate(
            flops=rows * width * HEAD, bytes_accessed=10 * rows * width, transcendentals=0
        ),
        compiler_params=SMALL,
    )(*(pltpu.with_memory_space_constraint(x, pltpu.HBM) for x in tokens))
    return tuple(held), sums


def sums_kernel(wanted, *refs):
    for (own, block), out in zip(wanted, refs[4:]):
        sums_of(refs[:4], block_start(own, block, refs[0].shape[1] // 2), out)


def sums(tokens, *wanted):
    rows, width = tokens[0].shape
    return pl.pallas_call(
        functools.partial(sums_kernel, wanted),
        name="sums",
        in_specs=[VMEM] * 4,
        out_specs=[VMEM] * len(wanted),
        out_shape=[jax.ShapeDtypeStruct((2, width // 4, HEAD), BF16)] * len(wanted),
        cost_estimate=pl.CostEstimate(
            flops=rows * width * HEAD * len(wanted),
            bytes_accessed=3 * rows * width * len(wanted),
            transcendentals=0,
        ),
        compiler_params=SMALL,
    )(*tokens)


def pair_kernel(keep_ref, got_ref, *slots):
    for s, slot in enumerate(slots):
        part = slot_rows(s, len(slots), slot.shape[1])
        for which in range(2):
            both = keep_ref[which, part].astype(F32) + got_ref[which, part].astype(F32)
            slot[which] = both.astype(BF16)


def pair_slots(keep, got, count):
    slot = jax.ShapeDtypeStruct((2, keep.shape[1] // count, HEAD), BF16)
    return pl.pallas_call(
        pair_kernel,
        name="pair",
        in_specs=[VMEM] * 2,
        out_specs=[VMEM] * count,
        out_shape=[slot] * count,
        compiler_params=SMALL,
    )(keep, got)


def totals_kernel(far_count, *refs):
    slots, sends = refs[:far_count], refs[far_count:]
    outer = lax.axis_index("outer")
    totals = []
    for which in range(2):
        total = slots[0][which].astype(F32)
        for slot in slots[1:]:
            total += slot[which].astype(F32)
        totals.append(total.astype(BF16))
    for s, send in zip(distances(len(sends) + 1), sends):
        upward = (outer ^ s) > outer
        send[...] = jnp.where(upward, totals[0], totals[1])


def group_sends(slots, outer_count):
    send = jax.ShapeDtypeStruct(slots[0].shape[1:], BF16)
    return pl.pallas_call(
        functools.partial(totals_kernel, len(slots)),
        name="totals",
        in_specs=[VMEM] * len(slots),
        out_specs=[VMEM] * (outer_count - 1),
        out_shape=[send] * (outer_count - 1),
        compiler_params=SMALL,
    )(*slots)


def scan_kernel(far_count, *refs):
    slots, others, outs = refs[:far_count], refs[far_count:-far_count], refs[-far_count:]
    outer = lax.axis_index("outer")
    _, far = near_far()
    for which in range(2):
        base = jnp.zeros(slots[0].shape[1:], F32)
        for s, other in zip(distances(len(others) + 1), others):
            below = (outer ^ s) < outer
            wanted = below if which == 0 else jnp.logical_not(below)
            base += jnp.where(wanted, other[...].astype(F32), 0.0)
        terms = [slot[which].astype(F32) for slot in slots]
        for s, out in enumerate(outs):
            total = base
            for t, term in enumerate(terms):
                if s != t:
                    below = (far ^ t) < (far ^ s)
                    wanted = below if which == 0 else jnp.logical_not(below)
                    total += jnp.where(wanted, term, 0.0)
            out[which] = total.astype(BF16)


def scan_slots(slots, others):
    far_count, slot = len(slots), jax.ShapeDtypeStruct(slots[0].shape, BF16)
    return pl.pallas_call(
        functools.partial(scan_kernel, far_count),
        name="scan",
        in_specs=[VMEM] * (far_count + len(others)),
        out_specs=[VMEM] * far_count,
        out_shape=[slot] * far_count,
        compiler_params=SMALL,
    )(*slots, *others)


def expand(slots, out, extras, extra_which):
    count, depth = len(slots) // 2, slots[0].shape[1]
    for n, slot in enumerate(slots):
        block, s = divmod(n, count)
        part = slot_rows(s, count, depth)
        into = slice(block * count * depth, (block + 1) * count * depth)
        target, extra = out.at[:, into], extras[block]
        for which in range(2):

            @pl.when(extra_which == which)
            def _():
                total = slot[which].astype(F32) + extra[which, part].astype(F32)
                target[which, part] = total.astype(BF16)

            @pl.when(extra_which != which)
            def _():
                target[which, part] = slot[which]


def theirs_kernel(*refs):
    slots, keep, out = refs[:-3], refs[-3:-1], refs[-1]
    near, _ = near_far()
    expand(slots, out, keep, near)


def state_for_neighbour(slots, keep):
    _, block, _ = keep[0].shape
    return pl.pallas_call(
        theirs_kernel,
        name="theirs",
        in_specs=[VMEM] * (len(slots) + 2),
        out_specs=VMEM,
        out_shape=jax.ShapeDtypeStruct((2, 2 * block, HEAD), BF16),
        compiler_params=SMALL,
    )(*slots, *keep)


def local_kernel(*refs):
    tokens, outs = refs[:4], refs[4:]
    rows, width = tokens[0].shape
    at = lax.broadcasted_iota(jnp.int32, (rows, rows), 0)
    to = lax.broadcasted_iota(jnp.int32, (rows, rows), 1)
    lower = at >= to

    def masked(a, b):
        return jnp.where(lower, dot(a, b, 1, 1), 0.0).astype(BF16)

    def second(cols, a, b):
        q, k, v, d = (ref[:, cols] for ref in tokens)
        att, gq, gk, gv = outs
        att[:, cols] = dot(a, v, 1, 0)
        gq[:, cols] = dot(b, k, 1, 0)
        gk[:, cols] = dot(b, q, 0, 0)
        gv[:, cols] = dot(a, d, 0, 0)

    last = None
    for h in range(width // HEAD):
        cols = slice(h * HEAD, (h + 1) * HEAD)
        q, k, v, d = (ref[:, cols] for ref in tokens)
        a, b = masked(q, k), masked(d, v)
        if last:
            second(*last)
        last = (cols, a, b)
    second(*last)


def local_part(tokens):
    rows, width = tokens[0].shape
    return pl.pallas_call(
        local_kernel,
        name="local",
        in_specs=[VMEM] * 4,
        out_specs=[VMEM] * 4,
        out_shape=[jax.ShapeDtypeStruct((rows, width), F32)] * 4,
        cost_estimate=pl.CostEstimate(
            flops=12 * rows * width * HEAD, bytes_accessed=24 * rows * width, transcendentals=0
        ),
        compiler_params=SMALL,
    )(*tokens)


def heads_of(own, p, half):
    piece = half // PIECES
    block, at = divmod(p, PIECES // 2)
    return block_start(own, block, half) + at * piece


def product_piece(scale, own, p, tokens, local, states, held):
    half = states.shape[1]
    piece = half // PIECES
    start = heads_of(own, p, half)
    for n in range(piece // HEAD):
        rows, cols = slice(p * piece + n * HEAD, p * piece + (n + 1) * HEAD), columns(start, n)
        q, k, v, d = (ref[:, cols] for ref in tokens)
        s, g = states[0, rows], states[1, rows]
        parts = (dot(q, s, 1, 0), dot(d, s, 1, 1), dot(v, g, 1, 1), dot(k, g, 1, 0))
        for i, part in enumerate(parts):
            out = (scale * (part + local[i][:, cols])).astype(BF16)
            held[i, :, n * HEAD : (n + 1) * HEAD] = out


def copies_out(own, p, held, outs, sems, half):
    there = pl.ds(pl.multiple_of(heads_of(own, p, half), half // PIECES), half // PIECES)
    return [
        pltpu.make_async_copy(held.at[i], out.at[:, there], sems.at[i, p])
        for i, out in enumerate(outs)
    ]


def finish_own_kernel(scale, slot_count, *refs):
    tokens, local, slots, refs = refs[:4], refs[4:8], refs[8 : 8 + slot_count], refs[8 + slot_count :]
    got, outs, (rest, states, held, sems) = refs[:2], refs[2:6], refs[6:]
    near, _ = near_far()
    expand(slots, states, got, 1 - near)
    half = states.shape[1]
    copies = []
    for p in range(PIECES):
        to = held.at[p] if p < PIECES - 1 else rest
        product_piece(scale, True, p, tokens, local, states, to)
        if p < PIECES - 1:
            copies += copies_out(True, p, to, outs, sems, half)
            for copy in copies[-4:]:
                copy.start()
    for copy in copies:
        copy.wait()


def finish_own(tokens, local, slots, got, scale):
    rows, width = tokens[0].shape
    half = width // 2
    out = jax.ShapeDtypeStruct((rows, width), BF16)
    piece = (4, rows, half // PIECES)
    *outs, rest = pl.pallas_call(
        functools.partial(finish_own_kernel, scale, len(slots)),
        name="finish_own",
        in_specs=[VMEM] * (10 + len(slots)),
        out_specs=[ANY] * 4 + [VMEM],
        out_shape=[out] * 4 + [pltpu.VMEM(piece, BF16)],
        scratch_shapes=[
            pltpu.VMEM((2, half, HEAD), BF16),
            pltpu.VMEM((PIECES - 1, *piece), BF16),
            pltpu.SemaphoreType.DMA((4, PIECES)),
        ],
        cost_estimate=pl.CostEstimate(
            flops=4 * rows * width * HEAD, bytes_accessed=17 * rows * width, transcendentals=0
        ),
        compiler_params=SMALL,
    )(*tokens, *local, *slots, *got)
    return outs, rest


def finish_other_kernel(scale, *refs):
    tokens, local, (states, rest), refs = refs[:4], refs[4:8], refs[8:10], refs[14:]
    outs, (held, sems, rest_sems) = refs[:4], refs[4:]
    half = states.shape[1]
    copies = copies_out(True, PIECES - 1, rest, outs, rest_sems, half)
    for copy in copies:
        copy.start()
    for p in range(PIECES):
        product_piece(scale, False, p, tokens, local, states, held.at[p])
        copies += copies_out(False, p, held.at[p], outs, sems, half)
        for copy in copies[-4:]:
            copy.start()
    for copy in copies:
        copy.wait()


def finish_other(tokens, local, states, rest, scale, before):
    rows, width = tokens[0].shape
    out = jax.ShapeDtypeStruct((rows, width), BF16)
    return pl.pallas_call(
        functools.partial(finish_other_kernel, scale),
        name="finish_other",
        in_specs=[VMEM] * 10 + [ANY] * 4,
        out_specs=[ANY] * 4,
        out_shape=[out] * 4,
        scratch_shapes=[
            pltpu.VMEM((PIECES, *rest.shape), BF16),
            pltpu.SemaphoreType.DMA((4, PIECES)),
            pltpu.SemaphoreType.DMA((4, PIECES)),
        ],
        input_output_aliases={10 + i: i for i in range(4)},
        cost_estimate=pl.CostEstimate(
            flops=4 * rows * width * HEAD, bytes_accessed=17 * rows * width, transcendentals=0
        ),
        compiler_params=SMALL,
    )(*tokens, *local, states, rest, *before)


def swap(x, axis, bits):
    return lax.ppermute(x, axis, [(i, i ^ bits) for i in range(lax.axis_size(axis))])


def swap_far(slots):
    return [slots[0]] + [swap(slots[s], "inner", 2 * s) for s in range(1, len(slots))]


def body(queries, keys, values, cotangent):
    far_count = lax.axis_size("inner") // 2
    outer_count = lax.axis_size("outer")
    scale = float(HEAD * queries.shape[0] * 2 * far_count * outer_count) ** (-0.5)
    tokens, give = load((queries, keys, values, cotangent))
    got = [swap(give, "inner", 1), swap(*sums(tokens, (False, 1)), "inner", 1)]
    keep = sums(tokens, (True, 0), (True, 1))
    slots = [slot for b in range(2) for slot in pair_slots(keep[b], got[b], far_count // 2)]
    slots, local = lax.optimization_barrier((swap_far(slots), local_part(tokens)))
    sends = group_sends(slots, outer_count)
    others = [swap(send, "outer", s) for s, send in zip(distances(outer_count), sends)]
    slots = swap_far(scan_slots(slots, others))
    arrived = swap(state_for_neighbour(slots, keep), "inner", 1)
    outs, rest = finish_own(tokens, local, slots, got, scale)
    return tuple(finish_other(tokens, local, arrived, rest, scale, outs))


def solution(mesh):
    spec = P(("outer", "inner"), None)
    return jax.shard_map(
        body, mesh=mesh, in_specs=(spec,) * 4, out_specs=(spec,) * 4, check_vma=False
    )
```

time: 38.6 us -> 36.8 us (0.953)
  waiting for transfers between devices: 15.1 us -> 13.8 us
  Pallas kernels: 9.85 us -> 8.61 us
  starting transfers between devices: 12.8 us -> 13.5 us
    ppermute x11 -> x12, waiting for transfers between devices: 15.1 us -> 13.8 us  [swap(): lax.ppermute(x, axis, [(i, i ^ bits) for i in range(lax.axis_size(axis))])]
    pallas_call x5 -> x6, Pallas kernels: 9.16 us -> 7.94 us  [the longest x1 2.16 us: local_part(): pl.pallas_call(local_kernel, name='local', in_specs=[VMEM] * 4, out_specs...]
    ppermute x11 -> x12, starting transfers between devices: 12.8 us -> 13.5 us  [swap(): lax.ppermute(x, axis, [(i, i ^ bits) for i in range(lax.axis_size(axis))])]
  transfers between devices with their start and end apart: 11 -> 12, of which waited for: 8 -> 8; matrix products, arithmetic and copies ran while one was open for 0% -> 0% of each run, Pallas kernels for 15% -> 12%
where the time goes in v10:
time: 36.8 us; the launch traced here: 36.7 us
  waiting for transfers between devices  13.8 us (38%)
  starting transfers between devices  13.5 us (37%)
  Pallas kernels  8.61 us (23%)
  between operations  0.71 us (2%)
    ppermute x12, waiting for transfers between devices, swap(): lax.ppermute(x, axis, [(i, i ^ bits) for i in range(lax.axis_size(axis))])  13.8 us
    ppermute x12, starting transfers between devices, swap(): lax.ppermute(x, axis, [(i, i ^ bits) for i in range(lax.axis_size(axis))])  13.5 us
    pallas_call x1, Pallas kernels, local_part(): pl.pallas_call(local_kernel, name='local', in_specs=[VMEM] * 4, out_specs...  2.16 us
    pallas_call x1, Pallas kernels, load(): pl.pallas_call(load_kernel, name='load', in_specs=[ANY] * 4, out_specs=[V...  1.84 us
    pallas_call x1, Pallas kernels, finish_other(): pl.pallas_call(functools.partial(finish_other_kernel, scale), name='finis...  1.64 us
    pallas_call x1, Pallas kernels, finish_own(): pl.pallas_call(functools.partial(finish_own_kernel, scale, len(slots)), n...  1.55 us
    pallas_call x2, Pallas kernels, sums(): pl.pallas_call(functools.partial(sums_kernel, wanted), name='sums', in_sp...  0.75 us
  transfers between devices with their start and end apart: 12, of which 8 were waited for; matrix products, arithmetic and copies ran while one was open for 0% of the time, Pallas kernels for 12%

profile of v10, /device:TPU:0, one launch (start us, length us, event | category | flops | bytes accessed | tf_op | source)
XLA Modules:
  0.0 36.7 jit_solution(1353315879765755872)
XLA Ops:
  0.6 1.8 %load.1 = (bf16[128,2048]{1,0:T(8,128)(2,1)S(1)}, bf16[128,2048]{1,0:T(8,128)(2,1)S(1)}, bf16[128,2048]{1,0:T(8,128)(2,1)S(1)}, bf16[128,2048]{1,0:T(8,128)(2,1)S(1)}, bf16[2,512,128]{2,1,0:T(8,128)(2,1)S(1)}) custom-call(bf16[128,2048]{1,0:T(8,128)(2,1)} %refs_0_.1, bf16[128,2048]{1,0:T(8,128)(2,1)} %refs_1_.1, bf16[128,2048]{1,0:T(8,128)(2,1)} %refs_2_.1, ...), custom_call_target="tpu_custom_call" | custom-call | flops 33554432 | bytes 2621440 | tf_op jit(solution)/shard_map/load/pallas_call | solution.py:72
  2.5 0.5 %collective-permute-start = (bf16[2,512,128]{2,1,0:T(8,128)(2,1)S(1)}, bf16[2,512,128]{2,1,0:T(8,128)(2,1)S(1)}, u32[]{:S(2)}, u32[]{:S(2)}) collective-permute-start(bf16[2,512,128]{2,1,0:T(8,128)(2,1)S(1)} %get-tuple-element.44), channel_id=1, source_target_pairs={{0,1},{1,0},{2,3},{3,2},{4,5},{5,4},{6,7},{7,6},{8,9},{9,8},{10,11... | collective-permute-start | bytes 786440 | tf_op jit(solution)/shard_map/ppermute | solution.py:378
  3.0 0.3 sums.3
  3.4 0.5 %sums.2 = (bf16[2,512,128]{2,1,0:T(8,128)(2,1)S(1)}, bf16[2,512,128]{2,1,0:T(8,128)(2,1)S(1)}) custom-call(bf16[128,2048]{1,0:T(8,128)(2,1)S(1)} %get-tuple-element.39.refs_0_, bf16[128,2048]{1,0:T(8,128)(2,1)S(1)} %get-tuple-element.40.refs_1_, bf16[128,2048]{1,0:T(8,128)(2,1)S(1)} %get-tuple-element.41.refs_2_, bf16[128,2048]{1,0:T(8,128)(2,1)S(1)} %get-tuple-element.42.refs_3_), custom_call_target="tpu_custom_call" | custom-call | flops 67108864 | bytes 1572864 | tf_op jit(solution)/shard_map/sums/pallas_call | solution.py:94
  3.9 0.3 collective-permute-done.got_ref.refs_12_
  4.2 2.9 %collective-permute-start.1 = (bf16[2,256,128]{2,1,0:T(8,128)(2,1)S(1)}, bf16[2,256,128]{2,1,0:T(8,128)(2,1)S(1)}, u32[]{:S(2)}, u32[]{:S(2)}) collective-permute-start(bf16[2,256,128]{2,1,0:T(8,128)(2,1)S(1)} %get-tuple-element.46), channel_id=1, source_target_pairs={{0,2},{1,3},{2,0},{3,1},{4,6},{5,7},{6,4},{7,5},{8,10},{9,11},{10,... | collective-permute-start | bytes 393224 | tf_op jit(solution)/shard_map/ppermute | solution.py:378
  7.2 1.6 %collective-permute-start.3 = (bf16[2,256,128]{2,1,0:T(8,128)(2,1)S(1)}, bf16[2,256,128]{2,1,0:T(8,128)(2,1)S(1)}, u32[]{:S(2)}, u32[]{:S(2)}) collective-permute-start(bf16[2,256,128]{2,1,0:T(8,128)(2,1)S(1)} %get-tuple-element.48), channel_id=1, source_target_pairs={{0,4},{1,5},{2,6},{3,7},{4,0},{5,1},{6,2},{7,3},{8,12},{9,13},{10,... | collective-permute-start | bytes 393224 | tf_op jit(solution)/shard_map/ppermute | solution.py:378
  8.8 0.3 collective-permute-start.4
  9.1 2.2 %local.1 = (f32[128,2048]{1,0:T(8,128)S(1)}, f32[128,2048]{1,0:T(8,128)S(1)}, f32[128,2048]{1,0:T(8,128)S(1)}, f32[128,2048]{1,0:T(8,128)S(1)}) custom-call(bf16[128,2048]{1,0:T(8,128)(2,1)S(1)} %get-tuple-element.39.refs_0_, bf16[128,2048]{1,0:T(8,128)(2,1)S(1)} %get-tuple-element.40.refs_1_, bf16[128,2048]{1,0:T(8,128)(2,1)S(1)} %get-tuple-element.41.refs_2_, ...), custom_call_target="tpu_custom_call" | custom-call | flops 402653184 | bytes 6291456 | tf_op jit(solution)/shard_map/local/pallas_call | solution.py:256
  11.3 4.1 %collective-permute-done.3.refs_2_ = bf16[2,256,128]{2,1,0:T(8,128)(2,1)S(1)} collective-permute-done((bf16[2,256,128]{2,1,0:T(8,128)(2,1)S(1)}, bf16[2,256,128]{2,1,0:T(8,128)(2,1)S(1)}, u32[]{:S(2)}, u32[]{:S(2)}) %collective-permute-start.3) | collective-permute-done | bytes 131104 | tf_op jit(solution)/shard_map/ppermute | solution.py:378
  15.5 3.7 %collective-permute-start.5 = (bf16[256,128]{1,0:T(8,128)(2,1)S(1)}, bf16[256,128]{1,0:T(8,128)(2,1)S(1)}, u32[]{:S(2)}, u32[]{:S(2)}) collective-permute-start(bf16[256,128]{1,0:T(8,128)(2,1)S(1)} %get-tuple-element.62), channel_id=1, source_target_pairs={{0,24},{8,16},{16,8},{24,0},{1,25},{9,17},{17,9},{25,1},{2,26},{10... | collective-permute-start | bytes 196616 | tf_op jit(solution)/shard_map/ppermute | solution.py:378
  19.1 0.8 %collective-permute-start.7 = (bf16[256,128]{1,0:T(8,128)(2,1)S(1)}, bf16[256,128]{1,0:T(8,128)(2,1)S(1)}, u32[]{:S(2)}, u32[]{:S(2)}) collective-permute-start(bf16[256,128]{1,0:T(8,128)(2,1)S(1)} %get-tuple-element.64), channel_id=1, source_target_pairs={{0,8},{8,0},{16,24},{24,16},{1,9},{9,1},{17,25},{25,17},{2,10},{10... | collective-permute-start | bytes 196616 | tf_op jit(solution)/shard_map/ppermute | solution.py:378
  19.9 1.7 %collective-permute-done.5.refs_4_ = bf16[256,128]{1,0:T(8,128)(2,1)S(1)} collective-permute-done((bf16[256,128]{1,0:T(8,128)(2,1)S(1)}, bf16[256,128]{1,0:T(8,128)(2,1)S(1)}, u32[]{:S(2)}, u32[]{:S(2)}) %collective-permute-start.5) | collective-permute-done | bytes 65568 | tf_op jit(solution)/shard_map/ppermute | solution.py:378
  21.6 2.7 %collective-permute-done.6.refs_5_ = bf16[256,128]{1,0:T(8,128)(2,1)S(1)} collective-permute-done((bf16[256,128]{1,0:T(8,128)(2,1)S(1)}, bf16[256,128]{1,0:T(8,128)(2,1)S(1)}, u32[]{:S(2)}, u32[]{:S(2)}) %collective-permute-start.6) | collective-permute-done | bytes 65568 | tf_op jit(solution)/shard_map/ppermute | solution.py:378
  24.3 0.3 scan.1
  24.6 1.3 %collective-permute-start.8 = (bf16[2,256,128]{2,1,0:T(8,128)(2,1)S(1)}, bf16[2,256,128]{2,1,0:T(8,128)(2,1)S(1)}, u32[]{:S(2)}, u32[]{:S(2)}) collective-permute-start(bf16[2,256,128]{2,1,0:T(8,128)(2,1)S(1)} %get-tuple-element.66), channel_id=1, source_target_pairs={{0,2},{1,3},{2,0},{3,1},{4,6},{5,7},{6,4},{7,5},{8,10},{9,11},{10,... | collective-permute-start | bytes 393224 | tf_op jit(solution)/shard_map/ppermute | solution.py:378
  25.9 1.2 %collective-permute-start.9 = (bf16[2,256,128]{2,1,0:T(8,128)(2,1)S(1)}, bf16[2,256,128]{2,1,0:T(8,128)(2,1)S(1)}, u32[]{:S(2)}, u32[]{:S(2)}) collective-permute-start(bf16[2,256,128]{2,1,0:T(8,128)(2,1)S(1)} %get-tuple-element.67), channel_id=1, source_target_pairs={{0,4},{1,5},{2,6},{3,7},{4,0},{5,1},{6,2},{7,3},{8,12},{9,13},{10,... | collective-permute-start | bytes 393224 | tf_op jit(solution)/shard_map/ppermute | solution.py:378
  27.1 1.1 %collective-permute-start.10 = (bf16[2,256,128]{2,1,0:T(8,128)(2,1)S(1)}, bf16[2,256,128]{2,1,0:T(8,128)(2,1)S(1)}, u32[]{:S(2)}, u32[]{:S(2)}) collective-permute-start(bf16[2,256,128]{2,1,0:T(8,128)(2,1)S(1)} %get-tuple-element.68), channel_id=1, source_target_pairs={{0,6},{1,7},{2,4},{3,5},{4,2},{5,3},{6,0},{7,1},{8,14},{9,15},{10,... | collective-permute-start | bytes 393224 | tf_op jit(solution)/shard_map/ppermute | solution.py:378
  28.2 2.8 %collective-permute-done.8.refs_1_.refs_9_ = bf16[2,256,128]{2,1,0:T(8,128)(2,1)S(1)} collective-permute-done((bf16[2,256,128]{2,1,0:T(8,128)(2,1)S(1)}, bf16[2,256,128]{2,1,0:T(8,128)(2,1)S(1)}, u32[]{:S(2)}, u32[]{:S(2)}) %collective-permute-start.8) | collective-permute-done | bytes 131104 | tf_op jit(solution)/shard_map/ppermute | solution.py:378
  31.0 1.0 %collective-permute-done.9.refs_2_.refs_10_ = bf16[2,256,128]{2,1,0:T(8,128)(2,1)S(1)} collective-permute-done((bf16[2,256,128]{2,1,0:T(8,128)(2,1)S(1)}, bf16[2,256,128]{2,1,0:T(8,128)(2,1)S(1)}, u32[]{:S(2)}, u32[]{:S(2)}) %collective-permute-start.9) | collective-permute-done | bytes 131104 | tf_op jit(solution)/shard_map/ppermute | solution.py:378
  32.0 1.0 %collective-permute-done.10.refs_3_.refs_11_ = bf16[2,256,128]{2,1,0:T(8,128)(2,1)S(1)} collective-permute-done((bf16[2,256,128]{2,1,0:T(8,128)(2,1)S(1)}, bf16[2,256,128]{2,1,0:T(8,128)(2,1)S(1)}, u32[]{:S(2)}, u32[]{:S(2)}) %collective-permute-start.10) | collective-permute-done | bytes 131104 | tf_op jit(solution)/shard_map/ppermute | solution.py:378
  33.2 1.6 %finish_own.1 = (bf16[128,2048]{1,0:T(8,128)(2,1)}, bf16[128,2048]{1,0:T(8,128)(2,1)}, bf16[128,2048]{1,0:T(8,128)(2,1)}, bf16[128,2048]{1,0:T(8,128)(2,1)}, bf16[4,128,256]{2,1,0:T(8,128)(2,1)S(1)}) custom-call(bf16[128,2048]{1,0:T(8,128)(2,1)S(1)} %get-tuple-element.39.refs_0_, bf16[128,2048]{1,0:T(8,128)(2,1)S(1)} %get-tuple-element.40.refs_1_, ...), custom_call_target="tpu_custom_call" | custom-call | flops 134217728 | bytes 4456448 | tf_op jit(solution)/shard_map/finish_own/pallas_call | solution.py:320
  34.7 0.3 collective-permute-done.11.refs_8_
  35.1 1.6 %finish_other.1 = (bf16[128,2048]{1,0:T(8,128)(2,1)}, bf16[128,2048]{1,0:T(8,128)(2,1)}, bf16[128,2048]{1,0:T(8,128)(2,1)}, bf16[128,2048]{1,0:T(8,128)(2,1)}) custom-call(bf16[128,2048]{1,0:T(8,128)(2,1)S(1)} %get-tuple-element.39.refs_0_, ...), custom_call_target="tpu_custom_call", output_to_operand_aliasing={{0}: (10, {}), {1}: (11, {}), {2}: (12, {}), {3}: (13, {})} | custom-call | flops 134217728 | bytes 4456448 | tf_op jit(solution)/shard_map/finish_other/pallas_call | solution.py:358
  (11 shorter events, 0.5 us)
Async XLA Ops:
  2.5 1.7 %collective-permute-start = (bf16[2,512,128]{2,1,0:T(8,128)(2,1)S(1)}, bf16[2,512,128]{2,1,0:T(8,128)(2,1)S(1)}, u32[]{:S(2)}, u32[]{:S(2)}) collective-permute-start(bf16[2,512,128]{2,1,0:T(8,128)(2,1)S(1)} %get-tuple-element.44), channel_id=1, source_target_pairs={{0,1},{1,0},{2,3},{3,2},{4,5},{5,4},{6,7},{7,6},{8,9},{9,8},{10,11... | collective-permute-start | bytes 786440 | tf_op jit(solution)/shard_map/ppermute | solution.py:378
  3.3 3.9 %collective-permute-start.2 = (bf16[2,512,128]{2,1,0:T(8,128)(2,1)S(1)}, bf16[2,512,128]{2,1,0:T(8,128)(2,1)S(1)}, u32[]{:S(2)}, u32[]{:S(2)}) collective-permute-start(bf16[2,512,128]{2,1,0:T(8,128)(2,1)S(1)} %sums.3), channel_id=1, source_target_pairs={{0,1},{1,0},{2,3},{3,2},{4,5},{5,4},{6,7},{7,6},{8,9},{9,8},{10,11... | collective-permute-start | bytes 786440 | tf_op jit(solution)/shard_map/ppermute | solution.py:378
  4.2 7.0 %collective-permute-start.1 = (bf16[2,256,128]{2,1,0:T(8,128)(2,1)S(1)}, bf16[2,256,128]{2,1,0:T(8,128)(2,1)S(1)}, u32[]{:S(2)}, u32[]{:S(2)}) collective-permute-start(bf16[2,256,128]{2,1,0:T(8,128)(2,1)S(1)} %get-tuple-element.46), channel_id=1, source_target_pairs={{0,2},{1,3},{2,0},{3,1},{4,6},{5,7},{6,4},{7,5},{8,10},{9,11},{10,... | collective-permute-start | bytes 393224 | tf_op jit(solution)/shard_map/ppermute | solution.py:378
  7.2 8.1 %collective-permute-start.3 = (bf16[2,256,128]{2,1,0:T(8,128)(2,1)S(1)}, bf16[2,256,128]{2,1,0:T(8,128)(2,1)S(1)}, u32[]{:S(2)}, u32[]{:S(2)}) collective-permute-start(bf16[2,256,128]{2,1,0:T(8,128)(2,1)S(1)} %get-tuple-element.48), channel_id=1, source_target_pairs={{0,4},{1,5},{2,6},{3,7},{4,0},{5,1},{6,2},{7,3},{8,12},{9,13},{10,... | collective-permute-start | bytes 393224 | tf_op jit(solution)/shard_map/ppermute | solution.py:378
  8.8 6.5 %collective-permute-start.4 = (bf16[2,256,128]{2,1,0:T(8,128)(2,1)S(1)}, bf16[2,256,128]{2,1,0:T(8,128)(2,1)S(1)}, u32[]{:S(2)}, u32[]{:S(2)}) collective-permute-start(bf16[2,256,128]{2,1,0:T(8,128)(2,1)S(1)} %get-tuple-element.49), channel_id=1, source_target_pairs={{0,6},{1,7},{2,4},{3,5},{4,2},{5,3},{6,0},{7,1},{8,14},{9,15},{10,... | collective-permute-start | bytes 393224 | tf_op jit(solution)/shard_map/ppermute | solution.py:378
  15.5 6.1 %collective-permute-start.5 = (bf16[256,128]{1,0:T(8,128)(2,1)S(1)}, bf16[256,128]{1,0:T(8,128)(2,1)S(1)}, u32[]{:S(2)}, u32[]{:S(2)}) collective-permute-start(bf16[256,128]{1,0:T(8,128)(2,1)S(1)} %get-tuple-element.62), channel_id=1, source_target_pairs={{0,24},{8,16},{16,8},{24,0},{1,25},{9,17},{17,9},{25,1},{2,26},{10... | collective-permute-start | bytes 196616 | tf_op jit(solution)/shard_map/ppermute | solution.py:378
  19.1 5.2 %collective-permute-start.6 = (bf16[256,128]{1,0:T(8,128)(2,1)S(1)}, bf16[256,128]{1,0:T(8,128)(2,1)S(1)}, u32[]{:S(2)}, u32[]{:S(2)}) collective-permute-start(bf16[256,128]{1,0:T(8,128)(2,1)S(1)} %get-tuple-element.63), channel_id=1, source_target_pairs={{0,16},{8,24},{16,0},{24,8},{1,17},{9,25},{17,1},{25,9},{2,18},{10... | collective-permute-start | bytes 196616 | tf_op jit(solution)/shard_map/ppermute | solution.py:378
  19.1 5.2 %collective-permute-start.7 = (bf16[256,128]{1,0:T(8,128)(2,1)S(1)}, bf16[256,128]{1,0:T(8,128)(2,1)S(1)}, u32[]{:S(2)}, u32[]{:S(2)}) collective-permute-start(bf16[256,128]{1,0:T(8,128)(2,1)S(1)} %get-tuple-element.64), channel_id=1, source_target_pairs={{0,8},{8,0},{16,24},{24,16},{1,9},{9,1},{17,25},{25,17},{2,10},{10... | collective-permute-start | bytes 196616 | tf_op jit(solution)/shard_map/ppermute | solution.py:378
  24.6 6.4 %collective-permute-start.8 = (bf16[2,256,128]{2,1,0:T(8,128)(2,1)S(1)}, bf16[2,256,128]{2,1,0:T(8,128)(2,1)S(1)}, u32[]{:S(2)}, u32[]{:S(2)}) collective-permute-start(bf16[2,256,128]{2,1,0:T(8,128)(2,1)S(1)} %get-tuple-element.66), channel_id=1, source_target_pairs={{0,2},{1,3},{2,0},{3,1},{4,6},{5,7},{6,4},{7,5},{8,10},{9,11},{10,... | collective-permute-start | bytes 393224 | tf_op jit(solution)/shard_map/ppermute | solution.py:378
  25.9 6.1 %collective-permute-start.9 = (bf16[2,256,128]{2,1,0:T(8,128)(2,1)S(1)}, bf16[2,256,128]{2,1,0:T(8,128)(2,1)S(1)}, u32[]{:S(2)}, u32[]{:S(2)}) collective-permute-start(bf16[2,256,128]{2,1,0:T(8,128)(2,1)S(1)} %get-tuple-element.67), channel_id=1, source_target_pairs={{0,4},{1,5},{2,6},{3,7},{4,0},{5,1},{6,2},{7,3},{8,12},{9,13},{10,... | collective-permute-start | bytes 393224 | tf_op jit(solution)/shard_map/ppermute | solution.py:378
  27.1 5.9 %collective-permute-start.10 = (bf16[2,256,128]{2,1,0:T(8,128)(2,1)S(1)}, bf16[2,256,128]{2,1,0:T(8,128)(2,1)S(1)}, u32[]{:S(2)}, u32[]{:S(2)}) collective-permute-start(bf16[2,256,128]{2,1,0:T(8,128)(2,1)S(1)} %get-tuple-element.68), channel_id=1, source_target_pairs={{0,6},{1,7},{2,4},{3,5},{4,2},{5,3},{6,0},{7,1},{8,14},{9,15},{10,... | collective-permute-start | bytes 393224 | tf_op jit(solution)/shard_map/ppermute | solution.py:378
  33.1 2.0 %collective-permute-start.11 = (bf16[2,1024,128]{2,1,0:T(8,128)(2,1)S(1)}, bf16[2,1024,128]{2,1,0:T(8,128)(2,1)S(1)}, u32[]{:S(2)}, u32[]{:S(2)}) collective-permute-start(bf16[2,1024,128]{2,1,0:T(8,128)(2,1)S(1)} %theirs.1), channel_id=1, source_target_pairs={{0,1},{1,0},{2,3},{3,2},{4,5},{5,4},{6,7},{7,6},{8,9},{9,8},{10,11... | collective-permute-start | bytes 1572872 | tf_op jit(solution)/shard_map/ppermute | solution.py:378

commit v11 on v10

--- a/solution.py
+++ b/solution.py
@@ -32,10 +32,32 @@
     return range(outer_count - 1, 0, -1)
 
 
+def exchanged(bits):
+    return bits ^ 3 if bits & 3 in (1, 2) and lax.axis_size("inner") > 4 else bits
+
+
+def place_of(side):
+    _, far = near_far()
+    if lax.axis_size("inner") <= 4:
+        return far
+    low, high = lax.rem(far, 2), lax.rem(lax.div(far, 2), 2)
+    other = far + low - high
+    return jnp.where(side == 1, far, other)
+
+
+def far_of(s):
+    near, far = near_far()
+    return jnp.where(near == 1, far ^ s, far ^ exchanged(s))
+
+
+def slot_order(count):
+    return [n ^ (n >> 1) for n in range(count)]
+
+
 def block_start(own, block, half):
-    near, far = near_far()
+    near, _ = near_far()
     side = near if own else 1 - near
-    top = lax.div(far, lax.axis_size("inner") // 4)
+    top = lax.div(place_of(side), lax.axis_size("inner") // 4)
     return side * half + (1 - top if block else top) * (half // 2)
 
 
@@ -44,8 +66,8 @@
 
 
 def slot_rows(s, count, depth):
-    _, far = near_far()
-    return pl.ds(pl.multiple_of(lax.rem(far ^ s, count) * depth, depth), depth)
+    near, _ = near_far()
+    return pl.ds(pl.multiple_of(lax.rem(place_of(near) ^ s, count) * depth, depth), depth)
 
 
 def sums_of(tokens, start, out):
@@ -106,18 +128,19 @@
     )(*tokens)
 
 
-def pair_kernel(keep_ref, got_ref, *slots):
-    for s, slot in enumerate(slots):
+def pair_kernel(block, keep_ref, got_ref, *slots):
+    count = len(slots)
+    for s, slot in zip(slot_order(2 * count)[block * count :], slots):
         part = slot_rows(s, len(slots), slot.shape[1])
         for which in range(2):
             both = keep_ref[which, part].astype(F32) + got_ref[which, part].astype(F32)
             slot[which] = both.astype(BF16)
 
 
-def pair_slots(keep, got, count):
+def pair_slots(block, keep, got, count):
     slot = jax.ShapeDtypeStruct((2, keep.shape[1] // count, HEAD), BF16)
     return pl.pallas_call(
-        pair_kernel,
+        functools.partial(pair_kernel, block),
         name="pair",
         in_specs=[VMEM] * 2,
         out_specs=[VMEM] * count,
@@ -155,7 +178,6 @@
 def scan_kernel(far_count, *refs):
     slots, others, outs = refs[:far_count], refs[far_count:-far_count], refs[-far_count:]
     outer = lax.axis_index("outer")
-    _, far = near_far()
     for which in range(2):
         base = jnp.zeros(slots[0].shape[1:], F32)
         for s, other in zip(distances(len(others) + 1), others):
@@ -163,11 +185,12 @@
             wanted = below if which == 0 else jnp.logical_not(below)
             base += jnp.where(wanted, other[...].astype(F32), 0.0)
         terms = [slot[which].astype(F32) for slot in slots]
+        fars = [far_of(s) for s in slot_order(far_count)]
         for s, out in enumerate(outs):
             total = base
             for t, term in enumerate(terms):
                 if s != t:
-                    below = (far ^ t) < (far ^ s)
+                    below = fars[t] < fars[s]
                     wanted = below if which == 0 else jnp.logical_not(below)
                     total += jnp.where(wanted, term, 0.0)
             out[which] = total.astype(BF16)
@@ -187,8 +210,8 @@
 
 def expand(slots, out, extras, extra_which):
     count, depth = len(slots) // 2, slots[0].shape[1]
-    for n, slot in enumerate(slots):
-        block, s = divmod(n, count)
+    for n, (s, slot) in enumerate(zip(slot_order(2 * count), slots)):
+        block = n // count
         part = slot_rows(s, count, depth)
         into = slice(block * count * depth, (block + 1) * count * depth)
         target, extra = out.at[:, into], extras[block]
@@ -379,7 +402,11 @@
 
 
 def swap_far(slots):
-    return [slots[0]] + [swap(slots[s], "inner", 2 * s) for s in range(1, len(slots))]
+    inner = range(lax.axis_size("inner"))
+    pairs = [
+        [(i, i ^ 2 * (s if i % 2 else exchanged(s))) for i in inner] for s in slot_order(len(slots))
+    ]
+    return [slots[0]] + [lax.ppermute(x, "inner", p) for x, p in zip(slots[1:], pairs[1:])]
 
 
 def body(queries, keys, values, cotangent):
@@ -389,7 +416,7 @@
     tokens, give = load((queries, keys, values, cotangent))
     got = [swap(give, "inner", 1), swap(*sums(tokens, (False, 1)), "inner", 1)]
     keep = sums(tokens, (True, 0), (True, 1))
-    slots = [slot for b in range(2) for slot in pair_slots(keep[b], got[b], far_count // 2)]
+    slots = [slot for b in range(2) for slot in pair_slots(b, keep[b], got[b], far_count // 2)]
     slots, local = lax.optimization_barrier((swap_far(slots), local_part(tokens)))
     sends = group_sends(slots, outer_count)
     others = [swap(send, "outer", s) for s, send in zip(distances(outer_count), sends)]

time: 36.8 us -> 37.6 us (1.022)
  starting transfers between devices: 13.5 us -> 14 us
    ppermute x0 -> x6, waiting for transfers between devices: none -> 8.62 us  [swap_far(): lax.ppermute(x, 'inner', p)]
    ppermute x12 -> x6, waiting for transfers between devices: 13.8 us -> 5.41 us  [swap(): lax.ppermute(x, axis, [(i, i ^ bits) for i in range(lax.axis_size(axis))])]
    ppermute x0 -> x6, starting transfers between devices: none -> 8.39 us  [swap_far(): lax.ppermute(x, 'inner', p)]
    ppermute x12 -> x6, starting transfers between devices: 13.5 us -> 5.65 us  [swap(): lax.ppermute(x, axis, [(i, i ^ bits) for i in range(lax.axis_size(axis))])]
  transfers between devices with their start and end apart: 12 -> 12, of which waited for: 8 -> 6; matrix products, arithmetic and copies ran while one was open for 0% -> 0% of each run, Pallas kernels for 12% -> 12%
where the time goes in v11:
time: 37.6 us; the launch traced here: 37.4 us
  starting transfers between devices  14 us (37%)
  waiting for transfers between devices  14 us (37%)
  Pallas kernels  8.63 us (23%)
  between operations  0.71 us (2%)
    ppermute x6, waiting for transfers between devices, swap_far(): lax.ppermute(x, 'inner', p)  8.62 us
    ppermute x6, starting transfers between devices, swap_far(): lax.ppermute(x, 'inner', p)  8.39 us
    ppermute x6, starting transfers between devices, swap(): lax.ppermute(x, axis, [(i, i ^ bits) for i in range(lax.axis_size(axis))])  5.65 us
    ppermute x6, waiting for transfers between devices, swap(): lax.ppermute(x, axis, [(i, i ^ bits) for i in range(lax.axis_size(axis))])  5.41 us
    pallas_call x1, Pallas kernels, local_part(): pl.pallas_call(local_kernel, name='local', in_specs=[VMEM] * 4, out_specs...  2.16 us
    pallas_call x1, Pallas kernels, load(): pl.pallas_call(load_kernel, name='load', in_specs=[ANY] * 4, out_specs=[V...  1.84 us
    pallas_call x1, Pallas kernels, finish_other(): pl.pallas_call(functools.partial(finish_other_kernel, scale), name='finis...  1.67 us
    pallas_call x1, Pallas kernels, finish_own(): pl.pallas_call(functools.partial(finish_own_kernel, scale, len(slots)), n...  1.52 us
  transfers between devices with their start and end apart: 12, of which 6 were waited for; matrix products, arithmetic and copies ran while one was open for 0% of the time, Pallas kernels for 12%

profile of v11, /device:TPU:0, one launch (start us, length us, event | category | flops | bytes accessed | tf_op | source)
XLA Modules:
  0.0 37.4 jit_solution(11456429352486050939)
XLA Ops:
  0.6 1.8 %load.1 = (bf16[128,2048]{1,0:T(8,128)(2,1)S(1)}, bf16[128,2048]{1,0:T(8,128)(2,1)S(1)}, bf16[128,2048]{1,0:T(8,128)(2,1)S(1)}, bf16[128,2048]{1,0:T(8,128)(2,1)S(1)}, bf16[2,512,128]{2,1,0:T(8,128)(2,1)S(1)}) custom-call(bf16[128,2048]{1,0:T(8,128)(2,1)} %refs_0_.1, bf16[128,2048]{1,0:T(8,128)(2,1)} %refs_1_.1, bf16[128,2048]{1,0:T(8,128)(2,1)} %refs_2_.1, ...), custom_call_target="tpu_custom_call" | custom-call | flops 33554432 | bytes 2621440 | tf_op jit(solution)/shard_map/load/pallas_call | solution.py:94
  2.5 0.5 %collective-permute-start = (bf16[2,512,128]{2,1,0:T(8,128)(2,1)S(1)}, bf16[2,512,128]{2,1,0:T(8,128)(2,1)S(1)}, u32[]{:S(2)}, u32[]{:S(2)}) collective-permute-start(bf16[2,512,128]{2,1,0:T(8,128)(2,1)S(1)} %get-tuple-element.44), channel_id=1, source_target_pairs={{0,1},{1,0},{2,3},{3,2},{4,5},{5,4},{6,7},{7,6},{8,9},{9,8},{10,11... | collective-permute-start | bytes 786440 | tf_op jit(solution)/shard_map/ppermute | solution.py:401
  3.0 0.3 sums.3
  3.4 0.5 %sums.2 = (bf16[2,512,128]{2,1,0:T(8,128)(2,1)S(1)}, bf16[2,512,128]{2,1,0:T(8,128)(2,1)S(1)}) custom-call(bf16[128,2048]{1,0:T(8,128)(2,1)S(1)} %get-tuple-element.39.refs_0_, bf16[128,2048]{1,0:T(8,128)(2,1)S(1)} %get-tuple-element.40.refs_1_, bf16[128,2048]{1,0:T(8,128)(2,1)S(1)} %get-tuple-element.41.refs_2_, bf16[128,2048]{1,0:T(8,128)(2,1)S(1)} %get-tuple-element.42.refs_3_), custom_call_target="tpu_custom_call" | custom-call | flops 67108864 | bytes 1572864 | tf_op jit(solution)/shard_map/sums/pallas_call | solution.py:116
  3.9 0.3 collective-permute-done.got_ref.refs_12_
  4.2 3.0 %collective-permute-start.1 = (bf16[2,256,128]{2,1,0:T(8,128)(2,1)S(1)}, bf16[2,256,128]{2,1,0:T(8,128)(2,1)S(1)}, u32[]{:S(2)}, u32[]{:S(2)}) collective-permute-start(bf16[2,256,128]{2,1,0:T(8,128)(2,1)S(1)} %get-tuple-element.46), channel_id=1, source_target_pairs={{0,4},{1,3},{2,6},{3,1},{4,0},{5,7},{6,2},{7,5},{8,12},{9,11},{10,... | collective-permute-start | bytes 393224 | tf_op jit(solution)/shard_map/ppermute | solution.py:409
  7.2 1.5 %collective-permute-start.3 = (bf16[2,256,128]{2,1,0:T(8,128)(2,1)S(1)}, bf16[2,256,128]{2,1,0:T(8,128)(2,1)S(1)}, u32[]{:S(2)}, u32[]{:S(2)}) collective-permute-start(bf16[2,256,128]{2,1,0:T(8,128)(2,1)S(1)} %get-tuple-element.48), channel_id=1, source_target_pairs={{0,6},{1,7},{2,4},{3,5},{4,2},{5,3},{6,0},{7,1},{8,14},{9,15},{10,... | collective-permute-start | bytes 393224 | tf_op jit(solution)/shard_map/ppermute | solution.py:409
  8.7 0.4 %collective-permute-start.4 = (bf16[2,256,128]{2,1,0:T(8,128)(2,1)S(1)}, bf16[2,256,128]{2,1,0:T(8,128)(2,1)S(1)}, u32[]{:S(2)}, u32[]{:S(2)}) collective-permute-start(bf16[2,256,128]{2,1,0:T(8,128)(2,1)S(1)} %get-tuple-element.49), channel_id=1, source_target_pairs={{0,2},{1,5},{2,0},{3,7},{4,6},{5,1},{6,4},{7,3},{8,10},{9,13},{10,... | collective-permute-start | bytes 393224 | tf_op jit(solution)/shard_map/ppermute | solution.py:409
  9.1 2.2 %local.1 = (f32[128,2048]{1,0:T(8,128)S(1)}, f32[128,2048]{1,0:T(8,128)S(1)}, f32[128,2048]{1,0:T(8,128)S(1)}, f32[128,2048]{1,0:T(8,128)S(1)}) custom-call(bf16[128,2048]{1,0:T(8,128)(2,1)S(1)} %get-tuple-element.39.refs_0_, bf16[128,2048]{1,0:T(8,128)(2,1)S(1)} %get-tuple-element.40.refs_1_, bf16[128,2048]{1,0:T(8,128)(2,1)S(1)} %get-tuple-element.41.refs_2_, ...), custom_call_target="tpu_custom_call" | custom-call | flops 402653184 | bytes 6291456 | tf_op jit(solution)/shard_map/local/pallas_call | solution.py:279
  11.3 2.4 %collective-permute-done.3.refs_2_ = bf16[2,256,128]{2,1,0:T(8,128)(2,1)S(1)} collective-permute-done((bf16[2,256,128]{2,1,0:T(8,128)(2,1)S(1)}, bf16[2,256,128]{2,1,0:T(8,128)(2,1)S(1)}, u32[]{:S(2)}, u32[]{:S(2)}) %collective-permute-start.3) | collective-permute-done | bytes 131104 | tf_op jit(solution)/shard_map/ppermute | solution.py:409
  13.7 1.3 %collective-permute-done.4.refs_3_ = bf16[2,256,128]{2,1,0:T(8,128)(2,1)S(1)} collective-permute-done((bf16[2,256,128]{2,1,0:T(8,128)(2,1)S(1)}, bf16[2,256,128]{2,1,0:T(8,128)(2,1)S(1)}, u32[]{:S(2)}, u32[]{:S(2)}) %collective-permute-start.4) | collective-permute-done | bytes 131104 | tf_op jit(solution)/shard_map/ppermute | solution.py:409
  15.0 3.7 %collective-permute-start.5 = (bf16[256,128]{1,0:T(8,128)(2,1)S(1)}, bf16[256,128]{1,0:T(8,128)(2,1)S(1)}, u32[]{:S(2)}, u32[]{:S(2)}) collective-permute-start(bf16[256,128]{1,0:T(8,128)(2,1)S(1)} %get-tuple-element.62), channel_id=1, source_target_pairs={{0,24},{8,16},{16,8},{24,0},{1,25},{9,17},{17,9},{25,1},{2,26},{10... | collective-permute-start | bytes 196616 | tf_op jit(solution)/shard_map/ppermute | solution.py:401
  18.7 0.8 %collective-permute-start.7 = (bf16[256,128]{1,0:T(8,128)(2,1)S(1)}, bf16[256,128]{1,0:T(8,128)(2,1)S(1)}, u32[]{:S(2)}, u32[]{:S(2)}) collective-permute-start(bf16[256,128]{1,0:T(8,128)(2,1)S(1)} %get-tuple-element.64), channel_id=1, source_target_pairs={{0,8},{8,0},{16,24},{24,16},{1,9},{9,1},{17,25},{25,17},{2,10},{10... | collective-permute-start | bytes 196616 | tf_op jit(solution)/shard_map/ppermute | solution.py:401
  19.5 1.9 %collective-permute-done.5.refs_4_ = bf16[256,128]{1,0:T(8,128)(2,1)S(1)} collective-permute-done((bf16[256,128]{1,0:T(8,128)(2,1)S(1)}, bf16[256,128]{1,0:T(8,128)(2,1)S(1)}, u32[]{:S(2)}, u32[]{:S(2)}) %collective-permute-start.5) | collective-permute-done | bytes 65568 | tf_op jit(solution)/shard_map/ppermute | solution.py:401
  21.4 3.2 %collective-permute-done.6.refs_5_ = bf16[256,128]{1,0:T(8,128)(2,1)S(1)} collective-permute-done((bf16[256,128]{1,0:T(8,128)(2,1)S(1)}, bf16[256,128]{1,0:T(8,128)(2,1)S(1)}, u32[]{:S(2)}, u32[]{:S(2)}) %collective-permute-start.6) | collective-permute-done | bytes 65568 | tf_op jit(solution)/shard_map/ppermute | solution.py:401
  24.6 0.3 scan.1
  24.9 1.0 %collective-permute-start.8 = (bf16[2,256,128]{2,1,0:T(8,128)(2,1)S(1)}, bf16[2,256,128]{2,1,0:T(8,128)(2,1)S(1)}, u32[]{:S(2)}, u32[]{:S(2)}) collective-permute-start(bf16[2,256,128]{2,1,0:T(8,128)(2,1)S(1)} %get-tuple-element.66), channel_id=1, source_target_pairs={{0,4},{1,3},{2,6},{3,1},{4,0},{5,7},{6,2},{7,5},{8,12},{9,11},{10,... | collective-permute-start | bytes 393224 | tf_op jit(solution)/shard_map/ppermute | solution.py:409
  26.0 1.6 %collective-permute-start.9 = (bf16[2,256,128]{2,1,0:T(8,128)(2,1)S(1)}, bf16[2,256,128]{2,1,0:T(8,128)(2,1)S(1)}, u32[]{:S(2)}, u32[]{:S(2)}) collective-permute-start(bf16[2,256,128]{2,1,0:T(8,128)(2,1)S(1)} %get-tuple-element.67), channel_id=1, source_target_pairs={{0,6},{1,7},{2,4},{3,5},{4,2},{5,3},{6,0},{7,1},{8,14},{9,15},{10,... | collective-permute-start | bytes 393224 | tf_op jit(solution)/shard_map/ppermute | solution.py:409
  27.5 1.0 %collective-permute-start.10 = (bf16[2,256,128]{2,1,0:T(8,128)(2,1)S(1)}, bf16[2,256,128]{2,1,0:T(8,128)(2,1)S(1)}, u32[]{:S(2)}, u32[]{:S(2)}) collective-permute-start(bf16[2,256,128]{2,1,0:T(8,128)(2,1)S(1)} %get-tuple-element.68), channel_id=1, source_target_pairs={{0,2},{1,5},{2,0},{3,7},{4,6},{5,1},{6,4},{7,3},{8,10},{9,13},{10,... | collective-permute-start | bytes 393224 | tf_op jit(solution)/shard_map/ppermute | solution.py:409
  28.5 5.0 %collective-permute-done.8.refs_1_.refs_9_ = bf16[2,256,128]{2,1,0:T(8,128)(2,1)S(1)} collective-permute-done((bf16[2,256,128]{2,1,0:T(8,128)(2,1)S(1)}, bf16[2,256,128]{2,1,0:T(8,128)(2,1)S(1)}, u32[]{:S(2)}, u32[]{:S(2)}) %collective-permute-start.8) | collective-permute-done | bytes 131104 | tf_op jit(solution)/shard_map/ppermute | solution.py:409
  33.5 0.1 theirs.1
  33.6 0.6 %collective-permute-start.11 = (bf16[2,1024,128]{2,1,0:T(8,128)(2,1)S(1)}, bf16[2,1024,128]{2,1,0:T(8,128)(2,1)S(1)}, u32[]{:S(2)}, u32[]{:S(2)}) collective-permute-start(bf16[2,1024,128]{2,1,0:T(8,128)(2,1)S(1)} %theirs.1), channel_id=1, source_target_pairs={{0,1},{1,0},{2,3},{3,2},{4,5},{5,4},{6,7},{7,6},{8,9},{9,8},{10,11... | collective-permute-start | bytes 1572872 | tf_op jit(solution)/shard_map/ppermute | solution.py:401
  34.2 1.5 %finish_own.1 = (bf16[128,2048]{1,0:T(8,128)(2,1)}, bf16[128,2048]{1,0:T(8,128)(2,1)}, bf16[128,2048]{1,0:T(8,128)(2,1)}, bf16[128,2048]{1,0:T(8,128)(2,1)}, bf16[4,128,256]{2,1,0:T(8,128)(2,1)S(1)}) custom-call(bf16[128,2048]{1,0:T(8,128)(2,1)S(1)} %get-tuple-element.39.refs_0_, bf16[128,2048]{1,0:T(8,128)(2,1)S(1)} %get-tuple-element.40.refs_1_, ...), custom_call_target="tpu_custom_call" | custom-call | flops 134217728 | bytes 4456448 | tf_op jit(solution)/shard_map/finish_own/pallas_call | solution.py:343
  35.7 1.7 %finish_other.1 = (bf16[128,2048]{1,0:T(8,128)(2,1)}, bf16[128,2048]{1,0:T(8,128)(2,1)}, bf16[128,2048]{1,0:T(8,128)(2,1)}, bf16[128,2048]{1,0:T(8,128)(2,1)}) custom-call(bf16[128,2048]{1,0:T(8,128)(2,1)S(1)} %get-tuple-element.39.refs_0_, ...), custom_call_target="tpu_custom_call", output_to_operand_aliasing={{0}: (10, {}), {1}: (11, {}), {2}: (12, {}), {3}: (13, {})} | custom-call | flops 134217728 | bytes 4456448 | tf_op jit(solution)/shard_map/finish_other/pallas_call | solution.py:381
  (11 shorter events, 0.4 us)
Async XLA Ops:
  2.5 1.7 %collective-permute-start = (bf16[2,512,128]{2,1,0:T(8,128)(2,1)S(1)}, bf16[2,512,128]{2,1,0:T(8,128)(2,1)S(1)}, u32[]{:S(2)}, u32[]{:S(2)}) collective-permute-start(bf16[2,512,128]{2,1,0:T(8,128)(2,1)S(1)} %get-tuple-element.44), channel_id=1, source_target_pairs={{0,1},{1,0},{2,3},{3,2},{4,5},{5,4},{6,7},{7,6},{8,9},{9,8},{10,11... | collective-permute-start | bytes 786440 | tf_op jit(solution)/shard_map/ppermute | solution.py:401
  3.3 3.9 %collective-permute-start.2 = (bf16[2,512,128]{2,1,0:T(8,128)(2,1)S(1)}, bf16[2,512,128]{2,1,0:T(8,128)(2,1)S(1)}, u32[]{:S(2)}, u32[]{:S(2)}) collective-permute-start(bf16[2,512,128]{2,1,0:T(8,128)(2,1)S(1)} %sums.3), channel_id=1, source_target_pairs={{0,1},{1,0},{2,3},{3,2},{4,5},{5,4},{6,7},{7,6},{8,9},{9,8},{10,11... | collective-permute-start | bytes 786440 | tf_op jit(solution)/shard_map/ppermute | solution.py:401
  4.2 7.1 %collective-permute-start.1 = (bf16[2,256,128]{2,1,0:T(8,128)(2,1)S(1)}, bf16[2,256,128]{2,1,0:T(8,128)(2,1)S(1)}, u32[]{:S(2)}, u32[]{:S(2)}) collective-permute-start(bf16[2,256,128]{2,1,0:T(8,128)(2,1)S(1)} %get-tuple-element.46), channel_id=1, source_target_pairs={{0,4},{1,3},{2,6},{3,1},{4,0},{5,7},{6,2},{7,5},{8,12},{9,11},{10,... | collective-permute-start | bytes 393224 | tf_op jit(solution)/shard_map/ppermute | solution.py:409
  7.2 6.4 %collective-permute-start.3 = (bf16[2,256,128]{2,1,0:T(8,128)(2,1)S(1)}, bf16[2,256,128]{2,1,0:T(8,128)(2,1)S(1)}, u32[]{:S(2)}, u32[]{:S(2)}) collective-permute-start(bf16[2,256,128]{2,1,0:T(8,128)(2,1)S(1)} %get-tuple-element.48), channel_id=1, source_target_pairs={{0,6},{1,7},{2,4},{3,5},{4,2},{5,3},{6,0},{7,1},{8,14},{9,15},{10,... | collective-permute-start | bytes 393224 | tf_op jit(solution)/shard_map/ppermute | solution.py:409
  8.7 6.2 %collective-permute-start.4 = (bf16[2,256,128]{2,1,0:T(8,128)(2,1)S(1)}, bf16[2,256,128]{2,1,0:T(8,128)(2,1)S(1)}, u32[]{:S(2)}, u32[]{:S(2)}) collective-permute-start(bf16[2,256,128]{2,1,0:T(8,128)(2,1)S(1)} %get-tuple-element.49), channel_id=1, source_target_pairs={{0,2},{1,5},{2,0},{3,7},{4,6},{5,1},{6,4},{7,3},{8,10},{9,13},{10,... | collective-permute-start | bytes 393224 | tf_op jit(solution)/shard_map/ppermute | solution.py:409
  15.0 6.4 %collective-permute-start.5 = (bf16[256,128]{1,0:T(8,128)(2,1)S(1)}, bf16[256,128]{1,0:T(8,128)(2,1)S(1)}, u32[]{:S(2)}, u32[]{:S(2)}) collective-permute-start(bf16[256,128]{1,0:T(8,128)(2,1)S(1)} %get-tuple-element.62), channel_id=1, source_target_pairs={{0,24},{8,16},{16,8},{24,0},{1,25},{9,17},{17,9},{25,1},{2,26},{10... | collective-permute-start | bytes 196616 | tf_op jit(solution)/shard_map/ppermute | solution.py:401
  18.7 5.9 %collective-permute-start.6 = (bf16[256,128]{1,0:T(8,128)(2,1)S(1)}, bf16[256,128]{1,0:T(8,128)(2,1)S(1)}, u32[]{:S(2)}, u32[]{:S(2)}) collective-permute-start(bf16[256,128]{1,0:T(8,128)(2,1)S(1)} %get-tuple-element.63), channel_id=1, source_target_pairs={{0,16},{8,24},{16,0},{24,8},{1,17},{9,25},{17,1},{25,9},{2,18},{10... | collective-permute-start | bytes 196616 | tf_op jit(solution)/shard_map/ppermute | solution.py:401
  18.7 5.9 %collective-permute-start.7 = (bf16[256,128]{1,0:T(8,128)(2,1)S(1)}, bf16[256,128]{1,0:T(8,128)(2,1)S(1)}, u32[]{:S(2)}, u32[]{:S(2)}) collective-permute-start(bf16[256,128]{1,0:T(8,128)(2,1)S(1)} %get-tuple-element.64), channel_id=1, source_target_pairs={{0,8},{8,0},{16,24},{24,16},{1,9},{9,1},{17,25},{25,17},{2,10},{10... | collective-permute-start | bytes 196616 | tf_op jit(solution)/shard_map/ppermute | solution.py:401
  24.9 8.5 %collective-permute-start.8 = (bf16[2,256,128]{2,1,0:T(8,128)(2,1)S(1)}, bf16[2,256,128]{2,1,0:T(8,128)(2,1)S(1)}, u32[]{:S(2)}, u32[]{:S(2)}) collective-permute-start(bf16[2,256,128]{2,1,0:T(8,128)(2,1)S(1)} %get-tuple-element.66), channel_id=1, source_target_pairs={{0,4},{1,3},{2,6},{3,1},{4,0},{5,7},{6,2},{7,5},{8,12},{9,11},{10,... | collective-permute-start | bytes 393224 | tf_op jit(solution)/shard_map/ppermute | solution.py:409
  26.0 7.5 %collective-permute-start.9 = (bf16[2,256,128]{2,1,0:T(8,128)(2,1)S(1)}, bf16[2,256,128]{2,1,0:T(8,128)(2,1)S(1)}, u32[]{:S(2)}, u32[]{:S(2)}) collective-permute-start(bf16[2,256,128]{2,1,0:T(8,128)(2,1)S(1)} %get-tuple-element.67), channel_id=1, source_target_pairs={{0,6},{1,7},{2,4},{3,5},{4,2},{5,3},{6,0},{7,1},{8,14},{9,15},{10,... | collective-permute-start | bytes 393224 | tf_op jit(solution)/shard_map/ppermute | solution.py:409
  27.5 6.0 %collective-permute-start.10 = (bf16[2,256,128]{2,1,0:T(8,128)(2,1)S(1)}, bf16[2,256,128]{2,1,0:T(8,128)(2,1)S(1)}, u32[]{:S(2)}, u32[]{:S(2)}) collective-permute-start(bf16[2,256,128]{2,1,0:T(8,128)(2,1)S(1)} %get-tuple-element.68), channel_id=1, source_target_pairs={{0,2},{1,5},{2,0},{3,7},{4,6},{5,1},{6,4},{7,3},{8,10},{9,13},{10,... | collective-permute-start | bytes 393224 | tf_op jit(solution)/shard_map/ppermute | solution.py:409
  33.6 2.1 %collective-permute-start.11 = (bf16[2,1024,128]{2,1,0:T(8,128)(2,1)S(1)}, bf16[2,1024,128]{2,1,0:T(8,128)(2,1)S(1)}, u32[]{:S(2)}, u32[]{:S(2)}) collective-permute-start(bf16[2,1024,128]{2,1,0:T(8,128)(2,1)S(1)} %theirs.1), channel_id=1, source_target_pairs={{0,1},{1,0},{2,3},{3,2},{4,5},{5,4},{6,7},{7,6},{8,9},{9,8},{10,11... | collective-permute-start | bytes 1572872 | tf_op jit(solution)/shard_map/ppermute | solution.py:401

commit v12 on v10

v12 whole, which is shorter than its diff:
```python
import functools

import jax
import jax.numpy as jnp
from jax import lax
from jax.experimental import pallas as pl
from jax.experimental.pallas import tpu as pltpu
from jax.sharding import PartitionSpec as P

HEAD = 128
PIECE = 256
MIB = 1024 * 1024
ANY = pl.BlockSpec(memory_space=pl.ANY)
VMEM = pl.BlockSpec(memory_space=pltpu.VMEM)
BF16 = jnp.bfloat16
F32 = jnp.float32
SMALL = pltpu.CompilerParams(vmem_limit_bytes=4 * MIB)


def dot(a, b, over_a, over_b):
    return lax.dot_general(
        a, b, (((over_a,), (over_b,)), ((), ())), preferred_element_type=F32
    )


def near_far():
    inner = lax.axis_index("inner")
    return lax.rem(inner, 2), lax.div(inner, 2)


def block_start(block, width):
    _, far = near_far()
    top = lax.div(far, lax.axis_size("inner") // 4)
    return (1 - top if block else top) * (width // 2)


def rows_at(start, n, size):
    return pl.ds(pl.multiple_of(start + n * size, size), size)


def slot_rows(s, count, depth):
    _, far = near_far()
    return rows_at(lax.rem(far ^ s, count) * depth, 0, depth)


def by_core(odd, even):
    near, _ = near_far()
    pl.when(near == 1)(odd)
    pl.when(near == 0)(even)


def block_sums(own, block, tokens, out):
    q, k, v, d = tokens
    start = block_start(block, q.shape[1])

    def add(a, b):
        for n in range(out.shape[0] // HEAD):
            cols = rows_at(start, n, HEAD)
            out[n * HEAD : (n + 1) * HEAD] = dot(a[:, cols], b[:, cols], 0, 0).astype(BF16)

    kinds = [lambda: add(k, v), lambda: add(q, d)]
    by_core(*(kinds if own else kinds[::-1]))


def load_kernel(*refs):
    tokens, held, (out, sems) = refs[:4], refs[4:8], refs[8:]
    copies = [
        pltpu.make_async_copy(ref, to, sems.at[i]) for i, (ref, to) in enumerate(zip(tokens, held))
    ]
    for copy in copies:
        copy.start()
    for copy in copies:
        copy.wait()
    block_sums(False, 0, held, out)


def load(tokens):
    rows, width = tokens[0].shape
    *held, sums = pl.pallas_call(
        load_kernel,
        name="load",
        in_specs=[ANY] * 4,
        out_specs=[VMEM] * 5,
        out_shape=[pltpu.VMEM((rows, width), BF16)] * 4 + [pltpu.VMEM((width // 2, HEAD), BF16)],
        scratch_shapes=[pltpu.SemaphoreType.DMA((4,))],
        cost_estimate=pl.CostEstimate(
            flops=rows * width * HEAD, bytes_accessed=10 * rows * width, transcendentals=0
        ),
        compiler_params=SMALL,
    )(*(pltpu.with_memory_space_constraint(x, pltpu.HBM) for x in tokens))
    return tuple(held), sums


def sums_kernel(wanted, *refs):
    for (own, block), out in zip(wanted, refs[4:]):
        block_sums(own, block, refs[:4], out)


def sums(tokens, *wanted):
    rows, width = tokens[0].shape
    return pl.pallas_call(
        functools.partial(sums_kernel, wanted),
        name="sums",
        in_specs=[VMEM] * 4,
        out_specs=[VMEM] * len(wanted),
        out_shape=[jax.ShapeDtypeStruct((width // 2, HEAD), BF16)] * len(wanted),
        cost_estimate=pl.CostEstimate(
            flops=rows * width * HEAD * len(wanted),
            bytes_accessed=3 * rows * width * len(wanted),
            transcendentals=0,
        ),
        compiler_params=SMALL,
    )(*tokens)


def pair_kernel(keep_ref, got_ref, *slots):
    for s, slot in enumerate(slots):
        part = slot_rows(s, len(slots), slot.shape[0])
        slot[...] = (keep_ref[part].astype(F32) + got_ref[part].astype(F32)).astype(BF16)


def pair_slots(keep, got, count):
    slot = jax.ShapeDtypeStruct((keep.shape[0] // count, HEAD), BF16)
    return pl.pallas_call(
        pair_kernel,
        name="pair",
        in_specs=[VMEM] * 2,
        out_specs=[VMEM] * count,
        out_shape=[slot] * count,
        compiler_params=SMALL,
    )(keep, got)


def total_kernel(*refs):
    total = refs[0][...].astype(F32)
    for slot in refs[1:-1]:
        total += slot[...].astype(F32)
    refs[-1][...] = total.astype(BF16)


def total_of(slots):
    return pl.pallas_call(
        total_kernel,
        name="total",
        in_specs=[VMEM] * len(slots),
        out_specs=VMEM,
        out_shape=jax.ShapeDtypeStruct(slots[0].shape, BF16),
        compiler_params=SMALL,
    )(*slots)


def scan_kernel(count, *refs):
    slots, others, outs = refs[:count], refs[count:-count], refs[-count:]
    near, far = near_far()
    base = others[0][...].astype(F32)
    for other in others[1:]:
        base += other[...].astype(F32)
    terms = [slot[...].astype(F32) for slot in slots]
    for s, out in enumerate(outs):
        total = base
        for t, term in enumerate(terms):
            if s != t:
                below = (far ^ t) < (far ^ s)
                wanted = jnp.where(near == 1, below, jnp.logical_not(below))
                total += jnp.where(wanted, term, 0.0)
        out[...] = total.astype(BF16)


def scan_slots(slots, others):
    count, slot = len(slots), jax.ShapeDtypeStruct(slots[0].shape, BF16)
    return pl.pallas_call(
        functools.partial(scan_kernel, count),
        name="scan",
        in_specs=[VMEM] * (count + len(others)),
        out_specs=[VMEM] * count,
        out_shape=[slot] * count,
        compiler_params=SMALL,
    )(*slots, *others)


def local_kernel(*refs):
    tokens, outs = refs[:4], refs[4:]
    rows, width = tokens[0].shape
    at = lax.broadcasted_iota(jnp.int32, (rows, rows), 0)
    to = lax.broadcasted_iota(jnp.int32, (rows, rows), 1)
    lower = at >= to

    def masked(a, b):
        return jnp.where(lower, dot(a, b, 1, 1), 0.0).astype(BF16)

    def second(cols, a, b):
        q, k, v, d = (ref[:, cols] for ref in tokens)
        att, gq, gv, gk = outs
        att[:, cols] = dot(a, v, 1, 0)
        gq[:, cols] = dot(b, k, 1, 0)
        gv[:, cols] = dot(a, d, 0, 0)
        gk[:, cols] = dot(b, q, 0, 0)

    last = None
    for h in range(width // HEAD):
        cols = slice(h * HEAD, (h + 1) * HEAD)
        q, k, v, d = (ref[:, cols] for ref in tokens)
        a, b = masked(q, k), masked(d, v)
        if last:
            second(*last)
        last = (cols, a, b)
    second(*last)


def local_part(tokens):
    rows, width = tokens[0].shape
    return pl.pallas_call(
        local_kernel,
        name="local",
        in_specs=[VMEM] * 4,
        out_specs=[VMEM] * 4,
        out_shape=[jax.ShapeDtypeStruct((rows, width), F32)] * 4,
        cost_estimate=pl.CostEstimate(
            flops=12 * rows * width * HEAD, bytes_accessed=24 * rows * width, transcendentals=0
        ),
        compiler_params=SMALL,
    )(*tokens)


def results(scale, tokens, local, outs, held, sems, states):
    a_ref, b_ref = tokens
    depth = held.shape[2] // len(states)
    piece = min(depth, PIECE)
    _, far = near_far()
    for s, state in enumerate(states):
        for p in range(depth // piece):
            at = s * depth + p * piece
            there = rows_at((far ^ s) * depth, p, piece)
            for n in range(piece // HEAD):
                cols = rows_at((far ^ s) * depth + p * piece, n, HEAD)
                x = state(slice(p * piece + n * HEAD, p * piece + (n + 1) * HEAD))
                parts = dot(a_ref[:, cols], x, 1, 0), dot(b_ref[:, cols], x, 1, 1)
                for i, part in enumerate(parts):
                    out = (scale * (part + local[i][:, cols])).astype(BF16)
                    held[i, :, at + n * HEAD : at + (n + 1) * HEAD] = out
            yield [
                pltpu.make_async_copy(
                    held.at[i, :, pl.ds(at, piece)],
                    out.at[:, there],
                    sems.at[i, s * (depth // piece) + p],
                )
                for i, out in enumerate(outs)
            ]


def kinds(tokens, local, outs):
    q, k, v, d = tokens
    return ((q, d), local[:2], outs[:2]), ((k, v), local[2:], outs[2:])


def finish_kernel(scale, count, own, *refs):
    tokens, local, slots, refs = refs[:4], refs[4:8], refs[8 : 8 + count], refs[8 + count :]
    got = refs[:2] if own else ()
    outs, held, sems = refs[-6:-2], refs[-2], refs[-1]
    depth = slots[0].shape[0]

    def state(s):
        if not own:
            return lambda part: slots[s][part]

        def read(part):
            _, far = near_far()
            more = got[2 * s // count]
            there = rows_at(lax.rem(far ^ s, count // 2) * depth + part.start, 0, HEAD)
            return (slots[s][part].astype(F32) + more[there].astype(F32)).astype(BF16)

        return read

    def run(kind):
        started = []
        for copies in results(scale, *kind, held, sems, [state(s) for s in range(count)]):
            for copy in copies:
                copy.start()
            started += copies
        for copy in started:
            copy.wait()

    of_s, of_g = kinds(tokens, local, outs)
    both = [lambda: run(of_s), lambda: run(of_g)]
    by_core(*(both if own else both[::-1]))


def finish(tokens, local, slots, scale, got=(), before=()):
    rows, width = tokens[0].shape
    count, depth = len(slots), slots[0].shape[0]
    out = jax.ShapeDtypeStruct((rows, width), BF16)
    inputs = [*tokens, *local, *slots, *got]
    return pl.pallas_call(
        functools.partial(finish_kernel, scale, count, bool(got)),
        name="finish_own" if got else "finish_other",
        in_specs=[VMEM] * len(inputs) + [ANY] * len(before),
        out_specs=[ANY] * 4,
        out_shape=[out] * 4,
        scratch_shapes=[
            pltpu.VMEM((2, rows, width), BF16),
            pltpu.SemaphoreType.DMA((2, width // min(depth, PIECE))),
        ],
        input_output_aliases={len(inputs) + i: i for i in range(len(before))},
        cost_estimate=pl.CostEstimate(
            flops=4 * rows * width * HEAD, bytes_accessed=17 * rows * width, transcendentals=0
        ),
        compiler_params=SMALL,
    )(*inputs, *before)


def swap(x, bits):
    return lax.ppermute(x, "inner", [(i, i ^ bits) for i in range(lax.axis_size("inner"))])


def swap_far(slots):
    return [slots[0]] + [swap(slots[s], 2 * s) for s in range(1, len(slots))]


def from_groups(total):
    groups, count = lax.axis_size("outer"), lax.axis_size("inner")
    return [
        lax.ppermute(
            total,
            ("outer", "inner"),
            [
                (z * count + i, (z ^ s) * count + i)
                for z in range(groups)
                for i in range(count)
                if (z < z ^ s) == (i % 2 == 1)
            ],
        )
        for s in range(1, groups)
    ]


def body(queries, keys, values, cotangent):
    far_count = lax.axis_size("inner") // 2
    scale = float(HEAD * queries.shape[0] * 2 * far_count * lax.axis_size("outer")) ** (-0.5)
    tokens, give = load((queries, keys, values, cotangent))
    got = [swap(give, 1), swap(*sums(tokens, (False, 1)), 1)]
    keep = sums(tokens, (True, 0), (True, 1))
    slots = [slot for b in range(2) for slot in pair_slots(keep[b], got[b], far_count // 2)]
    slots, local = lax.optimization_barrier((swap_far(slots), local_part(tokens)))
    slots = swap_far(scan_slots(slots, from_groups(total_of(slots))))
    arrived = [swap(slot, 1) for slot in slots]
    outs = finish(tokens, local, slots, scale, got=got)
    att, gq, gv, gk = finish(tokens, local, arrived, scale, before=outs)
    return att, gq, gk, gv


def solution(mesh):
    spec = P(("outer", "inner"), None)
    return jax.shard_map(
        body, mesh=mesh, in_specs=(spec,) * 4, out_specs=(spec,) * 4, check_vma=False
    )
```

time: 36.8 us -> 39.6 us (1.076)
  waiting for transfers between devices: 13.8 us -> 17.2 us
  starting transfers between devices: 13.5 us -> 12.9 us
    ppermute x12 -> x15, waiting for transfers between devices: 13.8 us -> 17.2 us  [the longest x12 9.01 us: swap(): lax.ppermute(x, 'inner', [(i, i ^ bits) for i in range(lax.axis_size('inn...]
    ppermute x12 -> x15, starting transfers between devices: 13.5 us -> 12.9 us  [the longest x12 9.04 us: swap(): lax.ppermute(x, 'inner', [(i, i ^ bits) for i in range(lax.axis_size('inn...]
    pallas_call x5 -> x4, Pallas kernels: 3.74 us -> 3.48 us  [the longest x2 3.11 us: finish(): pl.pallas_call(functools.partial(finish_kernel, scale, count, bool(got)),...]
  transfers between devices with their start and end apart: 12 -> 15, of which waited for: 8 -> 7; matrix products, arithmetic and copies ran while one was open for 0% -> 0% of each run, Pallas kernels for 12% -> 12%
where the time goes in v12:
time: 39.6 us; the launch traced here: 39.3 us
  waiting for transfers between devices  17.2 us (43%)
  starting transfers between devices  12.9 us (33%)
  Pallas kernels  8.48 us (21%)
  between operations  0.74 us (2%)
    ppermute x12, starting transfers between devices, swap(): lax.ppermute(x, 'inner', [(i, i ^ bits) for i in range(lax.axis_size('inn...  9.04 us
    ppermute x12, waiting for transfers between devices, swap(): lax.ppermute(x, 'inner', [(i, i ^ bits) for i in range(lax.axis_size('inn...  9.01 us
    ppermute x3, waiting for transfers between devices, from_groups(): lax.ppermute(total, ('outer', 'inner'), [(z * count + i, (z ^ s) * count...  8.19 us
    ppermute x3, starting transfers between devices, from_groups(): lax.ppermute(total, ('outer', 'inner'), [(z * count + i, (z ^ s) * count...  3.88 us
    pallas_call x2, Pallas kernels, finish(): pl.pallas_call(functools.partial(finish_kernel, scale, count, bool(got)),...  3.11 us
    pallas_call x1, Pallas kernels, local_part(): pl.pallas_call(local_kernel, name='local', in_specs=[VMEM] * 4, out_specs...  2.16 us
    pallas_call x1, Pallas kernels, load(): pl.pallas_call(load_kernel, name='load', in_specs=[ANY] * 4, out_specs=[V...  1.84 us
    pallas_call x2, Pallas kernels, sums(): pl.pallas_call(functools.partial(sums_kernel, wanted), name='sums', in_sp...  0.87 us
  transfers between devices with their start and end apart: 15, of which 7 were waited for; matrix products, arithmetic and copies ran while one was open for 0% of the time, Pallas kernels for 12%

profile of v12, /device:TPU:0, one launch (start us, length us, event | category | flops | bytes accessed | tf_op | source)
XLA Modules:
  0.0 39.3 jit_solution(6098186957408685945)
XLA Ops:
  0.6 1.8 %load.1 = (bf16[128,2048]{1,0:T(8,128)(2,1)S(1)}, bf16[128,2048]{1,0:T(8,128)(2,1)S(1)}, bf16[128,2048]{1,0:T(8,128)(2,1)S(1)}, bf16[128,2048]{1,0:T(8,128)(2,1)S(1)}, bf16[1024,128]{1,0:T(8,128)(2,1)S(1)}) custom-call(bf16[128,2048]{1,0:T(8,128)(2,1)} %refs_0_.1, bf16[128,2048]{1,0:T(8,128)(2,1)} %refs_1_.1, bf16[128,2048]{1,0:T(8,128)(2,1)} %refs_2_.1, ...), custom_call_target="tpu_custom_call" | custom-call | flops 33554432 | bytes 2621440 | tf_op jit(solution)/shard_map/load/pallas_call | solution.py:79
  2.5 0.5 %collective-permute-start = (bf16[1024,128]{1,0:T(8,128)(2,1)S(1)}, bf16[1024,128]{1,0:T(8,128)(2,1)S(1)}, u32[]{:S(2)}, u32[]{:S(2)}) collective-permute-start(bf16[1024,128]{1,0:T(8,128)(2,1)S(1)} %get-tuple-element.44), channel_id=1, source_target_pairs={{0,1},{1,0},{2,3},{3,2},{4,5},{5,4},{6,7},{7,6},{8,9},{9,8},{10,11... | collective-permute-start | bytes 786440 | tf_op jit(solution)/shard_map/ppermute | solution.py:312
  3.0 0.3 sums.3
  3.4 0.6 %sums.2 = (bf16[1024,128]{1,0:T(8,128)(2,1)S(1)}, bf16[1024,128]{1,0:T(8,128)(2,1)S(1)}) custom-call(bf16[128,2048]{1,0:T(8,128)(2,1)S(1)} %get-tuple-element.39.refs_0_, bf16[128,2048]{1,0:T(8,128)(2,1)S(1)} %get-tuple-element.40.refs_1_, bf16[128,2048]{1,0:T(8,128)(2,1)S(1)} %get-tuple-element.41.refs_2_, bf16[128,2048]{1,0:T(8,128)(2,1)S(1)} %get-tuple-element.42.refs_3_), custom_call_target="tpu_custom_call" | custom-call | flops 67108864 | bytes 1572864 | tf_op jit(solution)/shard_map/sums/pallas_call | solution.py:101
  4.0 0.2 collective-permute-done.got_ref.refs_12_
  4.2 2.9 %collective-permute-start.1 = (bf16[512,128]{1,0:T(8,128)(2,1)S(1)}, bf16[512,128]{1,0:T(8,128)(2,1)S(1)}, u32[]{:S(2)}, u32[]{:S(2)}) collective-permute-start(bf16[512,128]{1,0:T(8,128)(2,1)S(1)} %get-tuple-element.46), channel_id=1, source_target_pairs={{0,2},{1,3},{2,0},{3,1},{4,6},{5,7},{6,4},{7,5},{8,10},{9,11},{10,... | collective-permute-start | bytes 393224 | tf_op jit(solution)/shard_map/ppermute | solution.py:312
  7.2 1.6 %collective-permute-start.3 = (bf16[512,128]{1,0:T(8,128)(2,1)S(1)}, bf16[512,128]{1,0:T(8,128)(2,1)S(1)}, u32[]{:S(2)}, u32[]{:S(2)}) collective-permute-start(bf16[512,128]{1,0:T(8,128)(2,1)S(1)} %get-tuple-element.48), channel_id=1, source_target_pairs={{0,4},{1,5},{2,6},{3,7},{4,0},{5,1},{6,2},{7,3},{8,12},{9,13},{10,... | collective-permute-start | bytes 393224 | tf_op jit(solution)/shard_map/ppermute | solution.py:312
  8.8 0.3 collective-permute-start.4
  9.1 2.2 %local.1 = (f32[128,2048]{1,0:T(8,128)S(1)}, f32[128,2048]{1,0:T(8,128)S(1)}, f32[128,2048]{1,0:T(8,128)S(1)}, f32[128,2048]{1,0:T(8,128)S(1)}) custom-call(bf16[128,2048]{1,0:T(8,128)(2,1)S(1)} %get-tuple-element.39.refs_0_, bf16[128,2048]{1,0:T(8,128)(2,1)S(1)} %get-tuple-element.40.refs_1_, bf16[128,2048]{1,0:T(8,128)(2,1)S(1)} %get-tuple-element.41.refs_2_, ...), custom_call_target="tpu_custom_call" | custom-call | flops 402653184 | bytes 6291456 | tf_op jit(solution)/shard_map/local/pallas_call | solution.py:212
  11.3 4.1 %collective-permute-done.3.refs_2_ = bf16[512,128]{1,0:T(8,128)(2,1)S(1)} collective-permute-done((bf16[512,128]{1,0:T(8,128)(2,1)S(1)}, bf16[512,128]{1,0:T(8,128)(2,1)S(1)}, u32[]{:S(2)}, u32[]{:S(2)}) %collective-permute-start.3) | collective-permute-done | bytes 131104 | tf_op jit(solution)/shard_map/ppermute | solution.py:312
  15.4 1.3 %collective-permute-start.7 = (bf16[512,128]{1,0:T(8,128)(2,1)S(1)}, bf16[512,128]{1,0:T(8,128)(2,1)S(1)}, u32[]{:S(2)}, u32[]{:S(2)}) collective-permute-start(bf16[512,128]{1,0:T(8,128)(2,1)S(1)} %total.1), channel_id=1, source_target_pairs={{1,25},{3,27},{5,29},{7,31},{9,17},{11,19},{13,21},{15,23},{16,8},... | collective-permute-start | bytes 393224 | tf_op jit(solution)/shard_map/ppermute | solution.py:322
  16.7 1.3 %collective-permute-start.6 = (bf16[512,128]{1,0:T(8,128)(2,1)S(1)}, bf16[512,128]{1,0:T(8,128)(2,1)S(1)}, u32[]{:S(2)}, u32[]{:S(2)}) collective-permute-start(bf16[512,128]{1,0:T(8,128)(2,1)S(1)} %total.1), channel_id=1, source_target_pairs={{1,17},{3,19},{5,21},{7,23},{9,25},{11,27},{13,29},{15,31},{16,0},... | collective-permute-start | bytes 393224 | tf_op jit(solution)/shard_map/ppermute | solution.py:322
  18.0 1.3 %collective-permute-start.5 = (bf16[512,128]{1,0:T(8,128)(2,1)S(1)}, bf16[512,128]{1,0:T(8,128)(2,1)S(1)}, u32[]{:S(2)}, u32[]{:S(2)}) collective-permute-start(bf16[512,128]{1,0:T(8,128)(2,1)S(1)} %total.1), channel_id=1, source_target_pairs={{1,9},{3,11},{5,13},{7,15},{8,0},{10,2},{12,4},{14,6},{17,25},{19,... | collective-permute-start | bytes 393224 | tf_op jit(solution)/shard_map/ppermute | solution.py:322
  19.3 4.9 %collective-permute-done.7.refs_6_ = bf16[512,128]{1,0:T(8,128)(2,1)S(1)} collective-permute-done((bf16[512,128]{1,0:T(8,128)(2,1)S(1)}, bf16[512,128]{1,0:T(8,128)(2,1)S(1)}, u32[]{:S(2)}, u32[]{:S(2)}) %collective-permute-start.7) | collective-permute-done | bytes 131104 | tf_op jit(solution)/shard_map/ppermute | solution.py:322
  24.3 3.2 %collective-permute-done.6.refs_5_ = bf16[512,128]{1,0:T(8,128)(2,1)S(1)} collective-permute-done((bf16[512,128]{1,0:T(8,128)(2,1)S(1)}, bf16[512,128]{1,0:T(8,128)(2,1)S(1)}, u32[]{:S(2)}, u32[]{:S(2)}) %collective-permute-start.6) | collective-permute-done | bytes 131104 | tf_op jit(solution)/shard_map/ppermute | solution.py:322
  27.5 0.3 scan.1
  27.8 1.2 %collective-permute-start.9 = (bf16[512,128]{1,0:T(8,128)(2,1)S(1)}, bf16[512,128]{1,0:T(8,128)(2,1)S(1)}, u32[]{:S(2)}, u32[]{:S(2)}) collective-permute-start(bf16[512,128]{1,0:T(8,128)(2,1)S(1)} %get-tuple-element.63), channel_id=1, source_target_pairs={{0,2},{1,3},{2,0},{3,1},{4,6},{5,7},{6,4},{7,5},{8,10},{9,11},{10,... | collective-permute-start | bytes 393224 | tf_op jit(solution)/shard_map/ppermute | solution.py:312
  29.0 1.3 %collective-permute-start.11 = (bf16[512,128]{1,0:T(8,128)(2,1)S(1)}, bf16[512,128]{1,0:T(8,128)(2,1)S(1)}, u32[]{:S(2)}, u32[]{:S(2)}) collective-permute-start(bf16[512,128]{1,0:T(8,128)(2,1)S(1)} %get-tuple-element.64), channel_id=1, source_target_pairs={{0,4},{1,5},{2,6},{3,7},{4,0},{5,1},{6,2},{7,3},{8,12},{9,13},{10,... | collective-permute-start | bytes 393224 | tf_op jit(solution)/shard_map/ppermute | solution.py:312
  30.3 1.1 %collective-permute-start.13 = (bf16[512,128]{1,0:T(8,128)(2,1)S(1)}, bf16[512,128]{1,0:T(8,128)(2,1)S(1)}, u32[]{:S(2)}, u32[]{:S(2)}) collective-permute-start(bf16[512,128]{1,0:T(8,128)(2,1)S(1)} %get-tuple-element.65), channel_id=1, source_target_pairs={{0,6},{1,7},{2,4},{3,5},{4,2},{5,3},{6,0},{7,1},{8,14},{9,15},{10,... | collective-permute-start | bytes 393224 | tf_op jit(solution)/shard_map/ppermute | solution.py:312
  31.4 1.8 %collective-permute-done.9.refs_9_ = bf16[512,128]{1,0:T(8,128)(2,1)S(1)} collective-permute-done((bf16[512,128]{1,0:T(8,128)(2,1)S(1)}, bf16[512,128]{1,0:T(8,128)(2,1)S(1)}, u32[]{:S(2)}, u32[]{:S(2)}) %collective-permute-start.9) | collective-permute-done | bytes 131104 | tf_op jit(solution)/shard_map/ppermute | solution.py:312
  33.2 0.8 %collective-permute-done.11.refs_10_ = bf16[512,128]{1,0:T(8,128)(2,1)S(1)} collective-permute-done((bf16[512,128]{1,0:T(8,128)(2,1)S(1)}, bf16[512,128]{1,0:T(8,128)(2,1)S(1)}, u32[]{:S(2)}, u32[]{:S(2)}) %collective-permute-start.11) | collective-permute-done | bytes 131104 | tf_op jit(solution)/shard_map/ppermute | solution.py:312
  34.0 2.2 %collective-permute-done.13.refs_11_ = bf16[512,128]{1,0:T(8,128)(2,1)S(1)} collective-permute-done((bf16[512,128]{1,0:T(8,128)(2,1)S(1)}, bf16[512,128]{1,0:T(8,128)(2,1)S(1)}, u32[]{:S(2)}, u32[]{:S(2)}) %collective-permute-start.13) | collective-permute-done | bytes 131104 | tf_op jit(solution)/shard_map/ppermute | solution.py:312
  36.2 1.6 %finish_own.1 = (bf16[128,2048]{1,0:T(8,128)(2,1)}, bf16[128,2048]{1,0:T(8,128)(2,1)}, bf16[128,2048]{1,0:T(8,128)(2,1)}, bf16[128,2048]{1,0:T(8,128)(2,1)}) custom-call(bf16[128,2048]{1,0:T(8,128)(2,1)S(1)} %get-tuple-element.39.refs_0_, bf16[128,2048]{1,0:T(8,128)(2,1)S(1)} %get-tuple-element.40.refs_1_, bf16[128,2048]{1,0:T(8,128)(2,1)S(1)} %get-tuple-element.41.refs_2_, ...), custom_call_target="tpu_custom_call" | custom-call | flops 134217728 | bytes 4456448 | tf_op jit(solution)/shard_map/finish_own/pallas_call | solution.py:293
  37.8 1.6 %finish_other.1 = (bf16[128,2048]{1,0:T(8,128)(2,1)}, bf16[128,2048]{1,0:T(8,128)(2,1)}, bf16[128,2048]{1,0:T(8,128)(2,1)}, bf16[128,2048]{1,0:T(8,128)(2,1)}) custom-call(bf16[128,2048]{1,0:T(8,128)(2,1)S(1)} %get-tuple-element.39.refs_0_, ...), custom_call_target="tpu_custom_call", output_to_operand_aliasing={{0}: (12, {}), {1}: (13, {}), {2}: (14, {}), {3}: (15, {})} | custom-call | flops 134217728 | bytes 4456448 | tf_op jit(solution)/shard_map/finish_other/pallas_call | solution.py:293
  (16 shorter events, 0.4 us)
Async XLA Ops:
  2.5 1.7 %collective-permute-start = (bf16[1024,128]{1,0:T(8,128)(2,1)S(1)}, bf16[1024,128]{1,0:T(8,128)(2,1)S(1)}, u32[]{:S(2)}, u32[]{:S(2)}) collective-permute-start(bf16[1024,128]{1,0:T(8,128)(2,1)S(1)} %get-tuple-element.44), channel_id=1, source_target_pairs={{0,1},{1,0},{2,3},{3,2},{4,5},{5,4},{6,7},{7,6},{8,9},{9,8},{10,11... | collective-permute-start | bytes 786440 | tf_op jit(solution)/shard_map/ppermute | solution.py:312
  3.3 3.9 %collective-permute-start.2 = (bf16[1024,128]{1,0:T(8,128)(2,1)S(1)}, bf16[1024,128]{1,0:T(8,128)(2,1)S(1)}, u32[]{:S(2)}, u32[]{:S(2)}) collective-permute-start(bf16[1024,128]{1,0:T(8,128)(2,1)S(1)} %sums.3), channel_id=1, source_target_pairs={{0,1},{1,0},{2,3},{3,2},{4,5},{5,4},{6,7},{7,6},{8,9},{9,8},{10,11... | collective-permute-start | bytes 786440 | tf_op jit(solution)/shard_map/ppermute | solution.py:312
  4.2 7.1 %collective-permute-start.1 = (bf16[512,128]{1,0:T(8,128)(2,1)S(1)}, bf16[512,128]{1,0:T(8,128)(2,1)S(1)}, u32[]{:S(2)}, u32[]{:S(2)}) collective-permute-start(bf16[512,128]{1,0:T(8,128)(2,1)S(1)} %get-tuple-element.46), channel_id=1, source_target_pairs={{0,2},{1,3},{2,0},{3,1},{4,6},{5,7},{6,4},{7,5},{8,10},{9,11},{10,... | collective-permute-start | bytes 393224 | tf_op jit(solution)/shard_map/ppermute | solution.py:312
  7.2 8.1 %collective-permute-start.3 = (bf16[512,128]{1,0:T(8,128)(2,1)S(1)}, bf16[512,128]{1,0:T(8,128)(2,1)S(1)}, u32[]{:S(2)}, u32[]{:S(2)}) collective-permute-start(bf16[512,128]{1,0:T(8,128)(2,1)S(1)} %get-tuple-element.48), channel_id=1, source_target_pairs={{0,4},{1,5},{2,6},{3,7},{4,0},{5,1},{6,2},{7,3},{8,12},{9,13},{10,... | collective-permute-start | bytes 393224 | tf_op jit(solution)/shard_map/ppermute | solution.py:312
  8.8 6.6 %collective-permute-start.4 = (bf16[512,128]{1,0:T(8,128)(2,1)S(1)}, bf16[512,128]{1,0:T(8,128)(2,1)S(1)}, u32[]{:S(2)}, u32[]{:S(2)}) collective-permute-start(bf16[512,128]{1,0:T(8,128)(2,1)S(1)} %get-tuple-element.49), channel_id=1, source_target_pairs={{0,6},{1,7},{2,4},{3,5},{4,2},{5,3},{6,0},{7,1},{8,14},{9,15},{10,... | collective-permute-start | bytes 393224 | tf_op jit(solution)/shard_map/ppermute | solution.py:312
  15.4 8.8 %collective-permute-start.7 = (bf16[512,128]{1,0:T(8,128)(2,1)S(1)}, bf16[512,128]{1,0:T(8,128)(2,1)S(1)}, u32[]{:S(2)}, u32[]{:S(2)}) collective-permute-start(bf16[512,128]{1,0:T(8,128)(2,1)S(1)} %total.1), channel_id=1, source_target_pairs={{1,25},{3,27},{5,29},{7,31},{9,17},{11,19},{13,21},{15,23},{16,8},... | collective-permute-start | bytes 393224 | tf_op jit(solution)/shard_map/ppermute | solution.py:322
  16.7 10.8 %collective-permute-start.6 = (bf16[512,128]{1,0:T(8,128)(2,1)S(1)}, bf16[512,128]{1,0:T(8,128)(2,1)S(1)}, u32[]{:S(2)}, u32[]{:S(2)}) collective-permute-start(bf16[512,128]{1,0:T(8,128)(2,1)S(1)} %total.1), channel_id=1, source_target_pairs={{1,17},{3,19},{5,21},{7,23},{9,25},{11,27},{13,29},{15,31},{16,0},... | collective-permute-start | bytes 393224 | tf_op jit(solution)/shard_map/ppermute | solution.py:322
  18.0 9.5 %collective-permute-start.5 = (bf16[512,128]{1,0:T(8,128)(2,1)S(1)}, bf16[512,128]{1,0:T(8,128)(2,1)S(1)}, u32[]{:S(2)}, u32[]{:S(2)}) collective-permute-start(bf16[512,128]{1,0:T(8,128)(2,1)S(1)} %total.1), channel_id=1, source_target_pairs={{1,9},{3,11},{5,13},{7,15},{8,0},{10,2},{12,4},{14,6},{17,25},{19,... | collective-permute-start | bytes 393224 | tf_op jit(solution)/shard_map/ppermute | solution.py:322
  27.8 5.4 %collective-permute-start.9 = (bf16[512,128]{1,0:T(8,128)(2,1)S(1)}, bf16[512,128]{1,0:T(8,128)(2,1)S(1)}, u32[]{:S(2)}, u32[]{:S(2)}) collective-permute-start(bf16[512,128]{1,0:T(8,128)(2,1)S(1)} %get-tuple-element.63), channel_id=1, source_target_pairs={{0,2},{1,3},{2,0},{3,1},{4,6},{5,7},{6,4},{7,5},{8,10},{9,11},{10,... | collective-permute-start | bytes 393224 | tf_op jit(solution)/shard_map/ppermute | solution.py:312
  29.0 5.0 %collective-permute-start.11 = (bf16[512,128]{1,0:T(8,128)(2,1)S(1)}, bf16[512,128]{1,0:T(8,128)(2,1)S(1)}, u32[]{:S(2)}, u32[]{:S(2)}) collective-permute-start(bf16[512,128]{1,0:T(8,128)(2,1)S(1)} %get-tuple-element.64), channel_id=1, source_target_pairs={{0,4},{1,5},{2,6},{3,7},{4,0},{5,1},{6,2},{7,3},{8,12},{9,13},{10,... | collective-permute-start | bytes 393224 | tf_op jit(solution)/shard_map/ppermute | solution.py:312
  30.3 5.9 %collective-permute-start.13 = (bf16[512,128]{1,0:T(8,128)(2,1)S(1)}, bf16[512,128]{1,0:T(8,128)(2,1)S(1)}, u32[]{:S(2)}, u32[]{:S(2)}) collective-permute-start(bf16[512,128]{1,0:T(8,128)(2,1)S(1)} %get-tuple-element.65), channel_id=1, source_target_pairs={{0,6},{1,7},{2,4},{3,5},{4,2},{5,3},{6,0},{7,1},{8,14},{9,15},{10,... | collective-permute-start | bytes 393224 | tf_op jit(solution)/shard_map/ppermute | solution.py:312
  31.4 6.3 %collective-permute-start.8 = (bf16[512,128]{1,0:T(8,128)(2,1)S(1)}, bf16[512,128]{1,0:T(8,128)(2,1)S(1)}, u32[]{:S(2)}, u32[]{:S(2)}) collective-permute-start(bf16[512,128]{1,0:T(8,128)(2,1)S(1)} %get-tuple-element.62.refs_8_), channel_id=1, source_target_pairs={{0,1},{1,0},{2,3},{3,2},{4,5},{5,4},{6,7},{7,6},{8,9},{9,8},{10,11... | collective-permute-start | bytes 393224 | tf_op jit(solution)/shard_map/ppermute | solution.py:312
  33.2 4.6 %collective-permute-start.10 = (bf16[512,128]{1,0:T(8,128)(2,1)S(1)}, bf16[512,128]{1,0:T(8,128)(2,1)S(1)}, u32[]{:S(2)}, u32[]{:S(2)}) collective-permute-start(bf16[512,128]{1,0:T(8,128)(2,1)S(1)} %collective-permute-done.9.refs_9_), channel_id=1, source_target_pairs={{0,1},{1,0},{2,3},{3,2},{4,5},{5,4},{6,7},{7,6},{8,9},{9,8},{10,11... | collective-permute-start | bytes 393224 | tf_op jit(solution)/shard_map/ppermute | solution.py:312
  34.0 3.8 %collective-permute-start.12 = (bf16[512,128]{1,0:T(8,128)(2,1)S(1)}, bf16[512,128]{1,0:T(8,128)(2,1)S(1)}, u32[]{:S(2)}, u32[]{:S(2)}) collective-permute-start(bf16[512,128]{1,0:T(8,128)(2,1)S(1)} %collective-permute-done.11.refs_10_), channel_id=1, source_target_pairs={{0,1},{1,0},{2,3},{3,2},{4,5},{5,4},{6,7},{7,6},{8,9},{9,8},{10,11... | collective-permute-start | bytes 393224 | tf_op jit(solution)/shard_map/ppermute | solution.py:312
  36.2 1.6 %collective-permute-start.14 = (bf16[512,128]{1,0:T(8,128)(2,1)S(1)}, bf16[512,128]{1,0:T(8,128)(2,1)S(1)}, u32[]{:S(2)}, u32[]{:S(2)}) collective-permute-start(bf16[512,128]{1,0:T(8,128)(2,1)S(1)} %collective-permute-done.13.refs_11_), channel_id=1, source_target_pairs={{0,1},{1,0},{2,3},{3,2},{4,5},{5,4},{6,7},{7,6},{8,9},{9,8},{10,11... | collective-permute-start | bytes 393224 | tf_op jit(solution)/shard_map/ppermute | solution.py:312

commit v13 on v10

--- a/solution.py
+++ b/solution.py
@@ -185,41 +185,40 @@
     )(*slots, *others)
 
 
-def expand(slots, out, extras, extra_which):
-    count, depth = len(slots) // 2, slots[0].shape[1]
-    for n, slot in enumerate(slots):
-        block, s = divmod(n, count)
-        part = slot_rows(s, count, depth)
-        into = slice(block * count * depth, (block + 1) * count * depth)
-        target, extra = out.at[:, into], extras[block]
-        for which in range(2):
-
-            @pl.when(extra_which == which)
-            def _():
-                total = slot[which].astype(F32) + extra[which, part].astype(F32)
-                target[which, part] = total.astype(BF16)
-
-            @pl.when(extra_which != which)
-            def _():
-                target[which, part] = slot[which]
-
-
-def theirs_kernel(*refs):
-    slots, keep, out = refs[:-3], refs[-3:-1], refs[-1]
+def with_sums(slot, out, into, extra, part, extra_which):
+    for which in range(2):
+
+        @pl.when(extra_which == which)
+        def _():
+            total = slot[which].astype(F32) + extra[which, part].astype(F32)
+            out[which, into] = total.astype(BF16)
+
+        @pl.when(extra_which != which)
+        def _():
+            out[which, into] = slot[which]
+
+
+def placed_rows(s, count, depth):
+    _, far = near_far()
+    start = s // count * count * depth + lax.rem(far ^ s, count) * depth
+    return pl.ds(pl.multiple_of(start, depth), depth)
+
+
+def theirs_kernel(s, count, slot, keep, out):
+    depth = slot.shape[1]
     near, _ = near_far()
-    expand(slots, out, keep, near)
-
-
-def state_for_neighbour(slots, keep):
-    _, block, _ = keep[0].shape
-    return pl.pallas_call(
-        theirs_kernel,
+    with_sums(slot, out, pl.ds(0, depth), keep, slot_rows(s, count, depth), near)
+
+
+def state_for_neighbour(s, count, slot, keep):
+    return pl.pallas_call(
+        functools.partial(theirs_kernel, s, count),
         name="theirs",
-        in_specs=[VMEM] * (len(slots) + 2),
+        in_specs=[VMEM] * 2,
         out_specs=VMEM,
-        out_shape=jax.ShapeDtypeStruct((2, 2 * block, HEAD), BF16),
-        compiler_params=SMALL,
-    )(*slots, *keep)
+        out_shape=jax.ShapeDtypeStruct(slot.shape, BF16),
+        compiler_params=SMALL,
+    )(slot, keep[s // count])
 
 
 def local_kernel(*refs):
@@ -298,13 +297,17 @@
     tokens, local, slots, refs = refs[:4], refs[4:8], refs[8 : 8 + slot_count], refs[8 + slot_count :]
     got, outs, (rest, states, held, sems) = refs[:2], refs[2:6], refs[6:]
     near, _ = near_far()
-    expand(slots, states, got, 1 - near)
+    count, depth = slot_count // 2, slots[0].shape[1]
+    for s, slot in enumerate(slots):
+        into, part = placed_rows(s, count, depth), slot_rows(s, count, depth)
+        with_sums(slot, states, into, got[s // count], part, 1 - near)
     half = states.shape[1]
     copies = []
     for p in range(PIECES):
-        to = held.at[p] if p < PIECES - 1 else rest
+        late = p - PIECES // 2
+        to = held.at[p] if late < 0 else rest.at[late]
         product_piece(scale, True, p, tokens, local, states, to)
-        if p < PIECES - 1:
+        if late < 0:
             copies += copies_out(True, p, to, outs, sems, half)
             for copy in copies[-4:]:
                 copy.start()
@@ -316,16 +319,16 @@
     rows, width = tokens[0].shape
     half = width // 2
     out = jax.ShapeDtypeStruct((rows, width), BF16)
-    piece = (4, rows, half // PIECES)
+    pieces = (PIECES // 2, 4, rows, half // PIECES)
     *outs, rest = pl.pallas_call(
         functools.partial(finish_own_kernel, scale, len(slots)),
         name="finish_own",
         in_specs=[VMEM] * (10 + len(slots)),
         out_specs=[ANY] * 4 + [VMEM],
-        out_shape=[out] * 4 + [pltpu.VMEM(piece, BF16)],
+        out_shape=[out] * 4 + [pltpu.VMEM(pieces, BF16)],
         scratch_shapes=[
             pltpu.VMEM((2, half, HEAD), BF16),
-            pltpu.VMEM((PIECES - 1, *piece), BF16),
+            pltpu.VMEM(pieces, BF16),
             pltpu.SemaphoreType.DMA((4, PIECES)),
         ],
         cost_estimate=pl.CostEstimate(
@@ -336,13 +339,20 @@
     return outs, rest
 
 
-def finish_other_kernel(scale, *refs):
-    tokens, local, (states, rest), refs = refs[:4], refs[4:8], refs[8:10], refs[14:]
-    outs, (held, sems, rest_sems) = refs[:4], refs[4:]
+def finish_other_kernel(scale, slot_count, *refs):
+    tokens, local, slots, refs = refs[:4], refs[4:8], refs[8 : 8 + slot_count], refs[8 + slot_count :]
+    rest, outs, (states, held, sems, rest_sems) = refs[0], refs[5:9], refs[9:]
     half = states.shape[1]
-    copies = copies_out(True, PIECES - 1, rest, outs, rest_sems, half)
+    copies = []
+    for late in range(PIECES // 2):
+        copies += copies_out(True, PIECES // 2 + late, rest.at[late], outs, rest_sems, half)
     for copy in copies:
         copy.start()
+    count, depth = slot_count // 2, slots[0].shape[1]
+    for s, slot in enumerate(slots):
+        into = placed_rows(s, count, depth)
+        for which in range(2):
+            states[which, into] = slot[which]
     for p in range(PIECES):
         product_piece(scale, False, p, tokens, local, states, held.at[p])
         copies += copies_out(False, p, held.at[p], outs, sems, half)
@@ -352,26 +362,29 @@
         copy.wait()
 
 
-def finish_other(tokens, local, states, rest, scale, before):
-    rows, width = tokens[0].shape
+def finish_other(tokens, local, slots, rest, scale, before):
+    rows, width = tokens[0].shape
+    half = width // 2
     out = jax.ShapeDtypeStruct((rows, width), BF16)
-    return pl.pallas_call(
-        functools.partial(finish_other_kernel, scale),
+    inputs = [*tokens, *local, *slots, rest]
+    return pl.pallas_call(
+        functools.partial(finish_other_kernel, scale, len(slots)),
         name="finish_other",
-        in_specs=[VMEM] * 10 + [ANY] * 4,
+        in_specs=[VMEM] * len(inputs) + [ANY] * 4,
         out_specs=[ANY] * 4,
         out_shape=[out] * 4,
         scratch_shapes=[
-            pltpu.VMEM((PIECES, *rest.shape), BF16),
+            pltpu.VMEM((2, half, HEAD), BF16),
+            pltpu.VMEM((PIECES, 4, rows, half // PIECES), BF16),
             pltpu.SemaphoreType.DMA((4, PIECES)),
             pltpu.SemaphoreType.DMA((4, PIECES)),
         ],
-        input_output_aliases={10 + i: i for i in range(4)},
+        input_output_aliases={len(inputs) + i: i for i in range(4)},
         cost_estimate=pl.CostEstimate(
             flops=4 * rows * width * HEAD, bytes_accessed=17 * rows * width, transcendentals=0
         ),
         compiler_params=SMALL,
-    )(*tokens, *local, states, rest, *before)
+    )(*inputs, *before)
 
 
 def swap(x, axis, bits):
@@ -394,7 +407,8 @@
     sends = group_sends(slots, outer_count)
     others = [swap(send, "outer", s) for s, send in zip(distances(outer_count), sends)]
     slots = swap_far(scan_slots(slots, others))
-    arrived = swap(state_for_neighbour(slots, keep), "inner", 1)
+    theirs = [state_for_neighbour(s, far_count // 2, slot, keep) for s, slot in enumerate(slots)]
+    arrived = [swap(x, "inner", 1) for x in theirs]
     outs, rest = finish_own(tokens, local, slots, got, scale)
     return tuple(finish_other(tokens, local, arrived, rest, scale, outs))
 

time: 36.8 us -> 36.5 us (level)
  waiting for transfers between devices: 13.8 us -> 13.2 us
    ppermute x12 -> x15, waiting for transfers between devices: 13.8 us -> 13.2 us  [swap(): lax.ppermute(x, axis, [(i, i ^ bits) for i in range(lax.axis_size(axis))])]
    ppermute x12 -> x15, starting transfers between devices: 13.5 us -> 13.7 us  [swap(): lax.ppermute(x, axis, [(i, i ^ bits) for i in range(lax.axis_size(axis))])]
    pallas_call x2 -> x5, Pallas kernels: 1.76 us -> 1.8 us  [the longest x1 1.68 us: finish_other(): pl.pallas_call(functools.partial(finish_other_kernel, scale, len(slots)),...]
  transfers between devices with their start and end apart: 12 -> 15, of which waited for: 8 -> 7; matrix products, arithmetic and copies ran while one was open for 0% -> 0% of each run, Pallas kernels for 12% -> 13%
where the time goes in v13:
time: 36.5 us; the launch traced here: 36.4 us
  starting transfers between devices  13.7 us (38%)
  waiting for transfers between devices  13.2 us (36%)
  Pallas kernels  8.65 us (24%)
  between operations  0.79 us (2%)
    ppermute x15, starting transfers between devices, swap(): lax.ppermute(x, axis, [(i, i ^ bits) for i in range(lax.axis_size(axis))])  13.7 us
    ppermute x15, waiting for transfers between devices, swap(): lax.ppermute(x, axis, [(i, i ^ bits) for i in range(lax.axis_size(axis))])  13.2 us
    pallas_call x1, Pallas kernels, local_part(): pl.pallas_call(local_kernel, name='local', in_specs=[VMEM] * 4, out_specs...  2.16 us
    pallas_call x1, Pallas kernels, load(): pl.pallas_call(load_kernel, name='load', in_specs=[ANY] * 4, out_specs=[V...  1.84 us
    pallas_call x1, Pallas kernels, finish_other(): pl.pallas_call(functools.partial(finish_other_kernel, scale, len(slots)),...  1.68 us
    pallas_call x1, Pallas kernels, finish_own(): pl.pallas_call(functools.partial(finish_own_kernel, scale, len(slots)), n...  1.55 us
    pallas_call x2, Pallas kernels, sums(): pl.pallas_call(functools.partial(sums_kernel, wanted), name='sums', in_sp...  0.75 us
  transfers between devices with their start and end apart: 15, of which 7 were waited for; matrix products, arithmetic and copies ran while one was open for 0% of the time, Pallas kernels for 13%

profile of v13, /device:TPU:0, one launch (start us, length us, event | category | flops | bytes accessed | tf_op | source)
XLA Modules:
  0.0 36.4 jit_solution(9341788510154954111)
XLA Ops:
  0.6 1.8 %load.1 = (bf16[128,2048]{1,0:T(8,128)(2,1)S(1)}, bf16[128,2048]{1,0:T(8,128)(2,1)S(1)}, bf16[128,2048]{1,0:T(8,128)(2,1)S(1)}, bf16[128,2048]{1,0:T(8,128)(2,1)S(1)}, bf16[2,512,128]{2,1,0:T(8,128)(2,1)S(1)}) custom-call(bf16[128,2048]{1,0:T(8,128)(2,1)} %refs_0_.1, bf16[128,2048]{1,0:T(8,128)(2,1)} %refs_1_.1, bf16[128,2048]{1,0:T(8,128)(2,1)} %refs_2_.1, ...), custom_call_target="tpu_custom_call" | custom-call | flops 33554432 | bytes 2621440 | tf_op jit(solution)/shard_map/load/pallas_call | solution.py:72
  2.5 0.5 %collective-permute-start = (bf16[2,512,128]{2,1,0:T(8,128)(2,1)S(1)}, bf16[2,512,128]{2,1,0:T(8,128)(2,1)S(1)}, u32[]{:S(2)}, u32[]{:S(2)}) collective-permute-start(bf16[2,512,128]{2,1,0:T(8,128)(2,1)S(1)} %get-tuple-element.44), channel_id=1, source_target_pairs={{0,1},{1,0},{2,3},{3,2},{4,5},{5,4},{6,7},{7,6},{8,9},{9,8},{10,11... | collective-permute-start | bytes 786440 | tf_op jit(solution)/shard_map/ppermute | solution.py:391
  3.0 0.3 sums.3
  3.3 0.1 collective-permute-start.2
  3.4 0.5 %sums.2 = (bf16[2,512,128]{2,1,0:T(8,128)(2,1)S(1)}, bf16[2,512,128]{2,1,0:T(8,128)(2,1)S(1)}) custom-call(bf16[128,2048]{1,0:T(8,128)(2,1)S(1)} %get-tuple-element.39.refs_0_, bf16[128,2048]{1,0:T(8,128)(2,1)S(1)} %get-tuple-element.40.refs_1_, bf16[128,2048]{1,0:T(8,128)(2,1)S(1)} %get-tuple-element.41.refs_2_, bf16[128,2048]{1,0:T(8,128)(2,1)S(1)} %get-tuple-element.42.refs_3_), custom_call_target="tpu_custom_call" | custom-call | flops 67108864 | bytes 1572864 | tf_op jit(solution)/shard_map/sums/pallas_call | solution.py:94
  3.9 0.3 collective-permute-done.got_ref.refs_12_
  4.2 2.9 %collective-permute-start.1 = (bf16[2,256,128]{2,1,0:T(8,128)(2,1)S(1)}, bf16[2,256,128]{2,1,0:T(8,128)(2,1)S(1)}, u32[]{:S(2)}, u32[]{:S(2)}) collective-permute-start(bf16[2,256,128]{2,1,0:T(8,128)(2,1)S(1)} %get-tuple-element.46), channel_id=1, source_target_pairs={{0,2},{1,3},{2,0},{3,1},{4,6},{5,7},{6,4},{7,5},{8,10},{9,11},{10,... | collective-permute-start | bytes 393224 | tf_op jit(solution)/shard_map/ppermute | solution.py:391
  7.2 1.6 %collective-permute-start.3 = (bf16[2,256,128]{2,1,0:T(8,128)(2,1)S(1)}, bf16[2,256,128]{2,1,0:T(8,128)(2,1)S(1)}, u32[]{:S(2)}, u32[]{:S(2)}) collective-permute-start(bf16[2,256,128]{2,1,0:T(8,128)(2,1)S(1)} %get-tuple-element.48), channel_id=1, source_target_pairs={{0,4},{1,5},{2,6},{3,7},{4,0},{5,1},{6,2},{7,3},{8,12},{9,13},{10,... | collective-permute-start | bytes 393224 | tf_op jit(solution)/shard_map/ppermute | solution.py:391
  8.8 0.3 collective-permute-start.4
  9.1 2.2 %local.1 = (f32[128,2048]{1,0:T(8,128)S(1)}, f32[128,2048]{1,0:T(8,128)S(1)}, f32[128,2048]{1,0:T(8,128)S(1)}, f32[128,2048]{1,0:T(8,128)S(1)}) custom-call(bf16[128,2048]{1,0:T(8,128)(2,1)S(1)} %get-tuple-element.39.refs_0_, bf16[128,2048]{1,0:T(8,128)(2,1)S(1)} %get-tuple-element.40.refs_1_, bf16[128,2048]{1,0:T(8,128)(2,1)S(1)} %get-tuple-element.41.refs_2_, ...), custom_call_target="tpu_custom_call" | custom-call | flops 402653184 | bytes 6291456 | tf_op jit(solution)/shard_map/local/pallas_call | solution.py:255
  11.3 4.1 %collective-permute-done.3.refs_2_ = bf16[2,256,128]{2,1,0:T(8,128)(2,1)S(1)} collective-permute-done((bf16[2,256,128]{2,1,0:T(8,128)(2,1)S(1)}, bf16[2,256,128]{2,1,0:T(8,128)(2,1)S(1)}, u32[]{:S(2)}, u32[]{:S(2)}) %collective-permute-start.3) | collective-permute-done | bytes 131104 | tf_op jit(solution)/shard_map/ppermute | solution.py:391
  15.5 3.7 %collective-permute-start.5 = (bf16[256,128]{1,0:T(8,128)(2,1)S(1)}, bf16[256,128]{1,0:T(8,128)(2,1)S(1)}, u32[]{:S(2)}, u32[]{:S(2)}) collective-permute-start(bf16[256,128]{1,0:T(8,128)(2,1)S(1)} %get-tuple-element.62), channel_id=1, source_target_pairs={{0,24},{8,16},{16,8},{24,0},{1,25},{9,17},{17,9},{25,1},{2,26},{10... | collective-permute-start | bytes 196616 | tf_op jit(solution)/shard_map/ppermute | solution.py:391
  19.1 0.8 %collective-permute-start.7 = (bf16[256,128]{1,0:T(8,128)(2,1)S(1)}, bf16[256,128]{1,0:T(8,128)(2,1)S(1)}, u32[]{:S(2)}, u32[]{:S(2)}) collective-permute-start(bf16[256,128]{1,0:T(8,128)(2,1)S(1)} %get-tuple-element.64), channel_id=1, source_target_pairs={{0,8},{8,0},{16,24},{24,16},{1,9},{9,1},{17,25},{25,17},{2,10},{10... | collective-permute-start | bytes 196616 | tf_op jit(solution)/shard_map/ppermute | solution.py:391
  19.9 1.7 %collective-permute-done.5.refs_4_ = bf16[256,128]{1,0:T(8,128)(2,1)S(1)} collective-permute-done((bf16[256,128]{1,0:T(8,128)(2,1)S(1)}, bf16[256,128]{1,0:T(8,128)(2,1)S(1)}, u32[]{:S(2)}, u32[]{:S(2)}) %collective-permute-start.5) | collective-permute-done | bytes 65568 | tf_op jit(solution)/shard_map/ppermute | solution.py:391
  21.6 2.7 %collective-permute-done.6.refs_5_ = bf16[256,128]{1,0:T(8,128)(2,1)S(1)} collective-permute-done((bf16[256,128]{1,0:T(8,128)(2,1)S(1)}, bf16[256,128]{1,0:T(8,128)(2,1)S(1)}, u32[]{:S(2)}, u32[]{:S(2)}) %collective-permute-start.6) | collective-permute-done | bytes 65568 | tf_op jit(solution)/shard_map/ppermute | solution.py:391
  24.3 0.3 scan.1
  24.6 1.3 %collective-permute-start.9 = (bf16[2,256,128]{2,1,0:T(8,128)(2,1)S(1)}, bf16[2,256,128]{2,1,0:T(8,128)(2,1)S(1)}, u32[]{:S(2)}, u32[]{:S(2)}) collective-permute-start(bf16[2,256,128]{2,1,0:T(8,128)(2,1)S(1)} %get-tuple-element.66), channel_id=1, source_target_pairs={{0,2},{1,3},{2,0},{3,1},{4,6},{5,7},{6,4},{7,5},{8,10},{9,11},{10,... | collective-permute-start | bytes 393224 | tf_op jit(solution)/shard_map/ppermute | solution.py:391
  25.9 1.2 %collective-permute-start.11 = (bf16[2,256,128]{2,1,0:T(8,128)(2,1)S(1)}, bf16[2,256,128]{2,1,0:T(8,128)(2,1)S(1)}, u32[]{:S(2)}, u32[]{:S(2)}) collective-permute-start(bf16[2,256,128]{2,1,0:T(8,128)(2,1)S(1)} %get-tuple-element.67), channel_id=1, source_target_pairs={{0,4},{1,5},{2,6},{3,7},{4,0},{5,1},{6,2},{7,3},{8,12},{9,13},{10,... | collective-permute-start | bytes 393224 | tf_op jit(solution)/shard_map/ppermute | solution.py:391
  27.1 1.1 %collective-permute-start.13 = (bf16[2,256,128]{2,1,0:T(8,128)(2,1)S(1)}, bf16[2,256,128]{2,1,0:T(8,128)(2,1)S(1)}, u32[]{:S(2)}, u32[]{:S(2)}) collective-permute-start(bf16[2,256,128]{2,1,0:T(8,128)(2,1)S(1)} %get-tuple-element.68), channel_id=1, source_target_pairs={{0,6},{1,7},{2,4},{3,5},{4,2},{5,3},{6,0},{7,1},{8,14},{9,15},{10,... | collective-permute-start | bytes 393224 | tf_op jit(solution)/shard_map/ppermute | solution.py:391
  28.3 2.7 %collective-permute-done.9.slot.refs_9_ = bf16[2,256,128]{2,1,0:T(8,128)(2,1)S(1)} collective-permute-done((bf16[2,256,128]{2,1,0:T(8,128)(2,1)S(1)}, bf16[2,256,128]{2,1,0:T(8,128)(2,1)S(1)}, u32[]{:S(2)}, u32[]{:S(2)}) %collective-permute-start.9) | collective-permute-done | bytes 131104 | tf_op jit(solution)/shard_map/ppermute | solution.py:391
  31.1 0.8 %collective-permute-done.11.slot.refs_10_ = bf16[2,256,128]{2,1,0:T(8,128)(2,1)S(1)} collective-permute-done((bf16[2,256,128]{2,1,0:T(8,128)(2,1)S(1)}, bf16[2,256,128]{2,1,0:T(8,128)(2,1)S(1)}, u32[]{:S(2)}, u32[]{:S(2)}) %collective-permute-start.11) | collective-permute-done | bytes 131104 | tf_op jit(solution)/shard_map/ppermute | solution.py:391
  32.1 0.9 %collective-permute-done.13.slot.refs_11_ = bf16[2,256,128]{2,1,0:T(8,128)(2,1)S(1)} collective-permute-done((bf16[2,256,128]{2,1,0:T(8,128)(2,1)S(1)}, bf16[2,256,128]{2,1,0:T(8,128)(2,1)S(1)}, u32[]{:S(2)}, u32[]{:S(2)}) %collective-permute-start.13) | collective-permute-done | bytes 131104 | tf_op jit(solution)/shard_map/ppermute | solution.py:391
  33.1 1.5 %finish_own.1 = (bf16[128,2048]{1,0:T(8,128)(2,1)}, bf16[128,2048]{1,0:T(8,128)(2,1)}, bf16[128,2048]{1,0:T(8,128)(2,1)}, bf16[128,2048]{1,0:T(8,128)(2,1)}, bf16[2,4,128,256]{3,2,1,0:T(8,128)(2,1)S(1)}) custom-call(bf16[128,2048]{1,0:T(8,128)(2,1)S(1)} %get-tuple-element.39.refs_0_, bf16[128,2048]{1,0:T(8,128)(2,1)S(1)} %get-tuple-element.40.refs_1_, ...), custom_call_target="tpu_custom_call" | custom-call | flops 134217728 | bytes 4456448 | tf_op jit(solution)/shard_map/finish_own/pallas_call | solution.py:323
  34.7 1.7 %finish_other.1 = (bf16[128,2048]{1,0:T(8,128)(2,1)}, bf16[128,2048]{1,0:T(8,128)(2,1)}, bf16[128,2048]{1,0:T(8,128)(2,1)}, bf16[128,2048]{1,0:T(8,128)(2,1)}) custom-call(bf16[128,2048]{1,0:T(8,128)(2,1)S(1)} %get-tuple-element.39.refs_0_, ...), custom_call_target="tpu_custom_call", output_to_operand_aliasing={{0}: (13, {}), {1}: (14, {}), {2}: (15, {}), {3}: (16, {})} | custom-call | flops 134217728 | bytes 4456448 | tf_op jit(solution)/shard_map/finish_other/pallas_call | solution.py:370
  (20 shorter events, 0.6 us)
Async XLA Ops:
  2.5 1.7 %collective-permute-start = (bf16[2,512,128]{2,1,0:T(8,128)(2,1)S(1)}, bf16[2,512,128]{2,1,0:T(8,128)(2,1)S(1)}, u32[]{:S(2)}, u32[]{:S(2)}) collective-permute-start(bf16[2,512,128]{2,1,0:T(8,128)(2,1)S(1)} %get-tuple-element.44), channel_id=1, source_target_pairs={{0,1},{1,0},{2,3},{3,2},{4,5},{5,4},{6,7},{7,6},{8,9},{9,8},{10,11... | collective-permute-start | bytes 786440 | tf_op jit(solution)/shard_map/ppermute | solution.py:391
  3.3 3.9 %collective-permute-start.2 = (bf16[2,512,128]{2,1,0:T(8,128)(2,1)S(1)}, bf16[2,512,128]{2,1,0:T(8,128)(2,1)S(1)}, u32[]{:S(2)}, u32[]{:S(2)}) collective-permute-start(bf16[2,512,128]{2,1,0:T(8,128)(2,1)S(1)} %sums.3), channel_id=1, source_target_pairs={{0,1},{1,0},{2,3},{3,2},{4,5},{5,4},{6,7},{7,6},{8,9},{9,8},{10,11... | collective-permute-start | bytes 786440 | tf_op jit(solution)/shard_map/ppermute | solution.py:391
  4.2 7.0 %collective-permute-start.1 = (bf16[2,256,128]{2,1,0:T(8,128)(2,1)S(1)}, bf16[2,256,128]{2,1,0:T(8,128)(2,1)S(1)}, u32[]{:S(2)}, u32[]{:S(2)}) collective-permute-start(bf16[2,256,128]{2,1,0:T(8,128)(2,1)S(1)} %get-tuple-element.46), channel_id=1, source_target_pairs={{0,2},{1,3},{2,0},{3,1},{4,6},{5,7},{6,4},{7,5},{8,10},{9,11},{10,... | collective-permute-start | bytes 393224 | tf_op jit(solution)/shard_map/ppermute | solution.py:391
  7.2 8.1 %collective-permute-start.3 = (bf16[2,256,128]{2,1,0:T(8,128)(2,1)S(1)}, bf16[2,256,128]{2,1,0:T(8,128)(2,1)S(1)}, u32[]{:S(2)}, u32[]{:S(2)}) collective-permute-start(bf16[2,256,128]{2,1,0:T(8,128)(2,1)S(1)} %get-tuple-element.48), channel_id=1, source_target_pairs={{0,4},{1,5},{2,6},{3,7},{4,0},{5,1},{6,2},{7,3},{8,12},{9,13},{10,... | collective-permute-start | bytes 393224 | tf_op jit(solution)/shard_map/ppermute | solution.py:391
  8.8 6.5 %collective-permute-start.4 = (bf16[2,256,128]{2,1,0:T(8,128)(2,1)S(1)}, bf16[2,256,128]{2,1,0:T(8,128)(2,1)S(1)}, u32[]{:S(2)}, u32[]{:S(2)}) collective-permute-start(bf16[2,256,128]{2,1,0:T(8,128)(2,1)S(1)} %get-tuple-element.49), channel_id=1, source_target_pairs={{0,6},{1,7},{2,4},{3,5},{4,2},{5,3},{6,0},{7,1},{8,14},{9,15},{10,... | collective-permute-start | bytes 393224 | tf_op jit(solution)/shard_map/ppermute | solution.py:391
  15.5 6.1 %collective-permute-start.5 = (bf16[256,128]{1,0:T(8,128)(2,1)S(1)}, bf16[256,128]{1,0:T(8,128)(2,1)S(1)}, u32[]{:S(2)}, u32[]{:S(2)}) collective-permute-start(bf16[256,128]{1,0:T(8,128)(2,1)S(1)} %get-tuple-element.62), channel_id=1, source_target_pairs={{0,24},{8,16},{16,8},{24,0},{1,25},{9,17},{17,9},{25,1},{2,26},{10... | collective-permute-start | bytes 196616 | tf_op jit(solution)/shard_map/ppermute | solution.py:391
  19.1 5.2 %collective-permute-start.6 = (bf16[256,128]{1,0:T(8,128)(2,1)S(1)}, bf16[256,128]{1,0:T(8,128)(2,1)S(1)}, u32[]{:S(2)}, u32[]{:S(2)}) collective-permute-start(bf16[256,128]{1,0:T(8,128)(2,1)S(1)} %get-tuple-element.63), channel_id=1, source_target_pairs={{0,16},{8,24},{16,0},{24,8},{1,17},{9,25},{17,1},{25,9},{2,18},{10... | collective-permute-start | bytes 196616 | tf_op jit(solution)/shard_map/ppermute | solution.py:391
  19.1 5.2 %collective-permute-start.7 = (bf16[256,128]{1,0:T(8,128)(2,1)S(1)}, bf16[256,128]{1,0:T(8,128)(2,1)S(1)}, u32[]{:S(2)}, u32[]{:S(2)}) collective-permute-start(bf16[256,128]{1,0:T(8,128)(2,1)S(1)} %get-tuple-element.64), channel_id=1, source_target_pairs={{0,8},{8,0},{16,24},{24,16},{1,9},{9,1},{17,25},{25,17},{2,10},{10... | collective-permute-start | bytes 196616 | tf_op jit(solution)/shard_map/ppermute | solution.py:391
  24.6 6.4 %collective-permute-start.9 = (bf16[2,256,128]{2,1,0:T(8,128)(2,1)S(1)}, bf16[2,256,128]{2,1,0:T(8,128)(2,1)S(1)}, u32[]{:S(2)}, u32[]{:S(2)}) collective-permute-start(bf16[2,256,128]{2,1,0:T(8,128)(2,1)S(1)} %get-tuple-element.66), channel_id=1, source_target_pairs={{0,2},{1,3},{2,0},{3,1},{4,6},{5,7},{6,4},{7,5},{8,10},{9,11},{10,... | collective-permute-start | bytes 393224 | tf_op jit(solution)/shard_map/ppermute | solution.py:391
  25.9 6.1 %collective-permute-start.11 = (bf16[2,256,128]{2,1,0:T(8,128)(2,1)S(1)}, bf16[2,256,128]{2,1,0:T(8,128)(2,1)S(1)}, u32[]{:S(2)}, u32[]{:S(2)}) collective-permute-start(bf16[2,256,128]{2,1,0:T(8,128)(2,1)S(1)} %get-tuple-element.67), channel_id=1, source_target_pairs={{0,4},{1,5},{2,6},{3,7},{4,0},{5,1},{6,2},{7,3},{8,12},{9,13},{10,... | collective-permute-start | bytes 393224 | tf_op jit(solution)/shard_map/ppermute | solution.py:391
  27.1 5.9 %collective-permute-start.13 = (bf16[2,256,128]{2,1,0:T(8,128)(2,1)S(1)}, bf16[2,256,128]{2,1,0:T(8,128)(2,1)S(1)}, u32[]{:S(2)}, u32[]{:S(2)}) collective-permute-start(bf16[2,256,128]{2,1,0:T(8,128)(2,1)S(1)} %get-tuple-element.68), channel_id=1, source_target_pairs={{0,6},{1,7},{2,4},{3,5},{4,2},{5,3},{6,0},{7,1},{8,14},{9,15},{10,... | collective-permute-start | bytes 393224 | tf_op jit(solution)/shard_map/ppermute | solution.py:391
  28.2 6.4 %collective-permute-start.8 = (bf16[2,256,128]{2,1,0:T(8,128)(2,1)S(1)}, bf16[2,256,128]{2,1,0:T(8,128)(2,1)S(1)}, u32[]{:S(2)}, u32[]{:S(2)}) collective-permute-start(bf16[2,256,128]{2,1,0:T(8,128)(2,1)S(1)} %theirs.4), channel_id=1, source_target_pairs={{0,1},{1,0},{2,3},{3,2},{4,5},{5,4},{6,7},{7,6},{8,9},{9,8},{10,11... | collective-permute-start | bytes 393224 | tf_op jit(solution)/shard_map/ppermute | solution.py:391
  31.0 3.6 %collective-permute-start.10 = (bf16[2,256,128]{2,1,0:T(8,128)(2,1)S(1)}, bf16[2,256,128]{2,1,0:T(8,128)(2,1)S(1)}, u32[]{:S(2)}, u32[]{:S(2)}) collective-permute-start(bf16[2,256,128]{2,1,0:T(8,128)(2,1)S(1)} %theirs.5), channel_id=1, source_target_pairs={{0,1},{1,0},{2,3},{3,2},{4,5},{5,4},{6,7},{7,6},{8,9},{9,8},{10,11... | collective-permute-start | bytes 393224 | tf_op jit(solution)/shard_map/ppermute | solution.py:391
  32.0 2.6 %collective-permute-start.12 = (bf16[2,256,128]{2,1,0:T(8,128)(2,1)S(1)}, bf16[2,256,128]{2,1,0:T(8,128)(2,1)S(1)}, u32[]{:S(2)}, u32[]{:S(2)}) collective-permute-start(bf16[2,256,128]{2,1,0:T(8,128)(2,1)S(1)} %theirs.6), channel_id=1, source_target_pairs={{0,1},{1,0},{2,3},{3,2},{4,5},{5,4},{6,7},{7,6},{8,9},{9,8},{10,11... | collective-permute-start | bytes 393224 | tf_op jit(solution)/shard_map/ppermute | solution.py:391
  33.0 1.7 %collective-permute-start.14 = (bf16[2,256,128]{2,1,0:T(8,128)(2,1)S(1)}, bf16[2,256,128]{2,1,0:T(8,128)(2,1)S(1)}, u32[]{:S(2)}, u32[]{:S(2)}) collective-permute-start(bf16[2,256,128]{2,1,0:T(8,128)(2,1)S(1)} %theirs.7), channel_id=1, source_target_pairs={{0,1},{1,0},{2,3},{3,2},{4,5},{5,4},{6,7},{7,6},{8,9},{9,8},{10,11... | collective-permute-start | bytes 393224 | tf_op jit(solution)/shard_map/ppermute | solution.py:391

commit v14 on v13

--- a/solution.py
+++ b/solution.py
@@ -8,7 +8,7 @@
 from jax.sharding import PartitionSpec as P
 
 HEAD = 128
-PIECES = 4
+PIECES = 2
 MIB = 1024 * 1024
 ANY = pl.BlockSpec(memory_space=pl.ANY)
 VMEM = pl.BlockSpec(memory_space=pltpu.VMEM)
@@ -50,7 +50,8 @@
 
 def sums_of(tokens, start, out):
     for n in range(out.shape[1] // HEAD):
-        q, k, v, d = (ref[:, columns(start, n)] for ref in tokens)
+        cols = columns(start, n) if not isinstance(start, int) else pl.ds(start + n * HEAD, HEAD)
+        q, k, v, d = (ref[:, cols] for ref in tokens)
         out[0, n * HEAD : (n + 1) * HEAD] = dot(k, v, 0, 0).astype(BF16)
         out[1, n * HEAD : (n + 1) * HEAD] = dot(q, d, 0, 0).astype(BF16)
 
@@ -64,7 +65,10 @@
         copy.start()
     for copy in copies:
         copy.wait()
-    sums_of(held, block_start(False, 0, held[0].shape[1] // 2), out)
+    width = held[0].shape[1]
+    start = block_start(False, 0, width // 2)
+    for n in range(4):
+        pl.when(start == n * width // 4)(functools.partial(sums_of, held, n * width // 4, out))
 
 
 def load(tokens):
@@ -153,24 +157,23 @@
 
 
 def scan_kernel(far_count, *refs):
-    slots, others, outs = refs[:far_count], refs[far_count:-far_count], refs[-far_count:]
+    slots, others, refs = refs[:far_count], refs[far_count : -far_count - 2], refs[-far_count - 2 :]
+    outs, (held, scanned) = refs[:far_count], refs[far_count:]
     outer = lax.axis_index("outer")
     _, far = near_far()
+    for s, slot in enumerate(slots):
+        held[far ^ s] = slot[...]
     for which in range(2):
-        base = jnp.zeros(slots[0].shape[1:], F32)
+        total = jnp.zeros(held.shape[2:], F32)
         for s, other in zip(distances(len(others) + 1), others):
             below = (outer ^ s) < outer
             wanted = below if which == 0 else jnp.logical_not(below)
-            base += jnp.where(wanted, other[...].astype(F32), 0.0)
-        terms = [slot[which].astype(F32) for slot in slots]
-        for s, out in enumerate(outs):
-            total = base
-            for t, term in enumerate(terms):
-                if s != t:
-                    below = (far ^ t) < (far ^ s)
-                    wanted = below if which == 0 else jnp.logical_not(below)
-                    total += jnp.where(wanted, term, 0.0)
-            out[which] = total.astype(BF16)
+            total += jnp.where(wanted, other[...].astype(F32), 0.0)
+        for i in reversed(range(far_count)) if which else range(far_count):
+            scanned[i, which] = total.astype(BF16)
+            total += held[i, which].astype(F32)
+    for s, out in enumerate(outs):
+        out[...] = scanned[far ^ s]
 
 
 def scan_slots(slots, others):
@@ -181,33 +184,34 @@
         in_specs=[VMEM] * (far_count + len(others)),
         out_specs=[VMEM] * far_count,
         out_shape=[slot] * far_count,
+        scratch_shapes=[pltpu.VMEM((far_count, *slot.shape), BF16)] * 2,
         compiler_params=SMALL,
     )(*slots, *others)
 
 
-def with_sums(slot, out, into, extra, part, extra_which):
-    for which in range(2):
-
-        @pl.when(extra_which == which)
-        def _():
-            total = slot[which].astype(F32) + extra[which, part].astype(F32)
-            out[which, into] = total.astype(BF16)
-
-        @pl.when(extra_which != which)
-        def _():
-            out[which, into] = slot[which]
-
-
-def placed_rows(s, count, depth):
+def with_sums(slot, which, extra, part):
+    return (slot[which].astype(F32) + extra[which, part].astype(F32)).astype(BF16)
+
+
+def half_rows(s, depth):
     _, far = near_far()
-    start = s // count * count * depth + lax.rem(far ^ s, count) * depth
-    return pl.ds(pl.multiple_of(start, depth), depth)
+    return pl.ds(pl.multiple_of((far ^ s) * depth, depth), depth)
+
+
+def by_core(run):
+    near, _ = near_far()
+    for core in range(2):
+        pl.when(near == core)(functools.partial(run, core))
 
 
 def theirs_kernel(s, count, slot, keep, out):
-    depth = slot.shape[1]
-    near, _ = near_far()
-    with_sums(slot, out, pl.ds(0, depth), keep, slot_rows(s, count, depth), near)
+    part = slot_rows(s, count, slot.shape[1])
+
+    def run(core):
+        out[core] = with_sums(slot, core, keep, part)
+        out[1 - core] = slot[1 - core]
+
+    by_core(run)
 
 
 def state_for_neighbour(s, count, slot, keep):
@@ -265,18 +269,12 @@
     )(*tokens)
 
 
-def heads_of(own, p, half):
-    piece = half // PIECES
-    block, at = divmod(p, PIECES // 2)
-    return block_start(own, block, half) + at * piece
-
-
-def product_piece(scale, own, p, tokens, local, states, held):
+def product_piece(scale, side, p, tokens, local, states, held):
     half = states.shape[1]
     piece = half // PIECES
-    start = heads_of(own, p, half)
     for n in range(piece // HEAD):
-        rows, cols = slice(p * piece + n * HEAD, p * piece + (n + 1) * HEAD), columns(start, n)
+        at = p * piece + n * HEAD
+        rows, cols = slice(at, at + HEAD), slice(side * half + at, side * half + at + HEAD)
         q, k, v, d = (ref[:, cols] for ref in tokens)
         s, g = states[0, rows], states[1, rows]
         parts = (dot(q, s, 1, 0), dot(d, s, 1, 1), dot(v, g, 1, 1), dot(k, g, 1, 0))
@@ -285,8 +283,8 @@
             held[i, :, n * HEAD : (n + 1) * HEAD] = out
 
 
-def copies_out(own, p, held, outs, sems, half):
-    there = pl.ds(pl.multiple_of(heads_of(own, p, half), half // PIECES), half // PIECES)
+def copies_out(side, p, held, outs, sems, half):
+    there = pl.ds(side * half + p * half // PIECES, half // PIECES)
     return [
         pltpu.make_async_copy(held.at[i], out.at[:, there], sems.at[i, p])
         for i, out in enumerate(outs)
@@ -296,23 +294,27 @@
 def finish_own_kernel(scale, slot_count, *refs):
     tokens, local, slots, refs = refs[:4], refs[4:8], refs[8 : 8 + slot_count], refs[8 + slot_count :]
     got, outs, (rest, states, held, sems) = refs[:2], refs[2:6], refs[6:]
-    near, _ = near_far()
-    count, depth = slot_count // 2, slots[0].shape[1]
-    for s, slot in enumerate(slots):
-        into, part = placed_rows(s, count, depth), slot_rows(s, count, depth)
-        with_sums(slot, states, into, got[s // count], part, 1 - near)
-    half = states.shape[1]
-    copies = []
-    for p in range(PIECES):
-        late = p - PIECES // 2
-        to = held.at[p] if late < 0 else rest.at[late]
-        product_piece(scale, True, p, tokens, local, states, to)
-        if late < 0:
-            copies += copies_out(True, p, to, outs, sems, half)
-            for copy in copies[-4:]:
-                copy.start()
-    for copy in copies:
-        copy.wait()
+    count, depth, half = slot_count // 2, slots[0].shape[1], states.shape[1]
+
+    def run(core):
+        for s, slot in enumerate(slots):
+            into = half_rows(s, depth)
+            states[core, into] = slot[core]
+            part = slot_rows(s, count, depth)
+            states[1 - core, into] = with_sums(slot, 1 - core, got[s // count], part)
+        copies = []
+        for p in range(PIECES):
+            late = p - PIECES // 2
+            to = held.at[p] if late < 0 else rest.at[late]
+            product_piece(scale, core, p, tokens, local, states, to)
+            if late < 0:
+                copies += copies_out(core, p, to, outs, sems, half)
+                for copy in copies[-4:]:
+                    copy.start()
+        for copy in copies:
+            copy.wait()
+
+    by_core(run)
 
 
 def finish_own(tokens, local, slots, got, scale):
@@ -342,24 +344,25 @@
 def finish_other_kernel(scale, slot_count, *refs):
     tokens, local, slots, refs = refs[:4], refs[4:8], refs[8 : 8 + slot_count], refs[8 + slot_count :]
     rest, outs, (states, held, sems, rest_sems) = refs[0], refs[5:9], refs[9:]
-    half = states.shape[1]
-    copies = []
-    for late in range(PIECES // 2):
-        copies += copies_out(True, PIECES // 2 + late, rest.at[late], outs, rest_sems, half)
-    for copy in copies:
-        copy.start()
-    count, depth = slot_count // 2, slots[0].shape[1]
-    for s, slot in enumerate(slots):
-        into = placed_rows(s, count, depth)
-        for which in range(2):
-            states[which, into] = slot[which]
-    for p in range(PIECES):
-        product_piece(scale, False, p, tokens, local, states, held.at[p])
-        copies += copies_out(False, p, held.at[p], outs, sems, half)
-        for copy in copies[-4:]:
+    depth, half = slots[0].shape[1], states.shape[1]
+
+    def run(core):
+        copies = []
+        for late in range(PIECES // 2):
+            copies += copies_out(core, PIECES // 2 + late, rest.at[late], outs, rest_sems, half)
+        for copy in copies:
             copy.start()
-    for copy in copies:
-        copy.wait()
+        for s, slot in enumerate(slots):
+            states[:, half_rows(s, depth)] = slot[...]
+        for p in range(PIECES):
+            product_piece(scale, 1 - core, p, tokens, local, states, held.at[p])
+            copies += copies_out(1 - core, p, held.at[p], outs, sems, half)
+            for copy in copies[-4:]:
+                copy.start()
+        for copy in copies:
+            copy.wait()
+
+    by_core(run)
 
 
 def finish_other(tokens, local, slots, rest, scale, before):

time: 36.5 us -> 36.1 us (0.989)
  Pallas kernels: 8.65 us -> 8.19 us
where the time goes in v14:
time: 36.1 us; the launch traced here: 35.9 us
  starting transfers between devices  13.7 us (38%)
  waiting for transfers between devices  13.2 us (37%)
  Pallas kernels  8.19 us (23%)
  between operations  0.79 us (2%)
    ppermute x15, starting transfers between devices, swap(): lax.ppermute(x, axis, [(i, i ^ bits) for i in range(lax.axis_size(axis))])  13.7 us
    ppermute x15, waiting for transfers between devices, swap(): lax.ppermute(x, axis, [(i, i ^ bits) for i in range(lax.axis_size(axis))])  13.2 us
    pallas_call x1, Pallas kernels, local_part(): pl.pallas_call(local_kernel, name='local', in_specs=[VMEM] * 4, out_specs...  2.16 us
    pallas_call x1, Pallas kernels, load(): pl.pallas_call(load_kernel, name='load', in_specs=[ANY] * 4, out_specs=[V...  1.82 us
    pallas_call x1, Pallas kernels, finish_other(): pl.pallas_call(functools.partial(finish_other_kernel, scale, len(slots)),...  1.58 us
    pallas_call x1, Pallas kernels, finish_own(): pl.pallas_call(functools.partial(finish_own_kernel, scale, len(slots)), n...  1.37 us
    pallas_call x2, Pallas kernels, sums(): pl.pallas_call(functools.partial(sums_kernel, wanted), name='sums', in_sp...  0.75 us
  transfers between devices with their start and end apart: 15, of which 7 were waited for; matrix products, arithmetic and copies ran while one was open for 0% of the time, Pallas kernels for 13%

profile of v14, /device:TPU:0, one launch (start us, length us, event | category | flops | bytes accessed | tf_op | source)
XLA Modules:
  0.0 35.9 jit_solution(4367340491126530994)
XLA Ops:
  0.6 1.8 %load.1 = (bf16[128,2048]{1,0:T(8,128)(2,1)S(1)}, bf16[128,2048]{1,0:T(8,128)(2,1)S(1)}, bf16[128,2048]{1,0:T(8,128)(2,1)S(1)}, bf16[128,2048]{1,0:T(8,128)(2,1)S(1)}, bf16[2,512,128]{2,1,0:T(8,128)(2,1)S(1)}) custom-call(bf16[128,2048]{1,0:T(8,128)(2,1)} %refs_0_.1, bf16[128,2048]{1,0:T(8,128)(2,1)} %refs_1_.1, bf16[128,2048]{1,0:T(8,128)(2,1)} %refs_2_.1, ...), custom_call_target="tpu_custom_call" | custom-call | flops 33554432 | bytes 2621440 | tf_op jit(solution)/shard_map/load/pallas_call | solution.py:76
  2.5 0.5 %collective-permute-start = (bf16[2,512,128]{2,1,0:T(8,128)(2,1)S(1)}, bf16[2,512,128]{2,1,0:T(8,128)(2,1)S(1)}, u32[]{:S(2)}, u32[]{:S(2)}) collective-permute-start(bf16[2,512,128]{2,1,0:T(8,128)(2,1)S(1)} %get-tuple-element.44), channel_id=1, source_target_pairs={{0,1},{1,0},{2,3},{3,2},{4,5},{5,4},{6,7},{7,6},{8,9},{9,8},{10,11... | collective-permute-start | bytes 786440 | tf_op jit(solution)/shard_map/ppermute | solution.py:394
  3.0 0.3 sums.3
  3.3 0.1 collective-permute-start.2
  3.4 0.5 %sums.2 = (bf16[2,512,128]{2,1,0:T(8,128)(2,1)S(1)}, bf16[2,512,128]{2,1,0:T(8,128)(2,1)S(1)}) custom-call(bf16[128,2048]{1,0:T(8,128)(2,1)S(1)} %get-tuple-element.39.refs_0_, bf16[128,2048]{1,0:T(8,128)(2,1)S(1)} %get-tuple-element.40.refs_1_, bf16[128,2048]{1,0:T(8,128)(2,1)S(1)} %get-tuple-element.41.refs_2_, bf16[128,2048]{1,0:T(8,128)(2,1)S(1)} %get-tuple-element.42.refs_3_), custom_call_target="tpu_custom_call" | custom-call | flops 67108864 | bytes 1572864 | tf_op jit(solution)/shard_map/sums/pallas_call | solution.py:98
  3.9 0.3 collective-permute-done.got_ref.refs_12_
  4.2 2.9 %collective-permute-start.1 = (bf16[2,256,128]{2,1,0:T(8,128)(2,1)S(1)}, bf16[2,256,128]{2,1,0:T(8,128)(2,1)S(1)}, u32[]{:S(2)}, u32[]{:S(2)}) collective-permute-start(bf16[2,256,128]{2,1,0:T(8,128)(2,1)S(1)} %get-tuple-element.46), channel_id=1, source_target_pairs={{0,2},{1,3},{2,0},{3,1},{4,6},{5,7},{6,4},{7,5},{8,10},{9,11},{10,... | collective-permute-start | bytes 393224 | tf_op jit(solution)/shard_map/ppermute | solution.py:394
  7.2 1.6 %collective-permute-start.3 = (bf16[2,256,128]{2,1,0:T(8,128)(2,1)S(1)}, bf16[2,256,128]{2,1,0:T(8,128)(2,1)S(1)}, u32[]{:S(2)}, u32[]{:S(2)}) collective-permute-start(bf16[2,256,128]{2,1,0:T(8,128)(2,1)S(1)} %get-tuple-element.48), channel_id=1, source_target_pairs={{0,4},{1,5},{2,6},{3,7},{4,0},{5,1},{6,2},{7,3},{8,12},{9,13},{10,... | collective-permute-start | bytes 393224 | tf_op jit(solution)/shard_map/ppermute | solution.py:394
  8.8 0.3 collective-permute-start.4
  9.1 2.2 %local.1 = (f32[128,2048]{1,0:T(8,128)S(1)}, f32[128,2048]{1,0:T(8,128)S(1)}, f32[128,2048]{1,0:T(8,128)S(1)}, f32[128,2048]{1,0:T(8,128)S(1)}) custom-call(bf16[128,2048]{1,0:T(8,128)(2,1)S(1)} %get-tuple-element.39.refs_0_, bf16[128,2048]{1,0:T(8,128)(2,1)S(1)} %get-tuple-element.40.refs_1_, bf16[128,2048]{1,0:T(8,128)(2,1)S(1)} %get-tuple-element.41.refs_2_, ...), custom_call_target="tpu_custom_call" | custom-call | flops 402653184 | bytes 6291456 | tf_op jit(solution)/shard_map/local/pallas_call | solution.py:259
  11.3 4.1 %collective-permute-done.3.refs_2_ = bf16[2,256,128]{2,1,0:T(8,128)(2,1)S(1)} collective-permute-done((bf16[2,256,128]{2,1,0:T(8,128)(2,1)S(1)}, bf16[2,256,128]{2,1,0:T(8,128)(2,1)S(1)}, u32[]{:S(2)}, u32[]{:S(2)}) %collective-permute-start.3) | collective-permute-done | bytes 131104 | tf_op jit(solution)/shard_map/ppermute | solution.py:394
  15.4 3.7 %collective-permute-start.5 = (bf16[256,128]{1,0:T(8,128)(2,1)S(1)}, bf16[256,128]{1,0:T(8,128)(2,1)S(1)}, u32[]{:S(2)}, u32[]{:S(2)}) collective-permute-start(bf16[256,128]{1,0:T(8,128)(2,1)S(1)} %get-tuple-element.62), channel_id=1, source_target_pairs={{0,24},{8,16},{16,8},{24,0},{1,25},{9,17},{17,9},{25,1},{2,26},{10... | collective-permute-start | bytes 196616 | tf_op jit(solution)/shard_map/ppermute | solution.py:394
  19.1 0.8 %collective-permute-start.7 = (bf16[256,128]{1,0:T(8,128)(2,1)S(1)}, bf16[256,128]{1,0:T(8,128)(2,1)S(1)}, u32[]{:S(2)}, u32[]{:S(2)}) collective-permute-start(bf16[256,128]{1,0:T(8,128)(2,1)S(1)} %get-tuple-element.64), channel_id=1, source_target_pairs={{0,8},{8,0},{16,24},{24,16},{1,9},{9,1},{17,25},{25,17},{2,10},{10... | collective-permute-start | bytes 196616 | tf_op jit(solution)/shard_map/ppermute | solution.py:394
  19.9 1.7 %collective-permute-done.5.refs_4_ = bf16[256,128]{1,0:T(8,128)(2,1)S(1)} collective-permute-done((bf16[256,128]{1,0:T(8,128)(2,1)S(1)}, bf16[256,128]{1,0:T(8,128)(2,1)S(1)}, u32[]{:S(2)}, u32[]{:S(2)}) %collective-permute-start.5) | collective-permute-done | bytes 65568 | tf_op jit(solution)/shard_map/ppermute | solution.py:394
  21.6 2.7 %collective-permute-done.6.refs_5_ = bf16[256,128]{1,0:T(8,128)(2,1)S(1)} collective-permute-done((bf16[256,128]{1,0:T(8,128)(2,1)S(1)}, bf16[256,128]{1,0:T(8,128)(2,1)S(1)}, u32[]{:S(2)}, u32[]{:S(2)}) %collective-permute-start.6) | collective-permute-done | bytes 65568 | tf_op jit(solution)/shard_map/ppermute | solution.py:394
  24.3 0.2 scan.1
  24.5 1.3 %collective-permute-start.9 = (bf16[2,256,128]{2,1,0:T(8,128)(2,1)S(1)}, bf16[2,256,128]{2,1,0:T(8,128)(2,1)S(1)}, u32[]{:S(2)}, u32[]{:S(2)}) collective-permute-start(bf16[2,256,128]{2,1,0:T(8,128)(2,1)S(1)} %get-tuple-element.66), channel_id=1, source_target_pairs={{0,2},{1,3},{2,0},{3,1},{4,6},{5,7},{6,4},{7,5},{8,10},{9,11},{10,... | collective-permute-start | bytes 393224 | tf_op jit(solution)/shard_map/ppermute | solution.py:394
  25.8 1.2 %collective-permute-start.11 = (bf16[2,256,128]{2,1,0:T(8,128)(2,1)S(1)}, bf16[2,256,128]{2,1,0:T(8,128)(2,1)S(1)}, u32[]{:S(2)}, u32[]{:S(2)}) collective-permute-start(bf16[2,256,128]{2,1,0:T(8,128)(2,1)S(1)} %get-tuple-element.67), channel_id=1, source_target_pairs={{0,4},{1,5},{2,6},{3,7},{4,0},{5,1},{6,2},{7,3},{8,12},{9,13},{10,... | collective-permute-start | bytes 393224 | tf_op jit(solution)/shard_map/ppermute | solution.py:394
  26.9 1.1 %collective-permute-start.13 = (bf16[2,256,128]{2,1,0:T(8,128)(2,1)S(1)}, bf16[2,256,128]{2,1,0:T(8,128)(2,1)S(1)}, u32[]{:S(2)}, u32[]{:S(2)}) collective-permute-start(bf16[2,256,128]{2,1,0:T(8,128)(2,1)S(1)} %get-tuple-element.68), channel_id=1, source_target_pairs={{0,6},{1,7},{2,4},{3,5},{4,2},{5,3},{6,0},{7,1},{8,14},{9,15},{10,... | collective-permute-start | bytes 393224 | tf_op jit(solution)/shard_map/ppermute | solution.py:394
  28.1 2.7 %collective-permute-done.9.slot.refs_9_ = bf16[2,256,128]{2,1,0:T(8,128)(2,1)S(1)} collective-permute-done((bf16[2,256,128]{2,1,0:T(8,128)(2,1)S(1)}, bf16[2,256,128]{2,1,0:T(8,128)(2,1)S(1)}, u32[]{:S(2)}, u32[]{:S(2)}) %collective-permute-start.9) | collective-permute-done | bytes 131104 | tf_op jit(solution)/shard_map/ppermute | solution.py:394
  31.0 0.9 %collective-permute-done.11.slot.refs_10_ = bf16[2,256,128]{2,1,0:T(8,128)(2,1)S(1)} collective-permute-done((bf16[2,256,128]{2,1,0:T(8,128)(2,1)S(1)}, bf16[2,256,128]{2,1,0:T(8,128)(2,1)S(1)}, u32[]{:S(2)}, u32[]{:S(2)}) %collective-permute-start.11) | collective-permute-done | bytes 131104 | tf_op jit(solution)/shard_map/ppermute | solution.py:394
  31.9 0.9 %collective-permute-done.13.slot.refs_11_ = bf16[2,256,128]{2,1,0:T(8,128)(2,1)S(1)} collective-permute-done((bf16[2,256,128]{2,1,0:T(8,128)(2,1)S(1)}, bf16[2,256,128]{2,1,0:T(8,128)(2,1)S(1)}, u32[]{:S(2)}, u32[]{:S(2)}) %collective-permute-start.13) | collective-permute-done | bytes 131104 | tf_op jit(solution)/shard_map/ppermute | solution.py:394
  32.9 1.4 %finish_own.1 = (bf16[128,2048]{1,0:T(8,128)(2,1)}, bf16[128,2048]{1,0:T(8,128)(2,1)}, bf16[128,2048]{1,0:T(8,128)(2,1)}, bf16[128,2048]{1,0:T(8,128)(2,1)}, bf16[1,4,128,512]{3,2,1,0:T(8,128)(2,1)S(1)}) custom-call(bf16[128,2048]{1,0:T(8,128)(2,1)S(1)} %get-tuple-element.39.refs_0_, bf16[128,2048]{1,0:T(8,128)(2,1)S(1)} %get-tuple-element.40.refs_1_, ...), custom_call_target="tpu_custom_call" | custom-call | flops 134217728 | bytes 4456448 | tf_op jit(solution)/shard_map/finish_own/pallas_call | solution.py:325
  34.3 1.6 %finish_other.1 = (bf16[128,2048]{1,0:T(8,128)(2,1)}, bf16[128,2048]{1,0:T(8,128)(2,1)}, bf16[128,2048]{1,0:T(8,128)(2,1)}, bf16[128,2048]{1,0:T(8,128)(2,1)}) custom-call(bf16[128,2048]{1,0:T(8,128)(2,1)S(1)} %get-tuple-element.39.refs_0_, ...), custom_call_target="tpu_custom_call", output_to_operand_aliasing={{0}: (13, {}), {1}: (14, {}), {2}: (15, {}), {3}: (16, {})} | custom-call | flops 134217728 | bytes 4456448 | tf_op jit(solution)/shard_map/finish_other/pallas_call | solution.py:373
  (20 shorter events, 0.6 us)
Async XLA Ops:
  2.5 1.7 %collective-permute-start = (bf16[2,512,128]{2,1,0:T(8,128)(2,1)S(1)}, bf16[2,512,128]{2,1,0:T(8,128)(2,1)S(1)}, u32[]{:S(2)}, u32[]{:S(2)}) collective-permute-start(bf16[2,512,128]{2,1,0:T(8,128)(2,1)S(1)} %get-tuple-element.44), channel_id=1, source_target_pairs={{0,1},{1,0},{2,3},{3,2},{4,5},{5,4},{6,7},{7,6},{8,9},{9,8},{10,11... | collective-permute-start | bytes 786440 | tf_op jit(solution)/shard_map/ppermute | solution.py:394
  3.3 3.9 %collective-permute-start.2 = (bf16[2,512,128]{2,1,0:T(8,128)(2,1)S(1)}, bf16[2,512,128]{2,1,0:T(8,128)(2,1)S(1)}, u32[]{:S(2)}, u32[]{:S(2)}) collective-permute-start(bf16[2,512,128]{2,1,0:T(8,128)(2,1)S(1)} %sums.3), channel_id=1, source_target_pairs={{0,1},{1,0},{2,3},{3,2},{4,5},{5,4},{6,7},{7,6},{8,9},{9,8},{10,11... | collective-permute-start | bytes 786440 | tf_op jit(solution)/shard_map/ppermute | solution.py:394
  4.2 7.0 %collective-permute-start.1 = (bf16[2,256,128]{2,1,0:T(8,128)(2,1)S(1)}, bf16[2,256,128]{2,1,0:T(8,128)(2,1)S(1)}, u32[]{:S(2)}, u32[]{:S(2)}) collective-permute-start(bf16[2,256,128]{2,1,0:T(8,128)(2,1)S(1)} %get-tuple-element.46), channel_id=1, source_target_pairs={{0,2},{1,3},{2,0},{3,1},{4,6},{5,7},{6,4},{7,5},{8,10},{9,11},{10,... | collective-permute-start | bytes 393224 | tf_op jit(solution)/shard_map/ppermute | solution.py:394
  7.2 8.1 %collective-permute-start.3 = (bf16[2,256,128]{2,1,0:T(8,128)(2,1)S(1)}, bf16[2,256,128]{2,1,0:T(8,128)(2,1)S(1)}, u32[]{:S(2)}, u32[]{:S(2)}) collective-permute-start(bf16[2,256,128]{2,1,0:T(8,128)(2,1)S(1)} %get-tuple-element.48), channel_id=1, source_target_pairs={{0,4},{1,5},{2,6},{3,7},{4,0},{5,1},{6,2},{7,3},{8,12},{9,13},{10,... | collective-permute-start | bytes 393224 | tf_op jit(solution)/shard_map/ppermute | solution.py:394
  8.8 6.6 %collective-permute-start.4 = (bf16[2,256,128]{2,1,0:T(8,128)(2,1)S(1)}, bf16[2,256,128]{2,1,0:T(8,128)(2,1)S(1)}, u32[]{:S(2)}, u32[]{:S(2)}) collective-permute-start(bf16[2,256,128]{2,1,0:T(8,128)(2,1)S(1)} %get-tuple-element.49), channel_id=1, source_target_pairs={{0,6},{1,7},{2,4},{3,5},{4,2},{5,3},{6,0},{7,1},{8,14},{9,15},{10,... | collective-permute-start | bytes 393224 | tf_op jit(solution)/shard_map/ppermute | solution.py:394
  15.4 6.1 %collective-permute-start.5 = (bf16[256,128]{1,0:T(8,128)(2,1)S(1)}, bf16[256,128]{1,0:T(8,128)(2,1)S(1)}, u32[]{:S(2)}, u32[]{:S(2)}) collective-permute-start(bf16[256,128]{1,0:T(8,128)(2,1)S(1)} %get-tuple-element.62), channel_id=1, source_target_pairs={{0,24},{8,16},{16,8},{24,0},{1,25},{9,17},{17,9},{25,1},{2,26},{10... | collective-permute-start | bytes 196616 | tf_op jit(solution)/shard_map/ppermute | solution.py:394
  19.1 5.2 %collective-permute-start.6 = (bf16[256,128]{1,0:T(8,128)(2,1)S(1)}, bf16[256,128]{1,0:T(8,128)(2,1)S(1)}, u32[]{:S(2)}, u32[]{:S(2)}) collective-permute-start(bf16[256,128]{1,0:T(8,128)(2,1)S(1)} %get-tuple-element.63), channel_id=1, source_target_pairs={{0,16},{8,24},{16,0},{24,8},{1,17},{9,25},{17,1},{25,9},{2,18},{10... | collective-permute-start | bytes 196616 | tf_op jit(solution)/shard_map/ppermute | solution.py:394
  19.1 5.2 %collective-permute-start.7 = (bf16[256,128]{1,0:T(8,128)(2,1)S(1)}, bf16[256,128]{1,0:T(8,128)(2,1)S(1)}, u32[]{:S(2)}, u32[]{:S(2)}) collective-permute-start(bf16[256,128]{1,0:T(8,128)(2,1)S(1)} %get-tuple-element.64), channel_id=1, source_target_pairs={{0,8},{8,0},{16,24},{24,16},{1,9},{9,1},{17,25},{25,17},{2,10},{10... | collective-permute-start | bytes 196616 | tf_op jit(solution)/shard_map/ppermute | solution.py:394
  24.5 6.4 %collective-permute-start.9 = (bf16[2,256,128]{2,1,0:T(8,128)(2,1)S(1)}, bf16[2,256,128]{2,1,0:T(8,128)(2,1)S(1)}, u32[]{:S(2)}, u32[]{:S(2)}) collective-permute-start(bf16[2,256,128]{2,1,0:T(8,128)(2,1)S(1)} %get-tuple-element.66), channel_id=1, source_target_pairs={{0,2},{1,3},{2,0},{3,1},{4,6},{5,7},{6,4},{7,5},{8,10},{9,11},{10,... | collective-permute-start | bytes 393224 | tf_op jit(solution)/shard_map/ppermute | solution.py:394
  25.8 6.1 %collective-permute-start.11 = (bf16[2,256,128]{2,1,0:T(8,128)(2,1)S(1)}, bf16[2,256,128]{2,1,0:T(8,128)(2,1)S(1)}, u32[]{:S(2)}, u32[]{:S(2)}) collective-permute-start(bf16[2,256,128]{2,1,0:T(8,128)(2,1)S(1)} %get-tuple-element.67), channel_id=1, source_target_pairs={{0,4},{1,5},{2,6},{3,7},{4,0},{5,1},{6,2},{7,3},{8,12},{9,13},{10,... | collective-permute-start | bytes 393224 | tf_op jit(solution)/shard_map/ppermute | solution.py:394
  26.9 5.9 %collective-permute-start.13 = (bf16[2,256,128]{2,1,0:T(8,128)(2,1)S(1)}, bf16[2,256,128]{2,1,0:T(8,128)(2,1)S(1)}, u32[]{:S(2)}, u32[]{:S(2)}) collective-permute-start(bf16[2,256,128]{2,1,0:T(8,128)(2,1)S(1)} %get-tuple-element.68), channel_id=1, source_target_pairs={{0,6},{1,7},{2,4},{3,5},{4,2},{5,3},{6,0},{7,1},{8,14},{9,15},{10,... | collective-permute-start | bytes 393224 | tf_op jit(solution)/shard_map/ppermute | solution.py:394
  28.1 6.2 %collective-permute-start.8 = (bf16[2,256,128]{2,1,0:T(8,128)(2,1)S(1)}, bf16[2,256,128]{2,1,0:T(8,128)(2,1)S(1)}, u32[]{:S(2)}, u32[]{:S(2)}) collective-permute-start(bf16[2,256,128]{2,1,0:T(8,128)(2,1)S(1)} %theirs.4), channel_id=1, source_target_pairs={{0,1},{1,0},{2,3},{3,2},{4,5},{5,4},{6,7},{7,6},{8,9},{9,8},{10,11... | collective-permute-start | bytes 393224 | tf_op jit(solution)/shard_map/ppermute | solution.py:394
  30.9 3.4 %collective-permute-start.10 = (bf16[2,256,128]{2,1,0:T(8,128)(2,1)S(1)}, bf16[2,256,128]{2,1,0:T(8,128)(2,1)S(1)}, u32[]{:S(2)}, u32[]{:S(2)}) collective-permute-start(bf16[2,256,128]{2,1,0:T(8,128)(2,1)S(1)} %theirs.5), channel_id=1, source_target_pairs={{0,1},{1,0},{2,3},{3,2},{4,5},{5,4},{6,7},{7,6},{8,9},{9,8},{10,11... | collective-permute-start | bytes 393224 | tf_op jit(solution)/shard_map/ppermute | solution.py:394
  31.9 2.5 %collective-permute-start.12 = (bf16[2,256,128]{2,1,0:T(8,128)(2,1)S(1)}, bf16[2,256,128]{2,1,0:T(8,128)(2,1)S(1)}, u32[]{:S(2)}, u32[]{:S(2)}) collective-permute-start(bf16[2,256,128]{2,1,0:T(8,128)(2,1)S(1)} %theirs.6), channel_id=1, source_target_pairs={{0,1},{1,0},{2,3},{3,2},{4,5},{5,4},{6,7},{7,6},{8,9},{9,8},{10,11... | collective-permute-start | bytes 393224 | tf_op jit(solution)/shard_map/ppermute | solution.py:394
  32.8 1.5 %collective-permute-start.14 = (bf16[2,256,128]{2,1,0:T(8,128)(2,1)S(1)}, bf16[2,256,128]{2,1,0:T(8,128)(2,1)S(1)}, u32[]{:S(2)}, u32[]{:S(2)}) collective-permute-start(bf16[2,256,128]{2,1,0:T(8,128)(2,1)S(1)} %theirs.7), channel_id=1, source_target_pairs={{0,1},{1,0},{2,3},{3,2},{4,5},{5,4},{6,7},{7,6},{8,9},{9,8},{10,11... | collective-permute-start | bytes 393224 | tf_op jit(solution)/shard_map/ppermute | solution.py:394

commit v15 on v14

--- a/solution.py
+++ b/solution.py
@@ -8,7 +8,7 @@
 from jax.sharding import PartitionSpec as P
 
 HEAD = 128
-PIECES = 2
+PIECES = 4
 MIB = 1024 * 1024
 ANY = pl.BlockSpec(memory_space=pl.ANY)
 VMEM = pl.BlockSpec(memory_space=pltpu.VMEM)
@@ -48,12 +48,29 @@
     return pl.ds(pl.multiple_of(lax.rem(far ^ s, count) * depth, depth), depth)
 
 
+def one_ahead(products, use):
+    last = None
+    for key, product in products:
+        if last:
+            use(*last)
+        last = key, product
+    use(*last)
+
+
 def sums_of(tokens, start, out):
-    for n in range(out.shape[1] // HEAD):
-        cols = columns(start, n) if not isinstance(start, int) else pl.ds(start + n * HEAD, HEAD)
-        q, k, v, d = (ref[:, cols] for ref in tokens)
-        out[0, n * HEAD : (n + 1) * HEAD] = dot(k, v, 0, 0).astype(BF16)
-        out[1, n * HEAD : (n + 1) * HEAD] = dot(q, d, 0, 0).astype(BF16)
+    q, k, v, d = tokens
+
+    def products():
+        for n in range(out.shape[1] // HEAD):
+            cols = pl.ds(start + n * HEAD, HEAD) if isinstance(start, int) else columns(start, n)
+            for which, (a, b) in enumerate(((k, v), (q, d))):
+                yield (which, n), dot(a[:, cols], b[:, cols], 0, 0)
+
+    def use(key, product):
+        which, n = key
+        out[which, n * HEAD : (n + 1) * HEAD] = product.astype(BF16)
+
+    one_ahead(products(), use)
 
 
 def load_kernel(*refs):
@@ -269,18 +286,25 @@
     )(*tokens)
 
 
-def product_piece(scale, side, p, tokens, local, states, held):
+def all_products(scale, side, tokens, local, states, store):
     half = states.shape[1]
-    piece = half // PIECES
-    for n in range(piece // HEAD):
-        at = p * piece + n * HEAD
-        rows, cols = slice(at, at + HEAD), slice(side * half + at, side * half + at + HEAD)
-        q, k, v, d = (ref[:, cols] for ref in tokens)
-        s, g = states[0, rows], states[1, rows]
-        parts = (dot(q, s, 1, 0), dot(d, s, 1, 1), dot(v, g, 1, 1), dot(k, g, 1, 0))
-        for i, part in enumerate(parts):
-            out = (scale * (part + local[i][:, cols])).astype(BF16)
-            held[i, :, n * HEAD : (n + 1) * HEAD] = out
+    q, k, v, d = tokens
+
+    def products():
+        for h in range(half // HEAD):
+            rows = slice(h * HEAD, (h + 1) * HEAD)
+            cols = slice(side * half + h * HEAD, side * half + (h + 1) * HEAD)
+            s, g = states[0, rows], states[1, rows]
+            yield (h, 0, cols), dot(q[:, cols], s, 1, 0)
+            yield (h, 1, cols), dot(d[:, cols], s, 1, 1)
+            yield (h, 2, cols), dot(v[:, cols], g, 1, 1)
+            yield (h, 3, cols), dot(k[:, cols], g, 1, 0)
+
+    def use(key, product):
+        h, i, cols = key
+        store(h, i, (scale * (product + local[i][:, cols])).astype(BF16))
+
+    one_ahead(products(), use)
 
 
 def copies_out(side, p, held, outs, sems, half):
@@ -303,14 +327,19 @@
             part = slot_rows(s, count, depth)
             states[1 - core, into] = with_sums(slot, 1 - core, got[s // count], part)
         copies = []
-        for p in range(PIECES):
+        heads = half // PIECES // HEAD
+
+        def store(h, i, out):
+            p, n = divmod(h, heads)
             late = p - PIECES // 2
             to = held.at[p] if late < 0 else rest.at[late]
-            product_piece(scale, core, p, tokens, local, states, to)
-            if late < 0:
-                copies += copies_out(core, p, to, outs, sems, half)
+            to[i, :, n * HEAD : (n + 1) * HEAD] = out
+            if late < 0 and n == heads - 1 and i == 3:
+                copies.extend(copies_out(core, p, to, outs, sems, half))
                 for copy in copies[-4:]:
                     copy.start()
+
+        all_products(scale, core, tokens, local, states, store)
         for copy in copies:
             copy.wait()
 
@@ -354,11 +383,17 @@
             copy.start()
         for s, slot in enumerate(slots):
             states[:, half_rows(s, depth)] = slot[...]
-        for p in range(PIECES):
-            product_piece(scale, 1 - core, p, tokens, local, states, held.at[p])
-            copies += copies_out(1 - core, p, held.at[p], outs, sems, half)
-            for copy in copies[-4:]:
-                copy.start()
+        heads = half // PIECES // HEAD
+
+        def store(h, i, out):
+            p, n = divmod(h, heads)
+            held[p, i, :, n * HEAD : (n + 1) * HEAD] = out
+            if n == heads - 1 and i == 3:
+                copies.extend(copies_out(1 - core, p, held.at[p], outs, sems, half))
+                for copy in copies[-4:]:
+                    copy.start()
+
+        all_products(scale, 1 - core, tokens, local, states, store)
         for copy in copies:
             copy.wait()
 

time: 36.1 us -> 36.1 us (level)
  transfers between devices with their start and end apart: 15 -> 15, of which waited for: 7 -> 7; matrix products, arithmetic and copies ran while one was open for 0% -> 0% of each run, Pallas kernels for 13% -> 12%
where the time goes in v15:
time: 36.1 us; the launch traced here: 35.9 us
  starting transfers between devices  13.7 us (38%)
  waiting for transfers between devices  13.2 us (37%)
  Pallas kernels  8.23 us (23%)
  between operations  0.79 us (2%)
    ppermute x15, starting transfers between devices, swap(): lax.ppermute(x, axis, [(i, i ^ bits) for i in range(lax.axis_size(axis))])  13.7 us
    ppermute x15, waiting for transfers between devices, swap(): lax.ppermute(x, axis, [(i, i ^ bits) for i in range(lax.axis_size(axis))])  13.2 us
    pallas_call x1, Pallas kernels, local_part(): pl.pallas_call(local_kernel, name='local', in_specs=[VMEM] * 4, out_specs...  2.16 us
    pallas_call x1, Pallas kernels, load(): pl.pallas_call(load_kernel, name='load', in_specs=[ANY] * 4, out_specs=[V...  1.82 us
    pallas_call x1, Pallas kernels, finish_other(): pl.pallas_call(functools.partial(finish_other_kernel, scale, len(slots)),...  1.63 us
    pallas_call x1, Pallas kernels, finish_own(): pl.pallas_call(functools.partial(finish_own_kernel, scale, len(slots)), n...  1.36 us
    pallas_call x2, Pallas kernels, sums(): pl.pallas_call(functools.partial(sums_kernel, wanted), name='sums', in_sp...  0.75 us
  transfers between devices with their start and end apart: 15, of which 7 were waited for; matrix products, arithmetic and copies ran while one was open for 0% of the time, Pallas kernels for 12%

profile of v15, /device:TPU:0, one launch (start us, length us, event | category | flops | bytes accessed | tf_op | source)
XLA Modules:
  0.0 35.9 jit_solution(17539864797620232460)
XLA Ops:
  0.6 1.8 %load.1 = (bf16[128,2048]{1,0:T(8,128)(2,1)S(1)}, bf16[128,2048]{1,0:T(8,128)(2,1)S(1)}, bf16[128,2048]{1,0:T(8,128)(2,1)S(1)}, bf16[128,2048]{1,0:T(8,128)(2,1)S(1)}, bf16[2,512,128]{2,1,0:T(8,128)(2,1)S(1)}) custom-call(bf16[128,2048]{1,0:T(8,128)(2,1)} %refs_0_.1, bf16[128,2048]{1,0:T(8,128)(2,1)} %refs_1_.1, bf16[128,2048]{1,0:T(8,128)(2,1)} %refs_2_.1, ...), custom_call_target="tpu_custom_call" | custom-call | flops 33554432 | bytes 2621440 | tf_op jit(solution)/shard_map/load/pallas_call | solution.py:93
  2.5 0.5 %collective-permute-start = (bf16[2,512,128]{2,1,0:T(8,128)(2,1)S(1)}, bf16[2,512,128]{2,1,0:T(8,128)(2,1)S(1)}, u32[]{:S(2)}, u32[]{:S(2)}) collective-permute-start(bf16[2,512,128]{2,1,0:T(8,128)(2,1)S(1)} %get-tuple-element.44), channel_id=1, source_target_pairs={{0,1},{1,0},{2,3},{3,2},{4,5},{5,4},{6,7},{7,6},{8,9},{9,8},{10,11... | collective-permute-start | bytes 786440 | tf_op jit(solution)/shard_map/ppermute | solution.py:429
  3.0 0.3 sums.3
  3.3 0.1 collective-permute-start.2
  3.4 0.5 %sums.2 = (bf16[2,512,128]{2,1,0:T(8,128)(2,1)S(1)}, bf16[2,512,128]{2,1,0:T(8,128)(2,1)S(1)}) custom-call(bf16[128,2048]{1,0:T(8,128)(2,1)S(1)} %get-tuple-element.39.refs_0_, bf16[128,2048]{1,0:T(8,128)(2,1)S(1)} %get-tuple-element.40.refs_1_, bf16[128,2048]{1,0:T(8,128)(2,1)S(1)} %get-tuple-element.41.refs_2_, bf16[128,2048]{1,0:T(8,128)(2,1)S(1)} %get-tuple-element.42.refs_3_), custom_call_target="tpu_custom_call" | custom-call | flops 67108864 | bytes 1572864 | tf_op jit(solution)/shard_map/sums/pallas_call | solution.py:115
  3.9 0.3 collective-permute-done.got_ref.refs_12_
  4.2 2.9 %collective-permute-start.1 = (bf16[2,256,128]{2,1,0:T(8,128)(2,1)S(1)}, bf16[2,256,128]{2,1,0:T(8,128)(2,1)S(1)}, u32[]{:S(2)}, u32[]{:S(2)}) collective-permute-start(bf16[2,256,128]{2,1,0:T(8,128)(2,1)S(1)} %get-tuple-element.46), channel_id=1, source_target_pairs={{0,2},{1,3},{2,0},{3,1},{4,6},{5,7},{6,4},{7,5},{8,10},{9,11},{10,... | collective-permute-start | bytes 393224 | tf_op jit(solution)/shard_map/ppermute | solution.py:429
  7.2 1.6 %collective-permute-start.3 = (bf16[2,256,128]{2,1,0:T(8,128)(2,1)S(1)}, bf16[2,256,128]{2,1,0:T(8,128)(2,1)S(1)}, u32[]{:S(2)}, u32[]{:S(2)}) collective-permute-start(bf16[2,256,128]{2,1,0:T(8,128)(2,1)S(1)} %get-tuple-element.48), channel_id=1, source_target_pairs={{0,4},{1,5},{2,6},{3,7},{4,0},{5,1},{6,2},{7,3},{8,12},{9,13},{10,... | collective-permute-start | bytes 393224 | tf_op jit(solution)/shard_map/ppermute | solution.py:429
  8.8 0.3 collective-permute-start.4
  9.1 2.2 %local.1 = (f32[128,2048]{1,0:T(8,128)S(1)}, f32[128,2048]{1,0:T(8,128)S(1)}, f32[128,2048]{1,0:T(8,128)S(1)}, f32[128,2048]{1,0:T(8,128)S(1)}) custom-call(bf16[128,2048]{1,0:T(8,128)(2,1)S(1)} %get-tuple-element.39.refs_0_, bf16[128,2048]{1,0:T(8,128)(2,1)S(1)} %get-tuple-element.40.refs_1_, bf16[128,2048]{1,0:T(8,128)(2,1)S(1)} %get-tuple-element.41.refs_2_, ...), custom_call_target="tpu_custom_call" | custom-call | flops 402653184 | bytes 6291456 | tf_op jit(solution)/shard_map/local/pallas_call | solution.py:276
  11.3 4.1 %collective-permute-done.3.refs_2_ = bf16[2,256,128]{2,1,0:T(8,128)(2,1)S(1)} collective-permute-done((bf16[2,256,128]{2,1,0:T(8,128)(2,1)S(1)}, bf16[2,256,128]{2,1,0:T(8,128)(2,1)S(1)}, u32[]{:S(2)}, u32[]{:S(2)}) %collective-permute-start.3) | collective-permute-done | bytes 131104 | tf_op jit(solution)/shard_map/ppermute | solution.py:429
  15.4 3.7 %collective-permute-start.5 = (bf16[256,128]{1,0:T(8,128)(2,1)S(1)}, bf16[256,128]{1,0:T(8,128)(2,1)S(1)}, u32[]{:S(2)}, u32[]{:S(2)}) collective-permute-start(bf16[256,128]{1,0:T(8,128)(2,1)S(1)} %get-tuple-element.62), channel_id=1, source_target_pairs={{0,24},{8,16},{16,8},{24,0},{1,25},{9,17},{17,9},{25,1},{2,26},{10... | collective-permute-start | bytes 196616 | tf_op jit(solution)/shard_map/ppermute | solution.py:429
  19.1 0.8 %collective-permute-start.7 = (bf16[256,128]{1,0:T(8,128)(2,1)S(1)}, bf16[256,128]{1,0:T(8,128)(2,1)S(1)}, u32[]{:S(2)}, u32[]{:S(2)}) collective-permute-start(bf16[256,128]{1,0:T(8,128)(2,1)S(1)} %get-tuple-element.64), channel_id=1, source_target_pairs={{0,8},{8,0},{16,24},{24,16},{1,9},{9,1},{17,25},{25,17},{2,10},{10... | collective-permute-start | bytes 196616 | tf_op jit(solution)/shard_map/ppermute | solution.py:429
  19.9 1.7 %collective-permute-done.5.refs_4_ = bf16[256,128]{1,0:T(8,128)(2,1)S(1)} collective-permute-done((bf16[256,128]{1,0:T(8,128)(2,1)S(1)}, bf16[256,128]{1,0:T(8,128)(2,1)S(1)}, u32[]{:S(2)}, u32[]{:S(2)}) %collective-permute-start.5) | collective-permute-done | bytes 65568 | tf_op jit(solution)/shard_map/ppermute | solution.py:429
  21.6 2.7 %collective-permute-done.6.refs_5_ = bf16[256,128]{1,0:T(8,128)(2,1)S(1)} collective-permute-done((bf16[256,128]{1,0:T(8,128)(2,1)S(1)}, bf16[256,128]{1,0:T(8,128)(2,1)S(1)}, u32[]{:S(2)}, u32[]{:S(2)}) %collective-permute-start.6) | collective-permute-done | bytes 65568 | tf_op jit(solution)/shard_map/ppermute | solution.py:429
  24.3 0.2 scan.1
  24.5 1.3 %collective-permute-start.9 = (bf16[2,256,128]{2,1,0:T(8,128)(2,1)S(1)}, bf16[2,256,128]{2,1,0:T(8,128)(2,1)S(1)}, u32[]{:S(2)}, u32[]{:S(2)}) collective-permute-start(bf16[2,256,128]{2,1,0:T(8,128)(2,1)S(1)} %get-tuple-element.66), channel_id=1, source_target_pairs={{0,2},{1,3},{2,0},{3,1},{4,6},{5,7},{6,4},{7,5},{8,10},{9,11},{10,... | collective-permute-start | bytes 393224 | tf_op jit(solution)/shard_map/ppermute | solution.py:429
  25.8 1.2 %collective-permute-start.11 = (bf16[2,256,128]{2,1,0:T(8,128)(2,1)S(1)}, bf16[2,256,128]{2,1,0:T(8,128)(2,1)S(1)}, u32[]{:S(2)}, u32[]{:S(2)}) collective-permute-start(bf16[2,256,128]{2,1,0:T(8,128)(2,1)S(1)} %get-tuple-element.67), channel_id=1, source_target_pairs={{0,4},{1,5},{2,6},{3,7},{4,0},{5,1},{6,2},{7,3},{8,12},{9,13},{10,... | collective-permute-start | bytes 393224 | tf_op jit(solution)/shard_map/ppermute | solution.py:429
  26.9 1.1 %collective-permute-start.13 = (bf16[2,256,128]{2,1,0:T(8,128)(2,1)S(1)}, bf16[2,256,128]{2,1,0:T(8,128)(2,1)S(1)}, u32[]{:S(2)}, u32[]{:S(2)}) collective-permute-start(bf16[2,256,128]{2,1,0:T(8,128)(2,1)S(1)} %get-tuple-element.68), channel_id=1, source_target_pairs={{0,6},{1,7},{2,4},{3,5},{4,2},{5,3},{6,0},{7,1},{8,14},{9,15},{10,... | collective-permute-start | bytes 393224 | tf_op jit(solution)/shard_map/ppermute | solution.py:429
  28.1 2.7 %collective-permute-done.9.slot.refs_9_ = bf16[2,256,128]{2,1,0:T(8,128)(2,1)S(1)} collective-permute-done((bf16[2,256,128]{2,1,0:T(8,128)(2,1)S(1)}, bf16[2,256,128]{2,1,0:T(8,128)(2,1)S(1)}, u32[]{:S(2)}, u32[]{:S(2)}) %collective-permute-start.9) | collective-permute-done | bytes 131104 | tf_op jit(solution)/shard_map/ppermute | solution.py:429
  31.0 0.9 %collective-permute-done.11.slot.refs_10_ = bf16[2,256,128]{2,1,0:T(8,128)(2,1)S(1)} collective-permute-done((bf16[2,256,128]{2,1,0:T(8,128)(2,1)S(1)}, bf16[2,256,128]{2,1,0:T(8,128)(2,1)S(1)}, u32[]{:S(2)}, u32[]{:S(2)}) %collective-permute-start.11) | collective-permute-done | bytes 131104 | tf_op jit(solution)/shard_map/ppermute | solution.py:429
  31.9 0.9 %collective-permute-done.13.slot.refs_11_ = bf16[2,256,128]{2,1,0:T(8,128)(2,1)S(1)} collective-permute-done((bf16[2,256,128]{2,1,0:T(8,128)(2,1)S(1)}, bf16[2,256,128]{2,1,0:T(8,128)(2,1)S(1)}, u32[]{:S(2)}, u32[]{:S(2)}) %collective-permute-start.13) | collective-permute-done | bytes 131104 | tf_op jit(solution)/shard_map/ppermute | solution.py:429
  32.9 1.4 %finish_own.1 = (bf16[128,2048]{1,0:T(8,128)(2,1)}, bf16[128,2048]{1,0:T(8,128)(2,1)}, bf16[128,2048]{1,0:T(8,128)(2,1)}, bf16[128,2048]{1,0:T(8,128)(2,1)}, bf16[2,4,128,256]{3,2,1,0:T(8,128)(2,1)S(1)}) custom-call(bf16[128,2048]{1,0:T(8,128)(2,1)S(1)} %get-tuple-element.39.refs_0_, bf16[128,2048]{1,0:T(8,128)(2,1)S(1)} %get-tuple-element.40.refs_1_, ...), custom_call_target="tpu_custom_call" | custom-call | flops 134217728 | bytes 4456448 | tf_op jit(solution)/shard_map/finish_own/pallas_call | solution.py:354
  34.3 1.6 %finish_other.1 = (bf16[128,2048]{1,0:T(8,128)(2,1)}, bf16[128,2048]{1,0:T(8,128)(2,1)}, bf16[128,2048]{1,0:T(8,128)(2,1)}, bf16[128,2048]{1,0:T(8,128)(2,1)}) custom-call(bf16[128,2048]{1,0:T(8,128)(2,1)S(1)} %get-tuple-element.39.refs_0_, ...), custom_call_target="tpu_custom_call", output_to_operand_aliasing={{0}: (13, {}), {1}: (14, {}), {2}: (15, {}), {3}: (16, {})} | custom-call | flops 134217728 | bytes 4456448 | tf_op jit(solution)/shard_map/finish_other/pallas_call | solution.py:408
  (20 shorter events, 0.6 us)
Async XLA Ops:
  2.5 1.7 %collective-permute-start = (bf16[2,512,128]{2,1,0:T(8,128)(2,1)S(1)}, bf16[2,512,128]{2,1,0:T(8,128)(2,1)S(1)}, u32[]{:S(2)}, u32[]{:S(2)}) collective-permute-start(bf16[2,512,128]{2,1,0:T(8,128)(2,1)S(1)} %get-tuple-element.44), channel_id=1, source_target_pairs={{0,1},{1,0},{2,3},{3,2},{4,5},{5,4},{6,7},{7,6},{8,9},{9,8},{10,11... | collective-permute-start | bytes 786440 | tf_op jit(solution)/shard_map/ppermute | solution.py:429
  3.3 3.9 %collective-permute-start.2 = (bf16[2,512,128]{2,1,0:T(8,128)(2,1)S(1)}, bf16[2,512,128]{2,1,0:T(8,128)(2,1)S(1)}, u32[]{:S(2)}, u32[]{:S(2)}) collective-permute-start(bf16[2,512,128]{2,1,0:T(8,128)(2,1)S(1)} %sums.3), channel_id=1, source_target_pairs={{0,1},{1,0},{2,3},{3,2},{4,5},{5,4},{6,7},{7,6},{8,9},{9,8},{10,11... | collective-permute-start | bytes 786440 | tf_op jit(solution)/shard_map/ppermute | solution.py:429
  4.2 7.0 %collective-permute-start.1 = (bf16[2,256,128]{2,1,0:T(8,128)(2,1)S(1)}, bf16[2,256,128]{2,1,0:T(8,128)(2,1)S(1)}, u32[]{:S(2)}, u32[]{:S(2)}) collective-permute-start(bf16[2,256,128]{2,1,0:T(8,128)(2,1)S(1)} %get-tuple-element.46), channel_id=1, source_target_pairs={{0,2},{1,3},{2,0},{3,1},{4,6},{5,7},{6,4},{7,5},{8,10},{9,11},{10,... | collective-permute-start | bytes 393224 | tf_op jit(solution)/shard_map/ppermute | solution.py:429
  7.2 8.1 %collective-permute-start.3 = (bf16[2,256,128]{2,1,0:T(8,128)(2,1)S(1)}, bf16[2,256,128]{2,1,0:T(8,128)(2,1)S(1)}, u32[]{:S(2)}, u32[]{:S(2)}) collective-permute-start(bf16[2,256,128]{2,1,0:T(8,128)(2,1)S(1)} %get-tuple-element.48), channel_id=1, source_target_pairs={{0,4},{1,5},{2,6},{3,7},{4,0},{5,1},{6,2},{7,3},{8,12},{9,13},{10,... | collective-permute-start | bytes 393224 | tf_op jit(solution)/shard_map/ppermute | solution.py:429
  8.8 6.6 %collective-permute-start.4 = (bf16[2,256,128]{2,1,0:T(8,128)(2,1)S(1)}, bf16[2,256,128]{2,1,0:T(8,128)(2,1)S(1)}, u32[]{:S(2)}, u32[]{:S(2)}) collective-permute-start(bf16[2,256,128]{2,1,0:T(8,128)(2,1)S(1)} %get-tuple-element.49), channel_id=1, source_target_pairs={{0,6},{1,7},{2,4},{3,5},{4,2},{5,3},{6,0},{7,1},{8,14},{9,15},{10,... | collective-permute-start | bytes 393224 | tf_op jit(solution)/shard_map/ppermute | solution.py:429
  15.4 6.1 %collective-permute-start.5 = (bf16[256,128]{1,0:T(8,128)(2,1)S(1)}, bf16[256,128]{1,0:T(8,128)(2,1)S(1)}, u32[]{:S(2)}, u32[]{:S(2)}) collective-permute-start(bf16[256,128]{1,0:T(8,128)(2,1)S(1)} %get-tuple-element.62), channel_id=1, source_target_pairs={{0,24},{8,16},{16,8},{24,0},{1,25},{9,17},{17,9},{25,1},{2,26},{10... | collective-permute-start | bytes 196616 | tf_op jit(solution)/shard_map/ppermute | solution.py:429
  19.1 5.2 %collective-permute-start.6 = (bf16[256,128]{1,0:T(8,128)(2,1)S(1)}, bf16[256,128]{1,0:T(8,128)(2,1)S(1)}, u32[]{:S(2)}, u32[]{:S(2)}) collective-permute-start(bf16[256,128]{1,0:T(8,128)(2,1)S(1)} %get-tuple-element.63), channel_id=1, source_target_pairs={{0,16},{8,24},{16,0},{24,8},{1,17},{9,25},{17,1},{25,9},{2,18},{10... | collective-permute-start | bytes 196616 | tf_op jit(solution)/shard_map/ppermute | solution.py:429
  19.1 5.2 %collective-permute-start.7 = (bf16[256,128]{1,0:T(8,128)(2,1)S(1)}, bf16[256,128]{1,0:T(8,128)(2,1)S(1)}, u32[]{:S(2)}, u32[]{:S(2)}) collective-permute-start(bf16[256,128]{1,0:T(8,128)(2,1)S(1)} %get-tuple-element.64), channel_id=1, source_target_pairs={{0,8},{8,0},{16,24},{24,16},{1,9},{9,1},{17,25},{25,17},{2,10},{10... | collective-permute-start | bytes 196616 | tf_op jit(solution)/shard_map/ppermute | solution.py:429
  24.5 6.4 %collective-permute-start.9 = (bf16[2,256,128]{2,1,0:T(8,128)(2,1)S(1)}, bf16[2,256,128]{2,1,0:T(8,128)(2,1)S(1)}, u32[]{:S(2)}, u32[]{:S(2)}) collective-permute-start(bf16[2,256,128]{2,1,0:T(8,128)(2,1)S(1)} %get-tuple-element.66), channel_id=1, source_target_pairs={{0,2},{1,3},{2,0},{3,1},{4,6},{5,7},{6,4},{7,5},{8,10},{9,11},{10,... | collective-permute-start | bytes 393224 | tf_op jit(solution)/shard_map/ppermute | solution.py:429
  25.8 6.1 %collective-permute-start.11 = (bf16[2,256,128]{2,1,0:T(8,128)(2,1)S(1)}, bf16[2,256,128]{2,1,0:T(8,128)(2,1)S(1)}, u32[]{:S(2)}, u32[]{:S(2)}) collective-permute-start(bf16[2,256,128]{2,1,0:T(8,128)(2,1)S(1)} %get-tuple-element.67), channel_id=1, source_target_pairs={{0,4},{1,5},{2,6},{3,7},{4,0},{5,1},{6,2},{7,3},{8,12},{9,13},{10,... | collective-permute-start | bytes 393224 | tf_op jit(solution)/shard_map/ppermute | solution.py:429
  26.9 5.9 %collective-permute-start.13 = (bf16[2,256,128]{2,1,0:T(8,128)(2,1)S(1)}, bf16[2,256,128]{2,1,0:T(8,128)(2,1)S(1)}, u32[]{:S(2)}, u32[]{:S(2)}) collective-permute-start(bf16[2,256,128]{2,1,0:T(8,128)(2,1)S(1)} %get-tuple-element.68), channel_id=1, source_target_pairs={{0,6},{1,7},{2,4},{3,5},{4,2},{5,3},{6,0},{7,1},{8,14},{9,15},{10,... | collective-permute-start | bytes 393224 | tf_op jit(solution)/shard_map/ppermute | solution.py:429
  28.1 6.2 %collective-permute-start.8 = (bf16[2,256,128]{2,1,0:T(8,128)(2,1)S(1)}, bf16[2,256,128]{2,1,0:T(8,128)(2,1)S(1)}, u32[]{:S(2)}, u32[]{:S(2)}) collective-permute-start(bf16[2,256,128]{2,1,0:T(8,128)(2,1)S(1)} %theirs.4), channel_id=1, source_target_pairs={{0,1},{1,0},{2,3},{3,2},{4,5},{5,4},{6,7},{7,6},{8,9},{9,8},{10,11... | collective-permute-start | bytes 393224 | tf_op jit(solution)/shard_map/ppermute | solution.py:429
  30.9 3.4 %collective-permute-start.10 = (bf16[2,256,128]{2,1,0:T(8,128)(2,1)S(1)}, bf16[2,256,128]{2,1,0:T(8,128)(2,1)S(1)}, u32[]{:S(2)}, u32[]{:S(2)}) collective-permute-start(bf16[2,256,128]{2,1,0:T(8,128)(2,1)S(1)} %theirs.5), channel_id=1, source_target_pairs={{0,1},{1,0},{2,3},{3,2},{4,5},{5,4},{6,7},{7,6},{8,9},{9,8},{10,11... | collective-permute-start | bytes 393224 | tf_op jit(solution)/shard_map/ppermute | solution.py:429
  31.9 2.4 %collective-permute-start.12 = (bf16[2,256,128]{2,1,0:T(8,128)(2,1)S(1)}, bf16[2,256,128]{2,1,0:T(8,128)(2,1)S(1)}, u32[]{:S(2)}, u32[]{:S(2)}) collective-permute-start(bf16[2,256,128]{2,1,0:T(8,128)(2,1)S(1)} %theirs.6), channel_id=1, source_target_pairs={{0,1},{1,0},{2,3},{3,2},{4,5},{5,4},{6,7},{7,6},{8,9},{9,8},{10,11... | collective-permute-start | bytes 393224 | tf_op jit(solution)/shard_map/ppermute | solution.py:429
  32.8 1.5 %collective-permute-start.14 = (bf16[2,256,128]{2,1,0:T(8,128)(2,1)S(1)}, bf16[2,256,128]{2,1,0:T(8,128)(2,1)S(1)}, u32[]{:S(2)}, u32[]{:S(2)}) collective-permute-start(bf16[2,256,128]{2,1,0:T(8,128)(2,1)S(1)} %theirs.7), channel_id=1, source_target_pairs={{0,1},{1,0},{2,3},{3,2},{4,5},{5,4},{6,7},{7,6},{8,9},{9,8},{10,11... | collective-permute-start | bytes 393224 | tf_op jit(solution)/shard_map/ppermute | solution.py:429

commit v16 on v15

--- a/solution.py
+++ b/solution.py
@@ -8,7 +8,6 @@
 from jax.sharding import PartitionSpec as P
 
 HEAD = 128
-PIECES = 4
 MIB = 1024 * 1024
 ANY = pl.BlockSpec(memory_space=pl.ANY)
 VMEM = pl.BlockSpec(memory_space=pltpu.VMEM)
@@ -210,11 +209,6 @@
     return (slot[which].astype(F32) + extra[which, part].astype(F32)).astype(BF16)
 
 
-def half_rows(s, depth):
-    _, far = near_far()
-    return pl.ds(pl.multiple_of((far ^ s) * depth, depth), depth)
-
-
 def by_core(run):
     near, _ = near_far()
     for core in range(2):
@@ -286,140 +280,95 @@
     )(*tokens)
 
 
-def all_products(scale, side, tokens, local, states, store):
-    half = states.shape[1]
+def all_products(scale, start, tokens, local, states, store):
     q, k, v, d = tokens
 
     def products():
-        for h in range(half // HEAD):
-            rows = slice(h * HEAD, (h + 1) * HEAD)
-            cols = slice(side * half + h * HEAD, side * half + (h + 1) * HEAD)
+        for n in range(states.shape[1] // HEAD):
+            rows = slice(n * HEAD, (n + 1) * HEAD)
+            cols = slice(start + n * HEAD, start + (n + 1) * HEAD)
             s, g = states[0, rows], states[1, rows]
-            yield (h, 0, cols), dot(q[:, cols], s, 1, 0)
-            yield (h, 1, cols), dot(d[:, cols], s, 1, 1)
-            yield (h, 2, cols), dot(v[:, cols], g, 1, 1)
-            yield (h, 3, cols), dot(k[:, cols], g, 1, 0)
+            yield (rows, 0, cols), dot(q[:, cols], s, 1, 0)
+            yield (rows, 1, cols), dot(d[:, cols], s, 1, 1)
+            yield (rows, 2, cols), dot(v[:, cols], g, 1, 1)
+            yield (rows, 3, cols), dot(k[:, cols], g, 1, 0)
 
     def use(key, product):
-        h, i, cols = key
-        store(h, i, (scale * (product + local[i][:, cols])).astype(BF16))
+        rows, i, cols = key
+        store(rows, i, (scale * (product + local[i][:, cols])).astype(BF16))
 
     one_ahead(products(), use)
 
 
-def copies_out(side, p, held, outs, sems, half):
-    there = pl.ds(side * half + p * half // PIECES, half // PIECES)
+def copies_out(own, block, held, outs, sems):
+    size = held.shape[2]
+    start = block_start(own, block, outs[0].shape[1] // 2)
+    there = pl.ds(pl.multiple_of(start, size), size)
     return [
-        pltpu.make_async_copy(held.at[i], out.at[:, there], sems.at[i, p])
+        pltpu.make_async_copy(held.at[i], out.at[:, there], sems.at[i])
         for i, out in enumerate(outs)
     ]
 
 
-def finish_own_kernel(scale, slot_count, *refs):
-    tokens, local, slots, refs = refs[:4], refs[4:8], refs[8 : 8 + slot_count], refs[8 + slot_count :]
-    got, outs, (rest, states, held, sems) = refs[:2], refs[2:6], refs[6:]
-    count, depth, half = slot_count // 2, slots[0].shape[1], states.shape[1]
-
-    def run(core):
+def finish_kernel(scale, own, block, count, rests, hold, *refs):
+    tokens, local, slots, refs = refs[:4], refs[4:8], refs[8 : 8 + count], refs[8 + count :]
+    got, refs = (refs[0], refs[1:]) if own else (None, refs)
+    late, refs = refs[: len(rests)], refs[len(rests) :]
+    if hold:
+        held, states = refs
+    else:
+        outs, (states, held, sems) = refs[-7:-3], refs[-3:]
+    width, depth = tokens[0].shape[1], slots[0].shape[1]
+    copies = []
+    for n, (rest, where) in enumerate(zip(late, rests)):
+        copies += copies_out(*where, rest, outs, sems.at[n + 1])
+    for copy in copies:
+        copy.start()
+
+    def store(rows, i, out):
+        held[i, :, rows] = out
+
+    def run(quarter):
+        start = quarter * width // 4
+        core = quarter // 2 if own else 1 - quarter // 2
         for s, slot in enumerate(slots):
-            into = half_rows(s, depth)
-            states[core, into] = slot[core]
             part = slot_rows(s, count, depth)
-            states[1 - core, into] = with_sums(slot, 1 - core, got[s // count], part)
-        copies = []
-        heads = half // PIECES // HEAD
-
-        def store(h, i, out):
-            p, n = divmod(h, heads)
-            late = p - PIECES // 2
-            to = held.at[p] if late < 0 else rest.at[late]
-            to[i, :, n * HEAD : (n + 1) * HEAD] = out
-            if late < 0 and n == heads - 1 and i == 3:
-                copies.extend(copies_out(core, p, to, outs, sems, half))
-                for copy in copies[-4:]:
-                    copy.start()
-
-        all_products(scale, core, tokens, local, states, store)
-        for copy in copies:
+            if own:
+                states[core, part] = slot[core]
+                states[1 - core, part] = with_sums(slot, 1 - core, got, part)
+            else:
+                states[:, part] = slot[...]
+        all_products(scale, start, tokens, local, states, store)
+
+    start = block_start(own, block, width // 2)
+    for quarter in range(4):
+        pl.when(start == quarter * width // 4)(functools.partial(run, quarter))
+    if not hold:
+        last = copies_out(own, block, held, outs, sems.at[0])
+        for copy in last:
+            copy.start()
+        for copy in copies + last:
             copy.wait()
 
-    by_core(run)
-
-
-def finish_own(tokens, local, slots, got, scale):
+
+def finish(own, block, tokens, local, slots, scale, got=(), rests=(), before=(), hold=False):
     rows, width = tokens[0].shape
-    half = width // 2
     out = jax.ShapeDtypeStruct((rows, width), BF16)
-    pieces = (PIECES // 2, 4, rows, half // PIECES)
-    *outs, rest = pl.pallas_call(
-        functools.partial(finish_own_kernel, scale, len(slots)),
-        name="finish_own",
-        in_specs=[VMEM] * (10 + len(slots)),
-        out_specs=[ANY] * 4 + [VMEM],
-        out_shape=[out] * 4 + [pltpu.VMEM(pieces, BF16)],
-        scratch_shapes=[
-            pltpu.VMEM((2, half, HEAD), BF16),
-            pltpu.VMEM(pieces, BF16),
-            pltpu.SemaphoreType.DMA((4, PIECES)),
-        ],
+    piece = pltpu.VMEM((4, rows, width // 4), BF16)
+    inputs = [*tokens, *local, *slots, *got, *(x for _, x in rests)]
+    states = pltpu.VMEM((2, width // 4, HEAD), BF16)
+    wheres = [where for where, _ in rests]
+    return pl.pallas_call(
+        functools.partial(finish_kernel, scale, own, block, len(slots), wheres, hold),
+        name="finish",
+        in_specs=[VMEM] * len(inputs) + [ANY] * len(before),
+        out_specs=VMEM if hold else [ANY] * 4,
+        out_shape=piece if hold else [out] * 4,
+        scratch_shapes=[states]
+        + ([] if hold else [piece, pltpu.SemaphoreType.DMA((1 + len(rests), 4))]),
+        input_output_aliases={len(inputs) + i: i for i in range(len(before))},
         cost_estimate=pl.CostEstimate(
-            flops=4 * rows * width * HEAD, bytes_accessed=17 * rows * width, transcendentals=0
-        ),
-        compiler_params=SMALL,
-    )(*tokens, *local, *slots, *got)
-    return outs, rest
-
-
-def finish_other_kernel(scale, slot_count, *refs):
-    tokens, local, slots, refs = refs[:4], refs[4:8], refs[8 : 8 + slot_count], refs[8 + slot_count :]
-    rest, outs, (states, held, sems, rest_sems) = refs[0], refs[5:9], refs[9:]
-    depth, half = slots[0].shape[1], states.shape[1]
-
-    def run(core):
-        copies = []
-        for late in range(PIECES // 2):
-            copies += copies_out(core, PIECES // 2 + late, rest.at[late], outs, rest_sems, half)
-        for copy in copies:
-            copy.start()
-        for s, slot in enumerate(slots):
-            states[:, half_rows(s, depth)] = slot[...]
-        heads = half // PIECES // HEAD
-
-        def store(h, i, out):
-            p, n = divmod(h, heads)
-            held[p, i, :, n * HEAD : (n + 1) * HEAD] = out
-            if n == heads - 1 and i == 3:
-                copies.extend(copies_out(1 - core, p, held.at[p], outs, sems, half))
-                for copy in copies[-4:]:
-                    copy.start()
-
-        all_products(scale, 1 - core, tokens, local, states, store)
-        for copy in copies:
-            copy.wait()
-
-    by_core(run)
-
-
-def finish_other(tokens, local, slots, rest, scale, before):
-    rows, width = tokens[0].shape
-    half = width // 2
-    out = jax.ShapeDtypeStruct((rows, width), BF16)
-    inputs = [*tokens, *local, *slots, rest]
-    return pl.pallas_call(
-        functools.partial(finish_other_kernel, scale, len(slots)),
-        name="finish_other",
-        in_specs=[VMEM] * len(inputs) + [ANY] * 4,
-        out_specs=[ANY] * 4,
-        out_shape=[out] * 4,
-        scratch_shapes=[
-            pltpu.VMEM((2, half, HEAD), BF16),
-            pltpu.VMEM((PIECES, 4, rows, half // PIECES), BF16),
-            pltpu.SemaphoreType.DMA((4, PIECES)),
-            pltpu.SemaphoreType.DMA((4, PIECES)),
-        ],
-        input_output_aliases={len(inputs) + i: i for i in range(4)},
-        cost_estimate=pl.CostEstimate(
-            flops=4 * rows * width * HEAD, bytes_accessed=17 * rows * width, transcendentals=0
+            flops=2 * rows * width * HEAD, bytes_accessed=8 * rows * width, transcendentals=0
         ),
         compiler_params=SMALL,
     )(*inputs, *before)
@@ -445,10 +394,21 @@
     sends = group_sends(slots, outer_count)
     others = [swap(send, "outer", s) for s, send in zip(distances(outer_count), sends)]
     slots = swap_far(scan_slots(slots, others))
-    theirs = [state_for_neighbour(s, far_count // 2, slot, keep) for s, slot in enumerate(slots)]
-    arrived = [swap(x, "inner", 1) for x in theirs]
-    outs, rest = finish_own(tokens, local, slots, got, scale)
-    return tuple(finish_other(tokens, local, arrived, rest, scale, outs))
+    half = far_count // 2
+    arrived, outs, rests = [], (), []
+    for block in range(2):
+        part = slots[block * half : (block + 1) * half]
+        if block:
+            part, outs = lax.optimization_barrier((part, tuple(outs)))
+        for s, slot in enumerate(part):
+            theirs = state_for_neighbour(block * half + s, half, slot, keep)
+            arrived.append(swap(theirs, "inner", 1))
+        made = finish(True, block, tokens, local, part, scale, got=got[block : block + 1], hold=block)
+        outs = outs or made
+    rests.append(((True, 1), made))
+    made = finish(False, 0, tokens, local, arrived[:half], scale, hold=True)
+    rests.append(((False, 0), made))
+    return tuple(finish(False, 1, tokens, local, arrived[half:], scale, rests=rests, before=outs))
 
 
 def solution(mesh):

time: 36.1 us -> 35.9 us (level)
  waiting for transfers between devices: 13.2 us -> 12.2 us
  starting transfers between devices: 13.7 us -> 14.2 us
    ppermute x15, waiting for transfers between devices: 13.2 us -> 12.2 us  [swap(): lax.ppermute(x, axis, [(i, i ^ bits) for i in range(lax.axis_size(axis))])]
    ppermute x15, starting transfers between devices: 13.7 us -> 14.2 us  [swap(): lax.ppermute(x, axis, [(i, i ^ bits) for i in range(lax.axis_size(axis))])]
    pallas_call x2 -> x4, Pallas kernels: 2.99 us -> 3.33 us  [finish(): pl.pallas_call(functools.partial(finish_kernel, scale, own, block, len(sl...]
  transfers between devices with their start and end apart: 15 -> 15, of which waited for: 7 -> 7; matrix products, arithmetic and copies ran while one was open for 0% -> 0% of each run, Pallas kernels for 12% -> 15%
where the time goes in v16:
time: 35.9 us; the launch traced here: 35.7 us
  starting transfers between devices  14.2 us (40%)
  waiting for transfers between devices  12.2 us (34%)
  Pallas kernels  8.59 us (24%)
  between operations  0.8 us (2%)
    ppermute x15, starting transfers between devices, swap(): lax.ppermute(x, axis, [(i, i ^ bits) for i in range(lax.axis_size(axis))])  14.2 us
    ppermute x15, waiting for transfers between devices, swap(): lax.ppermute(x, axis, [(i, i ^ bits) for i in range(lax.axis_size(axis))])  12.2 us
    pallas_call x4, Pallas kernels, finish(): pl.pallas_call(functools.partial(finish_kernel, scale, own, block, len(sl...  3.33 us
    pallas_call x1, Pallas kernels, local_part(): pl.pallas_call(local_kernel, name='local', in_specs=[VMEM] * 4, out_specs...  2.16 us
    pallas_call x1, Pallas kernels, load(): pl.pallas_call(load_kernel, name='load', in_specs=[ANY] * 4, out_specs=[V...  1.82 us
    pallas_call x2, Pallas kernels, sums(): pl.pallas_call(functools.partial(sums_kernel, wanted), name='sums', in_sp...  0.75 us
  transfers between devices with their start and end apart: 15, of which 7 were waited for; matrix products, arithmetic and copies ran while one was open for 0% of the time, Pallas kernels for 15%

profile of v16, /device:TPU:0, one launch (start us, length us, event | category | flops | bytes accessed | tf_op | source)
XLA Modules:
  0.0 35.7 jit_solution(2795356245081378678)
XLA Ops:
  0.6 1.8 %load.1 = (bf16[128,2048]{1,0:T(8,128)(2,1)S(1)}, bf16[128,2048]{1,0:T(8,128)(2,1)S(1)}, bf16[128,2048]{1,0:T(8,128)(2,1)S(1)}, bf16[128,2048]{1,0:T(8,128)(2,1)S(1)}, bf16[2,512,128]{2,1,0:T(8,128)(2,1)S(1)}) custom-call(bf16[128,2048]{1,0:T(8,128)(2,1)} %refs_0_.1, bf16[128,2048]{1,0:T(8,128)(2,1)} %refs_1_.1, bf16[128,2048]{1,0:T(8,128)(2,1)} %refs_2_.1, ...), custom_call_target="tpu_custom_call" | custom-call | flops 33554432 | bytes 2621440 | tf_op jit(solution)/shard_map/load/pallas_call | solution.py:92
  2.5 0.5 %collective-permute-start = (bf16[2,512,128]{2,1,0:T(8,128)(2,1)S(1)}, bf16[2,512,128]{2,1,0:T(8,128)(2,1)S(1)}, u32[]{:S(2)}, u32[]{:S(2)}) collective-permute-start(bf16[2,512,128]{2,1,0:T(8,128)(2,1)S(1)} %get-tuple-element.49), channel_id=1, source_target_pairs={{0,1},{1,0},{2,3},{3,2},{4,5},{5,4},{6,7},{7,6},{8,9},{9,8},{10,11... | collective-permute-start | bytes 786440 | tf_op jit(solution)/shard_map/ppermute | solution.py:378
  3.0 0.3 sums.3
  3.4 0.5 %sums.2 = (bf16[2,512,128]{2,1,0:T(8,128)(2,1)S(1)}, bf16[2,512,128]{2,1,0:T(8,128)(2,1)S(1)}) custom-call(bf16[128,2048]{1,0:T(8,128)(2,1)S(1)} %get-tuple-element.44.refs_0_, bf16[128,2048]{1,0:T(8,128)(2,1)S(1)} %get-tuple-element.45.refs_1_, bf16[128,2048]{1,0:T(8,128)(2,1)S(1)} %get-tuple-element.46.refs_2_, bf16[128,2048]{1,0:T(8,128)(2,1)S(1)} %get-tuple-element.47.refs_3_), custom_call_target="tpu_custom_call" | custom-call | flops 67108864 | bytes 1572864 | tf_op jit(solution)/shard_map/sums/pallas_call | solution.py:114
  3.9 0.3 collective-permute-done.got_ref.refs_10_
  4.2 2.9 %collective-permute-start.1 = (bf16[2,256,128]{2,1,0:T(8,128)(2,1)S(1)}, bf16[2,256,128]{2,1,0:T(8,128)(2,1)S(1)}, u32[]{:S(2)}, u32[]{:S(2)}) collective-permute-start(bf16[2,256,128]{2,1,0:T(8,128)(2,1)S(1)} %get-tuple-element.51), channel_id=1, source_target_pairs={{0,2},{1,3},{2,0},{3,1},{4,6},{5,7},{6,4},{7,5},{8,10},{9,11},{10,... | collective-permute-start | bytes 393224 | tf_op jit(solution)/shard_map/ppermute | solution.py:378
  7.2 1.6 %collective-permute-start.3 = (bf16[2,256,128]{2,1,0:T(8,128)(2,1)S(1)}, bf16[2,256,128]{2,1,0:T(8,128)(2,1)S(1)}, u32[]{:S(2)}, u32[]{:S(2)}) collective-permute-start(bf16[2,256,128]{2,1,0:T(8,128)(2,1)S(1)} %get-tuple-element.53), channel_id=1, source_target_pairs={{0,4},{1,5},{2,6},{3,7},{4,0},{5,1},{6,2},{7,3},{8,12},{9,13},{10,... | collective-permute-start | bytes 393224 | tf_op jit(solution)/shard_map/ppermute | solution.py:378
  8.8 0.3 collective-permute-start.4
  9.1 2.2 %local.1 = (f32[128,2048]{1,0:T(8,128)S(1)}, f32[128,2048]{1,0:T(8,128)S(1)}, f32[128,2048]{1,0:T(8,128)S(1)}, f32[128,2048]{1,0:T(8,128)S(1)}) custom-call(bf16[128,2048]{1,0:T(8,128)(2,1)S(1)} %get-tuple-element.44.refs_0_, bf16[128,2048]{1,0:T(8,128)(2,1)S(1)} %get-tuple-element.45.refs_1_, bf16[128,2048]{1,0:T(8,128)(2,1)S(1)} %get-tuple-element.46.refs_2_, ...), custom_call_target="tpu_custom_call" | custom-call | flops 402653184 | bytes 6291456 | tf_op jit(solution)/shard_map/local/pallas_call | solution.py:270
  11.3 4.1 %collective-permute-done.3.refs_2_ = bf16[2,256,128]{2,1,0:T(8,128)(2,1)S(1)} collective-permute-done((bf16[2,256,128]{2,1,0:T(8,128)(2,1)S(1)}, bf16[2,256,128]{2,1,0:T(8,128)(2,1)S(1)}, u32[]{:S(2)}, u32[]{:S(2)}) %collective-permute-start.3) | collective-permute-done | bytes 131104 | tf_op jit(solution)/shard_map/ppermute | solution.py:378
  15.4 3.7 %collective-permute-start.5 = (bf16[256,128]{1,0:T(8,128)(2,1)S(1)}, bf16[256,128]{1,0:T(8,128)(2,1)S(1)}, u32[]{:S(2)}, u32[]{:S(2)}) collective-permute-start(bf16[256,128]{1,0:T(8,128)(2,1)S(1)} %get-tuple-element.67), channel_id=1, source_target_pairs={{0,24},{8,16},{16,8},{24,0},{1,25},{9,17},{17,9},{25,1},{2,26},{10... | collective-permute-start | bytes 196616 | tf_op jit(solution)/shard_map/ppermute | solution.py:378
  19.1 0.8 %collective-permute-start.7 = (bf16[256,128]{1,0:T(8,128)(2,1)S(1)}, bf16[256,128]{1,0:T(8,128)(2,1)S(1)}, u32[]{:S(2)}, u32[]{:S(2)}) collective-permute-start(bf16[256,128]{1,0:T(8,128)(2,1)S(1)} %get-tuple-element.69), channel_id=1, source_target_pairs={{0,8},{8,0},{16,24},{24,16},{1,9},{9,1},{17,25},{25,17},{2,10},{10... | collective-permute-start | bytes 196616 | tf_op jit(solution)/shard_map/ppermute | solution.py:378
  19.9 1.7 %collective-permute-done.5.refs_4_ = bf16[256,128]{1,0:T(8,128)(2,1)S(1)} collective-permute-done((bf16[256,128]{1,0:T(8,128)(2,1)S(1)}, bf16[256,128]{1,0:T(8,128)(2,1)S(1)}, u32[]{:S(2)}, u32[]{:S(2)}) %collective-permute-start.5) | collective-permute-done | bytes 65568 | tf_op jit(solution)/shard_map/ppermute | solution.py:378
  21.6 2.7 %collective-permute-done.6.refs_5_ = bf16[256,128]{1,0:T(8,128)(2,1)S(1)} collective-permute-done((bf16[256,128]{1,0:T(8,128)(2,1)S(1)}, bf16[256,128]{1,0:T(8,128)(2,1)S(1)}, u32[]{:S(2)}, u32[]{:S(2)}) %collective-permute-start.6) | collective-permute-done | bytes 65568 | tf_op jit(solution)/shard_map/ppermute | solution.py:378
  24.5 1.3 %collective-permute-start.10 = (bf16[2,256,128]{2,1,0:T(8,128)(2,1)S(1)}, bf16[2,256,128]{2,1,0:T(8,128)(2,1)S(1)}, u32[]{:S(2)}, u32[]{:S(2)}) collective-permute-start(bf16[2,256,128]{2,1,0:T(8,128)(2,1)S(1)} %get-tuple-element.73), channel_id=1, source_target_pairs={{0,2},{1,3},{2,0},{3,1},{4,6},{5,7},{6,4},{7,5},{8,10},{9,11},{10,... | collective-permute-start | bytes 393224 | tf_op jit(solution)/shard_map/ppermute | solution.py:378
  25.8 1.2 %collective-permute-start.8 = (bf16[2,256,128]{2,1,0:T(8,128)(2,1)S(1)}, bf16[2,256,128]{2,1,0:T(8,128)(2,1)S(1)}, u32[]{:S(2)}, u32[]{:S(2)}) collective-permute-start(bf16[2,256,128]{2,1,0:T(8,128)(2,1)S(1)} %get-tuple-element.70), channel_id=1, source_target_pairs={{0,4},{1,5},{2,6},{3,7},{4,0},{5,1},{6,2},{7,3},{8,12},{9,13},{10,... | collective-permute-start | bytes 393224 | tf_op jit(solution)/shard_map/ppermute | solution.py:378
  26.9 1.1 %collective-permute-start.9 = (bf16[2,256,128]{2,1,0:T(8,128)(2,1)S(1)}, bf16[2,256,128]{2,1,0:T(8,128)(2,1)S(1)}, u32[]{:S(2)}, u32[]{:S(2)}) collective-permute-start(bf16[2,256,128]{2,1,0:T(8,128)(2,1)S(1)} %get-tuple-element.71), channel_id=1, source_target_pairs={{0,6},{1,7},{2,4},{3,5},{4,2},{5,3},{6,0},{7,1},{8,14},{9,15},{10,... | collective-permute-start | bytes 393224 | tf_op jit(solution)/shard_map/ppermute | solution.py:378
  28.1 2.7 %collective-permute-done.10.refs_9_.slot = bf16[2,256,128]{2,1,0:T(8,128)(2,1)S(1)} collective-permute-done((bf16[2,256,128]{2,1,0:T(8,128)(2,1)S(1)}, bf16[2,256,128]{2,1,0:T(8,128)(2,1)S(1)}, u32[]{:S(2)}, u32[]{:S(2)}) %collective-permute-start.10) | collective-permute-done | bytes 131104 | tf_op jit(solution)/shard_map/ppermute | solution.py:378
  31.0 1.3 %finish.4 = (bf16[128,2048]{1,0:T(8,128)(2,1)}, bf16[128,2048]{1,0:T(8,128)(2,1)}, bf16[128,2048]{1,0:T(8,128)(2,1)}, bf16[128,2048]{1,0:T(8,128)(2,1)}) custom-call(bf16[128,2048]{1,0:T(8,128)(2,1)S(1)} %get-tuple-element.44.refs_0_, bf16[128,2048]{1,0:T(8,128)(2,1)S(1)} %get-tuple-element.45.refs_1_, bf16[128,2048]{1,0:T(8,128)(2,1)S(1)} %get-tuple-element.46.refs_2_, ...), custom_call_target="tpu_custom_call" | custom-call | flops 67108864 | bytes 2097152 | tf_op jit(solution)/shard_map/finish/pallas_call | solution.py:361
  32.2 0.6 %collective-permute-done.9.slot.refs_9_ = bf16[2,256,128]{2,1,0:T(8,128)(2,1)S(1)} collective-permute-done((bf16[2,256,128]{2,1,0:T(8,128)(2,1)S(1)}, bf16[2,256,128]{2,1,0:T(8,128)(2,1)S(1)}, u32[]{:S(2)}, u32[]{:S(2)}) %collective-permute-start.9) | collective-permute-done | bytes 131104 | tf_op jit(solution)/shard_map/ppermute | solution.py:378
  33.0 0.5 %collective-permute-start.11 = (bf16[2,256,128]{2,1,0:T(8,128)(2,1)S(1)}, bf16[2,256,128]{2,1,0:T(8,128)(2,1)S(1)}, u32[]{:S(2)}, u32[]{:S(2)}) collective-permute-start(bf16[2,256,128]{2,1,0:T(8,128)(2,1)S(1)} %theirs.4), channel_id=1, source_target_pairs={{0,1},{1,0},{2,3},{3,2},{4,5},{5,4},{6,7},{7,6},{8,9},{9,8},{10,11... | collective-permute-start | bytes 393224 | tf_op jit(solution)/shard_map/ppermute | solution.py:378
  33.5 0.4 %finish.5.refs_10_ = bf16[4,128,512]{2,1,0:T(8,128)(2,1)S(1)} custom-call(bf16[128,2048]{1,0:T(8,128)(2,1)S(1)} %get-tuple-element.44.refs_0_, bf16[128,2048]{1,0:T(8,128)(2,1)S(1)} %get-tuple-element.45.refs_1_, bf16[128,2048]{1,0:T(8,128)(2,1)S(1)} %get-tuple-element.46.refs_2_, bf16[128,2048]{1,0:T(8,128)(2,1)S(1)} %get-tuple-element.47.refs_3_, ...), custom_call_target="tpu_custom_call" | custom-call | flops 67108864 | bytes 2097152 | tf_op jit(solution)/shard_map/finish/pallas_call | solution.py:361
  33.9 0.4 %finish.6.refs_11_ = bf16[4,128,512]{2,1,0:T(8,128)(2,1)S(1)} custom-call(bf16[128,2048]{1,0:T(8,128)(2,1)S(1)} %get-tuple-element.44.refs_0_, bf16[128,2048]{1,0:T(8,128)(2,1)S(1)} %get-tuple-element.45.refs_1_, bf16[128,2048]{1,0:T(8,128)(2,1)S(1)} %get-tuple-element.46.refs_2_, bf16[128,2048]{1,0:T(8,128)(2,1)S(1)} %get-tuple-element.47.refs_3_, ...), custom_call_target="tpu_custom_call" | custom-call | flops 67108864 | bytes 2097152 | tf_op jit(solution)/shard_map/finish/pallas_call | solution.py:361
  34.5 1.3 %finish.7 = (bf16[128,2048]{1,0:T(8,128)(2,1)}, bf16[128,2048]{1,0:T(8,128)(2,1)}, bf16[128,2048]{1,0:T(8,128)(2,1)}, bf16[128,2048]{1,0:T(8,128)(2,1)}) custom-call(bf16[128,2048]{1,0:T(8,128)(2,1)S(1)} %get-tuple-element.44.refs_0_, ...), custom_call_target="tpu_custom_call", output_to_operand_aliasing={{0}: (12, {}), {1}: (13, {}), {2}: (14, {}), {3}: (15, {})} | custom-call | flops 67108864 | bytes 2097152 | tf_op jit(solution)/shard_map/finish/pallas_call | solution.py:361
  (22 shorter events, 1.0 us)
Async XLA Ops:
  2.5 1.7 %collective-permute-start = (bf16[2,512,128]{2,1,0:T(8,128)(2,1)S(1)}, bf16[2,512,128]{2,1,0:T(8,128)(2,1)S(1)}, u32[]{:S(2)}, u32[]{:S(2)}) collective-permute-start(bf16[2,512,128]{2,1,0:T(8,128)(2,1)S(1)} %get-tuple-element.49), channel_id=1, source_target_pairs={{0,1},{1,0},{2,3},{3,2},{4,5},{5,4},{6,7},{7,6},{8,9},{9,8},{10,11... | collective-permute-start | bytes 786440 | tf_op jit(solution)/shard_map/ppermute | solution.py:378
  3.3 3.9 %collective-permute-start.2 = (bf16[2,512,128]{2,1,0:T(8,128)(2,1)S(1)}, bf16[2,512,128]{2,1,0:T(8,128)(2,1)S(1)}, u32[]{:S(2)}, u32[]{:S(2)}) collective-permute-start(bf16[2,512,128]{2,1,0:T(8,128)(2,1)S(1)} %sums.3), channel_id=1, source_target_pairs={{0,1},{1,0},{2,3},{3,2},{4,5},{5,4},{6,7},{7,6},{8,9},{9,8},{10,11... | collective-permute-start | bytes 786440 | tf_op jit(solution)/shard_map/ppermute | solution.py:378
  4.2 7.0 %collective-permute-start.1 = (bf16[2,256,128]{2,1,0:T(8,128)(2,1)S(1)}, bf16[2,256,128]{2,1,0:T(8,128)(2,1)S(1)}, u32[]{:S(2)}, u32[]{:S(2)}) collective-permute-start(bf16[2,256,128]{2,1,0:T(8,128)(2,1)S(1)} %get-tuple-element.51), channel_id=1, source_target_pairs={{0,2},{1,3},{2,0},{3,1},{4,6},{5,7},{6,4},{7,5},{8,10},{9,11},{10,... | collective-permute-start | bytes 393224 | tf_op jit(solution)/shard_map/ppermute | solution.py:378
  7.2 8.1 %collective-permute-start.3 = (bf16[2,256,128]{2,1,0:T(8,128)(2,1)S(1)}, bf16[2,256,128]{2,1,0:T(8,128)(2,1)S(1)}, u32[]{:S(2)}, u32[]{:S(2)}) collective-permute-start(bf16[2,256,128]{2,1,0:T(8,128)(2,1)S(1)} %get-tuple-element.53), channel_id=1, source_target_pairs={{0,4},{1,5},{2,6},{3,7},{4,0},{5,1},{6,2},{7,3},{8,12},{9,13},{10,... | collective-permute-start | bytes 393224 | tf_op jit(solution)/shard_map/ppermute | solution.py:378
  8.8 6.6 %collective-permute-start.4 = (bf16[2,256,128]{2,1,0:T(8,128)(2,1)S(1)}, bf16[2,256,128]{2,1,0:T(8,128)(2,1)S(1)}, u32[]{:S(2)}, u32[]{:S(2)}) collective-permute-start(bf16[2,256,128]{2,1,0:T(8,128)(2,1)S(1)} %get-tuple-element.54), channel_id=1, source_target_pairs={{0,6},{1,7},{2,4},{3,5},{4,2},{5,3},{6,0},{7,1},{8,14},{9,15},{10,... | collective-permute-start | bytes 393224 | tf_op jit(solution)/shard_map/ppermute | solution.py:378
  15.4 6.1 %collective-permute-start.5 = (bf16[256,128]{1,0:T(8,128)(2,1)S(1)}, bf16[256,128]{1,0:T(8,128)(2,1)S(1)}, u32[]{:S(2)}, u32[]{:S(2)}) collective-permute-start(bf16[256,128]{1,0:T(8,128)(2,1)S(1)} %get-tuple-element.67), channel_id=1, source_target_pairs={{0,24},{8,16},{16,8},{24,0},{1,25},{9,17},{17,9},{25,1},{2,26},{10... | collective-permute-start | bytes 196616 | tf_op jit(solution)/shard_map/ppermute | solution.py:378
  19.1 5.2 %collective-permute-start.6 = (bf16[256,128]{1,0:T(8,128)(2,1)S(1)}, bf16[256,128]{1,0:T(8,128)(2,1)S(1)}, u32[]{:S(2)}, u32[]{:S(2)}) collective-permute-start(bf16[256,128]{1,0:T(8,128)(2,1)S(1)} %get-tuple-element.68), channel_id=1, source_target_pairs={{0,16},{8,24},{16,0},{24,8},{1,17},{9,25},{17,1},{25,9},{2,18},{10... | collective-permute-start | bytes 196616 | tf_op jit(solution)/shard_map/ppermute | solution.py:378
  19.1 5.2 %collective-permute-start.7 = (bf16[256,128]{1,0:T(8,128)(2,1)S(1)}, bf16[256,128]{1,0:T(8,128)(2,1)S(1)}, u32[]{:S(2)}, u32[]{:S(2)}) collective-permute-start(bf16[256,128]{1,0:T(8,128)(2,1)S(1)} %get-tuple-element.69), channel_id=1, source_target_pairs={{0,8},{8,0},{16,24},{24,16},{1,9},{9,1},{17,25},{25,17},{2,10},{10... | collective-permute-start | bytes 196616 | tf_op jit(solution)/shard_map/ppermute | solution.py:378
  24.5 6.4 %collective-permute-start.10 = (bf16[2,256,128]{2,1,0:T(8,128)(2,1)S(1)}, bf16[2,256,128]{2,1,0:T(8,128)(2,1)S(1)}, u32[]{:S(2)}, u32[]{:S(2)}) collective-permute-start(bf16[2,256,128]{2,1,0:T(8,128)(2,1)S(1)} %get-tuple-element.73), channel_id=1, source_target_pairs={{0,2},{1,3},{2,0},{3,1},{4,6},{5,7},{6,4},{7,5},{8,10},{9,11},{10,... | collective-permute-start | bytes 393224 | tf_op jit(solution)/shard_map/ppermute | solution.py:378
  25.8 6.5 %collective-permute-start.8 = (bf16[2,256,128]{2,1,0:T(8,128)(2,1)S(1)}, bf16[2,256,128]{2,1,0:T(8,128)(2,1)S(1)}, u32[]{:S(2)}, u32[]{:S(2)}) collective-permute-start(bf16[2,256,128]{2,1,0:T(8,128)(2,1)S(1)} %get-tuple-element.70), channel_id=1, source_target_pairs={{0,4},{1,5},{2,6},{3,7},{4,0},{5,1},{6,2},{7,3},{8,12},{9,13},{10,... | collective-permute-start | bytes 393224 | tf_op jit(solution)/shard_map/ppermute | solution.py:378
  26.9 5.9 %collective-permute-start.9 = (bf16[2,256,128]{2,1,0:T(8,128)(2,1)S(1)}, bf16[2,256,128]{2,1,0:T(8,128)(2,1)S(1)}, u32[]{:S(2)}, u32[]{:S(2)}) collective-permute-start(bf16[2,256,128]{2,1,0:T(8,128)(2,1)S(1)} %get-tuple-element.71), channel_id=1, source_target_pairs={{0,6},{1,7},{2,4},{3,5},{4,2},{5,3},{6,0},{7,1},{8,14},{9,15},{10,... | collective-permute-start | bytes 393224 | tf_op jit(solution)/shard_map/ppermute | solution.py:378
  28.1 5.8 %collective-permute-start.13 = (bf16[2,256,128]{2,1,0:T(8,128)(2,1)S(1)}, bf16[2,256,128]{2,1,0:T(8,128)(2,1)S(1)}, u32[]{:S(2)}, u32[]{:S(2)}) collective-permute-start(bf16[2,256,128]{2,1,0:T(8,128)(2,1)S(1)} %theirs.6), channel_id=1, source_target_pairs={{0,1},{1,0},{2,3},{3,2},{4,5},{5,4},{6,7},{7,6},{8,9},{9,8},{10,11... | collective-permute-start | bytes 393224 | tf_op jit(solution)/shard_map/ppermute | solution.py:378
  30.9 3.0 %collective-permute-start.14 = (bf16[2,256,128]{2,1,0:T(8,128)(2,1)S(1)}, bf16[2,256,128]{2,1,0:T(8,128)(2,1)S(1)}, u32[]{:S(2)}, u32[]{:S(2)}) collective-permute-start(bf16[2,256,128]{2,1,0:T(8,128)(2,1)S(1)} %theirs.7), channel_id=1, source_target_pairs={{0,1},{1,0},{2,3},{3,2},{4,5},{5,4},{6,7},{7,6},{8,9},{9,8},{10,11... | collective-permute-start | bytes 393224 | tf_op jit(solution)/shard_map/ppermute | solution.py:378
  32.9 1.4 %collective-permute-start.12 = (bf16[2,256,128]{2,1,0:T(8,128)(2,1)S(1)}, bf16[2,256,128]{2,1,0:T(8,128)(2,1)S(1)}, u32[]{:S(2)}, u32[]{:S(2)}) collective-permute-start(bf16[2,256,128]{2,1,0:T(8,128)(2,1)S(1)} %theirs.5), channel_id=1, source_target_pairs={{0,1},{1,0},{2,3},{3,2},{4,5},{5,4},{6,7},{7,6},{8,9},{9,8},{10,11... | collective-permute-start | bytes 393224 | tf_op jit(solution)/shard_map/ppermute | solution.py:378
  33.0 1.5 %collective-permute-start.11 = (bf16[2,256,128]{2,1,0:T(8,128)(2,1)S(1)}, bf16[2,256,128]{2,1,0:T(8,128)(2,1)S(1)}, u32[]{:S(2)}, u32[]{:S(2)}) collective-permute-start(bf16[2,256,128]{2,1,0:T(8,128)(2,1)S(1)} %theirs.4), channel_id=1, source_target_pairs={{0,1},{1,0},{2,3},{3,2},{4,5},{5,4},{6,7},{7,6},{8,9},{9,8},{10,11... | collective-permute-start | bytes 393224 | tf_op jit(solution)/shard_map/ppermute | solution.py:378

commit v17 on v16

--- a/solution.py
+++ b/solution.py
@@ -215,25 +215,27 @@
         pl.when(near == core)(functools.partial(run, core))
 
 
-def theirs_kernel(s, count, slot, keep, out):
-    part = slot_rows(s, count, slot.shape[1])
+def theirs_kernel(*refs):
+    slots, (keep, out) = refs[:-2], refs[-2:]
 
     def run(core):
-        out[core] = with_sums(slot, core, keep, part)
-        out[1 - core] = slot[1 - core]
+        for s, slot in enumerate(slots):
+            part = slot_rows(s, len(slots), slot.shape[1])
+            out[core, part] = with_sums(slot, core, keep, part)
+            out[1 - core, part] = slot[1 - core]
 
     by_core(run)
 
 
-def state_for_neighbour(s, count, slot, keep):
-    return pl.pallas_call(
-        functools.partial(theirs_kernel, s, count),
+def states_for_neighbour(slots, keep):
+    return pl.pallas_call(
+        theirs_kernel,
         name="theirs",
-        in_specs=[VMEM] * 2,
+        in_specs=[VMEM] * (len(slots) + 1),
         out_specs=VMEM,
-        out_shape=jax.ShapeDtypeStruct(slot.shape, BF16),
-        compiler_params=SMALL,
-    )(slot, keep[s // count])
+        out_shape=jax.ShapeDtypeStruct(keep.shape, BF16),
+        compiler_params=SMALL,
+    )(*slots, keep)
 
 
 def local_kernel(*refs):
@@ -300,12 +302,12 @@
     one_ahead(products(), use)
 
 
-def copies_out(own, block, held, outs, sems):
-    size = held.shape[2]
-    start = block_start(own, block, outs[0].shape[1] // 2)
+def copies_out(own, block, held, outs, sems, piece):
+    first, size = (0, held.shape[2]) if piece is None else (piece * held.shape[2] // 2, held.shape[2] // 2)
+    start = block_start(own, block, outs[0].shape[1] // 2) + first
     there = pl.ds(pl.multiple_of(start, size), size)
     return [
-        pltpu.make_async_copy(held.at[i], out.at[:, there], sems.at[i])
+        pltpu.make_async_copy(held.at[i, :, pl.ds(first, size)], out.at[:, there], sems.at[i])
         for i, out in enumerate(outs)
     ]
 
@@ -314,41 +316,43 @@
     tokens, local, slots, refs = refs[:4], refs[4:8], refs[8 : 8 + count], refs[8 + count :]
     got, refs = (refs[0], refs[1:]) if own else (None, refs)
     late, refs = refs[: len(rests)], refs[len(rests) :]
+    if own:
+        refs, states = refs[:-1], refs[-1]
+    else:
+        states = slots[0]
     if hold:
-        held, states = refs
+        (held,) = refs
     else:
-        outs, (states, held, sems) = refs[-7:-3], refs[-3:]
-    width, depth = tokens[0].shape[1], slots[0].shape[1]
+        outs, (held, sems) = refs[-6:-2], refs[-2:]
+    width = tokens[0].shape[1]
     copies = []
     for n, (rest, where) in enumerate(zip(late, rests)):
-        copies += copies_out(*where, rest, outs, sems.at[n + 1])
+        copies += copies_out(*where, rest, outs, sems.at[n + 2], None)
     for copy in copies:
         copy.start()
 
     def store(rows, i, out):
         held[i, :, rows] = out
+        for piece in range(2):
+            if not hold and i == 3 and rows.stop == (piece + 1) * states.shape[1] // 2:
+                for copy in copies_out(own, block, held, outs, sems.at[piece], piece):
+                    copy.start()
 
     def run(quarter):
-        start = quarter * width // 4
-        core = quarter // 2 if own else 1 - quarter // 2
-        for s, slot in enumerate(slots):
-            part = slot_rows(s, count, depth)
-            if own:
-                states[core, part] = slot[core]
-                states[1 - core, part] = with_sums(slot, 1 - core, got, part)
-            else:
-                states[:, part] = slot[...]
-        all_products(scale, start, tokens, local, states, store)
+        for s, slot in enumerate(slots if own else ()):
+            core, part = quarter // 2, slot_rows(s, count, slot.shape[1])
+            states[core, part] = slot[core]
+            states[1 - core, part] = with_sums(slot, 1 - core, got, part)
+        all_products(scale, quarter * width // 4, tokens, local, states, store)
 
     start = block_start(own, block, width // 2)
     for quarter in range(4):
         pl.when(start == quarter * width // 4)(functools.partial(run, quarter))
     if not hold:
-        last = copies_out(own, block, held, outs, sems.at[0])
-        for copy in last:
-            copy.start()
-        for copy in copies + last:
-            copy.wait()
+        for piece in range(2):
+            copies += copies_out(own, block, held, outs, sems.at[piece], piece)
+    for copy in copies:
+        copy.wait()
 
 
 def finish(own, block, tokens, local, slots, scale, got=(), rests=(), before=(), hold=False):
@@ -364,8 +368,8 @@
         in_specs=[VMEM] * len(inputs) + [ANY] * len(before),
         out_specs=VMEM if hold else [ANY] * 4,
         out_shape=piece if hold else [out] * 4,
-        scratch_shapes=[states]
-        + ([] if hold else [piece, pltpu.SemaphoreType.DMA((1 + len(rests), 4))]),
+        scratch_shapes=([] if hold else [piece, pltpu.SemaphoreType.DMA((2 + len(rests), 4))])
+        + ([states] if own else []),
         input_output_aliases={len(inputs) + i: i for i in range(len(before))},
         cost_estimate=pl.CostEstimate(
             flops=2 * rows * width * HEAD, bytes_accessed=8 * rows * width, transcendentals=0
@@ -395,20 +399,18 @@
     others = [swap(send, "outer", s) for s, send in zip(distances(outer_count), sends)]
     slots = swap_far(scan_slots(slots, others))
     half = far_count // 2
-    arrived, outs, rests = [], (), []
-    for block in range(2):
-        part = slots[block * half : (block + 1) * half]
-        if block:
-            part, outs = lax.optimization_barrier((part, tuple(outs)))
-        for s, slot in enumerate(part):
-            theirs = state_for_neighbour(block * half + s, half, slot, keep)
-            arrived.append(swap(theirs, "inner", 1))
-        made = finish(True, block, tokens, local, part, scale, got=got[block : block + 1], hold=block)
-        outs = outs or made
-    rests.append(((True, 1), made))
-    made = finish(False, 0, tokens, local, arrived[:half], scale, hold=True)
-    rests.append(((False, 0), made))
-    return tuple(finish(False, 1, tokens, local, arrived[half:], scale, rests=rests, before=outs))
+
+    def near_swap(block, part):
+        return swap(states_for_neighbour(part, keep[block]), "inner", 1)
+
+    arrived = [near_swap(0, slots[:half])]
+    outs = finish(True, 0, tokens, local, slots[:half], scale, got=got[:1])
+    part, outs = lax.optimization_barrier((slots[half:], tuple(outs)))
+    arrived.append(near_swap(1, part))
+    rest = finish(False, 0, tokens, local, arrived[:1], scale, hold=True)
+    rests = [((False, 0), rest)]
+    outs = finish(True, 1, tokens, local, part, scale, got=got[1:], rests=rests, before=outs)
+    return tuple(finish(False, 1, tokens, local, arrived[1:], scale, before=outs))
 
 
 def solution(mesh):

time: 35.9 us -> 35.9 us (level)
  Pallas kernels: 8.59 us -> 9.2 us
  starting transfers between devices: 14.2 us -> 13.6 us
    pallas_call x4, Pallas kernels: 3.33 us -> 3.96 us  [finish(): pl.pallas_call(functools.partial(finish_kernel, scale, own, block, len(sl...]
    ppermute x15 -> x13, starting transfers between devices: 14.2 us -> 13.6 us  [swap(): lax.ppermute(x, axis, [(i, i ^ bits) for i in range(lax.axis_size(axis))])]
    ppermute x15 -> x13, waiting for transfers between devices: 12.2 us -> 12.2 us  [swap(): lax.ppermute(x, axis, [(i, i ^ bits) for i in range(lax.axis_size(axis))])]
  transfers between devices with their start and end apart: 15 -> 13, of which waited for: 7 -> 6; matrix products, arithmetic and copies ran while one was open for 0% -> 0% of each run, Pallas kernels for 15% -> 17%
where the time goes in v17:
time: 35.9 us; the launch traced here: 35.7 us
  starting transfers between devices  13.6 us (38%)
  waiting for transfers between devices  12.2 us (34%)
  Pallas kernels  9.2 us (26%)
  between operations  0.77 us (2%)
    ppermute x13, starting transfers between devices, swap(): lax.ppermute(x, axis, [(i, i ^ bits) for i in range(lax.axis_size(axis))])  13.6 us
    ppermute x13, waiting for transfers between devices, swap(): lax.ppermute(x, axis, [(i, i ^ bits) for i in range(lax.axis_size(axis))])  12.2 us
    pallas_call x4, Pallas kernels, finish(): pl.pallas_call(functools.partial(finish_kernel, scale, own, block, len(sl...  3.96 us
    pallas_call x1, Pallas kernels, local_part(): pl.pallas_call(local_kernel, name='local', in_specs=[VMEM] * 4, out_specs...  2.16 us
    pallas_call x1, Pallas kernels, load(): pl.pallas_call(load_kernel, name='load', in_specs=[ANY] * 4, out_specs=[V...  1.82 us
    pallas_call x2, Pallas kernels, sums(): pl.pallas_call(functools.partial(sums_kernel, wanted), name='sums', in_sp...  0.75 us
  transfers between devices with their start and end apart: 13, of which 6 were waited for; matrix products, arithmetic and copies ran while one was open for 0% of the time, Pallas kernels for 17%

profile of v17, /device:TPU:0, one launch (start us, length us, event | category | flops | bytes accessed | tf_op | source)
XLA Modules:
  0.0 35.7 jit_solution(1198948226677478096)
XLA Ops:
  0.6 1.8 %load.1 = (bf16[128,2048]{1,0:T(8,128)(2,1)S(1)}, bf16[128,2048]{1,0:T(8,128)(2,1)S(1)}, bf16[128,2048]{1,0:T(8,128)(2,1)S(1)}, bf16[128,2048]{1,0:T(8,128)(2,1)S(1)}, bf16[2,512,128]{2,1,0:T(8,128)(2,1)S(1)}) custom-call(bf16[128,2048]{1,0:T(8,128)(2,1)} %refs_0_.1, bf16[128,2048]{1,0:T(8,128)(2,1)} %refs_1_.1, bf16[128,2048]{1,0:T(8,128)(2,1)} %refs_2_.1, ...), custom_call_target="tpu_custom_call" | custom-call | flops 33554432 | bytes 2621440 | tf_op jit(solution)/shard_map/load/pallas_call | solution.py:92
  2.5 0.5 %collective-permute-start = (bf16[2,512,128]{2,1,0:T(8,128)(2,1)S(1)}, bf16[2,512,128]{2,1,0:T(8,128)(2,1)S(1)}, u32[]{:S(2)}, u32[]{:S(2)}) collective-permute-start(bf16[2,512,128]{2,1,0:T(8,128)(2,1)S(1)} %get-tuple-element.53), channel_id=1, source_target_pairs={{0,1},{1,0},{2,3},{3,2},{4,5},{5,4},{6,7},{7,6},{8,9},{9,8},{10,11... | collective-permute-start | bytes 786440 | tf_op jit(solution)/shard_map/ppermute | solution.py:382
  3.0 0.3 sums.3
  3.4 0.5 %sums.2 = (bf16[2,512,128]{2,1,0:T(8,128)(2,1)S(1)}, bf16[2,512,128]{2,1,0:T(8,128)(2,1)S(1)}) custom-call(bf16[128,2048]{1,0:T(8,128)(2,1)S(1)} %get-tuple-element.48.refs_0_, bf16[128,2048]{1,0:T(8,128)(2,1)S(1)} %get-tuple-element.49.refs_1_, bf16[128,2048]{1,0:T(8,128)(2,1)S(1)} %get-tuple-element.50.refs_2_, bf16[128,2048]{1,0:T(8,128)(2,1)S(1)} %get-tuple-element.51.refs_3_), custom_call_target="tpu_custom_call" | custom-call | flops 67108864 | bytes 1572864 | tf_op jit(solution)/shard_map/sums/pallas_call | solution.py:114
  3.9 0.3 collective-permute-done.got_ref.refs_10_
  4.2 2.9 %collective-permute-start.1 = (bf16[2,256,128]{2,1,0:T(8,128)(2,1)S(1)}, bf16[2,256,128]{2,1,0:T(8,128)(2,1)S(1)}, u32[]{:S(2)}, u32[]{:S(2)}) collective-permute-start(bf16[2,256,128]{2,1,0:T(8,128)(2,1)S(1)} %get-tuple-element.55), channel_id=1, source_target_pairs={{0,2},{1,3},{2,0},{3,1},{4,6},{5,7},{6,4},{7,5},{8,10},{9,11},{10,... | collective-permute-start | bytes 393224 | tf_op jit(solution)/shard_map/ppermute | solution.py:382
  7.2 1.6 %collective-permute-start.3 = (bf16[2,256,128]{2,1,0:T(8,128)(2,1)S(1)}, bf16[2,256,128]{2,1,0:T(8,128)(2,1)S(1)}, u32[]{:S(2)}, u32[]{:S(2)}) collective-permute-start(bf16[2,256,128]{2,1,0:T(8,128)(2,1)S(1)} %get-tuple-element.57), channel_id=1, source_target_pairs={{0,4},{1,5},{2,6},{3,7},{4,0},{5,1},{6,2},{7,3},{8,12},{9,13},{10,... | collective-permute-start | bytes 393224 | tf_op jit(solution)/shard_map/ppermute | solution.py:382
  8.8 0.3 collective-permute-start.4
  9.1 2.2 %local.1 = (f32[128,2048]{1,0:T(8,128)S(1)}, f32[128,2048]{1,0:T(8,128)S(1)}, f32[128,2048]{1,0:T(8,128)S(1)}, f32[128,2048]{1,0:T(8,128)S(1)}) custom-call(bf16[128,2048]{1,0:T(8,128)(2,1)S(1)} %get-tuple-element.48.refs_0_, bf16[128,2048]{1,0:T(8,128)(2,1)S(1)} %get-tuple-element.49.refs_1_, bf16[128,2048]{1,0:T(8,128)(2,1)S(1)} %get-tuple-element.50.refs_2_, ...), custom_call_target="tpu_custom_call" | custom-call | flops 402653184 | bytes 6291456 | tf_op jit(solution)/shard_map/local/pallas_call | solution.py:272
  11.3 4.1 %collective-permute-done.3.refs_2_ = bf16[2,256,128]{2,1,0:T(8,128)(2,1)S(1)} collective-permute-done((bf16[2,256,128]{2,1,0:T(8,128)(2,1)S(1)}, bf16[2,256,128]{2,1,0:T(8,128)(2,1)S(1)}, u32[]{:S(2)}, u32[]{:S(2)}) %collective-permute-start.3) | collective-permute-done | bytes 131104 | tf_op jit(solution)/shard_map/ppermute | solution.py:382
  15.4 3.7 %collective-permute-start.5 = (bf16[256,128]{1,0:T(8,128)(2,1)S(1)}, bf16[256,128]{1,0:T(8,128)(2,1)S(1)}, u32[]{:S(2)}, u32[]{:S(2)}) collective-permute-start(bf16[256,128]{1,0:T(8,128)(2,1)S(1)} %get-tuple-element.71), channel_id=1, source_target_pairs={{0,24},{8,16},{16,8},{24,0},{1,25},{9,17},{17,9},{25,1},{2,26},{10... | collective-permute-start | bytes 196616 | tf_op jit(solution)/shard_map/ppermute | solution.py:382
  19.1 0.8 %collective-permute-start.7 = (bf16[256,128]{1,0:T(8,128)(2,1)S(1)}, bf16[256,128]{1,0:T(8,128)(2,1)S(1)}, u32[]{:S(2)}, u32[]{:S(2)}) collective-permute-start(bf16[256,128]{1,0:T(8,128)(2,1)S(1)} %get-tuple-element.73), channel_id=1, source_target_pairs={{0,8},{8,0},{16,24},{24,16},{1,9},{9,1},{17,25},{25,17},{2,10},{10... | collective-permute-start | bytes 196616 | tf_op jit(solution)/shard_map/ppermute | solution.py:382
  19.9 1.7 %collective-permute-done.5.refs_4_ = bf16[256,128]{1,0:T(8,128)(2,1)S(1)} collective-permute-done((bf16[256,128]{1,0:T(8,128)(2,1)S(1)}, bf16[256,128]{1,0:T(8,128)(2,1)S(1)}, u32[]{:S(2)}, u32[]{:S(2)}) %collective-permute-start.5) | collective-permute-done | bytes 65568 | tf_op jit(solution)/shard_map/ppermute | solution.py:382
  21.6 2.7 %collective-permute-done.6.refs_5_ = bf16[256,128]{1,0:T(8,128)(2,1)S(1)} collective-permute-done((bf16[256,128]{1,0:T(8,128)(2,1)S(1)}, bf16[256,128]{1,0:T(8,128)(2,1)S(1)}, u32[]{:S(2)}, u32[]{:S(2)}) %collective-permute-start.6) | collective-permute-done | bytes 65568 | tf_op jit(solution)/shard_map/ppermute | solution.py:382
  24.3 0.2 scan.1
  24.5 1.3 %collective-permute-start.10 = (bf16[2,256,128]{2,1,0:T(8,128)(2,1)S(1)}, bf16[2,256,128]{2,1,0:T(8,128)(2,1)S(1)}, u32[]{:S(2)}, u32[]{:S(2)}) collective-permute-start(bf16[2,256,128]{2,1,0:T(8,128)(2,1)S(1)} %get-tuple-element.77), channel_id=1, source_target_pairs={{0,2},{1,3},{2,0},{3,1},{4,6},{5,7},{6,4},{7,5},{8,10},{9,11},{10,... | collective-permute-start | bytes 393224 | tf_op jit(solution)/shard_map/ppermute | solution.py:382
  25.8 1.2 %collective-permute-start.8 = (bf16[2,256,128]{2,1,0:T(8,128)(2,1)S(1)}, bf16[2,256,128]{2,1,0:T(8,128)(2,1)S(1)}, u32[]{:S(2)}, u32[]{:S(2)}) collective-permute-start(bf16[2,256,128]{2,1,0:T(8,128)(2,1)S(1)} %get-tuple-element.74), channel_id=1, source_target_pairs={{0,4},{1,5},{2,6},{3,7},{4,0},{5,1},{6,2},{7,3},{8,12},{9,13},{10,... | collective-permute-start | bytes 393224 | tf_op jit(solution)/shard_map/ppermute | solution.py:382
  26.9 1.1 %collective-permute-start.9 = (bf16[2,256,128]{2,1,0:T(8,128)(2,1)S(1)}, bf16[2,256,128]{2,1,0:T(8,128)(2,1)S(1)}, u32[]{:S(2)}, u32[]{:S(2)}) collective-permute-start(bf16[2,256,128]{2,1,0:T(8,128)(2,1)S(1)} %get-tuple-element.75), channel_id=1, source_target_pairs={{0,6},{1,7},{2,4},{3,5},{4,2},{5,3},{6,0},{7,1},{8,14},{9,15},{10,... | collective-permute-start | bytes 393224 | tf_op jit(solution)/shard_map/ppermute | solution.py:382
  28.0 2.8 %collective-permute-done.10.refs_9_.refs_1_ = bf16[2,256,128]{2,1,0:T(8,128)(2,1)S(1)} collective-permute-done((bf16[2,256,128]{2,1,0:T(8,128)(2,1)S(1)}, bf16[2,256,128]{2,1,0:T(8,128)(2,1)S(1)}, u32[]{:S(2)}, u32[]{:S(2)}) %collective-permute-start.10) | collective-permute-done | bytes 131104 | tf_op jit(solution)/shard_map/ppermute | solution.py:382
  31.0 1.2 %finish.4 = (bf16[128,2048]{1,0:T(8,128)(2,1)}, bf16[128,2048]{1,0:T(8,128)(2,1)}, bf16[128,2048]{1,0:T(8,128)(2,1)}, bf16[128,2048]{1,0:T(8,128)(2,1)}) custom-call(bf16[128,2048]{1,0:T(8,128)(2,1)S(1)} %get-tuple-element.48.refs_0_, bf16[128,2048]{1,0:T(8,128)(2,1)S(1)} %get-tuple-element.49.refs_1_, bf16[128,2048]{1,0:T(8,128)(2,1)S(1)} %get-tuple-element.50.refs_2_, ...), custom_call_target="tpu_custom_call" | custom-call | flops 67108864 | bytes 2097152 | tf_op jit(solution)/shard_map/finish/pallas_call | solution.py:365
  32.2 0.6 %collective-permute-done.9.refs_1_.refs_9_ = bf16[2,256,128]{2,1,0:T(8,128)(2,1)S(1)} collective-permute-done((bf16[2,256,128]{2,1,0:T(8,128)(2,1)S(1)}, bf16[2,256,128]{2,1,0:T(8,128)(2,1)S(1)}, u32[]{:S(2)}, u32[]{:S(2)}) %collective-permute-start.9) | collective-permute-done | bytes 131104 | tf_op jit(solution)/shard_map/ppermute | solution.py:382
  32.9 0.4 %finish.5.refs_11_ = bf16[4,128,512]{2,1,0:T(8,128)(2,1)S(1)} custom-call(bf16[128,2048]{1,0:T(8,128)(2,1)S(1)} %get-tuple-element.48.refs_0_, bf16[128,2048]{1,0:T(8,128)(2,1)S(1)} %get-tuple-element.49.refs_1_, bf16[128,2048]{1,0:T(8,128)(2,1)S(1)} %get-tuple-element.50.refs_2_, bf16[128,2048]{1,0:T(8,128)(2,1)S(1)} %get-tuple-element.51.refs_3_, ...), custom_call_target="tpu_custom_call" | custom-call | flops 67108864 | bytes 2097152 | tf_op jit(solution)/shard_map/finish/pallas_call | solution.py:365
  33.3 1.2 %finish.6 = (bf16[128,2048]{1,0:T(8,128)(2,1)}, bf16[128,2048]{1,0:T(8,128)(2,1)}, bf16[128,2048]{1,0:T(8,128)(2,1)}, bf16[128,2048]{1,0:T(8,128)(2,1)}) custom-call(bf16[128,2048]{1,0:T(8,128)(2,1)S(1)} %get-tuple-element.48.refs_0_, ...), custom_call_target="tpu_custom_call", output_to_operand_aliasing={{0}: (12, {}), {1}: (13, {}), {2}: (14, {}), {3}: (15, {})} | custom-call | flops 67108864 | bytes 2097152 | tf_op jit(solution)/shard_map/finish/pallas_call | solution.py:365
  34.6 1.2 %finish.7 = (bf16[128,2048]{1,0:T(8,128)(2,1)}, bf16[128,2048]{1,0:T(8,128)(2,1)}, bf16[128,2048]{1,0:T(8,128)(2,1)}, bf16[128,2048]{1,0:T(8,128)(2,1)}) custom-call(bf16[128,2048]{1,0:T(8,128)(2,1)S(1)} %get-tuple-element.48.refs_0_, ...), custom_call_target="tpu_custom_call", output_to_operand_aliasing={{0}: (9, {}), {1}: (10, {}), {2}: (11, {}), {3}: (12, {})} | custom-call | flops 67108864 | bytes 2097152 | tf_op jit(solution)/shard_map/finish/pallas_call | solution.py:365
  (16 shorter events, 0.6 us)
Async XLA Ops:
  2.5 1.7 %collective-permute-start = (bf16[2,512,128]{2,1,0:T(8,128)(2,1)S(1)}, bf16[2,512,128]{2,1,0:T(8,128)(2,1)S(1)}, u32[]{:S(2)}, u32[]{:S(2)}) collective-permute-start(bf16[2,512,128]{2,1,0:T(8,128)(2,1)S(1)} %get-tuple-element.53), channel_id=1, source_target_pairs={{0,1},{1,0},{2,3},{3,2},{4,5},{5,4},{6,7},{7,6},{8,9},{9,8},{10,11... | collective-permute-start | bytes 786440 | tf_op jit(solution)/shard_map/ppermute | solution.py:382
  3.3 3.9 %collective-permute-start.2 = (bf16[2,512,128]{2,1,0:T(8,128)(2,1)S(1)}, bf16[2,512,128]{2,1,0:T(8,128)(2,1)S(1)}, u32[]{:S(2)}, u32[]{:S(2)}) collective-permute-start(bf16[2,512,128]{2,1,0:T(8,128)(2,1)S(1)} %sums.3), channel_id=1, source_target_pairs={{0,1},{1,0},{2,3},{3,2},{4,5},{5,4},{6,7},{7,6},{8,9},{9,8},{10,11... | collective-permute-start | bytes 786440 | tf_op jit(solution)/shard_map/ppermute | solution.py:382
  4.2 7.0 %collective-permute-start.1 = (bf16[2,256,128]{2,1,0:T(8,128)(2,1)S(1)}, bf16[2,256,128]{2,1,0:T(8,128)(2,1)S(1)}, u32[]{:S(2)}, u32[]{:S(2)}) collective-permute-start(bf16[2,256,128]{2,1,0:T(8,128)(2,1)S(1)} %get-tuple-element.55), channel_id=1, source_target_pairs={{0,2},{1,3},{2,0},{3,1},{4,6},{5,7},{6,4},{7,5},{8,10},{9,11},{10,... | collective-permute-start | bytes 393224 | tf_op jit(solution)/shard_map/ppermute | solution.py:382
  7.2 8.1 %collective-permute-start.3 = (bf16[2,256,128]{2,1,0:T(8,128)(2,1)S(1)}, bf16[2,256,128]{2,1,0:T(8,128)(2,1)S(1)}, u32[]{:S(2)}, u32[]{:S(2)}) collective-permute-start(bf16[2,256,128]{2,1,0:T(8,128)(2,1)S(1)} %get-tuple-element.57), channel_id=1, source_target_pairs={{0,4},{1,5},{2,6},{3,7},{4,0},{5,1},{6,2},{7,3},{8,12},{9,13},{10,... | collective-permute-start | bytes 393224 | tf_op jit(solution)/shard_map/ppermute | solution.py:382
  8.8 6.6 %collective-permute-start.4 = (bf16[2,256,128]{2,1,0:T(8,128)(2,1)S(1)}, bf16[2,256,128]{2,1,0:T(8,128)(2,1)S(1)}, u32[]{:S(2)}, u32[]{:S(2)}) collective-permute-start(bf16[2,256,128]{2,1,0:T(8,128)(2,1)S(1)} %get-tuple-element.58), channel_id=1, source_target_pairs={{0,6},{1,7},{2,4},{3,5},{4,2},{5,3},{6,0},{7,1},{8,14},{9,15},{10,... | collective-permute-start | bytes 393224 | tf_op jit(solution)/shard_map/ppermute | solution.py:382
  15.4 6.1 %collective-permute-start.5 = (bf16[256,128]{1,0:T(8,128)(2,1)S(1)}, bf16[256,128]{1,0:T(8,128)(2,1)S(1)}, u32[]{:S(2)}, u32[]{:S(2)}) collective-permute-start(bf16[256,128]{1,0:T(8,128)(2,1)S(1)} %get-tuple-element.71), channel_id=1, source_target_pairs={{0,24},{8,16},{16,8},{24,0},{1,25},{9,17},{17,9},{25,1},{2,26},{10... | collective-permute-start | bytes 196616 | tf_op jit(solution)/shard_map/ppermute | solution.py:382
  19.1 5.2 %collective-permute-start.6 = (bf16[256,128]{1,0:T(8,128)(2,1)S(1)}, bf16[256,128]{1,0:T(8,128)(2,1)S(1)}, u32[]{:S(2)}, u32[]{:S(2)}) collective-permute-start(bf16[256,128]{1,0:T(8,128)(2,1)S(1)} %get-tuple-element.72), channel_id=1, source_target_pairs={{0,16},{8,24},{16,0},{24,8},{1,17},{9,25},{17,1},{25,9},{2,18},{10... | collective-permute-start | bytes 196616 | tf_op jit(solution)/shard_map/ppermute | solution.py:382
  19.1 5.2 %collective-permute-start.7 = (bf16[256,128]{1,0:T(8,128)(2,1)S(1)}, bf16[256,128]{1,0:T(8,128)(2,1)S(1)}, u32[]{:S(2)}, u32[]{:S(2)}) collective-permute-start(bf16[256,128]{1,0:T(8,128)(2,1)S(1)} %get-tuple-element.73), channel_id=1, source_target_pairs={{0,8},{8,0},{16,24},{24,16},{1,9},{9,1},{17,25},{25,17},{2,10},{10... | collective-permute-start | bytes 196616 | tf_op jit(solution)/shard_map/ppermute | solution.py:382
  24.5 6.4 %collective-permute-start.10 = (bf16[2,256,128]{2,1,0:T(8,128)(2,1)S(1)}, bf16[2,256,128]{2,1,0:T(8,128)(2,1)S(1)}, u32[]{:S(2)}, u32[]{:S(2)}) collective-permute-start(bf16[2,256,128]{2,1,0:T(8,128)(2,1)S(1)} %get-tuple-element.77), channel_id=1, source_target_pairs={{0,2},{1,3},{2,0},{3,1},{4,6},{5,7},{6,4},{7,5},{8,10},{9,11},{10,... | collective-permute-start | bytes 393224 | tf_op jit(solution)/shard_map/ppermute | solution.py:382
  25.8 6.4 %collective-permute-start.8 = (bf16[2,256,128]{2,1,0:T(8,128)(2,1)S(1)}, bf16[2,256,128]{2,1,0:T(8,128)(2,1)S(1)}, u32[]{:S(2)}, u32[]{:S(2)}) collective-permute-start(bf16[2,256,128]{2,1,0:T(8,128)(2,1)S(1)} %get-tuple-element.74), channel_id=1, source_target_pairs={{0,4},{1,5},{2,6},{3,7},{4,0},{5,1},{6,2},{7,3},{8,12},{9,13},{10,... | collective-permute-start | bytes 393224 | tf_op jit(solution)/shard_map/ppermute | solution.py:382
  26.9 5.9 %collective-permute-start.9 = (bf16[2,256,128]{2,1,0:T(8,128)(2,1)S(1)}, bf16[2,256,128]{2,1,0:T(8,128)(2,1)S(1)}, u32[]{:S(2)}, u32[]{:S(2)}) collective-permute-start(bf16[2,256,128]{2,1,0:T(8,128)(2,1)S(1)} %get-tuple-element.75), channel_id=1, source_target_pairs={{0,6},{1,7},{2,4},{3,5},{4,2},{5,3},{6,0},{7,1},{8,14},{9,15},{10,... | collective-permute-start | bytes 393224 | tf_op jit(solution)/shard_map/ppermute | solution.py:382
  30.9 2.0 %collective-permute-start.12 = (bf16[2,512,128]{2,1,0:T(8,128)(2,1)S(1)}, bf16[2,512,128]{2,1,0:T(8,128)(2,1)S(1)}, u32[]{:S(2)}, u32[]{:S(2)}) collective-permute-start(bf16[2,512,128]{2,1,0:T(8,128)(2,1)S(1)} %theirs.3), channel_id=1, source_target_pairs={{0,1},{1,0},{2,3},{3,2},{4,5},{5,4},{6,7},{7,6},{8,9},{9,8},{10,11... | collective-permute-start | bytes 786440 | tf_op jit(solution)/shard_map/ppermute | solution.py:382
  32.8 1.7 %collective-permute-start.11 = (bf16[2,512,128]{2,1,0:T(8,128)(2,1)S(1)}, bf16[2,512,128]{2,1,0:T(8,128)(2,1)S(1)}, u32[]{:S(2)}, u32[]{:S(2)}) collective-permute-start(bf16[2,512,128]{2,1,0:T(8,128)(2,1)S(1)} %theirs.2), channel_id=1, source_target_pairs={{0,1},{1,0},{2,3},{3,2},{4,5},{5,4},{6,7},{7,6},{8,9},{9,8},{10,11... | collective-permute-start | bytes 786440 | tf_op jit(solution)/shard_map/ppermute | solution.py:382

commit v18 on v17

--- a/solution.py
+++ b/solution.py
@@ -8,6 +8,7 @@
 from jax.sharding import PartitionSpec as P
 
 HEAD = 128
+LOADS = 4
 MIB = 1024 * 1024
 ANY = pl.BlockSpec(memory_space=pl.ANY)
 VMEM = pl.BlockSpec(memory_space=pltpu.VMEM)
@@ -74,8 +75,11 @@
 
 def load_kernel(*refs):
     tokens, held, (out, sems) = refs[:4], refs[4:8], refs[8:]
+    rows = tokens[0].shape[0] // LOADS
     copies = [
-        pltpu.make_async_copy(ref, to, sems.at[i]) for i, (ref, to) in enumerate(zip(tokens, held))
+        pltpu.make_async_copy(ref.at[pl.ds(n * rows, rows)], to.at[pl.ds(n * rows, rows)], sems.at[i, n])
+        for n in range(LOADS)
+        for i, (ref, to) in enumerate(zip(tokens, held))
     ]
     for copy in copies:
         copy.start()
@@ -95,7 +99,7 @@
         in_specs=[ANY] * 4,
         out_specs=[VMEM] * 5,
         out_shape=[pltpu.VMEM((rows, width), BF16)] * 4 + [pltpu.VMEM((2, width // 4, HEAD), BF16)],
-        scratch_shapes=[pltpu.SemaphoreType.DMA((4,))],
+        scratch_shapes=[pltpu.SemaphoreType.DMA((4, LOADS))],
         cost_estimate=pl.CostEstimate(
             flops=rows * width * HEAD, bytes_accessed=10 * rows * width, transcendentals=0
         ),
@@ -407,10 +411,11 @@
     outs = finish(True, 0, tokens, local, slots[:half], scale, got=got[:1])
     part, outs = lax.optimization_barrier((slots[half:], tuple(outs)))
     arrived.append(near_swap(1, part))
-    rest = finish(False, 0, tokens, local, arrived[:1], scale, hold=True)
-    rests = [((False, 0), rest)]
-    outs = finish(True, 1, tokens, local, part, scale, got=got[1:], rests=rests, before=outs)
-    return tuple(finish(False, 1, tokens, local, arrived[1:], scale, before=outs))
+    rests = [
+        ((True, 1), finish(True, 1, tokens, local, part, scale, got=got[1:], hold=True)),
+        ((False, 0), finish(False, 0, tokens, local, arrived[:1], scale, hold=True)),
+    ]
+    return tuple(finish(False, 1, tokens, local, arrived[1:], scale, rests=rests, before=outs))
 
 
 def solution(mesh):

time: 35.9 us -> 36 us (level)
  waiting for transfers between devices: 12.2 us -> 12.9 us
  Pallas kernels: 9.2 us -> 8.69 us
    pallas_call x4, Pallas kernels: 3.96 us -> 3.27 us  [finish(): pl.pallas_call(functools.partial(finish_kernel, scale, own, block, len(sl...]
    ppermute x13, waiting for transfers between devices: 12.2 us -> 12.9 us  [swap(): lax.ppermute(x, axis, [(i, i ^ bits) for i in range(lax.axis_size(axis))])]
  transfers between devices with their start and end apart: 13 -> 13, of which waited for: 6 -> 7; matrix products, arithmetic and copies ran while one was open for 0% -> 0% of each run, Pallas kernels for 17% -> 14%
where the time goes in v18:
time: 36 us; the launch traced here: 35.9 us
  starting transfers between devices  13.6 us (38%)
  waiting for transfers between devices  12.9 us (36%)
  Pallas kernels  8.69 us (24%)
  between operations  0.76 us (2%)
    ppermute x13, starting transfers between devices, swap(): lax.ppermute(x, axis, [(i, i ^ bits) for i in range(lax.axis_size(axis))])  13.6 us
    ppermute x13, waiting for transfers between devices, swap(): lax.ppermute(x, axis, [(i, i ^ bits) for i in range(lax.axis_size(axis))])  12.9 us
    pallas_call x4, Pallas kernels, finish(): pl.pallas_call(functools.partial(finish_kernel, scale, own, block, len(sl...  3.27 us
    pallas_call x1, Pallas kernels, local_part(): pl.pallas_call(local_kernel, name='local', in_specs=[VMEM] * 4, out_specs...  2.16 us
    pallas_call x1, Pallas kernels, load(): pl.pallas_call(load_kernel, name='load', in_specs=[ANY] * 4, out_specs=[V...  2 us
    pallas_call x2, Pallas kernels, sums(): pl.pallas_call(functools.partial(sums_kernel, wanted), name='sums', in_sp...  0.75 us
  transfers between devices with their start and end apart: 13, of which 7 were waited for; matrix products, arithmetic and copies ran while one was open for 0% of the time, Pallas kernels for 14%

profile of v18, /device:TPU:0, one launch (start us, length us, event | category | flops | bytes accessed | tf_op | source)
XLA Modules:
  0.0 35.9 jit_solution(17626962288643486277)
XLA Ops:
  0.6 2.0 %load.1 = (bf16[128,2048]{1,0:T(8,128)(2,1)S(1)}, bf16[128,2048]{1,0:T(8,128)(2,1)S(1)}, bf16[128,2048]{1,0:T(8,128)(2,1)S(1)}, bf16[128,2048]{1,0:T(8,128)(2,1)S(1)}, bf16[2,512,128]{2,1,0:T(8,128)(2,1)S(1)}) custom-call(bf16[128,2048]{1,0:T(8,128)(2,1)} %refs_0_.1, bf16[128,2048]{1,0:T(8,128)(2,1)} %refs_1_.1, bf16[128,2048]{1,0:T(8,128)(2,1)} %refs_2_.1, ...), custom_call_target="tpu_custom_call" | custom-call | flops 33554432 | bytes 2621440 | tf_op jit(solution)/shard_map/load/pallas_call | solution.py:96
  2.6 0.5 %collective-permute-start = (bf16[2,512,128]{2,1,0:T(8,128)(2,1)S(1)}, bf16[2,512,128]{2,1,0:T(8,128)(2,1)S(1)}, u32[]{:S(2)}, u32[]{:S(2)}) collective-permute-start(bf16[2,512,128]{2,1,0:T(8,128)(2,1)S(1)} %get-tuple-element.49), channel_id=1, source_target_pairs={{0,1},{1,0},{2,3},{3,2},{4,5},{5,4},{6,7},{7,6},{8,9},{9,8},{10,11... | collective-permute-start | bytes 786440 | tf_op jit(solution)/shard_map/ppermute | solution.py:386
  3.2 0.3 sums.3
  3.6 0.5 %sums.2 = (bf16[2,512,128]{2,1,0:T(8,128)(2,1)S(1)}, bf16[2,512,128]{2,1,0:T(8,128)(2,1)S(1)}) custom-call(bf16[128,2048]{1,0:T(8,128)(2,1)S(1)} %get-tuple-element.44.refs_0_, bf16[128,2048]{1,0:T(8,128)(2,1)S(1)} %get-tuple-element.45.refs_1_, bf16[128,2048]{1,0:T(8,128)(2,1)S(1)} %get-tuple-element.46.refs_2_, bf16[128,2048]{1,0:T(8,128)(2,1)S(1)} %get-tuple-element.47.refs_3_), custom_call_target="tpu_custom_call" | custom-call | flops 67108864 | bytes 1572864 | tf_op jit(solution)/shard_map/sums/pallas_call | solution.py:118
  4.0 0.3 collective-permute-done.got_ref.refs_10_
  4.4 2.9 %collective-permute-start.1 = (bf16[2,256,128]{2,1,0:T(8,128)(2,1)S(1)}, bf16[2,256,128]{2,1,0:T(8,128)(2,1)S(1)}, u32[]{:S(2)}, u32[]{:S(2)}) collective-permute-start(bf16[2,256,128]{2,1,0:T(8,128)(2,1)S(1)} %get-tuple-element.51), channel_id=1, source_target_pairs={{0,2},{1,3},{2,0},{3,1},{4,6},{5,7},{6,4},{7,5},{8,10},{9,11},{10,... | collective-permute-start | bytes 393224 | tf_op jit(solution)/shard_map/ppermute | solution.py:386
  7.4 1.6 %collective-permute-start.3 = (bf16[2,256,128]{2,1,0:T(8,128)(2,1)S(1)}, bf16[2,256,128]{2,1,0:T(8,128)(2,1)S(1)}, u32[]{:S(2)}, u32[]{:S(2)}) collective-permute-start(bf16[2,256,128]{2,1,0:T(8,128)(2,1)S(1)} %get-tuple-element.53), channel_id=1, source_target_pairs={{0,4},{1,5},{2,6},{3,7},{4,0},{5,1},{6,2},{7,3},{8,12},{9,13},{10,... | collective-permute-start | bytes 393224 | tf_op jit(solution)/shard_map/ppermute | solution.py:386
  9.0 0.3 collective-permute-start.4
  9.3 2.2 %local.1 = (f32[128,2048]{1,0:T(8,128)S(1)}, f32[128,2048]{1,0:T(8,128)S(1)}, f32[128,2048]{1,0:T(8,128)S(1)}, f32[128,2048]{1,0:T(8,128)S(1)}) custom-call(bf16[128,2048]{1,0:T(8,128)(2,1)S(1)} %get-tuple-element.44.refs_0_, bf16[128,2048]{1,0:T(8,128)(2,1)S(1)} %get-tuple-element.45.refs_1_, bf16[128,2048]{1,0:T(8,128)(2,1)S(1)} %get-tuple-element.46.refs_2_, ...), custom_call_target="tpu_custom_call" | custom-call | flops 402653184 | bytes 6291456 | tf_op jit(solution)/shard_map/local/pallas_call | solution.py:276
  11.4 4.1 %collective-permute-done.3.refs_2_ = bf16[2,256,128]{2,1,0:T(8,128)(2,1)S(1)} collective-permute-done((bf16[2,256,128]{2,1,0:T(8,128)(2,1)S(1)}, bf16[2,256,128]{2,1,0:T(8,128)(2,1)S(1)}, u32[]{:S(2)}, u32[]{:S(2)}) %collective-permute-start.3) | collective-permute-done | bytes 131104 | tf_op jit(solution)/shard_map/ppermute | solution.py:386
  15.6 3.7 %collective-permute-start.5 = (bf16[256,128]{1,0:T(8,128)(2,1)S(1)}, bf16[256,128]{1,0:T(8,128)(2,1)S(1)}, u32[]{:S(2)}, u32[]{:S(2)}) collective-permute-start(bf16[256,128]{1,0:T(8,128)(2,1)S(1)} %get-tuple-element.67), channel_id=1, source_target_pairs={{0,24},{8,16},{16,8},{24,0},{1,25},{9,17},{17,9},{25,1},{2,26},{10... | collective-permute-start | bytes 196616 | tf_op jit(solution)/shard_map/ppermute | solution.py:386
  19.3 0.8 %collective-permute-start.7 = (bf16[256,128]{1,0:T(8,128)(2,1)S(1)}, bf16[256,128]{1,0:T(8,128)(2,1)S(1)}, u32[]{:S(2)}, u32[]{:S(2)}) collective-permute-start(bf16[256,128]{1,0:T(8,128)(2,1)S(1)} %get-tuple-element.69), channel_id=1, source_target_pairs={{0,8},{8,0},{16,24},{24,16},{1,9},{9,1},{17,25},{25,17},{2,10},{10... | collective-permute-start | bytes 196616 | tf_op jit(solution)/shard_map/ppermute | solution.py:386
  20.1 1.7 %collective-permute-done.5.refs_4_ = bf16[256,128]{1,0:T(8,128)(2,1)S(1)} collective-permute-done((bf16[256,128]{1,0:T(8,128)(2,1)S(1)}, bf16[256,128]{1,0:T(8,128)(2,1)S(1)}, u32[]{:S(2)}, u32[]{:S(2)}) %collective-permute-start.5) | collective-permute-done | bytes 65568 | tf_op jit(solution)/shard_map/ppermute | solution.py:386
  21.7 2.7 %collective-permute-done.6.refs_5_ = bf16[256,128]{1,0:T(8,128)(2,1)S(1)} collective-permute-done((bf16[256,128]{1,0:T(8,128)(2,1)S(1)}, bf16[256,128]{1,0:T(8,128)(2,1)S(1)}, u32[]{:S(2)}, u32[]{:S(2)}) %collective-permute-start.6) | collective-permute-done | bytes 65568 | tf_op jit(solution)/shard_map/ppermute | solution.py:386
  24.7 1.3 %collective-permute-start.10 = (bf16[2,256,128]{2,1,0:T(8,128)(2,1)S(1)}, bf16[2,256,128]{2,1,0:T(8,128)(2,1)S(1)}, u32[]{:S(2)}, u32[]{:S(2)}) collective-permute-start(bf16[2,256,128]{2,1,0:T(8,128)(2,1)S(1)} %get-tuple-element.73), channel_id=1, source_target_pairs={{0,2},{1,3},{2,0},{3,1},{4,6},{5,7},{6,4},{7,5},{8,10},{9,11},{10,... | collective-permute-start | bytes 393224 | tf_op jit(solution)/shard_map/ppermute | solution.py:386
  26.0 1.2 %collective-permute-start.8 = (bf16[2,256,128]{2,1,0:T(8,128)(2,1)S(1)}, bf16[2,256,128]{2,1,0:T(8,128)(2,1)S(1)}, u32[]{:S(2)}, u32[]{:S(2)}) collective-permute-start(bf16[2,256,128]{2,1,0:T(8,128)(2,1)S(1)} %get-tuple-element.70), channel_id=1, source_target_pairs={{0,4},{1,5},{2,6},{3,7},{4,0},{5,1},{6,2},{7,3},{8,12},{9,13},{10,... | collective-permute-start | bytes 393224 | tf_op jit(solution)/shard_map/ppermute | solution.py:386
  27.1 1.1 %collective-permute-start.9 = (bf16[2,256,128]{2,1,0:T(8,128)(2,1)S(1)}, bf16[2,256,128]{2,1,0:T(8,128)(2,1)S(1)}, u32[]{:S(2)}, u32[]{:S(2)}) collective-permute-start(bf16[2,256,128]{2,1,0:T(8,128)(2,1)S(1)} %get-tuple-element.71), channel_id=1, source_target_pairs={{0,6},{1,7},{2,4},{3,5},{4,2},{5,3},{6,0},{7,1},{8,14},{9,15},{10,... | collective-permute-start | bytes 393224 | tf_op jit(solution)/shard_map/ppermute | solution.py:386
  28.2 2.8 %collective-permute-done.10.refs_9_.refs_1_ = bf16[2,256,128]{2,1,0:T(8,128)(2,1)S(1)} collective-permute-done((bf16[2,256,128]{2,1,0:T(8,128)(2,1)S(1)}, bf16[2,256,128]{2,1,0:T(8,128)(2,1)S(1)}, u32[]{:S(2)}, u32[]{:S(2)}) %collective-permute-start.10) | collective-permute-done | bytes 131104 | tf_op jit(solution)/shard_map/ppermute | solution.py:386
  31.2 1.2 %finish.4 = (bf16[128,2048]{1,0:T(8,128)(2,1)}, bf16[128,2048]{1,0:T(8,128)(2,1)}, bf16[128,2048]{1,0:T(8,128)(2,1)}, bf16[128,2048]{1,0:T(8,128)(2,1)}) custom-call(bf16[128,2048]{1,0:T(8,128)(2,1)S(1)} %get-tuple-element.44.refs_0_, bf16[128,2048]{1,0:T(8,128)(2,1)S(1)} %get-tuple-element.45.refs_1_, bf16[128,2048]{1,0:T(8,128)(2,1)S(1)} %get-tuple-element.46.refs_2_, ...), custom_call_target="tpu_custom_call" | custom-call | flops 67108864 | bytes 2097152 | tf_op jit(solution)/shard_map/finish/pallas_call | solution.py:369
  32.4 0.6 %collective-permute-done.9.refs_1_.refs_9_ = bf16[2,256,128]{2,1,0:T(8,128)(2,1)S(1)} collective-permute-done((bf16[2,256,128]{2,1,0:T(8,128)(2,1)S(1)}, bf16[2,256,128]{2,1,0:T(8,128)(2,1)S(1)}, u32[]{:S(2)}, u32[]{:S(2)}) %collective-permute-start.9) | collective-permute-done | bytes 131104 | tf_op jit(solution)/shard_map/ppermute | solution.py:386
  33.1 0.4 %finish.5.refs_9_ = bf16[4,128,512]{2,1,0:T(8,128)(2,1)S(1)} custom-call(bf16[128,2048]{1,0:T(8,128)(2,1)S(1)} %get-tuple-element.44.refs_0_, bf16[128,2048]{1,0:T(8,128)(2,1)S(1)} %get-tuple-element.45.refs_1_, bf16[128,2048]{1,0:T(8,128)(2,1)S(1)} %get-tuple-element.46.refs_2_, bf16[128,2048]{1,0:T(8,128)(2,1)S(1)} %get-tuple-element.47.refs_3_, ...), custom_call_target="tpu_custom_call" | custom-call | flops 67108864 | bytes 2097152 | tf_op jit(solution)/shard_map/finish/pallas_call | solution.py:369
  33.6 0.4 %finish.6.refs_10_ = bf16[4,128,512]{2,1,0:T(8,128)(2,1)S(1)} custom-call(bf16[128,2048]{1,0:T(8,128)(2,1)S(1)} %get-tuple-element.44.refs_0_, bf16[128,2048]{1,0:T(8,128)(2,1)S(1)} %get-tuple-element.45.refs_1_, bf16[128,2048]{1,0:T(8,128)(2,1)S(1)} %get-tuple-element.46.refs_2_, bf16[128,2048]{1,0:T(8,128)(2,1)S(1)} %get-tuple-element.47.refs_3_, ...), custom_call_target="tpu_custom_call" | custom-call | flops 67108864 | bytes 2097152 | tf_op jit(solution)/shard_map/finish/pallas_call | solution.py:369
  34.0 0.7 %collective-permute-done.11.refs_8_ = bf16[2,512,128]{2,1,0:T(8,128)(2,1)S(1)} collective-permute-done((bf16[2,512,128]{2,1,0:T(8,128)(2,1)S(1)}, bf16[2,512,128]{2,1,0:T(8,128)(2,1)S(1)}, u32[]{:S(2)}, u32[]{:S(2)}) %collective-permute-start.11) | collective-permute-done | bytes 262176 | tf_op jit(solution)/shard_map/ppermute | solution.py:386
  34.6 1.3 %finish.7 = (bf16[128,2048]{1,0:T(8,128)(2,1)}, bf16[128,2048]{1,0:T(8,128)(2,1)}, bf16[128,2048]{1,0:T(8,128)(2,1)}, bf16[128,2048]{1,0:T(8,128)(2,1)}) custom-call(bf16[128,2048]{1,0:T(8,128)(2,1)S(1)} %get-tuple-element.44.refs_0_, ...), custom_call_target="tpu_custom_call", output_to_operand_aliasing={{0}: (11, {}), {1}: (12, {}), {2}: (13, {}), {3}: (14, {})} | custom-call | flops 67108864 | bytes 2097152 | tf_op jit(solution)/shard_map/finish/pallas_call | solution.py:369
  (16 shorter events, 0.8 us)
Async XLA Ops:
  2.6 1.7 %collective-permute-start = (bf16[2,512,128]{2,1,0:T(8,128)(2,1)S(1)}, bf16[2,512,128]{2,1,0:T(8,128)(2,1)S(1)}, u32[]{:S(2)}, u32[]{:S(2)}) collective-permute-start(bf16[2,512,128]{2,1,0:T(8,128)(2,1)S(1)} %get-tuple-element.49), channel_id=1, source_target_pairs={{0,1},{1,0},{2,3},{3,2},{4,5},{5,4},{6,7},{7,6},{8,9},{9,8},{10,11... | collective-permute-start | bytes 786440 | tf_op jit(solution)/shard_map/ppermute | solution.py:386
  3.5 3.9 %collective-permute-start.2 = (bf16[2,512,128]{2,1,0:T(8,128)(2,1)S(1)}, bf16[2,512,128]{2,1,0:T(8,128)(2,1)S(1)}, u32[]{:S(2)}, u32[]{:S(2)}) collective-permute-start(bf16[2,512,128]{2,1,0:T(8,128)(2,1)S(1)} %sums.3), channel_id=1, source_target_pairs={{0,1},{1,0},{2,3},{3,2},{4,5},{5,4},{6,7},{7,6},{8,9},{9,8},{10,11... | collective-permute-start | bytes 786440 | tf_op jit(solution)/shard_map/ppermute | solution.py:386
  4.4 7.0 %collective-permute-start.1 = (bf16[2,256,128]{2,1,0:T(8,128)(2,1)S(1)}, bf16[2,256,128]{2,1,0:T(8,128)(2,1)S(1)}, u32[]{:S(2)}, u32[]{:S(2)}) collective-permute-start(bf16[2,256,128]{2,1,0:T(8,128)(2,1)S(1)} %get-tuple-element.51), channel_id=1, source_target_pairs={{0,2},{1,3},{2,0},{3,1},{4,6},{5,7},{6,4},{7,5},{8,10},{9,11},{10,... | collective-permute-start | bytes 393224 | tf_op jit(solution)/shard_map/ppermute | solution.py:386
  7.4 8.1 %collective-permute-start.3 = (bf16[2,256,128]{2,1,0:T(8,128)(2,1)S(1)}, bf16[2,256,128]{2,1,0:T(8,128)(2,1)S(1)}, u32[]{:S(2)}, u32[]{:S(2)}) collective-permute-start(bf16[2,256,128]{2,1,0:T(8,128)(2,1)S(1)} %get-tuple-element.53), channel_id=1, source_target_pairs={{0,4},{1,5},{2,6},{3,7},{4,0},{5,1},{6,2},{7,3},{8,12},{9,13},{10,... | collective-permute-start | bytes 393224 | tf_op jit(solution)/shard_map/ppermute | solution.py:386
  9.0 6.5 %collective-permute-start.4 = (bf16[2,256,128]{2,1,0:T(8,128)(2,1)S(1)}, bf16[2,256,128]{2,1,0:T(8,128)(2,1)S(1)}, u32[]{:S(2)}, u32[]{:S(2)}) collective-permute-start(bf16[2,256,128]{2,1,0:T(8,128)(2,1)S(1)} %get-tuple-element.54), channel_id=1, source_target_pairs={{0,6},{1,7},{2,4},{3,5},{4,2},{5,3},{6,0},{7,1},{8,14},{9,15},{10,... | collective-permute-start | bytes 393224 | tf_op jit(solution)/shard_map/ppermute | solution.py:386
  15.6 6.1 %collective-permute-start.5 = (bf16[256,128]{1,0:T(8,128)(2,1)S(1)}, bf16[256,128]{1,0:T(8,128)(2,1)S(1)}, u32[]{:S(2)}, u32[]{:S(2)}) collective-permute-start(bf16[256,128]{1,0:T(8,128)(2,1)S(1)} %get-tuple-element.67), channel_id=1, source_target_pairs={{0,24},{8,16},{16,8},{24,0},{1,25},{9,17},{17,9},{25,1},{2,26},{10... | collective-permute-start | bytes 196616 | tf_op jit(solution)/shard_map/ppermute | solution.py:386
  19.3 5.2 %collective-permute-start.6 = (bf16[256,128]{1,0:T(8,128)(2,1)S(1)}, bf16[256,128]{1,0:T(8,128)(2,1)S(1)}, u32[]{:S(2)}, u32[]{:S(2)}) collective-permute-start(bf16[256,128]{1,0:T(8,128)(2,1)S(1)} %get-tuple-element.68), channel_id=1, source_target_pairs={{0,16},{8,24},{16,0},{24,8},{1,17},{9,25},{17,1},{25,9},{2,18},{10... | collective-permute-start | bytes 196616 | tf_op jit(solution)/shard_map/ppermute | solution.py:386
  19.3 5.2 %collective-permute-start.7 = (bf16[256,128]{1,0:T(8,128)(2,1)S(1)}, bf16[256,128]{1,0:T(8,128)(2,1)S(1)}, u32[]{:S(2)}, u32[]{:S(2)}) collective-permute-start(bf16[256,128]{1,0:T(8,128)(2,1)S(1)} %get-tuple-element.69), channel_id=1, source_target_pairs={{0,8},{8,0},{16,24},{24,16},{1,9},{9,1},{17,25},{25,17},{2,10},{10... | collective-permute-start | bytes 196616 | tf_op jit(solution)/shard_map/ppermute | solution.py:386
  24.7 6.4 %collective-permute-start.10 = (bf16[2,256,128]{2,1,0:T(8,128)(2,1)S(1)}, bf16[2,256,128]{2,1,0:T(8,128)(2,1)S(1)}, u32[]{:S(2)}, u32[]{:S(2)}) collective-permute-start(bf16[2,256,128]{2,1,0:T(8,128)(2,1)S(1)} %get-tuple-element.73), channel_id=1, source_target_pairs={{0,2},{1,3},{2,0},{3,1},{4,6},{5,7},{6,4},{7,5},{8,10},{9,11},{10,... | collective-permute-start | bytes 393224 | tf_op jit(solution)/shard_map/ppermute | solution.py:386
  26.0 6.4 %collective-permute-start.8 = (bf16[2,256,128]{2,1,0:T(8,128)(2,1)S(1)}, bf16[2,256,128]{2,1,0:T(8,128)(2,1)S(1)}, u32[]{:S(2)}, u32[]{:S(2)}) collective-permute-start(bf16[2,256,128]{2,1,0:T(8,128)(2,1)S(1)} %get-tuple-element.70), channel_id=1, source_target_pairs={{0,4},{1,5},{2,6},{3,7},{4,0},{5,1},{6,2},{7,3},{8,12},{9,13},{10,... | collective-permute-start | bytes 393224 | tf_op jit(solution)/shard_map/ppermute | solution.py:386
  27.1 5.9 %collective-permute-start.9 = (bf16[2,256,128]{2,1,0:T(8,128)(2,1)S(1)}, bf16[2,256,128]{2,1,0:T(8,128)(2,1)S(1)}, u32[]{:S(2)}, u32[]{:S(2)}) collective-permute-start(bf16[2,256,128]{2,1,0:T(8,128)(2,1)S(1)} %get-tuple-element.71), channel_id=1, source_target_pairs={{0,6},{1,7},{2,4},{3,5},{4,2},{5,3},{6,0},{7,1},{8,14},{9,15},{10,... | collective-permute-start | bytes 393224 | tf_op jit(solution)/shard_map/ppermute | solution.py:386
  31.1 2.4 %collective-permute-start.12 = (bf16[2,512,128]{2,1,0:T(8,128)(2,1)S(1)}, bf16[2,512,128]{2,1,0:T(8,128)(2,1)S(1)}, u32[]{:S(2)}, u32[]{:S(2)}) collective-permute-start(bf16[2,512,128]{2,1,0:T(8,128)(2,1)S(1)} %theirs.3), channel_id=1, source_target_pairs={{0,1},{1,0},{2,3},{3,2},{4,5},{5,4},{6,7},{7,6},{8,9},{9,8},{10,11... | collective-permute-start | bytes 786440 | tf_op jit(solution)/shard_map/ppermute | solution.py:386
  33.0 1.6 %collective-permute-start.11 = (bf16[2,512,128]{2,1,0:T(8,128)(2,1)S(1)}, bf16[2,512,128]{2,1,0:T(8,128)(2,1)S(1)}, u32[]{:S(2)}, u32[]{:S(2)}) collective-permute-start(bf16[2,512,128]{2,1,0:T(8,128)(2,1)S(1)} %theirs.2), channel_id=1, source_target_pairs={{0,1},{1,0},{2,3},{3,2},{4,5},{5,4},{6,7},{7,6},{8,9},{9,8},{10,11... | collective-permute-start | bytes 786440 | tf_op jit(solution)/shard_map/ppermute | solution.py:386

commit v19 on v16

--- a/solution.py
+++ b/solution.py
@@ -56,13 +56,14 @@
     use(*last)
 
 
-def sums_of(tokens, start, out):
+def sums_of(tokens, start, out, kinds=(0, 1)):
     q, k, v, d = tokens
 
     def products():
         for n in range(out.shape[1] // HEAD):
             cols = pl.ds(start + n * HEAD, HEAD) if isinstance(start, int) else columns(start, n)
-            for which, (a, b) in enumerate(((k, v), (q, d))):
+            for which in kinds:
+                a, b = ((k, v), (q, d))[which]
                 yield (which, n), dot(a[:, cols], b[:, cols], 0, 0)
 
     def use(key, product):
@@ -74,17 +75,18 @@
 
 def load_kernel(*refs):
     tokens, held, (out, sems) = refs[:4], refs[4:8], refs[8:]
-    copies = [
-        pltpu.make_async_copy(ref, to, sems.at[i]) for i, (ref, to) in enumerate(zip(tokens, held))
-    ]
-    for copy in copies:
-        copy.start()
-    for copy in copies:
-        copy.wait()
+    copies = [pltpu.make_async_copy(tokens[i], held[i], sems.at[i]) for i in range(4)]
     width = held[0].shape[1]
     start = block_start(False, 0, width // 2)
-    for n in range(4):
-        pl.when(start == n * width // 4)(functools.partial(sums_of, held, n * width // 4, out))
+    pairs = ((1, 2), (0, 3))
+    for i in pairs[0] + pairs[1]:
+        copies[i].start()
+    for kind, pair in enumerate(pairs):
+        for i in pair:
+            copies[i].wait()
+        for n in range(4):
+            at = n * width // 4
+            pl.when(start == at)(functools.partial(sums_of, held, at, out, (kind,)))
 
 
 def load(tokens):
@@ -300,17 +302,22 @@
     one_ahead(products(), use)
 
 
-def copies_out(own, block, held, outs, sems):
-    size = held.shape[2]
-    start = block_start(own, block, outs[0].shape[1] // 2)
-    there = pl.ds(pl.multiple_of(start, size), size)
+def group_start(own, first, count, depth, half):
+    near, far = near_far()
+    side = near if own else 1 - near
+    return side * half + lax.div(far ^ first, count) * (count * depth)
+
+
+def copies_out(own, first, count, depth, held, outs, sems):
+    start = group_start(own, first, count, depth, outs[0].shape[1] // 2)
+    there = pl.ds(pl.multiple_of(start, count * depth), count * depth)
     return [
         pltpu.make_async_copy(held.at[i], out.at[:, there], sems.at[i])
         for i, out in enumerate(outs)
     ]
 
 
-def finish_kernel(scale, own, block, count, rests, hold, *refs):
+def finish_kernel(scale, own, first, count, rests, hold, *refs):
     tokens, local, slots, refs = refs[:4], refs[4:8], refs[8 : 8 + count], refs[8 + count :]
     got, refs = (refs[0], refs[1:]) if own else (None, refs)
     late, refs = refs[: len(rests)], refs[len(rests) :]
@@ -321,17 +328,16 @@
     width, depth = tokens[0].shape[1], slots[0].shape[1]
     copies = []
     for n, (rest, where) in enumerate(zip(late, rests)):
-        copies += copies_out(*where, rest, outs, sems.at[n + 1])
+        copies += copies_out(*where, depth, rest, outs, sems.at[n + 1])
     for copy in copies:
         copy.start()
 
     def store(rows, i, out):
         held[i, :, rows] = out
 
-    def run(quarter):
-        start = quarter * width // 4
-        core = quarter // 2 if own else 1 - quarter // 2
-        for s, slot in enumerate(slots):
+    def run(start):
+        core = start * 2 // width if own else 1 - start * 2 // width
+        for s, slot in enumerate(slots, first):
             part = slot_rows(s, count, depth)
             if own:
                 states[core, part] = slot[core]
@@ -340,26 +346,27 @@
                 states[:, part] = slot[...]
         all_products(scale, start, tokens, local, states, store)
 
-    start = block_start(own, block, width // 2)
-    for quarter in range(4):
-        pl.when(start == quarter * width // 4)(functools.partial(run, quarter))
+    start = group_start(own, first, count, depth, width // 2)
+    for at in range(0, width, count * depth):
+        pl.when(start == at)(functools.partial(run, at))
     if not hold:
-        last = copies_out(own, block, held, outs, sems.at[0])
+        last = copies_out(own, first, count, depth, held, outs, sems.at[0])
         for copy in last:
             copy.start()
         for copy in copies + last:
             copy.wait()
 
 
-def finish(own, block, tokens, local, slots, scale, got=(), rests=(), before=(), hold=False):
+def finish(own, first, tokens, local, slots, scale, got=(), rests=(), before=(), hold=False):
     rows, width = tokens[0].shape
+    count, depth = len(slots), slots[0].shape[1]
     out = jax.ShapeDtypeStruct((rows, width), BF16)
-    piece = pltpu.VMEM((4, rows, width // 4), BF16)
+    piece = pltpu.VMEM((4, rows, count * depth), BF16)
     inputs = [*tokens, *local, *slots, *got, *(x for _, x in rests)]
-    states = pltpu.VMEM((2, width // 4, HEAD), BF16)
+    states = pltpu.VMEM((2, count * depth, HEAD), BF16)
     wheres = [where for where, _ in rests]
     return pl.pallas_call(
-        functools.partial(finish_kernel, scale, own, block, len(slots), wheres, hold),
+        functools.partial(finish_kernel, scale, own, first, count, wheres, hold),
         name="finish",
         in_specs=[VMEM] * len(inputs) + [ANY] * len(before),
         out_specs=VMEM if hold else [ANY] * 4,
@@ -368,7 +375,9 @@
         + ([] if hold else [piece, pltpu.SemaphoreType.DMA((1 + len(rests), 4))]),
         input_output_aliases={len(inputs) + i: i for i in range(len(before))},
         cost_estimate=pl.CostEstimate(
-            flops=2 * rows * width * HEAD, bytes_accessed=8 * rows * width, transcendentals=0
+            flops=8 * rows * count * depth * HEAD,
+            bytes_accessed=32 * rows * count * depth,
+            transcendentals=0,
         ),
         compiler_params=SMALL,
     )(*inputs, *before)
@@ -395,20 +404,25 @@
     others = [swap(send, "outer", s) for s, send in zip(distances(outer_count), sends)]
     slots = swap_far(scan_slots(slots, others))
     half = far_count // 2
-    arrived, outs, rests = [], (), []
-    for block in range(2):
-        part = slots[block * half : (block + 1) * half]
-        if block:
-            part, outs = lax.optimization_barrier((part, tuple(outs)))
-        for s, slot in enumerate(part):
-            theirs = state_for_neighbour(block * half + s, half, slot, keep)
-            arrived.append(swap(theirs, "inner", 1))
-        made = finish(True, block, tokens, local, part, scale, got=got[block : block + 1], hold=block)
-        outs = outs or made
-    rests.append(((True, 1), made))
-    made = finish(False, 0, tokens, local, arrived[:half], scale, hold=True)
-    rests.append(((False, 0), made))
-    return tuple(finish(False, 1, tokens, local, arrived[half:], scale, rests=rests, before=outs))
+    arrived = []
+    for s in range(far_count):
+        if s == half:
+            outs = finish(True, 0, tokens, local, slots[:half], scale, got=got[:1])
+            slots[s], outs = lax.optimization_barrier((slots[s], tuple(outs)))
+        elif s > half:
+            slots[s], theirs = lax.optimization_barrier((slots[s], theirs))
+        theirs = state_for_neighbour(s, half, slots[s], keep)
+        arrived.append(swap(theirs, "inner", 1))
+    held = finish(True, half, tokens, local, slots[half:], scale, got=got[1:], hold=True)
+    rests = [((True, half, half), held)]
+    first, count, least = 0, half, max(1, HEAD // slots[0].shape[1])
+    while first + least < far_count:
+        group = arrived[first : first + count]
+        held = finish(False, first, tokens, local, group, scale, hold=True)
+        rests.append(((False, first, count), held))
+        first, count = first + count, max(count if first == 0 and half == least else count // 2, least)
+    last = arrived[first:]
+    return tuple(finish(False, first, tokens, local, last, scale, rests=rests, before=outs))
 
 
 def solution(mesh):

time: 35.9 us -> 36.1 us (level)
  waiting for transfers between devices: 12.2 us -> 11.6 us
  starting transfers between devices: 14.2 us -> 14.7 us
    ppermute x15, waiting for transfers between devices: 12.2 us -> 11.6 us  [swap(): lax.ppermute(x, axis, [(i, i ^ bits) for i in range(lax.axis_size(axis))])]
    ppermute x15, starting transfers between devices: 14.2 us -> 14.7 us  [swap(): lax.ppermute(x, axis, [(i, i ^ bits) for i in range(lax.axis_size(axis))])]
    pallas_call x4 -> x5, Pallas kernels: 3.33 us -> 3.63 us  [finish(): pl.pallas_call(functools.partial(finish_kernel, scale, own, first, count,...]
  transfers between devices with their start and end apart: 15 -> 15, of which waited for: 7 -> 5; matrix products, arithmetic and copies ran while one was open for 0% -> 0% of each run, Pallas kernels for 15% -> 15%
where the time goes in v19:
time: 36.1 us; the launch traced here: 35.9 us
  starting transfers between devices  14.7 us (41%)
  waiting for transfers between devices  11.6 us (32%)
  Pallas kernels  8.86 us (25%)
  between operations  0.79 us (2%)
    ppermute x15, starting transfers between devices, swap(): lax.ppermute(x, axis, [(i, i ^ bits) for i in range(lax.axis_size(axis))])  14.7 us
    ppermute x15, waiting for transfers between devices, swap(): lax.ppermute(x, axis, [(i, i ^ bits) for i in range(lax.axis_size(axis))])  11.6 us
    pallas_call x5, Pallas kernels, finish(): pl.pallas_call(functools.partial(finish_kernel, scale, own, first, count,...  3.63 us
    pallas_call x1, Pallas kernels, local_part(): pl.pallas_call(local_kernel, name='local', in_specs=[VMEM] * 4, out_specs...  2.16 us
    pallas_call x1, Pallas kernels, load(): pl.pallas_call(load_kernel, name='load', in_specs=[ANY] * 4, out_specs=[V...  1.77 us
    pallas_call x2, Pallas kernels, sums(): pl.pallas_call(functools.partial(sums_kernel, wanted), name='sums', in_sp...  0.75 us
  transfers between devices with their start and end apart: 15, of which 5 were waited for; matrix products, arithmetic and copies ran while one was open for 0% of the time, Pallas kernels for 15%

profile of v19, /device:TPU:0, one launch (start us, length us, event | category | flops | bytes accessed | tf_op | source)
XLA Modules:
  0.0 35.9 jit_solution(18035378757050710529)
XLA Ops:
  0.6 1.8 %load.1 = (bf16[128,2048]{1,0:T(8,128)(2,1)S(1)}, bf16[128,2048]{1,0:T(8,128)(2,1)S(1)}, bf16[128,2048]{1,0:T(8,128)(2,1)S(1)}, bf16[128,2048]{1,0:T(8,128)(2,1)S(1)}, bf16[2,512,128]{2,1,0:T(8,128)(2,1)S(1)}) custom-call(bf16[128,2048]{1,0:T(8,128)(2,1)} %refs_0_.1, bf16[128,2048]{1,0:T(8,128)(2,1)} %refs_1_.1, bf16[128,2048]{1,0:T(8,128)(2,1)} %refs_2_.1, ...), custom_call_target="tpu_custom_call" | custom-call | flops 33554432 | bytes 2621440 | tf_op jit(solution)/shard_map/load/pallas_call | solution.py:94
  2.4 0.5 %collective-permute-start = (bf16[2,512,128]{2,1,0:T(8,128)(2,1)S(1)}, bf16[2,512,128]{2,1,0:T(8,128)(2,1)S(1)}, u32[]{:S(2)}, u32[]{:S(2)}) collective-permute-start(bf16[2,512,128]{2,1,0:T(8,128)(2,1)S(1)} %get-tuple-element.49), channel_id=1, source_target_pairs={{0,1},{1,0},{2,3},{3,2},{4,5},{5,4},{6,7},{7,6},{8,9},{9,8},{10,11... | collective-permute-start | bytes 786440 | tf_op jit(solution)/shard_map/ppermute | solution.py:387
  3.3 0.5 %sums.2 = (bf16[2,512,128]{2,1,0:T(8,128)(2,1)S(1)}, bf16[2,512,128]{2,1,0:T(8,128)(2,1)S(1)}) custom-call(bf16[128,2048]{1,0:T(8,128)(2,1)S(1)} %get-tuple-element.44.refs_0_, bf16[128,2048]{1,0:T(8,128)(2,1)S(1)} %get-tuple-element.45.refs_1_, bf16[128,2048]{1,0:T(8,128)(2,1)S(1)} %get-tuple-element.46.refs_2_, bf16[128,2048]{1,0:T(8,128)(2,1)S(1)} %get-tuple-element.47.refs_3_), custom_call_target="tpu_custom_call" | custom-call | flops 67108864 | bytes 1572864 | tf_op jit(solution)/shard_map/sums/pallas_call | solution.py:116
  3.8 0.3 collective-permute-done.got_ref.refs_10_
  4.2 2.9 %collective-permute-start.1 = (bf16[2,256,128]{2,1,0:T(8,128)(2,1)S(1)}, bf16[2,256,128]{2,1,0:T(8,128)(2,1)S(1)}, u32[]{:S(2)}, u32[]{:S(2)}) collective-permute-start(bf16[2,256,128]{2,1,0:T(8,128)(2,1)S(1)} %get-tuple-element.51), channel_id=1, source_target_pairs={{0,2},{1,3},{2,0},{3,1},{4,6},{5,7},{6,4},{7,5},{8,10},{9,11},{10,... | collective-permute-start | bytes 393224 | tf_op jit(solution)/shard_map/ppermute | solution.py:387
  7.1 1.6 %collective-permute-start.3 = (bf16[2,256,128]{2,1,0:T(8,128)(2,1)S(1)}, bf16[2,256,128]{2,1,0:T(8,128)(2,1)S(1)}, u32[]{:S(2)}, u32[]{:S(2)}) collective-permute-start(bf16[2,256,128]{2,1,0:T(8,128)(2,1)S(1)} %get-tuple-element.53), channel_id=1, source_target_pairs={{0,4},{1,5},{2,6},{3,7},{4,0},{5,1},{6,2},{7,3},{8,12},{9,13},{10,... | collective-permute-start | bytes 393224 | tf_op jit(solution)/shard_map/ppermute | solution.py:387
  8.7 0.3 collective-permute-start.4
  9.0 2.2 %local.1 = (f32[128,2048]{1,0:T(8,128)S(1)}, f32[128,2048]{1,0:T(8,128)S(1)}, f32[128,2048]{1,0:T(8,128)S(1)}, f32[128,2048]{1,0:T(8,128)S(1)}) custom-call(bf16[128,2048]{1,0:T(8,128)(2,1)S(1)} %get-tuple-element.44.refs_0_, bf16[128,2048]{1,0:T(8,128)(2,1)S(1)} %get-tuple-element.45.refs_1_, bf16[128,2048]{1,0:T(8,128)(2,1)S(1)} %get-tuple-element.46.refs_2_, ...), custom_call_target="tpu_custom_call" | custom-call | flops 402653184 | bytes 6291456 | tf_op jit(solution)/shard_map/local/pallas_call | solution.py:272
  11.2 4.1 %collective-permute-done.3.refs_2_ = bf16[2,256,128]{2,1,0:T(8,128)(2,1)S(1)} collective-permute-done((bf16[2,256,128]{2,1,0:T(8,128)(2,1)S(1)}, bf16[2,256,128]{2,1,0:T(8,128)(2,1)S(1)}, u32[]{:S(2)}, u32[]{:S(2)}) %collective-permute-start.3) | collective-permute-done | bytes 131104 | tf_op jit(solution)/shard_map/ppermute | solution.py:387
  15.4 3.7 %collective-permute-start.5 = (bf16[256,128]{1,0:T(8,128)(2,1)S(1)}, bf16[256,128]{1,0:T(8,128)(2,1)S(1)}, u32[]{:S(2)}, u32[]{:S(2)}) collective-permute-start(bf16[256,128]{1,0:T(8,128)(2,1)S(1)} %get-tuple-element.67), channel_id=1, source_target_pairs={{0,24},{8,16},{16,8},{24,0},{1,25},{9,17},{17,9},{25,1},{2,26},{10... | collective-permute-start | bytes 196616 | tf_op jit(solution)/shard_map/ppermute | solution.py:387
  19.0 0.8 %collective-permute-start.7 = (bf16[256,128]{1,0:T(8,128)(2,1)S(1)}, bf16[256,128]{1,0:T(8,128)(2,1)S(1)}, u32[]{:S(2)}, u32[]{:S(2)}) collective-permute-start(bf16[256,128]{1,0:T(8,128)(2,1)S(1)} %get-tuple-element.69), channel_id=1, source_target_pairs={{0,8},{8,0},{16,24},{24,16},{1,9},{9,1},{17,25},{25,17},{2,10},{10... | collective-permute-start | bytes 196616 | tf_op jit(solution)/shard_map/ppermute | solution.py:387
  19.8 1.7 %collective-permute-done.5.refs_4_ = bf16[256,128]{1,0:T(8,128)(2,1)S(1)} collective-permute-done((bf16[256,128]{1,0:T(8,128)(2,1)S(1)}, bf16[256,128]{1,0:T(8,128)(2,1)S(1)}, u32[]{:S(2)}, u32[]{:S(2)}) %collective-permute-start.5) | collective-permute-done | bytes 65568 | tf_op jit(solution)/shard_map/ppermute | solution.py:387
  21.5 2.7 %collective-permute-done.6.refs_5_ = bf16[256,128]{1,0:T(8,128)(2,1)S(1)} collective-permute-done((bf16[256,128]{1,0:T(8,128)(2,1)S(1)}, bf16[256,128]{1,0:T(8,128)(2,1)S(1)}, u32[]{:S(2)}, u32[]{:S(2)}) %collective-permute-start.6) | collective-permute-done | bytes 65568 | tf_op jit(solution)/shard_map/ppermute | solution.py:387
  24.4 1.3 %collective-permute-start.10 = (bf16[2,256,128]{2,1,0:T(8,128)(2,1)S(1)}, bf16[2,256,128]{2,1,0:T(8,128)(2,1)S(1)}, u32[]{:S(2)}, u32[]{:S(2)}) collective-permute-start(bf16[2,256,128]{2,1,0:T(8,128)(2,1)S(1)} %get-tuple-element.73), channel_id=1, source_target_pairs={{0,2},{1,3},{2,0},{3,1},{4,6},{5,7},{6,4},{7,5},{8,10},{9,11},{10,... | collective-permute-start | bytes 393224 | tf_op jit(solution)/shard_map/ppermute | solution.py:387
  25.7 1.2 %collective-permute-start.9 = (bf16[2,256,128]{2,1,0:T(8,128)(2,1)S(1)}, bf16[2,256,128]{2,1,0:T(8,128)(2,1)S(1)}, u32[]{:S(2)}, u32[]{:S(2)}) collective-permute-start(bf16[2,256,128]{2,1,0:T(8,128)(2,1)S(1)} %get-tuple-element.71), channel_id=1, source_target_pairs={{0,4},{1,5},{2,6},{3,7},{4,0},{5,1},{6,2},{7,3},{8,12},{9,13},{10,... | collective-permute-start | bytes 393224 | tf_op jit(solution)/shard_map/ppermute | solution.py:387
  26.9 1.1 %collective-permute-start.8 = (bf16[2,256,128]{2,1,0:T(8,128)(2,1)S(1)}, bf16[2,256,128]{2,1,0:T(8,128)(2,1)S(1)}, u32[]{:S(2)}, u32[]{:S(2)}) collective-permute-start(bf16[2,256,128]{2,1,0:T(8,128)(2,1)S(1)} %get-tuple-element.70), channel_id=1, source_target_pairs={{0,6},{1,7},{2,4},{3,5},{4,2},{5,3},{6,0},{7,1},{8,14},{9,15},{10,... | collective-permute-start | bytes 393224 | tf_op jit(solution)/shard_map/ppermute | solution.py:387
  28.0 2.8 %collective-permute-done.10.refs_9_.slot = bf16[2,256,128]{2,1,0:T(8,128)(2,1)S(1)} collective-permute-done((bf16[2,256,128]{2,1,0:T(8,128)(2,1)S(1)}, bf16[2,256,128]{2,1,0:T(8,128)(2,1)S(1)}, u32[]{:S(2)}, u32[]{:S(2)}) %collective-permute-start.10) | collective-permute-done | bytes 131104 | tf_op jit(solution)/shard_map/ppermute | solution.py:387
  30.8 1.2 %finish.5 = (bf16[128,2048]{1,0:T(8,128)(2,1)}, bf16[128,2048]{1,0:T(8,128)(2,1)}, bf16[128,2048]{1,0:T(8,128)(2,1)}, bf16[128,2048]{1,0:T(8,128)(2,1)}) custom-call(bf16[128,2048]{1,0:T(8,128)(2,1)S(1)} %get-tuple-element.44.refs_0_, bf16[128,2048]{1,0:T(8,128)(2,1)S(1)} %get-tuple-element.45.refs_1_, bf16[128,2048]{1,0:T(8,128)(2,1)S(1)} %get-tuple-element.46.refs_2_, ...), custom_call_target="tpu_custom_call" | custom-call | flops 67108864 | bytes 2097152 | tf_op jit(solution)/shard_map/finish/pallas_call | solution.py:368
  32.2 0.5 %collective-permute-start.12 = (bf16[2,256,128]{2,1,0:T(8,128)(2,1)S(1)}, bf16[2,256,128]{2,1,0:T(8,128)(2,1)S(1)}, u32[]{:S(2)}, u32[]{:S(2)}) collective-permute-start(bf16[2,256,128]{2,1,0:T(8,128)(2,1)S(1)} %theirs.6), channel_id=1, source_target_pairs={{0,1},{1,0},{2,3},{3,2},{4,5},{5,4},{6,7},{7,6},{8,9},{9,8},{10,11... | collective-permute-start | bytes 393224 | tf_op jit(solution)/shard_map/ppermute | solution.py:387
  32.9 0.5 %collective-permute-start.11 = (bf16[2,256,128]{2,1,0:T(8,128)(2,1)S(1)}, bf16[2,256,128]{2,1,0:T(8,128)(2,1)S(1)}, u32[]{:S(2)}, u32[]{:S(2)}) collective-permute-start(bf16[2,256,128]{2,1,0:T(8,128)(2,1)S(1)} %theirs.5), channel_id=1, source_target_pairs={{0,1},{1,0},{2,3},{3,2},{4,5},{5,4},{6,7},{7,6},{8,9},{9,8},{10,11... | collective-permute-start | bytes 393224 | tf_op jit(solution)/shard_map/ppermute | solution.py:387
  33.5 0.4 %finish.6.refs_9_ = bf16[4,128,512]{2,1,0:T(8,128)(2,1)S(1)} custom-call(bf16[128,2048]{1,0:T(8,128)(2,1)S(1)} %get-tuple-element.44.refs_0_, bf16[128,2048]{1,0:T(8,128)(2,1)S(1)} %get-tuple-element.45.refs_1_, bf16[128,2048]{1,0:T(8,128)(2,1)S(1)} %get-tuple-element.46.refs_2_, bf16[128,2048]{1,0:T(8,128)(2,1)S(1)} %get-tuple-element.47.refs_3_, ...), custom_call_target="tpu_custom_call" | custom-call | flops 67108864 | bytes 2097152 | tf_op jit(solution)/shard_map/finish/pallas_call | solution.py:368
  33.9 0.3 finish.8.refs_11_
  34.2 0.4 %finish.7.refs_10_ = bf16[4,128,512]{2,1,0:T(8,128)(2,1)S(1)} custom-call(bf16[128,2048]{1,0:T(8,128)(2,1)S(1)} %get-tuple-element.44.refs_0_, bf16[128,2048]{1,0:T(8,128)(2,1)S(1)} %get-tuple-element.45.refs_1_, bf16[128,2048]{1,0:T(8,128)(2,1)S(1)} %get-tuple-element.46.refs_2_, bf16[128,2048]{1,0:T(8,128)(2,1)S(1)} %get-tuple-element.47.refs_3_, ...), custom_call_target="tpu_custom_call" | custom-call | flops 67108864 | bytes 2097152 | tf_op jit(solution)/shard_map/finish/pallas_call | solution.py:368
  34.6 1.3 %finish.9 = (bf16[128,2048]{1,0:T(8,128)(2,1)}, bf16[128,2048]{1,0:T(8,128)(2,1)}, bf16[128,2048]{1,0:T(8,128)(2,1)}, bf16[128,2048]{1,0:T(8,128)(2,1)}) custom-call(bf16[128,2048]{1,0:T(8,128)(2,1)S(1)} %get-tuple-element.44.refs_0_, ...), custom_call_target="tpu_custom_call", output_to_operand_aliasing={{0}: (12, {}), {1}: (13, {}), {2}: (14, {}), {3}: (15, {})} | custom-call | flops 33554432 | bytes 1048576 | tf_op jit(solution)/shard_map/finish/pallas_call | solution.py:368
  (23 shorter events, 1.2 us)
Async XLA Ops:
  2.4 1.7 %collective-permute-start = (bf16[2,512,128]{2,1,0:T(8,128)(2,1)S(1)}, bf16[2,512,128]{2,1,0:T(8,128)(2,1)S(1)}, u32[]{:S(2)}, u32[]{:S(2)}) collective-permute-start(bf16[2,512,128]{2,1,0:T(8,128)(2,1)S(1)} %get-tuple-element.49), channel_id=1, source_target_pairs={{0,1},{1,0},{2,3},{3,2},{4,5},{5,4},{6,7},{7,6},{8,9},{9,8},{10,11... | collective-permute-start | bytes 786440 | tf_op jit(solution)/shard_map/ppermute | solution.py:387
  3.2 3.9 %collective-permute-start.2 = (bf16[2,512,128]{2,1,0:T(8,128)(2,1)S(1)}, bf16[2,512,128]{2,1,0:T(8,128)(2,1)S(1)}, u32[]{:S(2)}, u32[]{:S(2)}) collective-permute-start(bf16[2,512,128]{2,1,0:T(8,128)(2,1)S(1)} %sums.3), channel_id=1, source_target_pairs={{0,1},{1,0},{2,3},{3,2},{4,5},{5,4},{6,7},{7,6},{8,9},{9,8},{10,11... | collective-permute-start | bytes 786440 | tf_op jit(solution)/shard_map/ppermute | solution.py:387
  4.2 7.0 %collective-permute-start.1 = (bf16[2,256,128]{2,1,0:T(8,128)(2,1)S(1)}, bf16[2,256,128]{2,1,0:T(8,128)(2,1)S(1)}, u32[]{:S(2)}, u32[]{:S(2)}) collective-permute-start(bf16[2,256,128]{2,1,0:T(8,128)(2,1)S(1)} %get-tuple-element.51), channel_id=1, source_target_pairs={{0,2},{1,3},{2,0},{3,1},{4,6},{5,7},{6,4},{7,5},{8,10},{9,11},{10,... | collective-permute-start | bytes 393224 | tf_op jit(solution)/shard_map/ppermute | solution.py:387
  7.1 8.1 %collective-permute-start.3 = (bf16[2,256,128]{2,1,0:T(8,128)(2,1)S(1)}, bf16[2,256,128]{2,1,0:T(8,128)(2,1)S(1)}, u32[]{:S(2)}, u32[]{:S(2)}) collective-permute-start(bf16[2,256,128]{2,1,0:T(8,128)(2,1)S(1)} %get-tuple-element.53), channel_id=1, source_target_pairs={{0,4},{1,5},{2,6},{3,7},{4,0},{5,1},{6,2},{7,3},{8,12},{9,13},{10,... | collective-permute-start | bytes 393224 | tf_op jit(solution)/shard_map/ppermute | solution.py:387
  8.7 6.6 %collective-permute-start.4 = (bf16[2,256,128]{2,1,0:T(8,128)(2,1)S(1)}, bf16[2,256,128]{2,1,0:T(8,128)(2,1)S(1)}, u32[]{:S(2)}, u32[]{:S(2)}) collective-permute-start(bf16[2,256,128]{2,1,0:T(8,128)(2,1)S(1)} %get-tuple-element.54), channel_id=1, source_target_pairs={{0,6},{1,7},{2,4},{3,5},{4,2},{5,3},{6,0},{7,1},{8,14},{9,15},{10,... | collective-permute-start | bytes 393224 | tf_op jit(solution)/shard_map/ppermute | solution.py:387
  15.4 6.1 %collective-permute-start.5 = (bf16[256,128]{1,0:T(8,128)(2,1)S(1)}, bf16[256,128]{1,0:T(8,128)(2,1)S(1)}, u32[]{:S(2)}, u32[]{:S(2)}) collective-permute-start(bf16[256,128]{1,0:T(8,128)(2,1)S(1)} %get-tuple-element.67), channel_id=1, source_target_pairs={{0,24},{8,16},{16,8},{24,0},{1,25},{9,17},{17,9},{25,1},{2,26},{10... | collective-permute-start | bytes 196616 | tf_op jit(solution)/shard_map/ppermute | solution.py:387
  19.0 5.2 %collective-permute-start.6 = (bf16[256,128]{1,0:T(8,128)(2,1)S(1)}, bf16[256,128]{1,0:T(8,128)(2,1)S(1)}, u32[]{:S(2)}, u32[]{:S(2)}) collective-permute-start(bf16[256,128]{1,0:T(8,128)(2,1)S(1)} %get-tuple-element.68), channel_id=1, source_target_pairs={{0,16},{8,24},{16,0},{24,8},{1,17},{9,25},{17,1},{25,9},{2,18},{10... | collective-permute-start | bytes 196616 | tf_op jit(solution)/shard_map/ppermute | solution.py:387
  19.0 5.2 %collective-permute-start.7 = (bf16[256,128]{1,0:T(8,128)(2,1)S(1)}, bf16[256,128]{1,0:T(8,128)(2,1)S(1)}, u32[]{:S(2)}, u32[]{:S(2)}) collective-permute-start(bf16[256,128]{1,0:T(8,128)(2,1)S(1)} %get-tuple-element.69), channel_id=1, source_target_pairs={{0,8},{8,0},{16,24},{24,16},{1,9},{9,1},{17,25},{25,17},{2,10},{10... | collective-permute-start | bytes 196616 | tf_op jit(solution)/shard_map/ppermute | solution.py:387
  24.4 6.4 %collective-permute-start.10 = (bf16[2,256,128]{2,1,0:T(8,128)(2,1)S(1)}, bf16[2,256,128]{2,1,0:T(8,128)(2,1)S(1)}, u32[]{:S(2)}, u32[]{:S(2)}) collective-permute-start(bf16[2,256,128]{2,1,0:T(8,128)(2,1)S(1)} %get-tuple-element.73), channel_id=1, source_target_pairs={{0,2},{1,3},{2,0},{3,1},{4,6},{5,7},{6,4},{7,5},{8,10},{9,11},{10,... | collective-permute-start | bytes 393224 | tf_op jit(solution)/shard_map/ppermute | solution.py:387
  25.7 6.3 %collective-permute-start.9 = (bf16[2,256,128]{2,1,0:T(8,128)(2,1)S(1)}, bf16[2,256,128]{2,1,0:T(8,128)(2,1)S(1)}, u32[]{:S(2)}, u32[]{:S(2)}) collective-permute-start(bf16[2,256,128]{2,1,0:T(8,128)(2,1)S(1)} %get-tuple-element.71), channel_id=1, source_target_pairs={{0,4},{1,5},{2,6},{3,7},{4,0},{5,1},{6,2},{7,3},{8,12},{9,13},{10,... | collective-permute-start | bytes 393224 | tf_op jit(solution)/shard_map/ppermute | solution.py:387
  26.9 6.0 %collective-permute-start.8 = (bf16[2,256,128]{2,1,0:T(8,128)(2,1)S(1)}, bf16[2,256,128]{2,1,0:T(8,128)(2,1)S(1)}, u32[]{:S(2)}, u32[]{:S(2)}) collective-permute-start(bf16[2,256,128]{2,1,0:T(8,128)(2,1)S(1)} %get-tuple-element.70), channel_id=1, source_target_pairs={{0,6},{1,7},{2,4},{3,5},{4,2},{5,3},{6,0},{7,1},{8,14},{9,15},{10,... | collective-permute-start | bytes 393224 | tf_op jit(solution)/shard_map/ppermute | solution.py:387
  32.1 1.8 %collective-permute-start.14 = (bf16[2,256,128]{2,1,0:T(8,128)(2,1)S(1)}, bf16[2,256,128]{2,1,0:T(8,128)(2,1)S(1)}, u32[]{:S(2)}, u32[]{:S(2)}) collective-permute-start(bf16[2,256,128]{2,1,0:T(8,128)(2,1)S(1)} %theirs.4), channel_id=1, source_target_pairs={{0,1},{1,0},{2,3},{3,2},{4,5},{5,4},{6,7},{7,6},{8,9},{9,8},{10,11... | collective-permute-start | bytes 393224 | tf_op jit(solution)/shard_map/ppermute | solution.py:387
  32.2 2.0 %collective-permute-start.12 = (bf16[2,256,128]{2,1,0:T(8,128)(2,1)S(1)}, bf16[2,256,128]{2,1,0:T(8,128)(2,1)S(1)}, u32[]{:S(2)}, u32[]{:S(2)}) collective-permute-start(bf16[2,256,128]{2,1,0:T(8,128)(2,1)S(1)} %theirs.6), channel_id=1, source_target_pairs={{0,1},{1,0},{2,3},{3,2},{4,5},{5,4},{6,7},{7,6},{8,9},{9,8},{10,11... | collective-permute-start | bytes 393224 | tf_op jit(solution)/shard_map/ppermute | solution.py:387
  32.8 1.4 %collective-permute-start.13 = (bf16[2,256,128]{2,1,0:T(8,128)(2,1)S(1)}, bf16[2,256,128]{2,1,0:T(8,128)(2,1)S(1)}, u32[]{:S(2)}, u32[]{:S(2)}) collective-permute-start(bf16[2,256,128]{2,1,0:T(8,128)(2,1)S(1)} %theirs.7), channel_id=1, source_target_pairs={{0,1},{1,0},{2,3},{3,2},{4,5},{5,4},{6,7},{7,6},{8,9},{9,8},{10,11... | collective-permute-start | bytes 393224 | tf_op jit(solution)/shard_map/ppermute | solution.py:387
  32.9 1.7 %collective-permute-start.11 = (bf16[2,256,128]{2,1,0:T(8,128)(2,1)S(1)}, bf16[2,256,128]{2,1,0:T(8,128)(2,1)S(1)}, u32[]{:S(2)}, u32[]{:S(2)}) collective-permute-start(bf16[2,256,128]{2,1,0:T(8,128)(2,1)S(1)} %theirs.5), channel_id=1, source_target_pairs={{0,1},{1,0},{2,3},{3,2},{4,5},{5,4},{6,7},{7,6},{8,9},{9,8},{10,11... | collective-permute-start | bytes 393224 | tf_op jit(solution)/shard_map/ppermute | solution.py:387

commit v20 on v17

--- a/solution.py
+++ b/solution.py
@@ -56,13 +56,14 @@
     use(*last)
 
 
-def sums_of(tokens, start, out):
+def sums_of(tokens, start, out, kinds=(0, 1)):
     q, k, v, d = tokens
 
     def products():
         for n in range(out.shape[1] // HEAD):
             cols = pl.ds(start + n * HEAD, HEAD) if isinstance(start, int) else columns(start, n)
-            for which, (a, b) in enumerate(((k, v), (q, d))):
+            for which in kinds:
+                a, b = ((k, v), (q, d))[which]
                 yield (which, n), dot(a[:, cols], b[:, cols], 0, 0)
 
     def use(key, product):
@@ -74,17 +75,18 @@
 
 def load_kernel(*refs):
     tokens, held, (out, sems) = refs[:4], refs[4:8], refs[8:]
-    copies = [
-        pltpu.make_async_copy(ref, to, sems.at[i]) for i, (ref, to) in enumerate(zip(tokens, held))
-    ]
-    for copy in copies:
-        copy.start()
-    for copy in copies:
-        copy.wait()
+    copies = [pltpu.make_async_copy(tokens[i], held[i], sems.at[i]) for i in range(4)]
     width = held[0].shape[1]
     start = block_start(False, 0, width // 2)
-    for n in range(4):
-        pl.when(start == n * width // 4)(functools.partial(sums_of, held, n * width // 4, out))
+    pairs = ((1, 2), (0, 3))
+    for i in pairs[0] + pairs[1]:
+        copies[i].start()
+    for kind, pair in enumerate(pairs):
+        for i in pair:
+            copies[i].wait()
+        for n in range(4):
+            at = n * width // 4
+            pl.when(start == at)(functools.partial(sums_of, held, at, out, (kind,)))
 
 
 def load(tokens):
@@ -320,10 +322,10 @@
         refs, states = refs[:-1], refs[-1]
     else:
         states = slots[0]
-    if hold:
-        (held,) = refs
-    else:
-        outs, (held, sems) = refs[-6:-2], refs[-2:]
+    if not hold or rests:
+        *refs, sems = refs
+    *refs, held = refs
+    outs = refs[-4:]
     width = tokens[0].shape[1]
     copies = []
     for n, (rest, where) in enumerate(zip(late, rests)):
@@ -362,14 +364,16 @@
     inputs = [*tokens, *local, *slots, *got, *(x for _, x in rests)]
     states = pltpu.VMEM((2, width // 4, HEAD), BF16)
     wheres = [where for where, _ in rests]
+    writes = not hold or bool(rests)
     return pl.pallas_call(
         functools.partial(finish_kernel, scale, own, block, len(slots), wheres, hold),
         name="finish",
         in_specs=[VMEM] * len(inputs) + [ANY] * len(before),
-        out_specs=VMEM if hold else [ANY] * 4,
-        out_shape=piece if hold else [out] * 4,
-        scratch_shapes=([] if hold else [piece, pltpu.SemaphoreType.DMA((2 + len(rests), 4))])
-        + ([states] if own else []),
+        out_specs=[ANY] * 4 * writes + [VMEM] * hold,
+        out_shape=[out] * 4 * writes + [piece] * hold,
+        scratch_shapes=[piece] * (not hold)
+        + [pltpu.SemaphoreType.DMA((2 + len(rests), 4))] * writes
+        + [states] * own,
         input_output_aliases={len(inputs) + i: i for i in range(len(before))},
         cost_estimate=pl.CostEstimate(
             flops=2 * rows * width * HEAD, bytes_accessed=8 * rows * width, transcendentals=0
@@ -407,10 +411,13 @@
     outs = finish(True, 0, tokens, local, slots[:half], scale, got=got[:1])
     part, outs = lax.optimization_barrier((slots[half:], tuple(outs)))
     arrived.append(near_swap(1, part))
-    rest = finish(False, 0, tokens, local, arrived[:1], scale, hold=True)
+    (rest,) = finish(True, 1, tokens, local, part, scale, got=got[1:], hold=True)
+    rests = [((True, 1), rest)]
+    *outs, rest = finish(
+        False, 0, tokens, local, arrived[:1], scale, rests=rests, before=outs, hold=True
+    )
     rests = [((False, 0), rest)]
-    outs = finish(True, 1, tokens, local, part, scale, got=got[1:], rests=rests, before=outs)
-    return tuple(finish(False, 1, tokens, local, arrived[1:], scale, before=outs))
+    return tuple(finish(False, 1, tokens, local, arrived[1:], scale, rests=rests, before=outs))
 
 
 def solution(mesh):

time: 35.9 us -> 35.7 us (level)
  transfers between devices with their start and end apart: 13 -> 13, of which waited for: 6 -> 7; matrix products, arithmetic and copies ran while one was open for 0% -> 0% of each run, Pallas kernels for 17% -> 16%
where the time goes in v20:
time: 35.7 us; the launch traced here: 35.6 us
  starting transfers between devices  13.6 us (38%)
  waiting for transfers between devices  12.3 us (34%)
  Pallas kernels  8.87 us (25%)
  between operations  0.76 us (2%)
    ppermute x13, starting transfers between devices, swap(): lax.ppermute(x, axis, [(i, i ^ bits) for i in range(lax.axis_size(axis))])  13.6 us
    ppermute x13, waiting for transfers between devices, swap(): lax.ppermute(x, axis, [(i, i ^ bits) for i in range(lax.axis_size(axis))])  12.3 us
    pallas_call x4, Pallas kernels, finish(): pl.pallas_call(functools.partial(finish_kernel, scale, own, block, len(sl...  3.69 us
    pallas_call x1, Pallas kernels, local_part(): pl.pallas_call(local_kernel, name='local', in_specs=[VMEM] * 4, out_specs...  2.16 us
    pallas_call x1, Pallas kernels, load(): pl.pallas_call(load_kernel, name='load', in_specs=[ANY] * 4, out_specs=[V...  1.77 us
    pallas_call x2, Pallas kernels, sums(): pl.pallas_call(functools.partial(sums_kernel, wanted), name='sums', in_sp...  0.75 us
  transfers between devices with their start and end apart: 13, of which 7 were waited for; matrix products, arithmetic and copies ran while one was open for 0% of the time, Pallas kernels for 16%

profile of v20, /device:TPU:0, one launch (start us, length us, event | category | flops | bytes accessed | tf_op | source)
XLA Modules:
  0.0 35.6 jit_solution(15676190918768996483)
XLA Ops:
  0.6 1.8 %load.1 = (bf16[128,2048]{1,0:T(8,128)(2,1)S(1)}, bf16[128,2048]{1,0:T(8,128)(2,1)S(1)}, bf16[128,2048]{1,0:T(8,128)(2,1)S(1)}, bf16[128,2048]{1,0:T(8,128)(2,1)S(1)}, bf16[2,512,128]{2,1,0:T(8,128)(2,1)S(1)}) custom-call(bf16[128,2048]{1,0:T(8,128)(2,1)} %refs_0_.1, bf16[128,2048]{1,0:T(8,128)(2,1)} %refs_1_.1, bf16[128,2048]{1,0:T(8,128)(2,1)} %refs_2_.1, ...), custom_call_target="tpu_custom_call" | custom-call | flops 33554432 | bytes 2621440 | tf_op jit(solution)/shard_map/load/pallas_call | solution.py:94
  2.4 0.5 %collective-permute-start = (bf16[2,512,128]{2,1,0:T(8,128)(2,1)S(1)}, bf16[2,512,128]{2,1,0:T(8,128)(2,1)S(1)}, u32[]{:S(2)}, u32[]{:S(2)}) collective-permute-start(bf16[2,512,128]{2,1,0:T(8,128)(2,1)S(1)} %get-tuple-element.54), channel_id=1, source_target_pairs={{0,1},{1,0},{2,3},{3,2},{4,5},{5,4},{6,7},{7,6},{8,9},{9,8},{10,11... | collective-permute-start | bytes 786440 | tf_op jit(solution)/shard_map/ppermute | solution.py:386
  2.9 0.3 sums.3
  3.3 0.5 %sums.2 = (bf16[2,512,128]{2,1,0:T(8,128)(2,1)S(1)}, bf16[2,512,128]{2,1,0:T(8,128)(2,1)S(1)}) custom-call(bf16[128,2048]{1,0:T(8,128)(2,1)S(1)} %get-tuple-element.49.refs_0_, bf16[128,2048]{1,0:T(8,128)(2,1)S(1)} %get-tuple-element.50.refs_1_, bf16[128,2048]{1,0:T(8,128)(2,1)S(1)} %get-tuple-element.51.refs_2_, bf16[128,2048]{1,0:T(8,128)(2,1)S(1)} %get-tuple-element.52.refs_3_), custom_call_target="tpu_custom_call" | custom-call | flops 67108864 | bytes 1572864 | tf_op jit(solution)/shard_map/sums/pallas_call | solution.py:116
  3.8 0.3 collective-permute-done.got_ref.refs_10_
  4.2 2.9 %collective-permute-start.1 = (bf16[2,256,128]{2,1,0:T(8,128)(2,1)S(1)}, bf16[2,256,128]{2,1,0:T(8,128)(2,1)S(1)}, u32[]{:S(2)}, u32[]{:S(2)}) collective-permute-start(bf16[2,256,128]{2,1,0:T(8,128)(2,1)S(1)} %get-tuple-element.56), channel_id=1, source_target_pairs={{0,2},{1,3},{2,0},{3,1},{4,6},{5,7},{6,4},{7,5},{8,10},{9,11},{10,... | collective-permute-start | bytes 393224 | tf_op jit(solution)/shard_map/ppermute | solution.py:386
  7.1 1.6 %collective-permute-start.3 = (bf16[2,256,128]{2,1,0:T(8,128)(2,1)S(1)}, bf16[2,256,128]{2,1,0:T(8,128)(2,1)S(1)}, u32[]{:S(2)}, u32[]{:S(2)}) collective-permute-start(bf16[2,256,128]{2,1,0:T(8,128)(2,1)S(1)} %get-tuple-element.58), channel_id=1, source_target_pairs={{0,4},{1,5},{2,6},{3,7},{4,0},{5,1},{6,2},{7,3},{8,12},{9,13},{10,... | collective-permute-start | bytes 393224 | tf_op jit(solution)/shard_map/ppermute | solution.py:386
  8.7 0.3 collective-permute-start.4
  9.0 2.2 %local.1 = (f32[128,2048]{1,0:T(8,128)S(1)}, f32[128,2048]{1,0:T(8,128)S(1)}, f32[128,2048]{1,0:T(8,128)S(1)}, f32[128,2048]{1,0:T(8,128)S(1)}) custom-call(bf16[128,2048]{1,0:T(8,128)(2,1)S(1)} %get-tuple-element.49.refs_0_, bf16[128,2048]{1,0:T(8,128)(2,1)S(1)} %get-tuple-element.50.refs_1_, bf16[128,2048]{1,0:T(8,128)(2,1)S(1)} %get-tuple-element.51.refs_2_, ...), custom_call_target="tpu_custom_call" | custom-call | flops 402653184 | bytes 6291456 | tf_op jit(solution)/shard_map/local/pallas_call | solution.py:274
  11.2 4.1 %collective-permute-done.3.refs_2_ = bf16[2,256,128]{2,1,0:T(8,128)(2,1)S(1)} collective-permute-done((bf16[2,256,128]{2,1,0:T(8,128)(2,1)S(1)}, bf16[2,256,128]{2,1,0:T(8,128)(2,1)S(1)}, u32[]{:S(2)}, u32[]{:S(2)}) %collective-permute-start.3) | collective-permute-done | bytes 131104 | tf_op jit(solution)/shard_map/ppermute | solution.py:386
  15.4 3.7 %collective-permute-start.5 = (bf16[256,128]{1,0:T(8,128)(2,1)S(1)}, bf16[256,128]{1,0:T(8,128)(2,1)S(1)}, u32[]{:S(2)}, u32[]{:S(2)}) collective-permute-start(bf16[256,128]{1,0:T(8,128)(2,1)S(1)} %get-tuple-element.72), channel_id=1, source_target_pairs={{0,24},{8,16},{16,8},{24,0},{1,25},{9,17},{17,9},{25,1},{2,26},{10... | collective-permute-start | bytes 196616 | tf_op jit(solution)/shard_map/ppermute | solution.py:386
  19.0 0.8 %collective-permute-start.7 = (bf16[256,128]{1,0:T(8,128)(2,1)S(1)}, bf16[256,128]{1,0:T(8,128)(2,1)S(1)}, u32[]{:S(2)}, u32[]{:S(2)}) collective-permute-start(bf16[256,128]{1,0:T(8,128)(2,1)S(1)} %get-tuple-element.74), channel_id=1, source_target_pairs={{0,8},{8,0},{16,24},{24,16},{1,9},{9,1},{17,25},{25,17},{2,10},{10... | collective-permute-start | bytes 196616 | tf_op jit(solution)/shard_map/ppermute | solution.py:386
  19.8 1.7 %collective-permute-done.5.refs_4_ = bf16[256,128]{1,0:T(8,128)(2,1)S(1)} collective-permute-done((bf16[256,128]{1,0:T(8,128)(2,1)S(1)}, bf16[256,128]{1,0:T(8,128)(2,1)S(1)}, u32[]{:S(2)}, u32[]{:S(2)}) %collective-permute-start.5) | collective-permute-done | bytes 65568 | tf_op jit(solution)/shard_map/ppermute | solution.py:386
  21.5 2.7 %collective-permute-done.6.refs_5_ = bf16[256,128]{1,0:T(8,128)(2,1)S(1)} collective-permute-done((bf16[256,128]{1,0:T(8,128)(2,1)S(1)}, bf16[256,128]{1,0:T(8,128)(2,1)S(1)}, u32[]{:S(2)}, u32[]{:S(2)}) %collective-permute-start.6) | collective-permute-done | bytes 65568 | tf_op jit(solution)/shard_map/ppermute | solution.py:386
  24.2 0.2 scan.1
  24.4 1.3 %collective-permute-start.10 = (bf16[2,256,128]{2,1,0:T(8,128)(2,1)S(1)}, bf16[2,256,128]{2,1,0:T(8,128)(2,1)S(1)}, u32[]{:S(2)}, u32[]{:S(2)}) collective-permute-start(bf16[2,256,128]{2,1,0:T(8,128)(2,1)S(1)} %get-tuple-element.78), channel_id=1, source_target_pairs={{0,2},{1,3},{2,0},{3,1},{4,6},{5,7},{6,4},{7,5},{8,10},{9,11},{10,... | collective-permute-start | bytes 393224 | tf_op jit(solution)/shard_map/ppermute | solution.py:386
  25.7 1.2 %collective-permute-start.8 = (bf16[2,256,128]{2,1,0:T(8,128)(2,1)S(1)}, bf16[2,256,128]{2,1,0:T(8,128)(2,1)S(1)}, u32[]{:S(2)}, u32[]{:S(2)}) collective-permute-start(bf16[2,256,128]{2,1,0:T(8,128)(2,1)S(1)} %get-tuple-element.75), channel_id=1, source_target_pairs={{0,4},{1,5},{2,6},{3,7},{4,0},{5,1},{6,2},{7,3},{8,12},{9,13},{10,... | collective-permute-start | bytes 393224 | tf_op jit(solution)/shard_map/ppermute | solution.py:386
  26.9 1.1 %collective-permute-start.9 = (bf16[2,256,128]{2,1,0:T(8,128)(2,1)S(1)}, bf16[2,256,128]{2,1,0:T(8,128)(2,1)S(1)}, u32[]{:S(2)}, u32[]{:S(2)}) collective-permute-start(bf16[2,256,128]{2,1,0:T(8,128)(2,1)S(1)} %get-tuple-element.76), channel_id=1, source_target_pairs={{0,6},{1,7},{2,4},{3,5},{4,2},{5,3},{6,0},{7,1},{8,14},{9,15},{10,... | collective-permute-start | bytes 393224 | tf_op jit(solution)/shard_map/ppermute | solution.py:386
  28.0 2.8 %collective-permute-done.10.refs_9_.refs_1_ = bf16[2,256,128]{2,1,0:T(8,128)(2,1)S(1)} collective-permute-done((bf16[2,256,128]{2,1,0:T(8,128)(2,1)S(1)}, bf16[2,256,128]{2,1,0:T(8,128)(2,1)S(1)}, u32[]{:S(2)}, u32[]{:S(2)}) %collective-permute-start.10) | collective-permute-done | bytes 131104 | tf_op jit(solution)/shard_map/ppermute | solution.py:386
  30.9 1.2 %finish.4 = (bf16[128,2048]{1,0:T(8,128)(2,1)}, bf16[128,2048]{1,0:T(8,128)(2,1)}, bf16[128,2048]{1,0:T(8,128)(2,1)}, bf16[128,2048]{1,0:T(8,128)(2,1)}) custom-call(bf16[128,2048]{1,0:T(8,128)(2,1)S(1)} %get-tuple-element.49.refs_0_, bf16[128,2048]{1,0:T(8,128)(2,1)S(1)} %get-tuple-element.50.refs_1_, bf16[128,2048]{1,0:T(8,128)(2,1)S(1)} %get-tuple-element.51.refs_2_, ...), custom_call_target="tpu_custom_call" | custom-call | flops 67108864 | bytes 2097152 | tf_op jit(solution)/shard_map/finish/pallas_call | solution.py:368
  32.1 0.6 %collective-permute-done.9.refs_1_.refs_9_ = bf16[2,256,128]{2,1,0:T(8,128)(2,1)S(1)} collective-permute-done((bf16[2,256,128]{2,1,0:T(8,128)(2,1)S(1)}, bf16[2,256,128]{2,1,0:T(8,128)(2,1)S(1)}, u32[]{:S(2)}, u32[]{:S(2)}) %collective-permute-start.9) | collective-permute-done | bytes 131104 | tf_op jit(solution)/shard_map/ppermute | solution.py:386
  32.9 0.4 %finish.5.refs_9_ = bf16[4,128,512]{2,1,0:T(8,128)(2,1)S(1)} custom-call(bf16[128,2048]{1,0:T(8,128)(2,1)S(1)} %get-tuple-element.49.refs_0_, bf16[128,2048]{1,0:T(8,128)(2,1)S(1)} %get-tuple-element.50.refs_1_, bf16[128,2048]{1,0:T(8,128)(2,1)S(1)} %get-tuple-element.51.refs_2_, bf16[128,2048]{1,0:T(8,128)(2,1)S(1)} %get-tuple-element.52.refs_3_, ...), custom_call_target="tpu_custom_call" | custom-call | flops 67108864 | bytes 2097152 | tf_op jit(solution)/shard_map/finish/pallas_call | solution.py:368
  33.3 0.9 %finish.6 = (bf16[128,2048]{1,0:T(8,128)(2,1)}, bf16[128,2048]{1,0:T(8,128)(2,1)}, bf16[128,2048]{1,0:T(8,128)(2,1)}, bf16[128,2048]{1,0:T(8,128)(2,1)}, bf16[4,128,512]{2,1,0:T(8,128)(2,1)S(1)}) custom-call(bf16[128,2048]{1,0:T(8,128)(2,1)S(1)} %get-tuple-element.49.refs_0_, ...), custom_call_target="tpu_custom_call", output_to_operand_aliasing={{0}: (10, {}), {1}: (11, {}), {2}: (12, {}), {3}: (13, {})} | custom-call | flops 67108864 | bytes 2097152 | tf_op jit(solution)/shard_map/finish/pallas_call | solution.py:368
  34.4 1.2 %finish.7 = (bf16[128,2048]{1,0:T(8,128)(2,1)}, bf16[128,2048]{1,0:T(8,128)(2,1)}, bf16[128,2048]{1,0:T(8,128)(2,1)}, bf16[128,2048]{1,0:T(8,128)(2,1)}) custom-call(bf16[128,2048]{1,0:T(8,128)(2,1)S(1)} %get-tuple-element.49.refs_0_, ...), custom_call_target="tpu_custom_call", output_to_operand_aliasing={{0}: (10, {}), {1}: (11, {}), {2}: (12, {}), {3}: (13, {})} | custom-call | flops 67108864 | bytes 2097152 | tf_op jit(solution)/shard_map/finish/pallas_call | solution.py:368
  (16 shorter events, 0.7 us)
Async XLA Ops:
  2.4 1.7 %collective-permute-start = (bf16[2,512,128]{2,1,0:T(8,128)(2,1)S(1)}, bf16[2,512,128]{2,1,0:T(8,128)(2,1)S(1)}, u32[]{:S(2)}, u32[]{:S(2)}) collective-permute-start(bf16[2,512,128]{2,1,0:T(8,128)(2,1)S(1)} %get-tuple-element.54), channel_id=1, source_target_pairs={{0,1},{1,0},{2,3},{3,2},{4,5},{5,4},{6,7},{7,6},{8,9},{9,8},{10,11... | collective-permute-start | bytes 786440 | tf_op jit(solution)/shard_map/ppermute | solution.py:386
  3.2 3.9 %collective-permute-start.2 = (bf16[2,512,128]{2,1,0:T(8,128)(2,1)S(1)}, bf16[2,512,128]{2,1,0:T(8,128)(2,1)S(1)}, u32[]{:S(2)}, u32[]{:S(2)}) collective-permute-start(bf16[2,512,128]{2,1,0:T(8,128)(2,1)S(1)} %sums.3), channel_id=1, source_target_pairs={{0,1},{1,0},{2,3},{3,2},{4,5},{5,4},{6,7},{7,6},{8,9},{9,8},{10,11... | collective-permute-start | bytes 786440 | tf_op jit(solution)/shard_map/ppermute | solution.py:386
  4.2 7.0 %collective-permute-start.1 = (bf16[2,256,128]{2,1,0:T(8,128)(2,1)S(1)}, bf16[2,256,128]{2,1,0:T(8,128)(2,1)S(1)}, u32[]{:S(2)}, u32[]{:S(2)}) collective-permute-start(bf16[2,256,128]{2,1,0:T(8,128)(2,1)S(1)} %get-tuple-element.56), channel_id=1, source_target_pairs={{0,2},{1,3},{2,0},{3,1},{4,6},{5,7},{6,4},{7,5},{8,10},{9,11},{10,... | collective-permute-start | bytes 393224 | tf_op jit(solution)/shard_map/ppermute | solution.py:386
  7.1 8.1 %collective-permute-start.3 = (bf16[2,256,128]{2,1,0:T(8,128)(2,1)S(1)}, bf16[2,256,128]{2,1,0:T(8,128)(2,1)S(1)}, u32[]{:S(2)}, u32[]{:S(2)}) collective-permute-start(bf16[2,256,128]{2,1,0:T(8,128)(2,1)S(1)} %get-tuple-element.58), channel_id=1, source_target_pairs={{0,4},{1,5},{2,6},{3,7},{4,0},{5,1},{6,2},{7,3},{8,12},{9,13},{10,... | collective-permute-start | bytes 393224 | tf_op jit(solution)/shard_map/ppermute | solution.py:386
  8.7 6.6 %collective-permute-start.4 = (bf16[2,256,128]{2,1,0:T(8,128)(2,1)S(1)}, bf16[2,256,128]{2,1,0:T(8,128)(2,1)S(1)}, u32[]{:S(2)}, u32[]{:S(2)}) collective-permute-start(bf16[2,256,128]{2,1,0:T(8,128)(2,1)S(1)} %get-tuple-element.59), channel_id=1, source_target_pairs={{0,6},{1,7},{2,4},{3,5},{4,2},{5,3},{6,0},{7,1},{8,14},{9,15},{10,... | collective-permute-start | bytes 393224 | tf_op jit(solution)/shard_map/ppermute | solution.py:386
  15.4 6.1 %collective-permute-start.5 = (bf16[256,128]{1,0:T(8,128)(2,1)S(1)}, bf16[256,128]{1,0:T(8,128)(2,1)S(1)}, u32[]{:S(2)}, u32[]{:S(2)}) collective-permute-start(bf16[256,128]{1,0:T(8,128)(2,1)S(1)} %get-tuple-element.72), channel_id=1, source_target_pairs={{0,24},{8,16},{16,8},{24,0},{1,25},{9,17},{17,9},{25,1},{2,26},{10... | collective-permute-start | bytes 196616 | tf_op jit(solution)/shard_map/ppermute | solution.py:386
  19.0 5.2 %collective-permute-start.6 = (bf16[256,128]{1,0:T(8,128)(2,1)S(1)}, bf16[256,128]{1,0:T(8,128)(2,1)S(1)}, u32[]{:S(2)}, u32[]{:S(2)}) collective-permute-start(bf16[256,128]{1,0:T(8,128)(2,1)S(1)} %get-tuple-element.73), channel_id=1, source_target_pairs={{0,16},{8,24},{16,0},{24,8},{1,17},{9,25},{17,1},{25,9},{2,18},{10... | collective-permute-start | bytes 196616 | tf_op jit(solution)/shard_map/ppermute | solution.py:386
  19.0 5.2 %collective-permute-start.7 = (bf16[256,128]{1,0:T(8,128)(2,1)S(1)}, bf16[256,128]{1,0:T(8,128)(2,1)S(1)}, u32[]{:S(2)}, u32[]{:S(2)}) collective-permute-start(bf16[256,128]{1,0:T(8,128)(2,1)S(1)} %get-tuple-element.74), channel_id=1, source_target_pairs={{0,8},{8,0},{16,24},{24,16},{1,9},{9,1},{17,25},{25,17},{2,10},{10... | collective-permute-start | bytes 196616 | tf_op jit(solution)/shard_map/ppermute | solution.py:386
  24.4 6.4 %collective-permute-start.10 = (bf16[2,256,128]{2,1,0:T(8,128)(2,1)S(1)}, bf16[2,256,128]{2,1,0:T(8,128)(2,1)S(1)}, u32[]{:S(2)}, u32[]{:S(2)}) collective-permute-start(bf16[2,256,128]{2,1,0:T(8,128)(2,1)S(1)} %get-tuple-element.78), channel_id=1, source_target_pairs={{0,2},{1,3},{2,0},{3,1},{4,6},{5,7},{6,4},{7,5},{8,10},{9,11},{10,... | collective-permute-start | bytes 393224 | tf_op jit(solution)/shard_map/ppermute | solution.py:386
  25.7 6.4 %collective-permute-start.8 = (bf16[2,256,128]{2,1,0:T(8,128)(2,1)S(1)}, bf16[2,256,128]{2,1,0:T(8,128)(2,1)S(1)}, u32[]{:S(2)}, u32[]{:S(2)}) collective-permute-start(bf16[2,256,128]{2,1,0:T(8,128)(2,1)S(1)} %get-tuple-element.75), channel_id=1, source_target_pairs={{0,4},{1,5},{2,6},{3,7},{4,0},{5,1},{6,2},{7,3},{8,12},{9,13},{10,... | collective-permute-start | bytes 393224 | tf_op jit(solution)/shard_map/ppermute | solution.py:386
  26.9 5.9 %collective-permute-start.9 = (bf16[2,256,128]{2,1,0:T(8,128)(2,1)S(1)}, bf16[2,256,128]{2,1,0:T(8,128)(2,1)S(1)}, u32[]{:S(2)}, u32[]{:S(2)}) collective-permute-start(bf16[2,256,128]{2,1,0:T(8,128)(2,1)S(1)} %get-tuple-element.76), channel_id=1, source_target_pairs={{0,6},{1,7},{2,4},{3,5},{4,2},{5,3},{6,0},{7,1},{8,14},{9,15},{10,... | collective-permute-start | bytes 393224 | tf_op jit(solution)/shard_map/ppermute | solution.py:386
  30.9 2.5 %collective-permute-start.12 = (bf16[2,512,128]{2,1,0:T(8,128)(2,1)S(1)}, bf16[2,512,128]{2,1,0:T(8,128)(2,1)S(1)}, u32[]{:S(2)}, u32[]{:S(2)}) collective-permute-start(bf16[2,512,128]{2,1,0:T(8,128)(2,1)S(1)} %theirs.3), channel_id=1, source_target_pairs={{0,1},{1,0},{2,3},{3,2},{4,5},{5,4},{6,7},{7,6},{8,9},{9,8},{10,11... | collective-permute-start | bytes 786440 | tf_op jit(solution)/shard_map/ppermute | solution.py:386
  32.8 1.6 %collective-permute-start.11 = (bf16[2,512,128]{2,1,0:T(8,128)(2,1)S(1)}, bf16[2,512,128]{2,1,0:T(8,128)(2,1)S(1)}, u32[]{:S(2)}, u32[]{:S(2)}) collective-permute-start(bf16[2,512,128]{2,1,0:T(8,128)(2,1)S(1)} %theirs.2), channel_id=1, source_target_pairs={{0,1},{1,0},{2,3},{3,2},{4,5},{5,4},{6,7},{7,6},{8,9},{9,8},{10,11... | collective-permute-start | bytes 786440 | tf_op jit(solution)/shard_map/ppermute | solution.py:386

commit v21 on v20

--- a/solution.py
+++ b/solution.py
@@ -31,10 +31,27 @@
     return range(outer_count - 1, 0, -1)
 
 
+def exchanged(bits):
+    return bits ^ 3 if bits & 3 in (1, 2) and lax.axis_size("inner") > 4 else bits
+
+
+def place_of(side):
+    _, far = near_far()
+    if lax.axis_size("inner") <= 4:
+        return far
+    low, high = lax.rem(far, 2), lax.rem(lax.div(far, 2), 2)
+    return jnp.where(side == 1, far, far + low - high)
+
+
+def far_of(s):
+    near, far = near_far()
+    return jnp.where(near == 1, far ^ s, far ^ exchanged(s))
+
+
 def block_start(own, block, half):
-    near, far = near_far()
+    near, _ = near_far()
     side = near if own else 1 - near
-    top = lax.div(far, lax.axis_size("inner") // 4)
+    top = lax.div(place_of(side), lax.axis_size("inner") // 4)
     return side * half + (1 - top if block else top) * (half // 2)
 
 
@@ -43,8 +60,8 @@
 
 
 def slot_rows(s, count, depth):
-    _, far = near_far()
-    return pl.ds(pl.multiple_of(lax.rem(far ^ s, count) * depth, depth), depth)
+    near, _ = near_far()
+    return pl.ds(pl.multiple_of(lax.rem(place_of(near) ^ s, count) * depth, depth), depth)
 
 
 def one_ahead(products, use):
@@ -178,9 +195,8 @@
     slots, others, refs = refs[:far_count], refs[far_count : -far_count - 2], refs[-far_count - 2 :]
     outs, (held, scanned) = refs[:far_count], refs[far_count:]
     outer = lax.axis_index("outer")
-    _, far = near_far()
     for s, slot in enumerate(slots):
-        held[far ^ s] = slot[...]
+        held[far_of(s)] = slot[...]
     for which in range(2):
         total = jnp.zeros(held.shape[2:], F32)
         for s, other in zip(distances(len(others) + 1), others):
@@ -191,7 +207,7 @@
             scanned[i, which] = total.astype(BF16)
             total += held[i, which].astype(F32)
     for s, out in enumerate(outs):
-        out[...] = scanned[far ^ s]
+        out[...] = scanned[far_of(s)]
 
 
 def scan_slots(slots, others):
@@ -387,7 +403,9 @@
 
 
 def swap_far(slots):
-    return [slots[0]] + [swap(slots[s], "inner", 2 * s) for s in range(1, len(slots))]
+    inner = range(lax.axis_size("inner"))
+    pairs = [[(i, i ^ 2 * (s if i % 2 else exchanged(s))) for i in inner] for s in range(len(slots))]
+    return [slots[0]] + [lax.ppermute(x, "inner", p) for x, p in zip(slots[1:], pairs[1:])]
 
 
 def body(queries, keys, values, cotangent):

time: 35.7 us -> 36.8 us (1.031)
  waiting for transfers between devices: 12.3 us -> 13.1 us
    ppermute x0 -> x6, starting transfers between devices: none -> 8.38 us  [swap_far(): lax.ppermute(x, 'inner', p)]
    ppermute x13 -> x7, starting transfers between devices: 13.6 us -> 5.24 us  [swap(): lax.ppermute(x, axis, [(i, i ^ bits) for i in range(lax.axis_size(axis))])]
    ppermute x0 -> x6, waiting for transfers between devices: none -> 8.07 us  [swap_far(): lax.ppermute(x, 'inner', p)]
    ppermute x13 -> x7, waiting for transfers between devices: 12.3 us -> 5.07 us  [swap(): lax.ppermute(x, axis, [(i, i ^ bits) for i in range(lax.axis_size(axis))])]
  transfers between devices with their start and end apart: 13 -> 13, of which waited for: 7 -> 8; matrix products, arithmetic and copies ran while one was open for 0% -> 0% of each run, Pallas kernels for 16% -> 16%
where the time goes in v21:
time: 36.8 us; the launch traced here: 36.4 us
  starting transfers between devices  13.6 us (37%)
  waiting for transfers between devices  13.1 us (36%)
  Pallas kernels  8.91 us (24%)
  between operations  0.76 us (2%)
    ppermute x6, starting transfers between devices, swap_far(): lax.ppermute(x, 'inner', p)  8.38 us
    ppermute x6, waiting for transfers between devices, swap_far(): lax.ppermute(x, 'inner', p)  8.07 us
    ppermute x7, starting transfers between devices, swap(): lax.ppermute(x, axis, [(i, i ^ bits) for i in range(lax.axis_size(axis))])  5.24 us
    ppermute x7, waiting for transfers between devices, swap(): lax.ppermute(x, axis, [(i, i ^ bits) for i in range(lax.axis_size(axis))])  5.07 us
    pallas_call x4, Pallas kernels, finish(): pl.pallas_call(functools.partial(finish_kernel, scale, own, block, len(sl...  3.7 us
    pallas_call x1, Pallas kernels, local_part(): pl.pallas_call(local_kernel, name='local', in_specs=[VMEM] * 4, out_specs...  2.16 us
    pallas_call x1, Pallas kernels, load(): pl.pallas_call(load_kernel, name='load', in_specs=[ANY] * 4, out_specs=[V...  1.77 us
    pallas_call x2, Pallas kernels, sums(): pl.pallas_call(functools.partial(sums_kernel, wanted), name='sums', in_sp...  0.75 us
  transfers between devices with their start and end apart: 13, of which 8 were waited for; matrix products, arithmetic and copies ran while one was open for 0% of the time, Pallas kernels for 16%

profile of v21, /device:TPU:0, one launch (start us, length us, event | category | flops | bytes accessed | tf_op | source)
XLA Modules:
  0.0 36.4 jit_solution(12077621263283241737)
XLA Ops:
  0.6 1.8 %load.1 = (bf16[128,2048]{1,0:T(8,128)(2,1)S(1)}, bf16[128,2048]{1,0:T(8,128)(2,1)S(1)}, bf16[128,2048]{1,0:T(8,128)(2,1)S(1)}, bf16[128,2048]{1,0:T(8,128)(2,1)S(1)}, bf16[2,512,128]{2,1,0:T(8,128)(2,1)S(1)}) custom-call(bf16[128,2048]{1,0:T(8,128)(2,1)} %refs_0_.1, bf16[128,2048]{1,0:T(8,128)(2,1)} %refs_1_.1, bf16[128,2048]{1,0:T(8,128)(2,1)} %refs_2_.1, ...), custom_call_target="tpu_custom_call" | custom-call | flops 33554432 | bytes 2621440 | tf_op jit(solution)/shard_map/load/pallas_call | solution.py:111
  2.4 0.5 %collective-permute-start = (bf16[2,512,128]{2,1,0:T(8,128)(2,1)S(1)}, bf16[2,512,128]{2,1,0:T(8,128)(2,1)S(1)}, u32[]{:S(2)}, u32[]{:S(2)}) collective-permute-start(bf16[2,512,128]{2,1,0:T(8,128)(2,1)S(1)} %get-tuple-element.54), channel_id=1, source_target_pairs={{0,1},{1,0},{2,3},{3,2},{4,5},{5,4},{6,7},{7,6},{8,9},{9,8},{10,11... | collective-permute-start | bytes 786440 | tf_op jit(solution)/shard_map/ppermute | solution.py:402
  2.9 0.3 sums.3
  3.3 0.5 %sums.2 = (bf16[2,512,128]{2,1,0:T(8,128)(2,1)S(1)}, bf16[2,512,128]{2,1,0:T(8,128)(2,1)S(1)}) custom-call(bf16[128,2048]{1,0:T(8,128)(2,1)S(1)} %get-tuple-element.49.refs_0_, bf16[128,2048]{1,0:T(8,128)(2,1)S(1)} %get-tuple-element.50.refs_1_, bf16[128,2048]{1,0:T(8,128)(2,1)S(1)} %get-tuple-element.51.refs_2_, bf16[128,2048]{1,0:T(8,128)(2,1)S(1)} %get-tuple-element.52.refs_3_), custom_call_target="tpu_custom_call" | custom-call | flops 67108864 | bytes 1572864 | tf_op jit(solution)/shard_map/sums/pallas_call | solution.py:133
  3.8 0.3 collective-permute-done.got_ref.refs_10_
  4.2 2.9 %collective-permute-start.1 = (bf16[2,256,128]{2,1,0:T(8,128)(2,1)S(1)}, bf16[2,256,128]{2,1,0:T(8,128)(2,1)S(1)}, u32[]{:S(2)}, u32[]{:S(2)}) collective-permute-start(bf16[2,256,128]{2,1,0:T(8,128)(2,1)S(1)} %get-tuple-element.56), channel_id=1, source_target_pairs={{0,4},{1,3},{2,6},{3,1},{4,0},{5,7},{6,2},{7,5},{8,12},{9,11},{10,... | collective-permute-start | bytes 393224 | tf_op jit(solution)/shard_map/ppermute | solution.py:408
  7.2 1.6 %collective-permute-start.3 = (bf16[2,256,128]{2,1,0:T(8,128)(2,1)S(1)}, bf16[2,256,128]{2,1,0:T(8,128)(2,1)S(1)}, u32[]{:S(2)}, u32[]{:S(2)}) collective-permute-start(bf16[2,256,128]{2,1,0:T(8,128)(2,1)S(1)} %get-tuple-element.58), channel_id=1, source_target_pairs={{0,2},{1,5},{2,0},{3,7},{4,6},{5,1},{6,4},{7,3},{8,10},{9,13},{10,... | collective-permute-start | bytes 393224 | tf_op jit(solution)/shard_map/ppermute | solution.py:408
  8.7 0.3 collective-permute-start.4
  9.1 2.2 %local.1 = (f32[128,2048]{1,0:T(8,128)S(1)}, f32[128,2048]{1,0:T(8,128)S(1)}, f32[128,2048]{1,0:T(8,128)S(1)}, f32[128,2048]{1,0:T(8,128)S(1)}) custom-call(bf16[128,2048]{1,0:T(8,128)(2,1)S(1)} %get-tuple-element.49.refs_0_, bf16[128,2048]{1,0:T(8,128)(2,1)S(1)} %get-tuple-element.50.refs_1_, bf16[128,2048]{1,0:T(8,128)(2,1)S(1)} %get-tuple-element.51.refs_2_, ...), custom_call_target="tpu_custom_call" | custom-call | flops 402653184 | bytes 6291456 | tf_op jit(solution)/shard_map/local/pallas_call | solution.py:290
  11.2 2.3 %collective-permute-done.3.refs_2_ = bf16[2,256,128]{2,1,0:T(8,128)(2,1)S(1)} collective-permute-done((bf16[2,256,128]{2,1,0:T(8,128)(2,1)S(1)}, bf16[2,256,128]{2,1,0:T(8,128)(2,1)S(1)}, u32[]{:S(2)}, u32[]{:S(2)}) %collective-permute-start.3) | collective-permute-done | bytes 131104 | tf_op jit(solution)/shard_map/ppermute | solution.py:408
  13.6 1.3 %collective-permute-done.4.refs_3_ = bf16[2,256,128]{2,1,0:T(8,128)(2,1)S(1)} collective-permute-done((bf16[2,256,128]{2,1,0:T(8,128)(2,1)S(1)}, bf16[2,256,128]{2,1,0:T(8,128)(2,1)S(1)}, u32[]{:S(2)}, u32[]{:S(2)}) %collective-permute-start.4) | collective-permute-done | bytes 131104 | tf_op jit(solution)/shard_map/ppermute | solution.py:408
  15.0 3.7 %collective-permute-start.5 = (bf16[256,128]{1,0:T(8,128)(2,1)S(1)}, bf16[256,128]{1,0:T(8,128)(2,1)S(1)}, u32[]{:S(2)}, u32[]{:S(2)}) collective-permute-start(bf16[256,128]{1,0:T(8,128)(2,1)S(1)} %get-tuple-element.72), channel_id=1, source_target_pairs={{0,24},{8,16},{16,8},{24,0},{1,25},{9,17},{17,9},{25,1},{2,26},{10... | collective-permute-start | bytes 196616 | tf_op jit(solution)/shard_map/ppermute | solution.py:402
  18.7 0.7 %collective-permute-start.7 = (bf16[256,128]{1,0:T(8,128)(2,1)S(1)}, bf16[256,128]{1,0:T(8,128)(2,1)S(1)}, u32[]{:S(2)}, u32[]{:S(2)}) collective-permute-start(bf16[256,128]{1,0:T(8,128)(2,1)S(1)} %get-tuple-element.74), channel_id=1, source_target_pairs={{0,8},{8,0},{16,24},{24,16},{1,9},{9,1},{17,25},{25,17},{2,10},{10... | collective-permute-start | bytes 196616 | tf_op jit(solution)/shard_map/ppermute | solution.py:402
  19.4 2.0 %collective-permute-done.5.refs_4_ = bf16[256,128]{1,0:T(8,128)(2,1)S(1)} collective-permute-done((bf16[256,128]{1,0:T(8,128)(2,1)S(1)}, bf16[256,128]{1,0:T(8,128)(2,1)S(1)}, u32[]{:S(2)}, u32[]{:S(2)}) %collective-permute-start.5) | collective-permute-done | bytes 65568 | tf_op jit(solution)/shard_map/ppermute | solution.py:402
  21.5 2.6 %collective-permute-done.6.refs_5_ = bf16[256,128]{1,0:T(8,128)(2,1)S(1)} collective-permute-done((bf16[256,128]{1,0:T(8,128)(2,1)S(1)}, bf16[256,128]{1,0:T(8,128)(2,1)S(1)}, u32[]{:S(2)}, u32[]{:S(2)}) %collective-permute-start.6) | collective-permute-done | bytes 65568 | tf_op jit(solution)/shard_map/ppermute | solution.py:402
  24.3 1.5 %collective-permute-start.10 = (bf16[2,256,128]{2,1,0:T(8,128)(2,1)S(1)}, bf16[2,256,128]{2,1,0:T(8,128)(2,1)S(1)}, u32[]{:S(2)}, u32[]{:S(2)}) collective-permute-start(bf16[2,256,128]{2,1,0:T(8,128)(2,1)S(1)} %get-tuple-element.78), channel_id=1, source_target_pairs={{0,4},{1,3},{2,6},{3,1},{4,0},{5,7},{6,2},{7,5},{8,12},{9,11},{10,... | collective-permute-start | bytes 393224 | tf_op jit(solution)/shard_map/ppermute | solution.py:408
  25.8 1.7 %collective-permute-start.8 = (bf16[2,256,128]{2,1,0:T(8,128)(2,1)S(1)}, bf16[2,256,128]{2,1,0:T(8,128)(2,1)S(1)}, u32[]{:S(2)}, u32[]{:S(2)}) collective-permute-start(bf16[2,256,128]{2,1,0:T(8,128)(2,1)S(1)} %get-tuple-element.75), channel_id=1, source_target_pairs={{0,2},{1,5},{2,0},{3,7},{4,6},{5,1},{6,4},{7,3},{8,10},{9,13},{10,... | collective-permute-start | bytes 393224 | tf_op jit(solution)/shard_map/ppermute | solution.py:408
  27.5 0.4 collective-permute-start.9
  27.9 3.2 %collective-permute-done.10.refs_9_.refs_1_ = bf16[2,256,128]{2,1,0:T(8,128)(2,1)S(1)} collective-permute-done((bf16[2,256,128]{2,1,0:T(8,128)(2,1)S(1)}, bf16[2,256,128]{2,1,0:T(8,128)(2,1)S(1)}, u32[]{:S(2)}, u32[]{:S(2)}) %collective-permute-start.10) | collective-permute-done | bytes 131104 | tf_op jit(solution)/shard_map/ppermute | solution.py:408
  31.2 1.2 %finish.4 = (bf16[128,2048]{1,0:T(8,128)(2,1)}, bf16[128,2048]{1,0:T(8,128)(2,1)}, bf16[128,2048]{1,0:T(8,128)(2,1)}, bf16[128,2048]{1,0:T(8,128)(2,1)}) custom-call(bf16[128,2048]{1,0:T(8,128)(2,1)S(1)} %get-tuple-element.49.refs_0_, bf16[128,2048]{1,0:T(8,128)(2,1)S(1)} %get-tuple-element.50.refs_1_, bf16[128,2048]{1,0:T(8,128)(2,1)S(1)} %get-tuple-element.51.refs_2_, ...), custom_call_target="tpu_custom_call" | custom-call | flops 67108864 | bytes 2097152 | tf_op jit(solution)/shard_map/finish/pallas_call | solution.py:384
  32.4 1.2 %collective-permute-done.9.refs_1_.refs_9_ = bf16[2,256,128]{2,1,0:T(8,128)(2,1)S(1)} collective-permute-done((bf16[2,256,128]{2,1,0:T(8,128)(2,1)S(1)}, bf16[2,256,128]{2,1,0:T(8,128)(2,1)S(1)}, u32[]{:S(2)}, u32[]{:S(2)}) %collective-permute-start.9) | collective-permute-done | bytes 131104 | tf_op jit(solution)/shard_map/ppermute | solution.py:408
  33.7 0.4 %finish.5.refs_9_ = bf16[4,128,512]{2,1,0:T(8,128)(2,1)S(1)} custom-call(bf16[128,2048]{1,0:T(8,128)(2,1)S(1)} %get-tuple-element.49.refs_0_, bf16[128,2048]{1,0:T(8,128)(2,1)S(1)} %get-tuple-element.50.refs_1_, bf16[128,2048]{1,0:T(8,128)(2,1)S(1)} %get-tuple-element.51.refs_2_, bf16[128,2048]{1,0:T(8,128)(2,1)S(1)} %get-tuple-element.52.refs_3_, ...), custom_call_target="tpu_custom_call" | custom-call | flops 67108864 | bytes 2097152 | tf_op jit(solution)/shard_map/finish/pallas_call | solution.py:384
  34.2 0.9 %finish.6 = (bf16[128,2048]{1,0:T(8,128)(2,1)}, bf16[128,2048]{1,0:T(8,128)(2,1)}, bf16[128,2048]{1,0:T(8,128)(2,1)}, bf16[128,2048]{1,0:T(8,128)(2,1)}, bf16[4,128,512]{2,1,0:T(8,128)(2,1)S(1)}) custom-call(bf16[128,2048]{1,0:T(8,128)(2,1)S(1)} %get-tuple-element.49.refs_0_, ...), custom_call_target="tpu_custom_call", output_to_operand_aliasing={{0}: (10, {}), {1}: (11, {}), {2}: (12, {}), {3}: (13, {})} | custom-call | flops 67108864 | bytes 2097152 | tf_op jit(solution)/shard_map/finish/pallas_call | solution.py:384
  35.3 1.2 %finish.7 = (bf16[128,2048]{1,0:T(8,128)(2,1)}, bf16[128,2048]{1,0:T(8,128)(2,1)}, bf16[128,2048]{1,0:T(8,128)(2,1)}, bf16[128,2048]{1,0:T(8,128)(2,1)}) custom-call(bf16[128,2048]{1,0:T(8,128)(2,1)S(1)} %get-tuple-element.49.refs_0_, ...), custom_call_target="tpu_custom_call", output_to_operand_aliasing={{0}: (10, {}), {1}: (11, {}), {2}: (12, {}), {3}: (13, {})} | custom-call | flops 67108864 | bytes 2097152 | tf_op jit(solution)/shard_map/finish/pallas_call | solution.py:384
  (16 shorter events, 0.9 us)
Async XLA Ops:
  2.4 1.7 %collective-permute-start = (bf16[2,512,128]{2,1,0:T(8,128)(2,1)S(1)}, bf16[2,512,128]{2,1,0:T(8,128)(2,1)S(1)}, u32[]{:S(2)}, u32[]{:S(2)}) collective-permute-start(bf16[2,512,128]{2,1,0:T(8,128)(2,1)S(1)} %get-tuple-element.54), channel_id=1, source_target_pairs={{0,1},{1,0},{2,3},{3,2},{4,5},{5,4},{6,7},{7,6},{8,9},{9,8},{10,11... | collective-permute-start | bytes 786440 | tf_op jit(solution)/shard_map/ppermute | solution.py:402
  3.2 3.9 %collective-permute-start.2 = (bf16[2,512,128]{2,1,0:T(8,128)(2,1)S(1)}, bf16[2,512,128]{2,1,0:T(8,128)(2,1)S(1)}, u32[]{:S(2)}, u32[]{:S(2)}) collective-permute-start(bf16[2,512,128]{2,1,0:T(8,128)(2,1)S(1)} %sums.3), channel_id=1, source_target_pairs={{0,1},{1,0},{2,3},{3,2},{4,5},{5,4},{6,7},{7,6},{8,9},{9,8},{10,11... | collective-permute-start | bytes 786440 | tf_op jit(solution)/shard_map/ppermute | solution.py:402
  4.2 7.1 %collective-permute-start.1 = (bf16[2,256,128]{2,1,0:T(8,128)(2,1)S(1)}, bf16[2,256,128]{2,1,0:T(8,128)(2,1)S(1)}, u32[]{:S(2)}, u32[]{:S(2)}) collective-permute-start(bf16[2,256,128]{2,1,0:T(8,128)(2,1)S(1)} %get-tuple-element.56), channel_id=1, source_target_pairs={{0,4},{1,3},{2,6},{3,1},{4,0},{5,7},{6,2},{7,5},{8,12},{9,11},{10,... | collective-permute-start | bytes 393224 | tf_op jit(solution)/shard_map/ppermute | solution.py:408
  7.2 6.4 %collective-permute-start.3 = (bf16[2,256,128]{2,1,0:T(8,128)(2,1)S(1)}, bf16[2,256,128]{2,1,0:T(8,128)(2,1)S(1)}, u32[]{:S(2)}, u32[]{:S(2)}) collective-permute-start(bf16[2,256,128]{2,1,0:T(8,128)(2,1)S(1)} %get-tuple-element.58), channel_id=1, source_target_pairs={{0,2},{1,5},{2,0},{3,7},{4,6},{5,1},{6,4},{7,3},{8,10},{9,13},{10,... | collective-permute-start | bytes 393224 | tf_op jit(solution)/shard_map/ppermute | solution.py:408
  8.7 6.2 %collective-permute-start.4 = (bf16[2,256,128]{2,1,0:T(8,128)(2,1)S(1)}, bf16[2,256,128]{2,1,0:T(8,128)(2,1)S(1)}, u32[]{:S(2)}, u32[]{:S(2)}) collective-permute-start(bf16[2,256,128]{2,1,0:T(8,128)(2,1)S(1)} %get-tuple-element.59), channel_id=1, source_target_pairs={{0,6},{1,7},{2,4},{3,5},{4,2},{5,3},{6,0},{7,1},{8,14},{9,15},{10,... | collective-permute-start | bytes 393224 | tf_op jit(solution)/shard_map/ppermute | solution.py:408
  15.0 6.5 %collective-permute-start.5 = (bf16[256,128]{1,0:T(8,128)(2,1)S(1)}, bf16[256,128]{1,0:T(8,128)(2,1)S(1)}, u32[]{:S(2)}, u32[]{:S(2)}) collective-permute-start(bf16[256,128]{1,0:T(8,128)(2,1)S(1)} %get-tuple-element.72), channel_id=1, source_target_pairs={{0,24},{8,16},{16,8},{24,0},{1,25},{9,17},{17,9},{25,1},{2,26},{10... | collective-permute-start | bytes 196616 | tf_op jit(solution)/shard_map/ppermute | solution.py:402
  18.7 5.4 %collective-permute-start.6 = (bf16[256,128]{1,0:T(8,128)(2,1)S(1)}, bf16[256,128]{1,0:T(8,128)(2,1)S(1)}, u32[]{:S(2)}, u32[]{:S(2)}) collective-permute-start(bf16[256,128]{1,0:T(8,128)(2,1)S(1)} %get-tuple-element.73), channel_id=1, source_target_pairs={{0,16},{8,24},{16,0},{24,8},{1,17},{9,25},{17,1},{25,9},{2,18},{10... | collective-permute-start | bytes 196616 | tf_op jit(solution)/shard_map/ppermute | solution.py:402
  18.7 5.4 %collective-permute-start.7 = (bf16[256,128]{1,0:T(8,128)(2,1)S(1)}, bf16[256,128]{1,0:T(8,128)(2,1)S(1)}, u32[]{:S(2)}, u32[]{:S(2)}) collective-permute-start(bf16[256,128]{1,0:T(8,128)(2,1)S(1)} %get-tuple-element.74), channel_id=1, source_target_pairs={{0,8},{8,0},{16,24},{24,16},{1,9},{9,1},{17,25},{25,17},{2,10},{10... | collective-permute-start | bytes 196616 | tf_op jit(solution)/shard_map/ppermute | solution.py:402
  24.3 6.7 %collective-permute-start.10 = (bf16[2,256,128]{2,1,0:T(8,128)(2,1)S(1)}, bf16[2,256,128]{2,1,0:T(8,128)(2,1)S(1)}, u32[]{:S(2)}, u32[]{:S(2)}) collective-permute-start(bf16[2,256,128]{2,1,0:T(8,128)(2,1)S(1)} %get-tuple-element.78), channel_id=1, source_target_pairs={{0,4},{1,3},{2,6},{3,1},{4,0},{5,7},{6,2},{7,5},{8,12},{9,11},{10,... | collective-permute-start | bytes 393224 | tf_op jit(solution)/shard_map/ppermute | solution.py:408
  25.8 6.6 %collective-permute-start.8 = (bf16[2,256,128]{2,1,0:T(8,128)(2,1)S(1)}, bf16[2,256,128]{2,1,0:T(8,128)(2,1)S(1)}, u32[]{:S(2)}, u32[]{:S(2)}) collective-permute-start(bf16[2,256,128]{2,1,0:T(8,128)(2,1)S(1)} %get-tuple-element.75), channel_id=1, source_target_pairs={{0,2},{1,5},{2,0},{3,7},{4,6},{5,1},{6,4},{7,3},{8,10},{9,13},{10,... | collective-permute-start | bytes 393224 | tf_op jit(solution)/shard_map/ppermute | solution.py:408
  27.5 6.1 %collective-permute-start.9 = (bf16[2,256,128]{2,1,0:T(8,128)(2,1)S(1)}, bf16[2,256,128]{2,1,0:T(8,128)(2,1)S(1)}, u32[]{:S(2)}, u32[]{:S(2)}) collective-permute-start(bf16[2,256,128]{2,1,0:T(8,128)(2,1)S(1)} %get-tuple-element.76), channel_id=1, source_target_pairs={{0,6},{1,7},{2,4},{3,5},{4,2},{5,3},{6,0},{7,1},{8,14},{9,15},{10,... | collective-permute-start | bytes 393224 | tf_op jit(solution)/shard_map/ppermute | solution.py:408
  31.1 3.1 %collective-permute-start.12 = (bf16[2,512,128]{2,1,0:T(8,128)(2,1)S(1)}, bf16[2,512,128]{2,1,0:T(8,128)(2,1)S(1)}, u32[]{:S(2)}, u32[]{:S(2)}) collective-permute-start(bf16[2,512,128]{2,1,0:T(8,128)(2,1)S(1)} %theirs.3), channel_id=1, source_target_pairs={{0,1},{1,0},{2,3},{3,2},{4,5},{5,4},{6,7},{7,6},{8,9},{9,8},{10,11... | collective-permute-start | bytes 786440 | tf_op jit(solution)/shard_map/ppermute | solution.py:402
  33.7 1.6 %collective-permute-start.11 = (bf16[2,512,128]{2,1,0:T(8,128)(2,1)S(1)}, bf16[2,512,128]{2,1,0:T(8,128)(2,1)S(1)}, u32[]{:S(2)}, u32[]{:S(2)}) collective-permute-start(bf16[2,512,128]{2,1,0:T(8,128)(2,1)S(1)} %theirs.2), channel_id=1, source_target_pairs={{0,1},{1,0},{2,3},{3,2},{4,5},{5,4},{6,7},{7,6},{8,9},{9,8},{10,11... | collective-permute-start | bytes 786440 | tf_op jit(solution)/shard_map/ppermute | solution.py:402

commit v22 on v20

--- a/solution.py
+++ b/solution.py
@@ -28,7 +28,8 @@
 
 
 def distances(outer_count):
-    return range(outer_count - 1, 0, -1)
+    order = list(range(outer_count - 1, 0, -1))
+    return order[1:2] + order[:1] + order[2:]
 
 
 def block_start(own, block, half):

time: 35.7 us -> 35.8 us (level)
  waiting for transfers between devices: 12.3 us -> 12.7 us
  transfers between devices with their start and end apart: 13 -> 13, of which waited for: 7 -> 8; matrix products, arithmetic and copies ran while one was open for 0% -> 0% of each run, Pallas kernels for 16% -> 16%
where the time goes in v22:
time: 35.8 us; the launch traced here: 35.7 us
  starting transfers between devices  13.4 us (37%)
  waiting for transfers between devices  12.7 us (35%)
  Pallas kernels  8.88 us (25%)
  between operations  0.76 us (2%)
    ppermute x13, starting transfers between devices, swap(): lax.ppermute(x, axis, [(i, i ^ bits) for i in range(lax.axis_size(axis))])  13.4 us
    ppermute x13, waiting for transfers between devices, swap(): lax.ppermute(x, axis, [(i, i ^ bits) for i in range(lax.axis_size(axis))])  12.7 us
    pallas_call x4, Pallas kernels, finish(): pl.pallas_call(functools.partial(finish_kernel, scale, own, block, len(sl...  3.69 us
    pallas_call x1, Pallas kernels, local_part(): pl.pallas_call(local_kernel, name='local', in_specs=[VMEM] * 4, out_specs...  2.16 us
    pallas_call x1, Pallas kernels, load(): pl.pallas_call(load_kernel, name='load', in_specs=[ANY] * 4, out_specs=[V...  1.77 us
    pallas_call x2, Pallas kernels, sums(): pl.pallas_call(functools.partial(sums_kernel, wanted), name='sums', in_sp...  0.75 us
  transfers between devices with their start and end apart: 13, of which 8 were waited for; matrix products, arithmetic and copies ran while one was open for 0% of the time, Pallas kernels for 16%

profile of v22, /device:TPU:0, one launch (start us, length us, event | category | flops | bytes accessed | tf_op | source)
XLA Modules:
  0.0 35.7 jit_solution(5761836743961816993)
XLA Ops:
  0.6 1.8 %load.1 = (bf16[128,2048]{1,0:T(8,128)(2,1)S(1)}, bf16[128,2048]{1,0:T(8,128)(2,1)S(1)}, bf16[128,2048]{1,0:T(8,128)(2,1)S(1)}, bf16[128,2048]{1,0:T(8,128)(2,1)S(1)}, bf16[2,512,128]{2,1,0:T(8,128)(2,1)S(1)}) custom-call(bf16[128,2048]{1,0:T(8,128)(2,1)} %refs_0_.1, bf16[128,2048]{1,0:T(8,128)(2,1)} %refs_1_.1, bf16[128,2048]{1,0:T(8,128)(2,1)} %refs_2_.1, ...), custom_call_target="tpu_custom_call" | custom-call | flops 33554432 | bytes 2621440 | tf_op jit(solution)/shard_map/load/pallas_call | solution.py:95
  2.4 0.5 %collective-permute-start = (bf16[2,512,128]{2,1,0:T(8,128)(2,1)S(1)}, bf16[2,512,128]{2,1,0:T(8,128)(2,1)S(1)}, u32[]{:S(2)}, u32[]{:S(2)}) collective-permute-start(bf16[2,512,128]{2,1,0:T(8,128)(2,1)S(1)} %get-tuple-element.54), channel_id=1, source_target_pairs={{0,1},{1,0},{2,3},{3,2},{4,5},{5,4},{6,7},{7,6},{8,9},{9,8},{10,11... | collective-permute-start | bytes 786440 | tf_op jit(solution)/shard_map/ppermute | solution.py:387
  2.9 0.3 sums.3
  3.3 0.5 %sums.2 = (bf16[2,512,128]{2,1,0:T(8,128)(2,1)S(1)}, bf16[2,512,128]{2,1,0:T(8,128)(2,1)S(1)}) custom-call(bf16[128,2048]{1,0:T(8,128)(2,1)S(1)} %get-tuple-element.49.refs_0_, bf16[128,2048]{1,0:T(8,128)(2,1)S(1)} %get-tuple-element.50.refs_1_, bf16[128,2048]{1,0:T(8,128)(2,1)S(1)} %get-tuple-element.51.refs_2_, bf16[128,2048]{1,0:T(8,128)(2,1)S(1)} %get-tuple-element.52.refs_3_), custom_call_target="tpu_custom_call" | custom-call | flops 67108864 | bytes 1572864 | tf_op jit(solution)/shard_map/sums/pallas_call | solution.py:117
  3.8 0.3 collective-permute-done.got_ref.refs_10_
  4.2 2.9 %collective-permute-start.1 = (bf16[2,256,128]{2,1,0:T(8,128)(2,1)S(1)}, bf16[2,256,128]{2,1,0:T(8,128)(2,1)S(1)}, u32[]{:S(2)}, u32[]{:S(2)}) collective-permute-start(bf16[2,256,128]{2,1,0:T(8,128)(2,1)S(1)} %get-tuple-element.56), channel_id=1, source_target_pairs={{0,2},{1,3},{2,0},{3,1},{4,6},{5,7},{6,4},{7,5},{8,10},{9,11},{10,... | collective-permute-start | bytes 393224 | tf_op jit(solution)/shard_map/ppermute | solution.py:387
  7.1 1.6 %collective-permute-start.3 = (bf16[2,256,128]{2,1,0:T(8,128)(2,1)S(1)}, bf16[2,256,128]{2,1,0:T(8,128)(2,1)S(1)}, u32[]{:S(2)}, u32[]{:S(2)}) collective-permute-start(bf16[2,256,128]{2,1,0:T(8,128)(2,1)S(1)} %get-tuple-element.58), channel_id=1, source_target_pairs={{0,4},{1,5},{2,6},{3,7},{4,0},{5,1},{6,2},{7,3},{8,12},{9,13},{10,... | collective-permute-start | bytes 393224 | tf_op jit(solution)/shard_map/ppermute | solution.py:387
  8.7 0.3 collective-permute-start.4
  9.0 2.2 %local.1 = (f32[128,2048]{1,0:T(8,128)S(1)}, f32[128,2048]{1,0:T(8,128)S(1)}, f32[128,2048]{1,0:T(8,128)S(1)}, f32[128,2048]{1,0:T(8,128)S(1)}) custom-call(bf16[128,2048]{1,0:T(8,128)(2,1)S(1)} %get-tuple-element.49.refs_0_, bf16[128,2048]{1,0:T(8,128)(2,1)S(1)} %get-tuple-element.50.refs_1_, bf16[128,2048]{1,0:T(8,128)(2,1)S(1)} %get-tuple-element.51.refs_2_, ...), custom_call_target="tpu_custom_call" | custom-call | flops 402653184 | bytes 6291456 | tf_op jit(solution)/shard_map/local/pallas_call | solution.py:275
  11.2 4.1 %collective-permute-done.3.refs_2_ = bf16[2,256,128]{2,1,0:T(8,128)(2,1)S(1)} collective-permute-done((bf16[2,256,128]{2,1,0:T(8,128)(2,1)S(1)}, bf16[2,256,128]{2,1,0:T(8,128)(2,1)S(1)}, u32[]{:S(2)}, u32[]{:S(2)}) %collective-permute-start.3) | collective-permute-done | bytes 131104 | tf_op jit(solution)/shard_map/ppermute | solution.py:387
  15.4 2.7 %collective-permute-start.5 = (bf16[256,128]{1,0:T(8,128)(2,1)S(1)}, bf16[256,128]{1,0:T(8,128)(2,1)S(1)}, u32[]{:S(2)}, u32[]{:S(2)}) collective-permute-start(bf16[256,128]{1,0:T(8,128)(2,1)S(1)} %get-tuple-element.72), channel_id=1, source_target_pairs={{0,16},{8,24},{16,0},{24,8},{1,17},{9,25},{17,1},{25,9},{2,18},{10... | collective-permute-start | bytes 196616 | tf_op jit(solution)/shard_map/ppermute | solution.py:387
  18.0 1.3 %collective-permute-start.6 = (bf16[256,128]{1,0:T(8,128)(2,1)S(1)}, bf16[256,128]{1,0:T(8,128)(2,1)S(1)}, u32[]{:S(2)}, u32[]{:S(2)}) collective-permute-start(bf16[256,128]{1,0:T(8,128)(2,1)S(1)} %get-tuple-element.73), channel_id=1, source_target_pairs={{0,24},{8,16},{16,8},{24,0},{1,25},{9,17},{17,9},{25,1},{2,26},{10... | collective-permute-start | bytes 196616 | tf_op jit(solution)/shard_map/ppermute | solution.py:387
  19.4 0.2 collective-permute-start.7
  19.6 3.1 %collective-permute-done.5.refs_4_ = bf16[256,128]{1,0:T(8,128)(2,1)S(1)} collective-permute-done((bf16[256,128]{1,0:T(8,128)(2,1)S(1)}, bf16[256,128]{1,0:T(8,128)(2,1)S(1)}, u32[]{:S(2)}, u32[]{:S(2)}) %collective-permute-start.5) | collective-permute-done | bytes 65568 | tf_op jit(solution)/shard_map/ppermute | solution.py:387
  22.7 1.5 %collective-permute-done.6.refs_5_ = bf16[256,128]{1,0:T(8,128)(2,1)S(1)} collective-permute-done((bf16[256,128]{1,0:T(8,128)(2,1)S(1)}, bf16[256,128]{1,0:T(8,128)(2,1)S(1)}, u32[]{:S(2)}, u32[]{:S(2)}) %collective-permute-start.6) | collective-permute-done | bytes 65568 | tf_op jit(solution)/shard_map/ppermute | solution.py:387
  24.6 1.2 %collective-permute-start.10 = (bf16[2,256,128]{2,1,0:T(8,128)(2,1)S(1)}, bf16[2,256,128]{2,1,0:T(8,128)(2,1)S(1)}, u32[]{:S(2)}, u32[]{:S(2)}) collective-permute-start(bf16[2,256,128]{2,1,0:T(8,128)(2,1)S(1)} %get-tuple-element.78), channel_id=1, source_target_pairs={{0,2},{1,3},{2,0},{3,1},{4,6},{5,7},{6,4},{7,5},{8,10},{9,11},{10,... | collective-permute-start | bytes 393224 | tf_op jit(solution)/shard_map/ppermute | solution.py:387
  25.7 1.3 %collective-permute-start.8 = (bf16[2,256,128]{2,1,0:T(8,128)(2,1)S(1)}, bf16[2,256,128]{2,1,0:T(8,128)(2,1)S(1)}, u32[]{:S(2)}, u32[]{:S(2)}) collective-permute-start(bf16[2,256,128]{2,1,0:T(8,128)(2,1)S(1)} %get-tuple-element.75), channel_id=1, source_target_pairs={{0,4},{1,5},{2,6},{3,7},{4,0},{5,1},{6,2},{7,3},{8,12},{9,13},{10,... | collective-permute-start | bytes 393224 | tf_op jit(solution)/shard_map/ppermute | solution.py:387
  27.0 1.1 %collective-permute-start.9 = (bf16[2,256,128]{2,1,0:T(8,128)(2,1)S(1)}, bf16[2,256,128]{2,1,0:T(8,128)(2,1)S(1)}, u32[]{:S(2)}, u32[]{:S(2)}) collective-permute-start(bf16[2,256,128]{2,1,0:T(8,128)(2,1)S(1)} %get-tuple-element.76), channel_id=1, source_target_pairs={{0,6},{1,7},{2,4},{3,5},{4,2},{5,3},{6,0},{7,1},{8,14},{9,15},{10,... | collective-permute-start | bytes 393224 | tf_op jit(solution)/shard_map/ppermute | solution.py:387
  28.1 1.8 %collective-permute-done.10.refs_9_.refs_1_ = bf16[2,256,128]{2,1,0:T(8,128)(2,1)S(1)} collective-permute-done((bf16[2,256,128]{2,1,0:T(8,128)(2,1)S(1)}, bf16[2,256,128]{2,1,0:T(8,128)(2,1)S(1)}, u32[]{:S(2)}, u32[]{:S(2)}) %collective-permute-start.10) | collective-permute-done | bytes 131104 | tf_op jit(solution)/shard_map/ppermute | solution.py:387
  30.1 1.2 %finish.4 = (bf16[128,2048]{1,0:T(8,128)(2,1)}, bf16[128,2048]{1,0:T(8,128)(2,1)}, bf16[128,2048]{1,0:T(8,128)(2,1)}, bf16[128,2048]{1,0:T(8,128)(2,1)}) custom-call(bf16[128,2048]{1,0:T(8,128)(2,1)S(1)} %get-tuple-element.49.refs_0_, bf16[128,2048]{1,0:T(8,128)(2,1)S(1)} %get-tuple-element.50.refs_1_, bf16[128,2048]{1,0:T(8,128)(2,1)S(1)} %get-tuple-element.51.refs_2_, ...), custom_call_target="tpu_custom_call" | custom-call | flops 67108864 | bytes 2097152 | tf_op jit(solution)/shard_map/finish/pallas_call | solution.py:369
  31.3 1.6 %collective-permute-done.9.refs_1_.refs_9_ = bf16[2,256,128]{2,1,0:T(8,128)(2,1)S(1)} collective-permute-done((bf16[2,256,128]{2,1,0:T(8,128)(2,1)S(1)}, bf16[2,256,128]{2,1,0:T(8,128)(2,1)S(1)}, u32[]{:S(2)}, u32[]{:S(2)}) %collective-permute-start.9) | collective-permute-done | bytes 131104 | tf_op jit(solution)/shard_map/ppermute | solution.py:387
  33.0 0.4 %finish.5.refs_9_ = bf16[4,128,512]{2,1,0:T(8,128)(2,1)S(1)} custom-call(bf16[128,2048]{1,0:T(8,128)(2,1)S(1)} %get-tuple-element.49.refs_0_, bf16[128,2048]{1,0:T(8,128)(2,1)S(1)} %get-tuple-element.50.refs_1_, bf16[128,2048]{1,0:T(8,128)(2,1)S(1)} %get-tuple-element.51.refs_2_, bf16[128,2048]{1,0:T(8,128)(2,1)S(1)} %get-tuple-element.52.refs_3_, ...), custom_call_target="tpu_custom_call" | custom-call | flops 67108864 | bytes 2097152 | tf_op jit(solution)/shard_map/finish/pallas_call | solution.py:369
  33.5 0.9 %finish.6 = (bf16[128,2048]{1,0:T(8,128)(2,1)}, bf16[128,2048]{1,0:T(8,128)(2,1)}, bf16[128,2048]{1,0:T(8,128)(2,1)}, bf16[128,2048]{1,0:T(8,128)(2,1)}, bf16[4,128,512]{2,1,0:T(8,128)(2,1)S(1)}) custom-call(bf16[128,2048]{1,0:T(8,128)(2,1)S(1)} %get-tuple-element.49.refs_0_, ...), custom_call_target="tpu_custom_call", output_to_operand_aliasing={{0}: (10, {}), {1}: (11, {}), {2}: (12, {}), {3}: (13, {})} | custom-call | flops 67108864 | bytes 2097152 | tf_op jit(solution)/shard_map/finish/pallas_call | solution.py:369
  34.5 1.2 %finish.7 = (bf16[128,2048]{1,0:T(8,128)(2,1)}, bf16[128,2048]{1,0:T(8,128)(2,1)}, bf16[128,2048]{1,0:T(8,128)(2,1)}, bf16[128,2048]{1,0:T(8,128)(2,1)}) custom-call(bf16[128,2048]{1,0:T(8,128)(2,1)S(1)} %get-tuple-element.49.refs_0_, ...), custom_call_target="tpu_custom_call", output_to_operand_aliasing={{0}: (10, {}), {1}: (11, {}), {2}: (12, {}), {3}: (13, {})} | custom-call | flops 67108864 | bytes 2097152 | tf_op jit(solution)/shard_map/finish/pallas_call | solution.py:369
  (16 shorter events, 1.1 us)
Async XLA Ops:
  2.4 1.7 %collective-permute-start = (bf16[2,512,128]{2,1,0:T(8,128)(2,1)S(1)}, bf16[2,512,128]{2,1,0:T(8,128)(2,1)S(1)}, u32[]{:S(2)}, u32[]{:S(2)}) collective-permute-start(bf16[2,512,128]{2,1,0:T(8,128)(2,1)S(1)} %get-tuple-element.54), channel_id=1, source_target_pairs={{0,1},{1,0},{2,3},{3,2},{4,5},{5,4},{6,7},{7,6},{8,9},{9,8},{10,11... | collective-permute-start | bytes 786440 | tf_op jit(solution)/shard_map/ppermute | solution.py:387
  3.2 3.9 %collective-permute-start.2 = (bf16[2,512,128]{2,1,0:T(8,128)(2,1)S(1)}, bf16[2,512,128]{2,1,0:T(8,128)(2,1)S(1)}, u32[]{:S(2)}, u32[]{:S(2)}) collective-permute-start(bf16[2,512,128]{2,1,0:T(8,128)(2,1)S(1)} %sums.3), channel_id=1, source_target_pairs={{0,1},{1,0},{2,3},{3,2},{4,5},{5,4},{6,7},{7,6},{8,9},{9,8},{10,11... | collective-permute-start | bytes 786440 | tf_op jit(solution)/shard_map/ppermute | solution.py:387
  4.2 7.0 %collective-permute-start.1 = (bf16[2,256,128]{2,1,0:T(8,128)(2,1)S(1)}, bf16[2,256,128]{2,1,0:T(8,128)(2,1)S(1)}, u32[]{:S(2)}, u32[]{:S(2)}) collective-permute-start(bf16[2,256,128]{2,1,0:T(8,128)(2,1)S(1)} %get-tuple-element.56), channel_id=1, source_target_pairs={{0,2},{1,3},{2,0},{3,1},{4,6},{5,7},{6,4},{7,5},{8,10},{9,11},{10,... | collective-permute-start | bytes 393224 | tf_op jit(solution)/shard_map/ppermute | solution.py:387
  7.1 8.1 %collective-permute-start.3 = (bf16[2,256,128]{2,1,0:T(8,128)(2,1)S(1)}, bf16[2,256,128]{2,1,0:T(8,128)(2,1)S(1)}, u32[]{:S(2)}, u32[]{:S(2)}) collective-permute-start(bf16[2,256,128]{2,1,0:T(8,128)(2,1)S(1)} %get-tuple-element.58), channel_id=1, source_target_pairs={{0,4},{1,5},{2,6},{3,7},{4,0},{5,1},{6,2},{7,3},{8,12},{9,13},{10,... | collective-permute-start | bytes 393224 | tf_op jit(solution)/shard_map/ppermute | solution.py:387
  8.7 6.6 %collective-permute-start.4 = (bf16[2,256,128]{2,1,0:T(8,128)(2,1)S(1)}, bf16[2,256,128]{2,1,0:T(8,128)(2,1)S(1)}, u32[]{:S(2)}, u32[]{:S(2)}) collective-permute-start(bf16[2,256,128]{2,1,0:T(8,128)(2,1)S(1)} %get-tuple-element.59), channel_id=1, source_target_pairs={{0,6},{1,7},{2,4},{3,5},{4,2},{5,3},{6,0},{7,1},{8,14},{9,15},{10,... | collective-permute-start | bytes 393224 | tf_op jit(solution)/shard_map/ppermute | solution.py:387
  15.4 7.3 %collective-permute-start.5 = (bf16[256,128]{1,0:T(8,128)(2,1)S(1)}, bf16[256,128]{1,0:T(8,128)(2,1)S(1)}, u32[]{:S(2)}, u32[]{:S(2)}) collective-permute-start(bf16[256,128]{1,0:T(8,128)(2,1)S(1)} %get-tuple-element.72), channel_id=1, source_target_pairs={{0,16},{8,24},{16,0},{24,8},{1,17},{9,25},{17,1},{25,9},{2,18},{10... | collective-permute-start | bytes 196616 | tf_op jit(solution)/shard_map/ppermute | solution.py:387
  18.0 6.2 %collective-permute-start.6 = (bf16[256,128]{1,0:T(8,128)(2,1)S(1)}, bf16[256,128]{1,0:T(8,128)(2,1)S(1)}, u32[]{:S(2)}, u32[]{:S(2)}) collective-permute-start(bf16[256,128]{1,0:T(8,128)(2,1)S(1)} %get-tuple-element.73), channel_id=1, source_target_pairs={{0,24},{8,16},{16,8},{24,0},{1,25},{9,17},{17,9},{25,1},{2,26},{10... | collective-permute-start | bytes 196616 | tf_op jit(solution)/shard_map/ppermute | solution.py:387
  19.4 5.0 %collective-permute-start.7 = (bf16[256,128]{1,0:T(8,128)(2,1)S(1)}, bf16[256,128]{1,0:T(8,128)(2,1)S(1)}, u32[]{:S(2)}, u32[]{:S(2)}) collective-permute-start(bf16[256,128]{1,0:T(8,128)(2,1)S(1)} %get-tuple-element.74), channel_id=1, source_target_pairs={{0,8},{8,0},{16,24},{24,16},{1,9},{9,1},{17,25},{25,17},{2,10},{10... | collective-permute-start | bytes 196616 | tf_op jit(solution)/shard_map/ppermute | solution.py:387
  24.6 5.4 %collective-permute-start.10 = (bf16[2,256,128]{2,1,0:T(8,128)(2,1)S(1)}, bf16[2,256,128]{2,1,0:T(8,128)(2,1)S(1)}, u32[]{:S(2)}, u32[]{:S(2)}) collective-permute-start(bf16[2,256,128]{2,1,0:T(8,128)(2,1)S(1)} %get-tuple-element.78), channel_id=1, source_target_pairs={{0,2},{1,3},{2,0},{3,1},{4,6},{5,7},{6,4},{7,5},{8,10},{9,11},{10,... | collective-permute-start | bytes 393224 | tf_op jit(solution)/shard_map/ppermute | solution.py:387
  25.7 5.5 %collective-permute-start.8 = (bf16[2,256,128]{2,1,0:T(8,128)(2,1)S(1)}, bf16[2,256,128]{2,1,0:T(8,128)(2,1)S(1)}, u32[]{:S(2)}, u32[]{:S(2)}) collective-permute-start(bf16[2,256,128]{2,1,0:T(8,128)(2,1)S(1)} %get-tuple-element.75), channel_id=1, source_target_pairs={{0,4},{1,5},{2,6},{3,7},{4,0},{5,1},{6,2},{7,3},{8,12},{9,13},{10,... | collective-permute-start | bytes 393224 | tf_op jit(solution)/shard_map/ppermute | solution.py:387
  27.0 5.9 %collective-permute-start.9 = (bf16[2,256,128]{2,1,0:T(8,128)(2,1)S(1)}, bf16[2,256,128]{2,1,0:T(8,128)(2,1)S(1)}, u32[]{:S(2)}, u32[]{:S(2)}) collective-permute-start(bf16[2,256,128]{2,1,0:T(8,128)(2,1)S(1)} %get-tuple-element.76), channel_id=1, source_target_pairs={{0,6},{1,7},{2,4},{3,5},{4,2},{5,3},{6,0},{7,1},{8,14},{9,15},{10,... | collective-permute-start | bytes 393224 | tf_op jit(solution)/shard_map/ppermute | solution.py:387
  30.0 3.5 %collective-permute-start.12 = (bf16[2,512,128]{2,1,0:T(8,128)(2,1)S(1)}, bf16[2,512,128]{2,1,0:T(8,128)(2,1)S(1)}, u32[]{:S(2)}, u32[]{:S(2)}) collective-permute-start(bf16[2,512,128]{2,1,0:T(8,128)(2,1)S(1)} %theirs.3), channel_id=1, source_target_pairs={{0,1},{1,0},{2,3},{3,2},{4,5},{5,4},{6,7},{7,6},{8,9},{9,8},{10,11... | collective-permute-start | bytes 786440 | tf_op jit(solution)/shard_map/ppermute | solution.py:387
  32.9 1.6 %collective-permute-start.11 = (bf16[2,512,128]{2,1,0:T(8,128)(2,1)S(1)}, bf16[2,512,128]{2,1,0:T(8,128)(2,1)S(1)}, u32[]{:S(2)}, u32[]{:S(2)}) collective-permute-start(bf16[2,512,128]{2,1,0:T(8,128)(2,1)S(1)} %theirs.2), channel_id=1, source_target_pairs={{0,1},{1,0},{2,3},{3,2},{4,5},{5,4},{6,7},{7,6},{8,9},{9,8},{10,11... | collective-permute-start | bytes 786440 | tf_op jit(solution)/shard_map/ppermute | solution.py:387

commit v23 on v20

--- a/solution.py
+++ b/solution.py
@@ -73,37 +73,37 @@
     one_ahead(products(), use)
 
 
-def load_kernel(*refs):
-    tokens, held, (out, sems) = refs[:4], refs[4:8], refs[8:]
-    copies = [pltpu.make_async_copy(tokens[i], held[i], sems.at[i]) for i in range(4)]
-    width = held[0].shape[1]
-    start = block_start(False, 0, width // 2)
+def give_kernel(*refs):
+    tokens, (out, held, sems) = refs[:4], refs[4:]
+    width = tokens[0].shape[1]
+    start = pl.multiple_of(block_start(False, 0, width // 2), width // 4)
     pairs = ((1, 2), (0, 3))
+    copies = [
+        pltpu.make_async_copy(ref.at[:, pl.ds(start, width // 4)], held.at[i], sems.at[i])
+        for i, ref in enumerate(tokens)
+    ]
     for i in pairs[0] + pairs[1]:
         copies[i].start()
     for kind, pair in enumerate(pairs):
         for i in pair:
             copies[i].wait()
-        for n in range(4):
-            at = n * width // 4
-            pl.when(start == at)(functools.partial(sums_of, held, at, out, (kind,)))
-
-
-def load(tokens):
+        sums_of([held.at[i] for i in range(4)], 0, out, (kind,))
+
+
+def first_sums(tokens):
     rows, width = tokens[0].shape
-    *held, sums = pl.pallas_call(
-        load_kernel,
-        name="load",
+    return pl.pallas_call(
+        give_kernel,
+        name="first_sums",
         in_specs=[ANY] * 4,
-        out_specs=[VMEM] * 5,
-        out_shape=[pltpu.VMEM((rows, width), BF16)] * 4 + [pltpu.VMEM((2, width // 4, HEAD), BF16)],
-        scratch_shapes=[pltpu.SemaphoreType.DMA((4,))],
+        out_specs=VMEM,
+        out_shape=pltpu.VMEM((2, width // 4, HEAD), BF16),
+        scratch_shapes=[pltpu.VMEM((4, rows, width // 4), BF16), pltpu.SemaphoreType.DMA((4,))],
         cost_estimate=pl.CostEstimate(
-            flops=rows * width * HEAD, bytes_accessed=10 * rows * width, transcendentals=0
+            flops=rows * width * HEAD, bytes_accessed=3 * rows * width, transcendentals=0
         ),
         compiler_params=SMALL,
     )(*(pltpu.with_memory_space_constraint(x, pltpu.HBM) for x in tokens))
-    return tuple(held), sums
 
 
 def sums_kernel(wanted, *refs):
@@ -394,7 +394,8 @@
     far_count = lax.axis_size("inner") // 2
     outer_count = lax.axis_size("outer")
     scale = float(HEAD * queries.shape[0] * 2 * far_count * outer_count) ** (-0.5)
-    tokens, give = load((queries, keys, values, cotangent))
+    tokens = (queries, keys, values, cotangent)
+    give = first_sums(tokens)
     got = [swap(give, "inner", 1), swap(*sums(tokens, (False, 1)), "inner", 1)]
     keep = sums(tokens, (True, 0), (True, 1))
     slots = [slot for b in range(2) for slot in pair_slots(keep[b], got[b], far_count // 2)]

time: 35.7 us -> 35.6 us (level)
  no operation moved by 1% of the time
where the time goes in v23:
time: 35.6 us; the launch traced here: 35.5 us
  starting transfers between devices  13.6 us (38%)
  waiting for transfers between devices  12.3 us (35%)
  Pallas kernels  8.71 us (24%)
  between operations  0.79 us (2%)
    ppermute x13, starting transfers between devices, swap(): lax.ppermute(x, axis, [(i, i ^ bits) for i in range(lax.axis_size(axis))])  13.6 us
    ppermute x13, waiting for transfers between devices, swap(): lax.ppermute(x, axis, [(i, i ^ bits) for i in range(lax.axis_size(axis))])  12.3 us
    pallas_call x4, Pallas kernels, finish(): pl.pallas_call(functools.partial(finish_kernel, scale, own, block, len(sl...  3.69 us
    pallas_call x1, Pallas kernels, local_part(): pl.pallas_call(local_kernel, name='local', in_specs=[VMEM] * 4, out_specs...  2.16 us
    pallas_call x1, Pallas kernels, first_sums(): pl.pallas_call(give_kernel, name='first_sums', in_specs=[ANY] * 4, out_sp...  1.59 us
    pallas_call x2, Pallas kernels, sums(): pl.pallas_call(functools.partial(sums_kernel, wanted), name='sums', in_sp...  0.77 us
  transfers between devices with their start and end apart: 13, of which 7 were waited for; matrix products, arithmetic and copies ran while one was open for 0% of the time, Pallas kernels for 16%

profile of v23, /device:TPU:0, one launch (start us, length us, event | category | flops | bytes accessed | tf_op | source)
XLA Modules:
  0.0 35.5 jit_solution(7066633193578035859)
XLA Ops:
  0.7 1.6 %first_sums.1 = bf16[2,512,128]{2,1,0:T(8,128)(2,1)S(1)} custom-call(bf16[128,2048]{1,0:T(8,128)(2,1)} %refs_0_.15, bf16[128,2048]{1,0:T(8,128)(2,1)} %refs_1_.15, bf16[128,2048]{1,0:T(8,128)(2,1)} %refs_2_.15, bf16[128,2048]{1,0:T(8,128)(2,1)} %refs_3_.15), custom_call_target="tpu_custom_call" | custom-call | flops 33554432 | bytes 786432 | tf_op jit(solution)/shard_map/first_sums/pallas_call | solution.py:95
  2.3 0.5 %collective-permute-start = (bf16[2,512,128]{2,1,0:T(8,128)(2,1)S(1)}, bf16[2,512,128]{2,1,0:T(8,128)(2,1)S(1)}, u32[]{:S(2)}, u32[]{:S(2)}) collective-permute-start(bf16[2,512,128]{2,1,0:T(8,128)(2,1)S(1)} %first_sums.1), channel_id=1, source_target_pairs={{0,1},{1,0},{2,3},{3,2},{4,5},{5,4},{6,7},{7,6},{8,9},{9,8},{10,11... | collective-permute-start | bytes 786440 | tf_op jit(solution)/shard_map/ppermute | solution.py:386
  2.8 0.3 sums.3
  3.2 0.5 %sums.2 = (bf16[2,512,128]{2,1,0:T(8,128)(2,1)S(1)}, bf16[2,512,128]{2,1,0:T(8,128)(2,1)S(1)}) custom-call(bf16[128,2048]{1,0:T(8,128)(2,1)S(1)} %copy-done, bf16[128,2048]{1,0:T(8,128)(2,1)S(1)} %copy-done.1, bf16[128,2048]{1,0:T(8,128)(2,1)S(1)} %copy-done.2, bf16[128,2048]{1,0:T(8,128)(2,1)S(1)} %copy-done.3), custom_call_target="tpu_custom_call" | custom-call | flops 67108864 | bytes 1572864 | tf_op jit(solution)/shard_map/sums/pallas_call | solution.py:116
  3.7 0.2 collective-permute-done.got_ref.refs_10_
  4.0 2.9 %collective-permute-start.1 = (bf16[2,256,128]{2,1,0:T(8,128)(2,1)S(1)}, bf16[2,256,128]{2,1,0:T(8,128)(2,1)S(1)}, u32[]{:S(2)}, u32[]{:S(2)}) collective-permute-start(bf16[2,256,128]{2,1,0:T(8,128)(2,1)S(1)} %get-tuple-element.46), channel_id=1, source_target_pairs={{0,2},{1,3},{2,0},{3,1},{4,6},{5,7},{6,4},{7,5},{8,10},{9,11},{10,... | collective-permute-start | bytes 393224 | tf_op jit(solution)/shard_map/ppermute | solution.py:386
  7.0 1.6 %collective-permute-start.3 = (bf16[2,256,128]{2,1,0:T(8,128)(2,1)S(1)}, bf16[2,256,128]{2,1,0:T(8,128)(2,1)S(1)}, u32[]{:S(2)}, u32[]{:S(2)}) collective-permute-start(bf16[2,256,128]{2,1,0:T(8,128)(2,1)S(1)} %get-tuple-element.48), channel_id=1, source_target_pairs={{0,4},{1,5},{2,6},{3,7},{4,0},{5,1},{6,2},{7,3},{8,12},{9,13},{10,... | collective-permute-start | bytes 393224 | tf_op jit(solution)/shard_map/ppermute | solution.py:386
  8.6 0.3 collective-permute-start.4
  8.9 2.2 %local.1 = (f32[128,2048]{1,0:T(8,128)S(1)}, f32[128,2048]{1,0:T(8,128)S(1)}, f32[128,2048]{1,0:T(8,128)S(1)}, f32[128,2048]{1,0:T(8,128)S(1)}) custom-call(bf16[128,2048]{1,0:T(8,128)(2,1)S(1)} %copy-done, bf16[128,2048]{1,0:T(8,128)(2,1)S(1)} %copy-done.1, bf16[128,2048]{1,0:T(8,128)(2,1)S(1)} %copy-done.2, bf16[128,2048]{1,0:T(8,128)(2,1)S(1)} %copy-done.3), custom_call_target="tpu_custom_call" | custom-call | flops 402653184 | bytes 6291456 | tf_op jit(solution)/shard_map/local/pallas_call | solution.py:274
  11.1 4.0 %collective-permute-done.3.refs_2_ = bf16[2,256,128]{2,1,0:T(8,128)(2,1)S(1)} collective-permute-done((bf16[2,256,128]{2,1,0:T(8,128)(2,1)S(1)}, bf16[2,256,128]{2,1,0:T(8,128)(2,1)S(1)}, u32[]{:S(2)}, u32[]{:S(2)}) %collective-permute-start.3) | collective-permute-done | bytes 131104 | tf_op jit(solution)/shard_map/ppermute | solution.py:386
  15.2 3.7 %collective-permute-start.5 = (bf16[256,128]{1,0:T(8,128)(2,1)S(1)}, bf16[256,128]{1,0:T(8,128)(2,1)S(1)}, u32[]{:S(2)}, u32[]{:S(2)}) collective-permute-start(bf16[256,128]{1,0:T(8,128)(2,1)S(1)} %get-tuple-element.62), channel_id=1, source_target_pairs={{0,24},{8,16},{16,8},{24,0},{1,25},{9,17},{17,9},{25,1},{2,26},{10... | collective-permute-start | bytes 196616 | tf_op jit(solution)/shard_map/ppermute | solution.py:386
  18.9 0.8 %collective-permute-start.7 = (bf16[256,128]{1,0:T(8,128)(2,1)S(1)}, bf16[256,128]{1,0:T(8,128)(2,1)S(1)}, u32[]{:S(2)}, u32[]{:S(2)}) collective-permute-start(bf16[256,128]{1,0:T(8,128)(2,1)S(1)} %get-tuple-element.64), channel_id=1, source_target_pairs={{0,8},{8,0},{16,24},{24,16},{1,9},{9,1},{17,25},{25,17},{2,10},{10... | collective-permute-start | bytes 196616 | tf_op jit(solution)/shard_map/ppermute | solution.py:386
  19.7 1.7 %collective-permute-done.5.refs_4_ = bf16[256,128]{1,0:T(8,128)(2,1)S(1)} collective-permute-done((bf16[256,128]{1,0:T(8,128)(2,1)S(1)}, bf16[256,128]{1,0:T(8,128)(2,1)S(1)}, u32[]{:S(2)}, u32[]{:S(2)}) %collective-permute-start.5) | collective-permute-done | bytes 65568 | tf_op jit(solution)/shard_map/ppermute | solution.py:386
  21.4 2.7 %collective-permute-done.6.refs_5_ = bf16[256,128]{1,0:T(8,128)(2,1)S(1)} collective-permute-done((bf16[256,128]{1,0:T(8,128)(2,1)S(1)}, bf16[256,128]{1,0:T(8,128)(2,1)S(1)}, u32[]{:S(2)}, u32[]{:S(2)}) %collective-permute-start.6) | collective-permute-done | bytes 65568 | tf_op jit(solution)/shard_map/ppermute | solution.py:386
  24.1 0.2 scan.1
  24.3 1.3 %collective-permute-start.10 = (bf16[2,256,128]{2,1,0:T(8,128)(2,1)S(1)}, bf16[2,256,128]{2,1,0:T(8,128)(2,1)S(1)}, u32[]{:S(2)}, u32[]{:S(2)}) collective-permute-start(bf16[2,256,128]{2,1,0:T(8,128)(2,1)S(1)} %get-tuple-element.68), channel_id=1, source_target_pairs={{0,2},{1,3},{2,0},{3,1},{4,6},{5,7},{6,4},{7,5},{8,10},{9,11},{10,... | collective-permute-start | bytes 393224 | tf_op jit(solution)/shard_map/ppermute | solution.py:386
  25.6 1.2 %collective-permute-start.8 = (bf16[2,256,128]{2,1,0:T(8,128)(2,1)S(1)}, bf16[2,256,128]{2,1,0:T(8,128)(2,1)S(1)}, u32[]{:S(2)}, u32[]{:S(2)}) collective-permute-start(bf16[2,256,128]{2,1,0:T(8,128)(2,1)S(1)} %get-tuple-element.65), channel_id=1, source_target_pairs={{0,4},{1,5},{2,6},{3,7},{4,0},{5,1},{6,2},{7,3},{8,12},{9,13},{10,... | collective-permute-start | bytes 393224 | tf_op jit(solution)/shard_map/ppermute | solution.py:386
  26.8 1.1 %collective-permute-start.9 = (bf16[2,256,128]{2,1,0:T(8,128)(2,1)S(1)}, bf16[2,256,128]{2,1,0:T(8,128)(2,1)S(1)}, u32[]{:S(2)}, u32[]{:S(2)}) collective-permute-start(bf16[2,256,128]{2,1,0:T(8,128)(2,1)S(1)} %get-tuple-element.66), channel_id=1, source_target_pairs={{0,6},{1,7},{2,4},{3,5},{4,2},{5,3},{6,0},{7,1},{8,14},{9,15},{10,... | collective-permute-start | bytes 393224 | tf_op jit(solution)/shard_map/ppermute | solution.py:386
  27.8 2.8 %collective-permute-done.10.refs_9_.refs_1_ = bf16[2,256,128]{2,1,0:T(8,128)(2,1)S(1)} collective-permute-done((bf16[2,256,128]{2,1,0:T(8,128)(2,1)S(1)}, bf16[2,256,128]{2,1,0:T(8,128)(2,1)S(1)}, u32[]{:S(2)}, u32[]{:S(2)}) %collective-permute-start.10) | collective-permute-done | bytes 131104 | tf_op jit(solution)/shard_map/ppermute | solution.py:386
  30.8 1.2 %finish.4 = (bf16[128,2048]{1,0:T(8,128)(2,1)}, bf16[128,2048]{1,0:T(8,128)(2,1)}, bf16[128,2048]{1,0:T(8,128)(2,1)}, bf16[128,2048]{1,0:T(8,128)(2,1)}) custom-call(bf16[128,2048]{1,0:T(8,128)(2,1)S(1)} %copy-done, bf16[128,2048]{1,0:T(8,128)(2,1)S(1)} %copy-done.1, bf16[128,2048]{1,0:T(8,128)(2,1)S(1)} %copy-done.2, bf16[128,2048]{1,0:T(8,128)(2,1)S(1)} %copy-done.3, ...), custom_call_target="tpu_custom_call" | custom-call | flops 67108864 | bytes 2097152 | tf_op jit(solution)/shard_map/finish/pallas_call | solution.py:368
  32.0 0.6 %collective-permute-done.9.refs_1_.refs_9_ = bf16[2,256,128]{2,1,0:T(8,128)(2,1)S(1)} collective-permute-done((bf16[2,256,128]{2,1,0:T(8,128)(2,1)S(1)}, bf16[2,256,128]{2,1,0:T(8,128)(2,1)S(1)}, u32[]{:S(2)}, u32[]{:S(2)}) %collective-permute-start.9) | collective-permute-done | bytes 131104 | tf_op jit(solution)/shard_map/ppermute | solution.py:386
  32.8 0.4 %finish.5.refs_9_ = bf16[4,128,512]{2,1,0:T(8,128)(2,1)S(1)} custom-call(bf16[128,2048]{1,0:T(8,128)(2,1)S(1)} %copy-done, bf16[128,2048]{1,0:T(8,128)(2,1)S(1)} %copy-done.1, bf16[128,2048]{1,0:T(8,128)(2,1)S(1)} %copy-done.2, bf16[128,2048]{1,0:T(8,128)(2,1)S(1)} %copy-done.3, f32[128,2048]{1,0:T(8,128)S(1)} %get-tuple-element.54.refs_4_, ...), custom_call_target="tpu_custom_call" | custom-call | flops 67108864 | bytes 2097152 | tf_op jit(solution)/shard_map/finish/pallas_call | solution.py:368
  33.2 0.9 %finish.6 = (bf16[128,2048]{1,0:T(8,128)(2,1)}, bf16[128,2048]{1,0:T(8,128)(2,1)}, bf16[128,2048]{1,0:T(8,128)(2,1)}, bf16[128,2048]{1,0:T(8,128)(2,1)}, bf16[4,128,512]{2,1,0:T(8,128)(2,1)S(1)}) custom-call(bf16[128,2048]{1,0:T(8,128)(2,1)S(1)} %copy-done, ...), custom_call_target="tpu_custom_call", output_to_operand_aliasing={{0}: (10, {}), {1}: (11, {}), {2}: (12, {}), {3}: (13, {})} | custom-call | flops 67108864 | bytes 2097152 | tf_op jit(solution)/shard_map/finish/pallas_call | solution.py:368
  34.3 1.2 %finish.7 = (bf16[128,2048]{1,0:T(8,128)(2,1)}, bf16[128,2048]{1,0:T(8,128)(2,1)}, bf16[128,2048]{1,0:T(8,128)(2,1)}, bf16[128,2048]{1,0:T(8,128)(2,1)}) custom-call(bf16[128,2048]{1,0:T(8,128)(2,1)S(1)} %copy-done, bf16[128,2048]{1,0:T(8,128)(2,1)S(1)} %copy-done.1, ...), custom_call_target="tpu_custom_call", output_to_operand_aliasing={{0}: (10, {}), {1}: (11, {}), {2}: (12, {}), {3}: (13, {})} | custom-call | flops 67108864 | bytes 2097152 | tf_op jit(solution)/shard_map/finish/pallas_call | solution.py:368
  (24 shorter events, 0.8 us)
Async XLA Ops:
  0.6 2.2 %copy-start.3 = (bf16[128,2048]{1,0:T(8,128)(2,1)S(1)}, bf16[128,2048]{1,0:T(8,128)(2,1)}, u32[]{:S(2)}) copy-start(bf16[128,2048]{1,0:T(8,128)(2,1)} %refs_3_.15) | copy-start | bytes 1572868
  0.6 2.1 %copy-start.2 = (bf16[128,2048]{1,0:T(8,128)(2,1)S(1)}, bf16[128,2048]{1,0:T(8,128)(2,1)}, u32[]{:S(2)}) copy-start(bf16[128,2048]{1,0:T(8,128)(2,1)} %refs_2_.15) | copy-start | bytes 1572868
  0.7 2.1 %copy-start.1 = (bf16[128,2048]{1,0:T(8,128)(2,1)S(1)}, bf16[128,2048]{1,0:T(8,128)(2,1)}, u32[]{:S(2)}) copy-start(bf16[128,2048]{1,0:T(8,128)(2,1)} %refs_1_.15) | copy-start | bytes 1572868
  0.7 2.1 %copy-start = (bf16[128,2048]{1,0:T(8,128)(2,1)S(1)}, bf16[128,2048]{1,0:T(8,128)(2,1)}, u32[]{:S(2)}) copy-start(bf16[128,2048]{1,0:T(8,128)(2,1)} %refs_0_.15) | copy-start | bytes 1572868
  2.3 1.7 %collective-permute-start = (bf16[2,512,128]{2,1,0:T(8,128)(2,1)S(1)}, bf16[2,512,128]{2,1,0:T(8,128)(2,1)S(1)}, u32[]{:S(2)}, u32[]{:S(2)}) collective-permute-start(bf16[2,512,128]{2,1,0:T(8,128)(2,1)S(1)} %first_sums.1), channel_id=1, source_target_pairs={{0,1},{1,0},{2,3},{3,2},{4,5},{5,4},{6,7},{7,6},{8,9},{9,8},{10,11... | collective-permute-start | bytes 786440 | tf_op jit(solution)/shard_map/ppermute | solution.py:386
  3.1 3.8 %collective-permute-start.2 = (bf16[2,512,128]{2,1,0:T(8,128)(2,1)S(1)}, bf16[2,512,128]{2,1,0:T(8,128)(2,1)S(1)}, u32[]{:S(2)}, u32[]{:S(2)}) collective-permute-start(bf16[2,512,128]{2,1,0:T(8,128)(2,1)S(1)} %sums.3), channel_id=1, source_target_pairs={{0,1},{1,0},{2,3},{3,2},{4,5},{5,4},{6,7},{7,6},{8,9},{9,8},{10,11... | collective-permute-start | bytes 786440 | tf_op jit(solution)/shard_map/ppermute | solution.py:386
  4.0 7.1 %collective-permute-start.1 = (bf16[2,256,128]{2,1,0:T(8,128)(2,1)S(1)}, bf16[2,256,128]{2,1,0:T(8,128)(2,1)S(1)}, u32[]{:S(2)}, u32[]{:S(2)}) collective-permute-start(bf16[2,256,128]{2,1,0:T(8,128)(2,1)S(1)} %get-tuple-element.46), channel_id=1, source_target_pairs={{0,2},{1,3},{2,0},{3,1},{4,6},{5,7},{6,4},{7,5},{8,10},{9,11},{10,... | collective-permute-start | bytes 393224 | tf_op jit(solution)/shard_map/ppermute | solution.py:386
  7.0 8.1 %collective-permute-start.3 = (bf16[2,256,128]{2,1,0:T(8,128)(2,1)S(1)}, bf16[2,256,128]{2,1,0:T(8,128)(2,1)S(1)}, u32[]{:S(2)}, u32[]{:S(2)}) collective-permute-start(bf16[2,256,128]{2,1,0:T(8,128)(2,1)S(1)} %get-tuple-element.48), channel_id=1, source_target_pairs={{0,4},{1,5},{2,6},{3,7},{4,0},{5,1},{6,2},{7,3},{8,12},{9,13},{10,... | collective-permute-start | bytes 393224 | tf_op jit(solution)/shard_map/ppermute | solution.py:386
  8.6 6.6 %collective-permute-start.4 = (bf16[2,256,128]{2,1,0:T(8,128)(2,1)S(1)}, bf16[2,256,128]{2,1,0:T(8,128)(2,1)S(1)}, u32[]{:S(2)}, u32[]{:S(2)}) collective-permute-start(bf16[2,256,128]{2,1,0:T(8,128)(2,1)S(1)} %get-tuple-element.49), channel_id=1, source_target_pairs={{0,6},{1,7},{2,4},{3,5},{4,2},{5,3},{6,0},{7,1},{8,14},{9,15},{10,... | collective-permute-start | bytes 393224 | tf_op jit(solution)/shard_map/ppermute | solution.py:386
  15.2 6.1 %collective-permute-start.5 = (bf16[256,128]{1,0:T(8,128)(2,1)S(1)}, bf16[256,128]{1,0:T(8,128)(2,1)S(1)}, u32[]{:S(2)}, u32[]{:S(2)}) collective-permute-start(bf16[256,128]{1,0:T(8,128)(2,1)S(1)} %get-tuple-element.62), channel_id=1, source_target_pairs={{0,24},{8,16},{16,8},{24,0},{1,25},{9,17},{17,9},{25,1},{2,26},{10... | collective-permute-start | bytes 196616 | tf_op jit(solution)/shard_map/ppermute | solution.py:386
  18.9 5.2 %collective-permute-start.6 = (bf16[256,128]{1,0:T(8,128)(2,1)S(1)}, bf16[256,128]{1,0:T(8,128)(2,1)S(1)}, u32[]{:S(2)}, u32[]{:S(2)}) collective-permute-start(bf16[256,128]{1,0:T(8,128)(2,1)S(1)} %get-tuple-element.63), channel_id=1, source_target_pairs={{0,16},{8,24},{16,0},{24,8},{1,17},{9,25},{17,1},{25,9},{2,18},{10... | collective-permute-start | bytes 196616 | tf_op jit(solution)/shard_map/ppermute | solution.py:386
  18.9 5.2 %collective-permute-start.7 = (bf16[256,128]{1,0:T(8,128)(2,1)S(1)}, bf16[256,128]{1,0:T(8,128)(2,1)S(1)}, u32[]{:S(2)}, u32[]{:S(2)}) collective-permute-start(bf16[256,128]{1,0:T(8,128)(2,1)S(1)} %get-tuple-element.64), channel_id=1, source_target_pairs={{0,8},{8,0},{16,24},{24,16},{1,9},{9,1},{17,25},{25,17},{2,10},{10... | collective-permute-start | bytes 196616 | tf_op jit(solution)/shard_map/ppermute | solution.py:386
  24.3 6.4 %collective-permute-start.10 = (bf16[2,256,128]{2,1,0:T(8,128)(2,1)S(1)}, bf16[2,256,128]{2,1,0:T(8,128)(2,1)S(1)}, u32[]{:S(2)}, u32[]{:S(2)}) collective-permute-start(bf16[2,256,128]{2,1,0:T(8,128)(2,1)S(1)} %get-tuple-element.68), channel_id=1, source_target_pairs={{0,2},{1,3},{2,0},{3,1},{4,6},{5,7},{6,4},{7,5},{8,10},{9,11},{10,... | collective-permute-start | bytes 393224 | tf_op jit(solution)/shard_map/ppermute | solution.py:386
  25.6 6.4 %collective-permute-start.8 = (bf16[2,256,128]{2,1,0:T(8,128)(2,1)S(1)}, bf16[2,256,128]{2,1,0:T(8,128)(2,1)S(1)}, u32[]{:S(2)}, u32[]{:S(2)}) collective-permute-start(bf16[2,256,128]{2,1,0:T(8,128)(2,1)S(1)} %get-tuple-element.65), channel_id=1, source_target_pairs={{0,4},{1,5},{2,6},{3,7},{4,0},{5,1},{6,2},{7,3},{8,12},{9,13},{10,... | collective-permute-start | bytes 393224 | tf_op jit(solution)/shard_map/ppermute | solution.py:386
  26.8 5.9 %collective-permute-start.9 = (bf16[2,256,128]{2,1,0:T(8,128)(2,1)S(1)}, bf16[2,256,128]{2,1,0:T(8,128)(2,1)S(1)}, u32[]{:S(2)}, u32[]{:S(2)}) collective-permute-start(bf16[2,256,128]{2,1,0:T(8,128)(2,1)S(1)} %get-tuple-element.66), channel_id=1, source_target_pairs={{0,6},{1,7},{2,4},{3,5},{4,2},{5,3},{6,0},{7,1},{8,14},{9,15},{10,... | collective-permute-start | bytes 393224 | tf_op jit(solution)/shard_map/ppermute | solution.py:386
  30.7 2.5 %collective-permute-start.12 = (bf16[2,512,128]{2,1,0:T(8,128)(2,1)S(1)}, bf16[2,512,128]{2,1,0:T(8,128)(2,1)S(1)}, u32[]{:S(2)}, u32[]{:S(2)}) collective-permute-start(bf16[2,512,128]{2,1,0:T(8,128)(2,1)S(1)} %theirs.3), channel_id=1, source_target_pairs={{0,1},{1,0},{2,3},{3,2},{4,5},{5,4},{6,7},{7,6},{8,9},{9,8},{10,11... | collective-permute-start | bytes 786440 | tf_op jit(solution)/shard_map/ppermute | solution.py:386
  32.7 1.6 %collective-permute-start.11 = (bf16[2,512,128]{2,1,0:T(8,128)(2,1)S(1)}, bf16[2,512,128]{2,1,0:T(8,128)(2,1)S(1)}, u32[]{:S(2)}, u32[]{:S(2)}) collective-permute-start(bf16[2,512,128]{2,1,0:T(8,128)(2,1)S(1)} %theirs.2), channel_id=1, source_target_pairs={{0,1},{1,0},{2,3},{3,2},{4,5},{5,4},{6,7},{7,6},{8,9},{9,8},{10,11... | collective-permute-start | bytes 786440 | tf_op jit(solution)/shard_map/ppermute | solution.py:386

commit v24 on v20

--- a/solution.py
+++ b/solution.py
@@ -128,7 +128,7 @@
     )(*tokens)
 
 
-def pair_kernel(keep_ref, got_ref, *slots):
+def pair_kernel(keep_ref, got_ref, _, *slots):
     for s, slot in enumerate(slots):
         part = slot_rows(s, len(slots), slot.shape[1])
         for which in range(2):
@@ -136,16 +136,16 @@
             slot[which] = both.astype(BF16)
 
 
-def pair_slots(keep, got, count):
+def pair_slots(keep, got, count, after):
     slot = jax.ShapeDtypeStruct((2, keep.shape[1] // count, HEAD), BF16)
     return pl.pallas_call(
         pair_kernel,
         name="pair",
-        in_specs=[VMEM] * 2,
+        in_specs=[VMEM] * 2 + [ANY],
         out_specs=[VMEM] * count,
         out_shape=[slot] * count,
         compiler_params=SMALL,
-    )(keep, got)
+    )(keep, got, after)
 
 
 def totals_kernel(far_count, *refs):
@@ -240,8 +240,12 @@
     )(*slots, keep)
 
 
-def local_kernel(*refs):
-    tokens, outs = refs[:4], refs[4:]
+def local_kernel(core, *refs):
+    near, _ = near_far()
+    pl.when(near == core)(functools.partial(local_products, refs[:4], refs[-4:]))
+
+
+def local_products(tokens, outs):
     rows, width = tokens[0].shape
     at = lax.broadcasted_iota(jnp.int32, (rows, rows), 0)
     to = lax.broadcasted_iota(jnp.int32, (rows, rows), 1)
@@ -269,19 +273,17 @@
     second(*last)
 
 
-def local_part(tokens):
+def local_part(core, tokens, after):
     rows, width = tokens[0].shape
     return pl.pallas_call(
-        local_kernel,
+        functools.partial(local_kernel, core),
         name="local",
-        in_specs=[VMEM] * 4,
+        in_specs=[VMEM] * 4 + [ANY],
         out_specs=[VMEM] * 4,
         out_shape=[jax.ShapeDtypeStruct((rows, width), F32)] * 4,
-        cost_estimate=pl.CostEstimate(
-            flops=12 * rows * width * HEAD, bytes_accessed=24 * rows * width, transcendentals=0
-        ),
-        compiler_params=SMALL,
-    )(*tokens)
+        cost_estimate=pl.CostEstimate(flops=0, bytes_accessed=0, transcendentals=0),
+        compiler_params=SMALL,
+    )(*tokens, after)
 
 
 def all_products(scale, start, tokens, local, states, store):
@@ -315,7 +317,7 @@
 
 
 def finish_kernel(scale, own, block, count, rests, hold, *refs):
-    tokens, local, slots, refs = refs[:4], refs[4:8], refs[8 : 8 + count], refs[8 + count :]
+    tokens, locals_, slots, refs = refs[:4], refs[4:12], refs[12 : 12 + count], refs[12 + count :]
     got, refs = (refs[0], refs[1:]) if own else (None, refs)
     late, refs = refs[: len(rests)], refs[len(rests) :]
     if own:
@@ -341,8 +343,10 @@
                     copy.start()
 
     def run(quarter):
+        core = quarter // 2 if own else 1 - quarter // 2
+        local = locals_[4 * core : 4 * core + 4]
         for s, slot in enumerate(slots if own else ()):
-            core, part = quarter // 2, slot_rows(s, count, slot.shape[1])
+            part = slot_rows(s, count, slot.shape[1])
             states[core, part] = slot[core]
             states[1 - core, part] = with_sums(slot, 1 - core, got, part)
         all_products(scale, quarter * width // 4, tokens, local, states, store)
@@ -397,8 +401,12 @@
     tokens, give = load((queries, keys, values, cotangent))
     got = [swap(give, "inner", 1), swap(*sums(tokens, (False, 1)), "inner", 1)]
     keep = sums(tokens, (True, 0), (True, 1))
-    slots = [slot for b in range(2) for slot in pair_slots(keep[b], got[b], far_count // 2)]
-    slots, local = lax.optimization_barrier((swap_far(slots), local_part(tokens)))
+    early = local_part(0, tokens, keep[1])
+    slots = []
+    for b in range(2):
+        slots += pair_slots(keep[b], got[b], far_count // 2, slots[0] if slots else early[0])
+    slots, late = lax.optimization_barrier((swap_far(slots), local_part(1, tokens, slots[-1])))
+    local = [*early, *late]
     sends = group_sends(slots, outer_count)
     others = [swap(send, "outer", s) for s, send in zip(distances(outer_count), sends)]
     slots = swap_far(scan_slots(slots, others))

time: 35.7 us -> 35.8 us (level)
    pallas_call x3 -> x4, Pallas kernels: 2.28 us -> 2.31 us  [the longest x2 2.17 us: local_part(): pl.pallas_call(functools.partial(local_kernel, core), name='local', in_sp...]
  transfers between devices with their start and end apart: 13 -> 13, of which waited for: 7 -> 8; matrix products, arithmetic and copies ran while one was open for 0% -> 0% of each run, Pallas kernels for 16% -> 16%
where the time goes in v24:
time: 35.8 us; the launch traced here: 35.7 us
  starting transfers between devices  13.4 us (37%)
  waiting for transfers between devices  12.6 us (35%)
  Pallas kernels  8.91 us (25%)
  between operations  0.76 us (2%)
    ppermute x13, starting transfers between devices, swap(): lax.ppermute(x, axis, [(i, i ^ bits) for i in range(lax.axis_size(axis))])  13.4 us
    ppermute x13, waiting for transfers between devices, swap(): lax.ppermute(x, axis, [(i, i ^ bits) for i in range(lax.axis_size(axis))])  12.6 us
    pallas_call x4, Pallas kernels, finish(): pl.pallas_call(functools.partial(finish_kernel, scale, own, block, len(sl...  3.69 us
    pallas_call x2, Pallas kernels, local_part(): pl.pallas_call(functools.partial(local_kernel, core), name='local', in_sp...  2.17 us
    pallas_call x1, Pallas kernels, load(): pl.pallas_call(load_kernel, name='load', in_specs=[ANY] * 4, out_specs=[V...  1.77 us
    pallas_call x2, Pallas kernels, sums(): pl.pallas_call(functools.partial(sums_kernel, wanted), name='sums', in_sp...  0.75 us
  transfers between devices with their start and end apart: 13, of which 8 were waited for; matrix products, arithmetic and copies ran while one was open for 0% of the time, Pallas kernels for 16%

profile of v24, /device:TPU:0, one launch (start us, length us, event | category | flops | bytes accessed | tf_op | source)
XLA Modules:
  0.0 35.7 jit_solution(10284916527292400777)
XLA Ops:
  0.6 1.8 %load.1 = (bf16[128,2048]{1,0:T(8,128)(2,1)S(1)}, bf16[128,2048]{1,0:T(8,128)(2,1)S(1)}, bf16[128,2048]{1,0:T(8,128)(2,1)S(1)}, bf16[128,2048]{1,0:T(8,128)(2,1)S(1)}, bf16[2,512,128]{2,1,0:T(8,128)(2,1)S(1)}) custom-call(bf16[128,2048]{1,0:T(8,128)(2,1)} %refs_0_.1, bf16[128,2048]{1,0:T(8,128)(2,1)} %refs_1_.1, bf16[128,2048]{1,0:T(8,128)(2,1)} %refs_2_.1, ...), custom_call_target="tpu_custom_call" | custom-call | flops 33554432 | bytes 2621440 | tf_op jit(solution)/shard_map/load/pallas_call | solution.py:94
  2.4 0.5 %collective-permute-start = (bf16[2,512,128]{2,1,0:T(8,128)(2,1)S(1)}, bf16[2,512,128]{2,1,0:T(8,128)(2,1)S(1)}, u32[]{:S(2)}, u32[]{:S(2)}) collective-permute-start(bf16[2,512,128]{2,1,0:T(8,128)(2,1)S(1)} %get-tuple-element.63), channel_id=1, source_target_pairs={{0,1},{1,0},{2,3},{3,2},{4,5},{5,4},{6,7},{7,6},{8,9},{9,8},{10,11... | collective-permute-start | bytes 786440 | tf_op jit(solution)/shard_map/ppermute | solution.py:390
  2.9 0.3 sums.3
  3.3 0.5 %sums.2 = (bf16[2,512,128]{2,1,0:T(8,128)(2,1)S(1)}, bf16[2,512,128]{2,1,0:T(8,128)(2,1)S(1)}) custom-call(bf16[128,2048]{1,0:T(8,128)(2,1)S(1)} %get-tuple-element.53.refs_0_, bf16[128,2048]{1,0:T(8,128)(2,1)S(1)} %get-tuple-element.54.refs_1_, bf16[128,2048]{1,0:T(8,128)(2,1)S(1)} %get-tuple-element.55.refs_2_, bf16[128,2048]{1,0:T(8,128)(2,1)S(1)} %get-tuple-element.56.refs_3_), custom_call_target="tpu_custom_call" | custom-call | flops 67108864 | bytes 1572864 | tf_op jit(solution)/shard_map/sums/pallas_call | solution.py:116
  3.8 2.2 %local.2 = (f32[128,2048]{1,0:T(8,128)S(1)}, f32[128,2048]{1,0:T(8,128)S(1)}, f32[128,2048]{1,0:T(8,128)S(1)}, f32[128,2048]{1,0:T(8,128)S(1)}) custom-call(bf16[128,2048]{1,0:T(8,128)(2,1)S(1)} %get-tuple-element.53.refs_0_, bf16[128,2048]{1,0:T(8,128)(2,1)S(1)} %get-tuple-element.54.refs_1_, bf16[128,2048]{1,0:T(8,128)(2,1)S(1)} %get-tuple-element.55.refs_2_, ...), custom_call_target="tpu_custom_call" | custom-call | tf_op jit(solution)/shard_map/local/pallas_call | solution.py:278
  6.1 3.0 %collective-permute-start.1 = (bf16[2,256,128]{2,1,0:T(8,128)(2,1)S(1)}, bf16[2,256,128]{2,1,0:T(8,128)(2,1)S(1)}, u32[]{:S(2)}, u32[]{:S(2)}) collective-permute-start(bf16[2,256,128]{2,1,0:T(8,128)(2,1)S(1)} %get-tuple-element.65), channel_id=1, source_target_pairs={{0,2},{1,3},{2,0},{3,1},{4,6},{5,7},{6,4},{7,5},{8,10},{9,11},{10,... | collective-permute-start | bytes 393224 | tf_op jit(solution)/shard_map/ppermute | solution.py:390
  9.2 1.6 %collective-permute-start.3 = (bf16[2,256,128]{2,1,0:T(8,128)(2,1)S(1)}, bf16[2,256,128]{2,1,0:T(8,128)(2,1)S(1)}, u32[]{:S(2)}, u32[]{:S(2)}) collective-permute-start(bf16[2,256,128]{2,1,0:T(8,128)(2,1)S(1)} %get-tuple-element.66), channel_id=1, source_target_pairs={{0,4},{1,5},{2,6},{3,7},{4,0},{5,1},{6,2},{7,3},{8,12},{9,13},{10,... | collective-permute-start | bytes 393224 | tf_op jit(solution)/shard_map/ppermute | solution.py:390
  10.8 2.4 %collective-permute-done.1.refs_1_ = bf16[2,256,128]{2,1,0:T(8,128)(2,1)S(1)} collective-permute-done((bf16[2,256,128]{2,1,0:T(8,128)(2,1)S(1)}, bf16[2,256,128]{2,1,0:T(8,128)(2,1)S(1)}, u32[]{:S(2)}, u32[]{:S(2)}) %collective-permute-start.1) | collective-permute-done | bytes 131104 | tf_op jit(solution)/shard_map/ppermute | solution.py:390
  13.2 1.8 %collective-permute-done.3.refs_2_ = bf16[2,256,128]{2,1,0:T(8,128)(2,1)S(1)} collective-permute-done((bf16[2,256,128]{2,1,0:T(8,128)(2,1)S(1)}, bf16[2,256,128]{2,1,0:T(8,128)(2,1)S(1)}, u32[]{:S(2)}, u32[]{:S(2)}) %collective-permute-start.3) | collective-permute-done | bytes 131104 | tf_op jit(solution)/shard_map/ppermute | solution.py:390
  15.1 1.5 %collective-permute-done.4.refs_3_ = bf16[2,256,128]{2,1,0:T(8,128)(2,1)S(1)} collective-permute-done((bf16[2,256,128]{2,1,0:T(8,128)(2,1)S(1)}, bf16[2,256,128]{2,1,0:T(8,128)(2,1)S(1)}, u32[]{:S(2)}, u32[]{:S(2)}) %collective-permute-start.4) | collective-permute-done | bytes 131104 | tf_op jit(solution)/shard_map/ppermute | solution.py:390
  16.7 3.7 %collective-permute-start.5 = (bf16[256,128]{1,0:T(8,128)(2,1)S(1)}, bf16[256,128]{1,0:T(8,128)(2,1)S(1)}, u32[]{:S(2)}, u32[]{:S(2)}) collective-permute-start(bf16[256,128]{1,0:T(8,128)(2,1)S(1)} %get-tuple-element.80), channel_id=1, source_target_pairs={{0,24},{8,16},{16,8},{24,0},{1,25},{9,17},{17,9},{25,1},{2,26},{10... | collective-permute-start | bytes 196616 | tf_op jit(solution)/shard_map/ppermute | solution.py:390
  20.4 0.8 %collective-permute-start.7 = (bf16[256,128]{1,0:T(8,128)(2,1)S(1)}, bf16[256,128]{1,0:T(8,128)(2,1)S(1)}, u32[]{:S(2)}, u32[]{:S(2)}) collective-permute-start(bf16[256,128]{1,0:T(8,128)(2,1)S(1)} %get-tuple-element.82), channel_id=1, source_target_pairs={{0,8},{8,0},{16,24},{24,16},{1,9},{9,1},{17,25},{25,17},{2,10},{10... | collective-permute-start | bytes 196616 | tf_op jit(solution)/shard_map/ppermute | solution.py:390
  21.2 2.2 %collective-permute-done.5.refs_4_ = bf16[256,128]{1,0:T(8,128)(2,1)S(1)} collective-permute-done((bf16[256,128]{1,0:T(8,128)(2,1)S(1)}, bf16[256,128]{1,0:T(8,128)(2,1)S(1)}, u32[]{:S(2)}, u32[]{:S(2)}) %collective-permute-start.5) | collective-permute-done | bytes 65568 | tf_op jit(solution)/shard_map/ppermute | solution.py:390
  23.4 2.1 %collective-permute-done.6.refs_5_ = bf16[256,128]{1,0:T(8,128)(2,1)S(1)} collective-permute-done((bf16[256,128]{1,0:T(8,128)(2,1)S(1)}, bf16[256,128]{1,0:T(8,128)(2,1)S(1)}, u32[]{:S(2)}, u32[]{:S(2)}) %collective-permute-start.6) | collective-permute-done | bytes 65568 | tf_op jit(solution)/shard_map/ppermute | solution.py:390
  25.5 0.2 scan.1
  25.8 0.6 %collective-permute-start.10 = (bf16[2,256,128]{2,1,0:T(8,128)(2,1)S(1)}, bf16[2,256,128]{2,1,0:T(8,128)(2,1)S(1)}, u32[]{:S(2)}, u32[]{:S(2)}) collective-permute-start(bf16[2,256,128]{2,1,0:T(8,128)(2,1)S(1)} %get-tuple-element.86), channel_id=1, source_target_pairs={{0,2},{1,3},{2,0},{3,1},{4,6},{5,7},{6,4},{7,5},{8,10},{9,11},{10,... | collective-permute-start | bytes 393224 | tf_op jit(solution)/shard_map/ppermute | solution.py:390
  26.4 0.6 %collective-permute-start.8 = (bf16[2,256,128]{2,1,0:T(8,128)(2,1)S(1)}, bf16[2,256,128]{2,1,0:T(8,128)(2,1)S(1)}, u32[]{:S(2)}, u32[]{:S(2)}) collective-permute-start(bf16[2,256,128]{2,1,0:T(8,128)(2,1)S(1)} %get-tuple-element.83), channel_id=1, source_target_pairs={{0,4},{1,5},{2,6},{3,7},{4,0},{5,1},{6,2},{7,3},{8,12},{9,13},{10,... | collective-permute-start | bytes 393224 | tf_op jit(solution)/shard_map/ppermute | solution.py:390
  27.0 2.3 %collective-permute-start.9 = (bf16[2,256,128]{2,1,0:T(8,128)(2,1)S(1)}, bf16[2,256,128]{2,1,0:T(8,128)(2,1)S(1)}, u32[]{:S(2)}, u32[]{:S(2)}) collective-permute-start(bf16[2,256,128]{2,1,0:T(8,128)(2,1)S(1)} %get-tuple-element.84), channel_id=1, source_target_pairs={{0,6},{1,7},{2,4},{3,5},{4,2},{5,3},{6,0},{7,1},{8,14},{9,15},{10,... | collective-permute-start | bytes 393224 | tf_op jit(solution)/shard_map/ppermute | solution.py:390
  29.3 1.5 %collective-permute-done.10.refs_13_.refs_1_ = bf16[2,256,128]{2,1,0:T(8,128)(2,1)S(1)} collective-permute-done((bf16[2,256,128]{2,1,0:T(8,128)(2,1)S(1)}, bf16[2,256,128]{2,1,0:T(8,128)(2,1)S(1)}, u32[]{:S(2)}, u32[]{:S(2)}) %collective-permute-start.10) | collective-permute-done | bytes 131104 | tf_op jit(solution)/shard_map/ppermute | solution.py:390
  30.9 1.2 %finish.4 = (bf16[128,2048]{1,0:T(8,128)(2,1)}, bf16[128,2048]{1,0:T(8,128)(2,1)}, bf16[128,2048]{1,0:T(8,128)(2,1)}, bf16[128,2048]{1,0:T(8,128)(2,1)}) custom-call(bf16[128,2048]{1,0:T(8,128)(2,1)S(1)} %get-tuple-element.53.refs_0_, bf16[128,2048]{1,0:T(8,128)(2,1)S(1)} %get-tuple-element.54.refs_1_, bf16[128,2048]{1,0:T(8,128)(2,1)S(1)} %get-tuple-element.55.refs_2_, ...), custom_call_target="tpu_custom_call" | custom-call | flops 67108864 | bytes 2097152 | tf_op jit(solution)/shard_map/finish/pallas_call | solution.py:372
  32.1 0.7 %collective-permute-done.9.refs_1_.refs_13_ = bf16[2,256,128]{2,1,0:T(8,128)(2,1)S(1)} collective-permute-done((bf16[2,256,128]{2,1,0:T(8,128)(2,1)S(1)}, bf16[2,256,128]{2,1,0:T(8,128)(2,1)S(1)}, u32[]{:S(2)}, u32[]{:S(2)}) %collective-permute-start.9) | collective-permute-done | bytes 131104 | tf_op jit(solution)/shard_map/ppermute | solution.py:390
  33.0 0.4 %finish.5.refs_13_ = bf16[4,128,512]{2,1,0:T(8,128)(2,1)S(1)} custom-call(bf16[128,2048]{1,0:T(8,128)(2,1)S(1)} %get-tuple-element.53.refs_0_, bf16[128,2048]{1,0:T(8,128)(2,1)S(1)} %get-tuple-element.54.refs_1_, bf16[128,2048]{1,0:T(8,128)(2,1)S(1)} %get-tuple-element.55.refs_2_, bf16[128,2048]{1,0:T(8,128)(2,1)S(1)} %get-tuple-element.56.refs_3_, ...), custom_call_target="tpu_custom_call" | custom-call | flops 67108864 | bytes 2097152 | tf_op jit(solution)/shard_map/finish/pallas_call | solution.py:372
  33.4 0.9 %finish.6 = (bf16[128,2048]{1,0:T(8,128)(2,1)}, bf16[128,2048]{1,0:T(8,128)(2,1)}, bf16[128,2048]{1,0:T(8,128)(2,1)}, bf16[128,2048]{1,0:T(8,128)(2,1)}, bf16[4,128,512]{2,1,0:T(8,128)(2,1)S(1)}) custom-call(bf16[128,2048]{1,0:T(8,128)(2,1)S(1)} %get-tuple-element.53.refs_0_, ...), custom_call_target="tpu_custom_call", output_to_operand_aliasing={{0}: (14, {}), {1}: (15, {}), {2}: (16, {}), {3}: (17, {})} | custom-call | flops 67108864 | bytes 2097152 | tf_op jit(solution)/shard_map/finish/pallas_call | solution.py:372
  34.5 1.2 %finish.7 = (bf16[128,2048]{1,0:T(8,128)(2,1)}, bf16[128,2048]{1,0:T(8,128)(2,1)}, bf16[128,2048]{1,0:T(8,128)(2,1)}, bf16[128,2048]{1,0:T(8,128)(2,1)}) custom-call(bf16[128,2048]{1,0:T(8,128)(2,1)S(1)} %get-tuple-element.53.refs_0_, ...), custom_call_target="tpu_custom_call", output_to_operand_aliasing={{0}: (14, {}), {1}: (15, {}), {2}: (16, {}), {3}: (17, {})} | custom-call | flops 67108864 | bytes 2097152 | tf_op jit(solution)/shard_map/finish/pallas_call | solution.py:372
  (17 shorter events, 0.8 us)
Async XLA Ops:
  2.4 3.6 %collective-permute-start = (bf16[2,512,128]{2,1,0:T(8,128)(2,1)S(1)}, bf16[2,512,128]{2,1,0:T(8,128)(2,1)S(1)}, u32[]{:S(2)}, u32[]{:S(2)}) collective-permute-start(bf16[2,512,128]{2,1,0:T(8,128)(2,1)S(1)} %get-tuple-element.63), channel_id=1, source_target_pairs={{0,1},{1,0},{2,3},{3,2},{4,5},{5,4},{6,7},{7,6},{8,9},{9,8},{10,11... | collective-permute-start | bytes 786440 | tf_op jit(solution)/shard_map/ppermute | solution.py:390
  3.2 5.9 %collective-permute-start.2 = (bf16[2,512,128]{2,1,0:T(8,128)(2,1)S(1)}, bf16[2,512,128]{2,1,0:T(8,128)(2,1)S(1)}, u32[]{:S(2)}, u32[]{:S(2)}) collective-permute-start(bf16[2,512,128]{2,1,0:T(8,128)(2,1)S(1)} %sums.3), channel_id=1, source_target_pairs={{0,1},{1,0},{2,3},{3,2},{4,5},{5,4},{6,7},{7,6},{8,9},{9,8},{10,11... | collective-permute-start | bytes 786440 | tf_op jit(solution)/shard_map/ppermute | solution.py:390
  6.1 7.1 %collective-permute-start.1 = (bf16[2,256,128]{2,1,0:T(8,128)(2,1)S(1)}, bf16[2,256,128]{2,1,0:T(8,128)(2,1)S(1)}, u32[]{:S(2)}, u32[]{:S(2)}) collective-permute-start(bf16[2,256,128]{2,1,0:T(8,128)(2,1)S(1)} %get-tuple-element.65), channel_id=1, source_target_pairs={{0,2},{1,3},{2,0},{3,1},{4,6},{5,7},{6,4},{7,5},{8,10},{9,11},{10,... | collective-permute-start | bytes 393224 | tf_op jit(solution)/shard_map/ppermute | solution.py:390
  9.2 5.9 %collective-permute-start.3 = (bf16[2,256,128]{2,1,0:T(8,128)(2,1)S(1)}, bf16[2,256,128]{2,1,0:T(8,128)(2,1)S(1)}, u32[]{:S(2)}, u32[]{:S(2)}) collective-permute-start(bf16[2,256,128]{2,1,0:T(8,128)(2,1)S(1)} %get-tuple-element.66), channel_id=1, source_target_pairs={{0,4},{1,5},{2,6},{3,7},{4,0},{5,1},{6,2},{7,3},{8,12},{9,13},{10,... | collective-permute-start | bytes 393224 | tf_op jit(solution)/shard_map/ppermute | solution.py:390
  10.7 5.9 %collective-permute-start.4 = (bf16[2,256,128]{2,1,0:T(8,128)(2,1)S(1)}, bf16[2,256,128]{2,1,0:T(8,128)(2,1)S(1)}, u32[]{:S(2)}, u32[]{:S(2)}) collective-permute-start(bf16[2,256,128]{2,1,0:T(8,128)(2,1)S(1)} %get-tuple-element.67.refs_4_), channel_id=1, source_target_pairs={{0,6},{1,7},{2,4},{3,5},{4,2},{5,3},{6,0},{7,1},{8,14},{9,15},{10,... | collective-permute-start | bytes 393224 | tf_op jit(solution)/shard_map/ppermute | solution.py:390
  16.7 6.7 %collective-permute-start.5 = (bf16[256,128]{1,0:T(8,128)(2,1)S(1)}, bf16[256,128]{1,0:T(8,128)(2,1)S(1)}, u32[]{:S(2)}, u32[]{:S(2)}) collective-permute-start(bf16[256,128]{1,0:T(8,128)(2,1)S(1)} %get-tuple-element.80), channel_id=1, source_target_pairs={{0,24},{8,16},{16,8},{24,0},{1,25},{9,17},{17,9},{25,1},{2,26},{10... | collective-permute-start | bytes 196616 | tf_op jit(solution)/shard_map/ppermute | solution.py:390
  20.4 5.2 %collective-permute-start.6 = (bf16[256,128]{1,0:T(8,128)(2,1)S(1)}, bf16[256,128]{1,0:T(8,128)(2,1)S(1)}, u32[]{:S(2)}, u32[]{:S(2)}) collective-permute-start(bf16[256,128]{1,0:T(8,128)(2,1)S(1)} %get-tuple-element.81), channel_id=1, source_target_pairs={{0,16},{8,24},{16,0},{24,8},{1,17},{9,25},{17,1},{25,9},{2,18},{10... | collective-permute-start | bytes 196616 | tf_op jit(solution)/shard_map/ppermute | solution.py:390
  20.4 5.2 %collective-permute-start.7 = (bf16[256,128]{1,0:T(8,128)(2,1)S(1)}, bf16[256,128]{1,0:T(8,128)(2,1)S(1)}, u32[]{:S(2)}, u32[]{:S(2)}) collective-permute-start(bf16[256,128]{1,0:T(8,128)(2,1)S(1)} %get-tuple-element.82), channel_id=1, source_target_pairs={{0,8},{8,0},{16,24},{24,16},{1,9},{9,1},{17,25},{25,17},{2,10},{10... | collective-permute-start | bytes 196616 | tf_op jit(solution)/shard_map/ppermute | solution.py:390
  25.8 5.0 %collective-permute-start.10 = (bf16[2,256,128]{2,1,0:T(8,128)(2,1)S(1)}, bf16[2,256,128]{2,1,0:T(8,128)(2,1)S(1)}, u32[]{:S(2)}, u32[]{:S(2)}) collective-permute-start(bf16[2,256,128]{2,1,0:T(8,128)(2,1)S(1)} %get-tuple-element.86), channel_id=1, source_target_pairs={{0,2},{1,3},{2,0},{3,1},{4,6},{5,7},{6,4},{7,5},{8,10},{9,11},{10,... | collective-permute-start | bytes 393224 | tf_op jit(solution)/shard_map/ppermute | solution.py:390
  26.4 5.8 %collective-permute-start.8 = (bf16[2,256,128]{2,1,0:T(8,128)(2,1)S(1)}, bf16[2,256,128]{2,1,0:T(8,128)(2,1)S(1)}, u32[]{:S(2)}, u32[]{:S(2)}) collective-permute-start(bf16[2,256,128]{2,1,0:T(8,128)(2,1)S(1)} %get-tuple-element.83), channel_id=1, source_target_pairs={{0,4},{1,5},{2,6},{3,7},{4,0},{5,1},{6,2},{7,3},{8,12},{9,13},{10,... | collective-permute-start | bytes 393224 | tf_op jit(solution)/shard_map/ppermute | solution.py:390
  27.0 5.9 %collective-permute-start.9 = (bf16[2,256,128]{2,1,0:T(8,128)(2,1)S(1)}, bf16[2,256,128]{2,1,0:T(8,128)(2,1)S(1)}, u32[]{:S(2)}, u32[]{:S(2)}) collective-permute-start(bf16[2,256,128]{2,1,0:T(8,128)(2,1)S(1)} %get-tuple-element.84), channel_id=1, source_target_pairs={{0,6},{1,7},{2,4},{3,5},{4,2},{5,3},{6,0},{7,1},{8,14},{9,15},{10,... | collective-permute-start | bytes 393224 | tf_op jit(solution)/shard_map/ppermute | solution.py:390
  30.8 2.6 %collective-permute-start.12 = (bf16[2,512,128]{2,1,0:T(8,128)(2,1)S(1)}, bf16[2,512,128]{2,1,0:T(8,128)(2,1)S(1)}, u32[]{:S(2)}, u32[]{:S(2)}) collective-permute-start(bf16[2,512,128]{2,1,0:T(8,128)(2,1)S(1)} %theirs.3), channel_id=1, source_target_pairs={{0,1},{1,0},{2,3},{3,2},{4,5},{5,4},{6,7},{7,6},{8,9},{9,8},{10,11... | collective-permute-start | bytes 786440 | tf_op jit(solution)/shard_map/ppermute | solution.py:390
  32.9 1.6 %collective-permute-start.11 = (bf16[2,512,128]{2,1,0:T(8,128)(2,1)S(1)}, bf16[2,512,128]{2,1,0:T(8,128)(2,1)S(1)}, u32[]{:S(2)}, u32[]{:S(2)}) collective-permute-start(bf16[2,512,128]{2,1,0:T(8,128)(2,1)S(1)} %theirs.2), channel_id=1, source_target_pairs={{0,1},{1,0},{2,3},{3,2},{4,5},{5,4},{6,7},{7,6},{8,9},{9,8},{10,11... | collective-permute-start | bytes 786440 | tf_op jit(solution)/shard_map/ppermute | solution.py:390

commit v25 on v24

--- a/solution.py
+++ b/solution.py
@@ -401,12 +401,12 @@
     tokens, give = load((queries, keys, values, cotangent))
     got = [swap(give, "inner", 1), swap(*sums(tokens, (False, 1)), "inner", 1)]
     keep = sums(tokens, (True, 0), (True, 1))
-    early = local_part(0, tokens, keep[1])
+    early = local_part(1, tokens, keep[1])
     slots = []
     for b in range(2):
         slots += pair_slots(keep[b], got[b], far_count // 2, slots[0] if slots else early[0])
-    slots, late = lax.optimization_barrier((swap_far(slots), local_part(1, tokens, slots[-1])))
-    local = [*early, *late]
+    slots, late = lax.optimization_barrier((swap_far(slots), local_part(0, tokens, slots[-1])))
+    local = [*late, *early]
     sends = group_sends(slots, outer_count)
     others = [swap(send, "outer", s) for s, send in zip(distances(outer_count), sends)]
     slots = swap_far(scan_slots(slots, others))

time: 35.8 us -> 37.8 us (1.056)
  waiting for transfers between devices: 12.6 us -> 14.4 us
    ppermute x13, waiting for transfers between devices: 12.6 us -> 14.4 us  [swap(): lax.ppermute(x, axis, [(i, i ^ bits) for i in range(lax.axis_size(axis))])]
  transfers between devices with their start and end apart: 13 -> 13, of which waited for: 8 -> 8; matrix products, arithmetic and copies ran while one was open for 0% -> 0% of each run, Pallas kernels for 16% -> 15%
where the time goes in v25:
time: 37.8 us; the launch traced here: 37.7 us
  waiting for transfers between devices  14.4 us (38%)
  starting transfers between devices  13.6 us (36%)
  Pallas kernels  8.9 us (24%)
  between operations  0.77 us (2%)
    ppermute x13, waiting for transfers between devices, swap(): lax.ppermute(x, axis, [(i, i ^ bits) for i in range(lax.axis_size(axis))])  14.4 us
    ppermute x13, starting transfers between devices, swap(): lax.ppermute(x, axis, [(i, i ^ bits) for i in range(lax.axis_size(axis))])  13.6 us
    pallas_call x4, Pallas kernels, finish(): pl.pallas_call(functools.partial(finish_kernel, scale, own, block, len(sl...  3.69 us
    pallas_call x2, Pallas kernels, local_part(): pl.pallas_call(functools.partial(local_kernel, core), name='local', in_sp...  2.17 us
    pallas_call x1, Pallas kernels, load(): pl.pallas_call(load_kernel, name='load', in_specs=[ANY] * 4, out_specs=[V...  1.77 us
  transfers between devices with their start and end apart: 13, of which 8 were waited for; matrix products, arithmetic and copies ran while one was open for 0% of the time, Pallas kernels for 15%

profile of v25, /device:TPU:0, one launch (start us, length us, event | category | flops | bytes accessed | tf_op | source)
XLA Modules:
  0.0 37.7 jit_solution(17223201100363004203)
XLA Ops:
  0.6 1.8 %load.1 = (bf16[128,2048]{1,0:T(8,128)(2,1)S(1)}, bf16[128,2048]{1,0:T(8,128)(2,1)S(1)}, bf16[128,2048]{1,0:T(8,128)(2,1)S(1)}, bf16[128,2048]{1,0:T(8,128)(2,1)S(1)}, bf16[2,512,128]{2,1,0:T(8,128)(2,1)S(1)}) custom-call(bf16[128,2048]{1,0:T(8,128)(2,1)} %refs_0_.1, bf16[128,2048]{1,0:T(8,128)(2,1)} %refs_1_.1, bf16[128,2048]{1,0:T(8,128)(2,1)} %refs_2_.1, ...), custom_call_target="tpu_custom_call" | custom-call | flops 33554432 | bytes 2621440 | tf_op jit(solution)/shard_map/load/pallas_call | solution.py:94
  2.4 0.5 %collective-permute-start = (bf16[2,512,128]{2,1,0:T(8,128)(2,1)S(1)}, bf16[2,512,128]{2,1,0:T(8,128)(2,1)S(1)}, u32[]{:S(2)}, u32[]{:S(2)}) collective-permute-start(bf16[2,512,128]{2,1,0:T(8,128)(2,1)S(1)} %get-tuple-element.58), channel_id=1, source_target_pairs={{0,1},{1,0},{2,3},{3,2},{4,5},{5,4},{6,7},{7,6},{8,9},{9,8},{10,11... | collective-permute-start | bytes 786440 | tf_op jit(solution)/shard_map/ppermute | solution.py:390
  2.9 0.3 sums.3
  3.3 0.5 %sums.2 = (bf16[2,512,128]{2,1,0:T(8,128)(2,1)S(1)}, bf16[2,512,128]{2,1,0:T(8,128)(2,1)S(1)}) custom-call(bf16[128,2048]{1,0:T(8,128)(2,1)S(1)} %get-tuple-element.53.refs_0_, bf16[128,2048]{1,0:T(8,128)(2,1)S(1)} %get-tuple-element.54.refs_1_, bf16[128,2048]{1,0:T(8,128)(2,1)S(1)} %get-tuple-element.55.refs_2_, bf16[128,2048]{1,0:T(8,128)(2,1)S(1)} %get-tuple-element.56.refs_3_), custom_call_target="tpu_custom_call" | custom-call | flops 67108864 | bytes 1572864 | tf_op jit(solution)/shard_map/sums/pallas_call | solution.py:116
  3.8 0.3 collective-permute-done.got_ref.refs_14_
  4.2 2.9 %collective-permute-start.1 = (bf16[2,256,128]{2,1,0:T(8,128)(2,1)S(1)}, bf16[2,256,128]{2,1,0:T(8,128)(2,1)S(1)}, u32[]{:S(2)}, u32[]{:S(2)}) collective-permute-start(bf16[2,256,128]{2,1,0:T(8,128)(2,1)S(1)} %get-tuple-element.62), channel_id=1, source_target_pairs={{0,2},{1,3},{2,0},{3,1},{4,6},{5,7},{6,4},{7,5},{8,10},{9,11},{10,... | collective-permute-start | bytes 393224 | tf_op jit(solution)/shard_map/ppermute | solution.py:390
  7.1 1.6 %collective-permute-start.3 = (bf16[2,256,128]{2,1,0:T(8,128)(2,1)S(1)}, bf16[2,256,128]{2,1,0:T(8,128)(2,1)S(1)}, u32[]{:S(2)}, u32[]{:S(2)}) collective-permute-start(bf16[2,256,128]{2,1,0:T(8,128)(2,1)S(1)} %get-tuple-element.63), channel_id=1, source_target_pairs={{0,4},{1,5},{2,6},{3,7},{4,0},{5,1},{6,2},{7,3},{8,12},{9,13},{10,... | collective-permute-start | bytes 393224 | tf_op jit(solution)/shard_map/ppermute | solution.py:390
  8.7 0.3 collective-permute-start.4
  9.0 2.2 %local.3 = (f32[128,2048]{1,0:T(8,128)S(1)}, f32[128,2048]{1,0:T(8,128)S(1)}, f32[128,2048]{1,0:T(8,128)S(1)}, f32[128,2048]{1,0:T(8,128)S(1)}) custom-call(bf16[128,2048]{1,0:T(8,128)(2,1)S(1)} %get-tuple-element.53.refs_0_, bf16[128,2048]{1,0:T(8,128)(2,1)S(1)} %get-tuple-element.54.refs_1_, bf16[128,2048]{1,0:T(8,128)(2,1)S(1)} %get-tuple-element.55.refs_2_, ...), custom_call_target="tpu_custom_call" | custom-call | tf_op jit(solution)/shard_map/local/pallas_call | solution.py:278
  11.2 3.3 %collective-permute-done.3.refs_2_ = bf16[2,256,128]{2,1,0:T(8,128)(2,1)S(1)} collective-permute-done((bf16[2,256,128]{2,1,0:T(8,128)(2,1)S(1)}, bf16[2,256,128]{2,1,0:T(8,128)(2,1)S(1)}, u32[]{:S(2)}, u32[]{:S(2)}) %collective-permute-start.3) | collective-permute-done | bytes 131104 | tf_op jit(solution)/shard_map/ppermute | solution.py:390
  14.5 1.1 %collective-permute-done.4.refs_3_ = bf16[2,256,128]{2,1,0:T(8,128)(2,1)S(1)} collective-permute-done((bf16[2,256,128]{2,1,0:T(8,128)(2,1)S(1)}, bf16[2,256,128]{2,1,0:T(8,128)(2,1)S(1)}, u32[]{:S(2)}, u32[]{:S(2)}) %collective-permute-start.4) | collective-permute-done | bytes 131104 | tf_op jit(solution)/shard_map/ppermute | solution.py:390
  15.8 3.7 %collective-permute-start.5 = (bf16[256,128]{1,0:T(8,128)(2,1)S(1)}, bf16[256,128]{1,0:T(8,128)(2,1)S(1)}, u32[]{:S(2)}, u32[]{:S(2)}) collective-permute-start(bf16[256,128]{1,0:T(8,128)(2,1)S(1)} %get-tuple-element.80), channel_id=1, source_target_pairs={{0,24},{8,16},{16,8},{24,0},{1,25},{9,17},{17,9},{25,1},{2,26},{10... | collective-permute-start | bytes 196616 | tf_op jit(solution)/shard_map/ppermute | solution.py:390
  19.4 0.8 %collective-permute-start.7 = (bf16[256,128]{1,0:T(8,128)(2,1)S(1)}, bf16[256,128]{1,0:T(8,128)(2,1)S(1)}, u32[]{:S(2)}, u32[]{:S(2)}) collective-permute-start(bf16[256,128]{1,0:T(8,128)(2,1)S(1)} %get-tuple-element.82), channel_id=1, source_target_pairs={{0,8},{8,0},{16,24},{24,16},{1,9},{9,1},{17,25},{25,17},{2,10},{10... | collective-permute-start | bytes 196616 | tf_op jit(solution)/shard_map/ppermute | solution.py:390
  20.2 2.2 %collective-permute-done.5.refs_4_ = bf16[256,128]{1,0:T(8,128)(2,1)S(1)} collective-permute-done((bf16[256,128]{1,0:T(8,128)(2,1)S(1)}, bf16[256,128]{1,0:T(8,128)(2,1)S(1)}, u32[]{:S(2)}, u32[]{:S(2)}) %collective-permute-start.5) | collective-permute-done | bytes 65568 | tf_op jit(solution)/shard_map/ppermute | solution.py:390
  22.4 3.2 %collective-permute-done.6.refs_5_ = bf16[256,128]{1,0:T(8,128)(2,1)S(1)} collective-permute-done((bf16[256,128]{1,0:T(8,128)(2,1)S(1)}, bf16[256,128]{1,0:T(8,128)(2,1)S(1)}, u32[]{:S(2)}, u32[]{:S(2)}) %collective-permute-start.6) | collective-permute-done | bytes 65568 | tf_op jit(solution)/shard_map/ppermute | solution.py:390
  25.8 0.9 %collective-permute-start.10 = (bf16[2,256,128]{2,1,0:T(8,128)(2,1)S(1)}, bf16[2,256,128]{2,1,0:T(8,128)(2,1)S(1)}, u32[]{:S(2)}, u32[]{:S(2)}) collective-permute-start(bf16[2,256,128]{2,1,0:T(8,128)(2,1)S(1)} %get-tuple-element.86), channel_id=1, source_target_pairs={{0,2},{1,3},{2,0},{3,1},{4,6},{5,7},{6,4},{7,5},{8,10},{9,11},{10,... | collective-permute-start | bytes 393224 | tf_op jit(solution)/shard_map/ppermute | solution.py:390
  26.7 0.9 %collective-permute-start.8 = (bf16[2,256,128]{2,1,0:T(8,128)(2,1)S(1)}, bf16[2,256,128]{2,1,0:T(8,128)(2,1)S(1)}, u32[]{:S(2)}, u32[]{:S(2)}) collective-permute-start(bf16[2,256,128]{2,1,0:T(8,128)(2,1)S(1)} %get-tuple-element.83), channel_id=1, source_target_pairs={{0,4},{1,5},{2,6},{3,7},{4,0},{5,1},{6,2},{7,3},{8,12},{9,13},{10,... | collective-permute-start | bytes 393224 | tf_op jit(solution)/shard_map/ppermute | solution.py:390
  27.6 1.7 %collective-permute-start.9 = (bf16[2,256,128]{2,1,0:T(8,128)(2,1)S(1)}, bf16[2,256,128]{2,1,0:T(8,128)(2,1)S(1)}, u32[]{:S(2)}, u32[]{:S(2)}) collective-permute-start(bf16[2,256,128]{2,1,0:T(8,128)(2,1)S(1)} %get-tuple-element.84), channel_id=1, source_target_pairs={{0,6},{1,7},{2,4},{3,5},{4,2},{5,3},{6,0},{7,1},{8,14},{9,15},{10,... | collective-permute-start | bytes 393224 | tf_op jit(solution)/shard_map/ppermute | solution.py:390
  29.4 2.9 %collective-permute-done.10.refs_13_.refs_1_ = bf16[2,256,128]{2,1,0:T(8,128)(2,1)S(1)} collective-permute-done((bf16[2,256,128]{2,1,0:T(8,128)(2,1)S(1)}, bf16[2,256,128]{2,1,0:T(8,128)(2,1)S(1)}, u32[]{:S(2)}, u32[]{:S(2)}) %collective-permute-start.10) | collective-permute-done | bytes 131104 | tf_op jit(solution)/shard_map/ppermute | solution.py:390
  32.4 1.2 %finish.4 = (bf16[128,2048]{1,0:T(8,128)(2,1)}, bf16[128,2048]{1,0:T(8,128)(2,1)}, bf16[128,2048]{1,0:T(8,128)(2,1)}, bf16[128,2048]{1,0:T(8,128)(2,1)}) custom-call(bf16[128,2048]{1,0:T(8,128)(2,1)S(1)} %get-tuple-element.53.refs_0_, bf16[128,2048]{1,0:T(8,128)(2,1)S(1)} %get-tuple-element.54.refs_1_, bf16[128,2048]{1,0:T(8,128)(2,1)S(1)} %get-tuple-element.55.refs_2_, ...), custom_call_target="tpu_custom_call" | custom-call | flops 67108864 | bytes 2097152 | tf_op jit(solution)/shard_map/finish/pallas_call | solution.py:372
  33.6 1.3 %collective-permute-done.9.refs_1_.refs_13_ = bf16[2,256,128]{2,1,0:T(8,128)(2,1)S(1)} collective-permute-done((bf16[2,256,128]{2,1,0:T(8,128)(2,1)S(1)}, bf16[2,256,128]{2,1,0:T(8,128)(2,1)S(1)}, u32[]{:S(2)}, u32[]{:S(2)}) %collective-permute-start.9) | collective-permute-done | bytes 131104 | tf_op jit(solution)/shard_map/ppermute | solution.py:390
  35.0 0.4 %finish.5.refs_13_ = bf16[4,128,512]{2,1,0:T(8,128)(2,1)S(1)} custom-call(bf16[128,2048]{1,0:T(8,128)(2,1)S(1)} %get-tuple-element.53.refs_0_, bf16[128,2048]{1,0:T(8,128)(2,1)S(1)} %get-tuple-element.54.refs_1_, bf16[128,2048]{1,0:T(8,128)(2,1)S(1)} %get-tuple-element.55.refs_2_, bf16[128,2048]{1,0:T(8,128)(2,1)S(1)} %get-tuple-element.56.refs_3_, ...), custom_call_target="tpu_custom_call" | custom-call | flops 67108864 | bytes 2097152 | tf_op jit(solution)/shard_map/finish/pallas_call | solution.py:372
  35.4 0.9 %finish.6 = (bf16[128,2048]{1,0:T(8,128)(2,1)}, bf16[128,2048]{1,0:T(8,128)(2,1)}, bf16[128,2048]{1,0:T(8,128)(2,1)}, bf16[128,2048]{1,0:T(8,128)(2,1)}, bf16[4,128,512]{2,1,0:T(8,128)(2,1)S(1)}) custom-call(bf16[128,2048]{1,0:T(8,128)(2,1)S(1)} %get-tuple-element.53.refs_0_, ...), custom_call_target="tpu_custom_call", output_to_operand_aliasing={{0}: (14, {}), {1}: (15, {}), {2}: (16, {}), {3}: (17, {})} | custom-call | flops 67108864 | bytes 2097152 | tf_op jit(solution)/shard_map/finish/pallas_call | solution.py:372
  36.5 1.2 %finish.7 = (bf16[128,2048]{1,0:T(8,128)(2,1)}, bf16[128,2048]{1,0:T(8,128)(2,1)}, bf16[128,2048]{1,0:T(8,128)(2,1)}, bf16[128,2048]{1,0:T(8,128)(2,1)}) custom-call(bf16[128,2048]{1,0:T(8,128)(2,1)S(1)} %get-tuple-element.53.refs_0_, ...), custom_call_target="tpu_custom_call", output_to_operand_aliasing={{0}: (14, {}), {1}: (15, {}), {2}: (16, {}), {3}: (17, {})} | custom-call | flops 67108864 | bytes 2097152 | tf_op jit(solution)/shard_map/finish/pallas_call | solution.py:372
  (17 shorter events, 1.0 us)
Async XLA Ops:
  2.4 1.7 %collective-permute-start = (bf16[2,512,128]{2,1,0:T(8,128)(2,1)S(1)}, bf16[2,512,128]{2,1,0:T(8,128)(2,1)S(1)}, u32[]{:S(2)}, u32[]{:S(2)}) collective-permute-start(bf16[2,512,128]{2,1,0:T(8,128)(2,1)S(1)} %get-tuple-element.58), channel_id=1, source_target_pairs={{0,1},{1,0},{2,3},{3,2},{4,5},{5,4},{6,7},{7,6},{8,9},{9,8},{10,11... | collective-permute-start | bytes 786440 | tf_op jit(solution)/shard_map/ppermute | solution.py:390
  3.2 3.9 %collective-permute-start.2 = (bf16[2,512,128]{2,1,0:T(8,128)(2,1)S(1)}, bf16[2,512,128]{2,1,0:T(8,128)(2,1)S(1)}, u32[]{:S(2)}, u32[]{:S(2)}) collective-permute-start(bf16[2,512,128]{2,1,0:T(8,128)(2,1)S(1)} %sums.3), channel_id=1, source_target_pairs={{0,1},{1,0},{2,3},{3,2},{4,5},{5,4},{6,7},{7,6},{8,9},{9,8},{10,11... | collective-permute-start | bytes 786440 | tf_op jit(solution)/shard_map/ppermute | solution.py:390
  4.2 7.0 %collective-permute-start.1 = (bf16[2,256,128]{2,1,0:T(8,128)(2,1)S(1)}, bf16[2,256,128]{2,1,0:T(8,128)(2,1)S(1)}, u32[]{:S(2)}, u32[]{:S(2)}) collective-permute-start(bf16[2,256,128]{2,1,0:T(8,128)(2,1)S(1)} %get-tuple-element.62), channel_id=1, source_target_pairs={{0,2},{1,3},{2,0},{3,1},{4,6},{5,7},{6,4},{7,5},{8,10},{9,11},{10,... | collective-permute-start | bytes 393224 | tf_op jit(solution)/shard_map/ppermute | solution.py:390
  7.1 7.4 %collective-permute-start.3 = (bf16[2,256,128]{2,1,0:T(8,128)(2,1)S(1)}, bf16[2,256,128]{2,1,0:T(8,128)(2,1)S(1)}, u32[]{:S(2)}, u32[]{:S(2)}) collective-permute-start(bf16[2,256,128]{2,1,0:T(8,128)(2,1)S(1)} %get-tuple-element.63), channel_id=1, source_target_pairs={{0,4},{1,5},{2,6},{3,7},{4,0},{5,1},{6,2},{7,3},{8,12},{9,13},{10,... | collective-permute-start | bytes 393224 | tf_op jit(solution)/shard_map/ppermute | solution.py:390
  8.7 6.9 %collective-permute-start.4 = (bf16[2,256,128]{2,1,0:T(8,128)(2,1)S(1)}, bf16[2,256,128]{2,1,0:T(8,128)(2,1)S(1)}, u32[]{:S(2)}, u32[]{:S(2)}) collective-permute-start(bf16[2,256,128]{2,1,0:T(8,128)(2,1)S(1)} %get-tuple-element.64.refs_4_), channel_id=1, source_target_pairs={{0,6},{1,7},{2,4},{3,5},{4,2},{5,3},{6,0},{7,1},{8,14},{9,15},{10,... | collective-permute-start | bytes 393224 | tf_op jit(solution)/shard_map/ppermute | solution.py:390
  15.8 6.7 %collective-permute-start.5 = (bf16[256,128]{1,0:T(8,128)(2,1)S(1)}, bf16[256,128]{1,0:T(8,128)(2,1)S(1)}, u32[]{:S(2)}, u32[]{:S(2)}) collective-permute-start(bf16[256,128]{1,0:T(8,128)(2,1)S(1)} %get-tuple-element.80), channel_id=1, source_target_pairs={{0,24},{8,16},{16,8},{24,0},{1,25},{9,17},{17,9},{25,1},{2,26},{10... | collective-permute-start | bytes 196616 | tf_op jit(solution)/shard_map/ppermute | solution.py:390
  19.4 6.2 %collective-permute-start.6 = (bf16[256,128]{1,0:T(8,128)(2,1)S(1)}, bf16[256,128]{1,0:T(8,128)(2,1)S(1)}, u32[]{:S(2)}, u32[]{:S(2)}) collective-permute-start(bf16[256,128]{1,0:T(8,128)(2,1)S(1)} %get-tuple-element.81), channel_id=1, source_target_pairs={{0,16},{8,24},{16,0},{24,8},{1,17},{9,25},{17,1},{25,9},{2,18},{10... | collective-permute-start | bytes 196616 | tf_op jit(solution)/shard_map/ppermute | solution.py:390
  19.4 6.2 %collective-permute-start.7 = (bf16[256,128]{1,0:T(8,128)(2,1)S(1)}, bf16[256,128]{1,0:T(8,128)(2,1)S(1)}, u32[]{:S(2)}, u32[]{:S(2)}) collective-permute-start(bf16[256,128]{1,0:T(8,128)(2,1)S(1)} %get-tuple-element.82), channel_id=1, source_target_pairs={{0,8},{8,0},{16,24},{24,16},{1,9},{9,1},{17,25},{25,17},{2,10},{10... | collective-permute-start | bytes 196616 | tf_op jit(solution)/shard_map/ppermute | solution.py:390
  25.8 6.4 %collective-permute-start.10 = (bf16[2,256,128]{2,1,0:T(8,128)(2,1)S(1)}, bf16[2,256,128]{2,1,0:T(8,128)(2,1)S(1)}, u32[]{:S(2)}, u32[]{:S(2)}) collective-permute-start(bf16[2,256,128]{2,1,0:T(8,128)(2,1)S(1)} %get-tuple-element.86), channel_id=1, source_target_pairs={{0,2},{1,3},{2,0},{3,1},{4,6},{5,7},{6,4},{7,5},{8,10},{9,11},{10,... | collective-permute-start | bytes 393224 | tf_op jit(solution)/shard_map/ppermute | solution.py:390
  26.7 6.9 %collective-permute-start.8 = (bf16[2,256,128]{2,1,0:T(8,128)(2,1)S(1)}, bf16[2,256,128]{2,1,0:T(8,128)(2,1)S(1)}, u32[]{:S(2)}, u32[]{:S(2)}) collective-permute-start(bf16[2,256,128]{2,1,0:T(8,128)(2,1)S(1)} %get-tuple-element.83), channel_id=1, source_target_pairs={{0,4},{1,5},{2,6},{3,7},{4,0},{5,1},{6,2},{7,3},{8,12},{9,13},{10,... | collective-permute-start | bytes 393224 | tf_op jit(solution)/shard_map/ppermute | solution.py:390
  27.6 7.2 %collective-permute-start.9 = (bf16[2,256,128]{2,1,0:T(8,128)(2,1)S(1)}, bf16[2,256,128]{2,1,0:T(8,128)(2,1)S(1)}, u32[]{:S(2)}, u32[]{:S(2)}) collective-permute-start(bf16[2,256,128]{2,1,0:T(8,128)(2,1)S(1)} %get-tuple-element.84), channel_id=1, source_target_pairs={{0,6},{1,7},{2,4},{3,5},{4,2},{5,3},{6,0},{7,1},{8,14},{9,15},{10,... | collective-permute-start | bytes 393224 | tf_op jit(solution)/shard_map/ppermute | solution.py:390
  32.3 3.2 %collective-permute-start.12 = (bf16[2,512,128]{2,1,0:T(8,128)(2,1)S(1)}, bf16[2,512,128]{2,1,0:T(8,128)(2,1)S(1)}, u32[]{:S(2)}, u32[]{:S(2)}) collective-permute-start(bf16[2,512,128]{2,1,0:T(8,128)(2,1)S(1)} %theirs.3), channel_id=1, source_target_pairs={{0,1},{1,0},{2,3},{3,2},{4,5},{5,4},{6,7},{7,6},{8,9},{9,8},{10,11... | collective-permute-start | bytes 786440 | tf_op jit(solution)/shard_map/ppermute | solution.py:390
  34.9 1.6 %collective-permute-start.11 = (bf16[2,512,128]{2,1,0:T(8,128)(2,1)S(1)}, bf16[2,512,128]{2,1,0:T(8,128)(2,1)S(1)}, u32[]{:S(2)}, u32[]{:S(2)}) collective-permute-start(bf16[2,512,128]{2,1,0:T(8,128)(2,1)S(1)} %theirs.2), channel_id=1, source_target_pairs={{0,1},{1,0},{2,3},{3,2},{4,5},{5,4},{6,7},{7,6},{8,9},{9,8},{10,11... | collective-permute-start | bytes 786440 | tf_op jit(solution)/shard_map/ppermute | solution.py:390

commit v26 on v20

--- a/solution.py
+++ b/solution.py
@@ -36,6 +36,14 @@
     side = near if own else 1 - near
     top = lax.div(far, lax.axis_size("inner") // 4)
     return side * half + (1 - top if block else top) * (half // 2)
+
+
+def slot_order(count):
+    return [n ^ (n >> 1) for n in range(count)]
+
+
+def block_slots(block, count):
+    return slot_order(2 * count)[block * count : (block + 1) * count]
 
 
 def columns(start, n):
@@ -128,18 +136,18 @@
     )(*tokens)
 
 
-def pair_kernel(keep_ref, got_ref, *slots):
-    for s, slot in enumerate(slots):
+def pair_kernel(block, keep_ref, got_ref, *slots):
+    for s, slot in zip(block_slots(block, len(slots)), slots):
         part = slot_rows(s, len(slots), slot.shape[1])
         for which in range(2):
             both = keep_ref[which, part].astype(F32) + got_ref[which, part].astype(F32)
             slot[which] = both.astype(BF16)
 
 
-def pair_slots(keep, got, count):
+def pair_slots(block, keep, got, count):
     slot = jax.ShapeDtypeStruct((2, keep.shape[1] // count, HEAD), BF16)
     return pl.pallas_call(
-        pair_kernel,
+        functools.partial(pair_kernel, block),
         name="pair",
         in_specs=[VMEM] * 2,
         out_specs=[VMEM] * count,
@@ -179,7 +187,7 @@
     outs, (held, scanned) = refs[:far_count], refs[far_count:]
     outer = lax.axis_index("outer")
     _, far = near_far()
-    for s, slot in enumerate(slots):
+    for s, slot in zip(slot_order(far_count), slots):
         held[far ^ s] = slot[...]
     for which in range(2):
         total = jnp.zeros(held.shape[2:], F32)
@@ -190,7 +198,7 @@
         for i in reversed(range(far_count)) if which else range(far_count):
             scanned[i, which] = total.astype(BF16)
             total += held[i, which].astype(F32)
-    for s, out in enumerate(outs):
+    for s, out in zip(slot_order(far_count), outs):
         out[...] = scanned[far ^ s]
 
 
@@ -217,11 +225,11 @@
         pl.when(near == core)(functools.partial(run, core))
 
 
-def theirs_kernel(*refs):
+def theirs_kernel(block, *refs):
     slots, (keep, out) = refs[:-2], refs[-2:]
 
     def run(core):
-        for s, slot in enumerate(slots):
+        for s, slot in zip(block_slots(block, len(slots)), slots):
             part = slot_rows(s, len(slots), slot.shape[1])
             out[core, part] = with_sums(slot, core, keep, part)
             out[1 - core, part] = slot[1 - core]
@@ -229,9 +237,9 @@
     by_core(run)
 
 
-def states_for_neighbour(slots, keep):
-    return pl.pallas_call(
-        theirs_kernel,
+def states_for_neighbour(block, slots, keep):
+    return pl.pallas_call(
+        functools.partial(theirs_kernel, block),
         name="theirs",
         in_specs=[VMEM] * (len(slots) + 1),
         out_specs=VMEM,
@@ -341,7 +349,7 @@
                     copy.start()
 
     def run(quarter):
-        for s, slot in enumerate(slots if own else ()):
+        for s, slot in zip(block_slots(block, count), slots if own else ()):
             core, part = quarter // 2, slot_rows(s, count, slot.shape[1])
             states[core, part] = slot[core]
             states[1 - core, part] = with_sums(slot, 1 - core, got, part)
@@ -387,7 +395,8 @@
 
 
 def swap_far(slots):
-    return [slots[0]] + [swap(slots[s], "inner", 2 * s) for s in range(1, len(slots))]
+    order = slot_order(len(slots))
+    return [slots[0]] + [swap(slots[n], "inner", 2 * order[n]) for n in range(1, len(slots))]
 
 
 def body(queries, keys, values, cotangent):
@@ -397,7 +406,7 @@
     tokens, give = load((queries, keys, values, cotangent))
     got = [swap(give, "inner", 1), swap(*sums(tokens, (False, 1)), "inner", 1)]
     keep = sums(tokens, (True, 0), (True, 1))
-    slots = [slot for b in range(2) for slot in pair_slots(keep[b], got[b], far_count // 2)]
+    slots = [slot for b in range(2) for slot in pair_slots(b, keep[b], got[b], far_count // 2)]
     slots, local = lax.optimization_barrier((swap_far(slots), local_part(tokens)))
     sends = group_sends(slots, outer_count)
     others = [swap(send, "outer", s) for s, send in zip(distances(outer_count), sends)]
@@ -405,7 +414,7 @@
     half = far_count // 2
 
     def near_swap(block, part):
-        return swap(states_for_neighbour(part, keep[block]), "inner", 1)
+        return swap(states_for_neighbour(block, part, keep[block]), "inner", 1)
 
     arrived = [near_swap(0, slots[:half])]
     outs = finish(True, 0, tokens, local, slots[:half], scale, got=got[:1])

time: 35.7 us -> 37.9 us (1.062)
  waiting for transfers between devices: 12.3 us -> 14.5 us
    ppermute x13, waiting for transfers between devices: 12.3 us -> 14.5 us  [swap(): lax.ppermute(x, axis, [(i, i ^ bits) for i in range(lax.axis_size(axis))])]
  transfers between devices with their start and end apart: 13 -> 13, of which waited for: 7 -> 9; matrix products, arithmetic and copies ran while one was open for 0% -> 0% of each run, Pallas kernels for 16% -> 15%
where the time goes in v26:
time: 37.9 us; the launch traced here: 37.7 us
  waiting for transfers between devices  14.5 us (38%)
  starting transfers between devices  13.6 us (36%)
  Pallas kernels  8.88 us (23%)
  between operations  0.76 us (2%)
    ppermute x13, waiting for transfers between devices, swap(): lax.ppermute(x, axis, [(i, i ^ bits) for i in range(lax.axis_size(axis))])  14.5 us
    ppermute x13, starting transfers between devices, swap(): lax.ppermute(x, axis, [(i, i ^ bits) for i in range(lax.axis_size(axis))])  13.6 us
    pallas_call x4, Pallas kernels, finish(): pl.pallas_call(functools.partial(finish_kernel, scale, own, block, len(sl...  3.69 us
    pallas_call x1, Pallas kernels, local_part(): pl.pallas_call(local_kernel, name='local', in_specs=[VMEM] * 4, out_specs...  2.16 us
    pallas_call x1, Pallas kernels, load(): pl.pallas_call(load_kernel, name='load', in_specs=[ANY] * 4, out_specs=[V...  1.77 us
  transfers between devices with their start and end apart: 13, of which 9 were waited for; matrix products, arithmetic and copies ran while one was open for 0% of the time, Pallas kernels for 15%

profile of v26, /device:TPU:0, one launch (start us, length us, event | category | flops | bytes accessed | tf_op | source)
XLA Modules:
  0.0 37.7 jit_solution(10461286056204355177)
XLA Ops:
  0.6 1.8 %load.1 = (bf16[128,2048]{1,0:T(8,128)(2,1)S(1)}, bf16[128,2048]{1,0:T(8,128)(2,1)S(1)}, bf16[128,2048]{1,0:T(8,128)(2,1)S(1)}, bf16[128,2048]{1,0:T(8,128)(2,1)S(1)}, bf16[2,512,128]{2,1,0:T(8,128)(2,1)S(1)}) custom-call(bf16[128,2048]{1,0:T(8,128)(2,1)} %refs_0_.1, bf16[128,2048]{1,0:T(8,128)(2,1)} %refs_1_.1, bf16[128,2048]{1,0:T(8,128)(2,1)} %refs_2_.1, ...), custom_call_target="tpu_custom_call" | custom-call | flops 33554432 | bytes 2621440 | tf_op jit(solution)/shard_map/load/pallas_call | solution.py:102
  2.4 0.5 %collective-permute-start = (bf16[2,512,128]{2,1,0:T(8,128)(2,1)S(1)}, bf16[2,512,128]{2,1,0:T(8,128)(2,1)S(1)}, u32[]{:S(2)}, u32[]{:S(2)}) collective-permute-start(bf16[2,512,128]{2,1,0:T(8,128)(2,1)S(1)} %get-tuple-element.54), channel_id=1, source_target_pairs={{0,1},{1,0},{2,3},{3,2},{4,5},{5,4},{6,7},{7,6},{8,9},{9,8},{10,11... | collective-permute-start | bytes 786440 | tf_op jit(solution)/shard_map/ppermute | solution.py:394
  2.9 0.3 sums.3
  3.3 0.5 %sums.2 = (bf16[2,512,128]{2,1,0:T(8,128)(2,1)S(1)}, bf16[2,512,128]{2,1,0:T(8,128)(2,1)S(1)}) custom-call(bf16[128,2048]{1,0:T(8,128)(2,1)S(1)} %get-tuple-element.49.refs_0_, bf16[128,2048]{1,0:T(8,128)(2,1)S(1)} %get-tuple-element.50.refs_1_, bf16[128,2048]{1,0:T(8,128)(2,1)S(1)} %get-tuple-element.51.refs_2_, bf16[128,2048]{1,0:T(8,128)(2,1)S(1)} %get-tuple-element.52.refs_3_), custom_call_target="tpu_custom_call" | custom-call | flops 67108864 | bytes 1572864 | tf_op jit(solution)/shard_map/sums/pallas_call | solution.py:124
  3.8 0.3 collective-permute-done.got_ref.refs_10_
  4.2 2.9 %collective-permute-start.1 = (bf16[2,256,128]{2,1,0:T(8,128)(2,1)S(1)}, bf16[2,256,128]{2,1,0:T(8,128)(2,1)S(1)}, u32[]{:S(2)}, u32[]{:S(2)}) collective-permute-start(bf16[2,256,128]{2,1,0:T(8,128)(2,1)S(1)} %get-tuple-element.56), channel_id=1, source_target_pairs={{0,2},{1,3},{2,0},{3,1},{4,6},{5,7},{6,4},{7,5},{8,10},{9,11},{10,... | collective-permute-start | bytes 393224 | tf_op jit(solution)/shard_map/ppermute | solution.py:394
  7.1 1.6 %collective-permute-start.3 = (bf16[2,256,128]{2,1,0:T(8,128)(2,1)S(1)}, bf16[2,256,128]{2,1,0:T(8,128)(2,1)S(1)}, u32[]{:S(2)}, u32[]{:S(2)}) collective-permute-start(bf16[2,256,128]{2,1,0:T(8,128)(2,1)S(1)} %get-tuple-element.58), channel_id=1, source_target_pairs={{0,6},{1,7},{2,4},{3,5},{4,2},{5,3},{6,0},{7,1},{8,14},{9,15},{10,... | collective-permute-start | bytes 393224 | tf_op jit(solution)/shard_map/ppermute | solution.py:394
  8.7 0.3 collective-permute-start.4
  9.0 2.2 %local.1 = (f32[128,2048]{1,0:T(8,128)S(1)}, f32[128,2048]{1,0:T(8,128)S(1)}, f32[128,2048]{1,0:T(8,128)S(1)}, f32[128,2048]{1,0:T(8,128)S(1)}) custom-call(bf16[128,2048]{1,0:T(8,128)(2,1)S(1)} %get-tuple-element.49.refs_0_, bf16[128,2048]{1,0:T(8,128)(2,1)S(1)} %get-tuple-element.50.refs_1_, bf16[128,2048]{1,0:T(8,128)(2,1)S(1)} %get-tuple-element.51.refs_2_, ...), custom_call_target="tpu_custom_call" | custom-call | flops 402653184 | bytes 6291456 | tf_op jit(solution)/shard_map/local/pallas_call | solution.py:282
  11.2 3.8 %collective-permute-done.3.refs_2_ = bf16[2,256,128]{2,1,0:T(8,128)(2,1)S(1)} collective-permute-done((bf16[2,256,128]{2,1,0:T(8,128)(2,1)S(1)}, bf16[2,256,128]{2,1,0:T(8,128)(2,1)S(1)}, u32[]{:S(2)}, u32[]{:S(2)}) %collective-permute-start.3) | collective-permute-done | bytes 131104 | tf_op jit(solution)/shard_map/ppermute | solution.py:394
  15.0 1.8 %collective-permute-done.4.refs_3_ = bf16[2,256,128]{2,1,0:T(8,128)(2,1)S(1)} collective-permute-done((bf16[2,256,128]{2,1,0:T(8,128)(2,1)S(1)}, bf16[2,256,128]{2,1,0:T(8,128)(2,1)S(1)}, u32[]{:S(2)}, u32[]{:S(2)}) %collective-permute-start.4) | collective-permute-done | bytes 131104 | tf_op jit(solution)/shard_map/ppermute | solution.py:394
  16.9 3.7 %collective-permute-start.5 = (bf16[256,128]{1,0:T(8,128)(2,1)S(1)}, bf16[256,128]{1,0:T(8,128)(2,1)S(1)}, u32[]{:S(2)}, u32[]{:S(2)}) collective-permute-start(bf16[256,128]{1,0:T(8,128)(2,1)S(1)} %get-tuple-element.72), channel_id=1, source_target_pairs={{0,24},{8,16},{16,8},{24,0},{1,25},{9,17},{17,9},{25,1},{2,26},{10... | collective-permute-start | bytes 196616 | tf_op jit(solution)/shard_map/ppermute | solution.py:394
  20.6 0.8 %collective-permute-start.7 = (bf16[256,128]{1,0:T(8,128)(2,1)S(1)}, bf16[256,128]{1,0:T(8,128)(2,1)S(1)}, u32[]{:S(2)}, u32[]{:S(2)}) collective-permute-start(bf16[256,128]{1,0:T(8,128)(2,1)S(1)} %get-tuple-element.74), channel_id=1, source_target_pairs={{0,8},{8,0},{16,24},{24,16},{1,9},{9,1},{17,25},{25,17},{2,10},{10... | collective-permute-start | bytes 196616 | tf_op jit(solution)/shard_map/ppermute | solution.py:394
  21.4 2.5 %collective-permute-done.5.refs_4_ = bf16[256,128]{1,0:T(8,128)(2,1)S(1)} collective-permute-done((bf16[256,128]{1,0:T(8,128)(2,1)S(1)}, bf16[256,128]{1,0:T(8,128)(2,1)S(1)}, u32[]{:S(2)}, u32[]{:S(2)}) %collective-permute-start.5) | collective-permute-done | bytes 65568 | tf_op jit(solution)/shard_map/ppermute | solution.py:394
  23.8 2.1 %collective-permute-done.6.refs_5_ = bf16[256,128]{1,0:T(8,128)(2,1)S(1)} collective-permute-done((bf16[256,128]{1,0:T(8,128)(2,1)S(1)}, bf16[256,128]{1,0:T(8,128)(2,1)S(1)}, u32[]{:S(2)}, u32[]{:S(2)}) %collective-permute-start.6) | collective-permute-done | bytes 65568 | tf_op jit(solution)/shard_map/ppermute | solution.py:394
  26.2 1.1 %collective-permute-start.10 = (bf16[2,256,128]{2,1,0:T(8,128)(2,1)S(1)}, bf16[2,256,128]{2,1,0:T(8,128)(2,1)S(1)}, u32[]{:S(2)}, u32[]{:S(2)}) collective-permute-start(bf16[2,256,128]{2,1,0:T(8,128)(2,1)S(1)} %get-tuple-element.78), channel_id=1, source_target_pairs={{0,2},{1,3},{2,0},{3,1},{4,6},{5,7},{6,4},{7,5},{8,10},{9,11},{10,... | collective-permute-start | bytes 393224 | tf_op jit(solution)/shard_map/ppermute | solution.py:394
  27.3 0.8 %collective-permute-start.8 = (bf16[2,256,128]{2,1,0:T(8,128)(2,1)S(1)}, bf16[2,256,128]{2,1,0:T(8,128)(2,1)S(1)}, u32[]{:S(2)}, u32[]{:S(2)}) collective-permute-start(bf16[2,256,128]{2,1,0:T(8,128)(2,1)S(1)} %get-tuple-element.75), channel_id=1, source_target_pairs={{0,6},{1,7},{2,4},{3,5},{4,2},{5,3},{6,0},{7,1},{8,14},{9,15},{10,... | collective-permute-start | bytes 393224 | tf_op jit(solution)/shard_map/ppermute | solution.py:394
  28.1 1.6 %collective-permute-start.9 = (bf16[2,256,128]{2,1,0:T(8,128)(2,1)S(1)}, bf16[2,256,128]{2,1,0:T(8,128)(2,1)S(1)}, u32[]{:S(2)}, u32[]{:S(2)}) collective-permute-start(bf16[2,256,128]{2,1,0:T(8,128)(2,1)S(1)} %get-tuple-element.76), channel_id=1, source_target_pairs={{0,4},{1,5},{2,6},{3,7},{4,0},{5,1},{6,2},{7,3},{8,12},{9,13},{10,... | collective-permute-start | bytes 393224 | tf_op jit(solution)/shard_map/ppermute | solution.py:394
  29.8 2.7 %collective-permute-done.10.refs_9_.refs_1_ = bf16[2,256,128]{2,1,0:T(8,128)(2,1)S(1)} collective-permute-done((bf16[2,256,128]{2,1,0:T(8,128)(2,1)S(1)}, bf16[2,256,128]{2,1,0:T(8,128)(2,1)S(1)}, u32[]{:S(2)}, u32[]{:S(2)}) %collective-permute-start.10) | collective-permute-done | bytes 131104 | tf_op jit(solution)/shard_map/ppermute | solution.py:394
  32.6 1.2 %finish.4 = (bf16[128,2048]{1,0:T(8,128)(2,1)}, bf16[128,2048]{1,0:T(8,128)(2,1)}, bf16[128,2048]{1,0:T(8,128)(2,1)}, bf16[128,2048]{1,0:T(8,128)(2,1)}) custom-call(bf16[128,2048]{1,0:T(8,128)(2,1)S(1)} %get-tuple-element.49.refs_0_, bf16[128,2048]{1,0:T(8,128)(2,1)S(1)} %get-tuple-element.50.refs_1_, bf16[128,2048]{1,0:T(8,128)(2,1)S(1)} %get-tuple-element.51.refs_2_, ...), custom_call_target="tpu_custom_call" | custom-call | flops 67108864 | bytes 2097152 | tf_op jit(solution)/shard_map/finish/pallas_call | solution.py:376
  33.8 1.1 %collective-permute-done.9.refs_1_.refs_9_ = bf16[2,256,128]{2,1,0:T(8,128)(2,1)S(1)} collective-permute-done((bf16[2,256,128]{2,1,0:T(8,128)(2,1)S(1)}, bf16[2,256,128]{2,1,0:T(8,128)(2,1)S(1)}, u32[]{:S(2)}, u32[]{:S(2)}) %collective-permute-start.9) | collective-permute-done | bytes 131104 | tf_op jit(solution)/shard_map/ppermute | solution.py:394
  35.0 0.4 %finish.5.refs_9_ = bf16[4,128,512]{2,1,0:T(8,128)(2,1)S(1)} custom-call(bf16[128,2048]{1,0:T(8,128)(2,1)S(1)} %get-tuple-element.49.refs_0_, bf16[128,2048]{1,0:T(8,128)(2,1)S(1)} %get-tuple-element.50.refs_1_, bf16[128,2048]{1,0:T(8,128)(2,1)S(1)} %get-tuple-element.51.refs_2_, bf16[128,2048]{1,0:T(8,128)(2,1)S(1)} %get-tuple-element.52.refs_3_, ...), custom_call_target="tpu_custom_call" | custom-call | flops 67108864 | bytes 2097152 | tf_op jit(solution)/shard_map/finish/pallas_call | solution.py:376
  35.5 0.9 %finish.6 = (bf16[128,2048]{1,0:T(8,128)(2,1)}, bf16[128,2048]{1,0:T(8,128)(2,1)}, bf16[128,2048]{1,0:T(8,128)(2,1)}, bf16[128,2048]{1,0:T(8,128)(2,1)}, bf16[4,128,512]{2,1,0:T(8,128)(2,1)S(1)}) custom-call(bf16[128,2048]{1,0:T(8,128)(2,1)S(1)} %get-tuple-element.49.refs_0_, ...), custom_call_target="tpu_custom_call", output_to_operand_aliasing={{0}: (10, {}), {1}: (11, {}), {2}: (12, {}), {3}: (13, {})} | custom-call | flops 67108864 | bytes 2097152 | tf_op jit(solution)/shard_map/finish/pallas_call | solution.py:376
  36.5 1.2 %finish.7 = (bf16[128,2048]{1,0:T(8,128)(2,1)}, bf16[128,2048]{1,0:T(8,128)(2,1)}, bf16[128,2048]{1,0:T(8,128)(2,1)}, bf16[128,2048]{1,0:T(8,128)(2,1)}) custom-call(bf16[128,2048]{1,0:T(8,128)(2,1)S(1)} %get-tuple-element.49.refs_0_, ...), custom_call_target="tpu_custom_call", output_to_operand_aliasing={{0}: (10, {}), {1}: (11, {}), {2}: (12, {}), {3}: (13, {})} | custom-call | flops 67108864 | bytes 2097152 | tf_op jit(solution)/shard_map/finish/pallas_call | solution.py:376
  (16 shorter events, 1.0 us)
Async XLA Ops:
  2.4 1.7 %collective-permute-start = (bf16[2,512,128]{2,1,0:T(8,128)(2,1)S(1)}, bf16[2,512,128]{2,1,0:T(8,128)(2,1)S(1)}, u32[]{:S(2)}, u32[]{:S(2)}) collective-permute-start(bf16[2,512,128]{2,1,0:T(8,128)(2,1)S(1)} %get-tuple-element.54), channel_id=1, source_target_pairs={{0,1},{1,0},{2,3},{3,2},{4,5},{5,4},{6,7},{7,6},{8,9},{9,8},{10,11... | collective-permute-start | bytes 786440 | tf_op jit(solution)/shard_map/ppermute | solution.py:394
  3.2 3.9 %collective-permute-start.2 = (bf16[2,512,128]{2,1,0:T(8,128)(2,1)S(1)}, bf16[2,512,128]{2,1,0:T(8,128)(2,1)S(1)}, u32[]{:S(2)}, u32[]{:S(2)}) collective-permute-start(bf16[2,512,128]{2,1,0:T(8,128)(2,1)S(1)} %sums.3), channel_id=1, source_target_pairs={{0,1},{1,0},{2,3},{3,2},{4,5},{5,4},{6,7},{7,6},{8,9},{9,8},{10,11... | collective-permute-start | bytes 786440 | tf_op jit(solution)/shard_map/ppermute | solution.py:394
  4.2 7.0 %collective-permute-start.1 = (bf16[2,256,128]{2,1,0:T(8,128)(2,1)S(1)}, bf16[2,256,128]{2,1,0:T(8,128)(2,1)S(1)}, u32[]{:S(2)}, u32[]{:S(2)}) collective-permute-start(bf16[2,256,128]{2,1,0:T(8,128)(2,1)S(1)} %get-tuple-element.56), channel_id=1, source_target_pairs={{0,2},{1,3},{2,0},{3,1},{4,6},{5,7},{6,4},{7,5},{8,10},{9,11},{10,... | collective-permute-start | bytes 393224 | tf_op jit(solution)/shard_map/ppermute | solution.py:394
  7.1 7.8 %collective-permute-start.3 = (bf16[2,256,128]{2,1,0:T(8,128)(2,1)S(1)}, bf16[2,256,128]{2,1,0:T(8,128)(2,1)S(1)}, u32[]{:S(2)}, u32[]{:S(2)}) collective-permute-start(bf16[2,256,128]{2,1,0:T(8,128)(2,1)S(1)} %get-tuple-element.58), channel_id=1, source_target_pairs={{0,6},{1,7},{2,4},{3,5},{4,2},{5,3},{6,0},{7,1},{8,14},{9,15},{10,... | collective-permute-start | bytes 393224 | tf_op jit(solution)/shard_map/ppermute | solution.py:394
  8.7 8.1 %collective-permute-start.4 = (bf16[2,256,128]{2,1,0:T(8,128)(2,1)S(1)}, bf16[2,256,128]{2,1,0:T(8,128)(2,1)S(1)}, u32[]{:S(2)}, u32[]{:S(2)}) collective-permute-start(bf16[2,256,128]{2,1,0:T(8,128)(2,1)S(1)} %get-tuple-element.59), channel_id=1, source_target_pairs={{0,4},{1,5},{2,6},{3,7},{4,0},{5,1},{6,2},{7,3},{8,12},{9,13},{10,... | collective-permute-start | bytes 393224 | tf_op jit(solution)/shard_map/ppermute | solution.py:394
  16.9 6.9 %collective-permute-start.5 = (bf16[256,128]{1,0:T(8,128)(2,1)S(1)}, bf16[256,128]{1,0:T(8,128)(2,1)S(1)}, u32[]{:S(2)}, u32[]{:S(2)}) collective-permute-start(bf16[256,128]{1,0:T(8,128)(2,1)S(1)} %get-tuple-element.72), channel_id=1, source_target_pairs={{0,24},{8,16},{16,8},{24,0},{1,25},{9,17},{17,9},{25,1},{2,26},{10... | collective-permute-start | bytes 196616 | tf_op jit(solution)/shard_map/ppermute | solution.py:394
  20.6 5.4 %collective-permute-start.6 = (bf16[256,128]{1,0:T(8,128)(2,1)S(1)}, bf16[256,128]{1,0:T(8,128)(2,1)S(1)}, u32[]{:S(2)}, u32[]{:S(2)}) collective-permute-start(bf16[256,128]{1,0:T(8,128)(2,1)S(1)} %get-tuple-element.73), channel_id=1, source_target_pairs={{0,16},{8,24},{16,0},{24,8},{1,17},{9,25},{17,1},{25,9},{2,18},{10... | collective-permute-start | bytes 196616 | tf_op jit(solution)/shard_map/ppermute | solution.py:394
  20.6 5.4 %collective-permute-start.7 = (bf16[256,128]{1,0:T(8,128)(2,1)S(1)}, bf16[256,128]{1,0:T(8,128)(2,1)S(1)}, u32[]{:S(2)}, u32[]{:S(2)}) collective-permute-start(bf16[256,128]{1,0:T(8,128)(2,1)S(1)} %get-tuple-element.74), channel_id=1, source_target_pairs={{0,8},{8,0},{16,24},{24,16},{1,9},{9,1},{17,25},{25,17},{2,10},{10... | collective-permute-start | bytes 196616 | tf_op jit(solution)/shard_map/ppermute | solution.py:394
  26.2 6.3 %collective-permute-start.10 = (bf16[2,256,128]{2,1,0:T(8,128)(2,1)S(1)}, bf16[2,256,128]{2,1,0:T(8,128)(2,1)S(1)}, u32[]{:S(2)}, u32[]{:S(2)}) collective-permute-start(bf16[2,256,128]{2,1,0:T(8,128)(2,1)S(1)} %get-tuple-element.78), channel_id=1, source_target_pairs={{0,2},{1,3},{2,0},{3,1},{4,6},{5,7},{6,4},{7,5},{8,10},{9,11},{10,... | collective-permute-start | bytes 393224 | tf_op jit(solution)/shard_map/ppermute | solution.py:394
  27.3 6.5 %collective-permute-start.8 = (bf16[2,256,128]{2,1,0:T(8,128)(2,1)S(1)}, bf16[2,256,128]{2,1,0:T(8,128)(2,1)S(1)}, u32[]{:S(2)}, u32[]{:S(2)}) collective-permute-start(bf16[2,256,128]{2,1,0:T(8,128)(2,1)S(1)} %get-tuple-element.75), channel_id=1, source_target_pairs={{0,6},{1,7},{2,4},{3,5},{4,2},{5,3},{6,0},{7,1},{8,14},{9,15},{10,... | collective-permute-start | bytes 393224 | tf_op jit(solution)/shard_map/ppermute | solution.py:394
  28.1 6.8 %collective-permute-start.9 = (bf16[2,256,128]{2,1,0:T(8,128)(2,1)S(1)}, bf16[2,256,128]{2,1,0:T(8,128)(2,1)S(1)}, u32[]{:S(2)}, u32[]{:S(2)}) collective-permute-start(bf16[2,256,128]{2,1,0:T(8,128)(2,1)S(1)} %get-tuple-element.76), channel_id=1, source_target_pairs={{0,4},{1,5},{2,6},{3,7},{4,0},{5,1},{6,2},{7,3},{8,12},{9,13},{10,... | collective-permute-start | bytes 393224 | tf_op jit(solution)/shard_map/ppermute | solution.py:394
  32.5 2.9 %collective-permute-start.12 = (bf16[2,512,128]{2,1,0:T(8,128)(2,1)S(1)}, bf16[2,512,128]{2,1,0:T(8,128)(2,1)S(1)}, u32[]{:S(2)}, u32[]{:S(2)}) collective-permute-start(bf16[2,512,128]{2,1,0:T(8,128)(2,1)S(1)} %theirs.3), channel_id=1, source_target_pairs={{0,1},{1,0},{2,3},{3,2},{4,5},{5,4},{6,7},{7,6},{8,9},{9,8},{10,11... | collective-permute-start | bytes 786440 | tf_op jit(solution)/shard_map/ppermute | solution.py:394
  34.9 1.6 %collective-permute-start.11 = (bf16[2,512,128]{2,1,0:T(8,128)(2,1)S(1)}, bf16[2,512,128]{2,1,0:T(8,128)(2,1)S(1)}, u32[]{:S(2)}, u32[]{:S(2)}) collective-permute-start(bf16[2,512,128]{2,1,0:T(8,128)(2,1)S(1)} %theirs.2), channel_id=1, source_target_pairs={{0,1},{1,0},{2,3},{3,2},{4,5},{5,4},{6,7},{7,6},{8,9},{9,8},{10,11... | collective-permute-start | bytes 786440 | tf_op jit(solution)/shard_map/ppermute | solution.py:394

commit v27 on v20

--- a/solution.py
+++ b/solution.py
@@ -28,7 +28,7 @@
 
 
 def distances(outer_count):
-    return range(outer_count - 1, 0, -1)
+    return [outer_count - 1, *range(1, outer_count - 1)]
 
 
 def block_start(own, block, half):

time: 35.7 us -> 35.7 us (level)
  transfers between devices with their start and end apart: 13 -> 13, of which waited for: 7 -> 8; matrix products, arithmetic and copies ran while one was open for 0% -> 0% of each run, Pallas kernels for 16% -> 16%
where the time goes in v27:
time: 35.7 us; the launch traced here: 35.6 us
  starting transfers between devices  13.6 us (38%)
  waiting for transfers between devices  12.3 us (34%)
  Pallas kernels  8.87 us (25%)
  between operations  0.76 us (2%)
    ppermute x13, starting transfers between devices, swap(): lax.ppermute(x, axis, [(i, i ^ bits) for i in range(lax.axis_size(axis))])  13.6 us
    ppermute x13, waiting for transfers between devices, swap(): lax.ppermute(x, axis, [(i, i ^ bits) for i in range(lax.axis_size(axis))])  12.3 us
    pallas_call x4, Pallas kernels, finish(): pl.pallas_call(functools.partial(finish_kernel, scale, own, block, len(sl...  3.69 us
    pallas_call x1, Pallas kernels, local_part(): pl.pallas_call(local_kernel, name='local', in_specs=[VMEM] * 4, out_specs...  2.16 us
    pallas_call x1, Pallas kernels, load(): pl.pallas_call(load_kernel, name='load', in_specs=[ANY] * 4, out_specs=[V...  1.77 us
    pallas_call x2, Pallas kernels, sums(): pl.pallas_call(functools.partial(sums_kernel, wanted), name='sums', in_sp...  0.75 us
  transfers between devices with their start and end apart: 13, of which 8 were waited for; matrix products, arithmetic and copies ran while one was open for 0% of the time, Pallas kernels for 16%

profile of v27, /device:TPU:0, one launch (start us, length us, event | category | flops | bytes accessed | tf_op | source)
XLA Modules:
  0.0 35.6 jit_solution(14704494977398300123)
XLA Ops:
  0.6 1.8 %load.1 = (bf16[128,2048]{1,0:T(8,128)(2,1)S(1)}, bf16[128,2048]{1,0:T(8,128)(2,1)S(1)}, bf16[128,2048]{1,0:T(8,128)(2,1)S(1)}, bf16[128,2048]{1,0:T(8,128)(2,1)S(1)}, bf16[2,512,128]{2,1,0:T(8,128)(2,1)S(1)}) custom-call(bf16[128,2048]{1,0:T(8,128)(2,1)} %refs_0_.1, bf16[128,2048]{1,0:T(8,128)(2,1)} %refs_1_.1, bf16[128,2048]{1,0:T(8,128)(2,1)} %refs_2_.1, ...), custom_call_target="tpu_custom_call" | custom-call | flops 33554432 | bytes 2621440 | tf_op jit(solution)/shard_map/load/pallas_call | solution.py:94
  2.4 0.5 %collective-permute-start = (bf16[2,512,128]{2,1,0:T(8,128)(2,1)S(1)}, bf16[2,512,128]{2,1,0:T(8,128)(2,1)S(1)}, u32[]{:S(2)}, u32[]{:S(2)}) collective-permute-start(bf16[2,512,128]{2,1,0:T(8,128)(2,1)S(1)} %get-tuple-element.54), channel_id=1, source_target_pairs={{0,1},{1,0},{2,3},{3,2},{4,5},{5,4},{6,7},{7,6},{8,9},{9,8},{10,11... | collective-permute-start | bytes 786440 | tf_op jit(solution)/shard_map/ppermute | solution.py:386
  2.9 0.3 sums.3
  3.3 0.5 %sums.2 = (bf16[2,512,128]{2,1,0:T(8,128)(2,1)S(1)}, bf16[2,512,128]{2,1,0:T(8,128)(2,1)S(1)}) custom-call(bf16[128,2048]{1,0:T(8,128)(2,1)S(1)} %get-tuple-element.49.refs_0_, bf16[128,2048]{1,0:T(8,128)(2,1)S(1)} %get-tuple-element.50.refs_1_, bf16[128,2048]{1,0:T(8,128)(2,1)S(1)} %get-tuple-element.51.refs_2_, bf16[128,2048]{1,0:T(8,128)(2,1)S(1)} %get-tuple-element.52.refs_3_), custom_call_target="tpu_custom_call" | custom-call | flops 67108864 | bytes 1572864 | tf_op jit(solution)/shard_map/sums/pallas_call | solution.py:116
  3.8 0.3 collective-permute-done.got_ref.refs_10_
  4.2 2.9 %collective-permute-start.1 = (bf16[2,256,128]{2,1,0:T(8,128)(2,1)S(1)}, bf16[2,256,128]{2,1,0:T(8,128)(2,1)S(1)}, u32[]{:S(2)}, u32[]{:S(2)}) collective-permute-start(bf16[2,256,128]{2,1,0:T(8,128)(2,1)S(1)} %get-tuple-element.56), channel_id=1, source_target_pairs={{0,2},{1,3},{2,0},{3,1},{4,6},{5,7},{6,4},{7,5},{8,10},{9,11},{10,... | collective-permute-start | bytes 393224 | tf_op jit(solution)/shard_map/ppermute | solution.py:386
  7.1 1.6 %collective-permute-start.3 = (bf16[2,256,128]{2,1,0:T(8,128)(2,1)S(1)}, bf16[2,256,128]{2,1,0:T(8,128)(2,1)S(1)}, u32[]{:S(2)}, u32[]{:S(2)}) collective-permute-start(bf16[2,256,128]{2,1,0:T(8,128)(2,1)S(1)} %get-tuple-element.58), channel_id=1, source_target_pairs={{0,4},{1,5},{2,6},{3,7},{4,0},{5,1},{6,2},{7,3},{8,12},{9,13},{10,... | collective-permute-start | bytes 393224 | tf_op jit(solution)/shard_map/ppermute | solution.py:386
  8.7 0.3 collective-permute-start.4
  9.0 2.2 %local.1 = (f32[128,2048]{1,0:T(8,128)S(1)}, f32[128,2048]{1,0:T(8,128)S(1)}, f32[128,2048]{1,0:T(8,128)S(1)}, f32[128,2048]{1,0:T(8,128)S(1)}) custom-call(bf16[128,2048]{1,0:T(8,128)(2,1)S(1)} %get-tuple-element.49.refs_0_, bf16[128,2048]{1,0:T(8,128)(2,1)S(1)} %get-tuple-element.50.refs_1_, bf16[128,2048]{1,0:T(8,128)(2,1)S(1)} %get-tuple-element.51.refs_2_, ...), custom_call_target="tpu_custom_call" | custom-call | flops 402653184 | bytes 6291456 | tf_op jit(solution)/shard_map/local/pallas_call | solution.py:274
  11.2 4.1 %collective-permute-done.3.refs_2_ = bf16[2,256,128]{2,1,0:T(8,128)(2,1)S(1)} collective-permute-done((bf16[2,256,128]{2,1,0:T(8,128)(2,1)S(1)}, bf16[2,256,128]{2,1,0:T(8,128)(2,1)S(1)}, u32[]{:S(2)}, u32[]{:S(2)}) %collective-permute-start.3) | collective-permute-done | bytes 131104 | tf_op jit(solution)/shard_map/ppermute | solution.py:386
  15.4 3.7 %collective-permute-start.5 = (bf16[256,128]{1,0:T(8,128)(2,1)S(1)}, bf16[256,128]{1,0:T(8,128)(2,1)S(1)}, u32[]{:S(2)}, u32[]{:S(2)}) collective-permute-start(bf16[256,128]{1,0:T(8,128)(2,1)S(1)} %get-tuple-element.72), channel_id=1, source_target_pairs={{0,24},{8,16},{16,8},{24,0},{1,25},{9,17},{17,9},{25,1},{2,26},{10... | collective-permute-start | bytes 196616 | tf_op jit(solution)/shard_map/ppermute | solution.py:386
  19.0 0.8 %collective-permute-start.7 = (bf16[256,128]{1,0:T(8,128)(2,1)S(1)}, bf16[256,128]{1,0:T(8,128)(2,1)S(1)}, u32[]{:S(2)}, u32[]{:S(2)}) collective-permute-start(bf16[256,128]{1,0:T(8,128)(2,1)S(1)} %get-tuple-element.74), channel_id=1, source_target_pairs={{0,16},{8,24},{16,0},{24,8},{1,17},{9,25},{17,1},{25,9},{2,18},{10... | collective-permute-start | bytes 196616 | tf_op jit(solution)/shard_map/ppermute | solution.py:386
  19.8 1.7 %collective-permute-done.5.refs_4_ = bf16[256,128]{1,0:T(8,128)(2,1)S(1)} collective-permute-done((bf16[256,128]{1,0:T(8,128)(2,1)S(1)}, bf16[256,128]{1,0:T(8,128)(2,1)S(1)}, u32[]{:S(2)}, u32[]{:S(2)}) %collective-permute-start.5) | collective-permute-done | bytes 65568 | tf_op jit(solution)/shard_map/ppermute | solution.py:386
  21.6 1.7 %collective-permute-done.6.refs_5_ = bf16[256,128]{1,0:T(8,128)(2,1)S(1)} collective-permute-done((bf16[256,128]{1,0:T(8,128)(2,1)S(1)}, bf16[256,128]{1,0:T(8,128)(2,1)S(1)}, u32[]{:S(2)}, u32[]{:S(2)}) %collective-permute-start.6) | collective-permute-done | bytes 65568 | tf_op jit(solution)/shard_map/ppermute | solution.py:386
  23.3 0.9 %collective-permute-done.7.refs_6_ = bf16[256,128]{1,0:T(8,128)(2,1)S(1)} collective-permute-done((bf16[256,128]{1,0:T(8,128)(2,1)S(1)}, bf16[256,128]{1,0:T(8,128)(2,1)S(1)}, u32[]{:S(2)}, u32[]{:S(2)}) %collective-permute-start.7) | collective-permute-done | bytes 65568 | tf_op jit(solution)/shard_map/ppermute | solution.py:386
  24.4 1.2 %collective-permute-start.10 = (bf16[2,256,128]{2,1,0:T(8,128)(2,1)S(1)}, bf16[2,256,128]{2,1,0:T(8,128)(2,1)S(1)}, u32[]{:S(2)}, u32[]{:S(2)}) collective-permute-start(bf16[2,256,128]{2,1,0:T(8,128)(2,1)S(1)} %get-tuple-element.78), channel_id=1, source_target_pairs={{0,2},{1,3},{2,0},{3,1},{4,6},{5,7},{6,4},{7,5},{8,10},{9,11},{10,... | collective-permute-start | bytes 393224 | tf_op jit(solution)/shard_map/ppermute | solution.py:386
  25.6 1.3 %collective-permute-start.8 = (bf16[2,256,128]{2,1,0:T(8,128)(2,1)S(1)}, bf16[2,256,128]{2,1,0:T(8,128)(2,1)S(1)}, u32[]{:S(2)}, u32[]{:S(2)}) collective-permute-start(bf16[2,256,128]{2,1,0:T(8,128)(2,1)S(1)} %get-tuple-element.75), channel_id=1, source_target_pairs={{0,4},{1,5},{2,6},{3,7},{4,0},{5,1},{6,2},{7,3},{8,12},{9,13},{10,... | collective-permute-start | bytes 393224 | tf_op jit(solution)/shard_map/ppermute | solution.py:386
  26.9 1.1 %collective-permute-start.9 = (bf16[2,256,128]{2,1,0:T(8,128)(2,1)S(1)}, bf16[2,256,128]{2,1,0:T(8,128)(2,1)S(1)}, u32[]{:S(2)}, u32[]{:S(2)}) collective-permute-start(bf16[2,256,128]{2,1,0:T(8,128)(2,1)S(1)} %get-tuple-element.76), channel_id=1, source_target_pairs={{0,6},{1,7},{2,4},{3,5},{4,2},{5,3},{6,0},{7,1},{8,14},{9,15},{10,... | collective-permute-start | bytes 393224 | tf_op jit(solution)/shard_map/ppermute | solution.py:386
  28.0 2.7 %collective-permute-done.10.refs_9_.refs_1_ = bf16[2,256,128]{2,1,0:T(8,128)(2,1)S(1)} collective-permute-done((bf16[2,256,128]{2,1,0:T(8,128)(2,1)S(1)}, bf16[2,256,128]{2,1,0:T(8,128)(2,1)S(1)}, u32[]{:S(2)}, u32[]{:S(2)}) %collective-permute-start.10) | collective-permute-done | bytes 131104 | tf_op jit(solution)/shard_map/ppermute | solution.py:386
  30.8 1.2 %finish.4 = (bf16[128,2048]{1,0:T(8,128)(2,1)}, bf16[128,2048]{1,0:T(8,128)(2,1)}, bf16[128,2048]{1,0:T(8,128)(2,1)}, bf16[128,2048]{1,0:T(8,128)(2,1)}) custom-call(bf16[128,2048]{1,0:T(8,128)(2,1)S(1)} %get-tuple-element.49.refs_0_, bf16[128,2048]{1,0:T(8,128)(2,1)S(1)} %get-tuple-element.50.refs_1_, bf16[128,2048]{1,0:T(8,128)(2,1)S(1)} %get-tuple-element.51.refs_2_, ...), custom_call_target="tpu_custom_call" | custom-call | flops 67108864 | bytes 2097152 | tf_op jit(solution)/shard_map/finish/pallas_call | solution.py:368
  32.0 0.7 %collective-permute-done.9.refs_1_.refs_9_ = bf16[2,256,128]{2,1,0:T(8,128)(2,1)S(1)} collective-permute-done((bf16[2,256,128]{2,1,0:T(8,128)(2,1)S(1)}, bf16[2,256,128]{2,1,0:T(8,128)(2,1)S(1)}, u32[]{:S(2)}, u32[]{:S(2)}) %collective-permute-start.9) | collective-permute-done | bytes 131104 | tf_op jit(solution)/shard_map/ppermute | solution.py:386
  32.9 0.4 %finish.5.refs_9_ = bf16[4,128,512]{2,1,0:T(8,128)(2,1)S(1)} custom-call(bf16[128,2048]{1,0:T(8,128)(2,1)S(1)} %get-tuple-element.49.refs_0_, bf16[128,2048]{1,0:T(8,128)(2,1)S(1)} %get-tuple-element.50.refs_1_, bf16[128,2048]{1,0:T(8,128)(2,1)S(1)} %get-tuple-element.51.refs_2_, bf16[128,2048]{1,0:T(8,128)(2,1)S(1)} %get-tuple-element.52.refs_3_, ...), custom_call_target="tpu_custom_call" | custom-call | flops 67108864 | bytes 2097152 | tf_op jit(solution)/shard_map/finish/pallas_call | solution.py:368
  33.3 0.9 %finish.6 = (bf16[128,2048]{1,0:T(8,128)(2,1)}, bf16[128,2048]{1,0:T(8,128)(2,1)}, bf16[128,2048]{1,0:T(8,128)(2,1)}, bf16[128,2048]{1,0:T(8,128)(2,1)}, bf16[4,128,512]{2,1,0:T(8,128)(2,1)S(1)}) custom-call(bf16[128,2048]{1,0:T(8,128)(2,1)S(1)} %get-tuple-element.49.refs_0_, ...), custom_call_target="tpu_custom_call", output_to_operand_aliasing={{0}: (10, {}), {1}: (11, {}), {2}: (12, {}), {3}: (13, {})} | custom-call | flops 67108864 | bytes 2097152 | tf_op jit(solution)/shard_map/finish/pallas_call | solution.py:368
  34.4 1.2 %finish.7 = (bf16[128,2048]{1,0:T(8,128)(2,1)}, bf16[128,2048]{1,0:T(8,128)(2,1)}, bf16[128,2048]{1,0:T(8,128)(2,1)}, bf16[128,2048]{1,0:T(8,128)(2,1)}) custom-call(bf16[128,2048]{1,0:T(8,128)(2,1)S(1)} %get-tuple-element.49.refs_0_, ...), custom_call_target="tpu_custom_call", output_to_operand_aliasing={{0}: (10, {}), {1}: (11, {}), {2}: (12, {}), {3}: (13, {})} | custom-call | flops 67108864 | bytes 2097152 | tf_op jit(solution)/shard_map/finish/pallas_call | solution.py:368
  (16 shorter events, 0.9 us)
Async XLA Ops:
  2.4 1.7 %collective-permute-start = (bf16[2,512,128]{2,1,0:T(8,128)(2,1)S(1)}, bf16[2,512,128]{2,1,0:T(8,128)(2,1)S(1)}, u32[]{:S(2)}, u32[]{:S(2)}) collective-permute-start(bf16[2,512,128]{2,1,0:T(8,128)(2,1)S(1)} %get-tuple-element.54), channel_id=1, source_target_pairs={{0,1},{1,0},{2,3},{3,2},{4,5},{5,4},{6,7},{7,6},{8,9},{9,8},{10,11... | collective-permute-start | bytes 786440 | tf_op jit(solution)/shard_map/ppermute | solution.py:386
  3.2 3.9 %collective-permute-start.2 = (bf16[2,512,128]{2,1,0:T(8,128)(2,1)S(1)}, bf16[2,512,128]{2,1,0:T(8,128)(2,1)S(1)}, u32[]{:S(2)}, u32[]{:S(2)}) collective-permute-start(bf16[2,512,128]{2,1,0:T(8,128)(2,1)S(1)} %sums.3), channel_id=1, source_target_pairs={{0,1},{1,0},{2,3},{3,2},{4,5},{5,4},{6,7},{7,6},{8,9},{9,8},{10,11... | collective-permute-start | bytes 786440 | tf_op jit(solution)/shard_map/ppermute | solution.py:386
  4.2 7.0 %collective-permute-start.1 = (bf16[2,256,128]{2,1,0:T(8,128)(2,1)S(1)}, bf16[2,256,128]{2,1,0:T(8,128)(2,1)S(1)}, u32[]{:S(2)}, u32[]{:S(2)}) collective-permute-start(bf16[2,256,128]{2,1,0:T(8,128)(2,1)S(1)} %get-tuple-element.56), channel_id=1, source_target_pairs={{0,2},{1,3},{2,0},{3,1},{4,6},{5,7},{6,4},{7,5},{8,10},{9,11},{10,... | collective-permute-start | bytes 393224 | tf_op jit(solution)/shard_map/ppermute | solution.py:386
  7.1 8.1 %collective-permute-start.3 = (bf16[2,256,128]{2,1,0:T(8,128)(2,1)S(1)}, bf16[2,256,128]{2,1,0:T(8,128)(2,1)S(1)}, u32[]{:S(2)}, u32[]{:S(2)}) collective-permute-start(bf16[2,256,128]{2,1,0:T(8,128)(2,1)S(1)} %get-tuple-element.58), channel_id=1, source_target_pairs={{0,4},{1,5},{2,6},{3,7},{4,0},{5,1},{6,2},{7,3},{8,12},{9,13},{10,... | collective-permute-start | bytes 393224 | tf_op jit(solution)/shard_map/ppermute | solution.py:386
  8.7 6.6 %collective-permute-start.4 = (bf16[2,256,128]{2,1,0:T(8,128)(2,1)S(1)}, bf16[2,256,128]{2,1,0:T(8,128)(2,1)S(1)}, u32[]{:S(2)}, u32[]{:S(2)}) collective-permute-start(bf16[2,256,128]{2,1,0:T(8,128)(2,1)S(1)} %get-tuple-element.59), channel_id=1, source_target_pairs={{0,6},{1,7},{2,4},{3,5},{4,2},{5,3},{6,0},{7,1},{8,14},{9,15},{10,... | collective-permute-start | bytes 393224 | tf_op jit(solution)/shard_map/ppermute | solution.py:386
  15.4 6.2 %collective-permute-start.5 = (bf16[256,128]{1,0:T(8,128)(2,1)S(1)}, bf16[256,128]{1,0:T(8,128)(2,1)S(1)}, u32[]{:S(2)}, u32[]{:S(2)}) collective-permute-start(bf16[256,128]{1,0:T(8,128)(2,1)S(1)} %get-tuple-element.72), channel_id=1, source_target_pairs={{0,24},{8,16},{16,8},{24,0},{1,25},{9,17},{17,9},{25,1},{2,26},{10... | collective-permute-start | bytes 196616 | tf_op jit(solution)/shard_map/ppermute | solution.py:386
  19.0 4.3 %collective-permute-start.6 = (bf16[256,128]{1,0:T(8,128)(2,1)S(1)}, bf16[256,128]{1,0:T(8,128)(2,1)S(1)}, u32[]{:S(2)}, u32[]{:S(2)}) collective-permute-start(bf16[256,128]{1,0:T(8,128)(2,1)S(1)} %get-tuple-element.73), channel_id=1, source_target_pairs={{0,8},{8,0},{16,24},{24,16},{1,9},{9,1},{17,25},{25,17},{2,10},{10... | collective-permute-start | bytes 196616 | tf_op jit(solution)/shard_map/ppermute | solution.py:386
  19.0 5.2 %collective-permute-start.7 = (bf16[256,128]{1,0:T(8,128)(2,1)S(1)}, bf16[256,128]{1,0:T(8,128)(2,1)S(1)}, u32[]{:S(2)}, u32[]{:S(2)}) collective-permute-start(bf16[256,128]{1,0:T(8,128)(2,1)S(1)} %get-tuple-element.74), channel_id=1, source_target_pairs={{0,16},{8,24},{16,0},{24,8},{1,17},{9,25},{17,1},{25,9},{2,18},{10... | collective-permute-start | bytes 196616 | tf_op jit(solution)/shard_map/ppermute | solution.py:386
  24.4 6.2 %collective-permute-start.10 = (bf16[2,256,128]{2,1,0:T(8,128)(2,1)S(1)}, bf16[2,256,128]{2,1,0:T(8,128)(2,1)S(1)}, u32[]{:S(2)}, u32[]{:S(2)}) collective-permute-start(bf16[2,256,128]{2,1,0:T(8,128)(2,1)S(1)} %get-tuple-element.78), channel_id=1, source_target_pairs={{0,2},{1,3},{2,0},{3,1},{4,6},{5,7},{6,4},{7,5},{8,10},{9,11},{10,... | collective-permute-start | bytes 393224 | tf_op jit(solution)/shard_map/ppermute | solution.py:386
  25.6 6.4 %collective-permute-start.8 = (bf16[2,256,128]{2,1,0:T(8,128)(2,1)S(1)}, bf16[2,256,128]{2,1,0:T(8,128)(2,1)S(1)}, u32[]{:S(2)}, u32[]{:S(2)}) collective-permute-start(bf16[2,256,128]{2,1,0:T(8,128)(2,1)S(1)} %get-tuple-element.75), channel_id=1, source_target_pairs={{0,4},{1,5},{2,6},{3,7},{4,0},{5,1},{6,2},{7,3},{8,12},{9,13},{10,... | collective-permute-start | bytes 393224 | tf_op jit(solution)/shard_map/ppermute | solution.py:386
  26.9 5.9 %collective-permute-start.9 = (bf16[2,256,128]{2,1,0:T(8,128)(2,1)S(1)}, bf16[2,256,128]{2,1,0:T(8,128)(2,1)S(1)}, u32[]{:S(2)}, u32[]{:S(2)}) collective-permute-start(bf16[2,256,128]{2,1,0:T(8,128)(2,1)S(1)} %get-tuple-element.76), channel_id=1, source_target_pairs={{0,6},{1,7},{2,4},{3,5},{4,2},{5,3},{6,0},{7,1},{8,14},{9,15},{10,... | collective-permute-start | bytes 393224 | tf_op jit(solution)/shard_map/ppermute | solution.py:386
  30.7 2.6 %collective-permute-start.12 = (bf16[2,512,128]{2,1,0:T(8,128)(2,1)S(1)}, bf16[2,512,128]{2,1,0:T(8,128)(2,1)S(1)}, u32[]{:S(2)}, u32[]{:S(2)}) collective-permute-start(bf16[2,512,128]{2,1,0:T(8,128)(2,1)S(1)} %theirs.3), channel_id=1, source_target_pairs={{0,1},{1,0},{2,3},{3,2},{4,5},{5,4},{6,7},{7,6},{8,9},{9,8},{10,11... | collective-permute-start | bytes 786440 | tf_op jit(solution)/shard_map/ppermute | solution.py:386
  32.8 1.6 %collective-permute-start.11 = (bf16[2,512,128]{2,1,0:T(8,128)(2,1)S(1)}, bf16[2,512,128]{2,1,0:T(8,128)(2,1)S(1)}, u32[]{:S(2)}, u32[]{:S(2)}) collective-permute-start(bf16[2,512,128]{2,1,0:T(8,128)(2,1)S(1)} %theirs.2), channel_id=1, source_target_pairs={{0,1},{1,0},{2,3},{3,2},{4,5},{5,4},{6,7},{7,6},{8,9},{9,8},{10,11... | collective-permute-start | bytes 786440 | tf_op jit(solution)/shard_map/ppermute | solution.py:386

commit v28 on v24

--- a/solution.py
+++ b/solution.py
@@ -240,13 +240,18 @@
     )(*slots, keep)
 
 
-def local_kernel(core, *refs):
+def local_kernel(early, *refs):
     near, _ = near_far()
-    pl.when(near == core)(functools.partial(local_products, refs[:4], refs[-4:]))
-
-
-def local_products(tokens, outs):
-    rows, width = tokens[0].shape
+    tokens, outs = refs[:4], refs[-4:]
+    heads = tokens[0].shape[1] // HEAD
+    even = range(heads // 2) if early else range(heads // 2, heads)
+    pl.when(near == 0)(functools.partial(local_products, tokens, outs, even))
+    if not early:
+        pl.when(near == 1)(functools.partial(local_products, tokens, outs, range(heads)))
+
+
+def local_products(tokens, outs, heads):
+    rows = tokens[0].shape[0]
     at = lax.broadcasted_iota(jnp.int32, (rows, rows), 0)
     to = lax.broadcasted_iota(jnp.int32, (rows, rows), 1)
     lower = at >= to
@@ -263,7 +268,7 @@
         gv[:, cols] = dot(a, d, 0, 0)
 
     last = None
-    for h in range(width // HEAD):
+    for h in heads:
         cols = slice(h * HEAD, (h + 1) * HEAD)
         q, k, v, d = (ref[:, cols] for ref in tokens)
         a, b = masked(q, k), masked(d, v)
@@ -273,14 +278,15 @@
     second(*last)
 
 
-def local_part(core, tokens, after):
+def local_part(early, tokens, after):
     rows, width = tokens[0].shape
-    return pl.pallas_call(
-        functools.partial(local_kernel, core),
+    out = jax.ShapeDtypeStruct((rows, width // 2 if early else width), F32)
+    return pl.pallas_call(
+        functools.partial(local_kernel, early),
         name="local",
         in_specs=[VMEM] * 4 + [ANY],
         out_specs=[VMEM] * 4,
-        out_shape=[jax.ShapeDtypeStruct((rows, width), F32)] * 4,
+        out_shape=[out] * 4,
         cost_estimate=pl.CostEstimate(flops=0, bytes_accessed=0, transcendentals=0),
         compiler_params=SMALL,
     )(*tokens, after)
@@ -344,7 +350,7 @@
 
     def run(quarter):
         core = quarter // 2 if own else 1 - quarter // 2
-        local = locals_[4 * core : 4 * core + 4]
+        local = locals_[:4] if core == quarter // 2 == 0 else locals_[4:]
         for s, slot in enumerate(slots if own else ()):
             part = slot_rows(s, count, slot.shape[1])
             states[core, part] = slot[core]
@@ -401,11 +407,11 @@
     tokens, give = load((queries, keys, values, cotangent))
     got = [swap(give, "inner", 1), swap(*sums(tokens, (False, 1)), "inner", 1)]
     keep = sums(tokens, (True, 0), (True, 1))
-    early = local_part(0, tokens, keep[1])
+    early = local_part(True, tokens, keep[1])
     slots = []
     for b in range(2):
         slots += pair_slots(keep[b], got[b], far_count // 2, slots[0] if slots else early[0])
-    slots, late = lax.optimization_barrier((swap_far(slots), local_part(1, tokens, slots[-1])))
+    slots, late = lax.optimization_barrier((swap_far(slots), local_part(False, tokens, slots[-1])))
     local = [*early, *late]
     sends = group_sends(slots, outer_count)
     others = [swap(send, "outer", s) for s, send in zip(distances(outer_count), sends)]

time: 35.8 us -> 35.8 us (level)
  transfers between devices with their start and end apart: 13 -> 13, of which waited for: 8 -> 7; matrix products, arithmetic and copies ran while one was open for 0% -> 0% of each run, Pallas kernels for 16% -> 16%
where the time goes in v28:
time: 35.8 us; the launch traced here: 35.6 us
  starting transfers between devices  13.5 us (38%)
  waiting for transfers between devices  12.3 us (34%)
  Pallas kernels  9.07 us (25%)
  between operations  0.76 us (2%)
    ppermute x13, starting transfers between devices, swap(): lax.ppermute(x, axis, [(i, i ^ bits) for i in range(lax.axis_size(axis))])  13.5 us
    ppermute x13, waiting for transfers between devices, swap(): lax.ppermute(x, axis, [(i, i ^ bits) for i in range(lax.axis_size(axis))])  12.3 us
    pallas_call x4, Pallas kernels, finish(): pl.pallas_call(functools.partial(finish_kernel, scale, own, block, len(sl...  3.66 us
    pallas_call x2, Pallas kernels, local_part(): pl.pallas_call(functools.partial(local_kernel, early), name='local', in_s...  2.35 us
    pallas_call x1, Pallas kernels, load(): pl.pallas_call(load_kernel, name='load', in_specs=[ANY] * 4, out_specs=[V...  1.77 us
    pallas_call x2, Pallas kernels, sums(): pl.pallas_call(functools.partial(sums_kernel, wanted), name='sums', in_sp...  0.75 us
  transfers between devices with their start and end apart: 13, of which 7 were waited for; matrix products, arithmetic and copies ran while one was open for 0% of the time, Pallas kernels for 16%

profile of v28, /device:TPU:0, one launch (start us, length us, event | category | flops | bytes accessed | tf_op | source)
XLA Modules:
  0.0 35.6 jit_solution(3963216112903894398)
XLA Ops:
  0.6 1.8 %load.1 = (bf16[128,2048]{1,0:T(8,128)(2,1)S(1)}, bf16[128,2048]{1,0:T(8,128)(2,1)S(1)}, bf16[128,2048]{1,0:T(8,128)(2,1)S(1)}, bf16[128,2048]{1,0:T(8,128)(2,1)S(1)}, bf16[2,512,128]{2,1,0:T(8,128)(2,1)S(1)}) custom-call(bf16[128,2048]{1,0:T(8,128)(2,1)} %refs_0_.1, bf16[128,2048]{1,0:T(8,128)(2,1)} %refs_1_.1, bf16[128,2048]{1,0:T(8,128)(2,1)} %refs_2_.1, ...), custom_call_target="tpu_custom_call" | custom-call | flops 33554432 | bytes 2621440 | tf_op jit(solution)/shard_map/load/pallas_call | solution.py:94
  2.4 0.5 %collective-permute-start = (bf16[2,512,128]{2,1,0:T(8,128)(2,1)S(1)}, bf16[2,512,128]{2,1,0:T(8,128)(2,1)S(1)}, u32[]{:S(2)}, u32[]{:S(2)}) collective-permute-start(bf16[2,512,128]{2,1,0:T(8,128)(2,1)S(1)} %get-tuple-element.63), channel_id=1, source_target_pairs={{0,1},{1,0},{2,3},{3,2},{4,5},{5,4},{6,7},{7,6},{8,9},{9,8},{10,11... | collective-permute-start | bytes 786440 | tf_op jit(solution)/shard_map/ppermute | solution.py:396
  2.9 0.3 sums.3
  3.3 0.5 %sums.2 = (bf16[2,512,128]{2,1,0:T(8,128)(2,1)S(1)}, bf16[2,512,128]{2,1,0:T(8,128)(2,1)S(1)}) custom-call(bf16[128,2048]{1,0:T(8,128)(2,1)S(1)} %get-tuple-element.53.refs_0_, bf16[128,2048]{1,0:T(8,128)(2,1)S(1)} %get-tuple-element.54.refs_1_, bf16[128,2048]{1,0:T(8,128)(2,1)S(1)} %get-tuple-element.55.refs_2_, bf16[128,2048]{1,0:T(8,128)(2,1)S(1)} %get-tuple-element.56.refs_3_), custom_call_target="tpu_custom_call" | custom-call | flops 67108864 | bytes 1572864 | tf_op jit(solution)/shard_map/sums/pallas_call | solution.py:116
  3.8 1.2 %local.2 = (f32[128,1024]{1,0:T(8,128)S(1)}, f32[128,1024]{1,0:T(8,128)S(1)}, f32[128,1024]{1,0:T(8,128)S(1)}, f32[128,1024]{1,0:T(8,128)S(1)}) custom-call(bf16[128,2048]{1,0:T(8,128)(2,1)S(1)} %get-tuple-element.53.refs_0_, bf16[128,2048]{1,0:T(8,128)(2,1)S(1)} %get-tuple-element.54.refs_1_, bf16[128,2048]{1,0:T(8,128)(2,1)S(1)} %get-tuple-element.55.refs_2_, ...), custom_call_target="tpu_custom_call" | custom-call | tf_op jit(solution)/shard_map/local/pallas_call | solution.py:284
  5.1 3.0 %collective-permute-start.1 = (bf16[2,256,128]{2,1,0:T(8,128)(2,1)S(1)}, bf16[2,256,128]{2,1,0:T(8,128)(2,1)S(1)}, u32[]{:S(2)}, u32[]{:S(2)}) collective-permute-start(bf16[2,256,128]{2,1,0:T(8,128)(2,1)S(1)} %get-tuple-element.65), channel_id=1, source_target_pairs={{0,2},{1,3},{2,0},{3,1},{4,6},{5,7},{6,4},{7,5},{8,10},{9,11},{10,... | collective-permute-start | bytes 393224 | tf_op jit(solution)/shard_map/ppermute | solution.py:396
  8.2 1.6 %collective-permute-start.3 = (bf16[2,256,128]{2,1,0:T(8,128)(2,1)S(1)}, bf16[2,256,128]{2,1,0:T(8,128)(2,1)S(1)}, u32[]{:S(2)}, u32[]{:S(2)}) collective-permute-start(bf16[2,256,128]{2,1,0:T(8,128)(2,1)S(1)} %get-tuple-element.66), channel_id=1, source_target_pairs={{0,4},{1,5},{2,6},{3,7},{4,0},{5,1},{6,2},{7,3},{8,12},{9,13},{10,... | collective-permute-start | bytes 393224 | tf_op jit(solution)/shard_map/ppermute | solution.py:396
  9.8 1.2 %local.3 = (f32[128,2048]{1,0:T(8,128)S(1)}, f32[128,2048]{1,0:T(8,128)S(1)}, f32[128,2048]{1,0:T(8,128)S(1)}, f32[128,2048]{1,0:T(8,128)S(1)}) custom-call(bf16[128,2048]{1,0:T(8,128)(2,1)S(1)} %get-tuple-element.53.refs_0_, bf16[128,2048]{1,0:T(8,128)(2,1)S(1)} %get-tuple-element.54.refs_1_, bf16[128,2048]{1,0:T(8,128)(2,1)S(1)} %get-tuple-element.55.refs_2_, ...), custom_call_target="tpu_custom_call" | custom-call | tf_op jit(solution)/shard_map/local/pallas_call | solution.py:284
  11.0 1.0 %collective-permute-done.1.refs_1_ = bf16[2,256,128]{2,1,0:T(8,128)(2,1)S(1)} collective-permute-done((bf16[2,256,128]{2,1,0:T(8,128)(2,1)S(1)}, bf16[2,256,128]{2,1,0:T(8,128)(2,1)S(1)}, u32[]{:S(2)}, u32[]{:S(2)}) %collective-permute-start.1) | collective-permute-done | bytes 131104 | tf_op jit(solution)/shard_map/ppermute | solution.py:396
  11.9 4.1 %collective-permute-done.3.refs_2_ = bf16[2,256,128]{2,1,0:T(8,128)(2,1)S(1)} collective-permute-done((bf16[2,256,128]{2,1,0:T(8,128)(2,1)S(1)}, bf16[2,256,128]{2,1,0:T(8,128)(2,1)S(1)}, u32[]{:S(2)}, u32[]{:S(2)}) %collective-permute-start.3) | collective-permute-done | bytes 131104 | tf_op jit(solution)/shard_map/ppermute | solution.py:396
  16.1 3.7 %collective-permute-start.5 = (bf16[256,128]{1,0:T(8,128)(2,1)S(1)}, bf16[256,128]{1,0:T(8,128)(2,1)S(1)}, u32[]{:S(2)}, u32[]{:S(2)}) collective-permute-start(bf16[256,128]{1,0:T(8,128)(2,1)S(1)} %get-tuple-element.80), channel_id=1, source_target_pairs={{0,24},{8,16},{16,8},{24,0},{1,25},{9,17},{17,9},{25,1},{2,26},{10... | collective-permute-start | bytes 196616 | tf_op jit(solution)/shard_map/ppermute | solution.py:396
  19.8 0.8 %collective-permute-start.7 = (bf16[256,128]{1,0:T(8,128)(2,1)S(1)}, bf16[256,128]{1,0:T(8,128)(2,1)S(1)}, u32[]{:S(2)}, u32[]{:S(2)}) collective-permute-start(bf16[256,128]{1,0:T(8,128)(2,1)S(1)} %get-tuple-element.82), channel_id=1, source_target_pairs={{0,8},{8,0},{16,24},{24,16},{1,9},{9,1},{17,25},{25,17},{2,10},{10... | collective-permute-start | bytes 196616 | tf_op jit(solution)/shard_map/ppermute | solution.py:396
  20.6 2.0 %collective-permute-done.5.refs_4_ = bf16[256,128]{1,0:T(8,128)(2,1)S(1)} collective-permute-done((bf16[256,128]{1,0:T(8,128)(2,1)S(1)}, bf16[256,128]{1,0:T(8,128)(2,1)S(1)}, u32[]{:S(2)}, u32[]{:S(2)}) %collective-permute-start.5) | collective-permute-done | bytes 65568 | tf_op jit(solution)/shard_map/ppermute | solution.py:396
  22.6 2.4 %collective-permute-done.6.refs_5_ = bf16[256,128]{1,0:T(8,128)(2,1)S(1)} collective-permute-done((bf16[256,128]{1,0:T(8,128)(2,1)S(1)}, bf16[256,128]{1,0:T(8,128)(2,1)S(1)}, u32[]{:S(2)}, u32[]{:S(2)}) %collective-permute-start.6) | collective-permute-done | bytes 65568 | tf_op jit(solution)/shard_map/ppermute | solution.py:396
  25.0 0.2 scan.1
  25.2 1.0 %collective-permute-start.10 = (bf16[2,256,128]{2,1,0:T(8,128)(2,1)S(1)}, bf16[2,256,128]{2,1,0:T(8,128)(2,1)S(1)}, u32[]{:S(2)}, u32[]{:S(2)}) collective-permute-start(bf16[2,256,128]{2,1,0:T(8,128)(2,1)S(1)} %get-tuple-element.86), channel_id=1, source_target_pairs={{0,2},{1,3},{2,0},{3,1},{4,6},{5,7},{6,4},{7,5},{8,10},{9,11},{10,... | collective-permute-start | bytes 393224 | tf_op jit(solution)/shard_map/ppermute | solution.py:396
  26.1 0.8 %collective-permute-start.8 = (bf16[2,256,128]{2,1,0:T(8,128)(2,1)S(1)}, bf16[2,256,128]{2,1,0:T(8,128)(2,1)S(1)}, u32[]{:S(2)}, u32[]{:S(2)}) collective-permute-start(bf16[2,256,128]{2,1,0:T(8,128)(2,1)S(1)} %get-tuple-element.83), channel_id=1, source_target_pairs={{0,4},{1,5},{2,6},{3,7},{4,0},{5,1},{6,2},{7,3},{8,12},{9,13},{10,... | collective-permute-start | bytes 393224 | tf_op jit(solution)/shard_map/ppermute | solution.py:396
  26.9 1.8 %collective-permute-start.9 = (bf16[2,256,128]{2,1,0:T(8,128)(2,1)S(1)}, bf16[2,256,128]{2,1,0:T(8,128)(2,1)S(1)}, u32[]{:S(2)}, u32[]{:S(2)}) collective-permute-start(bf16[2,256,128]{2,1,0:T(8,128)(2,1)S(1)} %get-tuple-element.84), channel_id=1, source_target_pairs={{0,6},{1,7},{2,4},{3,5},{4,2},{5,3},{6,0},{7,1},{8,14},{9,15},{10,... | collective-permute-start | bytes 393224 | tf_op jit(solution)/shard_map/ppermute | solution.py:396
  28.7 2.4 %collective-permute-done.10.refs_13_.refs_1_ = bf16[2,256,128]{2,1,0:T(8,128)(2,1)S(1)} collective-permute-done((bf16[2,256,128]{2,1,0:T(8,128)(2,1)S(1)}, bf16[2,256,128]{2,1,0:T(8,128)(2,1)S(1)}, u32[]{:S(2)}, u32[]{:S(2)}) %collective-permute-start.10) | collective-permute-done | bytes 131104 | tf_op jit(solution)/shard_map/ppermute | solution.py:396
  31.2 1.2 %finish.4 = (bf16[128,2048]{1,0:T(8,128)(2,1)}, bf16[128,2048]{1,0:T(8,128)(2,1)}, bf16[128,2048]{1,0:T(8,128)(2,1)}, bf16[128,2048]{1,0:T(8,128)(2,1)}) custom-call(bf16[128,2048]{1,0:T(8,128)(2,1)S(1)} %get-tuple-element.53.refs_0_, bf16[128,2048]{1,0:T(8,128)(2,1)S(1)} %get-tuple-element.54.refs_1_, bf16[128,2048]{1,0:T(8,128)(2,1)S(1)} %get-tuple-element.55.refs_2_, ...), custom_call_target="tpu_custom_call" | custom-call | flops 67108864 | bytes 2097152 | tf_op jit(solution)/shard_map/finish/pallas_call | solution.py:378
  32.4 0.4 %collective-permute-done.9.refs_1_.refs_13_ = bf16[2,256,128]{2,1,0:T(8,128)(2,1)S(1)} collective-permute-done((bf16[2,256,128]{2,1,0:T(8,128)(2,1)S(1)}, bf16[2,256,128]{2,1,0:T(8,128)(2,1)S(1)}, u32[]{:S(2)}, u32[]{:S(2)}) %collective-permute-start.9) | collective-permute-done | bytes 131104 | tf_op jit(solution)/shard_map/ppermute | solution.py:396
  33.0 0.4 %finish.5.refs_13_ = bf16[4,128,512]{2,1,0:T(8,128)(2,1)S(1)} custom-call(bf16[128,2048]{1,0:T(8,128)(2,1)S(1)} %get-tuple-element.53.refs_0_, bf16[128,2048]{1,0:T(8,128)(2,1)S(1)} %get-tuple-element.54.refs_1_, bf16[128,2048]{1,0:T(8,128)(2,1)S(1)} %get-tuple-element.55.refs_2_, bf16[128,2048]{1,0:T(8,128)(2,1)S(1)} %get-tuple-element.56.refs_3_, ...), custom_call_target="tpu_custom_call" | custom-call | flops 67108864 | bytes 2097152 | tf_op jit(solution)/shard_map/finish/pallas_call | solution.py:378
  33.5 0.9 %finish.6 = (bf16[128,2048]{1,0:T(8,128)(2,1)}, bf16[128,2048]{1,0:T(8,128)(2,1)}, bf16[128,2048]{1,0:T(8,128)(2,1)}, bf16[128,2048]{1,0:T(8,128)(2,1)}, bf16[4,128,512]{2,1,0:T(8,128)(2,1)S(1)}) custom-call(bf16[128,2048]{1,0:T(8,128)(2,1)S(1)} %get-tuple-element.53.refs_0_, ...), custom_call_target="tpu_custom_call", output_to_operand_aliasing={{0}: (14, {}), {1}: (15, {}), {2}: (16, {}), {3}: (17, {})} | custom-call | flops 67108864 | bytes 2097152 | tf_op jit(solution)/shard_map/finish/pallas_call | solution.py:378
  34.5 1.2 %finish.7 = (bf16[128,2048]{1,0:T(8,128)(2,1)}, bf16[128,2048]{1,0:T(8,128)(2,1)}, bf16[128,2048]{1,0:T(8,128)(2,1)}, bf16[128,2048]{1,0:T(8,128)(2,1)}) custom-call(bf16[128,2048]{1,0:T(8,128)(2,1)S(1)} %get-tuple-element.53.refs_0_, ...), custom_call_target="tpu_custom_call", output_to_operand_aliasing={{0}: (14, {}), {1}: (15, {}), {2}: (16, {}), {3}: (17, {})} | custom-call | flops 67108864 | bytes 2097152 | tf_op jit(solution)/shard_map/finish/pallas_call | solution.py:378
  (17 shorter events, 0.8 us)
Async XLA Ops:
  2.4 2.6 %collective-permute-start = (bf16[2,512,128]{2,1,0:T(8,128)(2,1)S(1)}, bf16[2,512,128]{2,1,0:T(8,128)(2,1)S(1)}, u32[]{:S(2)}, u32[]{:S(2)}) collective-permute-start(bf16[2,512,128]{2,1,0:T(8,128)(2,1)S(1)} %get-tuple-element.63), channel_id=1, source_target_pairs={{0,1},{1,0},{2,3},{3,2},{4,5},{5,4},{6,7},{7,6},{8,9},{9,8},{10,11... | collective-permute-start | bytes 786440 | tf_op jit(solution)/shard_map/ppermute | solution.py:396
  3.2 4.9 %collective-permute-start.2 = (bf16[2,512,128]{2,1,0:T(8,128)(2,1)S(1)}, bf16[2,512,128]{2,1,0:T(8,128)(2,1)S(1)}, u32[]{:S(2)}, u32[]{:S(2)}) collective-permute-start(bf16[2,512,128]{2,1,0:T(8,128)(2,1)S(1)} %sums.3), channel_id=1, source_target_pairs={{0,1},{1,0},{2,3},{3,2},{4,5},{5,4},{6,7},{7,6},{8,9},{9,8},{10,11... | collective-permute-start | bytes 786440 | tf_op jit(solution)/shard_map/ppermute | solution.py:396
  5.1 6.8 %collective-permute-start.1 = (bf16[2,256,128]{2,1,0:T(8,128)(2,1)S(1)}, bf16[2,256,128]{2,1,0:T(8,128)(2,1)S(1)}, u32[]{:S(2)}, u32[]{:S(2)}) collective-permute-start(bf16[2,256,128]{2,1,0:T(8,128)(2,1)S(1)} %get-tuple-element.65), channel_id=1, source_target_pairs={{0,2},{1,3},{2,0},{3,1},{4,6},{5,7},{6,4},{7,5},{8,10},{9,11},{10,... | collective-permute-start | bytes 393224 | tf_op jit(solution)/shard_map/ppermute | solution.py:396
  8.2 7.8 %collective-permute-start.3 = (bf16[2,256,128]{2,1,0:T(8,128)(2,1)S(1)}, bf16[2,256,128]{2,1,0:T(8,128)(2,1)S(1)}, u32[]{:S(2)}, u32[]{:S(2)}) collective-permute-start(bf16[2,256,128]{2,1,0:T(8,128)(2,1)S(1)} %get-tuple-element.66), channel_id=1, source_target_pairs={{0,4},{1,5},{2,6},{3,7},{4,0},{5,1},{6,2},{7,3},{8,12},{9,13},{10,... | collective-permute-start | bytes 393224 | tf_op jit(solution)/shard_map/ppermute | solution.py:396
  9.8 6.3 %collective-permute-start.4 = (bf16[2,256,128]{2,1,0:T(8,128)(2,1)S(1)}, bf16[2,256,128]{2,1,0:T(8,128)(2,1)S(1)}, u32[]{:S(2)}, u32[]{:S(2)}) collective-permute-start(bf16[2,256,128]{2,1,0:T(8,128)(2,1)S(1)} %get-tuple-element.67.refs_4_), channel_id=1, source_target_pairs={{0,6},{1,7},{2,4},{3,5},{4,2},{5,3},{6,0},{7,1},{8,14},{9,15},{10,... | collective-permute-start | bytes 393224 | tf_op jit(solution)/shard_map/ppermute | solution.py:396
  16.1 6.5 %collective-permute-start.5 = (bf16[256,128]{1,0:T(8,128)(2,1)S(1)}, bf16[256,128]{1,0:T(8,128)(2,1)S(1)}, u32[]{:S(2)}, u32[]{:S(2)}) collective-permute-start(bf16[256,128]{1,0:T(8,128)(2,1)S(1)} %get-tuple-element.80), channel_id=1, source_target_pairs={{0,24},{8,16},{16,8},{24,0},{1,25},{9,17},{17,9},{25,1},{2,26},{10... | collective-permute-start | bytes 196616 | tf_op jit(solution)/shard_map/ppermute | solution.py:396
  19.8 5.2 %collective-permute-start.6 = (bf16[256,128]{1,0:T(8,128)(2,1)S(1)}, bf16[256,128]{1,0:T(8,128)(2,1)S(1)}, u32[]{:S(2)}, u32[]{:S(2)}) collective-permute-start(bf16[256,128]{1,0:T(8,128)(2,1)S(1)} %get-tuple-element.81), channel_id=1, source_target_pairs={{0,16},{8,24},{16,0},{24,8},{1,17},{9,25},{17,1},{25,9},{2,18},{10... | collective-permute-start | bytes 196616 | tf_op jit(solution)/shard_map/ppermute | solution.py:396
  19.8 5.2 %collective-permute-start.7 = (bf16[256,128]{1,0:T(8,128)(2,1)S(1)}, bf16[256,128]{1,0:T(8,128)(2,1)S(1)}, u32[]{:S(2)}, u32[]{:S(2)}) collective-permute-start(bf16[256,128]{1,0:T(8,128)(2,1)S(1)} %get-tuple-element.82), channel_id=1, source_target_pairs={{0,8},{8,0},{16,24},{24,16},{1,9},{9,1},{17,25},{25,17},{2,10},{10... | collective-permute-start | bytes 196616 | tf_op jit(solution)/shard_map/ppermute | solution.py:396
  25.2 5.9 %collective-permute-start.10 = (bf16[2,256,128]{2,1,0:T(8,128)(2,1)S(1)}, bf16[2,256,128]{2,1,0:T(8,128)(2,1)S(1)}, u32[]{:S(2)}, u32[]{:S(2)}) collective-permute-start(bf16[2,256,128]{2,1,0:T(8,128)(2,1)S(1)} %get-tuple-element.86), channel_id=1, source_target_pairs={{0,2},{1,3},{2,0},{3,1},{4,6},{5,7},{6,4},{7,5},{8,10},{9,11},{10,... | collective-permute-start | bytes 393224 | tf_op jit(solution)/shard_map/ppermute | solution.py:396
  26.1 6.3 %collective-permute-start.8 = (bf16[2,256,128]{2,1,0:T(8,128)(2,1)S(1)}, bf16[2,256,128]{2,1,0:T(8,128)(2,1)S(1)}, u32[]{:S(2)}, u32[]{:S(2)}) collective-permute-start(bf16[2,256,128]{2,1,0:T(8,128)(2,1)S(1)} %get-tuple-element.83), channel_id=1, source_target_pairs={{0,4},{1,5},{2,6},{3,7},{4,0},{5,1},{6,2},{7,3},{8,12},{9,13},{10,... | collective-permute-start | bytes 393224 | tf_op jit(solution)/shard_map/ppermute | solution.py:396
  26.9 5.9 %collective-permute-start.9 = (bf16[2,256,128]{2,1,0:T(8,128)(2,1)S(1)}, bf16[2,256,128]{2,1,0:T(8,128)(2,1)S(1)}, u32[]{:S(2)}, u32[]{:S(2)}) collective-permute-start(bf16[2,256,128]{2,1,0:T(8,128)(2,1)S(1)} %get-tuple-element.84), channel_id=1, source_target_pairs={{0,6},{1,7},{2,4},{3,5},{4,2},{5,3},{6,0},{7,1},{8,14},{9,15},{10,... | collective-permute-start | bytes 393224 | tf_op jit(solution)/shard_map/ppermute | solution.py:396
  31.1 2.3 %collective-permute-start.12 = (bf16[2,512,128]{2,1,0:T(8,128)(2,1)S(1)}, bf16[2,512,128]{2,1,0:T(8,128)(2,1)S(1)}, u32[]{:S(2)}, u32[]{:S(2)}) collective-permute-start(bf16[2,512,128]{2,1,0:T(8,128)(2,1)S(1)} %theirs.3), channel_id=1, source_target_pairs={{0,1},{1,0},{2,3},{3,2},{4,5},{5,4},{6,7},{7,6},{8,9},{9,8},{10,11... | collective-permute-start | bytes 786440 | tf_op jit(solution)/shard_map/ppermute | solution.py:396
  32.9 1.6 %collective-permute-start.11 = (bf16[2,512,128]{2,1,0:T(8,128)(2,1)S(1)}, bf16[2,512,128]{2,1,0:T(8,128)(2,1)S(1)}, u32[]{:S(2)}, u32[]{:S(2)}) collective-permute-start(bf16[2,512,128]{2,1,0:T(8,128)(2,1)S(1)} %theirs.2), channel_id=1, source_target_pairs={{0,1},{1,0},{2,3},{3,2},{4,5},{5,4},{6,7},{7,6},{8,9},{9,8},{10,11... | collective-permute-start | bytes 786440 | tf_op jit(solution)/shard_map/ppermute | solution.py:396

commit v29 on v23

--- a/solution.py
+++ b/solution.py
@@ -28,7 +28,7 @@
 
 
 def distances(outer_count):
-    return range(outer_count - 1, 0, -1)
+    return [outer_count - 1, *range(1, outer_count - 1)]
 
 
 def block_start(own, block, half):

time: 35.6 us -> 35.6 us (level)
  transfers between devices with their start and end apart: 13 -> 13, of which waited for: 7 -> 8; matrix products, arithmetic and copies ran while one was open for 0% -> 0% of each run, Pallas kernels for 16% -> 16%
where the time goes in v29:
time: 35.6 us; the launch traced here: 35.5 us
  starting transfers between devices  13.6 us (38%)
  waiting for transfers between devices  12.3 us (35%)
  Pallas kernels  8.71 us (24%)
  between operations  0.79 us (2%)
    ppermute x13, starting transfers between devices, swap(): lax.ppermute(x, axis, [(i, i ^ bits) for i in range(lax.axis_size(axis))])  13.6 us
    ppermute x13, waiting for transfers between devices, swap(): lax.ppermute(x, axis, [(i, i ^ bits) for i in range(lax.axis_size(axis))])  12.3 us
    pallas_call x4, Pallas kernels, finish(): pl.pallas_call(functools.partial(finish_kernel, scale, own, block, len(sl...  3.69 us
    pallas_call x1, Pallas kernels, local_part(): pl.pallas_call(local_kernel, name='local', in_specs=[VMEM] * 4, out_specs...  2.16 us
    pallas_call x1, Pallas kernels, first_sums(): pl.pallas_call(give_kernel, name='first_sums', in_specs=[ANY] * 4, out_sp...  1.59 us
    pallas_call x2, Pallas kernels, sums(): pl.pallas_call(functools.partial(sums_kernel, wanted), name='sums', in_sp...  0.77 us
  transfers between devices with their start and end apart: 13, of which 8 were waited for; matrix products, arithmetic and copies ran while one was open for 0% of the time, Pallas kernels for 16%

profile of v29, /device:TPU:0, one launch (start us, length us, event | category | flops | bytes accessed | tf_op | source)
XLA Modules:
  0.0 35.5 jit_solution(4700449016908592437)
XLA Ops:
  0.7 1.6 %first_sums.1 = bf16[2,512,128]{2,1,0:T(8,128)(2,1)S(1)} custom-call(bf16[128,2048]{1,0:T(8,128)(2,1)} %refs_0_.15, bf16[128,2048]{1,0:T(8,128)(2,1)} %refs_1_.15, bf16[128,2048]{1,0:T(8,128)(2,1)} %refs_2_.15, bf16[128,2048]{1,0:T(8,128)(2,1)} %refs_3_.15), custom_call_target="tpu_custom_call" | custom-call | flops 33554432 | bytes 786432 | tf_op jit(solution)/shard_map/first_sums/pallas_call | solution.py:95
  2.3 0.5 %collective-permute-start = (bf16[2,512,128]{2,1,0:T(8,128)(2,1)S(1)}, bf16[2,512,128]{2,1,0:T(8,128)(2,1)S(1)}, u32[]{:S(2)}, u32[]{:S(2)}) collective-permute-start(bf16[2,512,128]{2,1,0:T(8,128)(2,1)S(1)} %first_sums.1), channel_id=1, source_target_pairs={{0,1},{1,0},{2,3},{3,2},{4,5},{5,4},{6,7},{7,6},{8,9},{9,8},{10,11... | collective-permute-start | bytes 786440 | tf_op jit(solution)/shard_map/ppermute | solution.py:386
  2.8 0.3 sums.3
  3.2 0.5 %sums.2 = (bf16[2,512,128]{2,1,0:T(8,128)(2,1)S(1)}, bf16[2,512,128]{2,1,0:T(8,128)(2,1)S(1)}) custom-call(bf16[128,2048]{1,0:T(8,128)(2,1)S(1)} %copy-done, bf16[128,2048]{1,0:T(8,128)(2,1)S(1)} %copy-done.1, bf16[128,2048]{1,0:T(8,128)(2,1)S(1)} %copy-done.2, bf16[128,2048]{1,0:T(8,128)(2,1)S(1)} %copy-done.3), custom_call_target="tpu_custom_call" | custom-call | flops 67108864 | bytes 1572864 | tf_op jit(solution)/shard_map/sums/pallas_call | solution.py:116
  3.7 0.2 collective-permute-done.got_ref.refs_10_
  4.0 2.9 %collective-permute-start.1 = (bf16[2,256,128]{2,1,0:T(8,128)(2,1)S(1)}, bf16[2,256,128]{2,1,0:T(8,128)(2,1)S(1)}, u32[]{:S(2)}, u32[]{:S(2)}) collective-permute-start(bf16[2,256,128]{2,1,0:T(8,128)(2,1)S(1)} %get-tuple-element.46), channel_id=1, source_target_pairs={{0,2},{1,3},{2,0},{3,1},{4,6},{5,7},{6,4},{7,5},{8,10},{9,11},{10,... | collective-permute-start | bytes 393224 | tf_op jit(solution)/shard_map/ppermute | solution.py:386
  7.0 1.6 %collective-permute-start.3 = (bf16[2,256,128]{2,1,0:T(8,128)(2,1)S(1)}, bf16[2,256,128]{2,1,0:T(8,128)(2,1)S(1)}, u32[]{:S(2)}, u32[]{:S(2)}) collective-permute-start(bf16[2,256,128]{2,1,0:T(8,128)(2,1)S(1)} %get-tuple-element.48), channel_id=1, source_target_pairs={{0,4},{1,5},{2,6},{3,7},{4,0},{5,1},{6,2},{7,3},{8,12},{9,13},{10,... | collective-permute-start | bytes 393224 | tf_op jit(solution)/shard_map/ppermute | solution.py:386
  8.6 0.3 collective-permute-start.4
  8.9 2.2 %local.1 = (f32[128,2048]{1,0:T(8,128)S(1)}, f32[128,2048]{1,0:T(8,128)S(1)}, f32[128,2048]{1,0:T(8,128)S(1)}, f32[128,2048]{1,0:T(8,128)S(1)}) custom-call(bf16[128,2048]{1,0:T(8,128)(2,1)S(1)} %copy-done, bf16[128,2048]{1,0:T(8,128)(2,1)S(1)} %copy-done.1, bf16[128,2048]{1,0:T(8,128)(2,1)S(1)} %copy-done.2, bf16[128,2048]{1,0:T(8,128)(2,1)S(1)} %copy-done.3), custom_call_target="tpu_custom_call" | custom-call | flops 402653184 | bytes 6291456 | tf_op jit(solution)/shard_map/local/pallas_call | solution.py:274
  11.1 4.0 %collective-permute-done.3.refs_2_ = bf16[2,256,128]{2,1,0:T(8,128)(2,1)S(1)} collective-permute-done((bf16[2,256,128]{2,1,0:T(8,128)(2,1)S(1)}, bf16[2,256,128]{2,1,0:T(8,128)(2,1)S(1)}, u32[]{:S(2)}, u32[]{:S(2)}) %collective-permute-start.3) | collective-permute-done | bytes 131104 | tf_op jit(solution)/shard_map/ppermute | solution.py:386
  15.2 3.7 %collective-permute-start.5 = (bf16[256,128]{1,0:T(8,128)(2,1)S(1)}, bf16[256,128]{1,0:T(8,128)(2,1)S(1)}, u32[]{:S(2)}, u32[]{:S(2)}) collective-permute-start(bf16[256,128]{1,0:T(8,128)(2,1)S(1)} %get-tuple-element.62), channel_id=1, source_target_pairs={{0,24},{8,16},{16,8},{24,0},{1,25},{9,17},{17,9},{25,1},{2,26},{10... | collective-permute-start | bytes 196616 | tf_op jit(solution)/shard_map/ppermute | solution.py:386
  18.9 0.8 %collective-permute-start.7 = (bf16[256,128]{1,0:T(8,128)(2,1)S(1)}, bf16[256,128]{1,0:T(8,128)(2,1)S(1)}, u32[]{:S(2)}, u32[]{:S(2)}) collective-permute-start(bf16[256,128]{1,0:T(8,128)(2,1)S(1)} %get-tuple-element.64), channel_id=1, source_target_pairs={{0,16},{8,24},{16,0},{24,8},{1,17},{9,25},{17,1},{25,9},{2,18},{10... | collective-permute-start | bytes 196616 | tf_op jit(solution)/shard_map/ppermute | solution.py:386
  19.7 1.7 %collective-permute-done.5.refs_4_ = bf16[256,128]{1,0:T(8,128)(2,1)S(1)} collective-permute-done((bf16[256,128]{1,0:T(8,128)(2,1)S(1)}, bf16[256,128]{1,0:T(8,128)(2,1)S(1)}, u32[]{:S(2)}, u32[]{:S(2)}) %collective-permute-start.5) | collective-permute-done | bytes 65568 | tf_op jit(solution)/shard_map/ppermute | solution.py:386
  21.4 1.7 %collective-permute-done.6.refs_5_ = bf16[256,128]{1,0:T(8,128)(2,1)S(1)} collective-permute-done((bf16[256,128]{1,0:T(8,128)(2,1)S(1)}, bf16[256,128]{1,0:T(8,128)(2,1)S(1)}, u32[]{:S(2)}, u32[]{:S(2)}) %collective-permute-start.6) | collective-permute-done | bytes 65568 | tf_op jit(solution)/shard_map/ppermute | solution.py:386
  23.2 0.9 %collective-permute-done.7.refs_6_ = bf16[256,128]{1,0:T(8,128)(2,1)S(1)} collective-permute-done((bf16[256,128]{1,0:T(8,128)(2,1)S(1)}, bf16[256,128]{1,0:T(8,128)(2,1)S(1)}, u32[]{:S(2)}, u32[]{:S(2)}) %collective-permute-start.7) | collective-permute-done | bytes 65568 | tf_op jit(solution)/shard_map/ppermute | solution.py:386
  24.3 1.2 %collective-permute-start.10 = (bf16[2,256,128]{2,1,0:T(8,128)(2,1)S(1)}, bf16[2,256,128]{2,1,0:T(8,128)(2,1)S(1)}, u32[]{:S(2)}, u32[]{:S(2)}) collective-permute-start(bf16[2,256,128]{2,1,0:T(8,128)(2,1)S(1)} %get-tuple-element.68), channel_id=1, source_target_pairs={{0,2},{1,3},{2,0},{3,1},{4,6},{5,7},{6,4},{7,5},{8,10},{9,11},{10,... | collective-permute-start | bytes 393224 | tf_op jit(solution)/shard_map/ppermute | solution.py:386
  25.5 1.3 %collective-permute-start.8 = (bf16[2,256,128]{2,1,0:T(8,128)(2,1)S(1)}, bf16[2,256,128]{2,1,0:T(8,128)(2,1)S(1)}, u32[]{:S(2)}, u32[]{:S(2)}) collective-permute-start(bf16[2,256,128]{2,1,0:T(8,128)(2,1)S(1)} %get-tuple-element.65), channel_id=1, source_target_pairs={{0,4},{1,5},{2,6},{3,7},{4,0},{5,1},{6,2},{7,3},{8,12},{9,13},{10,... | collective-permute-start | bytes 393224 | tf_op jit(solution)/shard_map/ppermute | solution.py:386
  26.8 1.1 %collective-permute-start.9 = (bf16[2,256,128]{2,1,0:T(8,128)(2,1)S(1)}, bf16[2,256,128]{2,1,0:T(8,128)(2,1)S(1)}, u32[]{:S(2)}, u32[]{:S(2)}) collective-permute-start(bf16[2,256,128]{2,1,0:T(8,128)(2,1)S(1)} %get-tuple-element.66), channel_id=1, source_target_pairs={{0,6},{1,7},{2,4},{3,5},{4,2},{5,3},{6,0},{7,1},{8,14},{9,15},{10,... | collective-permute-start | bytes 393224 | tf_op jit(solution)/shard_map/ppermute | solution.py:386
  27.8 2.7 %collective-permute-done.10.refs_9_.refs_1_ = bf16[2,256,128]{2,1,0:T(8,128)(2,1)S(1)} collective-permute-done((bf16[2,256,128]{2,1,0:T(8,128)(2,1)S(1)}, bf16[2,256,128]{2,1,0:T(8,128)(2,1)S(1)}, u32[]{:S(2)}, u32[]{:S(2)}) %collective-permute-start.10) | collective-permute-done | bytes 131104 | tf_op jit(solution)/shard_map/ppermute | solution.py:386
  30.7 1.2 %finish.4 = (bf16[128,2048]{1,0:T(8,128)(2,1)}, bf16[128,2048]{1,0:T(8,128)(2,1)}, bf16[128,2048]{1,0:T(8,128)(2,1)}, bf16[128,2048]{1,0:T(8,128)(2,1)}) custom-call(bf16[128,2048]{1,0:T(8,128)(2,1)S(1)} %copy-done, bf16[128,2048]{1,0:T(8,128)(2,1)S(1)} %copy-done.1, bf16[128,2048]{1,0:T(8,128)(2,1)S(1)} %copy-done.2, bf16[128,2048]{1,0:T(8,128)(2,1)S(1)} %copy-done.3, ...), custom_call_target="tpu_custom_call" | custom-call | flops 67108864 | bytes 2097152 | tf_op jit(solution)/shard_map/finish/pallas_call | solution.py:368
  31.9 0.8 %collective-permute-done.9.refs_1_.refs_9_ = bf16[2,256,128]{2,1,0:T(8,128)(2,1)S(1)} collective-permute-done((bf16[2,256,128]{2,1,0:T(8,128)(2,1)S(1)}, bf16[2,256,128]{2,1,0:T(8,128)(2,1)S(1)}, u32[]{:S(2)}, u32[]{:S(2)}) %collective-permute-start.9) | collective-permute-done | bytes 131104 | tf_op jit(solution)/shard_map/ppermute | solution.py:386
  32.8 0.4 %finish.5.refs_9_ = bf16[4,128,512]{2,1,0:T(8,128)(2,1)S(1)} custom-call(bf16[128,2048]{1,0:T(8,128)(2,1)S(1)} %copy-done, bf16[128,2048]{1,0:T(8,128)(2,1)S(1)} %copy-done.1, bf16[128,2048]{1,0:T(8,128)(2,1)S(1)} %copy-done.2, bf16[128,2048]{1,0:T(8,128)(2,1)S(1)} %copy-done.3, f32[128,2048]{1,0:T(8,128)S(1)} %get-tuple-element.54.refs_4_, ...), custom_call_target="tpu_custom_call" | custom-call | flops 67108864 | bytes 2097152 | tf_op jit(solution)/shard_map/finish/pallas_call | solution.py:368
  33.2 0.9 %finish.6 = (bf16[128,2048]{1,0:T(8,128)(2,1)}, bf16[128,2048]{1,0:T(8,128)(2,1)}, bf16[128,2048]{1,0:T(8,128)(2,1)}, bf16[128,2048]{1,0:T(8,128)(2,1)}, bf16[4,128,512]{2,1,0:T(8,128)(2,1)S(1)}) custom-call(bf16[128,2048]{1,0:T(8,128)(2,1)S(1)} %copy-done, ...), custom_call_target="tpu_custom_call", output_to_operand_aliasing={{0}: (10, {}), {1}: (11, {}), {2}: (12, {}), {3}: (13, {})} | custom-call | flops 67108864 | bytes 2097152 | tf_op jit(solution)/shard_map/finish/pallas_call | solution.py:368
  34.3 1.2 %finish.7 = (bf16[128,2048]{1,0:T(8,128)(2,1)}, bf16[128,2048]{1,0:T(8,128)(2,1)}, bf16[128,2048]{1,0:T(8,128)(2,1)}, bf16[128,2048]{1,0:T(8,128)(2,1)}) custom-call(bf16[128,2048]{1,0:T(8,128)(2,1)S(1)} %copy-done, bf16[128,2048]{1,0:T(8,128)(2,1)S(1)} %copy-done.1, ...), custom_call_target="tpu_custom_call", output_to_operand_aliasing={{0}: (10, {}), {1}: (11, {}), {2}: (12, {}), {3}: (13, {})} | custom-call | flops 67108864 | bytes 2097152 | tf_op jit(solution)/shard_map/finish/pallas_call | solution.py:368
  (24 shorter events, 1.0 us)
Async XLA Ops:
  0.6 2.2 %copy-start.3 = (bf16[128,2048]{1,0:T(8,128)(2,1)S(1)}, bf16[128,2048]{1,0:T(8,128)(2,1)}, u32[]{:S(2)}) copy-start(bf16[128,2048]{1,0:T(8,128)(2,1)} %refs_3_.15) | copy-start | bytes 1572868
  0.6 2.1 %copy-start.2 = (bf16[128,2048]{1,0:T(8,128)(2,1)S(1)}, bf16[128,2048]{1,0:T(8,128)(2,1)}, u32[]{:S(2)}) copy-start(bf16[128,2048]{1,0:T(8,128)(2,1)} %refs_2_.15) | copy-start | bytes 1572868
  0.7 2.1 %copy-start.1 = (bf16[128,2048]{1,0:T(8,128)(2,1)S(1)}, bf16[128,2048]{1,0:T(8,128)(2,1)}, u32[]{:S(2)}) copy-start(bf16[128,2048]{1,0:T(8,128)(2,1)} %refs_1_.15) | copy-start | bytes 1572868
  0.7 2.1 %copy-start = (bf16[128,2048]{1,0:T(8,128)(2,1)S(1)}, bf16[128,2048]{1,0:T(8,128)(2,1)}, u32[]{:S(2)}) copy-start(bf16[128,2048]{1,0:T(8,128)(2,1)} %refs_0_.15) | copy-start | bytes 1572868
  2.3 1.7 %collective-permute-start = (bf16[2,512,128]{2,1,0:T(8,128)(2,1)S(1)}, bf16[2,512,128]{2,1,0:T(8,128)(2,1)S(1)}, u32[]{:S(2)}, u32[]{:S(2)}) collective-permute-start(bf16[2,512,128]{2,1,0:T(8,128)(2,1)S(1)} %first_sums.1), channel_id=1, source_target_pairs={{0,1},{1,0},{2,3},{3,2},{4,5},{5,4},{6,7},{7,6},{8,9},{9,8},{10,11... | collective-permute-start | bytes 786440 | tf_op jit(solution)/shard_map/ppermute | solution.py:386
  3.1 3.8 %collective-permute-start.2 = (bf16[2,512,128]{2,1,0:T(8,128)(2,1)S(1)}, bf16[2,512,128]{2,1,0:T(8,128)(2,1)S(1)}, u32[]{:S(2)}, u32[]{:S(2)}) collective-permute-start(bf16[2,512,128]{2,1,0:T(8,128)(2,1)S(1)} %sums.3), channel_id=1, source_target_pairs={{0,1},{1,0},{2,3},{3,2},{4,5},{5,4},{6,7},{7,6},{8,9},{9,8},{10,11... | collective-permute-start | bytes 786440 | tf_op jit(solution)/shard_map/ppermute | solution.py:386
  4.0 7.1 %collective-permute-start.1 = (bf16[2,256,128]{2,1,0:T(8,128)(2,1)S(1)}, bf16[2,256,128]{2,1,0:T(8,128)(2,1)S(1)}, u32[]{:S(2)}, u32[]{:S(2)}) collective-permute-start(bf16[2,256,128]{2,1,0:T(8,128)(2,1)S(1)} %get-tuple-element.46), channel_id=1, source_target_pairs={{0,2},{1,3},{2,0},{3,1},{4,6},{5,7},{6,4},{7,5},{8,10},{9,11},{10,... | collective-permute-start | bytes 393224 | tf_op jit(solution)/shard_map/ppermute | solution.py:386
  7.0 8.1 %collective-permute-start.3 = (bf16[2,256,128]{2,1,0:T(8,128)(2,1)S(1)}, bf16[2,256,128]{2,1,0:T(8,128)(2,1)S(1)}, u32[]{:S(2)}, u32[]{:S(2)}) collective-permute-start(bf16[2,256,128]{2,1,0:T(8,128)(2,1)S(1)} %get-tuple-element.48), channel_id=1, source_target_pairs={{0,4},{1,5},{2,6},{3,7},{4,0},{5,1},{6,2},{7,3},{8,12},{9,13},{10,... | collective-permute-start | bytes 393224 | tf_op jit(solution)/shard_map/ppermute | solution.py:386
  8.6 6.6 %collective-permute-start.4 = (bf16[2,256,128]{2,1,0:T(8,128)(2,1)S(1)}, bf16[2,256,128]{2,1,0:T(8,128)(2,1)S(1)}, u32[]{:S(2)}, u32[]{:S(2)}) collective-permute-start(bf16[2,256,128]{2,1,0:T(8,128)(2,1)S(1)} %get-tuple-element.49), channel_id=1, source_target_pairs={{0,6},{1,7},{2,4},{3,5},{4,2},{5,3},{6,0},{7,1},{8,14},{9,15},{10,... | collective-permute-start | bytes 393224 | tf_op jit(solution)/shard_map/ppermute | solution.py:386
  15.2 6.2 %collective-permute-start.5 = (bf16[256,128]{1,0:T(8,128)(2,1)S(1)}, bf16[256,128]{1,0:T(8,128)(2,1)S(1)}, u32[]{:S(2)}, u32[]{:S(2)}) collective-permute-start(bf16[256,128]{1,0:T(8,128)(2,1)S(1)} %get-tuple-element.62), channel_id=1, source_target_pairs={{0,24},{8,16},{16,8},{24,0},{1,25},{9,17},{17,9},{25,1},{2,26},{10... | collective-permute-start | bytes 196616 | tf_op jit(solution)/shard_map/ppermute | solution.py:386
  18.9 4.3 %collective-permute-start.6 = (bf16[256,128]{1,0:T(8,128)(2,1)S(1)}, bf16[256,128]{1,0:T(8,128)(2,1)S(1)}, u32[]{:S(2)}, u32[]{:S(2)}) collective-permute-start(bf16[256,128]{1,0:T(8,128)(2,1)S(1)} %get-tuple-element.63), channel_id=1, source_target_pairs={{0,8},{8,0},{16,24},{24,16},{1,9},{9,1},{17,25},{25,17},{2,10},{10... | collective-permute-start | bytes 196616 | tf_op jit(solution)/shard_map/ppermute | solution.py:386
  18.9 5.2 %collective-permute-start.7 = (bf16[256,128]{1,0:T(8,128)(2,1)S(1)}, bf16[256,128]{1,0:T(8,128)(2,1)S(1)}, u32[]{:S(2)}, u32[]{:S(2)}) collective-permute-start(bf16[256,128]{1,0:T(8,128)(2,1)S(1)} %get-tuple-element.64), channel_id=1, source_target_pairs={{0,16},{8,24},{16,0},{24,8},{1,17},{9,25},{17,1},{25,9},{2,18},{10... | collective-permute-start | bytes 196616 | tf_op jit(solution)/shard_map/ppermute | solution.py:386
  24.3 6.2 %collective-permute-start.10 = (bf16[2,256,128]{2,1,0:T(8,128)(2,1)S(1)}, bf16[2,256,128]{2,1,0:T(8,128)(2,1)S(1)}, u32[]{:S(2)}, u32[]{:S(2)}) collective-permute-start(bf16[2,256,128]{2,1,0:T(8,128)(2,1)S(1)} %get-tuple-element.68), channel_id=1, source_target_pairs={{0,2},{1,3},{2,0},{3,1},{4,6},{5,7},{6,4},{7,5},{8,10},{9,11},{10,... | collective-permute-start | bytes 393224 | tf_op jit(solution)/shard_map/ppermute | solution.py:386
  25.5 6.4 %collective-permute-start.8 = (bf16[2,256,128]{2,1,0:T(8,128)(2,1)S(1)}, bf16[2,256,128]{2,1,0:T(8,128)(2,1)S(1)}, u32[]{:S(2)}, u32[]{:S(2)}) collective-permute-start(bf16[2,256,128]{2,1,0:T(8,128)(2,1)S(1)} %get-tuple-element.65), channel_id=1, source_target_pairs={{0,4},{1,5},{2,6},{3,7},{4,0},{5,1},{6,2},{7,3},{8,12},{9,13},{10,... | collective-permute-start | bytes 393224 | tf_op jit(solution)/shard_map/ppermute | solution.py:386
  26.8 5.9 %collective-permute-start.9 = (bf16[2,256,128]{2,1,0:T(8,128)(2,1)S(1)}, bf16[2,256,128]{2,1,0:T(8,128)(2,1)S(1)}, u32[]{:S(2)}, u32[]{:S(2)}) collective-permute-start(bf16[2,256,128]{2,1,0:T(8,128)(2,1)S(1)} %get-tuple-element.66), channel_id=1, source_target_pairs={{0,6},{1,7},{2,4},{3,5},{4,2},{5,3},{6,0},{7,1},{8,14},{9,15},{10,... | collective-permute-start | bytes 393224 | tf_op jit(solution)/shard_map/ppermute | solution.py:386
  30.6 2.6 %collective-permute-start.12 = (bf16[2,512,128]{2,1,0:T(8,128)(2,1)S(1)}, bf16[2,512,128]{2,1,0:T(8,128)(2,1)S(1)}, u32[]{:S(2)}, u32[]{:S(2)}) collective-permute-start(bf16[2,512,128]{2,1,0:T(8,128)(2,1)S(1)} %theirs.3), channel_id=1, source_target_pairs={{0,1},{1,0},{2,3},{3,2},{4,5},{5,4},{6,7},{7,6},{8,9},{9,8},{10,11... | collective-permute-start | bytes 786440 | tf_op jit(solution)/shard_map/ppermute | solution.py:386
  32.7 1.6 %collective-permute-start.11 = (bf16[2,512,128]{2,1,0:T(8,128)(2,1)S(1)}, bf16[2,512,128]{2,1,0:T(8,128)(2,1)S(1)}, u32[]{:S(2)}, u32[]{:S(2)}) collective-permute-start(bf16[2,512,128]{2,1,0:T(8,128)(2,1)S(1)} %theirs.2), channel_id=1, source_target_pairs={{0,1},{1,0},{2,3},{3,2},{4,5},{5,4},{6,7},{7,6},{8,9},{9,8},{10,11... | collective-permute-start | bytes 786440 | tf_op jit(solution)/shard_map/ppermute | solution.py:386

commit v30 on v29

--- a/solution.py
+++ b/solution.py
@@ -31,10 +31,21 @@
     return [outer_count - 1, *range(1, outer_count - 1)]
 
 
+def exchanged(bits):
+    return bits ^ 3 if bits & 3 in (1, 2) and lax.axis_size("inner") > 4 else bits
+
+
+def place():
+    _, far = near_far()
+    if lax.axis_size("inner") <= 4:
+        return far
+    return far + lax.rem(far, 2) - lax.rem(lax.div(far, 2), 2)
+
+
 def block_start(own, block, half):
-    near, far = near_far()
+    near, _ = near_far()
     side = near if own else 1 - near
-    top = lax.div(far, lax.axis_size("inner") // 4)
+    top = lax.div(place(), lax.axis_size("inner") // 4)
     return side * half + (1 - top if block else top) * (half // 2)
 
 
@@ -43,8 +54,7 @@
 
 
 def slot_rows(s, count, depth):
-    _, far = near_far()
-    return pl.ds(pl.multiple_of(lax.rem(far ^ s, count) * depth, depth), depth)
+    return pl.ds(pl.multiple_of(lax.rem(place() ^ s, count) * depth, depth), depth)
 
 
 def one_ahead(products, use):
@@ -180,7 +190,7 @@
     outer = lax.axis_index("outer")
     _, far = near_far()
     for s, slot in enumerate(slots):
-        held[far ^ s] = slot[...]
+        held[far ^ exchanged(s)] = slot[...]
     for which in range(2):
         total = jnp.zeros(held.shape[2:], F32)
         for s, other in zip(distances(len(others) + 1), others):
@@ -191,7 +201,7 @@
             scanned[i, which] = total.astype(BF16)
             total += held[i, which].astype(F32)
     for s, out in enumerate(outs):
-        out[...] = scanned[far ^ s]
+        out[...] = scanned[far ^ exchanged(s)]
 
 
 def scan_slots(slots, others):
@@ -387,7 +397,7 @@
 
 
 def swap_far(slots):
-    return [slots[0]] + [swap(slots[s], "inner", 2 * s) for s in range(1, len(slots))]
+    return [slots[0]] + [swap(slots[s], "inner", 2 * exchanged(s)) for s in range(1, len(slots))]
 
 
 def body(queries, keys, values, cotangent):

time: 35.6 us -> 36.2 us (1.017)
  waiting for transfers between devices: 12.3 us -> 12.8 us
    ppermute x13, waiting for transfers between devices: 12.3 us -> 12.8 us  [swap(): lax.ppermute(x, axis, [(i, i ^ bits) for i in range(lax.axis_size(axis))])]
  transfers between devices with their start and end apart: 13 -> 13, of which waited for: 8 -> 9; matrix products, arithmetic and copies ran while one was open for 0% -> 0% of each run, Pallas kernels for 16% -> 16%
where the time goes in v30:
time: 36.2 us; the launch traced here: 36 us
  starting transfers between devices  13.7 us (38%)
  waiting for transfers between devices  12.8 us (35%)
  Pallas kernels  8.74 us (24%)
  between operations  0.79 us (2%)
    ppermute x13, starting transfers between devices, swap(): lax.ppermute(x, axis, [(i, i ^ bits) for i in range(lax.axis_size(axis))])  13.7 us
    ppermute x13, waiting for transfers between devices, swap(): lax.ppermute(x, axis, [(i, i ^ bits) for i in range(lax.axis_size(axis))])  12.8 us
    pallas_call x4, Pallas kernels, finish(): pl.pallas_call(functools.partial(finish_kernel, scale, own, block, len(sl...  3.7 us
    pallas_call x1, Pallas kernels, local_part(): pl.pallas_call(local_kernel, name='local', in_specs=[VMEM] * 4, out_specs...  2.16 us
    pallas_call x1, Pallas kernels, first_sums(): pl.pallas_call(give_kernel, name='first_sums', in_specs=[ANY] * 4, out_sp...  1.59 us
    pallas_call x2, Pallas kernels, sums(): pl.pallas_call(functools.partial(sums_kernel, wanted), name='sums', in_sp...  0.77 us
  transfers between devices with their start and end apart: 13, of which 9 were waited for; matrix products, arithmetic and copies ran while one was open for 0% of the time, Pallas kernels for 16%

profile of v30, /device:TPU:0, one launch (start us, length us, event | category | flops | bytes accessed | tf_op | source)
XLA Modules:
  0.0 36.0 jit_solution(1921970940284263433)
XLA Ops:
  0.7 1.6 %first_sums.1 = bf16[2,512,128]{2,1,0:T(8,128)(2,1)S(1)} custom-call(bf16[128,2048]{1,0:T(8,128)(2,1)} %refs_0_.15, bf16[128,2048]{1,0:T(8,128)(2,1)} %refs_1_.15, bf16[128,2048]{1,0:T(8,128)(2,1)} %refs_2_.15, bf16[128,2048]{1,0:T(8,128)(2,1)} %refs_3_.15), custom_call_target="tpu_custom_call" | custom-call | flops 33554432 | bytes 786432 | tf_op jit(solution)/shard_map/first_sums/pallas_call | solution.py:105
  2.3 0.5 %collective-permute-start = (bf16[2,512,128]{2,1,0:T(8,128)(2,1)S(1)}, bf16[2,512,128]{2,1,0:T(8,128)(2,1)S(1)}, u32[]{:S(2)}, u32[]{:S(2)}) collective-permute-start(bf16[2,512,128]{2,1,0:T(8,128)(2,1)S(1)} %first_sums.1), channel_id=1, source_target_pairs={{0,1},{1,0},{2,3},{3,2},{4,5},{5,4},{6,7},{7,6},{8,9},{9,8},{10,11... | collective-permute-start | bytes 786440 | tf_op jit(solution)/shard_map/ppermute | solution.py:396
  2.8 0.3 sums.3
  3.2 0.5 %sums.2 = (bf16[2,512,128]{2,1,0:T(8,128)(2,1)S(1)}, bf16[2,512,128]{2,1,0:T(8,128)(2,1)S(1)}) custom-call(bf16[128,2048]{1,0:T(8,128)(2,1)S(1)} %copy-done, bf16[128,2048]{1,0:T(8,128)(2,1)S(1)} %copy-done.1, bf16[128,2048]{1,0:T(8,128)(2,1)S(1)} %copy-done.2, bf16[128,2048]{1,0:T(8,128)(2,1)S(1)} %copy-done.3), custom_call_target="tpu_custom_call" | custom-call | flops 67108864 | bytes 1572864 | tf_op jit(solution)/shard_map/sums/pallas_call | solution.py:126
  4.0 3.0 %collective-permute-start.1 = (bf16[2,256,128]{2,1,0:T(8,128)(2,1)S(1)}, bf16[2,256,128]{2,1,0:T(8,128)(2,1)S(1)}, u32[]{:S(2)}, u32[]{:S(2)}) collective-permute-start(bf16[2,256,128]{2,1,0:T(8,128)(2,1)S(1)} %get-tuple-element.46), channel_id=1, source_target_pairs={{0,4},{1,5},{2,6},{3,7},{4,0},{5,1},{6,2},{7,3},{8,12},{9,13},{10,... | collective-permute-start | bytes 393224 | tf_op jit(solution)/shard_map/ppermute | solution.py:396
  7.0 1.6 %collective-permute-start.3 = (bf16[2,256,128]{2,1,0:T(8,128)(2,1)S(1)}, bf16[2,256,128]{2,1,0:T(8,128)(2,1)S(1)}, u32[]{:S(2)}, u32[]{:S(2)}) collective-permute-start(bf16[2,256,128]{2,1,0:T(8,128)(2,1)S(1)} %get-tuple-element.48), channel_id=1, source_target_pairs={{0,2},{1,3},{2,0},{3,1},{4,6},{5,7},{6,4},{7,5},{8,10},{9,11},{10,... | collective-permute-start | bytes 393224 | tf_op jit(solution)/shard_map/ppermute | solution.py:396
  8.6 0.4 %collective-permute-start.4 = (bf16[2,256,128]{2,1,0:T(8,128)(2,1)S(1)}, bf16[2,256,128]{2,1,0:T(8,128)(2,1)S(1)}, u32[]{:S(2)}, u32[]{:S(2)}) collective-permute-start(bf16[2,256,128]{2,1,0:T(8,128)(2,1)S(1)} %get-tuple-element.49), channel_id=1, source_target_pairs={{0,6},{1,7},{2,4},{3,5},{4,2},{5,3},{6,0},{7,1},{8,14},{9,15},{10,... | collective-permute-start | bytes 393224 | tf_op jit(solution)/shard_map/ppermute | solution.py:396
  9.0 2.2 %local.1 = (f32[128,2048]{1,0:T(8,128)S(1)}, f32[128,2048]{1,0:T(8,128)S(1)}, f32[128,2048]{1,0:T(8,128)S(1)}, f32[128,2048]{1,0:T(8,128)S(1)}) custom-call(bf16[128,2048]{1,0:T(8,128)(2,1)S(1)} %copy-done, bf16[128,2048]{1,0:T(8,128)(2,1)S(1)} %copy-done.1, bf16[128,2048]{1,0:T(8,128)(2,1)S(1)} %copy-done.2, bf16[128,2048]{1,0:T(8,128)(2,1)S(1)} %copy-done.3), custom_call_target="tpu_custom_call" | custom-call | flops 402653184 | bytes 6291456 | tf_op jit(solution)/shard_map/local/pallas_call | solution.py:284
  11.1 2.3 %collective-permute-done.3.refs_2_ = bf16[2,256,128]{2,1,0:T(8,128)(2,1)S(1)} collective-permute-done((bf16[2,256,128]{2,1,0:T(8,128)(2,1)S(1)}, bf16[2,256,128]{2,1,0:T(8,128)(2,1)S(1)}, u32[]{:S(2)}, u32[]{:S(2)}) %collective-permute-start.3) | collective-permute-done | bytes 131104 | tf_op jit(solution)/shard_map/ppermute | solution.py:396
  13.5 2.0 %collective-permute-done.4.refs_3_ = bf16[2,256,128]{2,1,0:T(8,128)(2,1)S(1)} collective-permute-done((bf16[2,256,128]{2,1,0:T(8,128)(2,1)S(1)}, bf16[2,256,128]{2,1,0:T(8,128)(2,1)S(1)}, u32[]{:S(2)}, u32[]{:S(2)}) %collective-permute-start.4) | collective-permute-done | bytes 131104 | tf_op jit(solution)/shard_map/ppermute | solution.py:396
  15.6 3.7 %collective-permute-start.5 = (bf16[256,128]{1,0:T(8,128)(2,1)S(1)}, bf16[256,128]{1,0:T(8,128)(2,1)S(1)}, u32[]{:S(2)}, u32[]{:S(2)}) collective-permute-start(bf16[256,128]{1,0:T(8,128)(2,1)S(1)} %get-tuple-element.62), channel_id=1, source_target_pairs={{0,24},{8,16},{16,8},{24,0},{1,25},{9,17},{17,9},{25,1},{2,26},{10... | collective-permute-start | bytes 196616 | tf_op jit(solution)/shard_map/ppermute | solution.py:396
  19.3 0.8 %collective-permute-start.7 = (bf16[256,128]{1,0:T(8,128)(2,1)S(1)}, bf16[256,128]{1,0:T(8,128)(2,1)S(1)}, u32[]{:S(2)}, u32[]{:S(2)}) collective-permute-start(bf16[256,128]{1,0:T(8,128)(2,1)S(1)} %get-tuple-element.64), channel_id=1, source_target_pairs={{0,16},{8,24},{16,0},{24,8},{1,17},{9,25},{17,1},{25,9},{2,18},{10... | collective-permute-start | bytes 196616 | tf_op jit(solution)/shard_map/ppermute | solution.py:396
  20.1 1.8 %collective-permute-done.5.refs_4_ = bf16[256,128]{1,0:T(8,128)(2,1)S(1)} collective-permute-done((bf16[256,128]{1,0:T(8,128)(2,1)S(1)}, bf16[256,128]{1,0:T(8,128)(2,1)S(1)}, u32[]{:S(2)}, u32[]{:S(2)}) %collective-permute-start.5) | collective-permute-done | bytes 65568 | tf_op jit(solution)/shard_map/ppermute | solution.py:396
  21.8 2.0 %collective-permute-done.6.refs_5_ = bf16[256,128]{1,0:T(8,128)(2,1)S(1)} collective-permute-done((bf16[256,128]{1,0:T(8,128)(2,1)S(1)}, bf16[256,128]{1,0:T(8,128)(2,1)S(1)}, u32[]{:S(2)}, u32[]{:S(2)}) %collective-permute-start.6) | collective-permute-done | bytes 65568 | tf_op jit(solution)/shard_map/ppermute | solution.py:396
  23.9 0.7 %collective-permute-done.7.refs_6_ = bf16[256,128]{1,0:T(8,128)(2,1)S(1)} collective-permute-done((bf16[256,128]{1,0:T(8,128)(2,1)S(1)}, bf16[256,128]{1,0:T(8,128)(2,1)S(1)}, u32[]{:S(2)}, u32[]{:S(2)}) %collective-permute-start.7) | collective-permute-done | bytes 65568 | tf_op jit(solution)/shard_map/ppermute | solution.py:396
  24.8 1.1 %collective-permute-start.10 = (bf16[2,256,128]{2,1,0:T(8,128)(2,1)S(1)}, bf16[2,256,128]{2,1,0:T(8,128)(2,1)S(1)}, u32[]{:S(2)}, u32[]{:S(2)}) collective-permute-start(bf16[2,256,128]{2,1,0:T(8,128)(2,1)S(1)} %get-tuple-element.68), channel_id=1, source_target_pairs={{0,4},{1,5},{2,6},{3,7},{4,0},{5,1},{6,2},{7,3},{8,12},{9,13},{10,... | collective-permute-start | bytes 393224 | tf_op jit(solution)/shard_map/ppermute | solution.py:396
  25.8 1.5 %collective-permute-start.8 = (bf16[2,256,128]{2,1,0:T(8,128)(2,1)S(1)}, bf16[2,256,128]{2,1,0:T(8,128)(2,1)S(1)}, u32[]{:S(2)}, u32[]{:S(2)}) collective-permute-start(bf16[2,256,128]{2,1,0:T(8,128)(2,1)S(1)} %get-tuple-element.65), channel_id=1, source_target_pairs={{0,2},{1,3},{2,0},{3,1},{4,6},{5,7},{6,4},{7,5},{8,10},{9,11},{10,... | collective-permute-start | bytes 393224 | tf_op jit(solution)/shard_map/ppermute | solution.py:396
  27.3 1.0 %collective-permute-start.9 = (bf16[2,256,128]{2,1,0:T(8,128)(2,1)S(1)}, bf16[2,256,128]{2,1,0:T(8,128)(2,1)S(1)}, u32[]{:S(2)}, u32[]{:S(2)}) collective-permute-start(bf16[2,256,128]{2,1,0:T(8,128)(2,1)S(1)} %get-tuple-element.66), channel_id=1, source_target_pairs={{0,6},{1,7},{2,4},{3,5},{4,2},{5,3},{6,0},{7,1},{8,14},{9,15},{10,... | collective-permute-start | bytes 393224 | tf_op jit(solution)/shard_map/ppermute | solution.py:396
  28.3 2.9 %collective-permute-done.10.refs_9_.refs_1_ = bf16[2,256,128]{2,1,0:T(8,128)(2,1)S(1)} collective-permute-done((bf16[2,256,128]{2,1,0:T(8,128)(2,1)S(1)}, bf16[2,256,128]{2,1,0:T(8,128)(2,1)S(1)}, u32[]{:S(2)}, u32[]{:S(2)}) %collective-permute-start.10) | collective-permute-done | bytes 131104 | tf_op jit(solution)/shard_map/ppermute | solution.py:396
  31.3 1.2 %finish.4 = (bf16[128,2048]{1,0:T(8,128)(2,1)}, bf16[128,2048]{1,0:T(8,128)(2,1)}, bf16[128,2048]{1,0:T(8,128)(2,1)}, bf16[128,2048]{1,0:T(8,128)(2,1)}) custom-call(bf16[128,2048]{1,0:T(8,128)(2,1)S(1)} %copy-done, bf16[128,2048]{1,0:T(8,128)(2,1)S(1)} %copy-done.1, bf16[128,2048]{1,0:T(8,128)(2,1)S(1)} %copy-done.2, bf16[128,2048]{1,0:T(8,128)(2,1)S(1)} %copy-done.3, ...), custom_call_target="tpu_custom_call" | custom-call | flops 67108864 | bytes 2097152 | tf_op jit(solution)/shard_map/finish/pallas_call | solution.py:378
  32.5 0.7 %collective-permute-done.9.refs_1_.refs_9_ = bf16[2,256,128]{2,1,0:T(8,128)(2,1)S(1)} collective-permute-done((bf16[2,256,128]{2,1,0:T(8,128)(2,1)S(1)}, bf16[2,256,128]{2,1,0:T(8,128)(2,1)S(1)}, u32[]{:S(2)}, u32[]{:S(2)}) %collective-permute-start.9) | collective-permute-done | bytes 131104 | tf_op jit(solution)/shard_map/ppermute | solution.py:396
  33.3 0.4 %finish.5.refs_9_ = bf16[4,128,512]{2,1,0:T(8,128)(2,1)S(1)} custom-call(bf16[128,2048]{1,0:T(8,128)(2,1)S(1)} %copy-done, bf16[128,2048]{1,0:T(8,128)(2,1)S(1)} %copy-done.1, bf16[128,2048]{1,0:T(8,128)(2,1)S(1)} %copy-done.2, bf16[128,2048]{1,0:T(8,128)(2,1)S(1)} %copy-done.3, f32[128,2048]{1,0:T(8,128)S(1)} %get-tuple-element.54.refs_4_, ...), custom_call_target="tpu_custom_call" | custom-call | flops 67108864 | bytes 2097152 | tf_op jit(solution)/shard_map/finish/pallas_call | solution.py:378
  33.8 0.9 %finish.6 = (bf16[128,2048]{1,0:T(8,128)(2,1)}, bf16[128,2048]{1,0:T(8,128)(2,1)}, bf16[128,2048]{1,0:T(8,128)(2,1)}, bf16[128,2048]{1,0:T(8,128)(2,1)}, bf16[4,128,512]{2,1,0:T(8,128)(2,1)S(1)}) custom-call(bf16[128,2048]{1,0:T(8,128)(2,1)S(1)} %copy-done, ...), custom_call_target="tpu_custom_call", output_to_operand_aliasing={{0}: (10, {}), {1}: (11, {}), {2}: (12, {}), {3}: (13, {})} | custom-call | flops 67108864 | bytes 2097152 | tf_op jit(solution)/shard_map/finish/pallas_call | solution.py:378
  34.9 1.2 %finish.7 = (bf16[128,2048]{1,0:T(8,128)(2,1)}, bf16[128,2048]{1,0:T(8,128)(2,1)}, bf16[128,2048]{1,0:T(8,128)(2,1)}, bf16[128,2048]{1,0:T(8,128)(2,1)}) custom-call(bf16[128,2048]{1,0:T(8,128)(2,1)S(1)} %copy-done, bf16[128,2048]{1,0:T(8,128)(2,1)S(1)} %copy-done.1, ...), custom_call_target="tpu_custom_call", output_to_operand_aliasing={{0}: (10, {}), {1}: (11, {}), {2}: (12, {}), {3}: (13, {})} | custom-call | flops 67108864 | bytes 2097152 | tf_op jit(solution)/shard_map/finish/pallas_call | solution.py:378
  (24 shorter events, 1.2 us)
Async XLA Ops:
  0.6 2.2 %copy-start.3 = (bf16[128,2048]{1,0:T(8,128)(2,1)S(1)}, bf16[128,2048]{1,0:T(8,128)(2,1)}, u32[]{:S(2)}) copy-start(bf16[128,2048]{1,0:T(8,128)(2,1)} %refs_3_.15) | copy-start | bytes 1572868
  0.6 2.2 %copy-start.2 = (bf16[128,2048]{1,0:T(8,128)(2,1)S(1)}, bf16[128,2048]{1,0:T(8,128)(2,1)}, u32[]{:S(2)}) copy-start(bf16[128,2048]{1,0:T(8,128)(2,1)} %refs_2_.15) | copy-start | bytes 1572868
  0.7 2.1 %copy-start.1 = (bf16[128,2048]{1,0:T(8,128)(2,1)S(1)}, bf16[128,2048]{1,0:T(8,128)(2,1)}, u32[]{:S(2)}) copy-start(bf16[128,2048]{1,0:T(8,128)(2,1)} %refs_1_.15) | copy-start | bytes 1572868
  0.7 2.1 %copy-start = (bf16[128,2048]{1,0:T(8,128)(2,1)S(1)}, bf16[128,2048]{1,0:T(8,128)(2,1)}, u32[]{:S(2)}) copy-start(bf16[128,2048]{1,0:T(8,128)(2,1)} %refs_0_.15) | copy-start | bytes 1572868
  2.3 1.7 %collective-permute-start = (bf16[2,512,128]{2,1,0:T(8,128)(2,1)S(1)}, bf16[2,512,128]{2,1,0:T(8,128)(2,1)S(1)}, u32[]{:S(2)}, u32[]{:S(2)}) collective-permute-start(bf16[2,512,128]{2,1,0:T(8,128)(2,1)S(1)} %first_sums.1), channel_id=1, source_target_pairs={{0,1},{1,0},{2,3},{3,2},{4,5},{5,4},{6,7},{7,6},{8,9},{9,8},{10,11... | collective-permute-start | bytes 786440 | tf_op jit(solution)/shard_map/ppermute | solution.py:396
  3.1 3.9 %collective-permute-start.2 = (bf16[2,512,128]{2,1,0:T(8,128)(2,1)S(1)}, bf16[2,512,128]{2,1,0:T(8,128)(2,1)S(1)}, u32[]{:S(2)}, u32[]{:S(2)}) collective-permute-start(bf16[2,512,128]{2,1,0:T(8,128)(2,1)S(1)} %sums.3), channel_id=1, source_target_pairs={{0,1},{1,0},{2,3},{3,2},{4,5},{5,4},{6,7},{7,6},{8,9},{9,8},{10,11... | collective-permute-start | bytes 786440 | tf_op jit(solution)/shard_map/ppermute | solution.py:396
  4.0 7.1 %collective-permute-start.1 = (bf16[2,256,128]{2,1,0:T(8,128)(2,1)S(1)}, bf16[2,256,128]{2,1,0:T(8,128)(2,1)S(1)}, u32[]{:S(2)}, u32[]{:S(2)}) collective-permute-start(bf16[2,256,128]{2,1,0:T(8,128)(2,1)S(1)} %get-tuple-element.46), channel_id=1, source_target_pairs={{0,4},{1,5},{2,6},{3,7},{4,0},{5,1},{6,2},{7,3},{8,12},{9,13},{10,... | collective-permute-start | bytes 393224 | tf_op jit(solution)/shard_map/ppermute | solution.py:396
  7.0 6.4 %collective-permute-start.3 = (bf16[2,256,128]{2,1,0:T(8,128)(2,1)S(1)}, bf16[2,256,128]{2,1,0:T(8,128)(2,1)S(1)}, u32[]{:S(2)}, u32[]{:S(2)}) collective-permute-start(bf16[2,256,128]{2,1,0:T(8,128)(2,1)S(1)} %get-tuple-element.48), channel_id=1, source_target_pairs={{0,2},{1,3},{2,0},{3,1},{4,6},{5,7},{6,4},{7,5},{8,10},{9,11},{10,... | collective-permute-start | bytes 393224 | tf_op jit(solution)/shard_map/ppermute | solution.py:396
  8.6 6.9 %collective-permute-start.4 = (bf16[2,256,128]{2,1,0:T(8,128)(2,1)S(1)}, bf16[2,256,128]{2,1,0:T(8,128)(2,1)S(1)}, u32[]{:S(2)}, u32[]{:S(2)}) collective-permute-start(bf16[2,256,128]{2,1,0:T(8,128)(2,1)S(1)} %get-tuple-element.49), channel_id=1, source_target_pairs={{0,6},{1,7},{2,4},{3,5},{4,2},{5,3},{6,0},{7,1},{8,14},{9,15},{10,... | collective-permute-start | bytes 393224 | tf_op jit(solution)/shard_map/ppermute | solution.py:396
  15.6 6.2 %collective-permute-start.5 = (bf16[256,128]{1,0:T(8,128)(2,1)S(1)}, bf16[256,128]{1,0:T(8,128)(2,1)S(1)}, u32[]{:S(2)}, u32[]{:S(2)}) collective-permute-start(bf16[256,128]{1,0:T(8,128)(2,1)S(1)} %get-tuple-element.62), channel_id=1, source_target_pairs={{0,24},{8,16},{16,8},{24,0},{1,25},{9,17},{17,9},{25,1},{2,26},{10... | collective-permute-start | bytes 196616 | tf_op jit(solution)/shard_map/ppermute | solution.py:396
  19.3 4.6 %collective-permute-start.6 = (bf16[256,128]{1,0:T(8,128)(2,1)S(1)}, bf16[256,128]{1,0:T(8,128)(2,1)S(1)}, u32[]{:S(2)}, u32[]{:S(2)}) collective-permute-start(bf16[256,128]{1,0:T(8,128)(2,1)S(1)} %get-tuple-element.63), channel_id=1, source_target_pairs={{0,8},{8,0},{16,24},{24,16},{1,9},{9,1},{17,25},{25,17},{2,10},{10... | collective-permute-start | bytes 196616 | tf_op jit(solution)/shard_map/ppermute | solution.py:396
  19.3 5.3 %collective-permute-start.7 = (bf16[256,128]{1,0:T(8,128)(2,1)S(1)}, bf16[256,128]{1,0:T(8,128)(2,1)S(1)}, u32[]{:S(2)}, u32[]{:S(2)}) collective-permute-start(bf16[256,128]{1,0:T(8,128)(2,1)S(1)} %get-tuple-element.64), channel_id=1, source_target_pairs={{0,16},{8,24},{16,0},{24,8},{1,17},{9,25},{17,1},{25,9},{2,18},{10... | collective-permute-start | bytes 196616 | tf_op jit(solution)/shard_map/ppermute | solution.py:396
  24.8 6.4 %collective-permute-start.10 = (bf16[2,256,128]{2,1,0:T(8,128)(2,1)S(1)}, bf16[2,256,128]{2,1,0:T(8,128)(2,1)S(1)}, u32[]{:S(2)}, u32[]{:S(2)}) collective-permute-start(bf16[2,256,128]{2,1,0:T(8,128)(2,1)S(1)} %get-tuple-element.68), channel_id=1, source_target_pairs={{0,4},{1,5},{2,6},{3,7},{4,0},{5,1},{6,2},{7,3},{8,12},{9,13},{10,... | collective-permute-start | bytes 393224 | tf_op jit(solution)/shard_map/ppermute | solution.py:396
  25.8 6.7 %collective-permute-start.8 = (bf16[2,256,128]{2,1,0:T(8,128)(2,1)S(1)}, bf16[2,256,128]{2,1,0:T(8,128)(2,1)S(1)}, u32[]{:S(2)}, u32[]{:S(2)}) collective-permute-start(bf16[2,256,128]{2,1,0:T(8,128)(2,1)S(1)} %get-tuple-element.65), channel_id=1, source_target_pairs={{0,2},{1,3},{2,0},{3,1},{4,6},{5,7},{6,4},{7,5},{8,10},{9,11},{10,... | collective-permute-start | bytes 393224 | tf_op jit(solution)/shard_map/ppermute | solution.py:396
  27.3 5.9 %collective-permute-start.9 = (bf16[2,256,128]{2,1,0:T(8,128)(2,1)S(1)}, bf16[2,256,128]{2,1,0:T(8,128)(2,1)S(1)}, u32[]{:S(2)}, u32[]{:S(2)}) collective-permute-start(bf16[2,256,128]{2,1,0:T(8,128)(2,1)S(1)} %get-tuple-element.66), channel_id=1, source_target_pairs={{0,6},{1,7},{2,4},{3,5},{4,2},{5,3},{6,0},{7,1},{8,14},{9,15},{10,... | collective-permute-start | bytes 393224 | tf_op jit(solution)/shard_map/ppermute | solution.py:396
  31.3 2.5 %collective-permute-start.12 = (bf16[2,512,128]{2,1,0:T(8,128)(2,1)S(1)}, bf16[2,512,128]{2,1,0:T(8,128)(2,1)S(1)}, u32[]{:S(2)}, u32[]{:S(2)}) collective-permute-start(bf16[2,512,128]{2,1,0:T(8,128)(2,1)S(1)} %theirs.3), channel_id=1, source_target_pairs={{0,1},{1,0},{2,3},{3,2},{4,5},{5,4},{6,7},{7,6},{8,9},{9,8},{10,11... | collective-permute-start | bytes 786440 | tf_op jit(solution)/shard_map/ppermute | solution.py:396
  33.3 1.6 %collective-permute-start.11 = (bf16[2,512,128]{2,1,0:T(8,128)(2,1)S(1)}, bf16[2,512,128]{2,1,0:T(8,128)(2,1)S(1)}, u32[]{:S(2)}, u32[]{:S(2)}) collective-permute-start(bf16[2,512,128]{2,1,0:T(8,128)(2,1)S(1)} %theirs.2), channel_id=1, source_target_pairs={{0,1},{1,0},{2,3},{3,2},{4,5},{5,4},{6,7},{7,6},{8,9},{9,8},{10,11... | collective-permute-start | bytes 786440 | tf_op jit(solution)/shard_map/ppermute | solution.py:396

commit v31 on v29

--- a/solution.py
+++ b/solution.py
@@ -304,10 +304,15 @@
     one_ahead(products(), use)
 
 
+def piece_of(width, piece):
+    last = width - HEAD
+    return (0, width) if piece is None else ((0, last), (last, HEAD))[piece]
+
+
 def copies_out(own, block, held, outs, sems, piece):
-    first, size = (0, held.shape[2]) if piece is None else (piece * held.shape[2] // 2, held.shape[2] // 2)
+    first, size = piece_of(held.shape[2], piece)
     start = block_start(own, block, outs[0].shape[1] // 2) + first
-    there = pl.ds(pl.multiple_of(start, size), size)
+    there = pl.ds(pl.multiple_of(start, HEAD), size)
     return [
         pltpu.make_async_copy(held.at[i, :, pl.ds(first, size)], out.at[:, there], sems.at[i])
         for i, out in enumerate(outs)
@@ -336,7 +341,7 @@
     def store(rows, i, out):
         held[i, :, rows] = out
         for piece in range(2):
-            if not hold and i == 3 and rows.stop == (piece + 1) * states.shape[1] // 2:
+            if not hold and i == 3 and rows.stop == sum(piece_of(states.shape[1], piece)):
                 for copy in copies_out(own, block, held, outs, sems.at[piece], piece):
                     copy.start()
 

time: 35.6 us -> 35.6 us (level)
  no operation moved by 1% of the time
where the time goes in v31:
time: 35.6 us; the launch traced here: 35.5 us
  starting transfers between devices  13.6 us (38%)
  waiting for transfers between devices  12.3 us (35%)
  Pallas kernels  8.76 us (25%)
  between operations  0.79 us (2%)
    ppermute x13, starting transfers between devices, swap(): lax.ppermute(x, axis, [(i, i ^ bits) for i in range(lax.axis_size(axis))])  13.6 us
    ppermute x13, waiting for transfers between devices, swap(): lax.ppermute(x, axis, [(i, i ^ bits) for i in range(lax.axis_size(axis))])  12.3 us
    pallas_call x4, Pallas kernels, finish(): pl.pallas_call(functools.partial(finish_kernel, scale, own, block, len(sl...  3.74 us
    pallas_call x1, Pallas kernels, local_part(): pl.pallas_call(local_kernel, name='local', in_specs=[VMEM] * 4, out_specs...  2.16 us
    pallas_call x1, Pallas kernels, first_sums(): pl.pallas_call(give_kernel, name='first_sums', in_specs=[ANY] * 4, out_sp...  1.59 us
    pallas_call x2, Pallas kernels, sums(): pl.pallas_call(functools.partial(sums_kernel, wanted), name='sums', in_sp...  0.77 us
  transfers between devices with their start and end apart: 13, of which 8 were waited for; matrix products, arithmetic and copies ran while one was open for 0% of the time, Pallas kernels for 16%

profile of v31, /device:TPU:0, one launch (start us, length us, event | category | flops | bytes accessed | tf_op | source)
XLA Modules:
  0.0 35.5 jit_solution(9750392892368574333)
XLA Ops:
  0.7 1.6 %first_sums.1 = bf16[2,512,128]{2,1,0:T(8,128)(2,1)S(1)} custom-call(bf16[128,2048]{1,0:T(8,128)(2,1)} %refs_0_.15, bf16[128,2048]{1,0:T(8,128)(2,1)} %refs_1_.15, bf16[128,2048]{1,0:T(8,128)(2,1)} %refs_2_.15, bf16[128,2048]{1,0:T(8,128)(2,1)} %refs_3_.15), custom_call_target="tpu_custom_call" | custom-call | flops 33554432 | bytes 786432 | tf_op jit(solution)/shard_map/first_sums/pallas_call | solution.py:95
  2.3 0.5 %collective-permute-start = (bf16[2,512,128]{2,1,0:T(8,128)(2,1)S(1)}, bf16[2,512,128]{2,1,0:T(8,128)(2,1)S(1)}, u32[]{:S(2)}, u32[]{:S(2)}) collective-permute-start(bf16[2,512,128]{2,1,0:T(8,128)(2,1)S(1)} %first_sums.1), channel_id=1, source_target_pairs={{0,1},{1,0},{2,3},{3,2},{4,5},{5,4},{6,7},{7,6},{8,9},{9,8},{10,11... | collective-permute-start | bytes 786440 | tf_op jit(solution)/shard_map/ppermute | solution.py:391
  2.8 0.3 sums.3
  3.2 0.5 %sums.2 = (bf16[2,512,128]{2,1,0:T(8,128)(2,1)S(1)}, bf16[2,512,128]{2,1,0:T(8,128)(2,1)S(1)}) custom-call(bf16[128,2048]{1,0:T(8,128)(2,1)S(1)} %copy-done, bf16[128,2048]{1,0:T(8,128)(2,1)S(1)} %copy-done.1, bf16[128,2048]{1,0:T(8,128)(2,1)S(1)} %copy-done.2, bf16[128,2048]{1,0:T(8,128)(2,1)S(1)} %copy-done.3), custom_call_target="tpu_custom_call" | custom-call | flops 67108864 | bytes 1572864 | tf_op jit(solution)/shard_map/sums/pallas_call | solution.py:116
  3.7 0.2 collective-permute-done.got_ref.refs_10_
  4.0 2.9 %collective-permute-start.1 = (bf16[2,256,128]{2,1,0:T(8,128)(2,1)S(1)}, bf16[2,256,128]{2,1,0:T(8,128)(2,1)S(1)}, u32[]{:S(2)}, u32[]{:S(2)}) collective-permute-start(bf16[2,256,128]{2,1,0:T(8,128)(2,1)S(1)} %get-tuple-element.46), channel_id=1, source_target_pairs={{0,2},{1,3},{2,0},{3,1},{4,6},{5,7},{6,4},{7,5},{8,10},{9,11},{10,... | collective-permute-start | bytes 393224 | tf_op jit(solution)/shard_map/ppermute | solution.py:391
  7.0 1.6 %collective-permute-start.3 = (bf16[2,256,128]{2,1,0:T(8,128)(2,1)S(1)}, bf16[2,256,128]{2,1,0:T(8,128)(2,1)S(1)}, u32[]{:S(2)}, u32[]{:S(2)}) collective-permute-start(bf16[2,256,128]{2,1,0:T(8,128)(2,1)S(1)} %get-tuple-element.48), channel_id=1, source_target_pairs={{0,4},{1,5},{2,6},{3,7},{4,0},{5,1},{6,2},{7,3},{8,12},{9,13},{10,... | collective-permute-start | bytes 393224 | tf_op jit(solution)/shard_map/ppermute | solution.py:391
  8.6 0.3 collective-permute-start.4
  8.9 2.2 %local.1 = (f32[128,2048]{1,0:T(8,128)S(1)}, f32[128,2048]{1,0:T(8,128)S(1)}, f32[128,2048]{1,0:T(8,128)S(1)}, f32[128,2048]{1,0:T(8,128)S(1)}) custom-call(bf16[128,2048]{1,0:T(8,128)(2,1)S(1)} %copy-done, bf16[128,2048]{1,0:T(8,128)(2,1)S(1)} %copy-done.1, bf16[128,2048]{1,0:T(8,128)(2,1)S(1)} %copy-done.2, bf16[128,2048]{1,0:T(8,128)(2,1)S(1)} %copy-done.3), custom_call_target="tpu_custom_call" | custom-call | flops 402653184 | bytes 6291456 | tf_op jit(solution)/shard_map/local/pallas_call | solution.py:274
  11.1 4.0 %collective-permute-done.3.refs_2_ = bf16[2,256,128]{2,1,0:T(8,128)(2,1)S(1)} collective-permute-done((bf16[2,256,128]{2,1,0:T(8,128)(2,1)S(1)}, bf16[2,256,128]{2,1,0:T(8,128)(2,1)S(1)}, u32[]{:S(2)}, u32[]{:S(2)}) %collective-permute-start.3) | collective-permute-done | bytes 131104 | tf_op jit(solution)/shard_map/ppermute | solution.py:391
  15.2 3.7 %collective-permute-start.5 = (bf16[256,128]{1,0:T(8,128)(2,1)S(1)}, bf16[256,128]{1,0:T(8,128)(2,1)S(1)}, u32[]{:S(2)}, u32[]{:S(2)}) collective-permute-start(bf16[256,128]{1,0:T(8,128)(2,1)S(1)} %get-tuple-element.62), channel_id=1, source_target_pairs={{0,24},{8,16},{16,8},{24,0},{1,25},{9,17},{17,9},{25,1},{2,26},{10... | collective-permute-start | bytes 196616 | tf_op jit(solution)/shard_map/ppermute | solution.py:391
  18.9 0.8 %collective-permute-start.7 = (bf16[256,128]{1,0:T(8,128)(2,1)S(1)}, bf16[256,128]{1,0:T(8,128)(2,1)S(1)}, u32[]{:S(2)}, u32[]{:S(2)}) collective-permute-start(bf16[256,128]{1,0:T(8,128)(2,1)S(1)} %get-tuple-element.64), channel_id=1, source_target_pairs={{0,16},{8,24},{16,0},{24,8},{1,17},{9,25},{17,1},{25,9},{2,18},{10... | collective-permute-start | bytes 196616 | tf_op jit(solution)/shard_map/ppermute | solution.py:391
  19.7 1.7 %collective-permute-done.5.refs_4_ = bf16[256,128]{1,0:T(8,128)(2,1)S(1)} collective-permute-done((bf16[256,128]{1,0:T(8,128)(2,1)S(1)}, bf16[256,128]{1,0:T(8,128)(2,1)S(1)}, u32[]{:S(2)}, u32[]{:S(2)}) %collective-permute-start.5) | collective-permute-done | bytes 65568 | tf_op jit(solution)/shard_map/ppermute | solution.py:391
  21.4 1.7 %collective-permute-done.6.refs_5_ = bf16[256,128]{1,0:T(8,128)(2,1)S(1)} collective-permute-done((bf16[256,128]{1,0:T(8,128)(2,1)S(1)}, bf16[256,128]{1,0:T(8,128)(2,1)S(1)}, u32[]{:S(2)}, u32[]{:S(2)}) %collective-permute-start.6) | collective-permute-done | bytes 65568 | tf_op jit(solution)/shard_map/ppermute | solution.py:391
  23.2 0.9 %collective-permute-done.7.refs_6_ = bf16[256,128]{1,0:T(8,128)(2,1)S(1)} collective-permute-done((bf16[256,128]{1,0:T(8,128)(2,1)S(1)}, bf16[256,128]{1,0:T(8,128)(2,1)S(1)}, u32[]{:S(2)}, u32[]{:S(2)}) %collective-permute-start.7) | collective-permute-done | bytes 65568 | tf_op jit(solution)/shard_map/ppermute | solution.py:391
  24.3 1.2 %collective-permute-start.10 = (bf16[2,256,128]{2,1,0:T(8,128)(2,1)S(1)}, bf16[2,256,128]{2,1,0:T(8,128)(2,1)S(1)}, u32[]{:S(2)}, u32[]{:S(2)}) collective-permute-start(bf16[2,256,128]{2,1,0:T(8,128)(2,1)S(1)} %get-tuple-element.68), channel_id=1, source_target_pairs={{0,2},{1,3},{2,0},{3,1},{4,6},{5,7},{6,4},{7,5},{8,10},{9,11},{10,... | collective-permute-start | bytes 393224 | tf_op jit(solution)/shard_map/ppermute | solution.py:391
  25.5 1.3 %collective-permute-start.8 = (bf16[2,256,128]{2,1,0:T(8,128)(2,1)S(1)}, bf16[2,256,128]{2,1,0:T(8,128)(2,1)S(1)}, u32[]{:S(2)}, u32[]{:S(2)}) collective-permute-start(bf16[2,256,128]{2,1,0:T(8,128)(2,1)S(1)} %get-tuple-element.65), channel_id=1, source_target_pairs={{0,4},{1,5},{2,6},{3,7},{4,0},{5,1},{6,2},{7,3},{8,12},{9,13},{10,... | collective-permute-start | bytes 393224 | tf_op jit(solution)/shard_map/ppermute | solution.py:391
  26.8 1.1 %collective-permute-start.9 = (bf16[2,256,128]{2,1,0:T(8,128)(2,1)S(1)}, bf16[2,256,128]{2,1,0:T(8,128)(2,1)S(1)}, u32[]{:S(2)}, u32[]{:S(2)}) collective-permute-start(bf16[2,256,128]{2,1,0:T(8,128)(2,1)S(1)} %get-tuple-element.66), channel_id=1, source_target_pairs={{0,6},{1,7},{2,4},{3,5},{4,2},{5,3},{6,0},{7,1},{8,14},{9,15},{10,... | collective-permute-start | bytes 393224 | tf_op jit(solution)/shard_map/ppermute | solution.py:391
  27.8 2.7 %collective-permute-done.10.refs_9_.refs_1_ = bf16[2,256,128]{2,1,0:T(8,128)(2,1)S(1)} collective-permute-done((bf16[2,256,128]{2,1,0:T(8,128)(2,1)S(1)}, bf16[2,256,128]{2,1,0:T(8,128)(2,1)S(1)}, u32[]{:S(2)}, u32[]{:S(2)}) %collective-permute-start.10) | collective-permute-done | bytes 131104 | tf_op jit(solution)/shard_map/ppermute | solution.py:391
  30.7 1.2 %finish.4 = (bf16[128,2048]{1,0:T(8,128)(2,1)}, bf16[128,2048]{1,0:T(8,128)(2,1)}, bf16[128,2048]{1,0:T(8,128)(2,1)}, bf16[128,2048]{1,0:T(8,128)(2,1)}) custom-call(bf16[128,2048]{1,0:T(8,128)(2,1)S(1)} %copy-done, bf16[128,2048]{1,0:T(8,128)(2,1)S(1)} %copy-done.1, bf16[128,2048]{1,0:T(8,128)(2,1)S(1)} %copy-done.2, bf16[128,2048]{1,0:T(8,128)(2,1)S(1)} %copy-done.3, ...), custom_call_target="tpu_custom_call" | custom-call | flops 67108864 | bytes 2097152 | tf_op jit(solution)/shard_map/finish/pallas_call | solution.py:373
  31.9 0.7 %collective-permute-done.9.refs_1_.refs_9_ = bf16[2,256,128]{2,1,0:T(8,128)(2,1)S(1)} collective-permute-done((bf16[2,256,128]{2,1,0:T(8,128)(2,1)S(1)}, bf16[2,256,128]{2,1,0:T(8,128)(2,1)S(1)}, u32[]{:S(2)}, u32[]{:S(2)}) %collective-permute-start.9) | collective-permute-done | bytes 131104 | tf_op jit(solution)/shard_map/ppermute | solution.py:391
  32.8 0.4 %finish.5.refs_9_ = bf16[4,128,512]{2,1,0:T(8,128)(2,1)S(1)} custom-call(bf16[128,2048]{1,0:T(8,128)(2,1)S(1)} %copy-done, bf16[128,2048]{1,0:T(8,128)(2,1)S(1)} %copy-done.1, bf16[128,2048]{1,0:T(8,128)(2,1)S(1)} %copy-done.2, bf16[128,2048]{1,0:T(8,128)(2,1)S(1)} %copy-done.3, f32[128,2048]{1,0:T(8,128)S(1)} %get-tuple-element.54.refs_4_, ...), custom_call_target="tpu_custom_call" | custom-call | flops 67108864 | bytes 2097152 | tf_op jit(solution)/shard_map/finish/pallas_call | solution.py:373
  33.2 0.9 %finish.6 = (bf16[128,2048]{1,0:T(8,128)(2,1)}, bf16[128,2048]{1,0:T(8,128)(2,1)}, bf16[128,2048]{1,0:T(8,128)(2,1)}, bf16[128,2048]{1,0:T(8,128)(2,1)}, bf16[4,128,512]{2,1,0:T(8,128)(2,1)S(1)}) custom-call(bf16[128,2048]{1,0:T(8,128)(2,1)S(1)} %copy-done, ...), custom_call_target="tpu_custom_call", output_to_operand_aliasing={{0}: (10, {}), {1}: (11, {}), {2}: (12, {}), {3}: (13, {})} | custom-call | flops 67108864 | bytes 2097152 | tf_op jit(solution)/shard_map/finish/pallas_call | solution.py:373
  34.3 1.2 %finish.7 = (bf16[128,2048]{1,0:T(8,128)(2,1)}, bf16[128,2048]{1,0:T(8,128)(2,1)}, bf16[128,2048]{1,0:T(8,128)(2,1)}, bf16[128,2048]{1,0:T(8,128)(2,1)}) custom-call(bf16[128,2048]{1,0:T(8,128)(2,1)S(1)} %copy-done, bf16[128,2048]{1,0:T(8,128)(2,1)S(1)} %copy-done.1, ...), custom_call_target="tpu_custom_call", output_to_operand_aliasing={{0}: (10, {}), {1}: (11, {}), {2}: (12, {}), {3}: (13, {})} | custom-call | flops 67108864 | bytes 2097152 | tf_op jit(solution)/shard_map/finish/pallas_call | solution.py:373
  (24 shorter events, 1.0 us)
Async XLA Ops:
  0.6 2.2 %copy-start.3 = (bf16[128,2048]{1,0:T(8,128)(2,1)S(1)}, bf16[128,2048]{1,0:T(8,128)(2,1)}, u32[]{:S(2)}) copy-start(bf16[128,2048]{1,0:T(8,128)(2,1)} %refs_3_.15) | copy-start | bytes 1572868
  0.6 2.1 %copy-start.2 = (bf16[128,2048]{1,0:T(8,128)(2,1)S(1)}, bf16[128,2048]{1,0:T(8,128)(2,1)}, u32[]{:S(2)}) copy-start(bf16[128,2048]{1,0:T(8,128)(2,1)} %refs_2_.15) | copy-start | bytes 1572868
  0.7 2.1 %copy-start.1 = (bf16[128,2048]{1,0:T(8,128)(2,1)S(1)}, bf16[128,2048]{1,0:T(8,128)(2,1)}, u32[]{:S(2)}) copy-start(bf16[128,2048]{1,0:T(8,128)(2,1)} %refs_1_.15) | copy-start | bytes 1572868
  0.7 2.1 %copy-start = (bf16[128,2048]{1,0:T(8,128)(2,1)S(1)}, bf16[128,2048]{1,0:T(8,128)(2,1)}, u32[]{:S(2)}) copy-start(bf16[128,2048]{1,0:T(8,128)(2,1)} %refs_0_.15) | copy-start | bytes 1572868
  2.3 1.7 %collective-permute-start = (bf16[2,512,128]{2,1,0:T(8,128)(2,1)S(1)}, bf16[2,512,128]{2,1,0:T(8,128)(2,1)S(1)}, u32[]{:S(2)}, u32[]{:S(2)}) collective-permute-start(bf16[2,512,128]{2,1,0:T(8,128)(2,1)S(1)} %first_sums.1), channel_id=1, source_target_pairs={{0,1},{1,0},{2,3},{3,2},{4,5},{5,4},{6,7},{7,6},{8,9},{9,8},{10,11... | collective-permute-start | bytes 786440 | tf_op jit(solution)/shard_map/ppermute | solution.py:391
  3.1 3.8 %collective-permute-start.2 = (bf16[2,512,128]{2,1,0:T(8,128)(2,1)S(1)}, bf16[2,512,128]{2,1,0:T(8,128)(2,1)S(1)}, u32[]{:S(2)}, u32[]{:S(2)}) collective-permute-start(bf16[2,512,128]{2,1,0:T(8,128)(2,1)S(1)} %sums.3), channel_id=1, source_target_pairs={{0,1},{1,0},{2,3},{3,2},{4,5},{5,4},{6,7},{7,6},{8,9},{9,8},{10,11... | collective-permute-start | bytes 786440 | tf_op jit(solution)/shard_map/ppermute | solution.py:391
  4.0 7.1 %collective-permute-start.1 = (bf16[2,256,128]{2,1,0:T(8,128)(2,1)S(1)}, bf16[2,256,128]{2,1,0:T(8,128)(2,1)S(1)}, u32[]{:S(2)}, u32[]{:S(2)}) collective-permute-start(bf16[2,256,128]{2,1,0:T(8,128)(2,1)S(1)} %get-tuple-element.46), channel_id=1, source_target_pairs={{0,2},{1,3},{2,0},{3,1},{4,6},{5,7},{6,4},{7,5},{8,10},{9,11},{10,... | collective-permute-start | bytes 393224 | tf_op jit(solution)/shard_map/ppermute | solution.py:391
  7.0 8.1 %collective-permute-start.3 = (bf16[2,256,128]{2,1,0:T(8,128)(2,1)S(1)}, bf16[2,256,128]{2,1,0:T(8,128)(2,1)S(1)}, u32[]{:S(2)}, u32[]{:S(2)}) collective-permute-start(bf16[2,256,128]{2,1,0:T(8,128)(2,1)S(1)} %get-tuple-element.48), channel_id=1, source_target_pairs={{0,4},{1,5},{2,6},{3,7},{4,0},{5,1},{6,2},{7,3},{8,12},{9,13},{10,... | collective-permute-start | bytes 393224 | tf_op jit(solution)/shard_map/ppermute | solution.py:391
  8.6 6.6 %collective-permute-start.4 = (bf16[2,256,128]{2,1,0:T(8,128)(2,1)S(1)}, bf16[2,256,128]{2,1,0:T(8,128)(2,1)S(1)}, u32[]{:S(2)}, u32[]{:S(2)}) collective-permute-start(bf16[2,256,128]{2,1,0:T(8,128)(2,1)S(1)} %get-tuple-element.49), channel_id=1, source_target_pairs={{0,6},{1,7},{2,4},{3,5},{4,2},{5,3},{6,0},{7,1},{8,14},{9,15},{10,... | collective-permute-start | bytes 393224 | tf_op jit(solution)/shard_map/ppermute | solution.py:391
  15.2 6.2 %collective-permute-start.5 = (bf16[256,128]{1,0:T(8,128)(2,1)S(1)}, bf16[256,128]{1,0:T(8,128)(2,1)S(1)}, u32[]{:S(2)}, u32[]{:S(2)}) collective-permute-start(bf16[256,128]{1,0:T(8,128)(2,1)S(1)} %get-tuple-element.62), channel_id=1, source_target_pairs={{0,24},{8,16},{16,8},{24,0},{1,25},{9,17},{17,9},{25,1},{2,26},{10... | collective-permute-start | bytes 196616 | tf_op jit(solution)/shard_map/ppermute | solution.py:391
  18.9 4.3 %collective-permute-start.6 = (bf16[256,128]{1,0:T(8,128)(2,1)S(1)}, bf16[256,128]{1,0:T(8,128)(2,1)S(1)}, u32[]{:S(2)}, u32[]{:S(2)}) collective-permute-start(bf16[256,128]{1,0:T(8,128)(2,1)S(1)} %get-tuple-element.63), channel_id=1, source_target_pairs={{0,8},{8,0},{16,24},{24,16},{1,9},{9,1},{17,25},{25,17},{2,10},{10... | collective-permute-start | bytes 196616 | tf_op jit(solution)/shard_map/ppermute | solution.py:391
  18.9 5.2 %collective-permute-start.7 = (bf16[256,128]{1,0:T(8,128)(2,1)S(1)}, bf16[256,128]{1,0:T(8,128)(2,1)S(1)}, u32[]{:S(2)}, u32[]{:S(2)}) collective-permute-start(bf16[256,128]{1,0:T(8,128)(2,1)S(1)} %get-tuple-element.64), channel_id=1, source_target_pairs={{0,16},{8,24},{16,0},{24,8},{1,17},{9,25},{17,1},{25,9},{2,18},{10... | collective-permute-start | bytes 196616 | tf_op jit(solution)/shard_map/ppermute | solution.py:391
  24.3 6.2 %collective-permute-start.10 = (bf16[2,256,128]{2,1,0:T(8,128)(2,1)S(1)}, bf16[2,256,128]{2,1,0:T(8,128)(2,1)S(1)}, u32[]{:S(2)}, u32[]{:S(2)}) collective-permute-start(bf16[2,256,128]{2,1,0:T(8,128)(2,1)S(1)} %get-tuple-element.68), channel_id=1, source_target_pairs={{0,2},{1,3},{2,0},{3,1},{4,6},{5,7},{6,4},{7,5},{8,10},{9,11},{10,... | collective-permute-start | bytes 393224 | tf_op jit(solution)/shard_map/ppermute | solution.py:391
  25.5 6.4 %collective-permute-start.8 = (bf16[2,256,128]{2,1,0:T(8,128)(2,1)S(1)}, bf16[2,256,128]{2,1,0:T(8,128)(2,1)S(1)}, u32[]{:S(2)}, u32[]{:S(2)}) collective-permute-start(bf16[2,256,128]{2,1,0:T(8,128)(2,1)S(1)} %get-tuple-element.65), channel_id=1, source_target_pairs={{0,4},{1,5},{2,6},{3,7},{4,0},{5,1},{6,2},{7,3},{8,12},{9,13},{10,... | collective-permute-start | bytes 393224 | tf_op jit(solution)/shard_map/ppermute | solution.py:391
  26.8 5.9 %collective-permute-start.9 = (bf16[2,256,128]{2,1,0:T(8,128)(2,1)S(1)}, bf16[2,256,128]{2,1,0:T(8,128)(2,1)S(1)}, u32[]{:S(2)}, u32[]{:S(2)}) collective-permute-start(bf16[2,256,128]{2,1,0:T(8,128)(2,1)S(1)} %get-tuple-element.66), channel_id=1, source_target_pairs={{0,6},{1,7},{2,4},{3,5},{4,2},{5,3},{6,0},{7,1},{8,14},{9,15},{10,... | collective-permute-start | bytes 393224 | tf_op jit(solution)/shard_map/ppermute | solution.py:391
  30.6 2.6 %collective-permute-start.12 = (bf16[2,512,128]{2,1,0:T(8,128)(2,1)S(1)}, bf16[2,512,128]{2,1,0:T(8,128)(2,1)S(1)}, u32[]{:S(2)}, u32[]{:S(2)}) collective-permute-start(bf16[2,512,128]{2,1,0:T(8,128)(2,1)S(1)} %theirs.3), channel_id=1, source_target_pairs={{0,1},{1,0},{2,3},{3,2},{4,5},{5,4},{6,7},{7,6},{8,9},{9,8},{10,11... | collective-permute-start | bytes 786440 | tf_op jit(solution)/shard_map/ppermute | solution.py:391
  32.7 1.6 %collective-permute-start.11 = (bf16[2,512,128]{2,1,0:T(8,128)(2,1)S(1)}, bf16[2,512,128]{2,1,0:T(8,128)(2,1)S(1)}, u32[]{:S(2)}, u32[]{:S(2)}) collective-permute-start(bf16[2,512,128]{2,1,0:T(8,128)(2,1)S(1)} %theirs.2), channel_id=1, source_target_pairs={{0,1},{1,0},{2,3},{3,2},{4,5},{5,4},{6,7},{7,6},{8,9},{9,8},{10,11... | collective-permute-start | bytes 786440 | tf_op jit(solution)/shard_map/ppermute | solution.py:391

commit v32 on v29

--- a/solution.py
+++ b/solution.py
@@ -396,8 +396,8 @@
     scale = float(HEAD * queries.shape[0] * 2 * far_count * outer_count) ** (-0.5)
     tokens = (queries, keys, values, cotangent)
     give = first_sums(tokens)
-    got = [swap(give, "inner", 1), swap(*sums(tokens, (False, 1)), "inner", 1)]
-    keep = sums(tokens, (True, 0), (True, 1))
+    *keep, give_rest = sums(tokens, (True, 0), (True, 1), (False, 1))
+    got = [swap(give, "inner", 1), swap(give_rest, "inner", 1)]
     slots = [slot for b in range(2) for slot in pair_slots(keep[b], got[b], far_count // 2)]
     slots, local = lax.optimization_barrier((swap_far(slots), local_part(tokens)))
     sends = group_sends(slots, outer_count)

time: 35.6 us -> 36.5 us (1.025)
  waiting for transfers between devices: 12.3 us -> 12.9 us
  starting transfers between devices: 13.6 us -> 14 us
    ppermute x13, waiting for transfers between devices: 12.3 us -> 12.9 us  [swap(): lax.ppermute(x, axis, [(i, i ^ bits) for i in range(lax.axis_size(axis))])]
    pallas_call x2 -> x1, Pallas kernels: 0.77 us -> 0.65 us  [sums(): pl.pallas_call(functools.partial(sums_kernel, wanted), name='sums', in_sp...]
  transfers between devices with their start and end apart: 13 -> 13, of which waited for: 8 -> 8; matrix products, arithmetic and copies ran while one was open for 0% -> 0% of each run, Pallas kernels for 16% -> 15%
where the time goes in v32:
time: 36.5 us; the launch traced here: 36.3 us
  starting transfers between devices  14 us (38%)
  waiting for transfers between devices  12.9 us (35%)
  Pallas kernels  8.59 us (24%)
  between operations  0.78 us (2%)
    ppermute x13, starting transfers between devices, swap(): lax.ppermute(x, axis, [(i, i ^ bits) for i in range(lax.axis_size(axis))])  14 us
    ppermute x13, waiting for transfers between devices, swap(): lax.ppermute(x, axis, [(i, i ^ bits) for i in range(lax.axis_size(axis))])  12.9 us
    pallas_call x4, Pallas kernels, finish(): pl.pallas_call(functools.partial(finish_kernel, scale, own, block, len(sl...  3.68 us
    pallas_call x1, Pallas kernels, local_part(): pl.pallas_call(local_kernel, name='local', in_specs=[VMEM] * 4, out_specs...  2.16 us
    pallas_call x1, Pallas kernels, first_sums(): pl.pallas_call(give_kernel, name='first_sums', in_specs=[ANY] * 4, out_sp...  1.59 us
  transfers between devices with their start and end apart: 13, of which 8 were waited for; matrix products, arithmetic and copies ran while one was open for 0% of the time, Pallas kernels for 15%

profile of v32, /device:TPU:0, one launch (start us, length us, event | category | flops | bytes accessed | tf_op | source)
XLA Modules:
  0.0 36.3 jit_solution(11443696059862334729)
XLA Ops:
  0.7 1.6 %first_sums.1 = bf16[2,512,128]{2,1,0:T(8,128)(2,1)S(1)} custom-call(bf16[128,2048]{1,0:T(8,128)(2,1)} %refs_0_.13, bf16[128,2048]{1,0:T(8,128)(2,1)} %refs_1_.13, bf16[128,2048]{1,0:T(8,128)(2,1)} %refs_2_.13, bf16[128,2048]{1,0:T(8,128)(2,1)} %refs_3_.13), custom_call_target="tpu_custom_call" | custom-call | flops 33554432 | bytes 786432 | tf_op jit(solution)/shard_map/first_sums/pallas_call | solution.py:95
  2.3 0.5 %collective-permute-start = (bf16[2,512,128]{2,1,0:T(8,128)(2,1)S(1)}, bf16[2,512,128]{2,1,0:T(8,128)(2,1)S(1)}, u32[]{:S(2)}, u32[]{:S(2)}) collective-permute-start(bf16[2,512,128]{2,1,0:T(8,128)(2,1)S(1)} %first_sums.1), channel_id=1, source_target_pairs={{0,1},{1,0},{2,3},{3,2},{4,5},{5,4},{6,7},{7,6},{8,9},{9,8},{10,11... | collective-permute-start | bytes 786440 | tf_op jit(solution)/shard_map/ppermute | solution.py:386
  2.8 0.7 %sums.1 = (bf16[2,512,128]{2,1,0:T(8,128)(2,1)S(1)}, bf16[2,512,128]{2,1,0:T(8,128)(2,1)S(1)}, bf16[2,512,128]{2,1,0:T(8,128)(2,1)S(1)}) custom-call(bf16[128,2048]{1,0:T(8,128)(2,1)S(1)} %copy-done, bf16[128,2048]{1,0:T(8,128)(2,1)S(1)} %copy-done.1, bf16[128,2048]{1,0:T(8,128)(2,1)S(1)} %copy-done.2, bf16[128,2048]{1,0:T(8,128)(2,1)S(1)} %copy-done.3), custom_call_target="tpu_custom_call" | custom-call | flops 100663296 | bytes 2359296 | tf_op jit(solution)/shard_map/sums/pallas_call | solution.py:116
  3.6 0.4 %collective-permute-done.got_ref.refs_10_ = bf16[2,512,128]{2,1,0:T(8,128)(2,1)S(1)} collective-permute-done((bf16[2,512,128]{2,1,0:T(8,128)(2,1)S(1)}, bf16[2,512,128]{2,1,0:T(8,128)(2,1)S(1)}, u32[]{:S(2)}, u32[]{:S(2)}) %collective-permute-start) | collective-permute-done | bytes 262176 | tf_op jit(solution)/shard_map/ppermute | solution.py:386
  4.0 2.9 %collective-permute-start.1 = (bf16[2,256,128]{2,1,0:T(8,128)(2,1)S(1)}, bf16[2,256,128]{2,1,0:T(8,128)(2,1)S(1)}, u32[]{:S(2)}, u32[]{:S(2)}) collective-permute-start(bf16[2,256,128]{2,1,0:T(8,128)(2,1)S(1)} %get-tuple-element.47), channel_id=1, source_target_pairs={{0,2},{1,3},{2,0},{3,1},{4,6},{5,7},{6,4},{7,5},{8,10},{9,11},{10,... | collective-permute-start | bytes 393224 | tf_op jit(solution)/shard_map/ppermute | solution.py:386
  7.0 1.6 %collective-permute-start.3 = (bf16[2,256,128]{2,1,0:T(8,128)(2,1)S(1)}, bf16[2,256,128]{2,1,0:T(8,128)(2,1)S(1)}, u32[]{:S(2)}, u32[]{:S(2)}) collective-permute-start(bf16[2,256,128]{2,1,0:T(8,128)(2,1)S(1)} %get-tuple-element.50), channel_id=1, source_target_pairs={{0,4},{1,5},{2,6},{3,7},{4,0},{5,1},{6,2},{7,3},{8,12},{9,13},{10,... | collective-permute-start | bytes 393224 | tf_op jit(solution)/shard_map/ppermute | solution.py:386
  8.6 0.7 %collective-permute-start.4 = (bf16[2,256,128]{2,1,0:T(8,128)(2,1)S(1)}, bf16[2,256,128]{2,1,0:T(8,128)(2,1)S(1)}, u32[]{:S(2)}, u32[]{:S(2)}) collective-permute-start(bf16[2,256,128]{2,1,0:T(8,128)(2,1)S(1)} %get-tuple-element.51), channel_id=1, source_target_pairs={{0,6},{1,7},{2,4},{3,5},{4,2},{5,3},{6,0},{7,1},{8,14},{9,15},{10,... | collective-permute-start | bytes 393224 | tf_op jit(solution)/shard_map/ppermute | solution.py:386
  9.3 2.2 %local.1 = (f32[128,2048]{1,0:T(8,128)S(1)}, f32[128,2048]{1,0:T(8,128)S(1)}, f32[128,2048]{1,0:T(8,128)S(1)}, f32[128,2048]{1,0:T(8,128)S(1)}) custom-call(bf16[128,2048]{1,0:T(8,128)(2,1)S(1)} %copy-done, bf16[128,2048]{1,0:T(8,128)(2,1)S(1)} %copy-done.1, bf16[128,2048]{1,0:T(8,128)(2,1)S(1)} %copy-done.2, bf16[128,2048]{1,0:T(8,128)(2,1)S(1)} %copy-done.3), custom_call_target="tpu_custom_call" | custom-call | flops 402653184 | bytes 6291456 | tf_op jit(solution)/shard_map/local/pallas_call | solution.py:274
  11.5 3.7 %collective-permute-done.3.refs_2_ = bf16[2,256,128]{2,1,0:T(8,128)(2,1)S(1)} collective-permute-done((bf16[2,256,128]{2,1,0:T(8,128)(2,1)S(1)}, bf16[2,256,128]{2,1,0:T(8,128)(2,1)S(1)}, u32[]{:S(2)}, u32[]{:S(2)}) %collective-permute-start.3) | collective-permute-done | bytes 131104 | tf_op jit(solution)/shard_map/ppermute | solution.py:386
  15.2 3.7 %collective-permute-start.5 = (bf16[256,128]{1,0:T(8,128)(2,1)S(1)}, bf16[256,128]{1,0:T(8,128)(2,1)S(1)}, u32[]{:S(2)}, u32[]{:S(2)}) collective-permute-start(bf16[256,128]{1,0:T(8,128)(2,1)S(1)} %get-tuple-element.64), channel_id=1, source_target_pairs={{0,24},{8,16},{16,8},{24,0},{1,25},{9,17},{17,9},{25,1},{2,26},{10... | collective-permute-start | bytes 196616 | tf_op jit(solution)/shard_map/ppermute | solution.py:386
  18.9 0.8 %collective-permute-start.7 = (bf16[256,128]{1,0:T(8,128)(2,1)S(1)}, bf16[256,128]{1,0:T(8,128)(2,1)S(1)}, u32[]{:S(2)}, u32[]{:S(2)}) collective-permute-start(bf16[256,128]{1,0:T(8,128)(2,1)S(1)} %get-tuple-element.66), channel_id=1, source_target_pairs={{0,16},{8,24},{16,0},{24,8},{1,17},{9,25},{17,1},{25,9},{2,18},{10... | collective-permute-start | bytes 196616 | tf_op jit(solution)/shard_map/ppermute | solution.py:386
  19.7 1.7 %collective-permute-done.5.refs_4_ = bf16[256,128]{1,0:T(8,128)(2,1)S(1)} collective-permute-done((bf16[256,128]{1,0:T(8,128)(2,1)S(1)}, bf16[256,128]{1,0:T(8,128)(2,1)S(1)}, u32[]{:S(2)}, u32[]{:S(2)}) %collective-permute-start.5) | collective-permute-done | bytes 65568 | tf_op jit(solution)/shard_map/ppermute | solution.py:386
  21.4 1.7 %collective-permute-done.6.refs_5_ = bf16[256,128]{1,0:T(8,128)(2,1)S(1)} collective-permute-done((bf16[256,128]{1,0:T(8,128)(2,1)S(1)}, bf16[256,128]{1,0:T(8,128)(2,1)S(1)}, u32[]{:S(2)}, u32[]{:S(2)}) %collective-permute-start.6) | collective-permute-done | bytes 65568 | tf_op jit(solution)/shard_map/ppermute | solution.py:386
  23.2 0.9 %collective-permute-done.7.refs_6_ = bf16[256,128]{1,0:T(8,128)(2,1)S(1)} collective-permute-done((bf16[256,128]{1,0:T(8,128)(2,1)S(1)}, bf16[256,128]{1,0:T(8,128)(2,1)S(1)}, u32[]{:S(2)}, u32[]{:S(2)}) %collective-permute-start.7) | collective-permute-done | bytes 65568 | tf_op jit(solution)/shard_map/ppermute | solution.py:386
  24.1 0.2 scan.1
  24.3 1.5 %collective-permute-start.10 = (bf16[2,256,128]{2,1,0:T(8,128)(2,1)S(1)}, bf16[2,256,128]{2,1,0:T(8,128)(2,1)S(1)}, u32[]{:S(2)}, u32[]{:S(2)}) collective-permute-start(bf16[2,256,128]{2,1,0:T(8,128)(2,1)S(1)} %get-tuple-element.70), channel_id=1, source_target_pairs={{0,2},{1,3},{2,0},{3,1},{4,6},{5,7},{6,4},{7,5},{8,10},{9,11},{10,... | collective-permute-start | bytes 393224 | tf_op jit(solution)/shard_map/ppermute | solution.py:386
  25.8 1.5 %collective-permute-start.8 = (bf16[2,256,128]{2,1,0:T(8,128)(2,1)S(1)}, bf16[2,256,128]{2,1,0:T(8,128)(2,1)S(1)}, u32[]{:S(2)}, u32[]{:S(2)}) collective-permute-start(bf16[2,256,128]{2,1,0:T(8,128)(2,1)S(1)} %get-tuple-element.67), channel_id=1, source_target_pairs={{0,4},{1,5},{2,6},{3,7},{4,0},{5,1},{6,2},{7,3},{8,12},{9,13},{10,... | collective-permute-start | bytes 393224 | tf_op jit(solution)/shard_map/ppermute | solution.py:386
  27.3 0.5 %collective-permute-start.9 = (bf16[2,256,128]{2,1,0:T(8,128)(2,1)S(1)}, bf16[2,256,128]{2,1,0:T(8,128)(2,1)S(1)}, u32[]{:S(2)}, u32[]{:S(2)}) collective-permute-start(bf16[2,256,128]{2,1,0:T(8,128)(2,1)S(1)} %get-tuple-element.68), channel_id=1, source_target_pairs={{0,6},{1,7},{2,4},{3,5},{4,2},{5,3},{6,0},{7,1},{8,14},{9,15},{10,... | collective-permute-start | bytes 393224 | tf_op jit(solution)/shard_map/ppermute | solution.py:386
  27.8 2.6 %collective-permute-done.10.refs_9_.refs_1_ = bf16[2,256,128]{2,1,0:T(8,128)(2,1)S(1)} collective-permute-done((bf16[2,256,128]{2,1,0:T(8,128)(2,1)S(1)}, bf16[2,256,128]{2,1,0:T(8,128)(2,1)S(1)}, u32[]{:S(2)}, u32[]{:S(2)}) %collective-permute-start.10) | collective-permute-done | bytes 131104 | tf_op jit(solution)/shard_map/ppermute | solution.py:386
  30.5 1.2 %finish.4 = (bf16[128,2048]{1,0:T(8,128)(2,1)}, bf16[128,2048]{1,0:T(8,128)(2,1)}, bf16[128,2048]{1,0:T(8,128)(2,1)}, bf16[128,2048]{1,0:T(8,128)(2,1)}) custom-call(bf16[128,2048]{1,0:T(8,128)(2,1)S(1)} %copy-done, bf16[128,2048]{1,0:T(8,128)(2,1)S(1)} %copy-done.1, bf16[128,2048]{1,0:T(8,128)(2,1)S(1)} %copy-done.2, bf16[128,2048]{1,0:T(8,128)(2,1)S(1)} %copy-done.3, ...), custom_call_target="tpu_custom_call" | custom-call | flops 67108864 | bytes 2097152 | tf_op jit(solution)/shard_map/finish/pallas_call | solution.py:368
  31.7 1.8 %collective-permute-done.8.refs_0_.refs_8_ = bf16[2,256,128]{2,1,0:T(8,128)(2,1)S(1)} collective-permute-done((bf16[2,256,128]{2,1,0:T(8,128)(2,1)S(1)}, bf16[2,256,128]{2,1,0:T(8,128)(2,1)S(1)}, u32[]{:S(2)}, u32[]{:S(2)}) %collective-permute-start.8) | collective-permute-done | bytes 131104 | tf_op jit(solution)/shard_map/ppermute | solution.py:386
  33.6 0.4 %finish.5.refs_9_ = bf16[4,128,512]{2,1,0:T(8,128)(2,1)S(1)} custom-call(bf16[128,2048]{1,0:T(8,128)(2,1)S(1)} %copy-done, bf16[128,2048]{1,0:T(8,128)(2,1)S(1)} %copy-done.1, bf16[128,2048]{1,0:T(8,128)(2,1)S(1)} %copy-done.2, bf16[128,2048]{1,0:T(8,128)(2,1)S(1)} %copy-done.3, f32[128,2048]{1,0:T(8,128)S(1)} %get-tuple-element.56.refs_4_, ...), custom_call_target="tpu_custom_call" | custom-call | flops 67108864 | bytes 2097152 | tf_op jit(solution)/shard_map/finish/pallas_call | solution.py:368
  34.1 0.9 %finish.6 = (bf16[128,2048]{1,0:T(8,128)(2,1)}, bf16[128,2048]{1,0:T(8,128)(2,1)}, bf16[128,2048]{1,0:T(8,128)(2,1)}, bf16[128,2048]{1,0:T(8,128)(2,1)}, bf16[4,128,512]{2,1,0:T(8,128)(2,1)S(1)}) custom-call(bf16[128,2048]{1,0:T(8,128)(2,1)S(1)} %copy-done, ...), custom_call_target="tpu_custom_call", output_to_operand_aliasing={{0}: (10, {}), {1}: (11, {}), {2}: (12, {}), {3}: (13, {})} | custom-call | flops 67108864 | bytes 2097152 | tf_op jit(solution)/shard_map/finish/pallas_call | solution.py:368
  35.2 1.2 %finish.7 = (bf16[128,2048]{1,0:T(8,128)(2,1)}, bf16[128,2048]{1,0:T(8,128)(2,1)}, bf16[128,2048]{1,0:T(8,128)(2,1)}, bf16[128,2048]{1,0:T(8,128)(2,1)}) custom-call(bf16[128,2048]{1,0:T(8,128)(2,1)S(1)} %copy-done, bf16[128,2048]{1,0:T(8,128)(2,1)S(1)} %copy-done.1, ...), custom_call_target="tpu_custom_call", output_to_operand_aliasing={{0}: (10, {}), {1}: (11, {}), {2}: (12, {}), {3}: (13, {})} | custom-call | flops 67108864 | bytes 2097152 | tf_op jit(solution)/shard_map/finish/pallas_call | solution.py:368
  (23 shorter events, 0.7 us)
Async XLA Ops:
  0.6 2.2 %copy-start.3 = (bf16[128,2048]{1,0:T(8,128)(2,1)S(1)}, bf16[128,2048]{1,0:T(8,128)(2,1)}, u32[]{:S(2)}) copy-start(bf16[128,2048]{1,0:T(8,128)(2,1)} %refs_3_.13) | copy-start | bytes 1572868
  0.6 2.1 %copy-start.2 = (bf16[128,2048]{1,0:T(8,128)(2,1)S(1)}, bf16[128,2048]{1,0:T(8,128)(2,1)}, u32[]{:S(2)}) copy-start(bf16[128,2048]{1,0:T(8,128)(2,1)} %refs_2_.13) | copy-start | bytes 1572868
  0.7 2.1 %copy-start.1 = (bf16[128,2048]{1,0:T(8,128)(2,1)S(1)}, bf16[128,2048]{1,0:T(8,128)(2,1)}, u32[]{:S(2)}) copy-start(bf16[128,2048]{1,0:T(8,128)(2,1)} %refs_1_.13) | copy-start | bytes 1572868
  0.7 2.1 %copy-start = (bf16[128,2048]{1,0:T(8,128)(2,1)S(1)}, bf16[128,2048]{1,0:T(8,128)(2,1)}, u32[]{:S(2)}) copy-start(bf16[128,2048]{1,0:T(8,128)(2,1)} %refs_0_.13) | copy-start | bytes 1572868
  2.3 1.7 %collective-permute-start = (bf16[2,512,128]{2,1,0:T(8,128)(2,1)S(1)}, bf16[2,512,128]{2,1,0:T(8,128)(2,1)S(1)}, u32[]{:S(2)}, u32[]{:S(2)}) collective-permute-start(bf16[2,512,128]{2,1,0:T(8,128)(2,1)S(1)} %first_sums.1), channel_id=1, source_target_pairs={{0,1},{1,0},{2,3},{3,2},{4,5},{5,4},{6,7},{7,6},{8,9},{9,8},{10,11... | collective-permute-start | bytes 786440 | tf_op jit(solution)/shard_map/ppermute | solution.py:386
  3.5 3.5 %collective-permute-start.2 = (bf16[2,512,128]{2,1,0:T(8,128)(2,1)S(1)}, bf16[2,512,128]{2,1,0:T(8,128)(2,1)S(1)}, u32[]{:S(2)}, u32[]{:S(2)}) collective-permute-start(bf16[2,512,128]{2,1,0:T(8,128)(2,1)S(1)} %get-tuple-element.49), channel_id=1, source_target_pairs={{0,1},{1,0},{2,3},{3,2},{4,5},{5,4},{6,7},{7,6},{8,9},{9,8},{10,11... | collective-permute-start | bytes 786440 | tf_op jit(solution)/shard_map/ppermute | solution.py:386
  4.0 7.4 %collective-permute-start.1 = (bf16[2,256,128]{2,1,0:T(8,128)(2,1)S(1)}, bf16[2,256,128]{2,1,0:T(8,128)(2,1)S(1)}, u32[]{:S(2)}, u32[]{:S(2)}) collective-permute-start(bf16[2,256,128]{2,1,0:T(8,128)(2,1)S(1)} %get-tuple-element.47), channel_id=1, source_target_pairs={{0,2},{1,3},{2,0},{3,1},{4,6},{5,7},{6,4},{7,5},{8,10},{9,11},{10,... | collective-permute-start | bytes 393224 | tf_op jit(solution)/shard_map/ppermute | solution.py:386
  7.0 8.1 %collective-permute-start.3 = (bf16[2,256,128]{2,1,0:T(8,128)(2,1)S(1)}, bf16[2,256,128]{2,1,0:T(8,128)(2,1)S(1)}, u32[]{:S(2)}, u32[]{:S(2)}) collective-permute-start(bf16[2,256,128]{2,1,0:T(8,128)(2,1)S(1)} %get-tuple-element.50), channel_id=1, source_target_pairs={{0,4},{1,5},{2,6},{3,7},{4,0},{5,1},{6,2},{7,3},{8,12},{9,13},{10,... | collective-permute-start | bytes 393224 | tf_op jit(solution)/shard_map/ppermute | solution.py:386
  8.6 6.6 %collective-permute-start.4 = (bf16[2,256,128]{2,1,0:T(8,128)(2,1)S(1)}, bf16[2,256,128]{2,1,0:T(8,128)(2,1)S(1)}, u32[]{:S(2)}, u32[]{:S(2)}) collective-permute-start(bf16[2,256,128]{2,1,0:T(8,128)(2,1)S(1)} %get-tuple-element.51), channel_id=1, source_target_pairs={{0,6},{1,7},{2,4},{3,5},{4,2},{5,3},{6,0},{7,1},{8,14},{9,15},{10,... | collective-permute-start | bytes 393224 | tf_op jit(solution)/shard_map/ppermute | solution.py:386
  15.2 6.2 %collective-permute-start.5 = (bf16[256,128]{1,0:T(8,128)(2,1)S(1)}, bf16[256,128]{1,0:T(8,128)(2,1)S(1)}, u32[]{:S(2)}, u32[]{:S(2)}) collective-permute-start(bf16[256,128]{1,0:T(8,128)(2,1)S(1)} %get-tuple-element.64), channel_id=1, source_target_pairs={{0,24},{8,16},{16,8},{24,0},{1,25},{9,17},{17,9},{25,1},{2,26},{10... | collective-permute-start | bytes 196616 | tf_op jit(solution)/shard_map/ppermute | solution.py:386
  18.9 4.3 %collective-permute-start.6 = (bf16[256,128]{1,0:T(8,128)(2,1)S(1)}, bf16[256,128]{1,0:T(8,128)(2,1)S(1)}, u32[]{:S(2)}, u32[]{:S(2)}) collective-permute-start(bf16[256,128]{1,0:T(8,128)(2,1)S(1)} %get-tuple-element.65), channel_id=1, source_target_pairs={{0,8},{8,0},{16,24},{24,16},{1,9},{9,1},{17,25},{25,17},{2,10},{10... | collective-permute-start | bytes 196616 | tf_op jit(solution)/shard_map/ppermute | solution.py:386
  18.9 5.2 %collective-permute-start.7 = (bf16[256,128]{1,0:T(8,128)(2,1)S(1)}, bf16[256,128]{1,0:T(8,128)(2,1)S(1)}, u32[]{:S(2)}, u32[]{:S(2)}) collective-permute-start(bf16[256,128]{1,0:T(8,128)(2,1)S(1)} %get-tuple-element.66), channel_id=1, source_target_pairs={{0,16},{8,24},{16,0},{24,8},{1,17},{9,25},{17,1},{25,9},{2,18},{10... | collective-permute-start | bytes 196616 | tf_op jit(solution)/shard_map/ppermute | solution.py:386
  24.3 6.1 %collective-permute-start.10 = (bf16[2,256,128]{2,1,0:T(8,128)(2,1)S(1)}, bf16[2,256,128]{2,1,0:T(8,128)(2,1)S(1)}, u32[]{:S(2)}, u32[]{:S(2)}) collective-permute-start(bf16[2,256,128]{2,1,0:T(8,128)(2,1)S(1)} %get-tuple-element.70), channel_id=1, source_target_pairs={{0,2},{1,3},{2,0},{3,1},{4,6},{5,7},{6,4},{7,5},{8,10},{9,11},{10,... | collective-permute-start | bytes 393224 | tf_op jit(solution)/shard_map/ppermute | solution.py:386
  25.8 7.7 %collective-permute-start.8 = (bf16[2,256,128]{2,1,0:T(8,128)(2,1)S(1)}, bf16[2,256,128]{2,1,0:T(8,128)(2,1)S(1)}, u32[]{:S(2)}, u32[]{:S(2)}) collective-permute-start(bf16[2,256,128]{2,1,0:T(8,128)(2,1)S(1)} %get-tuple-element.67), channel_id=1, source_target_pairs={{0,4},{1,5},{2,6},{3,7},{4,0},{5,1},{6,2},{7,3},{8,12},{9,13},{10,... | collective-permute-start | bytes 393224 | tf_op jit(solution)/shard_map/ppermute | solution.py:386
  27.3 6.2 %collective-permute-start.9 = (bf16[2,256,128]{2,1,0:T(8,128)(2,1)S(1)}, bf16[2,256,128]{2,1,0:T(8,128)(2,1)S(1)}, u32[]{:S(2)}, u32[]{:S(2)}) collective-permute-start(bf16[2,256,128]{2,1,0:T(8,128)(2,1)S(1)} %get-tuple-element.68), channel_id=1, source_target_pairs={{0,6},{1,7},{2,4},{3,5},{4,2},{5,3},{6,0},{7,1},{8,14},{9,15},{10,... | collective-permute-start | bytes 393224 | tf_op jit(solution)/shard_map/ppermute | solution.py:386
  30.5 3.6 %collective-permute-start.12 = (bf16[2,512,128]{2,1,0:T(8,128)(2,1)S(1)}, bf16[2,512,128]{2,1,0:T(8,128)(2,1)S(1)}, u32[]{:S(2)}, u32[]{:S(2)}) collective-permute-start(bf16[2,512,128]{2,1,0:T(8,128)(2,1)S(1)} %theirs.3), channel_id=1, source_target_pairs={{0,1},{1,0},{2,3},{3,2},{4,5},{5,4},{6,7},{7,6},{8,9},{9,8},{10,11... | collective-permute-start | bytes 786440 | tf_op jit(solution)/shard_map/ppermute | solution.py:386
  33.5 1.6 %collective-permute-start.11 = (bf16[2,512,128]{2,1,0:T(8,128)(2,1)S(1)}, bf16[2,512,128]{2,1,0:T(8,128)(2,1)S(1)}, u32[]{:S(2)}, u32[]{:S(2)}) collective-permute-start(bf16[2,512,128]{2,1,0:T(8,128)(2,1)S(1)} %theirs.2), channel_id=1, source_target_pairs={{0,1},{1,0},{2,3},{3,2},{4,5},{5,4},{6,7},{7,6},{8,9},{9,8},{10,11... | collective-permute-start | bytes 786440 | tf_op jit(solution)/shard_map/ppermute | solution.py:386

commit v33 on v29

--- a/solution.py
+++ b/solution.py
@@ -107,8 +107,12 @@
 
 
 def sums_kernel(wanted, *refs):
+    width = refs[0].shape[1]
     for (own, block), out in zip(wanted, refs[4:]):
-        sums_of(refs[:4], block_start(own, block, refs[0].shape[1] // 2), out)
+        start = block_start(own, block, width // 2)
+        for n in range(4):
+            at = n * width // 4
+            pl.when(start == at)(functools.partial(sums_of, refs[:4], at, out))
 
 
 def sums(tokens, *wanted):

time: 35.6 us -> 35.6 us (level)
  no operation moved by 1% of the time
where the time goes in v33:
time: 35.6 us; the launch traced here: 35.4 us
  starting transfers between devices  13.6 us (38%)
  waiting for transfers between devices  12.2 us (34%)
  Pallas kernels  8.78 us (25%)
  between operations  0.8 us (2%)
    ppermute x13, starting transfers between devices, swap(): lax.ppermute(x, axis, [(i, i ^ bits) for i in range(lax.axis_size(axis))])  13.6 us
    ppermute x13, waiting for transfers between devices, swap(): lax.ppermute(x, axis, [(i, i ^ bits) for i in range(lax.axis_size(axis))])  12.2 us
    pallas_call x4, Pallas kernels, finish(): pl.pallas_call(functools.partial(finish_kernel, scale, own, block, len(sl...  3.68 us
    pallas_call x1, Pallas kernels, local_part(): pl.pallas_call(local_kernel, name='local', in_specs=[VMEM] * 4, out_specs...  2.15 us
    pallas_call x1, Pallas kernels, first_sums(): pl.pallas_call(give_kernel, name='first_sums', in_specs=[ANY] * 4, out_sp...  1.59 us
    pallas_call x2, Pallas kernels, sums(): pl.pallas_call(functools.partial(sums_kernel, wanted), name='sums', in_sp...  0.84 us
  transfers between devices with their start and end apart: 13, of which 8 were waited for; matrix products, arithmetic and copies ran while one was open for 0% of the time, Pallas kernels for 16%

profile of v33, /device:TPU:0, one launch (start us, length us, event | category | flops | bytes accessed | tf_op | source)
XLA Modules:
  0.0 35.4 jit_solution(5867473521997801391)
XLA Ops:
  0.7 1.6 %first_sums.1 = bf16[2,512,128]{2,1,0:T(8,128)(2,1)S(1)} custom-call(bf16[128,2048]{1,0:T(8,128)(2,1)} %refs_0_.15, bf16[128,2048]{1,0:T(8,128)(2,1)} %refs_1_.15, bf16[128,2048]{1,0:T(8,128)(2,1)} %refs_2_.15, bf16[128,2048]{1,0:T(8,128)(2,1)} %refs_3_.15), custom_call_target="tpu_custom_call" | custom-call | flops 33554432 | bytes 786432 | tf_op jit(solution)/shard_map/first_sums/pallas_call | solution.py:95
  2.3 0.5 %collective-permute-start = (bf16[2,512,128]{2,1,0:T(8,128)(2,1)S(1)}, bf16[2,512,128]{2,1,0:T(8,128)(2,1)S(1)}, u32[]{:S(2)}, u32[]{:S(2)}) collective-permute-start(bf16[2,512,128]{2,1,0:T(8,128)(2,1)S(1)} %first_sums.1), channel_id=1, source_target_pairs={{0,1},{1,0},{2,3},{3,2},{4,5},{5,4},{6,7},{7,6},{8,9},{9,8},{10,11... | collective-permute-start | bytes 786440 | tf_op jit(solution)/shard_map/ppermute | solution.py:390
  2.8 0.3 sums.3
  3.2 0.5 %sums.2 = (bf16[2,512,128]{2,1,0:T(8,128)(2,1)S(1)}, bf16[2,512,128]{2,1,0:T(8,128)(2,1)S(1)}) custom-call(bf16[128,2048]{1,0:T(8,128)(2,1)S(1)} %copy-done, bf16[128,2048]{1,0:T(8,128)(2,1)S(1)} %copy-done.1, bf16[128,2048]{1,0:T(8,128)(2,1)S(1)} %copy-done.2, bf16[128,2048]{1,0:T(8,128)(2,1)S(1)} %copy-done.3), custom_call_target="tpu_custom_call" | custom-call | flops 67108864 | bytes 1572864 | tf_op jit(solution)/shard_map/sums/pallas_call | solution.py:120
  4.0 2.9 %collective-permute-start.1 = (bf16[2,256,128]{2,1,0:T(8,128)(2,1)S(1)}, bf16[2,256,128]{2,1,0:T(8,128)(2,1)S(1)}, u32[]{:S(2)}, u32[]{:S(2)}) collective-permute-start(bf16[2,256,128]{2,1,0:T(8,128)(2,1)S(1)} %get-tuple-element.46), channel_id=1, source_target_pairs={{0,2},{1,3},{2,0},{3,1},{4,6},{5,7},{6,4},{7,5},{8,10},{9,11},{10,... | collective-permute-start | bytes 393224 | tf_op jit(solution)/shard_map/ppermute | solution.py:390
  7.0 1.6 %collective-permute-start.3 = (bf16[2,256,128]{2,1,0:T(8,128)(2,1)S(1)}, bf16[2,256,128]{2,1,0:T(8,128)(2,1)S(1)}, u32[]{:S(2)}, u32[]{:S(2)}) collective-permute-start(bf16[2,256,128]{2,1,0:T(8,128)(2,1)S(1)} %get-tuple-element.48), channel_id=1, source_target_pairs={{0,4},{1,5},{2,6},{3,7},{4,0},{5,1},{6,2},{7,3},{8,12},{9,13},{10,... | collective-permute-start | bytes 393224 | tf_op jit(solution)/shard_map/ppermute | solution.py:390
  8.6 0.3 collective-permute-start.4
  8.9 2.2 %local.1 = (f32[128,2048]{1,0:T(8,128)S(1)}, f32[128,2048]{1,0:T(8,128)S(1)}, f32[128,2048]{1,0:T(8,128)S(1)}, f32[128,2048]{1,0:T(8,128)S(1)}) custom-call(bf16[128,2048]{1,0:T(8,128)(2,1)S(1)} %copy-done, bf16[128,2048]{1,0:T(8,128)(2,1)S(1)} %copy-done.1, bf16[128,2048]{1,0:T(8,128)(2,1)S(1)} %copy-done.2, bf16[128,2048]{1,0:T(8,128)(2,1)S(1)} %copy-done.3), custom_call_target="tpu_custom_call" | custom-call | flops 402653184 | bytes 6291456 | tf_op jit(solution)/shard_map/local/pallas_call | solution.py:278
  11.1 4.0 %collective-permute-done.3.refs_2_ = bf16[2,256,128]{2,1,0:T(8,128)(2,1)S(1)} collective-permute-done((bf16[2,256,128]{2,1,0:T(8,128)(2,1)S(1)}, bf16[2,256,128]{2,1,0:T(8,128)(2,1)S(1)}, u32[]{:S(2)}, u32[]{:S(2)}) %collective-permute-start.3) | collective-permute-done | bytes 131104 | tf_op jit(solution)/shard_map/ppermute | solution.py:390
  15.2 3.7 %collective-permute-start.5 = (bf16[256,128]{1,0:T(8,128)(2,1)S(1)}, bf16[256,128]{1,0:T(8,128)(2,1)S(1)}, u32[]{:S(2)}, u32[]{:S(2)}) collective-permute-start(bf16[256,128]{1,0:T(8,128)(2,1)S(1)} %get-tuple-element.62), channel_id=1, source_target_pairs={{0,24},{8,16},{16,8},{24,0},{1,25},{9,17},{17,9},{25,1},{2,26},{10... | collective-permute-start | bytes 196616 | tf_op jit(solution)/shard_map/ppermute | solution.py:390
  18.9 0.8 %collective-permute-start.7 = (bf16[256,128]{1,0:T(8,128)(2,1)S(1)}, bf16[256,128]{1,0:T(8,128)(2,1)S(1)}, u32[]{:S(2)}, u32[]{:S(2)}) collective-permute-start(bf16[256,128]{1,0:T(8,128)(2,1)S(1)} %get-tuple-element.64), channel_id=1, source_target_pairs={{0,16},{8,24},{16,0},{24,8},{1,17},{9,25},{17,1},{25,9},{2,18},{10... | collective-permute-start | bytes 196616 | tf_op jit(solution)/shard_map/ppermute | solution.py:390
  19.7 1.7 %collective-permute-done.5.refs_4_ = bf16[256,128]{1,0:T(8,128)(2,1)S(1)} collective-permute-done((bf16[256,128]{1,0:T(8,128)(2,1)S(1)}, bf16[256,128]{1,0:T(8,128)(2,1)S(1)}, u32[]{:S(2)}, u32[]{:S(2)}) %collective-permute-start.5) | collective-permute-done | bytes 65568 | tf_op jit(solution)/shard_map/ppermute | solution.py:390
  21.4 1.7 %collective-permute-done.6.refs_5_ = bf16[256,128]{1,0:T(8,128)(2,1)S(1)} collective-permute-done((bf16[256,128]{1,0:T(8,128)(2,1)S(1)}, bf16[256,128]{1,0:T(8,128)(2,1)S(1)}, u32[]{:S(2)}, u32[]{:S(2)}) %collective-permute-start.6) | collective-permute-done | bytes 65568 | tf_op jit(solution)/shard_map/ppermute | solution.py:390
  23.2 0.9 %collective-permute-done.7.refs_6_ = bf16[256,128]{1,0:T(8,128)(2,1)S(1)} collective-permute-done((bf16[256,128]{1,0:T(8,128)(2,1)S(1)}, bf16[256,128]{1,0:T(8,128)(2,1)S(1)}, u32[]{:S(2)}, u32[]{:S(2)}) %collective-permute-start.7) | collective-permute-done | bytes 65568 | tf_op jit(solution)/shard_map/ppermute | solution.py:390
  24.1 0.2 scan.1
  24.3 1.2 %collective-permute-start.10 = (bf16[2,256,128]{2,1,0:T(8,128)(2,1)S(1)}, bf16[2,256,128]{2,1,0:T(8,128)(2,1)S(1)}, u32[]{:S(2)}, u32[]{:S(2)}) collective-permute-start(bf16[2,256,128]{2,1,0:T(8,128)(2,1)S(1)} %get-tuple-element.68), channel_id=1, source_target_pairs={{0,2},{1,3},{2,0},{3,1},{4,6},{5,7},{6,4},{7,5},{8,10},{9,11},{10,... | collective-permute-start | bytes 393224 | tf_op jit(solution)/shard_map/ppermute | solution.py:390
  25.5 1.3 %collective-permute-start.8 = (bf16[2,256,128]{2,1,0:T(8,128)(2,1)S(1)}, bf16[2,256,128]{2,1,0:T(8,128)(2,1)S(1)}, u32[]{:S(2)}, u32[]{:S(2)}) collective-permute-start(bf16[2,256,128]{2,1,0:T(8,128)(2,1)S(1)} %get-tuple-element.65), channel_id=1, source_target_pairs={{0,4},{1,5},{2,6},{3,7},{4,0},{5,1},{6,2},{7,3},{8,12},{9,13},{10,... | collective-permute-start | bytes 393224 | tf_op jit(solution)/shard_map/ppermute | solution.py:390
  26.8 1.1 %collective-permute-start.9 = (bf16[2,256,128]{2,1,0:T(8,128)(2,1)S(1)}, bf16[2,256,128]{2,1,0:T(8,128)(2,1)S(1)}, u32[]{:S(2)}, u32[]{:S(2)}) collective-permute-start(bf16[2,256,128]{2,1,0:T(8,128)(2,1)S(1)} %get-tuple-element.66), channel_id=1, source_target_pairs={{0,6},{1,7},{2,4},{3,5},{4,2},{5,3},{6,0},{7,1},{8,14},{9,15},{10,... | collective-permute-start | bytes 393224 | tf_op jit(solution)/shard_map/ppermute | solution.py:390
  27.8 2.7 %collective-permute-done.10.refs_9_.refs_1_ = bf16[2,256,128]{2,1,0:T(8,128)(2,1)S(1)} collective-permute-done((bf16[2,256,128]{2,1,0:T(8,128)(2,1)S(1)}, bf16[2,256,128]{2,1,0:T(8,128)(2,1)S(1)}, u32[]{:S(2)}, u32[]{:S(2)}) %collective-permute-start.10) | collective-permute-done | bytes 131104 | tf_op jit(solution)/shard_map/ppermute | solution.py:390
  30.7 1.2 %finish.4 = (bf16[128,2048]{1,0:T(8,128)(2,1)}, bf16[128,2048]{1,0:T(8,128)(2,1)}, bf16[128,2048]{1,0:T(8,128)(2,1)}, bf16[128,2048]{1,0:T(8,128)(2,1)}) custom-call(bf16[128,2048]{1,0:T(8,128)(2,1)S(1)} %copy-done, bf16[128,2048]{1,0:T(8,128)(2,1)S(1)} %copy-done.1, bf16[128,2048]{1,0:T(8,128)(2,1)S(1)} %copy-done.2, bf16[128,2048]{1,0:T(8,128)(2,1)S(1)} %copy-done.3, ...), custom_call_target="tpu_custom_call" | custom-call | flops 67108864 | bytes 2097152 | tf_op jit(solution)/shard_map/finish/pallas_call | solution.py:372
  31.9 0.8 %collective-permute-done.9.refs_1_.refs_9_ = bf16[2,256,128]{2,1,0:T(8,128)(2,1)S(1)} collective-permute-done((bf16[2,256,128]{2,1,0:T(8,128)(2,1)S(1)}, bf16[2,256,128]{2,1,0:T(8,128)(2,1)S(1)}, u32[]{:S(2)}, u32[]{:S(2)}) %collective-permute-start.9) | collective-permute-done | bytes 131104 | tf_op jit(solution)/shard_map/ppermute | solution.py:390
  32.8 0.4 %finish.5.refs_9_ = bf16[4,128,512]{2,1,0:T(8,128)(2,1)S(1)} custom-call(bf16[128,2048]{1,0:T(8,128)(2,1)S(1)} %copy-done, bf16[128,2048]{1,0:T(8,128)(2,1)S(1)} %copy-done.1, bf16[128,2048]{1,0:T(8,128)(2,1)S(1)} %copy-done.2, bf16[128,2048]{1,0:T(8,128)(2,1)S(1)} %copy-done.3, f32[128,2048]{1,0:T(8,128)S(1)} %get-tuple-element.54.refs_4_, ...), custom_call_target="tpu_custom_call" | custom-call | flops 67108864 | bytes 2097152 | tf_op jit(solution)/shard_map/finish/pallas_call | solution.py:372
  33.2 0.9 %finish.6 = (bf16[128,2048]{1,0:T(8,128)(2,1)}, bf16[128,2048]{1,0:T(8,128)(2,1)}, bf16[128,2048]{1,0:T(8,128)(2,1)}, bf16[128,2048]{1,0:T(8,128)(2,1)}, bf16[4,128,512]{2,1,0:T(8,128)(2,1)S(1)}) custom-call(bf16[128,2048]{1,0:T(8,128)(2,1)S(1)} %copy-done, ...), custom_call_target="tpu_custom_call", output_to_operand_aliasing={{0}: (10, {}), {1}: (11, {}), {2}: (12, {}), {3}: (13, {})} | custom-call | flops 67108864 | bytes 2097152 | tf_op jit(solution)/shard_map/finish/pallas_call | solution.py:372
  34.3 1.2 %finish.7 = (bf16[128,2048]{1,0:T(8,128)(2,1)}, bf16[128,2048]{1,0:T(8,128)(2,1)}, bf16[128,2048]{1,0:T(8,128)(2,1)}, bf16[128,2048]{1,0:T(8,128)(2,1)}) custom-call(bf16[128,2048]{1,0:T(8,128)(2,1)S(1)} %copy-done, bf16[128,2048]{1,0:T(8,128)(2,1)S(1)} %copy-done.1, ...), custom_call_target="tpu_custom_call", output_to_operand_aliasing={{0}: (10, {}), {1}: (11, {}), {2}: (12, {}), {3}: (13, {})} | custom-call | flops 67108864 | bytes 2097152 | tf_op jit(solution)/shard_map/finish/pallas_call | solution.py:372
  (24 shorter events, 0.9 us)
Async XLA Ops:
  0.6 2.2 %copy-start.3 = (bf16[128,2048]{1,0:T(8,128)(2,1)S(1)}, bf16[128,2048]{1,0:T(8,128)(2,1)}, u32[]{:S(2)}) copy-start(bf16[128,2048]{1,0:T(8,128)(2,1)} %refs_3_.15) | copy-start | bytes 1572868
  0.6 2.1 %copy-start.2 = (bf16[128,2048]{1,0:T(8,128)(2,1)S(1)}, bf16[128,2048]{1,0:T(8,128)(2,1)}, u32[]{:S(2)}) copy-start(bf16[128,2048]{1,0:T(8,128)(2,1)} %refs_2_.15) | copy-start | bytes 1572868
  0.7 2.1 %copy-start.1 = (bf16[128,2048]{1,0:T(8,128)(2,1)S(1)}, bf16[128,2048]{1,0:T(8,128)(2,1)}, u32[]{:S(2)}) copy-start(bf16[128,2048]{1,0:T(8,128)(2,1)} %refs_1_.15) | copy-start | bytes 1572868
  0.7 2.1 %copy-start = (bf16[128,2048]{1,0:T(8,128)(2,1)S(1)}, bf16[128,2048]{1,0:T(8,128)(2,1)}, u32[]{:S(2)}) copy-start(bf16[128,2048]{1,0:T(8,128)(2,1)} %refs_0_.15) | copy-start | bytes 1572868
  2.3 1.7 %collective-permute-start = (bf16[2,512,128]{2,1,0:T(8,128)(2,1)S(1)}, bf16[2,512,128]{2,1,0:T(8,128)(2,1)S(1)}, u32[]{:S(2)}, u32[]{:S(2)}) collective-permute-start(bf16[2,512,128]{2,1,0:T(8,128)(2,1)S(1)} %first_sums.1), channel_id=1, source_target_pairs={{0,1},{1,0},{2,3},{3,2},{4,5},{5,4},{6,7},{7,6},{8,9},{9,8},{10,11... | collective-permute-start | bytes 786440 | tf_op jit(solution)/shard_map/ppermute | solution.py:390
  3.1 3.8 %collective-permute-start.2 = (bf16[2,512,128]{2,1,0:T(8,128)(2,1)S(1)}, bf16[2,512,128]{2,1,0:T(8,128)(2,1)S(1)}, u32[]{:S(2)}, u32[]{:S(2)}) collective-permute-start(bf16[2,512,128]{2,1,0:T(8,128)(2,1)S(1)} %sums.3), channel_id=1, source_target_pairs={{0,1},{1,0},{2,3},{3,2},{4,5},{5,4},{6,7},{7,6},{8,9},{9,8},{10,11... | collective-permute-start | bytes 786440 | tf_op jit(solution)/shard_map/ppermute | solution.py:390
  4.0 7.1 %collective-permute-start.1 = (bf16[2,256,128]{2,1,0:T(8,128)(2,1)S(1)}, bf16[2,256,128]{2,1,0:T(8,128)(2,1)S(1)}, u32[]{:S(2)}, u32[]{:S(2)}) collective-permute-start(bf16[2,256,128]{2,1,0:T(8,128)(2,1)S(1)} %get-tuple-element.46), channel_id=1, source_target_pairs={{0,2},{1,3},{2,0},{3,1},{4,6},{5,7},{6,4},{7,5},{8,10},{9,11},{10,... | collective-permute-start | bytes 393224 | tf_op jit(solution)/shard_map/ppermute | solution.py:390
  7.0 8.1 %collective-permute-start.3 = (bf16[2,256,128]{2,1,0:T(8,128)(2,1)S(1)}, bf16[2,256,128]{2,1,0:T(8,128)(2,1)S(1)}, u32[]{:S(2)}, u32[]{:S(2)}) collective-permute-start(bf16[2,256,128]{2,1,0:T(8,128)(2,1)S(1)} %get-tuple-element.48), channel_id=1, source_target_pairs={{0,4},{1,5},{2,6},{3,7},{4,0},{5,1},{6,2},{7,3},{8,12},{9,13},{10,... | collective-permute-start | bytes 393224 | tf_op jit(solution)/shard_map/ppermute | solution.py:390
  8.6 6.6 %collective-permute-start.4 = (bf16[2,256,128]{2,1,0:T(8,128)(2,1)S(1)}, bf16[2,256,128]{2,1,0:T(8,128)(2,1)S(1)}, u32[]{:S(2)}, u32[]{:S(2)}) collective-permute-start(bf16[2,256,128]{2,1,0:T(8,128)(2,1)S(1)} %get-tuple-element.49), channel_id=1, source_target_pairs={{0,6},{1,7},{2,4},{3,5},{4,2},{5,3},{6,0},{7,1},{8,14},{9,15},{10,... | collective-permute-start | bytes 393224 | tf_op jit(solution)/shard_map/ppermute | solution.py:390
  15.2 6.2 %collective-permute-start.5 = (bf16[256,128]{1,0:T(8,128)(2,1)S(1)}, bf16[256,128]{1,0:T(8,128)(2,1)S(1)}, u32[]{:S(2)}, u32[]{:S(2)}) collective-permute-start(bf16[256,128]{1,0:T(8,128)(2,1)S(1)} %get-tuple-element.62), channel_id=1, source_target_pairs={{0,24},{8,16},{16,8},{24,0},{1,25},{9,17},{17,9},{25,1},{2,26},{10... | collective-permute-start | bytes 196616 | tf_op jit(solution)/shard_map/ppermute | solution.py:390
  18.9 4.3 %collective-permute-start.6 = (bf16[256,128]{1,0:T(8,128)(2,1)S(1)}, bf16[256,128]{1,0:T(8,128)(2,1)S(1)}, u32[]{:S(2)}, u32[]{:S(2)}) collective-permute-start(bf16[256,128]{1,0:T(8,128)(2,1)S(1)} %get-tuple-element.63), channel_id=1, source_target_pairs={{0,8},{8,0},{16,24},{24,16},{1,9},{9,1},{17,25},{25,17},{2,10},{10... | collective-permute-start | bytes 196616 | tf_op jit(solution)/shard_map/ppermute | solution.py:390
  18.9 5.2 %collective-permute-start.7 = (bf16[256,128]{1,0:T(8,128)(2,1)S(1)}, bf16[256,128]{1,0:T(8,128)(2,1)S(1)}, u32[]{:S(2)}, u32[]{:S(2)}) collective-permute-start(bf16[256,128]{1,0:T(8,128)(2,1)S(1)} %get-tuple-element.64), channel_id=1, source_target_pairs={{0,16},{8,24},{16,0},{24,8},{1,17},{9,25},{17,1},{25,9},{2,18},{10... | collective-permute-start | bytes 196616 | tf_op jit(solution)/shard_map/ppermute | solution.py:390
  24.3 6.2 %collective-permute-start.10 = (bf16[2,256,128]{2,1,0:T(8,128)(2,1)S(1)}, bf16[2,256,128]{2,1,0:T(8,128)(2,1)S(1)}, u32[]{:S(2)}, u32[]{:S(2)}) collective-permute-start(bf16[2,256,128]{2,1,0:T(8,128)(2,1)S(1)} %get-tuple-element.68), channel_id=1, source_target_pairs={{0,2},{1,3},{2,0},{3,1},{4,6},{5,7},{6,4},{7,5},{8,10},{9,11},{10,... | collective-permute-start | bytes 393224 | tf_op jit(solution)/shard_map/ppermute | solution.py:390
  25.5 6.4 %collective-permute-start.8 = (bf16[2,256,128]{2,1,0:T(8,128)(2,1)S(1)}, bf16[2,256,128]{2,1,0:T(8,128)(2,1)S(1)}, u32[]{:S(2)}, u32[]{:S(2)}) collective-permute-start(bf16[2,256,128]{2,1,0:T(8,128)(2,1)S(1)} %get-tuple-element.65), channel_id=1, source_target_pairs={{0,4},{1,5},{2,6},{3,7},{4,0},{5,1},{6,2},{7,3},{8,12},{9,13},{10,... | collective-permute-start | bytes 393224 | tf_op jit(solution)/shard_map/ppermute | solution.py:390
  26.8 5.9 %collective-permute-start.9 = (bf16[2,256,128]{2,1,0:T(8,128)(2,1)S(1)}, bf16[2,256,128]{2,1,0:T(8,128)(2,1)S(1)}, u32[]{:S(2)}, u32[]{:S(2)}) collective-permute-start(bf16[2,256,128]{2,1,0:T(8,128)(2,1)S(1)} %get-tuple-element.66), channel_id=1, source_target_pairs={{0,6},{1,7},{2,4},{3,5},{4,2},{5,3},{6,0},{7,1},{8,14},{9,15},{10,... | collective-permute-start | bytes 393224 | tf_op jit(solution)/shard_map/ppermute | solution.py:390
  30.6 2.6 %collective-permute-start.12 = (bf16[2,512,128]{2,1,0:T(8,128)(2,1)S(1)}, bf16[2,512,128]{2,1,0:T(8,128)(2,1)S(1)}, u32[]{:S(2)}, u32[]{:S(2)}) collective-permute-start(bf16[2,512,128]{2,1,0:T(8,128)(2,1)S(1)} %theirs.3), channel_id=1, source_target_pairs={{0,1},{1,0},{2,3},{3,2},{4,5},{5,4},{6,7},{7,6},{8,9},{9,8},{10,11... | collective-permute-start | bytes 786440 | tf_op jit(solution)/shard_map/ppermute | solution.py:390
  32.7 1.6 %collective-permute-start.11 = (bf16[2,512,128]{2,1,0:T(8,128)(2,1)S(1)}, bf16[2,512,128]{2,1,0:T(8,128)(2,1)S(1)}, u32[]{:S(2)}, u32[]{:S(2)}) collective-permute-start(bf16[2,512,128]{2,1,0:T(8,128)(2,1)S(1)} %theirs.2), channel_id=1, source_target_pairs={{0,1},{1,0},{2,3},{3,2},{4,5},{5,4},{6,7},{7,6},{8,9},{9,8},{10,11... | collective-permute-start | bytes 786440 | tf_op jit(solution)/shard_map/ppermute | solution.py:390
